TPU v7x, 32 devices: a whole 2x2x4 slice. The times are simulated.
32 devices in a mesh: grp: 2 (over y), ex: 4 (over z), feat: 4 (over x, core).
Axes of the slice: x: 2, y: 2, z: 4, core: 2. Of those that a mesh axis runs over, the one named last changes fastest.
Arguments:
- train_grads: bfloat16 [2048, 65536], P(('grp', 'ex'), 'feat'), parts along dimension 0, may hold values from -6 to 6
- test_grads: bfloat16 [256, 65536], P('ex', 'feat'), may hold values from -0.03125 to 0.03125
- hess_diag: float32 [65536], P('feat'), may hold values from 0.05 to 5
Outputs:
- scores: float32 [2048, 256], P(('grp', 'ex'), 'feat'), parts along dimension 0
There are 2 independent parts, one for each index of `grp`. A program takes and returns all parts, laid end to end along the dimension named above; an argument that names none is the same for every part. Nothing has to cross between parts.
All inputs are finite; a program needn't handle non-finite values.
Results may differ from a plain program's by a relative error of at most 0.0029.
Values may be sent and summed in bfloat16 or wider, within the bound.
No kernel may reach another device: no remote copies, remote signals or barrier semaphores. Data moves between devices by JAX's collectives and lax.ppermute only.
A program may use at most 64 MiB of HBM per device.

v0:
```python
import jax
import jax.numpy as jnp
from jax import lax
from jax.sharding import PartitionSpec as P


def on_device(train_grads, test_grads, hess_diag):
    inverse = 1.0 / (hess_diag + jnp.float32(0.1))
    precond = (test_grads.astype(jnp.float32) * inverse[None, :]).astype(jnp.bfloat16)
    contract = (((1,), (1,)), ((), ()))
    partial_sums = lax.dot_general(
        train_grads,
        lax.all_gather(precond, "ex", axis=0, tiled=True),
        contract,
        preferred_element_type=jnp.float32,
    )
    return lax.psum_scatter(partial_sums, "feat", scatter_dimension=1, tiled=True)


def solution(mesh):
    return jax.shard_map(
        on_device,
        mesh=mesh,
        in_specs=(P(("grp", "ex"), "feat"), P("ex", "feat"), P("feat")),
        out_specs=P(("grp", "ex"), "feat"),
        check_vma=False,
    )
```

profile of v0, /device:TPU:0, one launch (start us, length us, event | category | flops | bytes accessed | tf_op | source)
XLA Modules:
  0.0 197.4 jit_solution(4742927517441464688)
XLA Ops:
  6.5 0.0 all-gather.2.cloned.1.call-start
  6.5 0.9 add_divide_fusion
  7.4 3.3 %multiply_convert_fusion = bf16[64,16384]{1,0:T(8,128)(2,1)} fusion(bf16[64,16384]{1,0:T(8,128)(2,1)} %param.4, f32[16384]{0:T(1024)S(1)} %add_divide_fusion), kind=kLoop, calls=%fused_computation | loop fusion | flops 3145728 | bytes 4259840 | tf_op jit(solution)/shard_map/convert_element_type | solution.py:9
  10.7 0.0 all-gather.2.cloned.1.call-update
  10.8 0.0 reduce-scatter.2.cloned.1.call-start
  10.8 152.4 %all-gather.2.cloned.1.call-done = bf16[256,16384]{1,0:T(8,128)(2,1)} async-done(((bf16[64,16384]{1,0:T(8,128)(2,1)}), bf16[256,16384]{1,0:T(8,128)(2,1)}) %all-gather.2.cloned.1.call-update) | async-done | bytes 8388624 | tf_op jit(solution)/shard_map/all_gather | solution.py:13
  163.2 8.8 %convolution_bitcast_fusion = f32[256,256]{0,1:T(8,128)} fusion(bf16[256,16384]{1,0:T(8,128)(2,1)} %all-gather.2.cloned.1.call-done, bf16[256,16384]{1,0:T(8,128)(2,1)} %param.3), kind=kOutput, calls=%fused_computation.1 | convolution fusion | flops 2147483648 | bytes 17039360 | tf_op jit(solution)/shard_map/dot_general | solution.py:11
  172.1 0.0 reduce-scatter.2.cloned.1.call-update
  172.1 18.4 %reduce-scatter.2.cloned.1.call-done = f32[256,64]{0,1:T(8,128)} async-done(((f32[256,256]{0,1:T(8,128)}), f32[256,64]{0,1:T(8,128)}) %reduce-scatter.2.cloned.1.call-update) | async-done | bytes 65552 | tf_op jit(solution)/shard_map/reduce_scatter | solution.py:17
Async XLA Ops:
  6.5 156.7 %all-gather.2.cloned.1.call-start = ((), (), s32[]{:S(2)}) async-start(), calls=%async_computation.1 | async-start | bytes 10485760 | tf_op jit(solution)/shard_map/all_gather | solution.py:13
  10.8 179.8 %reduce-scatter.2.cloned.1.call-start = ((), (), s32[]{:S(2)}) async-start(), calls=%async_computation.2 | async-start | bytes 327680 | tf_op jit(solution)/shard_map/reduce_scatter | solution.py:17
Sparse Core Ops, SparseCore 0:
  10.9 152.3 all-gather.1
  172.2 18.2 reduce-scatter.1
where the time goes:
time: 198 us; the launch traced here: 197 us
  waiting for transfers between devices  171 us (86%)
  between operations  13.4 us (7%)
  matrix products  8.85 us (4%)
  other arithmetic  4.19 us (2%)
    all_gather x1, waiting for transfers between devices, on_device(): lax.all_gather(precond, 'ex', axis=0, tiled=True)  152 us
    reduce_scatter x1, waiting for transfers between devices, on_device(): lax.psum_scatter(partial_sums, 'feat', scatter_dimension=1, tiled=True)  18.4 us
    dot_general x1, matrix products, on_device(): lax.dot_general(train_grads, lax.all_gather(precond, 'ex', axis=0, tiled=...  8.85 us
  transfers between devices with their start and end apart: 2, of which 2 were waited for; matrix products, arithmetic and copies ran while one was open for 0% of the time, Pallas kernels for 0%

commit v1 on v0

v1 whole, which is shorter than its diff:
```python
import jax
import jax.numpy as jnp
from jax import lax
from jax.sharding import PartitionSpec as P

CHAINS = 2
CONTRACT = (((1,), (1,)), ((), ()))


def ring(n, shift):
    return [(i, (i + shift) % n) for i in range(n)]


def solution(mesh):
    n_grp, n_ex, n_feat = (mesh.shape[a] for a in ("grp", "ex", "feat"))

    def on_device(train, test, hess):
        feats = train.shape[1]
        queries = test.shape[0]
        grp, ex, feat = (lax.axis_index(a) for a in ("grp", "ex", "feat"))
        inverse = 1.0 / (hess + jnp.float32(0.1))
        precond = (test.astype(jnp.float32) * inverse[None, :]).astype(jnp.bfloat16)

        share = feats // n_grp
        width = share // CHAINS

        def times(block, start):
            part = lax.dynamic_slice_in_dim(train, start, block.shape[1], axis=1)
            return lax.dot_general(part, block, CONTRACT, preferred_element_type=jnp.float32)

        held = [
            lax.dynamic_slice_in_dim(precond, grp * share + k * width, width, axis=1)
            for k in range(CHAINS)
        ]
        sums = [times(precond, 0)]
        for step in range(1, n_ex):
            total = jnp.zeros((train.shape[0], queries), jnp.float32)
            for k in range(CHAINS):
                held[k] = lax.ppermute(held[k], "ex", ring(n_ex, 1))
                total += times(held[k], grp * share + k * width)
                for shift in range(1, n_grp):
                    other = lax.ppermute(held[k], "grp", ring(n_grp, shift))
                    source = (grp - shift) % n_grp
                    total += times(other, source * share + k * width)
            sums.append(total)

        stacked = jnp.stack(sums)
        order = (ex - jnp.arange(n_ex)) % n_ex
        blocks = jnp.take(stacked, order, axis=0)
        per_out = n_ex * queries // n_feat
        scores = jnp.moveaxis(blocks, 0, 1).reshape(train.shape[0], n_ex * queries)

        pieces = scores.reshape(train.shape[0], n_feat, per_out)
        pieces = jnp.moveaxis(pieces, 1, 0)
        bit = 1
        while bit < n_feat:
            mine = (feat // bit) % 2
            pairs = pieces.reshape((-1, 2) + pieces.shape[1:])
            keep = lax.dynamic_index_in_dim(pairs, mine, axis=1, keepdims=False)
            send = lax.dynamic_index_in_dim(pairs, 1 - mine, axis=1, keepdims=False)
            partner = [(i, i ^ bit) for i in range(n_feat)]
            pieces = keep + lax.ppermute(send, "feat", partner)
            bit *= 2
        return pieces[0]

    return jax.shard_map(
        on_device,
        mesh=mesh,
        in_specs=(P(("grp", "ex"), "feat"), P("ex", "feat"), P("feat")),
        out_specs=P(("grp", "ex"), "feat"),
        check_vma=False,
    )
```

time: 198 us -> 104 us (0.53)
  waiting for transfers between devices: 171 us -> 56.2 us
  starting transfers between devices: 0.04 us -> 16.6 us
  matrix products: 8.85 us -> 24.9 us
  between operations: 13.4 us -> 0.21 us
    all_gather x1 -> x0, waiting for transfers between devices: 152 us -> none  [on_device(): lax.all_gather(precond, 'ex', axis=0, tiled=True)]
    ppermute x0 -> x14, waiting for transfers between devices: none -> 56.2 us  [the longest x6 37.7 us: on_device(): held[k] = lax.ppermute(held[k], 'ex', ring(n_ex, 1))]
    reduce_scatter x1 -> x0, waiting for transfers between devices: 18.4 us -> none  [on_device(): lax.psum_scatter(partial_sums, 'feat', scatter_dimension=1, tiled=True)]
    ppermute x0 -> x14, starting transfers between devices: none -> 16.6 us  [the longest x6 10.5 us: on_device(): other = lax.ppermute(held[k], 'grp', ring(n_grp, shift))]
    dot_general x1 -> x13, matrix products: 8.85 us -> 24.9 us  [times(): lax.dot_general(part, block, CONTRACT, preferred_element_type=jnp.float32)]
  transfers between devices with their start and end apart: 2 -> 14, of which waited for: 2 -> 10; matrix products, arithmetic and copies ran while one was open for 0% -> 23% of each run, Pallas kernels for 0% -> 0%
where the time goes in v1:
time: 104 us; the launch traced here: 103 us
  waiting for transfers between devices  56.2 us (54%)
  matrix products  24.9 us (24%)
  starting transfers between devices  16.6 us (16%)
  other arithmetic  3.62 us (3%)
  local copies, waits for them, and re-layouts  1.67 us (2%)
    ppermute x6, waiting for transfers between devices, on_device(): held[k] = lax.ppermute(held[k], 'ex', ring(n_ex, 1))  37.7 us
    dot_general x13, matrix products, times(): lax.dot_general(part, block, CONTRACT, preferred_element_type=jnp.float32)  24.9 us
    ppermute x6, waiting for transfers between devices, on_device(): other = lax.ppermute(held[k], 'grp', ring(n_grp, shift))  14.2 us
    ppermute x6, starting transfers between devices, on_device(): other = lax.ppermute(held[k], 'grp', ring(n_grp, shift))  10.5 us
    ppermute x6, starting transfers between devices, on_device(): held[k] = lax.ppermute(held[k], 'ex', ring(n_ex, 1))  4.73 us
    ppermute x2, waiting for transfers between devices, on_device(): pieces = keep + lax.ppermute(send, 'feat', partner)  4.31 us
  transfers between devices with their start and end apart: 14, of which 10 were waited for; matrix products, arithmetic and copies ran while one was open for 23% of the time, Pallas kernels for 0%

profile of v1, /device:TPU:0, one launch (start us, length us, event | category | flops | bytes accessed | tf_op | source)
XLA Modules:
  0.0 103.2 jit_solution(15768360278977582497)
XLA Ops:
  0.0 0.9 add_divide_fusion
  0.9 2.0 %multiply_convert_fusion = bf16[64,16384]{1,0:T(8,128)(2,1)S(1)} fusion(bf16[64,16384]{1,0:T(8,128)(2,1)} %param.4, f32[16384]{0:T(1024)S(1)} %add_divide_fusion), kind=kLoop, calls=%fused_computation.1 | loop fusion | flops 3145728 | bytes 4259840 | tf_op jit(solution)/shard_map/convert_element_type | solution.py:22
  2.8 1.1 %constant_dynamic-slice_fusion.2 = (bf16[64,4096]{1,0:T(8,128)(2,1)}, bf16[64,4096]{1,0:T(8,128)(2,1)}) fusion(bf16[64,16384]{1,0:T(8,128)(2,1)S(1)} %multiply_convert_fusion, s32[]{:T(128)S(6)} %select_n.108, s32[]{:T(128)S(6)} %select_n.111), kind=kLoop, calls=%fused_computation.61 | loop fusion | bytes 2097160 | tf_op jit(solution)/shard_map/dynamic_slice | solution.py:32
  3.9 3.0 %collective-permute-start.2 = (bf16[64,4096]{1,0:T(8,128)(2,1)}, bf16[64,4096]{1,0:T(8,128)(2,1)S(1)}, u32[]{:S(2)}, u32[]{:S(2)}) collective-permute-start(bf16[64,4096]{1,0:T(8,128)(2,1)} %get-tuple-element.6), channel_id=1, source_target_pairs={{0,4},{4,8},{8,12},{12,0},{1,5},{5,9},{9,13},{13,1},{2,6},{6,10},{... | collective-permute-start | bytes 1572872 | tf_op jit(solution)/shard_map/ppermute | solution.py:39
  6.9 1.6 %collective-permute-start = (bf16[64,4096]{1,0:T(8,128)(2,1)}, bf16[64,4096]{1,0:T(8,128)(2,1)S(1)}, u32[]{:S(2)}, u32[]{:S(2)}) collective-permute-start(bf16[64,4096]{1,0:T(8,128)(2,1)} %get-tuple-element.5), channel_id=1, source_target_pairs={{0,4},{4,8},{8,12},{12,0},{1,5},{5,9},{9,13},{13,1},{2,6},{6,10},{... | collective-permute-start | bytes 1572872 | tf_op jit(solution)/shard_map/ppermute | solution.py:39
  8.5 6.0 %convolution_bitcast_fusion = f32[1,256,64]{1,2,0:T(8,128)S(1)} fusion(bf16[64,16384]{1,0:T(8,128)(2,1)S(1)} %multiply_convert_fusion, bf16[256,16384]{1,0:T(8,128)(2,1)} %param.3), kind=kOutput, calls=%fused_computation.26 | convolution fusion | flops 536870912 | bytes 10551296 | tf_op jit(solution)/shard_map/dot_general | solution.py:29
  14.6 7.3 %collective-permute-done.2 = bf16[64,4096]{1,0:T(8,128)(2,1)S(1)} collective-permute-done((bf16[64,4096]{1,0:T(8,128)(2,1)}, bf16[64,4096]{1,0:T(8,128)(2,1)S(1)}, u32[]{:S(2)}, u32[]{:S(2)}) %collective-permute-start.2) | collective-permute-done | bytes 524320 | tf_op jit(solution)/shard_map/ppermute | solution.py:39
  22.0 1.8 %collective-permute-start.3 = (bf16[64,4096]{1,0:T(8,128)(2,1)S(1)}, bf16[64,4096]{1,0:T(8,128)(2,1)S(1)}, u32[]{:S(2)}, u32[]{:S(2)}) collective-permute-start(bf16[64,4096]{1,0:T(8,128)(2,1)S(1)} %collective-permute-done.2), channel_id=1, source_target_pairs={{0,16},{16,0},{1,17},{17,1},{2,18},{18,2},{3,19},{19,3},{4,20},{20... | collective-permute-start | bytes 1572872 | tf_op jit(solution)/shard_map/ppermute | solution.py:42
  23.8 9.3 %collective-permute-done = bf16[64,4096]{1,0:T(8,128)(2,1)S(1)} collective-permute-done((bf16[64,4096]{1,0:T(8,128)(2,1)}, bf16[64,4096]{1,0:T(8,128)(2,1)S(1)}, u32[]{:S(2)}, u32[]{:S(2)}) %collective-permute-start) | collective-permute-done | bytes 524320 | tf_op jit(solution)/shard_map/ppermute | solution.py:39
  33.2 2.5 %fusion.10 = f32[256,64]{0,1:T(8,128)S(1)} fusion(bf16[64,4096]{1,0:T(8,128)(2,1)S(1)} %collective-permute-done.2, bf16[256,16384]{1,0:T(8,128)(2,1)} %param.3, s32[]{:T(128)S(6)} %select_n.111), kind=kOutput, calls=%fused_computation.12 | convolution fusion | flops 134217728 | bytes 2686980 | tf_op jit(solution)/shard_map/dot_general | solution.py:29
  35.7 2.4 %fusion.22 = f32[256,64]{0,1:T(8,128)S(1)} fusion(bf16[64,4096]{1,0:T(8,128)(2,1)S(1)} %collective-permute-done, bf16[256,16384]{1,0:T(8,128)(2,1)} %param.3, s32[]{:T(128)S(6)} %select_n.108), kind=kOutput, calls=%fused_computation.24 | convolution fusion | flops 134217728 | bytes 2686980 | tf_op jit(solution)/shard_map/dot_general | solution.py:29
  38.0 1.8 %collective-permute-start.1 = (bf16[64,4096]{1,0:T(8,128)(2,1)S(1)}, bf16[64,4096]{1,0:T(8,128)(2,1)S(1)}, u32[]{:S(2)}, u32[]{:S(2)}) collective-permute-start(bf16[64,4096]{1,0:T(8,128)(2,1)S(1)} %collective-permute-done), channel_id=1, source_target_pairs={{0,16},{16,0},{1,17},{17,1},{2,18},{18,2},{3,19},{19,3},{4,20},{20... | collective-permute-start | bytes 1572872 | tf_op jit(solution)/shard_map/ppermute | solution.py:42
  39.8 4.5 %collective-permute-done.6 = bf16[64,4096]{1,0:T(8,128)(2,1)S(1)} collective-permute-done((bf16[64,4096]{1,0:T(8,128)(2,1)S(1)}, bf16[64,4096]{1,0:T(8,128)(2,1)S(1)}, u32[]{:S(2)}, u32[]{:S(2)}) %collective-permute-start.6) | collective-permute-done | bytes 524320 | tf_op jit(solution)/shard_map/ppermute | solution.py:39
  44.4 1.8 %collective-permute-start.7 = (bf16[64,4096]{1,0:T(8,128)(2,1)S(1)}, bf16[64,4096]{1,0:T(8,128)(2,1)S(1)}, u32[]{:S(2)}, u32[]{:S(2)}) collective-permute-start(bf16[64,4096]{1,0:T(8,128)(2,1)S(1)} %collective-permute-done.6), channel_id=1, source_target_pairs={{0,16},{16,0},{1,17},{17,1},{2,18},{18,2},{3,19},{19,3},{4,20},{20... | collective-permute-start | bytes 1572872 | tf_op jit(solution)/shard_map/ppermute | solution.py:42
  46.1 2.3 %fusion.8 = f32[256,64]{0,1:T(8,128)S(1)} fusion(bf16[64,4096]{1,0:T(8,128)(2,1)S(1)} %collective-permute-done.6, bf16[256,16384]{1,0:T(8,128)(2,1)} %param.3, s32[]{:T(128)S(6)} %select_n.111), kind=kOutput, calls=%fused_computation.10 | convolution fusion | flops 134217728 | bytes 2686980 | tf_op jit(solution)/shard_map/dot_general | solution.py:29
  48.6 7.0 %collective-permute-done.4 = bf16[64,4096]{1,0:T(8,128)(2,1)S(1)} collective-permute-done((bf16[64,4096]{1,0:T(8,128)(2,1)S(1)}, bf16[64,4096]{1,0:T(8,128)(2,1)S(1)}, u32[]{:S(2)}, u32[]{:S(2)}) %collective-permute-start.4) | collective-permute-done | bytes 524320 | tf_op jit(solution)/shard_map/ppermute | solution.py:39
  55.6 2.3 %fusion.20 = f32[256,64]{0,1:T(8,128)S(1)} fusion(bf16[64,4096]{1,0:T(8,128)(2,1)S(1)} %collective-permute-done.4, bf16[256,16384]{1,0:T(8,128)(2,1)} %param.3, s32[]{:T(128)S(6)} %select_n.108), kind=kOutput, calls=%fused_computation.22 | convolution fusion | flops 134217728 | bytes 2686980 | tf_op jit(solution)/shard_map/dot_general | solution.py:29
  58.0 1.8 %collective-permute-start.5 = (bf16[64,4096]{1,0:T(8,128)(2,1)S(1)}, bf16[64,4096]{1,0:T(8,128)(2,1)S(1)}, u32[]{:S(2)}, u32[]{:S(2)}) collective-permute-start(bf16[64,4096]{1,0:T(8,128)(2,1)S(1)} %collective-permute-done.4), channel_id=1, source_target_pairs={{0,16},{16,0},{1,17},{17,1},{2,18},{18,2},{3,19},{19,3},{4,20},{20... | collective-permute-start | bytes 1572872 | tf_op jit(solution)/shard_map/ppermute | solution.py:42
  59.8 2.3 %fusion.4 = f32[256,64]{0,1:T(8,128)S(1)} fusion(bf16[64,4096]{1,0:T(8,128)(2,1)S(1)} %collective-permute-done.3, bf16[256,16384]{1,0:T(8,128)(2,1)} %param.3, s32[]{:T(128)S(6)} %select_n.112), kind=kOutput, calls=%fused_computation.6 | convolution fusion | flops 134217728 | bytes 2686980 | tf_op jit(solution)/shard_map/dot_general | solution.py:29
  62.2 2.4 %fusion.57 = f32[1,256,64]{1,2,0:T(8,128)S(1)} fusion(f32[256,64]{0,1:T(8,128)S(1)} %fusion.4, f32[256,64]{0,1:T(8,128)S(1)} %fusion.10, f32[256,64]{0,1:T(8,128)S(1)} %fusion.22, bf16[64,4096]{1,0:T(8,128)(2,1)S(1)} %collective-permute-done.1, bf16[256,16384]{1,0:T(8,128)(2,1)} %param.3, s32[]{:T(128)S(6)} %select_n.110), kind=kOutput, calls=%fused_computation.38 | convolution fusion | flops 134266880 | bytes 2883588 | tf_op jit(solution)/shard_map/dot_general | solution.py:29
  64.5 2.3 %collective-permute-done.10 = bf16[64,4096]{1,0:T(8,128)(2,1)S(1)} collective-permute-done((bf16[64,4096]{1,0:T(8,128)(2,1)S(1)}, bf16[64,4096]{1,0:T(8,128)(2,1)S(1)}, u32[]{:S(2)}, u32[]{:S(2)}) %collective-permute-start.10) | collective-permute-done | bytes 524320 | tf_op jit(solution)/shard_map/ppermute | solution.py:39
  66.8 1.8 %collective-permute-start.11 = (bf16[64,4096]{1,0:T(8,128)(2,1)S(1)}, bf16[64,4096]{1,0:T(8,128)(2,1)S(1)}, u32[]{:S(2)}, u32[]{:S(2)}) collective-permute-start(bf16[64,4096]{1,0:T(8,128)(2,1)S(1)} %collective-permute-done.10), channel_id=1, source_target_pairs={{0,16},{16,0},{1,17},{17,1},{2,18},{18,2},{3,19},{19,3},{4,20},{20... | collective-permute-start | bytes 1572872 | tf_op jit(solution)/shard_map/ppermute | solution.py:42
  69.4 0.8 fusion.2
  70.2 7.1 %collective-permute-done.8 = bf16[64,4096]{1,0:T(8,128)(2,1)S(1)} collective-permute-done((bf16[64,4096]{1,0:T(8,128)(2,1)S(1)}, bf16[64,4096]{1,0:T(8,128)(2,1)S(1)}, u32[]{:S(2)}, u32[]{:S(2)}) %collective-permute-start.8) | collective-permute-done | bytes 524320 | tf_op jit(solution)/shard_map/ppermute | solution.py:39
  77.2 1.5 %collective-permute-start.9 = (bf16[64,4096]{1,0:T(8,128)(2,1)S(1)}, bf16[64,4096]{1,0:T(8,128)(2,1)S(1)}, u32[]{:S(2)}, u32[]{:S(2)}) collective-permute-start(bf16[64,4096]{1,0:T(8,128)(2,1)S(1)} %collective-permute-done.8), channel_id=1, source_target_pairs={{0,16},{16,0},{1,17},{17,1},{2,18},{18,2},{3,19},{19,3},{4,20},{20... | collective-permute-start | bytes 1572872 | tf_op jit(solution)/shard_map/ppermute | solution.py:42
  78.8 0.8 fusion.48
  80.3 6.2 %collective-permute-done.11 = bf16[64,4096]{1,0:T(8,128)(2,1)S(1)} collective-permute-done((bf16[64,4096]{1,0:T(8,128)(2,1)S(1)}, bf16[64,4096]{1,0:T(8,128)(2,1)S(1)}, u32[]{:S(2)}, u32[]{:S(2)}) %collective-permute-start.11) | collective-permute-done | bytes 524320 | tf_op jit(solution)/shard_map/ppermute | solution.py:42
  87.3 8.0 %collective-permute-done.9 = bf16[64,4096]{1,0:T(8,128)(2,1)S(1)} collective-permute-done((bf16[64,4096]{1,0:T(8,128)(2,1)S(1)}, bf16[64,4096]{1,0:T(8,128)(2,1)S(1)}, u32[]{:S(2)}, u32[]{:S(2)}) %collective-permute-start.9) | collective-permute-done | bytes 524320 | tf_op jit(solution)/shard_map/ppermute | solution.py:42
  95.3 0.8 fusion.39
  96.9 1.3 %collective-permute-done.12 = f32[2,256,64]{1,2,0:T(8,128)S(1)} collective-permute-done((f32[2,256,64]{1,2,0:T(8,128)S(1)}, f32[2,256,64]{1,2,0:T(8,128)S(1)}, u32[]{:S(2)}, u32[]{:S(2)}) %collective-permute-start.12) | collective-permute-done | bytes 131104 | tf_op jit(solution)/shard_map/ppermute | solution.py:62
  98.2 1.3 %collective-permute-start.13 = (f32[1,256,64]{1,2,0:T(8,128)S(1)}, f32[1,256,64]{1,2,0:T(8,128)S(1)}, u32[]{:S(2)}, u32[]{:S(2)}) collective-permute-start(f32[1,256,64]{1,2,0:T(8,128)S(1)} %constant_dynamic-slice_fusion), channel_id=1, source_target_pairs={{0,2},{1,3},{2,0},{3,1},{4,6},{5,7},{6,4},{7,5},{8,10},{9,11},{10,... | collective-permute-start | bytes 196616 | tf_op jit(solution)/shard_map/ppermute | solution.py:62
  99.5 3.0 %collective-permute-done.13 = f32[1,256,64]{1,2,0:T(8,128)S(1)} collective-permute-done((f32[1,256,64]{1,2,0:T(8,128)S(1)}, f32[1,256,64]{1,2,0:T(8,128)S(1)}, u32[]{:S(2)}, u32[]{:S(2)}) %collective-permute-start.13) | collective-permute-done | bytes 65568 | tf_op jit(solution)/shard_map/ppermute | solution.py:62
  (27 shorter events, 3.9 us)
Async XLA Ops:
  3.9 18.0 %collective-permute-start.2 = (bf16[64,4096]{1,0:T(8,128)(2,1)}, bf16[64,4096]{1,0:T(8,128)(2,1)S(1)}, u32[]{:S(2)}, u32[]{:S(2)}) collective-permute-start(bf16[64,4096]{1,0:T(8,128)(2,1)} %get-tuple-element.6), channel_id=1, source_target_pairs={{0,4},{4,8},{8,12},{12,0},{1,5},{5,9},{9,13},{13,1},{2,6},{6,10},{... | collective-permute-start | bytes 1572872 | tf_op jit(solution)/shard_map/ppermute | solution.py:39
  6.9 26.2 %collective-permute-start = (bf16[64,4096]{1,0:T(8,128)(2,1)}, bf16[64,4096]{1,0:T(8,128)(2,1)S(1)}, u32[]{:S(2)}, u32[]{:S(2)}) collective-permute-start(bf16[64,4096]{1,0:T(8,128)(2,1)} %get-tuple-element.5), channel_id=1, source_target_pairs={{0,4},{4,8},{8,12},{12,0},{1,5},{5,9},{9,13},{13,1},{2,6},{6,10},{... | collective-permute-start | bytes 1572872 | tf_op jit(solution)/shard_map/ppermute | solution.py:39
  21.9 22.5 %collective-permute-start.6 = (bf16[64,4096]{1,0:T(8,128)(2,1)S(1)}, bf16[64,4096]{1,0:T(8,128)(2,1)S(1)}, u32[]{:S(2)}, u32[]{:S(2)}) collective-permute-start(bf16[64,4096]{1,0:T(8,128)(2,1)S(1)} %collective-permute-done.2), channel_id=1, source_target_pairs={{0,4},{4,8},{8,12},{12,0},{1,5},{5,9},{9,13},{13,1},{2,6},{6,10},{... | collective-permute-start | bytes 1572872 | tf_op jit(solution)/shard_map/ppermute | solution.py:39
  22.0 37.8 %collective-permute-start.3 = (bf16[64,4096]{1,0:T(8,128)(2,1)S(1)}, bf16[64,4096]{1,0:T(8,128)(2,1)S(1)}, u32[]{:S(2)}, u32[]{:S(2)}) collective-permute-start(bf16[64,4096]{1,0:T(8,128)(2,1)S(1)} %collective-permute-done.2), channel_id=1, source_target_pairs={{0,16},{16,0},{1,17},{17,1},{2,18},{18,2},{3,19},{19,3},{4,20},{20... | collective-permute-start | bytes 1572872 | tf_op jit(solution)/shard_map/ppermute | solution.py:42
  33.1 22.5 %collective-permute-start.4 = (bf16[64,4096]{1,0:T(8,128)(2,1)S(1)}, bf16[64,4096]{1,0:T(8,128)(2,1)S(1)}, u32[]{:S(2)}, u32[]{:S(2)}) collective-permute-start(bf16[64,4096]{1,0:T(8,128)(2,1)S(1)} %collective-permute-done), channel_id=1, source_target_pairs={{0,4},{4,8},{8,12},{12,0},{1,5},{5,9},{9,13},{13,1},{2,6},{6,10},{... | collective-permute-start | bytes 1572872 | tf_op jit(solution)/shard_map/ppermute | solution.py:39
  33.2 35.4 %slice-start = ((s8[8388608]{0:T(1024)(128)(4,1)}), s8[4194304]{0:T(1024)(128)(4,1)S(1)}, s32[]{:S(2)}) async-start(s8[8388608]{0:T(1024)(128)(4,1)} %bitcast.33), calls=%async_computation | async-start | bytes 8388608
  38.0 24.1 %collective-permute-start.1 = (bf16[64,4096]{1,0:T(8,128)(2,1)S(1)}, bf16[64,4096]{1,0:T(8,128)(2,1)S(1)}, u32[]{:S(2)}, u32[]{:S(2)}) collective-permute-start(bf16[64,4096]{1,0:T(8,128)(2,1)S(1)} %collective-permute-done), channel_id=1, source_target_pairs={{0,16},{16,0},{1,17},{17,1},{2,18},{18,2},{3,19},{19,3},{4,20},{20... | collective-permute-start | bytes 1572872 | tf_op jit(solution)/shard_map/ppermute | solution.py:42
  44.4 25.0 %collective-permute-start.7 = (bf16[64,4096]{1,0:T(8,128)(2,1)S(1)}, bf16[64,4096]{1,0:T(8,128)(2,1)S(1)}, u32[]{:S(2)}, u32[]{:S(2)}) collective-permute-start(bf16[64,4096]{1,0:T(8,128)(2,1)S(1)} %collective-permute-done.6), channel_id=1, source_target_pairs={{0,16},{16,0},{1,17},{17,1},{2,18},{18,2},{3,19},{19,3},{4,20},{20... | collective-permute-start | bytes 1572872 | tf_op jit(solution)/shard_map/ppermute | solution.py:42
  48.5 20.1 %slice-start.1 = ((s8[8388608]{0:T(1024)(128)(4,1)}), s8[4194304]{0:T(1024)(128)(4,1)S(1)}, s32[]{:S(2)}) async-start(s8[8388608]{0:T(1024)(128)(4,1)} %bitcast.33), calls=%async_computation.1 | async-start | bytes 8388608
  48.5 18.3 %collective-permute-start.10 = (bf16[64,4096]{1,0:T(8,128)(2,1)S(1)}, bf16[64,4096]{1,0:T(8,128)(2,1)S(1)}, u32[]{:S(2)}, u32[]{:S(2)}) collective-permute-start(bf16[64,4096]{1,0:T(8,128)(2,1)S(1)} %collective-permute-done.6), channel_id=1, source_target_pairs={{0,4},{4,8},{8,12},{12,0},{1,5},{5,9},{9,13},{13,1},{2,6},{6,10},{... | collective-permute-start | bytes 1572872 | tf_op jit(solution)/shard_map/ppermute | solution.py:39
  58.0 20.8 %collective-permute-start.5 = (bf16[64,4096]{1,0:T(8,128)(2,1)S(1)}, bf16[64,4096]{1,0:T(8,128)(2,1)S(1)}, u32[]{:S(2)}, u32[]{:S(2)}) collective-permute-start(bf16[64,4096]{1,0:T(8,128)(2,1)S(1)} %collective-permute-done.4), channel_id=1, source_target_pairs={{0,16},{16,0},{1,17},{17,1},{2,18},{18,2},{3,19},{19,3},{4,20},{20... | collective-permute-start | bytes 1572872 | tf_op jit(solution)/shard_map/ppermute | solution.py:42
  59.8 17.5 %collective-permute-start.8 = (bf16[64,4096]{1,0:T(8,128)(2,1)S(1)}, bf16[64,4096]{1,0:T(8,128)(2,1)S(1)}, u32[]{:S(2)}, u32[]{:S(2)}) collective-permute-start(bf16[64,4096]{1,0:T(8,128)(2,1)S(1)} %collective-permute-done.4), channel_id=1, source_target_pairs={{0,4},{4,8},{8,12},{12,0},{1,5},{5,9},{9,13},{13,1},{2,6},{6,10},{... | collective-permute-start | bytes 1572872 | tf_op jit(solution)/shard_map/ppermute | solution.py:39
  66.8 19.7 %collective-permute-start.11 = (bf16[64,4096]{1,0:T(8,128)(2,1)S(1)}, bf16[64,4096]{1,0:T(8,128)(2,1)S(1)}, u32[]{:S(2)}, u32[]{:S(2)}) collective-permute-start(bf16[64,4096]{1,0:T(8,128)(2,1)S(1)} %collective-permute-done.10), channel_id=1, source_target_pairs={{0,16},{16,0},{1,17},{17,1},{2,18},{18,2},{3,19},{19,3},{4,20},{20... | collective-permute-start | bytes 1572872 | tf_op jit(solution)/shard_map/ppermute | solution.py:42
  77.2 18.0 %collective-permute-start.9 = (bf16[64,4096]{1,0:T(8,128)(2,1)S(1)}, bf16[64,4096]{1,0:T(8,128)(2,1)S(1)}, u32[]{:S(2)}, u32[]{:S(2)}) collective-permute-start(bf16[64,4096]{1,0:T(8,128)(2,1)S(1)} %collective-permute-done.8), channel_id=1, source_target_pairs={{0,16},{16,0},{1,17},{17,1},{2,18},{18,2},{3,19},{19,3},{4,20},{20... | collective-permute-start | bytes 1572872 | tf_op jit(solution)/shard_map/ppermute | solution.py:42
  96.8 1.4 %collective-permute-start.12 = (f32[2,256,64]{1,2,0:T(8,128)S(1)}, f32[2,256,64]{1,2,0:T(8,128)S(1)}, u32[]{:S(2)}, u32[]{:S(2)}) collective-permute-start(f32[2,256,64]{1,2,0:T(8,128)S(1)} %dynamic-slice_bitcast_fusion), channel_id=1, source_target_pairs={{0,1},{1,0},{2,3},{3,2},{4,5},{5,4},{6,7},{7,6},{8,9},{9,8},{10,11... | collective-permute-start | bytes 393224 | tf_op jit(solution)/shard_map/ppermute | solution.py:62
  98.2 4.3 %collective-permute-start.13 = (f32[1,256,64]{1,2,0:T(8,128)S(1)}, f32[1,256,64]{1,2,0:T(8,128)S(1)}, u32[]{:S(2)}, u32[]{:S(2)}) collective-permute-start(f32[1,256,64]{1,2,0:T(8,128)S(1)} %constant_dynamic-slice_fusion), channel_id=1, source_target_pairs={{0,2},{1,3},{2,0},{3,1},{4,6},{5,7},{6,4},{7,5},{8,10},{9,11},{10,... | collective-permute-start | bytes 196616 | tf_op jit(solution)/shard_map/ppermute | solution.py:62

commit v2 on v1

--- a/solution.py
+++ b/solution.py
@@ -3,7 +3,7 @@
 from jax import lax
 from jax.sharding import PartitionSpec as P
 
-CHAINS = 2
+CHAINS = 4
 CONTRACT = (((1,), (1,)), ((), ()))
 
 
@@ -19,20 +19,21 @@
         queries = test.shape[0]
         grp, ex, feat = (lax.axis_index(a) for a in ("grp", "ex", "feat"))
         inverse = 1.0 / (hess + jnp.float32(0.1))
-        precond = (test.astype(jnp.float32) * inverse[None, :]).astype(jnp.bfloat16)
 
         share = feats // n_grp
         width = share // CHAINS
 
         def times(block, start):
             part = lax.dynamic_slice_in_dim(train, start, block.shape[1], axis=1)
-            return lax.dot_general(part, block, CONTRACT, preferred_element_type=jnp.float32)
+            scale = lax.dynamic_slice_in_dim(inverse, start, block.shape[1], axis=0)
+            precond = (block.astype(jnp.float32) * scale[None, :]).astype(jnp.bfloat16)
+            return lax.dot_general(part, precond, CONTRACT, preferred_element_type=jnp.float32)
 
         held = [
-            lax.dynamic_slice_in_dim(precond, grp * share + k * width, width, axis=1)
+            lax.dynamic_slice_in_dim(test, grp * share + k * width, width, axis=1)
             for k in range(CHAINS)
         ]
-        sums = [times(precond, 0)]
+        sums = [times(test, 0)]
         for step in range(1, n_ex):
             total = jnp.zeros((train.shape[0], queries), jnp.float32)
             for k in range(CHAINS):

time: 104 us -> 100 us (0.962)
  waiting for transfers between devices: 56.2 us -> 36 us
  starting transfers between devices: 16.6 us -> 27.6 us
  matrix products: 24.9 us -> 32.4 us
  other arithmetic: 3.62 us -> 1.66 us
    ppermute x6 -> x12, waiting for transfers between devices: 37.7 us -> 26.1 us  [on_device(): held[k] = lax.ppermute(held[k], 'ex', ring(n_ex, 1))]
    ppermute x6 -> x12, waiting for transfers between devices: 14.2 us -> 5.89 us  [on_device(): other = lax.ppermute(held[k], 'grp', ring(n_grp, shift))]
    dot_general x13 -> x25, matrix products: 24.9 us -> 32.4 us  [times(): lax.dot_general(part, precond, CONTRACT, preferred_element_type=jnp.float32)]
    ppermute x6 -> x12, starting transfers between devices: 4.73 us -> 12.2 us  [on_device(): held[k] = lax.ppermute(held[k], 'ex', ring(n_ex, 1))]
    ppermute x6 -> x12, starting transfers between devices: 10.5 us -> 13.8 us  [on_device(): other = lax.ppermute(held[k], 'grp', ring(n_grp, shift))]
    convert_element_type x1 -> x0, other arithmetic: 1.96 us -> none  [on_device(): precond = (test.astype(jnp.float32) * inverse[None, :]).astype(jnp.bfloat16)]
  transfers between devices with their start and end apart: 14 -> 26, of which waited for: 10 -> 11; matrix products, arithmetic and copies ran while one was open for 23% -> 33% of each run, Pallas kernels for 0% -> 0%
where the time goes in v2:
time: 100 us; the launch traced here: 99.9 us
  waiting for transfers between devices  36 us (36%)
  matrix products  32.4 us (32%)
  starting transfers between devices  27.6 us (28%)
  local copies, waits for them, and re-layouts  1.89 us (2%)
  other arithmetic  1.66 us (2%)
    dot_general x25, matrix products, times(): lax.dot_general(part, precond, CONTRACT, preferred_element_type=jnp.float32)  32.4 us
    ppermute x12, waiting for transfers between devices, on_device(): held[k] = lax.ppermute(held[k], 'ex', ring(n_ex, 1))  26.1 us
    ppermute x12, starting transfers between devices, on_device(): other = lax.ppermute(held[k], 'grp', ring(n_grp, shift))  13.8 us
    ppermute x12, starting transfers between devices, on_device(): held[k] = lax.ppermute(held[k], 'ex', ring(n_ex, 1))  12.2 us
    ppermute x12, waiting for transfers between devices, on_device(): other = lax.ppermute(held[k], 'grp', ring(n_grp, shift))  5.89 us
    ppermute x2, waiting for transfers between devices, on_device(): pieces = keep + lax.ppermute(send, 'feat', partner)  4.07 us
  transfers between devices with their start and end apart: 26, of which 11 were waited for; matrix products, arithmetic and copies ran while one was open for 33% of the time, Pallas kernels for 0%

profile of v2, /device:TPU:0, one launch (start us, length us, event | category | flops | bytes accessed | tf_op | source)
XLA Modules:
  0.0 99.9 jit_solution(8081051325005524530)
XLA Ops:
  1.3 3.1 %collective-permute-start.2 = (bf16[64,2048]{1,0:T(8,128)(2,1)S(1)}, bf16[64,2048]{1,0:T(8,128)(2,1)S(1)}, u32[]{:S(2)}, u32[]{:S(2)}) collective-permute-start(bf16[64,2048]{1,0:T(8,128)(2,1)S(1)} %get-tuple-element.6), channel_id=1, source_target_pairs={{0,4},{4,8},{8,12},{12,0},{1,5},{5,9},{9,13},{13,1},{2,6},{6,10},{... | collective-permute-start | bytes 786440 | tf_op jit(solution)/shard_map/ppermute | solution.py:40
  4.3 1.6 %collective-permute-start = (bf16[64,2048]{1,0:T(8,128)(2,1)S(1)}, bf16[64,2048]{1,0:T(8,128)(2,1)S(1)}, u32[]{:S(2)}, u32[]{:S(2)}) collective-permute-start(bf16[64,2048]{1,0:T(8,128)(2,1)S(1)} %get-tuple-element.5), channel_id=1, source_target_pairs={{0,4},{4,8},{8,12},{12,0},{1,5},{5,9},{9,13},{13,1},{2,6},{6,10},{... | collective-permute-start | bytes 786440 | tf_op jit(solution)/shard_map/ppermute | solution.py:40
  5.9 1.6 %collective-permute-start.4 = (bf16[64,2048]{1,0:T(8,128)(2,1)S(1)}, bf16[64,2048]{1,0:T(8,128)(2,1)S(1)}, u32[]{:S(2)}, u32[]{:S(2)}) collective-permute-start(bf16[64,2048]{1,0:T(8,128)(2,1)S(1)} %get-tuple-element.8), channel_id=1, source_target_pairs={{0,4},{4,8},{8,12},{12,0},{1,5},{5,9},{9,13},{13,1},{2,6},{6,10},{... | collective-permute-start | bytes 786440 | tf_op jit(solution)/shard_map/ppermute | solution.py:40
  8.4 6.7 %fusion.2 = f32[1,256,64]{1,2,0:T(8,128)S(1)} fusion(bf16[256,16384]{1,0:T(8,128)(2,1)} %param.3, bf16[64,16384]{1,0:T(8,128)(2,1)} %param.4, f32[16384]{0:T(1024)S(1)} %add_divide_fusion), kind=kOutput, calls=%fused_computation.4 | convolution fusion | flops 540016640 | bytes 10616832 | tf_op jit(solution)/shard_map/dot_general | solution.py:30
  15.3 1.7 %collective-permute-start.3 = (bf16[64,2048]{1,0:T(8,128)(2,1)S(1)}, bf16[64,2048]{1,0:T(8,128)(2,1)S(1)}, u32[]{:S(2)}, u32[]{:S(2)}) collective-permute-start(bf16[64,2048]{1,0:T(8,128)(2,1)S(1)} %collective-permute-done.2), channel_id=1, source_target_pairs={{0,16},{16,0},{1,17},{17,1},{2,18},{18,2},{3,19},{19,3},{4,20},{20... | collective-permute-start | bytes 786440 | tf_op jit(solution)/shard_map/ppermute | solution.py:43
  17.0 1.6 %collective-permute-start.10 = (bf16[64,2048]{1,0:T(8,128)(2,1)S(1)}, bf16[64,2048]{1,0:T(8,128)(2,1)S(1)}, u32[]{:S(2)}, u32[]{:S(2)}) collective-permute-start(bf16[64,2048]{1,0:T(8,128)(2,1)S(1)} %collective-permute-done.2), channel_id=1, source_target_pairs={{0,4},{4,8},{8,12},{12,0},{1,5},{5,9},{9,13},{13,1},{2,6},{6,10},{... | collective-permute-start | bytes 786440 | tf_op jit(solution)/shard_map/ppermute | solution.py:40
  18.6 1.8 %fusion.40 = f32[256,64]{0,1:T(8,128)S(1)} fusion(bf16[256,16384]{1,0:T(8,128)(2,1)} %param.3, s32[]{:T(128)S(6)} %select_n.169, bf16[64,2048]{1,0:T(8,128)(2,1)S(1)} %collective-permute-done.2, f32[2048]{0:T(1024)S(1)} %get-tuple-element.14), kind=kOutput, calls=%fused_computation.54 | convolution fusion | flops 67502080 | bytes 1384452 | tf_op jit(solution)/shard_map/dot_general | solution.py:30
  21.0 1.7 %fusion.49 = f32[256,64]{0,1:T(8,128)S(1)} fusion(bf16[256,16384]{1,0:T(8,128)(2,1)} %param.3, s32[]{:T(128)S(6)} %select_n.166, bf16[64,2048]{1,0:T(8,128)(2,1)S(1)} %collective-permute-done, f32[2048]{0:T(1024)S(1)} %get-tuple-element.16), kind=kOutput, calls=%fused_computation.63 | convolution fusion | flops 67502080 | bytes 1384452 | tf_op jit(solution)/shard_map/dot_general | solution.py:30
  22.6 2.1 %collective-permute-done.4 = bf16[64,2048]{1,0:T(8,128)(2,1)S(1)} collective-permute-done((bf16[64,2048]{1,0:T(8,128)(2,1)S(1)}, bf16[64,2048]{1,0:T(8,128)(2,1)S(1)}, u32[]{:S(2)}, u32[]{:S(2)}) %collective-permute-start.4) | collective-permute-done | bytes 262176 | tf_op jit(solution)/shard_map/ppermute | solution.py:40
  24.7 1.8 %collective-permute-start.5 = (bf16[64,2048]{1,0:T(8,128)(2,1)S(1)}, bf16[64,2048]{1,0:T(8,128)(2,1)S(1)}, u32[]{:S(2)}, u32[]{:S(2)}) collective-permute-start(bf16[64,2048]{1,0:T(8,128)(2,1)S(1)} %collective-permute-done.4), channel_id=1, source_target_pairs={{0,16},{16,0},{1,17},{17,1},{2,18},{18,2},{3,19},{19,3},{4,20},{20... | collective-permute-start | bytes 786440 | tf_op jit(solution)/shard_map/ppermute | solution.py:43
  26.5 1.7 %fusion.31 = f32[256,64]{0,1:T(8,128)S(1)} fusion(bf16[256,16384]{1,0:T(8,128)(2,1)} %param.3, s32[]{:T(128)S(6)} %select_n.171, bf16[64,2048]{1,0:T(8,128)(2,1)S(1)} %collective-permute-done.4, f32[2048]{0:T(1024)S(1)} %get-tuple-element.12), kind=kOutput, calls=%fused_computation.45 | convolution fusion | flops 67502080 | bytes 1384452 | tf_op jit(solution)/shard_map/dot_general | solution.py:30
  28.2 2.2 %collective-permute-done.6 = bf16[64,2048]{1,0:T(8,128)(2,1)S(1)} collective-permute-done((bf16[64,2048]{1,0:T(8,128)(2,1)S(1)}, bf16[64,2048]{1,0:T(8,128)(2,1)S(1)}, u32[]{:S(2)}, u32[]{:S(2)}) %collective-permute-start.6) | collective-permute-done | bytes 262176 | tf_op jit(solution)/shard_map/ppermute | solution.py:40
  30.3 1.8 %collective-permute-start.7 = (bf16[64,2048]{1,0:T(8,128)(2,1)S(1)}, bf16[64,2048]{1,0:T(8,128)(2,1)S(1)}, u32[]{:S(2)}, u32[]{:S(2)}) collective-permute-start(bf16[64,2048]{1,0:T(8,128)(2,1)S(1)} %collective-permute-done.6), channel_id=1, source_target_pairs={{0,16},{16,0},{1,17},{17,1},{2,18},{18,2},{3,19},{19,3},{4,20},{20... | collective-permute-start | bytes 786440 | tf_op jit(solution)/shard_map/ppermute | solution.py:43
  32.1 1.7 %fusion.22 = f32[256,64]{0,1:T(8,128)S(1)} fusion(bf16[256,16384]{1,0:T(8,128)(2,1)} %param.3, s32[]{:T(128)S(6)} %select_n.173, bf16[64,2048]{1,0:T(8,128)(2,1)S(1)} %collective-permute-done.6, f32[2048]{0:T(1024)S(1)} %get-tuple-element.10), kind=kOutput, calls=%fused_computation.36 | convolution fusion | flops 67502080 | bytes 1384452 | tf_op jit(solution)/shard_map/dot_general | solution.py:30
  33.9 1.7 %fusion.14 = f32[256,64]{0,1:T(8,128)S(1)} fusion(f32[256,64]{0,1:T(8,128)S(1)} %fusion.40, f32[256,64]{0,1:T(8,128)S(1)} %fusion.49, bf16[256,16384]{1,0:T(8,128)(2,1)} %param.3, s32[]{:T(128)S(6)} %select_n.168, bf16[64,2048]{1,0:T(8,128)(2,1)S(1)} %collective-permute-done.1, f32[2048]{0:T(1024)S(1)} %get-tuple-element.15), kind=kOutput, calls=%fused_computation.28 | convolution fusion | flops 67534848 | bytes 1515524 | tf_op jit(solution)/shard_map/dot_general | solution.py:30
  36.9 1.8 %fusion.13 = f32[256,64]{0,1:T(8,128)S(1)} fusion(f32[256,64]{0,1:T(8,128)S(1)} %fusion.31, f32[256,64]{0,1:T(8,128)S(1)} %fusion.14, bf16[256,16384]{1,0:T(8,128)(2,1)} %param.3, s32[]{:T(128)S(6)} %select_n.170, bf16[64,2048]{1,0:T(8,128)(2,1)S(1)} %collective-permute-done.3, f32[2048]{0:T(1024)S(1)} %get-tuple-element.13), kind=kOutput, calls=%fused_computation.26 | convolution fusion | flops 67534848 | bytes 1515524 | tf_op jit(solution)/shard_map/dot_general | solution.py:30
  38.8 1.6 %collective-permute-start.14 = (bf16[64,2048]{1,0:T(8,128)(2,1)S(1)}, bf16[64,2048]{1,0:T(8,128)(2,1)S(1)}, u32[]{:S(2)}, u32[]{:S(2)}) collective-permute-start(bf16[64,2048]{1,0:T(8,128)(2,1)S(1)} %collective-permute-done.6), channel_id=1, source_target_pairs={{0,4},{4,8},{8,12},{12,0},{1,5},{5,9},{9,13},{13,1},{2,6},{6,10},{... | collective-permute-start | bytes 786440 | tf_op jit(solution)/shard_map/ppermute | solution.py:40
  40.4 4.5 %collective-permute-done.8 = bf16[64,2048]{1,0:T(8,128)(2,1)S(1)} collective-permute-done((bf16[64,2048]{1,0:T(8,128)(2,1)S(1)}, bf16[64,2048]{1,0:T(8,128)(2,1)S(1)}, u32[]{:S(2)}, u32[]{:S(2)}) %collective-permute-start.8) | collective-permute-done | bytes 262176 | tf_op jit(solution)/shard_map/ppermute | solution.py:40
  45.1 1.7 %fusion.12 = f32[256,64]{0,1:T(8,128)S(1)} fusion(f32[256,64]{0,1:T(8,128)S(1)} %fusion.22, f32[256,64]{0,1:T(8,128)S(1)} %fusion.13, bf16[256,16384]{1,0:T(8,128)(2,1)} %param.3, s32[]{:T(128)S(6)} %select_n.172, bf16[64,2048]{1,0:T(8,128)(2,1)S(1)} %collective-permute-done.5, f32[2048]{0:T(1024)S(1)} %get-tuple-element.11), kind=kOutput, calls=%fused_computation.24 | convolution fusion | flops 67534848 | bytes 1515524 | tf_op jit(solution)/shard_map/dot_general | solution.py:30
  46.8 1.7 %fusion.47 = f32[256,64]{0,1:T(8,128)S(1)} fusion(bf16[256,16384]{1,0:T(8,128)(2,1)} %param.3, s32[]{:T(128)S(6)} %select_n.166, bf16[64,2048]{1,0:T(8,128)(2,1)S(1)} %collective-permute-done.8, f32[2048]{0:T(1024)S(1)} %get-tuple-element.16), kind=kOutput, calls=%fused_computation.61 | convolution fusion | flops 67502080 | bytes 1384452 | tf_op jit(solution)/shard_map/dot_general | solution.py:30
  48.5 1.7 %fusion.38 = f32[256,64]{0,1:T(8,128)S(1)} fusion(bf16[256,16384]{1,0:T(8,128)(2,1)} %param.3, s32[]{:T(128)S(6)} %select_n.169, bf16[64,2048]{1,0:T(8,128)(2,1)S(1)} %collective-permute-done.10, f32[2048]{0:T(1024)S(1)} %get-tuple-element.14), kind=kOutput, calls=%fused_computation.52 | convolution fusion | flops 67502080 | bytes 1384452 | tf_op jit(solution)/shard_map/dot_general | solution.py:30
  50.2 1.8 %collective-permute-start.11 = (bf16[64,2048]{1,0:T(8,128)(2,1)S(1)}, bf16[64,2048]{1,0:T(8,128)(2,1)S(1)}, u32[]{:S(2)}, u32[]{:S(2)}) collective-permute-start(bf16[64,2048]{1,0:T(8,128)(2,1)S(1)} %collective-permute-done.10), channel_id=1, source_target_pairs={{0,16},{16,0},{1,17},{17,1},{2,18},{18,2},{3,19},{19,3},{4,20},{20... | collective-permute-start | bytes 786440 | tf_op jit(solution)/shard_map/ppermute | solution.py:43
  52.0 1.7 %fusion.29 = f32[256,64]{0,1:T(8,128)S(1)} fusion(bf16[256,16384]{1,0:T(8,128)(2,1)} %param.3, s32[]{:T(128)S(6)} %select_n.171, bf16[64,2048]{1,0:T(8,128)(2,1)S(1)} %collective-permute-done.12, f32[2048]{0:T(1024)S(1)} %get-tuple-element.12), kind=kOutput, calls=%fused_computation.43 | convolution fusion | flops 67502080 | bytes 1384452 | tf_op jit(solution)/shard_map/dot_general | solution.py:30
  54.0 1.7 %fusion.20 = f32[256,64]{0,1:T(8,128)S(1)} fusion(bf16[256,16384]{1,0:T(8,128)(2,1)} %param.3, s32[]{:T(128)S(6)} %select_n.173, bf16[64,2048]{1,0:T(8,128)(2,1)S(1)} %collective-permute-done.14, f32[2048]{0:T(1024)S(1)} %get-tuple-element.10), kind=kOutput, calls=%fused_computation.34 | convolution fusion | flops 67502080 | bytes 1384452 | tf_op jit(solution)/shard_map/dot_general | solution.py:30
  55.7 1.8 %collective-permute-start.15 = (bf16[64,2048]{1,0:T(8,128)(2,1)S(1)}, bf16[64,2048]{1,0:T(8,128)(2,1)S(1)}, u32[]{:S(2)}, u32[]{:S(2)}) collective-permute-start(bf16[64,2048]{1,0:T(8,128)(2,1)S(1)} %collective-permute-done.14), channel_id=1, source_target_pairs={{0,16},{16,0},{1,17},{17,1},{2,18},{18,2},{3,19},{19,3},{4,20},{20... | collective-permute-start | bytes 786440 | tf_op jit(solution)/shard_map/ppermute | solution.py:43
  57.5 1.7 %fusion.11 = f32[1,256,64]{1,2,0:T(8,128)S(1)} fusion(f32[256,64]{0,1:T(8,128)S(1)} %fusion.12, bf16[256,16384]{1,0:T(8,128)(2,1)} %param.3, s32[]{:T(128)S(6)} %select_n.174, bf16[64,2048]{1,0:T(8,128)(2,1)S(1)} %collective-permute-done.7, f32[2048]{0:T(1024)S(1)} %get-tuple-element.9), kind=kOutput, calls=%fused_computation.22 | convolution fusion | flops 67518464 | bytes 1449988 | tf_op jit(solution)/shard_map/dot_general | solution.py:30
  61.4 12.1 %collective-permute-done.16 = bf16[64,2048]{1,0:T(8,128)(2,1)S(1)} collective-permute-done((bf16[64,2048]{1,0:T(8,128)(2,1)S(1)}, bf16[64,2048]{1,0:T(8,128)(2,1)S(1)}, u32[]{:S(2)}, u32[]{:S(2)}) %collective-permute-start.16) | collective-permute-done | bytes 262176 | tf_op jit(solution)/shard_map/ppermute | solution.py:40
  77.5 4.1 %collective-permute-done.22 = bf16[64,2048]{1,0:T(8,128)(2,1)S(1)} collective-permute-done((bf16[64,2048]{1,0:T(8,128)(2,1)S(1)}, bf16[64,2048]{1,0:T(8,128)(2,1)S(1)}, u32[]{:S(2)}, u32[]{:S(2)}) %collective-permute-start.22) | collective-permute-done | bytes 262176 | tf_op jit(solution)/shard_map/ppermute | solution.py:40
  87.2 2.4 %collective-permute-done.21 = bf16[64,2048]{1,0:T(8,128)(2,1)S(1)} collective-permute-done((bf16[64,2048]{1,0:T(8,128)(2,1)S(1)}, bf16[64,2048]{1,0:T(8,128)(2,1)S(1)}, u32[]{:S(2)}, u32[]{:S(2)}) %collective-permute-start.21) | collective-permute-done | bytes 262176 | tf_op jit(solution)/shard_map/ppermute | solution.py:43
  90.0 2.4 %collective-permute-done.23 = bf16[64,2048]{1,0:T(8,128)(2,1)S(1)} collective-permute-done((bf16[64,2048]{1,0:T(8,128)(2,1)S(1)}, bf16[64,2048]{1,0:T(8,128)(2,1)S(1)}, u32[]{:S(2)}, u32[]{:S(2)}) %collective-permute-start.23) | collective-permute-done | bytes 262176 | tf_op jit(solution)/shard_map/ppermute | solution.py:43
  95.0 1.6 %collective-permute-start.25 = (f32[1,256,64]{1,2,0:T(8,128)S(1)}, f32[1,256,64]{1,2,0:T(8,128)S(1)}, u32[]{:S(2)}, u32[]{:S(2)}) collective-permute-start(f32[1,256,64]{1,2,0:T(8,128)S(1)} %constant_dynamic-slice_fusion), channel_id=1, source_target_pairs={{0,2},{1,3},{2,0},{3,1},{4,6},{5,7},{6,4},{7,5},{8,10},{9,11},{10,... | collective-permute-start | bytes 196616 | tf_op jit(solution)/shard_map/ppermute | solution.py:63
  96.5 2.8 %collective-permute-done.25 = f32[1,256,64]{1,2,0:T(8,128)S(1)} collective-permute-done((f32[1,256,64]{1,2,0:T(8,128)S(1)}, f32[1,256,64]{1,2,0:T(8,128)S(1)}, u32[]{:S(2)}, u32[]{:S(2)}) %collective-permute-start.25) | collective-permute-done | bytes 65568 | tf_op jit(solution)/shard_map/ppermute | solution.py:63
  (63 shorter events, 20.2 us)
Async XLA Ops:
  1.3 14.0 %collective-permute-start.2 = (bf16[64,2048]{1,0:T(8,128)(2,1)S(1)}, bf16[64,2048]{1,0:T(8,128)(2,1)S(1)}, u32[]{:S(2)}, u32[]{:S(2)}) collective-permute-start(bf16[64,2048]{1,0:T(8,128)(2,1)S(1)} %get-tuple-element.6), channel_id=1, source_target_pairs={{0,4},{4,8},{8,12},{12,0},{1,5},{5,9},{9,13},{13,1},{2,6},{6,10},{... | collective-permute-start | bytes 786440 | tf_op jit(solution)/shard_map/ppermute | solution.py:40
  4.3 16.1 %collective-permute-start = (bf16[64,2048]{1,0:T(8,128)(2,1)S(1)}, bf16[64,2048]{1,0:T(8,128)(2,1)S(1)}, u32[]{:S(2)}, u32[]{:S(2)}) collective-permute-start(bf16[64,2048]{1,0:T(8,128)(2,1)S(1)} %get-tuple-element.5), channel_id=1, source_target_pairs={{0,4},{4,8},{8,12},{12,0},{1,5},{5,9},{9,13},{13,1},{2,6},{6,10},{... | collective-permute-start | bytes 786440 | tf_op jit(solution)/shard_map/ppermute | solution.py:40
  5.9 18.8 %collective-permute-start.4 = (bf16[64,2048]{1,0:T(8,128)(2,1)S(1)}, bf16[64,2048]{1,0:T(8,128)(2,1)S(1)}, u32[]{:S(2)}, u32[]{:S(2)}) collective-permute-start(bf16[64,2048]{1,0:T(8,128)(2,1)S(1)} %get-tuple-element.8), channel_id=1, source_target_pairs={{0,4},{4,8},{8,12},{12,0},{1,5},{5,9},{9,13},{13,1},{2,6},{6,10},{... | collective-permute-start | bytes 786440 | tf_op jit(solution)/shard_map/ppermute | solution.py:40
  7.5 22.9 %collective-permute-start.6 = (bf16[64,2048]{1,0:T(8,128)(2,1)S(1)}, bf16[64,2048]{1,0:T(8,128)(2,1)S(1)}, u32[]{:S(2)}, u32[]{:S(2)}) collective-permute-start(bf16[64,2048]{1,0:T(8,128)(2,1)S(1)} %get-tuple-element.7), channel_id=1, source_target_pairs={{0,4},{4,8},{8,12},{12,0},{1,5},{5,9},{9,13},{13,1},{2,6},{6,10},{... | collective-permute-start | bytes 786440 | tf_op jit(solution)/shard_map/ppermute | solution.py:40
  15.3 20.3 %collective-permute-start.3 = (bf16[64,2048]{1,0:T(8,128)(2,1)S(1)}, bf16[64,2048]{1,0:T(8,128)(2,1)S(1)}, u32[]{:S(2)}, u32[]{:S(2)}) collective-permute-start(bf16[64,2048]{1,0:T(8,128)(2,1)S(1)} %collective-permute-done.2), channel_id=1, source_target_pairs={{0,16},{16,0},{1,17},{17,1},{2,18},{18,2},{3,19},{19,3},{4,20},{20... | collective-permute-start | bytes 786440 | tf_op jit(solution)/shard_map/ppermute | solution.py:43
  17.0 31.5 %collective-permute-start.10 = (bf16[64,2048]{1,0:T(8,128)(2,1)S(1)}, bf16[64,2048]{1,0:T(8,128)(2,1)S(1)}, u32[]{:S(2)}, u32[]{:S(2)}) collective-permute-start(bf16[64,2048]{1,0:T(8,128)(2,1)S(1)} %collective-permute-done.2), channel_id=1, source_target_pairs={{0,4},{4,8},{8,12},{12,0},{1,5},{5,9},{9,13},{13,1},{2,6},{6,10},{... | collective-permute-start | bytes 786440 | tf_op jit(solution)/shard_map/ppermute | solution.py:40
  18.6 40.7 %slice-start = ((s8[8388608]{0:T(1024)(128)(4,1)}), s8[4194304]{0:T(1024)(128)(4,1)S(1)}, s32[]{:S(2)}) async-start(s8[8388608]{0:T(1024)(128)(4,1)} %bitcast.20), calls=%async_computation | async-start | bytes 8388608
  20.4 13.4 %collective-permute-start.1 = (bf16[64,2048]{1,0:T(8,128)(2,1)S(1)}, bf16[64,2048]{1,0:T(8,128)(2,1)S(1)}, u32[]{:S(2)}, u32[]{:S(2)}) collective-permute-start(bf16[64,2048]{1,0:T(8,128)(2,1)S(1)} %collective-permute-done), channel_id=1, source_target_pairs={{0,16},{16,0},{1,17},{17,1},{2,18},{18,2},{3,19},{19,3},{4,20},{20... | collective-permute-start | bytes 786440 | tf_op jit(solution)/shard_map/ppermute | solution.py:43
  24.7 14.0 %collective-permute-start.5 = (bf16[64,2048]{1,0:T(8,128)(2,1)S(1)}, bf16[64,2048]{1,0:T(8,128)(2,1)S(1)}, u32[]{:S(2)}, u32[]{:S(2)}) collective-permute-start(bf16[64,2048]{1,0:T(8,128)(2,1)S(1)} %collective-permute-done.4), channel_id=1, source_target_pairs={{0,16},{16,0},{1,17},{17,1},{2,18},{18,2},{3,19},{19,3},{4,20},{20... | collective-permute-start | bytes 786440 | tf_op jit(solution)/shard_map/ppermute | solution.py:43
  30.3 27.2 %collective-permute-start.7 = (bf16[64,2048]{1,0:T(8,128)(2,1)S(1)}, bf16[64,2048]{1,0:T(8,128)(2,1)S(1)}, u32[]{:S(2)}, u32[]{:S(2)}) collective-permute-start(bf16[64,2048]{1,0:T(8,128)(2,1)S(1)} %collective-permute-done.6), channel_id=1, source_target_pairs={{0,16},{16,0},{1,17},{17,1},{2,18},{18,2},{3,19},{19,3},{4,20},{20... | collective-permute-start | bytes 786440 | tf_op jit(solution)/shard_map/ppermute | solution.py:43
  33.8 11.1 %collective-permute-start.8 = (bf16[64,2048]{1,0:T(8,128)(2,1)S(1)}, bf16[64,2048]{1,0:T(8,128)(2,1)S(1)}, u32[]{:S(2)}, u32[]{:S(2)}) collective-permute-start(bf16[64,2048]{1,0:T(8,128)(2,1)S(1)} %collective-permute-done), channel_id=1, source_target_pairs={{0,4},{4,8},{8,12},{12,0},{1,5},{5,9},{9,13},{13,1},{2,6},{6,10},{... | collective-permute-start | bytes 786440 | tf_op jit(solution)/shard_map/ppermute | solution.py:40
  35.5 16.5 %collective-permute-start.12 = (bf16[64,2048]{1,0:T(8,128)(2,1)S(1)}, bf16[64,2048]{1,0:T(8,128)(2,1)S(1)}, u32[]{:S(2)}, u32[]{:S(2)}) collective-permute-start(bf16[64,2048]{1,0:T(8,128)(2,1)S(1)} %collective-permute-done.4), channel_id=1, source_target_pairs={{0,4},{4,8},{8,12},{12,0},{1,5},{5,9},{9,13},{13,1},{2,6},{6,10},{... | collective-permute-start | bytes 786440 | tf_op jit(solution)/shard_map/ppermute | solution.py:40
  36.9 22.3 %slice-start.1 = ((s8[8388608]{0:T(1024)(128)(4,1)}), s8[4194304]{0:T(1024)(128)(4,1)S(1)}, s32[]{:S(2)}) async-start(s8[8388608]{0:T(1024)(128)(4,1)} %bitcast.20), calls=%async_computation.1 | async-start | bytes 8388608
  38.8 15.2 %collective-permute-start.14 = (bf16[64,2048]{1,0:T(8,128)(2,1)S(1)}, bf16[64,2048]{1,0:T(8,128)(2,1)S(1)}, u32[]{:S(2)}, u32[]{:S(2)}) collective-permute-start(bf16[64,2048]{1,0:T(8,128)(2,1)S(1)} %collective-permute-done.6), channel_id=1, source_target_pairs={{0,4},{4,8},{8,12},{12,0},{1,5},{5,9},{9,13},{13,1},{2,6},{6,10},{... | collective-permute-start | bytes 786440 | tf_op jit(solution)/shard_map/ppermute | solution.py:40
  44.9 14.3 %collective-permute-start.9 = (bf16[64,2048]{1,0:T(8,128)(2,1)S(1)}, bf16[64,2048]{1,0:T(8,128)(2,1)S(1)}, u32[]{:S(2)}, u32[]{:S(2)}) collective-permute-start(bf16[64,2048]{1,0:T(8,128)(2,1)S(1)} %collective-permute-done.8), channel_id=1, source_target_pairs={{0,16},{16,0},{1,17},{17,1},{2,18},{18,2},{3,19},{19,3},{4,20},{20... | collective-permute-start | bytes 786440 | tf_op jit(solution)/shard_map/ppermute | solution.py:43
  50.2 9.6 %collective-permute-start.11 = (bf16[64,2048]{1,0:T(8,128)(2,1)S(1)}, bf16[64,2048]{1,0:T(8,128)(2,1)S(1)}, u32[]{:S(2)}, u32[]{:S(2)}) collective-permute-start(bf16[64,2048]{1,0:T(8,128)(2,1)S(1)} %collective-permute-done.10), channel_id=1, source_target_pairs={{0,16},{16,0},{1,17},{17,1},{2,18},{18,2},{3,19},{19,3},{4,20},{20... | collective-permute-start | bytes 786440 | tf_op jit(solution)/shard_map/ppermute | solution.py:43
  53.7 29.2 %collective-permute-start.13 = (bf16[64,2048]{1,0:T(8,128)(2,1)S(1)}, bf16[64,2048]{1,0:T(8,128)(2,1)S(1)}, u32[]{:S(2)}, u32[]{:S(2)}) collective-permute-start(bf16[64,2048]{1,0:T(8,128)(2,1)S(1)} %collective-permute-done.12), channel_id=1, source_target_pairs={{0,16},{16,0},{1,17},{17,1},{2,18},{18,2},{3,19},{19,3},{4,20},{20... | collective-permute-start | bytes 786440 | tf_op jit(solution)/shard_map/ppermute | solution.py:43
  55.7 29.0 %collective-permute-start.15 = (bf16[64,2048]{1,0:T(8,128)(2,1)S(1)}, bf16[64,2048]{1,0:T(8,128)(2,1)S(1)}, u32[]{:S(2)}, u32[]{:S(2)}) collective-permute-start(bf16[64,2048]{1,0:T(8,128)(2,1)S(1)} %collective-permute-done.14), channel_id=1, source_target_pairs={{0,16},{16,0},{1,17},{17,1},{2,18},{18,2},{3,19},{19,3},{4,20},{20... | collective-permute-start | bytes 786440 | tf_op jit(solution)/shard_map/ppermute | solution.py:43
  57.5 16.4 %collective-permute-start.18 = (bf16[64,2048]{1,0:T(8,128)(2,1)S(1)}, bf16[64,2048]{1,0:T(8,128)(2,1)S(1)}, u32[]{:S(2)}, u32[]{:S(2)}) collective-permute-start(bf16[64,2048]{1,0:T(8,128)(2,1)S(1)} %collective-permute-done.10), channel_id=1, source_target_pairs={{0,4},{4,8},{8,12},{12,0},{1,5},{5,9},{9,13},{13,1},{2,6},{6,10},{... | collective-permute-start | bytes 786440 | tf_op jit(solution)/shard_map/ppermute | solution.py:40
  59.2 14.3 %collective-permute-start.16 = (bf16[64,2048]{1,0:T(8,128)(2,1)S(1)}, bf16[64,2048]{1,0:T(8,128)(2,1)S(1)}, u32[]{:S(2)}, u32[]{:S(2)}) collective-permute-start(bf16[64,2048]{1,0:T(8,128)(2,1)S(1)} %collective-permute-done.8), channel_id=1, source_target_pairs={{0,4},{4,8},{8,12},{12,0},{1,5},{5,9},{9,13},{13,1},{2,6},{6,10},{... | collective-permute-start | bytes 786440 | tf_op jit(solution)/shard_map/ppermute | solution.py:40
  59.8 16.5 %collective-permute-start.20 = (bf16[64,2048]{1,0:T(8,128)(2,1)S(1)}, bf16[64,2048]{1,0:T(8,128)(2,1)S(1)}, u32[]{:S(2)}, u32[]{:S(2)}) collective-permute-start(bf16[64,2048]{1,0:T(8,128)(2,1)S(1)} %collective-permute-done.12), channel_id=1, source_target_pairs={{0,4},{4,8},{8,12},{12,0},{1,5},{5,9},{9,13},{13,1},{2,6},{6,10},{... | collective-permute-start | bytes 786440 | tf_op jit(solution)/shard_map/ppermute | solution.py:40
  73.5 8.2 %collective-permute-start.22 = (bf16[64,2048]{1,0:T(8,128)(2,1)S(1)}, bf16[64,2048]{1,0:T(8,128)(2,1)S(1)}, u32[]{:S(2)}, u32[]{:S(2)}) collective-permute-start(bf16[64,2048]{1,0:T(8,128)(2,1)S(1)} %collective-permute-done.14), channel_id=1, source_target_pairs={{0,4},{4,8},{8,12},{12,0},{1,5},{5,9},{9,13},{13,1},{2,6},{6,10},{... | collective-permute-start | bytes 786440 | tf_op jit(solution)/shard_map/ppermute | solution.py:40
  73.9 11.2 %collective-permute-start.17 = (bf16[64,2048]{1,0:T(8,128)(2,1)S(1)}, bf16[64,2048]{1,0:T(8,128)(2,1)S(1)}, u32[]{:S(2)}, u32[]{:S(2)}) collective-permute-start(bf16[64,2048]{1,0:T(8,128)(2,1)S(1)} %collective-permute-done.16), channel_id=1, source_target_pairs={{0,16},{16,0},{1,17},{17,1},{2,18},{18,2},{3,19},{19,3},{4,20},{20... | collective-permute-start | bytes 786440 | tf_op jit(solution)/shard_map/ppermute | solution.py:43
  76.3 10.4 %collective-permute-start.19 = (bf16[64,2048]{1,0:T(8,128)(2,1)S(1)}, bf16[64,2048]{1,0:T(8,128)(2,1)S(1)}, u32[]{:S(2)}, u32[]{:S(2)}) collective-permute-start(bf16[64,2048]{1,0:T(8,128)(2,1)S(1)} %collective-permute-done.18), channel_id=1, source_target_pairs={{0,16},{16,0},{1,17},{17,1},{2,18},{18,2},{3,19},{19,3},{4,20},{20... | collective-permute-start | bytes 786440 | tf_op jit(solution)/shard_map/ppermute | solution.py:43
  81.6 7.9 %collective-permute-start.21 = (bf16[64,2048]{1,0:T(8,128)(2,1)S(1)}, bf16[64,2048]{1,0:T(8,128)(2,1)S(1)}, u32[]{:S(2)}, u32[]{:S(2)}) collective-permute-start(bf16[64,2048]{1,0:T(8,128)(2,1)S(1)} %collective-permute-done.20), channel_id=1, source_target_pairs={{0,16},{16,0},{1,17},{17,1},{2,18},{18,2},{3,19},{19,3},{4,20},{20... | collective-permute-start | bytes 786440 | tf_op jit(solution)/shard_map/ppermute | solution.py:43
  82.9 9.5 %collective-permute-start.23 = (bf16[64,2048]{1,0:T(8,128)(2,1)S(1)}, bf16[64,2048]{1,0:T(8,128)(2,1)S(1)}, u32[]{:S(2)}, u32[]{:S(2)}) collective-permute-start(bf16[64,2048]{1,0:T(8,128)(2,1)S(1)} %collective-permute-done.22), channel_id=1, source_target_pairs={{0,16},{16,0},{1,17},{17,1},{2,18},{18,2},{3,19},{19,3},{4,20},{20... | collective-permute-start | bytes 786440 | tf_op jit(solution)/shard_map/ppermute | solution.py:43
  93.5 1.4 %collective-permute-start.24 = (f32[2,256,64]{1,2,0:T(8,128)S(1)}, f32[2,256,64]{1,2,0:T(8,128)S(1)}, u32[]{:S(2)}, u32[]{:S(2)}) collective-permute-start(f32[2,256,64]{1,2,0:T(8,128)S(1)} %dynamic-slice_bitcast_fusion), channel_id=1, source_target_pairs={{0,1},{1,0},{2,3},{3,2},{4,5},{5,4},{6,7},{7,6},{8,9},{9,8},{10,11... | collective-permute-start | bytes 393224 | tf_op jit(solution)/shard_map/ppermute | solution.py:63
  95.0 4.3 %collective-permute-start.25 = (f32[1,256,64]{1,2,0:T(8,128)S(1)}, f32[1,256,64]{1,2,0:T(8,128)S(1)}, u32[]{:S(2)}, u32[]{:S(2)}) collective-permute-start(f32[1,256,64]{1,2,0:T(8,128)S(1)} %constant_dynamic-slice_fusion), channel_id=1, source_target_pairs={{0,2},{1,3},{2,0},{3,1},{4,6},{5,7},{6,4},{7,5},{8,10},{9,11},{10,... | collective-permute-start | bytes 196616 | tf_op jit(solution)/shard_map/ppermute | solution.py:63

commit v3 on v0

v3 whole, which is shorter than its diff:
```python
import jax
import jax.numpy as jnp
from jax import lax
from jax.sharding import PartitionSpec as P

CONTRACT = (((1,), (1,)), ((), ()))


GATES = {
    "R2B_": ("Y1A_",),
    "L2B_": ("Y1A_",),
    "Y1B_": ("Y1A_",),
    "M3A_": ("R2A_", "L2A_"),
    "Y2A_": ("R2A_", "L2A_"),
    "R1S_": ("Y1B_",),
    "L1S_": ("R2B_", "L2B_"),
    "Y2B_": ("R2B_", "L2B_"),
    "M3B_": ("Y2A_",),
    "M2S_": ("R1S_", "L1S_"),
    "R1T_": ("R1S_", "L1S_"),
    "L1T_": ("Y2B_",),
    "R2T_": ("F1",),
    "L2T_": ("F1",),
    "M3T_": ("F2",),
    "E1": ("G",),
}


def plan(feats, n_ex):
    if n_ex == 4:
        first, second = feats // 2, feats // 4
        ship = (2 * first + second) // 8
    else:
        first, second, ship = feats * 9 // 16, feats * 5 // 16, 0
    return ship, first, second, feats - first - second - ship


def solution(mesh):
    n_grp, n_ex, n_feat = (mesh.shape[a] for a in ("grp", "ex", "feat"))

    def on_device(train, test, hess):
        docs, feats = train.shape
        queries = test.shape[0]
        half = queries // n_grp
        grp, ex, feat = (lax.axis_index(a) for a in ("grp", "ex", "feat"))
        low = ex < n_ex // 2
        w_ship, w_first, w_second, w_last = plan(feats, n_ex)
        inverse = 1.0 / (hess + jnp.float32(0.1))

        rolled = lax.dynamic_slice_in_dim(
            jnp.concatenate([test] * 2, axis=0) if n_grp > 1 else test, grp * half, queries, axis=0
        )

        def among(members):
            found = jnp.bool_(False)
            for i in members:
                found = found | (ex == i)
            return found

        done = {}

        def send(name, block, axis, pairs):
            waits = [done[g] for g in GATES.get(name, ()) if g in done]
            if waits:
                block = lax.optimization_barrier((block, waits))[0]
            done[name] = lax.ppermute(block, axis, pairs)
            return done[name]

        class Spread:
            def __init__(self, name, block, first=0, last=n_ex - 1):
                self.name = name
                self.span = range(first, last + 1)
                self.right, self.left = {0: block}, {0: block}

            def hop(self, t, cargo=None):
                down = [(i + 1, i) for i in self.span if i + t < n_ex]
                up = [(i - 1, i) for i in self.span if i >= t]
                if not down and not up:
                    return None
                apart = not (
                    {s for s, _ in down} & {s for s, _ in up}
                    or {d for _, d in down} & {d for _, d in up}
                )
                if apart:
                    block = jnp.where(
                        among([s for s, _ in down]), self.right[t - 1], self.left[t - 1]
                    )
                    if cargo is not None:
                        block = jnp.where(is_end, cargo, block)
                        down, up = down + [ends[1]], up + [ends[0]]
                    block = send(f"M{t}{self.name}", block, "ex", down + up)
                    self.right[t] = self.left[t] = block
                else:
                    right, left = self.right[t - 1], self.left[t - 1]
                    if cargo is not None:
                        right = jnp.where(ex == n_ex - 1, cargo, right)
                        left = jnp.where(ex == 0, cargo, left)
                        down, up = down + [ends[1]], up + [ends[0]]
                    self.right[t] = send(f"R{t}{self.name}", right, "ex", down)
                    self.left[t] = send(f"L{t}{self.name}", left, "ex", up)
                return jnp.where(low, self.left[t], self.right[t])

            def take(self, t):
                if 2 * t <= n_ex:
                    return jnp.where(low, self.right[t], self.left[t])
                back = jnp.where(low, self.left[n_ex - t], self.right[n_ex - t])
                if t not in self.right:
                    return back
                arrived = (ex + t < n_ex) | (ex >= t)
                return jnp.where(arrived, jnp.where(low, self.right[t], self.left[t]), back)

        def swap(name, block):
            blocks = [block]
            for shift in range(1, n_grp):
                pairs = [(i, (i - shift) % n_grp) for i in range(n_grp)]
                blocks.append(send(name, block, "grp", pairs))
            return blocks

        def times(rows, docs_part, start):
            width = rows.shape[1]
            scale = inverse[start : start + width]
            precond = (rows.astype(jnp.float32) * scale[None, :]).astype(jnp.bfloat16)
            return lax.dot_general(precond, docs_part, CONTRACT, preferred_element_type=jnp.float32)

        direction = jnp.where(low, 1, -1)

        def sum_over_feat(name, sums):
            per_out = n_ex * queries // n_feat
            pieces = sums.reshape(n_ex * n_grp, half, docs)

            def rows_of(target):
                got = []
                for k in range(per_out // half):
                    place = target * (per_out // half) + k
                    t = (direction * (place // n_grp - ex)) % n_ex
                    h = (place % n_grp - grp) % n_grp
                    got.append(lax.dynamic_index_in_dim(pieces, t * n_grp + h, 0, keepdims=False))
                return jnp.concatenate(got, axis=0)

            bit = 1
            count = n_feat
            held = None
            while bit < n_feat:
                count //= 2
                mine = feat % (2 * bit)
                theirs = mine ^ bit
                partner = [(i, i ^ bit) for i in range(n_feat)]
                if held is None:
                    keep = jnp.stack([rows_of(2 * j + mine) for j in range(count)])
                    away = jnp.stack([rows_of(2 * j + theirs) for j in range(count)])
                else:
                    pairs = held.reshape(count, 2, per_out, docs)
                    up = mine // bit
                    keep = lax.dynamic_index_in_dim(pairs, up, 1, keepdims=False)
                    away = lax.dynamic_index_in_dim(pairs, 1 - up, 1, keepdims=False)
                held = keep + send(f"{name}{bit}", away, "feat", partner)
                bit *= 2
            return rows_of(0) if held is None else held[0]

        starts, at = [], 0
        for width in (w_ship, w_first, w_second, w_last):
            starts.append(at)
            at += width
        own = lambda start, width: rolled[:, start : start + width]

        ends = [(0, 1), (n_ex - 1, n_ex - 2)]
        is_end = (ex == 0) | (ex == n_ex - 1)
        a, b = Spread("A_", own(starts[1], w_first)[:half]), Spread("B_", own(starts[2], w_second)[:half])
        chunks = [(starts[1], w_first), (starts[2], w_second)]
        arrived = [[own(s, w)] for s, w in chunks]
        tail = Spread("T_", own(starts[3], w_last))
        shipped = Spread("S_", own(0, w_ship), 1, n_ex - 2) if w_ship else None

        groups = docs // half
        crates, crate_at = {}, 0

        def crate(width):
            nonlocal crate_at
            width //= groups
            piece = train[:, crate_at : crate_at + width].reshape(groups, half, width)
            crate_at += width
            return jnp.concatenate([piece[g] for g in range(groups)], axis=1)

        def uncrate(block):
            return jnp.concatenate(jnp.split(block, groups, axis=1), axis=0)

        cargo = {}
        if w_ship:
            cargo = {(2, 0): crate(w_first), (3, 0): crate(w_first), (2, 1): crate(w_second)}
        landed = {}
        for t in range(1, n_ex):
            for k, spread in enumerate((a, b)):
                landed[t, k] = spread.hop(t, cargo.get((t, k)))
                arrived[k].extend(swap(f"Y{t}{spread.name}", spread.take(t)))
            if t == 2 and shipped:
                for u in range(1, n_ex):
                    shipped.hop(u)
        if shipped:
            tail.hop(1)
        sums = jnp.zeros((n_ex * queries, docs), jnp.float32)
        if shipped:
            rows = jnp.concatenate([own(0, w_ship)] + [shipped.take(t) for t in range(1, n_ex)])
            away = jnp.concatenate([uncrate(landed[key]) for key in cargo], axis=1)
            sums = jnp.where(is_end, 0.0, times(rows, train[:, :w_ship], 0))
            far = sum_over_feat("F", times(rows, away, 0))
            back = send("G", far, "ex", [(d, s) for s, d in ends])
        for t in range(2 if shipped else 1, n_ex):
            tail.hop(t)
        for (s, w), rows in zip(chunks, arrived):
            sums += times(jnp.concatenate(rows), train[:, s : s + w], s)
        rows = jnp.concatenate([own(starts[3], w_last)] + [tail.take(t) for t in range(1, n_ex)])
        sums += times(rows, train[:, starts[3] :], starts[3])
        out = sum_over_feat("E", sums)
        if shipped:
            out += back
        return out.T

    return jax.shard_map(
        on_device,
        mesh=mesh,
        in_specs=(P(("grp", "ex"), "feat"), P("ex", "feat"), P("feat")),
        out_specs=P(("grp", "ex"), "feat"),
        check_vma=False,
    )
```

time: 198 us -> 139 us (0.70)
  waiting for transfers between devices: 171 us -> 38.8 us
  starting transfers between devices: 0.04 us -> 52.5 us
  local copies, waits for them, and re-layouts: 0 us -> 30.5 us
  between operations: 13.4 us -> 0.75 us
  other arithmetic: 4.19 us -> 10.9 us
  matrix products: 8.85 us -> 3.64 us
    all_gather x1 -> x0, waiting for transfers between devices: 152 us -> none  [on_device(): lax.all_gather(precond, 'ex', axis=0, tiled=True)]
    ppermute x0 -> x29, starting transfers between devices: none -> 52.5 us  [send(): done[name] = lax.ppermute(block, axis, pairs)]
    ppermute x0 -> x29, waiting for transfers between devices: none -> 38.8 us  [send(): done[name] = lax.ppermute(block, axis, pairs)]
    unnamed x0 -> x55, local copies, waits for them, and re-layouts: none -> 24.4 us
    reduce_scatter x1 -> x0, waiting for transfers between devices: 18.4 us -> none  [on_device(): lax.psum_scatter(partial_sums, 'feat', scatter_dimension=1, tiled=True)]
    unnamed x0 -> x6, other arithmetic: none -> 7.52 us
    dot_general x1 -> x5, matrix products: 8.85 us -> 3.64 us  [times(): lax.dot_general(precond, docs_part, CONTRACT, preferred_element_type=jnp....]
    convert_element_type x1 -> x0, other arithmetic: 3.34 us -> none  [on_device(): (test_grads.astype(jnp.float32) * inverse[None, :]).astype(jnp.bfloat16)]
  transfers between devices with their start and end apart: 2 -> 29, of which waited for: 2 -> 10; matrix products, arithmetic and copies ran while one was open for 0% -> 28% of each run, Pallas kernels for 0% -> 0%
where the time goes in v3:
time: 139 us; the launch traced here: 137 us
  starting transfers between devices  52.5 us (38%)
  waiting for transfers between devices  38.8 us (28%)
  local copies, waits for them, and re-layouts  30.5 us (22%)
  other arithmetic  10.9 us (8%)
  matrix products  3.64 us (3%)
    ppermute x29, starting transfers between devices, send(): done[name] = lax.ppermute(block, axis, pairs)  52.5 us
    ppermute x29, waiting for transfers between devices, send(): done[name] = lax.ppermute(block, axis, pairs)  38.8 us
    unnamed x55, local copies, waits for them, and re-layouts  24.4 us
    unnamed x6, other arithmetic  7.52 us
    dot_general x5, matrix products, times(): lax.dot_general(precond, docs_part, CONTRACT, preferred_element_type=jnp....  3.64 us
    concatenate x2, local copies, waits for them, and re-layouts, crate(): return jnp.concatenate([piece[g] for g in range(groups)], axis=1)  2.91 us
  transfers between devices with their start and end apart: 29, of which 10 were waited for; matrix products, arithmetic and copies ran while one was open for 28% of the time, Pallas kernels for 0%

profile of v3, /device:TPU:0, one launch (start us, length us, event | category | flops | bytes accessed | tf_op | source)
XLA Modules:
  0.0 137.2 jit_solution(14926396418066067689)
XLA Ops:
  0.0 2.3 %fusion.4 = bf16[64,16384]{1,0:T(8,128)(2,1)S(1)} fusion(s32[]{:T(128)S(6)} %select_n.404, bf16[64,16384]{1,0:T(8,128)(2,1)} %param.4), kind=kLoop, calls=%fused_computation.9 | loop fusion | flops 4194304 | bytes 4194308 | tf_op jit(solution)/shard_map/concatenate | solution.py:51
  4.5 5.6 %collective-permute-start.3 = (bf16[32,8192]{1,0:T(8,128)(2,1)}, bf16[32,8192]{1,0:T(8,128)(2,1)S(1)}, u32[]{:S(2)}, u32[]{:S(2)}) collective-permute-start(bf16[32,8192]{1,0:T(8,128)(2,1)} %slice.212), channel_id=1, source_target_pairs={{0,4},{4,8},{8,12},{1,5},{5,9},{9,13},{2,6},{6,10},{10,14},{3,7},{... | collective-permute-start | bytes 1572872 | tf_op jit(solution)/shard_map/ppermute | solution.py:66
  12.1 5.3 %collective-permute-start.1 = (bf16[32,4096]{1,0:T(8,128)(2,1)}, bf16[32,4096]{1,0:T(8,128)(2,1)}, u32[]{:S(2)}, u32[]{:S(2)}) collective-permute-start(bf16[32,4096]{1,0:T(8,128)(2,1)} %slice.211), channel_id=1, source_target_pairs={{0,4},{4,8},{8,12},{1,5},{5,9},{9,13},{2,6},{6,10},{10,14},{3,7},{... | collective-permute-start | bytes 786440 | tf_op jit(solution)/shard_map/ppermute | solution.py:66
  19.3 1.6 %constant_dynamic-update-slice_fusion.15 = (bf16[32,8192]{1,0:T(8,128)(2,1)}, bf16[32,8192]{1,0:T(8,128)(2,1)}) fusion(bf16[256,16384]{1,0:T(8,128)(2,1)} %param.3), kind=kLoop, calls=%fused_computation.77 | loop fusion | bytes 262144
  26.4 1.4 %constant_dynamic-update-slice_fusion.3 = bf16[32,4096]{1,0:T(8,128)(2,1)} fusion(bf16[32,4096]{1,0:T(8,128)(2,1)} %constant_dynamic-update-slice_fusion.4, bf16[256,16384]{1,0:T(8,128)(2,1)} %param.3), kind=kLoop, calls=%fused_computation.65 | loop fusion | bytes 65536
  30.5 1.5 %constant_dynamic-update-slice_fusion.14 = (bf16[32,8192]{1,0:T(8,128)(2,1)}, bf16[32,8192]{1,0:T(8,128)(2,1)}) fusion(bf16[32,8192]{1,0:T(8,128)(2,1)} %get-tuple-element.63, bf16[256,16384]{1,0:T(8,128)(2,1)} %param.3, bf16[32,8192]{1,0:T(8,128)(2,1)} %get-tuple-element.64), kind=kLoop, calls=%fused_computation.76 | loop fusion | bytes 262144
  32.0 1.5 %constant_dynamic-update-slice_fusion.13 = (bf16[32,8192]{1,0:T(8,128)(2,1)}, bf16[32,8192]{1,0:T(8,128)(2,1)}) fusion(bf16[32,8192]{1,0:T(8,128)(2,1)} %get-tuple-element.61, bf16[256,16384]{1,0:T(8,128)(2,1)} %param.3, bf16[32,8192]{1,0:T(8,128)(2,1)} %get-tuple-element.62), kind=kLoop, calls=%fused_computation.75 | loop fusion | bytes 262144
  33.6 1.6 %constant_dynamic-update-slice_fusion.12 = (bf16[32,8192]{1,0:T(8,128)(2,1)}, bf16[32,8192]{1,0:T(8,128)(2,1)}) fusion(bf16[32,8192]{1,0:T(8,128)(2,1)} %get-tuple-element.59, bf16[256,16384]{1,0:T(8,128)(2,1)} %param.3, bf16[32,8192]{1,0:T(8,128)(2,1)} %get-tuple-element.60), kind=kLoop, calls=%fused_computation.74 | loop fusion | bytes 262144
  35.1 1.6 %constant_dynamic-update-slice_fusion.11 = (bf16[32,8192]{1,0:T(8,128)(2,1)}, bf16[32,8192]{1,0:T(8,128)(2,1)}) fusion(bf16[32,8192]{1,0:T(8,128)(2,1)} %get-tuple-element.57, bf16[256,16384]{1,0:T(8,128)(2,1)} %param.3, bf16[32,8192]{1,0:T(8,128)(2,1)} %get-tuple-element.58), kind=kLoop, calls=%fused_computation.73 | loop fusion | bytes 262144
  36.7 1.6 %constant_dynamic-update-slice_fusion.10 = (bf16[32,8192]{1,0:T(8,128)(2,1)}, bf16[32,8192]{1,0:T(8,128)(2,1)}) fusion(bf16[32,8192]{1,0:T(8,128)(2,1)} %get-tuple-element.55, bf16[256,16384]{1,0:T(8,128)(2,1)} %param.3, bf16[32,8192]{1,0:T(8,128)(2,1)} %get-tuple-element.56), kind=kLoop, calls=%fused_computation.72 | loop fusion | bytes 262144
  38.3 1.4 %constant_dynamic-update-slice_fusion = bf16[32,4096]{1,0:T(8,128)(2,1)} fusion(bf16[32,4096]{1,0:T(8,128)(2,1)} %constant_dynamic-update-slice_fusion.1, bf16[256,16384]{1,0:T(8,128)(2,1)} %param.3), kind=kLoop, calls=%fused_computation.62 | loop fusion | bytes 65536 | tf_op jit(solution)/shard_map/concatenate | solution.py:182
  41.1 1.7 %constant_dynamic-update-slice_fusion.9 = (bf16[32,8192]{1,0:T(8,128)(2,1)}, bf16[32,8192]{1,0:T(8,128)(2,1)}) fusion(bf16[32,8192]{1,0:T(8,128)(2,1)} %get-tuple-element.53, bf16[256,16384]{1,0:T(8,128)(2,1)} %param.3, bf16[32,8192]{1,0:T(8,128)(2,1)} %get-tuple-element.54), kind=kLoop, calls=%fused_computation.71 | loop fusion | bytes 262144
  42.8 1.5 %constant_dynamic-update-slice_fusion.8 = (bf16[32,8192]{1,0:T(8,128)(2,1)}, bf16[32,8192]{1,0:T(8,128)(2,1)}) fusion(bf16[32,8192]{1,0:T(8,128)(2,1)} %get-tuple-element.51, bf16[256,16384]{1,0:T(8,128)(2,1)} %param.3, bf16[32,8192]{1,0:T(8,128)(2,1)} %get-tuple-element.52), kind=kLoop, calls=%fused_computation.70 | loop fusion | bytes 262144 | tf_op jit(solution)/shard_map/concatenate | solution.py:182
  44.4 2.1 %constant_dynamic-update-slice_fusion.29 = (bf16[256,8192]{1,0:T(8,128)(2,1)}, bf16[32,8192]{1,0:T(8,128)(2,1)S(1)}, bf16[32,8192]{1,0:T(8,128)(2,1)S(1)}, bf16[32,8192]{1,0:T(8,128)(2,1)S(1)}) fusion(bf16[256,8192]{1,0:T(8,128)(2,1)} %slice_dynamic-update-slice_fusion, bf16[32,8192]{1,0:T(8,128)(2,1)S(1)} %collective-permute-done.2, ...), kind=kLoop, calls=%fused_computation.91 | loop fusion | flops 786432 | bytes 3670019
  46.5 1.9 %collective-permute-start.4 = (bf16[32,8192]{1,0:T(8,128)(2,1)S(1)}, bf16[32,8192]{1,0:T(8,128)(2,1)S(1)}, u32[]{:S(2)}, u32[]{:S(2)}) collective-permute-start(bf16[32,8192]{1,0:T(8,128)(2,1)S(1)} %get-tuple-element.42), channel_id=1, source_target_pairs={{0,16},{16,0},{1,17},{17,1},{2,18},{18,2},{3,19},{19,3},{4,20},{20... | collective-permute-start | bytes 1572872 | tf_op jit(solution)/shard_map/ppermute | solution.py:66
  50.9 4.6 %collective-permute-start.12 = (bf16[32,8192]{1,0:T(8,128)(2,1)S(1)}, bf16[32,8192]{1,0:T(8,128)(2,1)S(1)}, u32[]{:S(2)}, u32[]{:S(2)}) collective-permute-start(bf16[32,8192]{1,0:T(8,128)(2,1)S(1)} %get-tuple-element.74), channel_id=1, source_target_pairs={{4,8},{8,12},{0,4},{5,9},{9,13},{1,5},{6,10},{10,14},{2,6},{7,11},... | collective-permute-start | bytes 1572872 | tf_op jit(solution)/shard_map/ppermute | solution.py:66
  55.5 3.8 %collective-permute-done.4 = bf16[32,8192]{1,0:T(8,128)(2,1)S(1)} collective-permute-done((bf16[32,8192]{1,0:T(8,128)(2,1)S(1)}, bf16[32,8192]{1,0:T(8,128)(2,1)S(1)}, u32[]{:S(2)}, u32[]{:S(2)}) %collective-permute-start.4) | collective-permute-done | bytes 524320 | tf_op jit(solution)/shard_map/ppermute | solution.py:66
  60.2 3.6 %collective-permute-done.11 = bf16[32,8192]{1,0:T(8,128)(2,1)S(1)} collective-permute-done((bf16[32,8192]{1,0:T(8,128)(2,1)S(1)}, bf16[32,8192]{1,0:T(8,128)(2,1)S(1)}, u32[]{:S(2)}, u32[]{:S(2)}) %collective-permute-start.11) | collective-permute-done | bytes 524320 | tf_op jit(solution)/shard_map/ppermute | solution.py:66
  64.9 2.2 %constant_dynamic-update-slice_fusion.27 = (bf16[256,8192]{1,0:T(8,128)(2,1)}, bf16[32,8192]{1,0:T(8,128)(2,1)S(1)}, bf16[32,8192]{1,0:T(8,128)(2,1)S(1)}, bf16[32,8192]{1,0:T(8,128)(2,1)S(1)}) fusion(bf16[256,8192]{1,0:T(8,128)(2,1)} %constant_dynamic-update-slice_fusion.28, bf16[32,8192]{1,0:T(8,128)(2,1)S(1)} %collective-permute-done.11, ...), kind=kLoop, calls=%fused_computation.89 | loop fusion | flops 1048576 | bytes 3670019
  67.5 1.4 %collective-permute-start.14 = (bf16[32,8192]{1,0:T(8,128)(2,1)S(1)}, bf16[32,8192]{1,0:T(8,128)(2,1)S(1)}, u32[]{:S(2)}, u32[]{:S(2)}) collective-permute-start(bf16[32,8192]{1,0:T(8,128)(2,1)S(1)} %get-tuple-element.28), channel_id=1, source_target_pairs={{4,0},{12,8},{8,12},{0,4},{5,1},{13,9},{9,13},{1,5},{6,2},{14,10},... | collective-permute-start | bytes 1572872 | tf_op jit(solution)/shard_map/ppermute | solution.py:66
  68.9 1.6 %collective-permute-start.5 = (bf16[32,4096]{1,0:T(8,128)(2,1)S(1)}, bf16[32,4096]{1,0:T(8,128)(2,1)S(1)}, u32[]{:S(2)}, u32[]{:S(2)}) collective-permute-start(bf16[32,4096]{1,0:T(8,128)(2,1)S(1)} %get-tuple-element.21), channel_id=1, source_target_pairs={{0,16},{16,0},{1,17},{17,1},{2,18},{18,2},{3,19},{19,3},{4,20},{20... | collective-permute-start | bytes 786440 | tf_op jit(solution)/shard_map/ppermute | solution.py:66
  70.5 2.5 %collective-permute-start.8 = (bf16[32,4096]{1,0:T(8,128)(2,1)S(1)}, bf16[32,4096]{1,0:T(8,128)(2,1)S(1)}, u32[]{:S(2)}, u32[]{:S(2)}) collective-permute-start(bf16[32,4096]{1,0:T(8,128)(2,1)S(1)} %get-tuple-element.24), channel_id=1, source_target_pairs={{4,8},{8,12},{0,4},{5,9},{9,13},{1,5},{6,10},{10,14},{2,6},{7,11},... | collective-permute-start | bytes 786440 | tf_op jit(solution)/shard_map/ppermute | solution.py:66
  74.5 9.6 %collective-permute-done.5 = bf16[32,4096]{1,0:T(8,128)(2,1)S(1)} collective-permute-done((bf16[32,4096]{1,0:T(8,128)(2,1)S(1)}, bf16[32,4096]{1,0:T(8,128)(2,1)S(1)}, u32[]{:S(2)}, u32[]{:S(2)}) %collective-permute-start.5) | collective-permute-done | bytes 262176 | tf_op jit(solution)/shard_map/ppermute | solution.py:66
  84.3 1.4 %collective-permute-start.16 = (bf16[32,4096]{1,0:T(8,128)(2,1)S(1)}, bf16[32,4096]{1,0:T(8,128)(2,1)S(1)}, u32[]{:S(2)}, u32[]{:S(2)}) collective-permute-start(bf16[32,4096]{1,0:T(8,128)(2,1)S(1)} %get-tuple-element.29), channel_id=1, source_target_pairs={{0,16},{16,0},{1,17},{17,1},{2,18},{18,2},{3,19},{19,3},{4,20},{20... | collective-permute-start | bytes 786440 | tf_op jit(solution)/shard_map/ppermute | solution.py:66
  85.7 3.3 %collective-permute-start.9 = (bf16[64,2560]{1,0:T(8,128)(2,1)S(1)}, bf16[64,2560]{1,0:T(8,128)(2,1)S(1)}, u32[]{:S(2)}, u32[]{:S(2)}) collective-permute-start(bf16[64,2560]{1,0:T(8,128)(2,1)S(1)} %copy-done), channel_id=1, source_target_pairs={{0,4},{4,8},{1,5},{5,9},{2,6},{6,10},{3,7},{7,11},{16,20},{20,24},... | collective-permute-start | bytes 983048 | tf_op jit(solution)/shard_map/ppermute | solution.py:66
  93.9 4.8 %collective-permute-start.20 = (bf16[64,1536]{1,0:T(8,128)(2,1)S(1)}, bf16[64,1536]{1,0:T(8,128)(2,1)S(1)}, u32[]{:S(2)}, u32[]{:S(2)}) collective-permute-start(bf16[64,1536]{1,0:T(8,128)(2,1)S(1)} %copy-done.2), channel_id=1, source_target_pairs={{0,4},{4,8},{8,12},{1,5},{5,9},{9,13},{2,6},{6,10},{10,14},{3,7},{... | collective-permute-start | bytes 589832 | tf_op jit(solution)/shard_map/ppermute | solution.py:66
  104.0 4.3 %collective-permute-done.18 = bf16[32,4096]{1,0:T(8,128)(2,1)S(1)} collective-permute-done((bf16[32,4096]{1,0:T(8,128)(2,1)S(1)}, bf16[32,4096]{1,0:T(8,128)(2,1)S(1)}, u32[]{:S(2)}, u32[]{:S(2)}) %collective-permute-start.18) | collective-permute-done | bytes 262176 | tf_op jit(solution)/shard_map/ppermute | solution.py:66
  111.4 2.1 %collective-permute-start.24 = (f32[1,64,256]{2,1,0:T(8,128)S(1)}, f32[1,64,256]{2,1,0:T(8,128)S(1)}, u32[]{:S(2)}, u32[]{:S(2)}) collective-permute-start(f32[1,64,256]{2,1,0:T(8,128)S(1)} %constant_dynamic-slice_fusion.1), channel_id=1, source_target_pairs={{0,2},{1,3},{2,0},{3,1},{4,6},{5,7},{6,4},{7,5},{8,10},{9,11},{10,... | collective-permute-start | bytes 196616 | tf_op jit(solution)/shard_map/ppermute | solution.py:66
  114.8 7.1 %collective-permute-done.22 = bf16[64,1536]{1,0:T(8,128)(2,1)S(1)} collective-permute-done((bf16[64,1536]{1,0:T(8,128)(2,1)S(1)}, bf16[64,1536]{1,0:T(8,128)(2,1)S(1)}, u32[]{:S(2)}, u32[]{:S(2)}) %collective-permute-start.22) | collective-permute-done | bytes 196640 | tf_op jit(solution)/shard_map/ppermute | solution.py:66
  124.6 4.9 %collective-permute-done.25 = bf16[64,1536]{1,0:T(8,128)(2,1)S(1)} collective-permute-done((bf16[64,1536]{1,0:T(8,128)(2,1)S(1)}, bf16[64,1536]{1,0:T(8,128)(2,1)S(1)}, u32[]{:S(2)}, u32[]{:S(2)}) %collective-permute-start.25) | collective-permute-done | bytes 196640 | tf_op jit(solution)/shard_map/ppermute | solution.py:66
  132.2 1.6 %collective-permute-start.28 = (f32[1,64,256]{2,1,0:T(8,128)S(1)}, f32[1,64,256]{2,1,0:T(8,128)S(1)}, u32[]{:S(2)}, u32[]{:S(2)}) collective-permute-start(f32[1,64,256]{2,1,0:T(8,128)S(1)} %constant_dynamic-slice_fusion), channel_id=1, source_target_pairs={{0,2},{1,3},{2,0},{3,1},{4,6},{5,7},{6,4},{7,5},{8,10},{9,11},{10,... | collective-permute-start | bytes 196616 | tf_op jit(solution)/shard_map/ppermute | solution.py:66
  133.8 2.8 %collective-permute-done.28 = f32[1,64,256]{2,1,0:T(8,128)S(1)} collective-permute-done((f32[1,64,256]{2,1,0:T(8,128)S(1)}, f32[1,64,256]{2,1,0:T(8,128)S(1)}, u32[]{:S(2)}, u32[]{:S(2)}) %collective-permute-start.28) | collective-permute-done | bytes 65568 | tf_op jit(solution)/shard_map/ppermute | solution.py:66
  (129 shorter events, 42.2 us)
Async XLA Ops:
  2.3 19.9 %copy-start.4 = (f32[16384]{0:T(1024)S(1)}, f32[16384]{0:T(1024)}, u32[]{:S(2)}) copy-start(f32[16384]{0:T(1024)} %param.5) | copy-start | bytes 196612
  3.2 41.2 %collective-permute-start.2 = (bf16[32,8192]{1,0:T(8,128)(2,1)}, bf16[32,8192]{1,0:T(8,128)(2,1)S(1)}, u32[]{:S(2)}, u32[]{:S(2)}) collective-permute-start(bf16[32,8192]{1,0:T(8,128)(2,1)} %slice.212), channel_id=1, source_target_pairs={{4,0},{8,4},{12,8},{5,1},{9,5},{13,9},{6,2},{10,6},{14,10},{7,3},{... | collective-permute-start | bytes 1572872 | tf_op jit(solution)/shard_map/ppermute | solution.py:66
  4.5 39.9 %collective-permute-start.3 = (bf16[32,8192]{1,0:T(8,128)(2,1)}, bf16[32,8192]{1,0:T(8,128)(2,1)S(1)}, u32[]{:S(2)}, u32[]{:S(2)}) collective-permute-start(bf16[32,8192]{1,0:T(8,128)(2,1)} %slice.212), channel_id=1, source_target_pairs={{0,4},{4,8},{8,12},{1,5},{5,9},{9,13},{2,6},{6,10},{10,14},{3,7},{... | collective-permute-start | bytes 1572872 | tf_op jit(solution)/shard_map/ppermute | solution.py:66
  10.8 37.6 %collective-permute-start = (bf16[32,4096]{1,0:T(8,128)(2,1)}, bf16[32,4096]{1,0:T(8,128)(2,1)S(1)}, u32[]{:S(2)}, u32[]{:S(2)}) collective-permute-start(bf16[32,4096]{1,0:T(8,128)(2,1)} %slice.211), channel_id=1, source_target_pairs={{4,0},{8,4},{12,8},{5,1},{9,5},{13,9},{6,2},{10,6},{14,10},{7,3},{... | collective-permute-start | bytes 786440 | tf_op jit(solution)/shard_map/ppermute | solution.py:66
  12.1 36.3 %collective-permute-start.1 = (bf16[32,4096]{1,0:T(8,128)(2,1)}, bf16[32,4096]{1,0:T(8,128)(2,1)}, u32[]{:S(2)}, u32[]{:S(2)}) collective-permute-start(bf16[32,4096]{1,0:T(8,128)(2,1)} %slice.211), channel_id=1, source_target_pairs={{0,4},{4,8},{8,12},{1,5},{5,9},{9,13},{2,6},{6,10},{10,14},{3,7},{... | collective-permute-start | bytes 786440 | tf_op jit(solution)/shard_map/ppermute | solution.py:66
  46.5 12.8 %collective-permute-start.4 = (bf16[32,8192]{1,0:T(8,128)(2,1)S(1)}, bf16[32,8192]{1,0:T(8,128)(2,1)S(1)}, u32[]{:S(2)}, u32[]{:S(2)}) collective-permute-start(bf16[32,8192]{1,0:T(8,128)(2,1)S(1)} %get-tuple-element.42), channel_id=1, source_target_pairs={{0,16},{16,0},{1,17},{17,1},{2,18},{18,2},{3,19},{19,3},{4,20},{20... | collective-permute-start | bytes 1572872 | tf_op jit(solution)/shard_map/ppermute | solution.py:66
  49.6 14.2 %collective-permute-start.11 = (bf16[32,8192]{1,0:T(8,128)(2,1)S(1)}, bf16[32,8192]{1,0:T(8,128)(2,1)S(1)}, u32[]{:S(2)}, u32[]{:S(2)}) collective-permute-start(bf16[32,8192]{1,0:T(8,128)(2,1)S(1)} %get-tuple-element.75), channel_id=1, source_target_pairs={{4,0},{8,4},{12,8},{5,1},{9,5},{13,9},{6,2},{10,6},{14,10},{7,3},{... | collective-permute-start | bytes 1572872 | tf_op jit(solution)/shard_map/ppermute | solution.py:66
  50.9 14.0 %collective-permute-start.12 = (bf16[32,8192]{1,0:T(8,128)(2,1)S(1)}, bf16[32,8192]{1,0:T(8,128)(2,1)S(1)}, u32[]{:S(2)}, u32[]{:S(2)}) collective-permute-start(bf16[32,8192]{1,0:T(8,128)(2,1)S(1)} %get-tuple-element.74), channel_id=1, source_target_pairs={{4,8},{8,12},{0,4},{5,9},{9,13},{1,5},{6,10},{10,14},{2,6},{7,11},... | collective-permute-start | bytes 1572872 | tf_op jit(solution)/shard_map/ppermute | solution.py:66
  64.9 20.8 %copy-start = (bf16[64,2560]{1,0:T(8,128)(2,1)S(1)}, bf16[64,2560]{1,0:T(8,128)(2,1)}, u32[]{:S(2)}) copy-start(bf16[64,2560]{1,0:T(8,128)(2,1)} %slice.210) | copy-start | bytes 983044
  67.1 22.7 %collective-permute-start.13 = (bf16[32,8192]{1,0:T(8,128)(2,1)S(1)}, bf16[32,8192]{1,0:T(8,128)(2,1)S(1)}, u32[]{:S(2)}, u32[]{:S(2)}) collective-permute-start(bf16[32,8192]{1,0:T(8,128)(2,1)S(1)} %get-tuple-element.27), channel_id=1, source_target_pairs={{0,16},{16,0},{1,17},{17,1},{2,18},{18,2},{3,19},{19,3},{4,20},{20... | collective-permute-start | bytes 1572872 | tf_op jit(solution)/shard_map/ppermute | solution.py:66
  67.5 23.2 %collective-permute-start.14 = (bf16[32,8192]{1,0:T(8,128)(2,1)S(1)}, bf16[32,8192]{1,0:T(8,128)(2,1)S(1)}, u32[]{:S(2)}, u32[]{:S(2)}) collective-permute-start(bf16[32,8192]{1,0:T(8,128)(2,1)S(1)} %get-tuple-element.28), channel_id=1, source_target_pairs={{4,0},{12,8},{8,12},{0,4},{5,1},{13,9},{9,13},{1,5},{6,2},{14,10},... | collective-permute-start | bytes 1572872 | tf_op jit(solution)/shard_map/ppermute | solution.py:66
  68.9 15.2 %collective-permute-start.5 = (bf16[32,4096]{1,0:T(8,128)(2,1)S(1)}, bf16[32,4096]{1,0:T(8,128)(2,1)S(1)}, u32[]{:S(2)}, u32[]{:S(2)}) collective-permute-start(bf16[32,4096]{1,0:T(8,128)(2,1)S(1)} %get-tuple-element.21), channel_id=1, source_target_pairs={{0,16},{16,0},{1,17},{17,1},{2,18},{18,2},{3,19},{19,3},{4,20},{20... | collective-permute-start | bytes 786440 | tf_op jit(solution)/shard_map/ppermute | solution.py:66
  70.5 13.6 %collective-permute-start.8 = (bf16[32,4096]{1,0:T(8,128)(2,1)S(1)}, bf16[32,4096]{1,0:T(8,128)(2,1)S(1)}, u32[]{:S(2)}, u32[]{:S(2)}) collective-permute-start(bf16[32,4096]{1,0:T(8,128)(2,1)S(1)} %get-tuple-element.24), channel_id=1, source_target_pairs={{4,8},{8,12},{0,4},{5,9},{9,13},{1,5},{6,10},{10,14},{2,6},{7,11},... | collective-permute-start | bytes 786440 | tf_op jit(solution)/shard_map/ppermute | solution.py:66
  73.1 11.1 %collective-permute-start.7 = (bf16[32,4096]{1,0:T(8,128)(2,1)S(1)}, bf16[32,4096]{1,0:T(8,128)(2,1)S(1)}, u32[]{:S(2)}, u32[]{:S(2)}) collective-permute-start(bf16[32,4096]{1,0:T(8,128)(2,1)S(1)} %get-tuple-element.23), channel_id=1, source_target_pairs={{4,0},{8,4},{12,8},{5,1},{9,5},{13,9},{6,2},{10,6},{14,10},{7,3},{... | collective-permute-start | bytes 786440 | tf_op jit(solution)/shard_map/ppermute | solution.py:66
  84.3 9.5 %collective-permute-start.16 = (bf16[32,4096]{1,0:T(8,128)(2,1)S(1)}, bf16[32,4096]{1,0:T(8,128)(2,1)S(1)}, u32[]{:S(2)}, u32[]{:S(2)}) collective-permute-start(bf16[32,4096]{1,0:T(8,128)(2,1)S(1)} %get-tuple-element.29), channel_id=1, source_target_pairs={{0,16},{16,0},{1,17},{17,1},{2,18},{18,2},{3,19},{19,3},{4,20},{20... | collective-permute-start | bytes 786440 | tf_op jit(solution)/shard_map/ppermute | solution.py:66
  85.7 13.0 %collective-permute-start.9 = (bf16[64,2560]{1,0:T(8,128)(2,1)S(1)}, bf16[64,2560]{1,0:T(8,128)(2,1)S(1)}, u32[]{:S(2)}, u32[]{:S(2)}) collective-permute-start(bf16[64,2560]{1,0:T(8,128)(2,1)S(1)} %copy-done), channel_id=1, source_target_pairs={{0,4},{4,8},{1,5},{5,9},{2,6},{6,10},{3,7},{7,11},{16,20},{20,24},... | collective-permute-start | bytes 983048 | tf_op jit(solution)/shard_map/ppermute | solution.py:66
  89.1 9.7 %collective-permute-start.6 = (bf16[64,2560]{1,0:T(8,128)(2,1)S(1)}, bf16[64,2560]{1,0:T(8,128)(2,1)S(1)}, u32[]{:S(2)}, u32[]{:S(2)}) collective-permute-start(bf16[64,2560]{1,0:T(8,128)(2,1)S(1)} %copy-done), channel_id=1, source_target_pairs={{8,4},{12,8},{9,5},{13,9},{10,6},{14,10},{11,7},{15,11},{24,20},{2... | collective-permute-start | bytes 983048 | tf_op jit(solution)/shard_map/ppermute | solution.py:66
  91.7 21.8 %collective-permute-start.15 = (bf16[32,8192]{1,0:T(8,128)(2,1)S(1)}, bf16[32,8192]{1,0:T(8,128)(2,1)S(1)}, u32[]{:S(2)}, u32[]{:S(2)}) collective-permute-start(bf16[32,8192]{1,0:T(8,128)(2,1)S(1)} %get-tuple-element.38), channel_id=1, source_target_pairs={{0,16},{16,0},{1,17},{17,1},{2,18},{18,2},{3,19},{19,3},{4,20},{20... | collective-permute-start | bytes 1572872 | tf_op jit(solution)/shard_map/ppermute | solution.py:66
  92.4 8.4 %collective-permute-start.17 = (bf16[32,4096]{1,0:T(8,128)(2,1)S(1)}, bf16[32,4096]{1,0:T(8,128)(2,1)S(1)}, u32[]{:S(2)}, u32[]{:S(2)}) collective-permute-start(bf16[32,4096]{1,0:T(8,128)(2,1)S(1)} %get-tuple-element.30), channel_id=1, source_target_pairs={{4,0},{8,12},{5,1},{9,13},{6,2},{10,14},{7,3},{11,15},{20,16},{24,... | collective-permute-start | bytes 786440 | tf_op jit(solution)/shard_map/ppermute | solution.py:66
  93.8 14.6 %slice-start = ((s8[8388608]{0:T(1024)(128)(4,1)}), s8[4194304]{0:T(1024)(128)(4,1)S(1)}, s32[]{:S(2)}) async-start(s8[8388608]{0:T(1024)(128)(4,1)} %bitcast.60), calls=%async_computation | async-start | bytes 8388608
  93.9 15.3 %collective-permute-start.20 = (bf16[64,1536]{1,0:T(8,128)(2,1)S(1)}, bf16[64,1536]{1,0:T(8,128)(2,1)S(1)}, u32[]{:S(2)}, u32[]{:S(2)}) collective-permute-start(bf16[64,1536]{1,0:T(8,128)(2,1)S(1)} %copy-done.2), channel_id=1, source_target_pairs={{0,4},{4,8},{8,12},{1,5},{5,9},{9,13},{2,6},{6,10},{10,14},{3,7},{... | collective-permute-start | bytes 589832 | tf_op jit(solution)/shard_map/ppermute | solution.py:66
  98.8 4.4 %collective-permute-start.10 = (bf16[64,2560]{1,0:T(8,128)(2,1)S(1)}, bf16[64,2560]{1,0:T(8,128)(2,1)S(1)}, u32[]{:S(2)}, u32[]{:S(2)}) collective-permute-start(bf16[64,2560]{1,0:T(8,128)(2,1)S(1)} %get-tuple-element.26), channel_id=1, source_target_pairs={{8,4},{4,8},{9,5},{5,9},{10,6},{6,10},{11,7},{7,11},{24,20},{20,24... | collective-permute-start | bytes 983048 | tf_op jit(solution)/shard_map/ppermute | solution.py:66
  99.5 10.5 %collective-permute-start.19 = (bf16[64,1536]{1,0:T(8,128)(2,1)S(1)}, bf16[64,1536]{1,0:T(8,128)(2,1)S(1)}, u32[]{:S(2)}, u32[]{:S(2)}) collective-permute-start(bf16[64,1536]{1,0:T(8,128)(2,1)S(1)} %copy-done.2), channel_id=1, source_target_pairs={{4,0},{8,4},{12,8},{5,1},{9,5},{13,9},{6,2},{10,6},{14,10},{7,3},{... | collective-permute-start | bytes 589832 | tf_op jit(solution)/shard_map/ppermute | solution.py:66
  101.9 6.4 %collective-permute-start.18 = (bf16[32,4096]{1,0:T(8,128)(2,1)S(1)}, bf16[32,4096]{1,0:T(8,128)(2,1)S(1)}, u32[]{:S(2)}, u32[]{:S(2)}) collective-permute-start(bf16[32,4096]{1,0:T(8,128)(2,1)S(1)} %get-tuple-element.44), channel_id=1, source_target_pairs={{0,16},{16,0},{1,17},{17,1},{2,18},{18,2},{3,19},{19,3},{4,20},{20... | collective-permute-start | bytes 786440 | tf_op jit(solution)/shard_map/ppermute | solution.py:66
  103.9 5.3 %collective-permute-start.21 = (f32[2,64,256]{2,1,0:T(8,128)S(1)}, f32[2,64,256]{2,1,0:T(8,128)S(1)}, u32[]{:S(2)}, u32[]{:S(2)}) collective-permute-start(f32[2,64,256]{2,1,0:T(8,128)S(1)} %pad_maximum_fusion), channel_id=1, source_target_pairs={{0,1},{1,0},{2,3},{3,2},{4,5},{5,4},{6,7},{7,6},{8,9},{9,8},{10,11... | collective-permute-start | bytes 393224 | tf_op jit(solution)/shard_map/ppermute | solution.py:66
  109.2 5.6 %collective-permute-start.23 = (bf16[64,1536]{1,0:T(8,128)(2,1)S(1)}, bf16[64,1536]{1,0:T(8,128)(2,1)S(1)}, u32[]{:S(2)}, u32[]{:S(2)}) collective-permute-start(bf16[64,1536]{1,0:T(8,128)(2,1)S(1)} %collective-permute-done.20), channel_id=1, source_target_pairs={{4,8},{8,12},{5,9},{9,13},{6,10},{10,14},{7,11},{11,15},{20,24},{2... | collective-permute-start | bytes 589832 | tf_op jit(solution)/shard_map/ppermute | solution.py:66
  110.0 11.9 %collective-permute-start.22 = (bf16[64,1536]{1,0:T(8,128)(2,1)S(1)}, bf16[64,1536]{1,0:T(8,128)(2,1)S(1)}, u32[]{:S(2)}, u32[]{:S(2)}) collective-permute-start(bf16[64,1536]{1,0:T(8,128)(2,1)S(1)} %collective-permute-done.19), channel_id=1, source_target_pairs={{4,0},{8,4},{5,1},{9,5},{6,2},{10,6},{7,3},{11,7},{20,16},{24,20},... | collective-permute-start | bytes 589832 | tf_op jit(solution)/shard_map/ppermute | solution.py:66
  111.4 10.6 %collective-permute-start.24 = (f32[1,64,256]{2,1,0:T(8,128)S(1)}, f32[1,64,256]{2,1,0:T(8,128)S(1)}, u32[]{:S(2)}, u32[]{:S(2)}) collective-permute-start(f32[1,64,256]{2,1,0:T(8,128)S(1)} %constant_dynamic-slice_fusion.1), channel_id=1, source_target_pairs={{0,2},{1,3},{2,0},{3,1},{4,6},{5,7},{6,4},{7,5},{8,10},{9,11},{10,... | collective-permute-start | bytes 196616 | tf_op jit(solution)/shard_map/ppermute | solution.py:66
  122.0 7.6 %collective-permute-start.25 = (bf16[64,1536]{1,0:T(8,128)(2,1)S(1)}, bf16[64,1536]{1,0:T(8,128)(2,1)S(1)}, u32[]{:S(2)}, u32[]{:S(2)}) collective-permute-start(bf16[64,1536]{1,0:T(8,128)(2,1)S(1)} %get-tuple-element.35), channel_id=1, source_target_pairs={{4,0},{8,12},{5,1},{9,13},{6,2},{10,14},{7,3},{11,15},{20,16},{24,... | collective-permute-start | bytes 589832 | tf_op jit(solution)/shard_map/ppermute | solution.py:66
  123.3 7.4 %collective-permute-start.26 = (f32[64,256]{1,0:T(8,128)S(1)}, f32[64,256]{1,0:T(8,128)S(1)}, u32[]{:S(2)}, u32[]{:S(2)}) collective-permute-start(f32[64,256]{1,0:T(8,128)S(1)} %add_bitcast_fusion), channel_id=1, source_target_pairs={{4,0},{8,12},{5,1},{9,13},{6,2},{10,14},{7,3},{11,15},{20,16},{24,... | collective-permute-start | bytes 196616 | tf_op jit(solution)/shard_map/ppermute | solution.py:66
  130.8 1.4 %collective-permute-start.27 = (f32[2,64,256]{2,1,0:T(8,128)S(1)}, f32[2,64,256]{2,1,0:T(8,128)S(1)}, u32[]{:S(2)}, u32[]{:S(2)}) collective-permute-start(f32[2,64,256]{2,1,0:T(8,128)S(1)} %pad_maximum_fusion.1), channel_id=1, source_target_pairs={{0,1},{1,0},{2,3},{3,2},{4,5},{5,4},{6,7},{7,6},{8,9},{9,8},{10,11... | collective-permute-start | bytes 393224 | tf_op jit(solution)/shard_map/ppermute | solution.py:66
  132.2 4.3 %collective-permute-start.28 = (f32[1,64,256]{2,1,0:T(8,128)S(1)}, f32[1,64,256]{2,1,0:T(8,128)S(1)}, u32[]{:S(2)}, u32[]{:S(2)}) collective-permute-start(f32[1,64,256]{2,1,0:T(8,128)S(1)} %constant_dynamic-slice_fusion), channel_id=1, source_target_pairs={{0,2},{1,3},{2,0},{3,1},{4,6},{5,7},{6,4},{7,5},{8,10},{9,11},{10,... | collective-permute-start | bytes 196616 | tf_op jit(solution)/shard_map/ppermute | solution.py:66
  (4 other events, 21.6 us)

commit v4 on v0

v4 whole, which is shorter than its diff:
```python
import functools

import jax
import jax.numpy as jnp
import numpy as np
from jax import lax
from jax.experimental import pallas as pl
from jax.experimental.pallas import tpu as pltpu
from jax.sharding import PartitionSpec as P

CONTRACT = (((1,), (1,)), ((), ()))
LANES = 128

GATES = {
    "E1S": ("Y1A",),
    "O1S": ("Y1A",),
    "Y1B": ("Y1A",),
    "E3A": ("E2A",),
    "Y2A": ("O2A",),
    "E2B": ("Y1B",),
    "O2B": ("O1S",),
    "O2S": ("Y2A",),
    "Y3A": ("Y2A",),
    "E1T": ("Y2A", "E3A"),
    "O1T": ("O2S",),
    "F1": ("Y3A",),
    "Y3B": ("Y2B",),
    "O2T": ("F1",),
    "E3T": ("F2", "Y2B"),
    "Z1": ("G",),
}


def plan(feats, n_ex):
    if n_ex == 4:
        first, second = feats // 2, feats // 4
        ship = (2 * first + second) // 8
    else:
        first, second, ship = feats // 2, feats * 3 // 8, 0
    return first, second, ship, feats - first - second - ship


def arrival(n_ex):
    if n_ex == 4:
        return [[0, 1, 2, 3], [1, 0, 2, 3], [2, 3, 1, 0], [3, 2, 1, 0]]
    return [[(i - t) % n_ex for t in range(n_ex)] for i in range(n_ex)]


def scores_kernel(n_rows, has_base, offsets, *refs):
    rows, (scale, train) = refs[:n_rows], refs[n_rows : n_rows + 2]
    base = refs[n_rows + 2] if has_base else None
    out, total = refs[-2:]
    step = pl.program_id(0)
    block = jnp.concatenate([r[...] for r in rows], axis=0)
    precond = (block.astype(jnp.float32) * scale[...]).astype(jnp.bfloat16)
    part = lax.dot_general(precond, train[...], CONTRACT, preferred_element_type=jnp.float32)

    @pl.when(step == 0)
    def _():
        total[...] = part

    @pl.when(step > 0)
    def _():
        total[...] += part

    @pl.when(step == pl.num_programs(0) - 1)
    def _():
        count = offsets.shape[0]
        size = out.shape[0] // count
        for i in range(count):
            at = pl.multiple_of(offsets[i], size)
            value = total[pl.ds(at, size), :]
            if has_base:
                value += base[i * size : (i + 1) * size, :]
            out[i * size : (i + 1) * size, :] = value


def scores(offsets, test, received, scale, train, start, width, train_start, base=None):
    docs = train.shape[0]
    tile = next(t for t in (1024, 512, 256, 128) if all(v % t == 0 for v in (start, width, train_start)))
    lead, at = start // tile, train_start // tile
    in_specs = [pl.BlockSpec((test.shape[0], tile), lambda k, _: (0, lead + k))]
    in_specs += [pl.BlockSpec((r.shape[0], tile), lambda k, _: (0, k)) for r in received]
    in_specs += [
        pl.BlockSpec((1, tile), lambda k, _: (0, lead + k)),
        pl.BlockSpec((docs, tile), lambda k, _: (0, at + k)),
    ]
    operands = [test, *received, scale, train]
    queries = test.shape[0] + sum(r.shape[0] for r in received)
    if base is not None:
        in_specs.append(pl.BlockSpec((queries, docs), lambda k, _: (0, 0)))
        operands.append(base)
    return pl.pallas_call(
        functools.partial(scores_kernel, 1 + len(received), base is not None),
        out_shape=jax.ShapeDtypeStruct((queries, docs), jnp.float32),
        grid_spec=pltpu.PrefetchScalarGridSpec(
            num_scalar_prefetch=1,
            grid=(width // tile,),
            in_specs=in_specs,
            out_specs=pl.BlockSpec((queries, docs), lambda k, _: (0, 0)),
            scratch_shapes=[pltpu.VMEM((queries, docs), jnp.float32)],
        ),
        cost_estimate=pl.CostEstimate(
            flops=2 * queries * docs * width,
            bytes_accessed=2 * (queries + docs) * width,
            transcendentals=0,
        ),
        compiler_params=pltpu.CompilerParams(vmem_limit_bytes=12 * 1024 * 1024),
    )(offsets, *operands)


def solution(mesh):
    n_grp, n_ex, n_feat = (mesh.shape[a] for a in ("grp", "ex", "feat"))
    assert n_grp <= 2

    def on_device(train, test, hess):
        docs, feats = train.shape
        queries = test.shape[0]
        half = queries // n_grp
        grp, ex, feat = (lax.axis_index(a) for a in ("grp", "ex", "feat"))
        is_end = (ex == 0) | (ex == n_ex - 1)
        scale = (1.0 / (hess + jnp.float32(0.1))).reshape(1, feats)

        whole, halved = [], []
        for i, owners in enumerate(arrival(n_ex)):
            for g in range(n_grp):
                whole.append([])
                halved.append([])
                for b in range(n_ex):
                    t = owners.index(b)
                    for h in range(n_grp):
                        whole[-1].append(t * queries + h * half)
                        halved[-1].append(t * queries + ((h - g) % n_grp if t else h) * half)
        row = ex * n_grp + grp
        whole, halved = (
            lax.dynamic_index_in_dim(jnp.asarray(np.array(v, np.int32)), row, 0, keepdims=False)
            for v in (whole, halved)
        )

        done = {}

        def send(name, block, axis, pairs):
            waits = [done[g] for g in GATES.get(name, ()) if g in done]
            if waits:
                block = lax.optimization_barrier((block, waits))[0]
            done[name] = lax.ppermute(block, axis, pairs)
            return done[name]

        def links(parity, toward):
            pairs = []
            for i in range(parity, n_ex - 1, 2):
                pairs += [(s, d) for s, d in ((i, i + 1), (i + 1, i)) if d in toward]
            return pairs

        everyone, inner, outer = range(n_ex), range(1, n_ex - 1), (0, n_ex - 1)

        class Line:
            def __init__(self, name, block, cargo=(None, None), shipping=False):
                self.name, self.block, self.cargo, self.shipping = name, block, cargo, shipping

            def outer(self, t):
                block = self.block if t == 1 else done[f"O{t - 1}{self.name}"]
                toward = everyone if t == 1 else outer
                if self.shipping:
                    toward = inner
                elif t > 1 and self.cargo[t - 2] is not None:
                    block = jnp.where(is_end, self.cargo[t - 2], block)
                    toward = everyone
                return send(f"E{t}{self.name}", block, "ex", links(0, toward))

            def middle(self, t):
                block = self.block if t == 1 else done[f"E{t - 1}{self.name}"]
                return send(f"O{t}{self.name}", block, "ex", links(1, inner))

            def take(self, t):
                if t == 1:
                    return done[f"E1{self.name}"]
                if self.shipping:
                    return done[f"O{t - 1}{self.name}"]
                return jnp.where(is_end, done[f"E{t}{self.name}"], done[f"O{t - 1}{self.name}"])

        def swap(name, block):
            if n_grp == 1:
                return [block]
            return [block, send(name, block, "grp", [(0, 1), (1, 0)])]

        def sum_over_feat(name, sums):
            held = sums.reshape(n_feat, -1, docs)
            bit = 1
            while bit < n_feat:
                pairs = held.reshape((-1, 2) + held.shape[1:])
                mine = (feat // bit) % 2
                keep = lax.dynamic_index_in_dim(pairs, mine, 1, keepdims=False)
                away = lax.dynamic_index_in_dim(pairs, 1 - mine, 1, keepdims=False)
                partner = [(i, i ^ bit) for i in range(n_feat)]
                held = keep + send(f"{name}{bit}", away, "feat", partner)
                bit *= 2
            return held[0]

        w_first, w_second, w_ship, w_last = plan(feats, n_ex)
        at_first, at_second, at_ship, at_last = np.cumsum([0, w_first, w_second, w_ship]).tolist()

        def part(start, width):
            if n_grp == 1:
                return test[:, start : start + width]
            return lax.dynamic_slice(test, (grp * half, start), (half, width))

        times = functools.partial(scores, test=test, scale=scale)
        halves = [("A", at_first, w_first), ("B", at_second, w_second)]
        got = {name: [] for name in "ABST"}
        base = None

        if n_ex == 4:
            ends = [(0, 1), (n_ex - 1, n_ex - 2)]
            groups = docs // half

            def crate(start, width):
                piece = train[:, start : start + width].reshape(groups, half, width)
                return jnp.moveaxis(piece, 0, 1).reshape(half, groups * width)

            def uncrate(block):
                return jnp.concatenate(jnp.split(block, groups, axis=1), axis=0)

            wide, narrow = w_first // groups, w_second // groups
            a = Line("A", part(at_first, w_first), (crate(at_ship, wide), crate(at_ship + wide, wide)))
            b = Line("B", part(at_second, w_second), (crate(at_ship + 2 * wide, narrow), None))
            s = Line("S", test[:, at_ship : at_ship + w_ship], shipping=True)
            tail = Line("T", test[:, at_last:])

            def swapped(line, t):
                got[line.name] += swap(f"Y{t}{line.name}", line.take(t))

            a.outer(1), a.middle(1), b.outer(1), b.middle(1)
            swapped(a, 1)
            a.outer(2), a.middle(2), s.outer(1), s.middle(1)
            swapped(b, 1), swapped(a, 2)
            a.outer(3), b.outer(2), b.middle(2), s.middle(2)
            swapped(a, 3)
            tail.outer(1), b.outer(3)
            swapped(b, 2)
            got["S"] = [s.take(t) for t in range(1, n_ex)]
            away = jnp.concatenate([uncrate(done[k]) for k in ("E2A", "E3A", "E2B")], axis=1)
            far = times(whole, received=got["S"], train=away, start=at_ship, width=w_ship, train_start=0)
            far = sum_over_feat("F", far)
            tail.middle(1), tail.outer(2), tail.middle(2)
            swapped(b, 3)
            back = send("G", far, "ex", [(d, s) for s, d in ends])
            tail.outer(3)
            got["T"] = [tail.take(t) for t in range(1, n_ex)]
            near = times(
                whole, received=got["S"], train=train, start=at_ship, width=w_ship, train_start=at_ship
            )
            base = jnp.where(is_end, 0.0, near)
        else:
            ring = [(i, (i + 1) % n_ex) for i in range(n_ex)]
            held = {"A": part(at_first, w_first), "B": part(at_second, w_second), "T": test[:, at_last:]}
            for t in range(1, n_ex):
                for name in held:
                    held[name] = send(f"R{t}{name}", held[name], "ex", ring)
                    got[name] += [held[name]] if name == "T" else swap(f"Y{t}{name}", held[name])

        for name, start, width in halves:
            base = times(
                halved, received=got[name], train=train, start=start, width=width, train_start=start,
                base=base,
            )
        total = times(
            whole, received=got["T"], train=train, start=at_last, width=w_last, train_start=at_last,
            base=base,
        )
        out = sum_over_feat("Z", total)
        if n_ex == 4:
            out += back
        return out.T

    return jax.shard_map(
        on_device,
        mesh=mesh,
        in_specs=(P(("grp", "ex"), "feat"), P("ex", "feat"), P("feat")),
        out_specs=P(("grp", "ex"), "feat"),
        check_vma=False,
    )
```

time: 198 us -> 133 us (0.67)
  waiting for transfers between devices: 171 us -> 46 us
  starting transfers between devices: 0.04 us -> 53.2 us
  local copies, waits for them, and re-layouts: 0 us -> 16.2 us
  Pallas kernels: 0 us -> 13.2 us
  between operations: 13.4 us -> 0.64 us
  matrix products: 8.85 us -> 0 us
    all_gather x1 -> x0, waiting for transfers between devices: 152 us -> none  [on_device(): lax.all_gather(precond, 'ex', axis=0, tiled=True)]
    ppermute x0 -> x29, starting transfers between devices: none -> 53.2 us  [send(): done[name] = lax.ppermute(block, axis, pairs)]
    ppermute x0 -> x29, waiting for transfers between devices: none -> 46 us  [send(): done[name] = lax.ppermute(block, axis, pairs)]
    reduce_scatter x1 -> x0, waiting for transfers between devices: 18.4 us -> none  [on_device(): lax.psum_scatter(partial_sums, 'feat', scatter_dimension=1, tiled=True)]
    pallas_call x0 -> x5, Pallas kernels: none -> 13.2 us  [scores(): pl.pallas_call(functools.partial(scores_kernel, 1 + len(received), base i...]
    dot_general x1 -> x0, matrix products: 8.85 us -> none  [on_device(): lax.dot_general(train_grads, lax.all_gather(precond, 'ex', axis=0, tiled=...]
    unnamed x0 -> x36, local copies, waits for them, and re-layouts: none -> 7.3 us
    dynamic_slice x0 -> x2, local copies, waits for them, and re-layouts: none -> 3.71 us  [part(): return lax.dynamic_slice(test, (grp * half, start), (half, width))]
  transfers between devices with their start and end apart: 2 -> 29, of which waited for: 2 -> 8; matrix products, arithmetic and copies ran while one was open for 0% -> 10% of each run, Pallas kernels for 0% -> 10%
where the time goes in v4:
time: 133 us; the launch traced here: 132 us
  starting transfers between devices  53.2 us (40%)
  waiting for transfers between devices  46 us (35%)
  local copies, waits for them, and re-layouts  16.2 us (12%)
  Pallas kernels  13.2 us (10%)
  other arithmetic  3.08 us (2%)
    ppermute x29, starting transfers between devices, send(): done[name] = lax.ppermute(block, axis, pairs)  53.2 us
    ppermute x29, waiting for transfers between devices, send(): done[name] = lax.ppermute(block, axis, pairs)  46 us
    pallas_call x5, Pallas kernels, scores(): pl.pallas_call(functools.partial(scores_kernel, 1 + len(received), base i...  13.2 us
    unnamed x36, local copies, waits for them, and re-layouts  7.3 us
    dynamic_slice x2, local copies, waits for them, and re-layouts, part(): return lax.dynamic_slice(test, (grp * half, start), (half, width))  3.71 us
  transfers between devices with their start and end apart: 29, of which 8 were waited for; matrix products, arithmetic and copies ran while one was open for 10% of the time, Pallas kernels for 10%

profile of v4, /device:TPU:0, one launch (start us, length us, event | category | flops | bytes accessed | tf_op | source)
XLA Modules:
  0.0 132.4 jit_solution(7030301821549416418)
XLA Ops:
  0.0 2.0 %constant_dynamic-slice_fusion.3 = bf16[32,8192]{1,0:T(8,128)(2,1)} fusion(bf16[64,16384]{1,0:T(8,128)(2,1)} %refs_0_.9, s32[]{:T(128)S(6)} %select_n.107), kind=kLoop, calls=%fused_computation.46 | loop fusion | bytes 1048580 | tf_op jit(solution)/shard_map/dynamic_slice | solution.py:206
  2.0 1.4 %collective-permute-start = (bf16[32,8192]{1,0:T(8,128)(2,1)}, bf16[32,8192]{1,0:T(8,128)(2,1)}, u32[]{:S(2)}, u32[]{:S(2)}) collective-permute-start(bf16[32,8192]{1,0:T(8,128)(2,1)} %constant_dynamic-slice_fusion.3), channel_id=1, source_target_pairs={{4,8},{8,4},{5,9},{9,5},{6,10},{10,6},{7,11},{11,7},{20,24},{24,20... | collective-permute-start | bytes 1572872 | tf_op jit(solution)/shard_map/ppermute | solution.py:146
  3.5 5.1 %collective-permute-start.2 = (bf16[32,8192]{1,0:T(8,128)(2,1)}, bf16[32,8192]{1,0:T(8,128)(2,1)S(1)}, u32[]{:S(2)}, u32[]{:S(2)}) collective-permute-start(bf16[32,8192]{1,0:T(8,128)(2,1)} %constant_dynamic-slice_fusion.3), channel_id=1, source_target_pairs={{0,4},{4,0},{8,12},{12,8},{1,5},{5,1},{9,13},{13,9},{2,6},{6,2},{1... | collective-permute-start | bytes 1572872 | tf_op jit(solution)/shard_map/ppermute | solution.py:146
  8.6 1.7 %constant_dynamic-slice_fusion.5 = bf16[32,4096]{1,0:T(8,128)(2,1)} fusion(bf16[64,16384]{1,0:T(8,128)(2,1)} %refs_0_.9, s32[]{:T(128)S(6)} %select_n.107), kind=kLoop, calls=%fused_computation.50 | loop fusion | bytes 524292 | tf_op jit(solution)/shard_map/dynamic_slice | solution.py:206
  10.3 1.4 %collective-permute-start.13 = (bf16[32,4096]{1,0:T(8,128)(2,1)}, bf16[32,4096]{1,0:T(8,128)(2,1)}, u32[]{:S(2)}, u32[]{:S(2)}) collective-permute-start(bf16[32,4096]{1,0:T(8,128)(2,1)} %constant_dynamic-slice_fusion.5), channel_id=1, source_target_pairs={{4,8},{8,4},{5,9},{9,5},{6,10},{10,6},{7,11},{11,7},{20,24},{24,20... | collective-permute-start | bytes 786440 | tf_op jit(solution)/shard_map/ppermute | solution.py:146
  12.5 2.2 %fusion.3 = (bf16[256,1024]{1,0:T(8,128)(2,1)}, bf16[256,1024]{1,0:T(8,128)(2,1)}) fusion(bf16[256,16384]{1,0:T(8,128)(2,1)} %refs_5_.3), kind=kLoop, calls=%fused_computation.51 | loop fusion | bytes 2097152 | tf_op jit(solution)/shard_map/slice | solution.py:218
  16.2 1.9 %copy.9 = bf16[4,8,8,1024]{3,1,2,0:T(8,128)(2,1)} copy(bf16[4,8,8,1024]{3,1,0,2:T(8,128)(2,1)} %bitcast.56) | data formatting | bytes 1048576
  18.1 1.9 %copy.10 = bf16[4,8,8,1024]{3,1,2,0:T(8,128)(2,1)} copy(bf16[4,8,8,1024]{3,1,0,2:T(8,128)(2,1)} %bitcast.55) | data formatting | bytes 1048576
  22.3 1.6 %collective-permute-start.7 = (bf16[32,8192]{1,0:T(8,128)(2,1)S(1)}, bf16[32,8192]{1,0:T(8,128)(2,1)S(1)}, u32[]{:S(2)}, u32[]{:S(2)}) collective-permute-start(bf16[32,8192]{1,0:T(8,128)(2,1)S(1)} %collective-permute-done.2.refs_1_), channel_id=1, source_target_pairs={{0,16},{16,0},{1,17},{17,1},{2,18},{18,2},{3,19},{19,3},{4,20},{20... | collective-permute-start | bytes 1572872 | tf_op jit(solution)/shard_map/ppermute | solution.py:146
  25.0 8.8 %collective-permute-start.1 = (bf16[32,8192]{1,0:T(8,128)(2,1)S(1)}, bf16[32,8192]{1,0:T(8,128)(2,1)S(1)}, u32[]{:S(2)}, u32[]{:S(2)}) collective-permute-start(bf16[32,8192]{1,0:T(8,128)(2,1)S(1)} %broadcast_select_fusion.3), channel_id=1, source_target_pairs={{0,4},{4,0},{8,12},{12,8},{1,5},{5,1},{9,13},{13,9},{2,6},{6,2},{1... | collective-permute-start | bytes 1572872 | tf_op jit(solution)/shard_map/ppermute | solution.py:146
  33.8 1.6 %collective-permute-done.7.refs_2_ = bf16[32,8192]{1,0:T(8,128)(2,1)S(1)} collective-permute-done((bf16[32,8192]{1,0:T(8,128)(2,1)S(1)}, bf16[32,8192]{1,0:T(8,128)(2,1)S(1)}, u32[]{:S(2)}, u32[]{:S(2)}) %collective-permute-start.7) | collective-permute-done | bytes 524320 | tf_op jit(solution)/shard_map/ppermute | solution.py:146
  35.4 10.1 %collective-permute-start.8 = (bf16[64,2560]{1,0:T(8,128)(2,1)}, bf16[64,2560]{1,0:T(8,128)(2,1)S(1)}, u32[]{:S(2)}, u32[]{:S(2)}) collective-permute-start(bf16[64,2560]{1,0:T(8,128)(2,1)} %slice.18), channel_id=1, source_target_pairs={{0,4},{12,8},{1,5},{13,9},{2,6},{14,10},{3,7},{15,11},{16,20},{28,... | collective-permute-start | bytes 983048 | tf_op jit(solution)/shard_map/ppermute | solution.py:146
  47.5 1.6 %collective-permute-start.4 = (bf16[32,8192]{1,0:T(8,128)(2,1)S(1)}, bf16[32,8192]{1,0:T(8,128)(2,1)S(1)}, u32[]{:S(2)}, u32[]{:S(2)}) collective-permute-start(bf16[32,8192]{1,0:T(8,128)(2,1)S(1)} %broadcast_select_fusion.2.refs_3_), channel_id=1, source_target_pairs={{0,16},{16,0},{1,17},{17,1},{2,18},{18,2},{3,19},{19,3},{4,20},{20... | collective-permute-start | bytes 1572872 | tf_op jit(solution)/shard_map/ppermute | solution.py:146
  49.7 14.5 %collective-permute-done.15.refs_2_ = bf16[32,4096]{1,0:T(8,128)(2,1)S(1)} collective-permute-done((bf16[32,4096]{1,0:T(8,128)(2,1)S(1)}, bf16[32,4096]{1,0:T(8,128)(2,1)S(1)}, u32[]{:S(2)}, u32[]{:S(2)}) %collective-permute-start.15) | collective-permute-done | bytes 262176 | tf_op jit(solution)/shard_map/ppermute | solution.py:146
  64.2 2.0 %collective-permute-start.16 = (bf16[32,4096]{1,0:T(8,128)(2,1)S(1)}, bf16[32,4096]{1,0:T(8,128)(2,1)S(1)}, u32[]{:S(2)}, u32[]{:S(2)}) collective-permute-start(bf16[32,4096]{1,0:T(8,128)(2,1)S(1)} %broadcast_select_fusion.6), channel_id=1, source_target_pairs={{0,4},{4,0},{8,12},{12,8},{1,5},{5,1},{9,13},{13,9},{2,6},{6,2},{1... | collective-permute-start | bytes 786440 | tf_op jit(solution)/shard_map/ppermute | solution.py:146
  67.0 1.6 %collective-permute-start.17 = (bf16[32,8192]{1,0:T(8,128)(2,1)S(1)}, bf16[32,8192]{1,0:T(8,128)(2,1)S(1)}, u32[]{:S(2)}, u32[]{:S(2)}) collective-permute-start(bf16[32,8192]{1,0:T(8,128)(2,1)S(1)} %broadcast_select_fusion.refs_5_), channel_id=1, source_target_pairs={{0,16},{16,0},{1,17},{17,1},{2,18},{18,2},{3,19},{19,3},{4,20},{20... | collective-permute-start | bytes 1572872 | tf_op jit(solution)/shard_map/ppermute | solution.py:146
  69.3 4.6 %collective-permute-start.6 = (bf16[64,1536]{1,0:T(8,128)(2,1)S(1)}, bf16[64,1536]{1,0:T(8,128)(2,1)S(1)}, u32[]{:S(2)}, u32[]{:S(2)}) collective-permute-start(bf16[64,1536]{1,0:T(8,128)(2,1)S(1)} %copy-done.3), channel_id=1, source_target_pairs={{0,4},{4,0},{8,12},{12,8},{1,5},{5,1},{9,13},{13,9},{2,6},{6,2},{1... | collective-permute-start | bytes 589832 | tf_op jit(solution)/shard_map/ppermute | solution.py:146
  74.6 1.3 collective-permute-start.24
  76.0 6.9 %collective-permute-done.24 = bf16[32,4096]{1,0:T(8,128)(2,1)S(1)} collective-permute-done((bf16[32,4096]{1,0:T(8,128)(2,1)S(1)}, bf16[32,4096]{1,0:T(8,128)(2,1)S(1)}, u32[]{:S(2)}, u32[]{:S(2)}) %collective-permute-start.24) | collective-permute-done | bytes 262176 | tf_op jit(solution)/shard_map/ppermute | solution.py:146
  83.4 1.3 collective-permute-start.25
  85.4 3.4 %copy-done = bf16[256,16384]{1,0:T(8,128)(2,1)S(1)} copy-done((bf16[256,16384]{1,0:T(8,128)(2,1)S(1)}, bf16[256,16384]{1,0:T(8,128)(2,1)}, u32[]{:S(2)}) %copy-start) | copy-done | bytes 8388632
  88.8 2.3 %shard_map.56 = f32[256,256]{1,0:T(8,128)S(1)} custom-call(s32[8]{0:T(128)S(1)} %fusion.1.offsets, bf16[64,16384]{1,0:T(8,128)(2,1)S(1)} %copy-done.1, bf16[64,2560]{1,0:T(8,128)(2,1)S(1)} %collective-permute-done.8.refs_1_, bf16[64,2560]{1,0:T(8,128)(2,1)S(1)} %collective-permute-done.12.refs_2_, bf16[64,2560]{1,0:T(8,128)(2,1)S(1)} %collective-permute-done.9.refs_3_, ...), custom_call_target="tpu_custom_call" | custom-call | flops 335544320 | bytes 2621440 | tf_op jit(solution)/shard_map/pallas_call | solution.py:93
  91.1 2.3 %shard_map.55 = f32[256,256]{1,0:T(8,128)S(1)} custom-call(s32[8]{0:T(128)S(1)} %fusion.1.offsets, bf16[64,16384]{1,0:T(8,128)(2,1)S(1)} %copy-done.1, bf16[64,2560]{1,0:T(8,128)(2,1)S(1)} %collective-permute-done.8.refs_1_, bf16[64,2560]{1,0:T(8,128)(2,1)S(1)} %collective-permute-done.12.refs_2_, bf16[64,2560]{1,0:T(8,128)(2,1)S(1)} %collective-permute-done.9.refs_3_, ...), custom_call_target="tpu_custom_call" | custom-call | flops 335544320 | bytes 2621440 | tf_op jit(solution)/shard_map/pallas_call | solution.py:93
  93.6 1.3 collective-permute-start.11
  95.0 1.6 %collective-permute-start.20 = (f32[1,64,256]{2,1,0:T(8,128)S(1)}, f32[1,64,256]{2,1,0:T(8,128)S(1)}, u32[]{:S(2)}, u32[]{:S(2)}) collective-permute-start(f32[1,64,256]{2,1,0:T(8,128)S(1)} %constant_dynamic-slice_fusion.2), channel_id=1, source_target_pairs={{0,2},{1,3},{2,0},{3,1},{4,6},{5,7},{6,4},{7,5},{8,10},{9,11},{10,... | collective-permute-start | bytes 196616 | tf_op jit(solution)/shard_map/ppermute | solution.py:146
  96.6 4.4 %shard_map.57.refs_9_ = f32[256,256]{1,0:T(8,128)S(1)} custom-call(s32[8]{0:T(128)S(1)} %fusion.2.offsets, bf16[64,16384]{1,0:T(8,128)(2,1)S(1)} %copy-done.1, bf16[32,8192]{1,0:T(8,128)(2,1)S(1)} %collective-permute-done.2.refs_1_, bf16[32,8192]{1,0:T(8,128)(2,1)S(1)} %collective-permute-done.7.refs_2_, ...), custom_call_target="tpu_custom_call" | custom-call | flops 1073741824 | bytes 8388608 | tf_op jit(solution)/shard_map/pallas_call | solution.py:93
  101.0 2.5 %shard_map.58.refs_6_ = f32[256,256]{1,0:T(8,128)S(1)} custom-call(s32[8]{0:T(128)S(1)} %fusion.2.offsets, bf16[64,16384]{1,0:T(8,128)(2,1)S(1)} %copy-done.1, bf16[32,4096]{1,0:T(8,128)(2,1)S(1)} %collective-permute-done.14.refs_1_, bf16[32,4096]{1,0:T(8,128)(2,1)S(1)} %collective-permute-done.15.refs_2_, ...), custom_call_target="tpu_custom_call" | custom-call | flops 536870912 | bytes 4194304 | tf_op jit(solution)/shard_map/pallas_call | solution.py:93
  104.2 1.3 collective-permute-start.26
  106.9 17.3 %collective-permute-done.22 = bf16[64,1536]{1,0:T(8,128)(2,1)S(1)} collective-permute-done((bf16[64,1536]{1,0:T(8,128)(2,1)S(1)}, bf16[64,1536]{1,0:T(8,128)(2,1)S(1)}, u32[]{:S(2)}, u32[]{:S(2)}) %collective-permute-start.22) | collective-permute-done | bytes 196640 | tf_op jit(solution)/shard_map/ppermute | solution.py:146
  124.2 1.6 %shard_map.59 = f32[256,256]{1,0:T(8,128)S(1)} custom-call(s32[8]{0:T(128)S(1)} %fusion.1.offsets, bf16[64,16384]{1,0:T(8,128)(2,1)S(1)} %copy-done.1, bf16[64,1536]{1,0:T(8,128)(2,1)S(1)} %collective-permute-done.6.refs_1_, bf16[64,1536]{1,0:T(8,128)(2,1)S(1)} %broadcast_select_fusion.8.refs_2_, bf16[64,1536]{1,0:T(8,128)(2,1)S(1)} %broadcast_select_fusion.7.refs_3_, ...), custom_call_target="tpu_custom_call" | custom-call | flops 201326592 | bytes 1572864 | tf_op jit(solution)/shard_map/pallas_call | solution.py:93
  126.0 1.3 %collective-permute-done.27 = f32[2,64,256]{2,1,0:T(8,128)S(1)} collective-permute-done((f32[2,64,256]{2,1,0:T(8,128)S(1)}, f32[2,64,256]{2,1,0:T(8,128)S(1)}, u32[]{:S(2)}, u32[]{:S(2)}) %collective-permute-start.27) | collective-permute-done | bytes 131104 | tf_op jit(solution)/shard_map/ppermute | solution.py:146
  128.0 3.7 %collective-permute-done.28 = f32[1,64,256]{2,1,0:T(8,128)S(1)} collective-permute-done((f32[1,64,256]{2,1,0:T(8,128)S(1)}, f32[1,64,256]{2,1,0:T(8,128)S(1)}, u32[]{:S(2)}, u32[]{:S(2)}) %collective-permute-start.28) | collective-permute-done | bytes 65568 | tf_op jit(solution)/shard_map/ppermute | solution.py:146
  (100 shorter events, 15.0 us)
Async XLA Ops:
  2.0 21.8 %collective-permute-start = (bf16[32,8192]{1,0:T(8,128)(2,1)}, bf16[32,8192]{1,0:T(8,128)(2,1)}, u32[]{:S(2)}, u32[]{:S(2)}) collective-permute-start(bf16[32,8192]{1,0:T(8,128)(2,1)} %constant_dynamic-slice_fusion.3), channel_id=1, source_target_pairs={{4,8},{8,4},{5,9},{9,5},{6,10},{10,6},{7,11},{11,7},{20,24},{24,20... | collective-permute-start | bytes 1572872 | tf_op jit(solution)/shard_map/ppermute | solution.py:146
  3.5 18.1 %collective-permute-start.2 = (bf16[32,8192]{1,0:T(8,128)(2,1)}, bf16[32,8192]{1,0:T(8,128)(2,1)S(1)}, u32[]{:S(2)}, u32[]{:S(2)}) collective-permute-start(bf16[32,8192]{1,0:T(8,128)(2,1)} %constant_dynamic-slice_fusion.3), channel_id=1, source_target_pairs={{0,4},{4,0},{8,12},{12,8},{1,5},{5,1},{9,13},{13,9},{2,6},{6,2},{1... | collective-permute-start | bytes 1572872 | tf_op jit(solution)/shard_map/ppermute | solution.py:146
  10.3 38.8 %collective-permute-start.14 = (bf16[32,4096]{1,0:T(8,128)(2,1)}, bf16[32,4096]{1,0:T(8,128)(2,1)S(1)}, u32[]{:S(2)}, u32[]{:S(2)}) collective-permute-start(bf16[32,4096]{1,0:T(8,128)(2,1)} %constant_dynamic-slice_fusion.5), channel_id=1, source_target_pairs={{0,4},{4,0},{8,12},{12,8},{1,5},{5,1},{9,13},{13,9},{2,6},{6,2},{1... | collective-permute-start | bytes 786440 | tf_op jit(solution)/shard_map/ppermute | solution.py:146
  10.3 11.2 %collective-permute-start.13 = (bf16[32,4096]{1,0:T(8,128)(2,1)}, bf16[32,4096]{1,0:T(8,128)(2,1)}, u32[]{:S(2)}, u32[]{:S(2)}) collective-permute-start(bf16[32,4096]{1,0:T(8,128)(2,1)} %constant_dynamic-slice_fusion.5), channel_id=1, source_target_pairs={{4,8},{8,4},{5,9},{9,5},{6,10},{10,6},{7,11},{11,7},{20,24},{24,20... | collective-permute-start | bytes 786440 | tf_op jit(solution)/shard_map/ppermute | solution.py:146
  20.1 26.2 %copy-start.2 = (bf16[4,8,8,1024]{3,1,2,0:T(8,128)(2,1)S(1)}, bf16[4,8,8,1024]{3,1,2,0:T(8,128)(2,1)}, u32[]{:S(2)}) copy-start(bf16[4,8,8,1024]{3,1,2,0:T(8,128)(2,1)} %copy.10) | copy-start | bytes 1572868
  21.6 24.6 %collective-permute-start.3 = (bf16[32,8192]{1,0:T(8,128)(2,1)S(1)}, bf16[32,8192]{1,0:T(8,128)(2,1)S(1)}, u32[]{:S(2)}, u32[]{:S(2)}) collective-permute-start(bf16[32,8192]{1,0:T(8,128)(2,1)S(1)} %collective-permute-done.2.refs_1_), channel_id=1, source_target_pairs={{4,8},{8,4},{5,9},{9,5},{6,10},{10,6},{7,11},{11,7},{20,24},{24,20... | collective-permute-start | bytes 1572872 | tf_op jit(solution)/shard_map/ppermute | solution.py:146
  22.3 13.1 %collective-permute-start.7 = (bf16[32,8192]{1,0:T(8,128)(2,1)S(1)}, bf16[32,8192]{1,0:T(8,128)(2,1)S(1)}, u32[]{:S(2)}, u32[]{:S(2)}) collective-permute-start(bf16[32,8192]{1,0:T(8,128)(2,1)S(1)} %collective-permute-done.2.refs_1_), channel_id=1, source_target_pairs={{0,16},{16,0},{1,17},{17,1},{2,18},{18,2},{3,19},{19,3},{4,20},{20... | collective-permute-start | bytes 1572872 | tf_op jit(solution)/shard_map/ppermute | solution.py:146
  25.0 21.3 %collective-permute-start.1 = (bf16[32,8192]{1,0:T(8,128)(2,1)S(1)}, bf16[32,8192]{1,0:T(8,128)(2,1)S(1)}, u32[]{:S(2)}, u32[]{:S(2)}) collective-permute-start(bf16[32,8192]{1,0:T(8,128)(2,1)S(1)} %broadcast_select_fusion.3), channel_id=1, source_target_pairs={{0,4},{4,0},{8,12},{12,8},{1,5},{5,1},{9,13},{13,9},{2,6},{6,2},{1... | collective-permute-start | bytes 1572872 | tf_op jit(solution)/shard_map/ppermute | solution.py:146
  35.4 33.1 %collective-permute-start.8 = (bf16[64,2560]{1,0:T(8,128)(2,1)}, bf16[64,2560]{1,0:T(8,128)(2,1)S(1)}, u32[]{:S(2)}, u32[]{:S(2)}) collective-permute-start(bf16[64,2560]{1,0:T(8,128)(2,1)} %slice.18), channel_id=1, source_target_pairs={{0,4},{12,8},{1,5},{13,9},{2,6},{14,10},{3,7},{15,11},{16,20},{28,... | collective-permute-start | bytes 983048 | tf_op jit(solution)/shard_map/ppermute | solution.py:146
  45.5 20.7 %collective-permute-start.12 = (bf16[64,2560]{1,0:T(8,128)(2,1)}, bf16[64,2560]{1,0:T(8,128)(2,1)S(1)}, u32[]{:S(2)}, u32[]{:S(2)}) collective-permute-start(bf16[64,2560]{1,0:T(8,128)(2,1)} %slice.18), channel_id=1, source_target_pairs={{4,8},{8,4},{5,9},{9,5},{6,10},{10,6},{7,11},{11,7},{20,24},{24,20... | collective-permute-start | bytes 983048 | tf_op jit(solution)/shard_map/ppermute | solution.py:146
  46.3 23.0 %copy-start.3 = (bf16[64,1536]{1,0:T(8,128)(2,1)S(1)}, bf16[64,1536]{1,0:T(8,128)(2,1)}, u32[]{:S(2)}) copy-start(bf16[64,1536]{1,0:T(8,128)(2,1)} %slice.15) | copy-start | bytes 589828
  46.3 20.6 %collective-permute-start.5 = (bf16[32,8192]{1,0:T(8,128)(2,1)S(1)}, bf16[32,8192]{1,0:T(8,128)(2,1)S(1)}, u32[]{:S(2)}, u32[]{:S(2)}) collective-permute-start(bf16[32,8192]{1,0:T(8,128)(2,1)S(1)} %broadcast_select_fusion.1), channel_id=1, source_target_pairs={{0,4},{4,0},{8,12},{12,8},{1,5},{5,1},{9,13},{13,9},{2,6},{6,2},{1... | collective-permute-start | bytes 1572872 | tf_op jit(solution)/shard_map/ppermute | solution.py:146
  47.5 19.5 %collective-permute-start.4 = (bf16[32,8192]{1,0:T(8,128)(2,1)S(1)}, bf16[32,8192]{1,0:T(8,128)(2,1)S(1)}, u32[]{:S(2)}, u32[]{:S(2)}) collective-permute-start(bf16[32,8192]{1,0:T(8,128)(2,1)S(1)} %broadcast_select_fusion.2.refs_3_), channel_id=1, source_target_pairs={{0,16},{16,0},{1,17},{17,1},{2,18},{18,2},{3,19},{19,3},{4,20},{20... | collective-permute-start | bytes 1572872 | tf_op jit(solution)/shard_map/ppermute | solution.py:146
  49.1 15.1 %collective-permute-start.15 = (bf16[32,4096]{1,0:T(8,128)(2,1)S(1)}, bf16[32,4096]{1,0:T(8,128)(2,1)S(1)}, u32[]{:S(2)}, u32[]{:S(2)}) collective-permute-start(bf16[32,4096]{1,0:T(8,128)(2,1)S(1)} %collective-permute-done.14.refs_1_), channel_id=1, source_target_pairs={{0,16},{16,0},{1,17},{17,1},{2,18},{18,2},{3,19},{19,3},{4,20},{20... | collective-permute-start | bytes 786440 | tf_op jit(solution)/shard_map/ppermute | solution.py:146
  49.6 46.9 %slice-start = ((s8[8388608]{0:T(1024)(128)(4,1)}), s8[4194304]{0:T(1024)(128)(4,1)S(1)}, s32[]{:S(2)}) async-start(s8[8388608]{0:T(1024)(128)(4,1)} %bitcast.41), calls=%async_computation | async-start | bytes 8388608
  64.2 9.7 %collective-permute-start.16 = (bf16[32,4096]{1,0:T(8,128)(2,1)S(1)}, bf16[32,4096]{1,0:T(8,128)(2,1)S(1)}, u32[]{:S(2)}, u32[]{:S(2)}) collective-permute-start(bf16[32,4096]{1,0:T(8,128)(2,1)S(1)} %broadcast_select_fusion.6), channel_id=1, source_target_pairs={{0,4},{4,0},{8,12},{12,8},{1,5},{5,1},{9,13},{13,9},{2,6},{6,2},{1... | collective-permute-start | bytes 786440 | tf_op jit(solution)/shard_map/ppermute | solution.py:146
  66.2 8.4 %collective-permute-start.23 = (bf16[32,4096]{1,0:T(8,128)(2,1)S(1)}, bf16[32,4096]{1,0:T(8,128)(2,1)S(1)}, u32[]{:S(2)}, u32[]{:S(2)}) collective-permute-start(bf16[32,4096]{1,0:T(8,128)(2,1)S(1)} %collective-permute-done.14.refs_1_), channel_id=1, source_target_pairs={{4,8},{8,4},{5,9},{9,5},{6,10},{10,6},{7,11},{11,7},{20,24},{24,20... | collective-permute-start | bytes 786440 | tf_op jit(solution)/shard_map/ppermute | solution.py:146
  67.0 26.5 %collective-permute-start.17 = (bf16[32,8192]{1,0:T(8,128)(2,1)S(1)}, bf16[32,8192]{1,0:T(8,128)(2,1)S(1)}, u32[]{:S(2)}, u32[]{:S(2)}) collective-permute-start(bf16[32,8192]{1,0:T(8,128)(2,1)S(1)} %broadcast_select_fusion.refs_5_), channel_id=1, source_target_pairs={{0,16},{16,0},{1,17},{17,1},{2,18},{18,2},{3,19},{19,3},{4,20},{20... | collective-permute-start | bytes 1572872 | tf_op jit(solution)/shard_map/ppermute | solution.py:146
  68.6 16.1 %collective-permute-start.9 = (bf16[64,2560]{1,0:T(8,128)(2,1)S(1)}, bf16[64,2560]{1,0:T(8,128)(2,1)S(1)}, u32[]{:S(2)}, u32[]{:S(2)}) collective-permute-start(bf16[64,2560]{1,0:T(8,128)(2,1)S(1)} %collective-permute-done.8.refs_1_), channel_id=1, source_target_pairs={{4,8},{8,4},{5,9},{9,5},{6,10},{10,6},{7,11},{11,7},{20,24},{24,20... | collective-permute-start | bytes 983048 | tf_op jit(solution)/shard_map/ppermute | solution.py:146
  69.3 34.2 %collective-permute-start.6 = (bf16[64,1536]{1,0:T(8,128)(2,1)S(1)}, bf16[64,1536]{1,0:T(8,128)(2,1)S(1)}, u32[]{:S(2)}, u32[]{:S(2)}) collective-permute-start(bf16[64,1536]{1,0:T(8,128)(2,1)S(1)} %copy-done.3), channel_id=1, source_target_pairs={{0,4},{4,0},{8,12},{12,8},{1,5},{5,1},{9,13},{13,9},{2,6},{6,2},{1... | collective-permute-start | bytes 589832 | tf_op jit(solution)/shard_map/ppermute | solution.py:146
  74.0 9.4 %collective-permute-start.21 = (bf16[32,4096]{1,0:T(8,128)(2,1)S(1)}, bf16[32,4096]{1,0:T(8,128)(2,1)S(1)}, u32[]{:S(2)}, u32[]{:S(2)}) collective-permute-start(bf16[32,4096]{1,0:T(8,128)(2,1)S(1)} %broadcast_select_fusion.5.refs_3_), channel_id=1, source_target_pairs={{0,16},{16,0},{1,17},{17,1},{2,18},{18,2},{3,19},{19,3},{4,20},{20... | collective-permute-start | bytes 786440 | tf_op jit(solution)/shard_map/ppermute | solution.py:146
  74.6 8.3 %collective-permute-start.24 = (bf16[32,4096]{1,0:T(8,128)(2,1)S(1)}, bf16[32,4096]{1,0:T(8,128)(2,1)S(1)}, u32[]{:S(2)}, u32[]{:S(2)}) collective-permute-start(bf16[32,4096]{1,0:T(8,128)(2,1)S(1)} %collective-permute-done.23), channel_id=1, source_target_pairs={{4,0},{8,12},{5,1},{9,13},{6,2},{10,14},{7,3},{11,15},{20,16},{24,... | collective-permute-start | bytes 786440 | tf_op jit(solution)/shard_map/ppermute | solution.py:146
  83.4 17.5 %collective-permute-start.25 = (bf16[32,4096]{1,0:T(8,128)(2,1)S(1)}, bf16[32,4096]{1,0:T(8,128)(2,1)S(1)}, u32[]{:S(2)}, u32[]{:S(2)}) collective-permute-start(bf16[32,4096]{1,0:T(8,128)(2,1)S(1)} %broadcast_select_fusion.4.refs_5_), channel_id=1, source_target_pairs={{0,16},{16,0},{1,17},{17,1},{2,18},{18,2},{3,19},{19,3},{4,20},{20... | collective-permute-start | bytes 786440 | tf_op jit(solution)/shard_map/ppermute | solution.py:146
  84.7 8.9 %collective-permute-start.10 = (bf16[64,1536]{1,0:T(8,128)(2,1)S(1)}, bf16[64,1536]{1,0:T(8,128)(2,1)S(1)}, u32[]{:S(2)}, u32[]{:S(2)}) collective-permute-start(bf16[64,1536]{1,0:T(8,128)(2,1)S(1)} %copy-done.3), channel_id=1, source_target_pairs={{4,8},{8,4},{5,9},{9,5},{6,10},{10,6},{7,11},{11,7},{20,24},{24,20... | collective-permute-start | bytes 589832 | tf_op jit(solution)/shard_map/ppermute | solution.py:146
  93.5 1.4 %collective-permute-start.18 = (f32[2,64,256]{2,1,0:T(8,128)S(1)}, f32[2,64,256]{2,1,0:T(8,128)S(1)}, u32[]{:S(2)}, u32[]{:S(2)}) collective-permute-start(f32[2,64,256]{2,1,0:T(8,128)S(1)} %dynamic-slice_bitcast_fusion.1), channel_id=1, source_target_pairs={{0,1},{1,0},{2,3},{3,2},{4,5},{5,4},{6,7},{7,6},{8,9},{9,8},{10,11... | collective-permute-start | bytes 393224 | tf_op jit(solution)/shard_map/ppermute | solution.py:146
  93.6 13.2 %collective-permute-start.11 = (bf16[64,1536]{1,0:T(8,128)(2,1)S(1)}, bf16[64,1536]{1,0:T(8,128)(2,1)S(1)}, u32[]{:S(2)}, u32[]{:S(2)}) collective-permute-start(bf16[64,1536]{1,0:T(8,128)(2,1)S(1)} %collective-permute-done.10), channel_id=1, source_target_pairs={{4,0},{8,12},{5,1},{9,13},{6,2},{10,14},{7,3},{11,15},{20,16},{24,... | collective-permute-start | bytes 589832 | tf_op jit(solution)/shard_map/ppermute | solution.py:146
  95.0 9.2 %collective-permute-start.20 = (f32[1,64,256]{2,1,0:T(8,128)S(1)}, f32[1,64,256]{2,1,0:T(8,128)S(1)}, u32[]{:S(2)}, u32[]{:S(2)}) collective-permute-start(f32[1,64,256]{2,1,0:T(8,128)S(1)} %constant_dynamic-slice_fusion.2), channel_id=1, source_target_pairs={{0,2},{1,3},{2,0},{3,1},{4,6},{5,7},{6,4},{7,5},{8,10},{9,11},{10,... | collective-permute-start | bytes 196616 | tf_op jit(solution)/shard_map/ppermute | solution.py:146
  103.5 2.0 %collective-permute-start.19 = (bf16[64,1536]{1,0:T(8,128)(2,1)S(1)}, bf16[64,1536]{1,0:T(8,128)(2,1)S(1)}, u32[]{:S(2)}, u32[]{:S(2)}) collective-permute-start(bf16[64,1536]{1,0:T(8,128)(2,1)S(1)} %collective-permute-done.6.refs_1_), channel_id=1, source_target_pairs={{4,8},{8,4},{5,9},{9,5},{6,10},{10,6},{7,11},{11,7},{20,24},{24,20... | collective-permute-start | bytes 589832 | tf_op jit(solution)/shard_map/ppermute | solution.py:146
  104.2 21.7 %collective-permute-start.26 = (f32[64,256]{1,0:T(8,128)S(1)}, f32[64,256]{1,0:T(8,128)S(1)}, u32[]{:S(2)}, u32[]{:S(2)}) collective-permute-start(f32[64,256]{1,0:T(8,128)S(1)} %add_bitcast_fusion), channel_id=1, source_target_pairs={{4,0},{8,12},{5,1},{9,13},{6,2},{10,14},{7,3},{11,15},{20,16},{24,... | collective-permute-start | bytes 196616 | tf_op jit(solution)/shard_map/ppermute | solution.py:146
  105.5 18.7 %collective-permute-start.22 = (bf16[64,1536]{1,0:T(8,128)(2,1)S(1)}, bf16[64,1536]{1,0:T(8,128)(2,1)S(1)}, u32[]{:S(2)}, u32[]{:S(2)}) collective-permute-start(bf16[64,1536]{1,0:T(8,128)(2,1)S(1)} %collective-permute-done.19), channel_id=1, source_target_pairs={{4,0},{8,12},{5,1},{9,13},{6,2},{10,14},{7,3},{11,15},{20,16},{24,... | collective-permute-start | bytes 589832 | tf_op jit(solution)/shard_map/ppermute | solution.py:146
  125.9 1.4 %collective-permute-start.27 = (f32[2,64,256]{2,1,0:T(8,128)S(1)}, f32[2,64,256]{2,1,0:T(8,128)S(1)}, u32[]{:S(2)}, u32[]{:S(2)}) collective-permute-start(f32[2,64,256]{2,1,0:T(8,128)S(1)} %dynamic-slice_bitcast_fusion), channel_id=1, source_target_pairs={{0,1},{1,0},{2,3},{3,2},{4,5},{5,4},{6,7},{7,6},{8,9},{9,8},{10,11... | collective-permute-start | bytes 393224 | tf_op jit(solution)/shard_map/ppermute | solution.py:146
  127.4 4.3 %collective-permute-start.28 = (f32[1,64,256]{2,1,0:T(8,128)S(1)}, f32[1,64,256]{2,1,0:T(8,128)S(1)}, u32[]{:S(2)}, u32[]{:S(2)}) collective-permute-start(f32[1,64,256]{2,1,0:T(8,128)S(1)} %constant_dynamic-slice_fusion), channel_id=1, source_target_pairs={{0,2},{1,3},{2,0},{3,1},{4,6},{5,7},{6,4},{7,5},{8,10},{9,11},{10,... | collective-permute-start | bytes 196616 | tf_op jit(solution)/shard_map/ppermute | solution.py:146
  (4 other events, 31.2 us)

commit v5 on v0

v5 whole, which is shorter than its diff:
```python
import functools

import jax
import jax.numpy as jnp
from jax import lax
from jax.experimental import pallas as pl
from jax.experimental.pallas import tpu as pltpu
from jax.sharding import PartitionSpec as P

CONTRACT = (((1,), (1,)), ((), ()))
LINE, RING = (8, 5, 2, 1), (8, 5, 0, 3)
KEPT = ((0, 1, 2, 3), (1, 0, 2, 3), (2, 3, 1, 0), (3, 2, 1, 0))

GATES = {
    "E1T": ("E1B", "O1B"),
    "O1T": ("E1B", "O1B"),
    "Y1B": ("Y1A",),
    "E2B": ("E2A",),
    "Y2A": ("Y1A",),
    "O2B": ("O2A",),
    "OS": ("O1T", "E1T"),
    "E3A": ("E1T",),
    "E3B": ("E2B",),
    "Y2B": ("Y2A",),
    "E2T": ("E2B", "Y2A"),
    "O2T": ("OS",),
    "Y3A": ("Y2A",),
    "F1": ("Y2B",),
    "E3T": ("F1", "E2T"),
    "Y3B": ("Y2B",),
    "Z1": ("G",),
}


def pack_kernel(n_grp, plans, test, *rest):
    outs, sem = rest[:-1], rest[-1]
    copies = []
    for out, parts in zip(outs, plans):
        for slot, (row, col) in enumerate(parts):
            _, rows, cols = out.shape
            at = lax.axis_index("grp") * rows if row is None and n_grp > 1 else row or 0
            source = test.at[pl.ds(pl.multiple_of(at, rows), rows), pl.ds(col, cols)]
            copies.append(pltpu.make_async_copy(source, out.at[slot], sem.at[len(copies)]))
    for copy in copies:
        copy.start()
    for copy in copies:
        copy.wait()


def pack(n_grp, test, plans, rows, cols):
    return pl.pallas_call(
        functools.partial(pack_kernel, n_grp, plans),
        out_shape=[jax.ShapeDtypeStruct((len(p), rows, cols), test.dtype) for p in plans],
        in_specs=[pl.BlockSpec(memory_space=pl.ANY)],
        out_specs=[pl.BlockSpec(memory_space=pl.ANY)] * len(plans),
        scratch_shapes=[pltpu.SemaphoreType.DMA((sum(len(p) for p in plans),))],
        cost_estimate=pl.CostEstimate(flops=0, bytes_accessed=1 << 20, transcendentals=0),
    )(test)


def scores_kernel(n_grp, n_ex, halved, n_rows, has_base, *refs):
    rows, (scale, train) = refs[:n_rows], refs[n_rows : n_rows + 2]
    base = refs[n_rows + 2] if has_base else None
    out, total = refs[-2:]
    step = pl.program_id(0)
    block = jnp.concatenate([r[...] for r in rows], axis=0)
    precond = (block.astype(jnp.float32) * scale[...]).astype(jnp.bfloat16)
    part = lax.dot_general(precond, train[...], CONTRACT, preferred_element_type=jnp.float32)

    @pl.when(step == 0)
    def _():
        total[...] = part

    @pl.when(step > 0)
    def _():
        total[...] += part

    @pl.when(step == pl.num_programs(0) - 1)
    def _():
        ex, grp = lax.axis_index("ex"), lax.axis_index("grp")
        queries = out.shape[0] // n_ex
        half = queries // n_grp
        for b in range(n_ex):
            if n_ex == 4:
                t = jnp.int32(0)
                for i, kept in enumerate(KEPT):
                    t = jnp.where(ex == i, kept.index(b), t)
            else:
                t = lax.rem(ex + (n_ex - b), n_ex)
            for h in range(n_grp):
                place = h
                if halved and n_grp > 1:
                    place = jnp.where(t == 0, h, lax.rem(h + n_grp - grp, n_grp))
                at = pl.multiple_of(t * queries + place * half, half)
                value = total[pl.ds(at, half), :]
                to = b * queries + h * half
                if has_base:
                    value += base[to : to + half, :]
                out[to : to + half, :] = value


def scores(n_grp, n_ex, test, received, scale, train, unit, start, count, train_start, halved=False, base=None):
    docs = train.shape[0]
    in_specs = [pl.BlockSpec((test.shape[0], unit), lambda k: (0, start + k))]
    operands = [test]
    for array, first in received:
        in_specs.append(
            pl.BlockSpec((None,) + array.shape[1:], functools.partial(lambda f, k: (f + k, 0, 0), first))
        )
        operands.append(array)
    in_specs += [
        pl.BlockSpec((1, unit), lambda k: (0, start + k)),
        pl.BlockSpec((docs, unit), lambda k: (0, train_start + k)),
    ]
    operands += [scale, train]
    queries = test.shape[0] * n_ex
    if base is not None:
        in_specs.append(pl.BlockSpec((queries, docs), lambda k: (0, 0)))
        operands.append(base)
    return pl.pallas_call(
        functools.partial(
            scores_kernel, n_grp, n_ex, halved, 1 + len(received), base is not None
        ),
        out_shape=jax.ShapeDtypeStruct((queries, docs), jnp.float32),
        grid=(count,),
        in_specs=in_specs,
        out_specs=pl.BlockSpec((queries, docs), lambda k: (0, 0)),
        scratch_shapes=[pltpu.VMEM((queries, docs), jnp.float32)],
        cost_estimate=pl.CostEstimate(
            flops=2 * queries * docs * unit * count,
            bytes_accessed=2 * (queries + docs) * unit * count,
            transcendentals=0,
        ),
        compiler_params=pltpu.CompilerParams(vmem_limit_bytes=16 * 1024 * 1024),
    )(*operands)


def solution(mesh):
    n_grp, n_ex, n_feat = (mesh.shape[a] for a in ("grp", "ex", "feat"))
    assert n_grp <= 2
    line = n_ex == 4

    def on_device(train, test, hess):
        docs, feats = train.shape
        queries = test.shape[0]
        half = queries // n_grp
        unit = feats // 16
        n_a, n_b, n_s, n_t = LINE if line else RING
        at_b, at_s, at_t = n_a, n_a + n_b, n_a + n_b + n_s
        ex, feat = lax.axis_index("ex"), lax.axis_index("feat")
        is_end = (ex == 0) | (ex == n_ex - 1)
        done = {}

        def send(name, block, axis, pairs):
            waits = [done[g] for g in GATES.get(name, ()) if g in done]
            if waits:
                block = lax.optimization_barrier((block, waits))[0]
            done[name] = lax.ppermute(block, axis, pairs)
            return done[name]

        outer = [(i, i ^ 1) for i in range(n_ex)]
        middle = [(0, 0), (1, 2), (2, 1), (3, 3)]
        ring = [(i, (i + 1) % n_ex) for i in range(n_ex)]

        def hop(name, block, t):
            if t > 1:
                send(f"E{t}{name}", block, "ex", outer)
                if t < n_ex - 1:
                    send(f"O{t}{name}", done[f"E1{name}"], "ex", middle)
            else:
                send(f"E1{name}", block, "ex", outer)
                send(f"O1{name}", block, "ex", middle)

        def taken(name, t):
            if t == 1:
                return done[f"E1{name}"]
            return jnp.where(is_end, done[f"E{t}{name}"], done[f"O{t - 1}{name}"])

        def swap(name, block):
            if n_grp == 1:
                return [(block, 0)]
            return [(block, 0), (send(name, block, "grp", [(0, 1), (1, 0)]), 0)]

        def sum_over_feat(name, sums):
            held = sums.reshape(n_feat, -1, docs)
            bit = 1
            while bit < n_feat:
                pairs = held.reshape((-1, 2) + held.shape[1:])
                mine = (feat // bit) % 2
                keep = lax.dynamic_index_in_dim(pairs, mine, 1, keepdims=False)
                away = lax.dynamic_index_in_dim(pairs, 1 - mine, 1, keepdims=False)
                partner = [(i, i ^ bit) for i in range(n_feat)]
                held = keep + send(f"{name}{bit}", away, "feat", partner)
                bit *= 2
            return held[0]

        def halves(first, count):
            return [(None, (first + k) * unit) for k in range(count)]

        (a,) = pack(n_grp, test, [halves(0, n_a)], half, unit)
        plans = [halves(at_b, n_b)]
        if line:
            plans.append([(h * half, (at_s + k) * unit) for h in range(n_grp) for k in range(n_s)])
        b, *own_s = pack(n_grp, test, plans, half, unit)
        (tail,) = pack(1, test, [[(0, (at_t + k) * unit) for k in range(n_t)]], queries, unit)
        scale = (1.0 / (hess + jnp.float32(0.1))).reshape(1, feats)
        times = functools.partial(scores, n_grp, n_ex, test, scale=scale, unit=unit)
        got = {"A": [], "B": [], "T": []}

        def swapped(name, t):
            got[name] += swap(f"Y{t}{name}", taken(name, t))

        base = back = None
        if line:
            own_s = own_s[0]
            n_own = own_s.shape[0]
            groups = docs // half

            def slots(first, last, column):
                piece = train[first * half : last * half, column * unit : (column + 1) * unit]
                return piece.reshape(last - first, half, unit)

            cut = n_a - n_own
            cargo_2a = jnp.concatenate([own_s, slots(0, cut, at_s)])
            cargo_2b = jnp.concatenate([slots(cut, groups, at_s)] + [tail[:, :half]] * (n_b - groups + cut))
            cargo_3a = slots(0, groups, at_s + 1)

            hop("A", a, 1), hop("B", b, 1)
            swapped("A", 1)
            hop("A", jnp.where(is_end, cargo_2a, done["O1A"]), 2)
            hop("T", tail, 1)
            swapped("B", 1), swapped("A", 2)
            hop("B", jnp.where(is_end, cargo_2b, done["O1B"]), 2)
            end_s = done["E2A"][:n_own]
            send("OS", jnp.concatenate([own_s, end_s]), "ex", middle)
            hop("A", jnp.where(is_end, cargo_3a, done["O2A"]), 3)
            hop("B", done["O2B"], 3)
            swapped("B", 2)
            hop("T", done["O1T"], 2)
            swapped("A", 3)
            rows_s = [(end_s, h * n_s) for h in range(n_grp)]
            rows_s += [(done["OS"], h * n_s) for h in range(2 * n_grp)]
            first = jnp.concatenate([done["E2A"][n_own:], done["E2B"][: groups - cut]])
            away = jnp.concatenate([first.reshape(docs, unit), done["E3A"].reshape(docs, unit)], axis=1)
            far = times(received=rows_s, train=away, start=at_s, count=n_s, train_start=0)
            far = sum_over_feat("F", far)
            swapped("B", 3)
            hop("T", done["O2T"], 3)
            back = send("G", far, "ex", outer)
            near = times(received=rows_s, train=train, start=at_s, count=n_s, train_start=at_s)
            base = jnp.where(is_end, 0.0, near)
            got["T"] = [(taken("T", t), 0) for t in range(1, n_ex)]
        else:
            held = {"A": a, "B": b, "T": tail}
            for t in range(1, n_ex):
                for name in held:
                    held[name] = send(f"R{t}{name}", held[name], "ex", ring)
                    got[name] += [(held[name], 0)] if name == "T" else swap(f"Y{t}{name}", held[name])

        for name, start, count in (("A", 0, n_a), ("T", at_t, n_t), ("B", at_b, n_b)):
            base = times(
                received=got[name], train=train, start=start, count=count, train_start=start,
                halved=name != "T" and n_grp > 1, base=base,
            )
        out = sum_over_feat("Z", base)
        if line:
            out += jnp.where(is_end, back, 0.0)
        return out.T

    return jax.shard_map(
        on_device,
        mesh=mesh,
        in_specs=(P(("grp", "ex"), "feat"), P("ex", "feat"), P("feat")),
        out_specs=P(("grp", "ex"), "feat"),
        check_vma=False,
    )
```

time: 198 us -> 134 us (0.68)
  waiting for transfers between devices: 171 us -> 31.9 us
  Pallas kernels: 0 us -> 49.2 us
  starting transfers between devices: 0.04 us -> 41.2 us
  between operations: 13.4 us -> 0.48 us
  matrix products: 8.85 us -> 0 us
  local copies, waits for them, and re-layouts: 0 us -> 6.78 us
    all_gather x1 -> x0, waiting for transfers between devices: 152 us -> none  [on_device(): lax.all_gather(precond, 'ex', axis=0, tiled=True)]
    pallas_call x0 -> x8, Pallas kernels: none -> 49.2 us  [the longest x3 41.2 us: pack(): pl.pallas_call(functools.partial(pack_kernel, n_grp, plans), out_shape=[j...]
    ppermute x0 -> x27, starting transfers between devices: none -> 41.2 us  [send(): done[name] = lax.ppermute(block, axis, pairs)]
    ppermute x0 -> x27, waiting for transfers between devices: none -> 31.9 us  [send(): done[name] = lax.ppermute(block, axis, pairs)]
    reduce_scatter x1 -> x0, waiting for transfers between devices: 18.4 us -> none  [on_device(): lax.psum_scatter(partial_sums, 'feat', scatter_dimension=1, tiled=True)]
    dot_general x1 -> x0, matrix products: 8.85 us -> none  [on_device(): lax.dot_general(train_grads, lax.all_gather(precond, 'ex', axis=0, tiled=...]
    unnamed x0 -> x12, local copies, waits for them, and re-layouts: none -> 3.4 us
    convert_element_type x1 -> x0, other arithmetic: 3.34 us -> none  [on_device(): (test_grads.astype(jnp.float32) * inverse[None, :]).astype(jnp.bfloat16)]
  transfers between devices with their start and end apart: 2 -> 27, of which waited for: 2 -> 9; matrix products, arithmetic and copies ran while one was open for 0% -> 5% of each run, Pallas kernels for 0% -> 24%
where the time goes in v5:
time: 134 us
  Pallas kernels  49.2 us (37%)
  starting transfers between devices  41.2 us (31%)
  waiting for transfers between devices  31.9 us (24%)
  local copies, waits for them, and re-layouts  6.78 us (5%)
  other arithmetic  4.06 us (3%)
    pallas_call x3, Pallas kernels, pack(): pl.pallas_call(functools.partial(pack_kernel, n_grp, plans), out_shape=[j...  41.2 us
    ppermute x27, starting transfers between devices, send(): done[name] = lax.ppermute(block, axis, pairs)  41.2 us
    ppermute x27, waiting for transfers between devices, send(): done[name] = lax.ppermute(block, axis, pairs)  31.9 us
    pallas_call x5, Pallas kernels, scores(): pl.pallas_call(functools.partial(scores_kernel, n_grp, n_ex, halved, 1 +...  8.06 us
    unnamed x12, local copies, waits for them, and re-layouts  3.4 us
  transfers between devices with their start and end apart: 27, of which 9 were waited for; matrix products, arithmetic and copies ran while one was open for 5% of the time, Pallas kernels for 24%

profile of v5, /device:TPU:0, one launch (start us, length us, event | category | flops | bytes accessed | tf_op | source)
XLA Modules:
  0.0 133.6 jit_solution(10590190021886474104)
XLA Ops:
  0.0 17.1 %shard_map.38 = bf16[8,32,1024]{2,1,0:T(8,128)(2,1)} custom-call(bf16[64,16384]{1,0:T(8,128)(2,1)} %refs_0_.9), custom_call_target="tpu_custom_call" | custom-call | bytes 1048576 | tf_op jit(solution)/shard_map/pallas_call | solution.py:51
  17.1 1.8 %collective-permute-start.5 = (bf16[8,32,1024]{2,1,0:T(8,128)(2,1)}, bf16[8,32,1024]{2,1,0:T(8,128)(2,1)S(1)}, u32[]{:S(2)}, u32[]{:S(2)}) collective-permute-start(bf16[8,32,1024]{2,1,0:T(8,128)(2,1)} %shard_map.38), channel_id=1, source_target_pairs={{0,0},{4,8},{8,4},{12,12},{1,1},{5,9},{9,5},{13,13},{2,2},{6,10},{... | collective-permute-start | bytes 1572872 | tf_op jit(solution)/shard_map/ppermute | solution.py:158
  18.9 4.9 %collective-permute-start.1 = (bf16[8,32,1024]{2,1,0:T(8,128)(2,1)}, bf16[8,32,1024]{2,1,0:T(8,128)(2,1)S(1)}, u32[]{:S(2)}, u32[]{:S(2)}) collective-permute-start(bf16[8,32,1024]{2,1,0:T(8,128)(2,1)} %shard_map.38), channel_id=1, source_target_pairs={{0,4},{4,0},{8,12},{12,8},{1,5},{5,1},{9,13},{13,9},{2,6},{6,2},{1... | collective-permute-start | bytes 1572872 | tf_op jit(solution)/shard_map/ppermute | solution.py:158
  23.8 19.0 %shard_map.37 = (bf16[5,32,1024]{2,1,0:T(8,128)(2,1)}, bf16[4,32,1024]{2,1,0:T(8,128)(2,1)}) custom-call(bf16[64,16384]{1,0:T(8,128)(2,1)} %refs_0_.9), custom_call_target="tpu_custom_call" | custom-call | bytes 1048576 | tf_op jit(solution)/shard_map/pallas_call | solution.py:51
  42.8 3.9 %collective-permute-start.4 = (bf16[5,32,1024]{2,1,0:T(8,128)(2,1)}, bf16[5,32,1024]{2,1,0:T(8,128)(2,1)}, u32[]{:S(2)}, u32[]{:S(2)}) collective-permute-start(bf16[5,32,1024]{2,1,0:T(8,128)(2,1)} %get-tuple-element.23), channel_id=1, source_target_pairs={{0,0},{4,8},{8,4},{12,12},{1,1},{5,9},{9,5},{13,13},{2,2},{6,10},{... | collective-permute-start | bytes 983048 | tf_op jit(solution)/shard_map/ppermute | solution.py:158
  46.7 1.8 %fusion.2 = (bf16[128,1024]{1,0:T(8,128)(2,1)}, bf16[128,1024]{1,0:T(8,128)(2,1)S(1)}) fusion(bf16[256,16384]{1,0:T(8,128)(2,1)} %refs_8_.5), kind=kLoop, calls=%fused_computation.24 | loop fusion | bytes 1048576 | tf_op jit(solution)/shard_map/slice | solution.py:220
  48.5 1.8 %fusion = bf16[8,32,1024]{2,1,0:T(8,128)(2,1)} fusion(bf16[8,32,1024]{2,1,0:T(8,128)(2,1)S(1)} %collective-permute-done.5, bf16[4,32,1024]{2,1,0:T(8,128)(2,1)} %get-tuple-element.25, bf16[4,32,1024]{2,1,0:T(8,128)(2,1)S(1)} %bitcast.39, pred[]{:T(512)S(6)} %or.3), kind=kLoop, calls=%fused_computation.3 | loop fusion | flops 524288 | bytes 1572865 | tf_op jit(solution)/shard_map/jit(_where)/select_n | solution.py:230
  50.3 2.0 %collective-permute-start.6 = (bf16[8,32,1024]{2,1,0:T(8,128)(2,1)}, bf16[8,32,1024]{2,1,0:T(8,128)(2,1)S(1)}, u32[]{:S(2)}, u32[]{:S(2)}) collective-permute-start(bf16[8,32,1024]{2,1,0:T(8,128)(2,1)} %fusion), channel_id=1, source_target_pairs={{0,4},{4,0},{8,12},{12,8},{1,5},{5,1},{9,13},{13,9},{2,6},{6,2},{1... | collective-permute-start | bytes 1572872 | tf_op jit(solution)/shard_map/ppermute | solution.py:158
  53.0 1.6 %collective-permute-start.2 = (bf16[8,32,1024]{2,1,0:T(8,128)(2,1)S(1)}, bf16[8,32,1024]{2,1,0:T(8,128)(2,1)S(1)}, u32[]{:S(2)}, u32[]{:S(2)}) collective-permute-start(bf16[8,32,1024]{2,1,0:T(8,128)(2,1)S(1)} %collective-permute-done.1.refs_1_), channel_id=1, source_target_pairs={{0,16},{16,0},{1,17},{17,1},{2,18},{18,2},{3,19},{19,3},{4,20},{20... | collective-permute-start | bytes 1572872 | tf_op jit(solution)/shard_map/ppermute | solution.py:158
  54.7 5.1 %shard_map.39 = bf16[1,64,1024]{2,1,0:T(8,128)(2,1)} custom-call(bf16[64,16384]{1,0:T(8,128)(2,1)} %refs_0_.9), custom_call_target="tpu_custom_call" | custom-call | bytes 1048576 | tf_op jit(solution)/shard_map/pallas_call | solution.py:51
  59.8 1.5 %slice.28 = bf16[1,32,1024]{2,1,0:T(8,128)(2,1)} slice(bf16[1,64,1024]{2,1,0:T(8,128)(2,1)} %shard_map.39), slice={[0:1], [0:32], [0:1024]} | slice | bytes 131072 | tf_op jit(solution)/shard_map/slice | solution.py:225
  61.3 1.7 %collective-permute-start.15 = (bf16[1,64,1024]{2,1,0:T(8,128)(2,1)}, bf16[1,64,1024]{2,1,0:T(8,128)(2,1)S(1)}, u32[]{:S(2)}, u32[]{:S(2)}) collective-permute-start(bf16[1,64,1024]{2,1,0:T(8,128)(2,1)} %shard_map.39), channel_id=1, source_target_pairs={{0,0},{4,8},{8,4},{12,12},{1,1},{5,9},{9,5},{13,13},{2,2},{6,10},{... | collective-permute-start | bytes 393224 | tf_op jit(solution)/shard_map/ppermute | solution.py:158
  63.0 3.7 %collective-permute-start.14 = (bf16[1,64,1024]{2,1,0:T(8,128)(2,1)}, bf16[1,64,1024]{2,1,0:T(8,128)(2,1)S(1)}, u32[]{:S(2)}, u32[]{:S(2)}) collective-permute-start(bf16[1,64,1024]{2,1,0:T(8,128)(2,1)} %shard_map.39), channel_id=1, source_target_pairs={{0,4},{4,0},{8,12},{12,8},{1,5},{5,1},{9,13},{13,9},{2,6},{6,2},{1... | collective-permute-start | bytes 393224 | tf_op jit(solution)/shard_map/ppermute | solution.py:158
  67.8 2.1 %collective-permute-done.14.refs_1_ = bf16[1,64,1024]{2,1,0:T(8,128)(2,1)S(1)} collective-permute-done((bf16[1,64,1024]{2,1,0:T(8,128)(2,1)}, bf16[1,64,1024]{2,1,0:T(8,128)(2,1)S(1)}, u32[]{:S(2)}, u32[]{:S(2)}) %collective-permute-start.14) | collective-permute-done | bytes 131104 | tf_op jit(solution)/shard_map/ppermute | solution.py:158
  69.9 1.5 %collective-permute-start.3 = (bf16[5,32,1024]{2,1,0:T(8,128)(2,1)S(1)}, bf16[5,32,1024]{2,1,0:T(8,128)(2,1)S(1)}, u32[]{:S(2)}, u32[]{:S(2)}) collective-permute-start(bf16[5,32,1024]{2,1,0:T(8,128)(2,1)S(1)} %collective-permute-done.refs_1_), channel_id=1, source_target_pairs={{0,16},{16,0},{1,17},{17,1},{2,18},{18,2},{3,19},{19,3},{4,20},{20... | collective-permute-start | bytes 983048 | tf_op jit(solution)/shard_map/ppermute | solution.py:158
  72.1 2.7 %collective-permute-start.19 = (bf16[8,32,1024]{2,1,0:T(8,128)(2,1)S(1)}, bf16[8,32,1024]{2,1,0:T(8,128)(2,1)S(1)}, u32[]{:S(2)}, u32[]{:S(2)}) collective-permute-start(bf16[8,32,1024]{2,1,0:T(8,128)(2,1)S(1)} %broadcast_select_fusion.1), channel_id=1, source_target_pairs={{0,4},{4,0},{8,12},{12,8},{1,5},{5,1},{9,13},{13,9},{2,6},{6,2},{1... | collective-permute-start | bytes 1572872 | tf_op jit(solution)/shard_map/ppermute | solution.py:158
  75.8 1.6 %collective-permute-start.8 = (bf16[8,32,1024]{2,1,0:T(8,128)(2,1)S(1)}, bf16[8,32,1024]{2,1,0:T(8,128)(2,1)S(1)}, u32[]{:S(2)}, u32[]{:S(2)}) collective-permute-start(bf16[8,32,1024]{2,1,0:T(8,128)(2,1)S(1)} %broadcast_select_fusion.2.refs_3_), channel_id=1, source_target_pairs={{0,16},{16,0},{1,17},{17,1},{2,18},{18,2},{3,19},{19,3},{4,20},{20... | collective-permute-start | bytes 1572872 | tf_op jit(solution)/shard_map/ppermute | solution.py:158
  77.3 14.5 %collective-permute-done.7 = bf16[5,32,1024]{2,1,0:T(8,128)(2,1)S(1)} collective-permute-done((bf16[5,32,1024]{2,1,0:T(8,128)(2,1)S(1)}, bf16[5,32,1024]{2,1,0:T(8,128)(2,1)S(1)}, u32[]{:S(2)}, u32[]{:S(2)}) %collective-permute-start.7) | collective-permute-done | bytes 327712 | tf_op jit(solution)/shard_map/ppermute | solution.py:158
  91.8 2.0 %collective-permute-start.12 = (bf16[5,32,1024]{2,1,0:T(8,128)(2,1)S(1)}, bf16[5,32,1024]{2,1,0:T(8,128)(2,1)S(1)}, u32[]{:S(2)}, u32[]{:S(2)}) collective-permute-start(bf16[5,32,1024]{2,1,0:T(8,128)(2,1)S(1)} %collective-permute-done.11), channel_id=1, source_target_pairs={{0,4},{4,0},{8,12},{12,8},{1,5},{5,1},{9,13},{13,9},{2,6},{6,2},{1... | collective-permute-start | bytes 983048 | tf_op jit(solution)/shard_map/ppermute | solution.py:158
  94.9 3.9 %collective-permute-start.16 = (bf16[1,64,1024]{2,1,0:T(8,128)(2,1)S(1)}, bf16[1,64,1024]{2,1,0:T(8,128)(2,1)S(1)}, u32[]{:S(2)}, u32[]{:S(2)}) collective-permute-start(bf16[1,64,1024]{2,1,0:T(8,128)(2,1)S(1)} %collective-permute-done.15), channel_id=1, source_target_pairs={{0,4},{4,0},{8,12},{12,8},{1,5},{5,1},{9,13},{13,9},{2,6},{6,2},{1... | collective-permute-start | bytes 393224 | tf_op jit(solution)/shard_map/ppermute | solution.py:158
  98.8 1.5 %collective-permute-start.9 = (bf16[5,32,1024]{2,1,0:T(8,128)(2,1)S(1)}, bf16[5,32,1024]{2,1,0:T(8,128)(2,1)S(1)}, u32[]{:S(2)}, u32[]{:S(2)}) collective-permute-start(bf16[5,32,1024]{2,1,0:T(8,128)(2,1)S(1)} %broadcast_select_fusion.4.refs_3_), channel_id=1, source_target_pairs={{0,16},{16,0},{1,17},{17,1},{2,18},{18,2},{3,19},{19,3},{4,20},{20... | collective-permute-start | bytes 983048 | tf_op jit(solution)/shard_map/ppermute | solution.py:158
  100.4 3.4 %copy-done = bf16[256,16384]{1,0:T(8,128)(2,1)S(1)} copy-done((bf16[256,16384]{1,0:T(8,128)(2,1)S(1)}, bf16[256,16384]{1,0:T(8,128)(2,1)}, u32[]{:S(2)}) %copy-start) | copy-done | bytes 8388632
  105.7 2.9 %collective-permute-done.9.refs_4_ = bf16[5,32,1024]{2,1,0:T(8,128)(2,1)S(1)} collective-permute-done((bf16[5,32,1024]{2,1,0:T(8,128)(2,1)S(1)}, bf16[5,32,1024]{2,1,0:T(8,128)(2,1)S(1)}, u32[]{:S(2)}, u32[]{:S(2)}) %collective-permute-start.9) | collective-permute-done | bytes 327712 | tf_op jit(solution)/shard_map/ppermute | solution.py:158
  108.7 2.0 %collective-permute-start.22 = (bf16[8,32,1024]{2,1,0:T(8,128)(2,1)S(1)}, bf16[8,32,1024]{2,1,0:T(8,128)(2,1)S(1)}, u32[]{:S(2)}, u32[]{:S(2)}) collective-permute-start(bf16[8,32,1024]{2,1,0:T(8,128)(2,1)S(1)} %broadcast_select_fusion.refs_5_), channel_id=1, source_target_pairs={{0,16},{16,0},{1,17},{17,1},{2,18},{18,2},{3,19},{19,3},{4,20},{20... | collective-permute-start | bytes 1572872 | tf_op jit(solution)/shard_map/ppermute | solution.py:158
  112.0 1.6 %collective-permute-start.23 = (f32[1,64,256]{2,1,0:T(8,128)S(1)}, f32[1,64,256]{2,1,0:T(8,128)S(1)}, u32[]{:S(2)}, u32[]{:S(2)}) collective-permute-start(f32[1,64,256]{2,1,0:T(8,128)S(1)} %constant_dynamic-slice_fusion.1), channel_id=1, source_target_pairs={{0,2},{1,3},{2,0},{3,1},{4,6},{5,7},{6,4},{7,5},{8,10},{9,11},{10,... | collective-permute-start | bytes 196616 | tf_op jit(solution)/shard_map/ppermute | solution.py:158
  113.8 2.6 %collective-permute-done.23 = f32[1,64,256]{2,1,0:T(8,128)S(1)} collective-permute-done((f32[1,64,256]{2,1,0:T(8,128)S(1)}, f32[1,64,256]{2,1,0:T(8,128)S(1)}, u32[]{:S(2)}, u32[]{:S(2)}) %collective-permute-start.23) | collective-permute-done | bytes 65568 | tf_op jit(solution)/shard_map/ppermute | solution.py:158
  116.5 4.2 %collective-permute-done.22.refs_6_ = bf16[8,32,1024]{2,1,0:T(8,128)(2,1)S(1)} collective-permute-done((bf16[8,32,1024]{2,1,0:T(8,128)(2,1)S(1)}, bf16[8,32,1024]{2,1,0:T(8,128)(2,1)S(1)}, u32[]{:S(2)}, u32[]{:S(2)}) %collective-permute-start.22) | collective-permute-done | bytes 524320 | tf_op jit(solution)/shard_map/ppermute | solution.py:158
  120.7 3.6 %shard_map.42.refs_6_ = f32[256,256]{1,0:T(8,128)S(1)} custom-call(bf16[64,16384]{1,0:T(8,128)(2,1)S(1)} %copy-done.1, bf16[8,32,1024]{2,1,0:T(8,128)(2,1)S(1)} %collective-permute-done.1.refs_1_, bf16[8,32,1024]{2,1,0:T(8,128)(2,1)S(1)} %collective-permute-done.2.refs_2_, bf16[8,32,1024]{2,1,0:T(8,128)(2,1)S(1)} %broadcast_select_fusion.2.refs_3_, ...), custom_call_target="tpu_custom_call" | custom-call | flops 1073741824 | bytes 8388608 | tf_op jit(solution)/shard_map/pallas_call | solution.py:120
  124.9 2.2 %shard_map.44 = f32[256,256]{1,0:T(8,128)S(1)} custom-call(bf16[64,16384]{1,0:T(8,128)(2,1)S(1)} %copy-done.1, bf16[5,32,1024]{2,1,0:T(8,128)(2,1)S(1)} %collective-permute-done.refs_1_, bf16[5,32,1024]{2,1,0:T(8,128)(2,1)S(1)} %collective-permute-done.3.refs_2_, bf16[5,32,1024]{2,1,0:T(8,128)(2,1)S(1)} %broadcast_select_fusion.4.refs_3_, ...), custom_call_target="tpu_custom_call" | custom-call | flops 671088640 | bytes 5242880 | tf_op jit(solution)/shard_map/pallas_call | solution.py:120
  127.2 1.3 collective-permute-done.25
  128.6 1.6 %collective-permute-start.26 = (f32[1,64,256]{2,1,0:T(8,128)S(1)}, f32[1,64,256]{2,1,0:T(8,128)S(1)}, u32[]{:S(2)}, u32[]{:S(2)}) collective-permute-start(f32[1,64,256]{2,1,0:T(8,128)S(1)} %constant_dynamic-slice_fusion), channel_id=1, source_target_pairs={{0,2},{1,3},{2,0},{3,1},{4,6},{5,7},{6,4},{7,5},{8,10},{9,11},{10,... | collective-permute-start | bytes 196616 | tf_op jit(solution)/shard_map/ppermute | solution.py:158
  130.2 2.7 %collective-permute-done.26 = f32[1,64,256]{2,1,0:T(8,128)S(1)} collective-permute-done((f32[1,64,256]{2,1,0:T(8,128)S(1)}, f32[1,64,256]{2,1,0:T(8,128)S(1)}, u32[]{:S(2)}, u32[]{:S(2)}) %collective-permute-start.26) | collective-permute-done | bytes 65568 | tf_op jit(solution)/shard_map/ppermute | solution.py:158
  (71 shorter events, 9.4 us)
Async XLA Ops:
  17.1 37.6 %copy-start.3 = (f32[16384]{0:T(1024)S(1)}, f32[16384]{0:T(1024)}, u32[]{:S(2)}) copy-start(f32[16384]{0:T(1024)} %param.5) | copy-start | bytes 196612
  17.1 31.4 %collective-permute-start.5 = (bf16[8,32,1024]{2,1,0:T(8,128)(2,1)}, bf16[8,32,1024]{2,1,0:T(8,128)(2,1)S(1)}, u32[]{:S(2)}, u32[]{:S(2)}) collective-permute-start(bf16[8,32,1024]{2,1,0:T(8,128)(2,1)} %shard_map.38), channel_id=1, source_target_pairs={{0,0},{4,8},{8,4},{12,12},{1,1},{5,9},{9,5},{13,13},{2,2},{6,10},{... | collective-permute-start | bytes 1572872 | tf_op jit(solution)/shard_map/ppermute | solution.py:158
  18.9 33.4 %collective-permute-start.1 = (bf16[8,32,1024]{2,1,0:T(8,128)(2,1)}, bf16[8,32,1024]{2,1,0:T(8,128)(2,1)S(1)}, u32[]{:S(2)}, u32[]{:S(2)}) collective-permute-start(bf16[8,32,1024]{2,1,0:T(8,128)(2,1)} %shard_map.38), channel_id=1, source_target_pairs={{0,4},{4,0},{8,12},{12,8},{1,5},{5,1},{9,13},{13,9},{2,6},{6,2},{1... | collective-permute-start | bytes 1572872 | tf_op jit(solution)/shard_map/ppermute | solution.py:158
  42.8 18.4 %collective-permute-start.4 = (bf16[5,32,1024]{2,1,0:T(8,128)(2,1)}, bf16[5,32,1024]{2,1,0:T(8,128)(2,1)}, u32[]{:S(2)}, u32[]{:S(2)}) collective-permute-start(bf16[5,32,1024]{2,1,0:T(8,128)(2,1)} %get-tuple-element.23), channel_id=1, source_target_pairs={{0,0},{4,8},{8,4},{12,12},{1,1},{5,9},{9,5},{13,13},{2,2},{6,10},{... | collective-permute-start | bytes 983048 | tf_op jit(solution)/shard_map/ppermute | solution.py:158
  46.7 14.6 %collective-permute-start = (bf16[5,32,1024]{2,1,0:T(8,128)(2,1)}, bf16[5,32,1024]{2,1,0:T(8,128)(2,1)S(1)}, u32[]{:S(2)}, u32[]{:S(2)}) collective-permute-start(bf16[5,32,1024]{2,1,0:T(8,128)(2,1)} %get-tuple-element.23), channel_id=1, source_target_pairs={{0,4},{4,0},{8,12},{12,8},{1,5},{5,1},{9,13},{13,9},{2,6},{6,2},{1... | collective-permute-start | bytes 983048 | tf_op jit(solution)/shard_map/ppermute | solution.py:158
  50.3 24.4 %collective-permute-start.6 = (bf16[8,32,1024]{2,1,0:T(8,128)(2,1)}, bf16[8,32,1024]{2,1,0:T(8,128)(2,1)S(1)}, u32[]{:S(2)}, u32[]{:S(2)}) collective-permute-start(bf16[8,32,1024]{2,1,0:T(8,128)(2,1)} %fusion), channel_id=1, source_target_pairs={{0,4},{4,0},{8,12},{12,8},{1,5},{5,1},{9,13},{13,9},{2,6},{6,2},{1... | collective-permute-start | bytes 1572872 | tf_op jit(solution)/shard_map/ppermute | solution.py:158
  52.3 15.3 %collective-permute-start.10 = (bf16[8,32,1024]{2,1,0:T(8,128)(2,1)S(1)}, bf16[8,32,1024]{2,1,0:T(8,128)(2,1)S(1)}, u32[]{:S(2)}, u32[]{:S(2)}) collective-permute-start(bf16[8,32,1024]{2,1,0:T(8,128)(2,1)S(1)} %collective-permute-done.1.refs_1_), channel_id=1, source_target_pairs={{0,0},{4,8},{8,4},{12,12},{1,1},{5,9},{9,5},{13,13},{2,2},{6,10},{... | collective-permute-start | bytes 1572872 | tf_op jit(solution)/shard_map/ppermute | solution.py:158
  53.0 14.7 %collective-permute-start.2 = (bf16[8,32,1024]{2,1,0:T(8,128)(2,1)S(1)}, bf16[8,32,1024]{2,1,0:T(8,128)(2,1)S(1)}, u32[]{:S(2)}, u32[]{:S(2)}) collective-permute-start(bf16[8,32,1024]{2,1,0:T(8,128)(2,1)S(1)} %collective-permute-done.1.refs_1_), channel_id=1, source_target_pairs={{0,16},{16,0},{1,17},{17,1},{2,18},{18,2},{3,19},{19,3},{4,20},{20... | collective-permute-start | bytes 1572872 | tf_op jit(solution)/shard_map/ppermute | solution.py:158
  54.7 13.0 %slice-start.2 = ((bf16[256,16384]{1,0:T(8,128)(2,1)}), bf16[256,1024]{1,0:T(8,128)(2,1)S(1)}, s32[]{:S(2)}) async-start(bf16[256,16384]{1,0:T(8,128)(2,1)} %refs_8_.5), calls=%async_computation.2 | async-start | bytes 1048576 | tf_op jit(solution)/shard_map/slice | solution.py:220
  61.3 13.6 %copy-start.2 = (bf16[4,32,1024]{2,1,0:T(8,128)(2,1)S(1)}, bf16[4,32,1024]{2,1,0:T(8,128)(2,1)}, u32[]{:S(2)}) copy-start(bf16[4,32,1024]{2,1,0:T(8,128)(2,1)} %get-tuple-element.25) | copy-start | bytes 786436
  61.3 13.7 %collective-permute-start.15 = (bf16[1,64,1024]{2,1,0:T(8,128)(2,1)}, bf16[1,64,1024]{2,1,0:T(8,128)(2,1)S(1)}, u32[]{:S(2)}, u32[]{:S(2)}) collective-permute-start(bf16[1,64,1024]{2,1,0:T(8,128)(2,1)} %shard_map.39), channel_id=1, source_target_pairs={{0,0},{4,8},{8,4},{12,12},{1,1},{5,9},{9,5},{13,13},{2,2},{6,10},{... | collective-permute-start | bytes 393224 | tf_op jit(solution)/shard_map/ppermute | solution.py:158
  63.0 6.9 %collective-permute-start.14 = (bf16[1,64,1024]{2,1,0:T(8,128)(2,1)}, bf16[1,64,1024]{2,1,0:T(8,128)(2,1)S(1)}, u32[]{:S(2)}, u32[]{:S(2)}) collective-permute-start(bf16[1,64,1024]{2,1,0:T(8,128)(2,1)} %shard_map.39), channel_id=1, source_target_pairs={{0,4},{4,0},{8,12},{12,8},{1,5},{5,1},{9,13},{13,9},{2,6},{6,2},{1... | collective-permute-start | bytes 393224 | tf_op jit(solution)/shard_map/ppermute | solution.py:158
  69.9 54.8 %collective-permute-start.3 = (bf16[5,32,1024]{2,1,0:T(8,128)(2,1)S(1)}, bf16[5,32,1024]{2,1,0:T(8,128)(2,1)S(1)}, u32[]{:S(2)}, u32[]{:S(2)}) collective-permute-start(bf16[5,32,1024]{2,1,0:T(8,128)(2,1)S(1)} %collective-permute-done.refs_1_), channel_id=1, source_target_pairs={{0,16},{16,0},{1,17},{17,1},{2,18},{18,2},{3,19},{19,3},{4,20},{20... | collective-permute-start | bytes 983048 | tf_op jit(solution)/shard_map/ppermute | solution.py:158
  71.4 4.4 %collective-permute-start.11 = (bf16[5,32,1024]{2,1,0:T(8,128)(2,1)S(1)}, bf16[5,32,1024]{2,1,0:T(8,128)(2,1)S(1)}, u32[]{:S(2)}, u32[]{:S(2)}) collective-permute-start(bf16[5,32,1024]{2,1,0:T(8,128)(2,1)S(1)} %collective-permute-done.refs_1_), channel_id=1, source_target_pairs={{0,0},{4,8},{8,4},{12,12},{1,1},{5,9},{9,5},{13,13},{2,2},{6,10},{... | collective-permute-start | bytes 983048 | tf_op jit(solution)/shard_map/ppermute | solution.py:158
  72.1 22.8 %collective-permute-start.19 = (bf16[8,32,1024]{2,1,0:T(8,128)(2,1)S(1)}, bf16[8,32,1024]{2,1,0:T(8,128)(2,1)S(1)}, u32[]{:S(2)}, u32[]{:S(2)}) collective-permute-start(bf16[8,32,1024]{2,1,0:T(8,128)(2,1)S(1)} %broadcast_select_fusion.1), channel_id=1, source_target_pairs={{0,4},{4,0},{8,12},{12,8},{1,5},{5,1},{9,13},{13,9},{2,6},{6,2},{1... | collective-permute-start | bytes 1572872 | tf_op jit(solution)/shard_map/ppermute | solution.py:158
  74.8 17.1 %collective-permute-start.7 = (bf16[5,32,1024]{2,1,0:T(8,128)(2,1)S(1)}, bf16[5,32,1024]{2,1,0:T(8,128)(2,1)S(1)}, u32[]{:S(2)}, u32[]{:S(2)}) collective-permute-start(bf16[5,32,1024]{2,1,0:T(8,128)(2,1)S(1)} %maximum_select_fusion), channel_id=1, source_target_pairs={{0,4},{4,0},{8,12},{12,8},{1,5},{5,1},{9,13},{13,9},{2,6},{6,2},{1... | collective-permute-start | bytes 983048 | tf_op jit(solution)/shard_map/ppermute | solution.py:158
  75.0 19.0 %collective-permute-start.17 = (bf16[8,32,1024]{2,1,0:T(8,128)(2,1)S(1)}, bf16[8,32,1024]{2,1,0:T(8,128)(2,1)S(1)}, u32[]{:S(2)}, u32[]{:S(2)}) collective-permute-start(bf16[8,32,1024]{2,1,0:T(8,128)(2,1)S(1)} %pad_maximum_fusion.1), channel_id=1, source_target_pairs={{0,0},{4,8},{8,4},{12,12},{1,1},{5,9},{9,5},{13,13},{2,2},{6,10},{... | collective-permute-start | bytes 1572872 | tf_op jit(solution)/shard_map/ppermute | solution.py:158
  75.7 45.0 %slice-start = ((s8[8388608]{0:T(1024)(128)(4,1)}), s8[4194304]{0:T(1024)(128)(4,1)S(1)}, s32[]{:S(2)}) async-start(s8[8388608]{0:T(1024)(128)(4,1)} %bitcast.24), calls=%async_computation | async-start | bytes 8388608
  75.8 19.1 %collective-permute-start.8 = (bf16[8,32,1024]{2,1,0:T(8,128)(2,1)S(1)}, bf16[8,32,1024]{2,1,0:T(8,128)(2,1)S(1)}, u32[]{:S(2)}, u32[]{:S(2)}) collective-permute-start(bf16[8,32,1024]{2,1,0:T(8,128)(2,1)S(1)} %broadcast_select_fusion.2.refs_3_), channel_id=1, source_target_pairs={{0,16},{16,0},{1,17},{17,1},{2,18},{18,2},{3,19},{19,3},{4,20},{20... | collective-permute-start | bytes 1572872 | tf_op jit(solution)/shard_map/ppermute | solution.py:158
  91.8 18.8 %collective-permute-start.12 = (bf16[5,32,1024]{2,1,0:T(8,128)(2,1)S(1)}, bf16[5,32,1024]{2,1,0:T(8,128)(2,1)S(1)}, u32[]{:S(2)}, u32[]{:S(2)}) collective-permute-start(bf16[5,32,1024]{2,1,0:T(8,128)(2,1)S(1)} %collective-permute-done.11), channel_id=1, source_target_pairs={{0,4},{4,0},{8,12},{12,8},{1,5},{5,1},{9,13},{13,9},{2,6},{6,2},{1... | collective-permute-start | bytes 983048 | tf_op jit(solution)/shard_map/ppermute | solution.py:158
  94.0 19.7 %collective-permute-start.18 = (bf16[1,64,1024]{2,1,0:T(8,128)(2,1)S(1)}, bf16[1,64,1024]{2,1,0:T(8,128)(2,1)S(1)}, u32[]{:S(2)}, u32[]{:S(2)}) collective-permute-start(bf16[1,64,1024]{2,1,0:T(8,128)(2,1)S(1)} %collective-permute-done.14.refs_1_), channel_id=1, source_target_pairs={{0,0},{4,8},{8,4},{12,12},{1,1},{5,9},{9,5},{13,13},{2,2},{6,10},{... | collective-permute-start | bytes 393224 | tf_op jit(solution)/shard_map/ppermute | solution.py:158
  94.9 18.7 %collective-permute-start.16 = (bf16[1,64,1024]{2,1,0:T(8,128)(2,1)S(1)}, bf16[1,64,1024]{2,1,0:T(8,128)(2,1)S(1)}, u32[]{:S(2)}, u32[]{:S(2)}) collective-permute-start(bf16[1,64,1024]{2,1,0:T(8,128)(2,1)S(1)} %collective-permute-done.15), channel_id=1, source_target_pairs={{0,4},{4,0},{8,12},{12,8},{1,5},{5,1},{9,13},{13,9},{2,6},{6,2},{1... | collective-permute-start | bytes 393224 | tf_op jit(solution)/shard_map/ppermute | solution.py:158
  98.8 9.9 %collective-permute-start.9 = (bf16[5,32,1024]{2,1,0:T(8,128)(2,1)S(1)}, bf16[5,32,1024]{2,1,0:T(8,128)(2,1)S(1)}, u32[]{:S(2)}, u32[]{:S(2)}) collective-permute-start(bf16[5,32,1024]{2,1,0:T(8,128)(2,1)S(1)} %broadcast_select_fusion.4.refs_3_), channel_id=1, source_target_pairs={{0,16},{16,0},{1,17},{17,1},{2,18},{18,2},{3,19},{19,3},{4,20},{20... | collective-permute-start | bytes 983048 | tf_op jit(solution)/shard_map/ppermute | solution.py:158
  103.8 16.9 %slice-start.1 = ((s8[8388608]{0:T(1024)(128)(4,1)}), s8[4194304]{0:T(1024)(128)(4,1)S(1)}, s32[]{:S(2)}) async-start(s8[8388608]{0:T(1024)(128)(4,1)} %bitcast.24), calls=%async_computation.1 | async-start | bytes 8388608
  108.7 12.0 %collective-permute-start.22 = (bf16[8,32,1024]{2,1,0:T(8,128)(2,1)S(1)}, bf16[8,32,1024]{2,1,0:T(8,128)(2,1)S(1)}, u32[]{:S(2)}, u32[]{:S(2)}) collective-permute-start(bf16[8,32,1024]{2,1,0:T(8,128)(2,1)S(1)} %broadcast_select_fusion.refs_5_), channel_id=1, source_target_pairs={{0,16},{16,0},{1,17},{17,1},{2,18},{18,2},{3,19},{19,3},{4,20},{20... | collective-permute-start | bytes 1572872 | tf_op jit(solution)/shard_map/ppermute | solution.py:158
  110.6 1.3 %collective-permute-start.20 = (f32[2,64,256]{2,1,0:T(8,128)S(1)}, f32[2,64,256]{2,1,0:T(8,128)S(1)}, u32[]{:S(2)}, u32[]{:S(2)}) collective-permute-start(f32[2,64,256]{2,1,0:T(8,128)S(1)} %dynamic-slice_bitcast_fusion.1), channel_id=1, source_target_pairs={{0,1},{1,0},{2,3},{3,2},{4,5},{5,4},{6,7},{7,6},{8,9},{9,8},{10,11... | collective-permute-start | bytes 393224 | tf_op jit(solution)/shard_map/ppermute | solution.py:158
  112.0 4.3 %collective-permute-start.23 = (f32[1,64,256]{2,1,0:T(8,128)S(1)}, f32[1,64,256]{2,1,0:T(8,128)S(1)}, u32[]{:S(2)}, u32[]{:S(2)}) collective-permute-start(f32[1,64,256]{2,1,0:T(8,128)S(1)} %constant_dynamic-slice_fusion.1), channel_id=1, source_target_pairs={{0,2},{1,3},{2,0},{3,1},{4,6},{5,7},{6,4},{7,5},{8,10},{9,11},{10,... | collective-permute-start | bytes 196616 | tf_op jit(solution)/shard_map/ppermute | solution.py:158
  113.6 11.2 %collective-permute-start.13 = (bf16[5,32,1024]{2,1,0:T(8,128)(2,1)S(1)}, bf16[5,32,1024]{2,1,0:T(8,128)(2,1)S(1)}, u32[]{:S(2)}, u32[]{:S(2)}) collective-permute-start(bf16[5,32,1024]{2,1,0:T(8,128)(2,1)S(1)} %broadcast_select_fusion.3.refs_5_), channel_id=1, source_target_pairs={{0,16},{16,0},{1,17},{17,1},{2,18},{18,2},{3,19},{19,3},{4,20},{20... | collective-permute-start | bytes 983048 | tf_op jit(solution)/shard_map/ppermute | solution.py:158
  113.7 10.5 %collective-permute-start.21 = (bf16[1,64,1024]{2,1,0:T(8,128)(2,1)S(1)}, bf16[1,64,1024]{2,1,0:T(8,128)(2,1)S(1)}, u32[]{:S(2)}, u32[]{:S(2)}) collective-permute-start(bf16[1,64,1024]{2,1,0:T(8,128)(2,1)S(1)} %collective-permute-done.18), channel_id=1, source_target_pairs={{0,4},{4,0},{8,12},{12,8},{1,5},{5,1},{9,13},{13,9},{2,6},{6,2},{1... | collective-permute-start | bytes 393224 | tf_op jit(solution)/shard_map/ppermute | solution.py:158
  116.4 10.8 %collective-permute-start.24 = (f32[64,256]{1,0:T(8,128)S(1)}, f32[64,256]{1,0:T(8,128)S(1)}, u32[]{:S(2)}, u32[]{:S(2)}) collective-permute-start(f32[64,256]{1,0:T(8,128)S(1)} %add_bitcast_fusion), channel_id=1, source_target_pairs={{0,4},{4,0},{8,12},{12,8},{1,5},{5,1},{9,13},{13,9},{2,6},{6,2},{1... | collective-permute-start | bytes 196616 | tf_op jit(solution)/shard_map/ppermute | solution.py:158
  127.1 1.4 %collective-permute-start.25 = (f32[2,64,256]{2,1,0:T(8,128)S(1)}, f32[2,64,256]{2,1,0:T(8,128)S(1)}, u32[]{:S(2)}, u32[]{:S(2)}) collective-permute-start(f32[2,64,256]{2,1,0:T(8,128)S(1)} %dynamic-slice_bitcast_fusion), channel_id=1, source_target_pairs={{0,1},{1,0},{2,3},{3,2},{4,5},{5,4},{6,7},{7,6},{8,9},{9,8},{10,11... | collective-permute-start | bytes 393224 | tf_op jit(solution)/shard_map/ppermute | solution.py:158
  128.6 4.3 %collective-permute-start.26 = (f32[1,64,256]{2,1,0:T(8,128)S(1)}, f32[1,64,256]{2,1,0:T(8,128)S(1)}, u32[]{:S(2)}, u32[]{:S(2)}) collective-permute-start(f32[1,64,256]{2,1,0:T(8,128)S(1)} %constant_dynamic-slice_fusion), channel_id=1, source_target_pairs={{0,2},{1,3},{2,0},{3,1},{4,6},{5,7},{6,4},{7,5},{8,10},{9,11},{10,... | collective-permute-start | bytes 196616 | tf_op jit(solution)/shard_map/ppermute | solution.py:158
  (2 other events, 9.8 us)

commit v6 on v0

v6 whole, which is shorter than its diff:
```python
import functools

import jax
import jax.numpy as jnp
from jax import lax
from jax.experimental import pallas as pl
from jax.experimental.pallas import tpu as pltpu
from jax.sharding import PartitionSpec as P

CONTRACT = (((1,), (1,)), ((), ()))
A, B, T = 8, 7, 1

GATES = {
    "R3A": ("Y1A",),
    "R1T": ("Y1B",),
    "R2T": ("Y2A",),
    "R3B": ("Y1B",),
    "R3T": ("R3B", "Y2B"),
}


def scores_kernel(n_grp, n_ex, halved, n_rows, has_base, *refs):
    rows, (scale, train) = refs[:n_rows], refs[n_rows : n_rows + 2]
    base = refs[n_rows + 2] if has_base else None
    out, total = refs[-2:]
    step = pl.program_id(0)
    block = jnp.concatenate([r[...] for r in rows], axis=0)
    precond = (block.astype(jnp.float32) * scale[...]).astype(jnp.bfloat16)
    part = lax.dot_general(precond, train[...], CONTRACT, preferred_element_type=jnp.float32)

    @pl.when(step == 0)
    def _():
        total[...] = part

    @pl.when(step > 0)
    def _():
        total[...] += part

    @pl.when(step == pl.num_programs(0) - 1)
    def _():
        ex, grp = lax.axis_index("ex"), lax.axis_index("grp")
        queries = out.shape[0] // n_ex
        half = queries // n_grp
        for b in range(n_ex):
            t = lax.rem(ex + (n_ex - b), n_ex)
            for h in range(n_grp):
                place = h
                if halved and n_grp > 1:
                    place = jnp.where(t == 0, h, lax.rem(h + n_grp - grp, n_grp))
                at = pl.multiple_of(t * queries + place * half, half)
                value = total[pl.ds(at, half), :]
                to = b * queries + h * half
                if has_base:
                    value += base[to : to + half, :]
                out[to : to + half, :] = value


def scores(n_grp, n_ex, test, scale, train, unit, start, received, halved, base=None):
    docs = train.shape[0]
    width = received[0].shape[1]
    column = lambda k: (0, start + k)
    in_specs = [pl.BlockSpec((test.shape[0], unit), column)]
    in_specs += [pl.BlockSpec((r.shape[0], unit), lambda k: (0, k)) for r in received]
    in_specs += [pl.BlockSpec((1, unit), column), pl.BlockSpec((docs, unit), column)]
    operands = [test, *received, scale, train]
    queries = test.shape[0] * n_ex
    if base is not None:
        in_specs.append(pl.BlockSpec((queries, docs), lambda k: (0, 0)))
        operands.append(base)
    return pl.pallas_call(
        functools.partial(
            scores_kernel, n_grp, n_ex, halved, 1 + len(received), base is not None
        ),
        out_shape=jax.ShapeDtypeStruct((queries, docs), jnp.float32),
        grid=(width // unit,),
        in_specs=in_specs,
        out_specs=pl.BlockSpec((queries, docs), lambda k: (0, 0)),
        scratch_shapes=[pltpu.VMEM((queries, docs), jnp.float32)],
        cost_estimate=pl.CostEstimate(
            flops=2 * queries * docs * width,
            bytes_accessed=2 * (queries + docs) * width,
            transcendentals=0,
        ),
        compiler_params=pltpu.CompilerParams(vmem_limit_bytes=16 * 1024 * 1024),
    )(*operands)


def solution(mesh):
    n_grp, n_ex, n_feat = (mesh.shape[a] for a in ("grp", "ex", "feat"))
    assert n_grp <= 2

    def on_device(train, test, hess):
        docs, feats = train.shape
        queries = test.shape[0]
        half = queries // n_grp
        unit = feats // (A + B + T)
        grp, feat = lax.axis_index("grp"), lax.axis_index("feat")
        done = {}

        def send(name, block, axis, pairs):
            waits = [done[g] for g in GATES.get(name, ()) if g in done]
            if waits:
                block = lax.optimization_barrier((block, waits))[0]
            done[name] = lax.ppermute(block, axis, pairs)
            return done[name]

        ring = [(i, (i + 1) % n_ex) for i in range(n_ex)]

        def swap(name, block):
            if n_grp == 1:
                return [block]
            return [block, send(name, block, "grp", [(0, 1), (1, 0)])]

        def sum_over_feat(name, sums):
            held = sums.reshape(n_feat, -1, docs)
            bit = 1
            while bit < n_feat:
                pairs = held.reshape((-1, 2) + held.shape[1:])
                mine = (feat // bit) % 2
                keep = lax.dynamic_index_in_dim(pairs, mine, 1, keepdims=False)
                away = lax.dynamic_index_in_dim(pairs, 1 - mine, 1, keepdims=False)
                partner = [(i, i ^ bit) for i in range(n_feat)]
                held = keep + send(f"{name}{bit}", away, "feat", partner)
                bit *= 2
            return held[0]

        def share(start, width):
            columns = slice(start * unit, (start + width) * unit)
            if n_grp == 1:
                return test[:, columns]
            return jnp.where(grp == 0, test[:half, columns], test[half:, columns])

        chunks = {"A": (0, A), "B": (A, B), "T": (A + B, T)}
        held = {"A": share(0, A), "B": share(A, B), "T": test[:, (A + B) * unit :]}
        got = {name: [] for name in chunks}
        for t in range(1, n_ex):
            for name in chunks:
                held[name] = send(f"R{t}{name}", held[name], "ex", ring)
                got[name] += [held[name]] if name == "T" else swap(f"Y{t}{name}", held[name])

        scale = (1.0 / (hess + jnp.float32(0.1))).reshape(1, feats)
        sums = None
        for name in "ATB":
            sums = scores(
                n_grp, n_ex, test, scale, train, unit, chunks[name][0], got[name],
                halved=name != "T" and n_grp > 1, base=sums,
            )
        return sum_over_feat("Z", sums).T

    return jax.shard_map(
        on_device,
        mesh=mesh,
        in_specs=(P(("grp", "ex"), "feat"), P("ex", "feat"), P("feat")),
        out_specs=P(("grp", "ex"), "feat"),
        check_vma=False,
    )
```

time: 198 us -> 115 us (0.58)
  waiting for transfers between devices: 171 us -> 70.6 us
  starting transfers between devices: 0.04 us -> 16.9 us
  between operations: 13.4 us -> 0.25 us
  Pallas kernels: 0 us -> 13.1 us
  local copies, waits for them, and re-layouts: 0 us -> 10.2 us
  matrix products: 8.85 us -> 0 us
    all_gather x1 -> x0, waiting for transfers between devices: 152 us -> none  [on_device(): lax.all_gather(precond, 'ex', axis=0, tiled=True)]
    ppermute x0 -> x17, waiting for transfers between devices: none -> 70.6 us  [send(): done[name] = lax.ppermute(block, axis, pairs)]
    reduce_scatter x1 -> x0, waiting for transfers between devices: 18.4 us -> none  [on_device(): lax.psum_scatter(partial_sums, 'feat', scatter_dimension=1, tiled=True)]
    ppermute x0 -> x17, starting transfers between devices: none -> 16.9 us  [send(): done[name] = lax.ppermute(block, axis, pairs)]
    pallas_call x0 -> x3, Pallas kernels: none -> 13.1 us  [scores(): pl.pallas_call(functools.partial(scores_kernel, n_grp, n_ex, halved, 1 +...]
    unnamed x0 -> x32, local copies, waits for them, and re-layouts: none -> 10.2 us
    dot_general x1 -> x0, matrix products: 8.85 us -> none  [on_device(): lax.dot_general(train_grads, lax.all_gather(precond, 'ex', axis=0, tiled=...]
    convert_element_type x1 -> x0, other arithmetic: 3.34 us -> none  [on_device(): (test_grads.astype(jnp.float32) * inverse[None, :]).astype(jnp.bfloat16)]
  transfers between devices with their start and end apart: 2 -> 17, of which waited for: 2 -> 9; matrix products, arithmetic and copies ran while one was open for 0% -> 1% of each run, Pallas kernels for 0% -> 7%
where the time goes in v6:
time: 115 us; the launch traced here: 114 us
  waiting for transfers between devices  70.6 us (61%)
  starting transfers between devices  16.9 us (15%)
  Pallas kernels  13.1 us (11%)
  local copies, waits for them, and re-layouts  10.2 us (9%)
  other arithmetic  3.28 us (3%)
    ppermute x17, waiting for transfers between devices, send(): done[name] = lax.ppermute(block, axis, pairs)  70.6 us
    ppermute x17, starting transfers between devices, send(): done[name] = lax.ppermute(block, axis, pairs)  16.9 us
    pallas_call x3, Pallas kernels, scores(): pl.pallas_call(functools.partial(scores_kernel, n_grp, n_ex, halved, 1 +...  13.1 us
    unnamed x32, local copies, waits for them, and re-layouts  10.2 us
    select_n x2, other arithmetic, share(): return jnp.where(grp == 0, test[:half, columns], test[half:, columns])  2.61 us
  transfers between devices with their start and end apart: 17, of which 9 were waited for; matrix products, arithmetic and copies ran while one was open for 1% of the time, Pallas kernels for 7%

profile of v6, /device:TPU:0, one launch (start us, length us, event | category | flops | bytes accessed | tf_op | source)
XLA Modules:
  0.0 114.3 jit_solution(12897801658033231228)
XLA Ops:
  0.0 1.4 %slice_select_fusion = bf16[32,8192]{1,0:T(8,128)(2,1)S(1)} fusion(bf16[64,16384]{1,0:T(8,128)(2,1)} %refs_0_.5, pred[]{:T(512)S(6)} %eq.7), kind=kLoop, calls=%fused_computation | loop fusion | flops 262144 | bytes 1572865 | tf_op jit(solution)/shard_map/jit(_where)/select_n | solution.py:131
  1.4 3.1 %collective-permute-start.7 = (bf16[32,8192]{1,0:T(8,128)(2,1)S(1)}, bf16[32,8192]{1,0:T(8,128)(2,1)S(1)}, u32[]{:S(2)}, u32[]{:S(2)}) collective-permute-start(bf16[32,8192]{1,0:T(8,128)(2,1)S(1)} %slice_select_fusion), channel_id=1, source_target_pairs={{0,4},{4,8},{8,12},{12,0},{1,5},{5,9},{9,13},{13,1},{2,6},{6,10},{... | collective-permute-start | bytes 1572872 | tf_op jit(solution)/shard_map/ppermute | solution.py:104
  4.5 1.2 %slice_select_fusion.1 = bf16[32,7168]{1,0:T(8,128)(2,1)S(1)} fusion(bf16[64,16384]{1,0:T(8,128)(2,1)} %refs_0_.5, pred[]{:T(512)S(6)} %eq.7), kind=kLoop, calls=%fused_computation.1 | loop fusion | flops 229376 | bytes 1376257 | tf_op jit(solution)/shard_map/jit(_where)/select_n | solution.py:131
  5.7 1.6 %collective-permute-start = (bf16[32,7168]{1,0:T(8,128)(2,1)S(1)}, bf16[32,7168]{1,0:T(8,128)(2,1)S(1)}, u32[]{:S(2)}, u32[]{:S(2)}) collective-permute-start(bf16[32,7168]{1,0:T(8,128)(2,1)S(1)} %slice_select_fusion.1), channel_id=1, source_target_pairs={{0,4},{4,8},{8,12},{12,0},{1,5},{5,9},{9,13},{13,1},{2,6},{6,10},{... | collective-permute-start | bytes 1376264 | tf_op jit(solution)/shard_map/ppermute | solution.py:104
  7.3 11.9 %collective-permute-done.7.refs_1_ = bf16[32,8192]{1,0:T(8,128)(2,1)S(1)} collective-permute-done((bf16[32,8192]{1,0:T(8,128)(2,1)S(1)}, bf16[32,8192]{1,0:T(8,128)(2,1)S(1)}, u32[]{:S(2)}, u32[]{:S(2)}) %collective-permute-start.7) | collective-permute-done | bytes 524320 | tf_op jit(solution)/shard_map/ppermute | solution.py:104
  19.3 1.7 %collective-permute-start.12 = (bf16[32,8192]{1,0:T(8,128)(2,1)S(1)}, bf16[32,8192]{1,0:T(8,128)(2,1)S(1)}, u32[]{:S(2)}, u32[]{:S(2)}) collective-permute-start(bf16[32,8192]{1,0:T(8,128)(2,1)S(1)} %collective-permute-done.7.refs_1_), channel_id=1, source_target_pairs={{0,16},{16,0},{1,17},{17,1},{2,18},{18,2},{3,19},{19,3},{4,20},{20... | collective-permute-start | bytes 1572872 | tf_op jit(solution)/shard_map/ppermute | solution.py:104
  21.0 8.1 %collective-permute-done.refs_1_ = bf16[32,7168]{1,0:T(8,128)(2,1)S(1)} collective-permute-done((bf16[32,7168]{1,0:T(8,128)(2,1)S(1)}, bf16[32,7168]{1,0:T(8,128)(2,1)S(1)}, u32[]{:S(2)}, u32[]{:S(2)}) %collective-permute-start) | collective-permute-done | bytes 458784 | tf_op jit(solution)/shard_map/ppermute | solution.py:104
  29.1 1.8 %collective-permute-start.1 = (bf16[32,7168]{1,0:T(8,128)(2,1)S(1)}, bf16[32,7168]{1,0:T(8,128)(2,1)S(1)}, u32[]{:S(2)}, u32[]{:S(2)}) collective-permute-start(bf16[32,7168]{1,0:T(8,128)(2,1)S(1)} %collective-permute-done.refs_1_), channel_id=1, source_target_pairs={{0,16},{16,0},{1,17},{17,1},{2,18},{18,2},{3,19},{19,3},{4,20},{20... | collective-permute-start | bytes 1376264 | tf_op jit(solution)/shard_map/ppermute | solution.py:104
  30.9 0.8 copy-done.7
  31.7 8.7 %collective-permute-done.8.refs_3_ = bf16[32,8192]{1,0:T(8,128)(2,1)S(1)} collective-permute-done((bf16[32,8192]{1,0:T(8,128)(2,1)S(1)}, bf16[32,8192]{1,0:T(8,128)(2,1)S(1)}, u32[]{:S(2)}, u32[]{:S(2)}) %collective-permute-start.8) | collective-permute-done | bytes 524320 | tf_op jit(solution)/shard_map/ppermute | solution.py:104
  40.3 1.8 %collective-permute-start.9 = (bf16[32,8192]{1,0:T(8,128)(2,1)S(1)}, bf16[32,8192]{1,0:T(8,128)(2,1)S(1)}, u32[]{:S(2)}, u32[]{:S(2)}) collective-permute-start(bf16[32,8192]{1,0:T(8,128)(2,1)S(1)} %collective-permute-done.8.refs_3_), channel_id=1, source_target_pairs={{0,16},{16,0},{1,17},{17,1},{2,18},{18,2},{3,19},{19,3},{4,20},{20... | collective-permute-start | bytes 1572872 | tf_op jit(solution)/shard_map/ppermute | solution.py:104
  42.1 0.8 copy-done.3
  42.9 0.8 copy-done.9
  43.7 6.5 %collective-permute-done.2.refs_3_ = bf16[32,7168]{1,0:T(8,128)(2,1)S(1)} collective-permute-done((bf16[32,7168]{1,0:T(8,128)(2,1)S(1)}, bf16[32,7168]{1,0:T(8,128)(2,1)S(1)}, u32[]{:S(2)}, u32[]{:S(2)}) %collective-permute-start.2) | collective-permute-done | bytes 458784 | tf_op jit(solution)/shard_map/ppermute | solution.py:104
  50.2 1.7 %collective-permute-start.3 = (bf16[32,7168]{1,0:T(8,128)(2,1)S(1)}, bf16[32,7168]{1,0:T(8,128)(2,1)S(1)}, u32[]{:S(2)}, u32[]{:S(2)}) collective-permute-start(bf16[32,7168]{1,0:T(8,128)(2,1)S(1)} %collective-permute-done.2.refs_3_), channel_id=1, source_target_pairs={{0,16},{16,0},{1,17},{17,1},{2,18},{18,2},{3,19},{19,3},{4,20},{20... | collective-permute-start | bytes 1376264 | tf_op jit(solution)/shard_map/ppermute | solution.py:104
  51.9 0.8 copy-done.11
  52.7 1.4 %collective-permute-start.6 = (bf16[64,1024]{1,0:T(8,128)(2,1)S(1)}, bf16[64,1024]{1,0:T(8,128)(2,1)S(1)}, u32[]{:S(2)}, u32[]{:S(2)}) collective-permute-start(bf16[64,1024]{1,0:T(8,128)(2,1)S(1)} %slice.17), channel_id=1, source_target_pairs={{0,4},{4,8},{8,12},{12,0},{1,5},{5,9},{9,13},{13,1},{2,6},{6,10},{... | collective-permute-start | bytes 393224 | tf_op jit(solution)/shard_map/ppermute | solution.py:104
  54.1 19.1 %collective-permute-done.6.refs_1_ = bf16[64,1024]{1,0:T(8,128)(2,1)S(1)} collective-permute-done((bf16[64,1024]{1,0:T(8,128)(2,1)S(1)}, bf16[64,1024]{1,0:T(8,128)(2,1)S(1)}, u32[]{:S(2)}, u32[]{:S(2)}) %collective-permute-start.6) | collective-permute-done | bytes 131104 | tf_op jit(solution)/shard_map/ppermute | solution.py:104
  73.2 0.8 copy-done.5
  74.0 1.5 %collective-permute-start.14 = (bf16[32,8192]{1,0:T(8,128)(2,1)}, bf16[32,8192]{1,0:T(8,128)(2,1)}, u32[]{:S(2)}, u32[]{:S(2)}) collective-permute-start(bf16[32,8192]{1,0:T(8,128)(2,1)} %collective-permute-done.13.refs_5_), channel_id=1, source_target_pairs={{0,16},{16,0},{1,17},{17,1},{2,18},{18,2},{3,19},{19,3},{4,20},{20... | collective-permute-start | bytes 1572872 | tf_op jit(solution)/shard_map/ppermute | solution.py:104
  76.1 0.8 copy-done.13
  76.8 4.0 %collective-permute-done.10.refs_2_ = bf16[64,1024]{1,0:T(8,128)(2,1)S(1)} collective-permute-done((bf16[64,1024]{1,0:T(8,128)(2,1)S(1)}, bf16[64,1024]{1,0:T(8,128)(2,1)S(1)}, u32[]{:S(2)}, u32[]{:S(2)}) %collective-permute-start.10) | collective-permute-done | bytes 131104 | tf_op jit(solution)/shard_map/ppermute | solution.py:104
  80.8 8.4 %collective-permute-done.14.refs_6_ = bf16[32,8192]{1,0:T(8,128)(2,1)} collective-permute-done((bf16[32,8192]{1,0:T(8,128)(2,1)}, bf16[32,8192]{1,0:T(8,128)(2,1)}, u32[]{:S(2)}, u32[]{:S(2)}) %collective-permute-start.14) | collective-permute-done | bytes 524320 | tf_op jit(solution)/shard_map/ppermute | solution.py:104
  89.2 3.4 %copy-done = bf16[256,16384]{1,0:T(8,128)(2,1)S(1)} copy-done((bf16[256,16384]{1,0:T(8,128)(2,1)S(1)}, bf16[256,16384]{1,0:T(8,128)(2,1)}, u32[]{:S(2)}) %copy-start) | copy-done | bytes 8388632
  92.6 1.0 copy-done.4
  93.6 1.0 copy-done.6
  94.7 6.3 %shard_map.37.refs_6_ = f32[256,256]{1,0:T(8,128)S(1)} custom-call(bf16[64,16384]{1,0:T(8,128)(2,1)S(1)} %copy-done.2, bf16[32,8192]{1,0:T(8,128)(2,1)S(1)} %collective-permute-done.7.refs_1_, bf16[32,8192]{1,0:T(8,128)(2,1)S(1)} %copy-done.4, bf16[32,8192]{1,0:T(8,128)(2,1)S(1)} %collective-permute-done.8.refs_3_, bf16[32,8192]{1,0:T(8,128)(2,1)S(1)} %copy-done.6, ...), custom_call_target="tpu_custom_call" | custom-call | flops 1073741824 | bytes 8388608 | tf_op jit(solution)/shard_map/pallas_call | solution.py:70
  101.0 1.4 %shard_map.38.refs_9_ = f32[256,256]{1,0:T(8,128)S(1)} custom-call(bf16[64,16384]{1,0:T(8,128)(2,1)S(1)} %copy-done.2, bf16[64,1024]{1,0:T(8,128)(2,1)S(1)} %collective-permute-done.6.refs_1_, bf16[64,1024]{1,0:T(8,128)(2,1)S(1)} %collective-permute-done.10.refs_2_, bf16[64,1024]{1,0:T(8,128)(2,1)} %collective-permute-done.11.refs_3_, ...), custom_call_target="tpu_custom_call" | custom-call | flops 134217728 | bytes 1048576 | tf_op jit(solution)/shard_map/pallas_call | solution.py:70
  102.5 5.4 %shard_map.39 = f32[256,256]{1,0:T(8,128)S(1)} custom-call(bf16[64,16384]{1,0:T(8,128)(2,1)S(1)} %copy-done.2, bf16[32,7168]{1,0:T(8,128)(2,1)S(1)} %copy-done.8, bf16[32,7168]{1,0:T(8,128)(2,1)S(1)} %copy-done.10, bf16[32,7168]{1,0:T(8,128)(2,1)S(1)} %copy-done.12, bf16[32,7168]{1,0:T(8,128)(2,1)S(1)} %copy-done.14, ...), custom_call_target="tpu_custom_call" | custom-call | flops 939524096 | bytes 7340032 | tf_op jit(solution)/shard_map/pallas_call | solution.py:70
  108.0 1.3 %collective-permute-done.15 = f32[2,64,256]{2,1,0:T(8,128)S(1)} collective-permute-done((f32[2,64,256]{2,1,0:T(8,128)S(1)}, f32[2,64,256]{2,1,0:T(8,128)S(1)}, u32[]{:S(2)}, u32[]{:S(2)}) %collective-permute-start.15) | collective-permute-done | bytes 131104 | tf_op jit(solution)/shard_map/ppermute | solution.py:104
  109.4 1.6 %collective-permute-start.16 = (f32[1,64,256]{2,1,0:T(8,128)S(1)}, f32[1,64,256]{2,1,0:T(8,128)S(1)}, u32[]{:S(2)}, u32[]{:S(2)}) collective-permute-start(f32[1,64,256]{2,1,0:T(8,128)S(1)} %constant_dynamic-slice_fusion), channel_id=1, source_target_pairs={{0,2},{1,3},{2,0},{3,1},{4,6},{5,7},{6,4},{7,5},{8,10},{9,11},{10,... | collective-permute-start | bytes 196616 | tf_op jit(solution)/shard_map/ppermute | solution.py:104
  110.9 2.8 %collective-permute-done.16 = f32[1,64,256]{2,1,0:T(8,128)S(1)} collective-permute-done((f32[1,64,256]{2,1,0:T(8,128)S(1)}, f32[1,64,256]{2,1,0:T(8,128)S(1)}, u32[]{:S(2)}, u32[]{:S(2)}) %collective-permute-start.16) | collective-permute-done | bytes 65568 | tf_op jit(solution)/shard_map/ppermute | solution.py:104
  (45 shorter events, 1.4 us)
Async XLA Ops:
  0.0 52.7 %copy-start.2 = (bf16[64,16384]{1,0:T(8,128)(2,1)S(1)}, bf16[64,16384]{1,0:T(8,128)(2,1)}, u32[]{:S(2)}) copy-start(bf16[64,16384]{1,0:T(8,128)(2,1)} %refs_0_.5) | copy-start | bytes 6291460
  0.0 80.8 %copy-start.15 = (f32[16384]{0:T(1024)S(1)}, f32[16384]{0:T(1024)}, u32[]{:S(2)}) copy-start(f32[16384]{0:T(1024)} %param.5) | copy-start | bytes 196612
  1.4 17.9 %collective-permute-start.7 = (bf16[32,8192]{1,0:T(8,128)(2,1)S(1)}, bf16[32,8192]{1,0:T(8,128)(2,1)S(1)}, u32[]{:S(2)}, u32[]{:S(2)}) collective-permute-start(bf16[32,8192]{1,0:T(8,128)(2,1)S(1)} %slice_select_fusion), channel_id=1, source_target_pairs={{0,4},{4,8},{8,12},{12,0},{1,5},{5,9},{9,13},{13,1},{2,6},{6,10},{... | collective-permute-start | bytes 1572872 | tf_op jit(solution)/shard_map/ppermute | solution.py:104
  5.7 23.4 %collective-permute-start = (bf16[32,7168]{1,0:T(8,128)(2,1)S(1)}, bf16[32,7168]{1,0:T(8,128)(2,1)S(1)}, u32[]{:S(2)}, u32[]{:S(2)}) collective-permute-start(bf16[32,7168]{1,0:T(8,128)(2,1)S(1)} %slice_select_fusion.1), channel_id=1, source_target_pairs={{0,4},{4,8},{8,12},{12,0},{1,5},{5,9},{9,13},{13,1},{2,6},{6,10},{... | collective-permute-start | bytes 1376264 | tf_op jit(solution)/shard_map/ppermute | solution.py:104
  19.3 21.1 %collective-permute-start.8 = (bf16[32,8192]{1,0:T(8,128)(2,1)S(1)}, bf16[32,8192]{1,0:T(8,128)(2,1)S(1)}, u32[]{:S(2)}, u32[]{:S(2)}) collective-permute-start(bf16[32,8192]{1,0:T(8,128)(2,1)S(1)} %collective-permute-done.7.refs_1_), channel_id=1, source_target_pairs={{0,4},{4,8},{8,12},{12,0},{1,5},{5,9},{9,13},{13,1},{2,6},{6,10},{... | collective-permute-start | bytes 1572872 | tf_op jit(solution)/shard_map/ppermute | solution.py:104
  19.3 22.8 %collective-permute-start.12 = (bf16[32,8192]{1,0:T(8,128)(2,1)S(1)}, bf16[32,8192]{1,0:T(8,128)(2,1)S(1)}, u32[]{:S(2)}, u32[]{:S(2)}) collective-permute-start(bf16[32,8192]{1,0:T(8,128)(2,1)S(1)} %collective-permute-done.7.refs_1_), channel_id=1, source_target_pairs={{0,16},{16,0},{1,17},{17,1},{2,18},{18,2},{3,19},{19,3},{4,20},{20... | collective-permute-start | bytes 1572872 | tf_op jit(solution)/shard_map/ppermute | solution.py:104
  29.1 13.8 %collective-permute-start.1 = (bf16[32,7168]{1,0:T(8,128)(2,1)S(1)}, bf16[32,7168]{1,0:T(8,128)(2,1)S(1)}, u32[]{:S(2)}, u32[]{:S(2)}) collective-permute-start(bf16[32,7168]{1,0:T(8,128)(2,1)S(1)} %collective-permute-done.refs_1_), channel_id=1, source_target_pairs={{0,16},{16,0},{1,17},{17,1},{2,18},{18,2},{3,19},{19,3},{4,20},{20... | collective-permute-start | bytes 1376264 | tf_op jit(solution)/shard_map/ppermute | solution.py:104
  30.9 19.3 %collective-permute-start.2 = (bf16[32,7168]{1,0:T(8,128)(2,1)S(1)}, bf16[32,7168]{1,0:T(8,128)(2,1)S(1)}, u32[]{:S(2)}, u32[]{:S(2)}) collective-permute-start(bf16[32,7168]{1,0:T(8,128)(2,1)S(1)} %collective-permute-done.refs_1_), channel_id=1, source_target_pairs={{0,4},{4,8},{8,12},{12,0},{1,5},{5,9},{9,13},{13,1},{2,6},{6,10},{... | collective-permute-start | bytes 1376264 | tf_op jit(solution)/shard_map/ppermute | solution.py:104
  30.9 0.8 copy-start.7
  40.3 32.9 %collective-permute-start.9 = (bf16[32,8192]{1,0:T(8,128)(2,1)S(1)}, bf16[32,8192]{1,0:T(8,128)(2,1)S(1)}, u32[]{:S(2)}, u32[]{:S(2)}) collective-permute-start(bf16[32,8192]{1,0:T(8,128)(2,1)S(1)} %collective-permute-done.8.refs_3_), channel_id=1, source_target_pairs={{0,16},{16,0},{1,17},{17,1},{2,18},{18,2},{3,19},{19,3},{4,20},{20... | collective-permute-start | bytes 1572872 | tf_op jit(solution)/shard_map/ppermute | solution.py:104
  42.1 0.8 copy-start.3
  42.9 31.1 %collective-permute-start.13 = (bf16[32,8192]{1,0:T(8,128)(2,1)S(1)}, bf16[32,8192]{1,0:T(8,128)(2,1)}, u32[]{:S(2)}, u32[]{:S(2)}) collective-permute-start(bf16[32,8192]{1,0:T(8,128)(2,1)S(1)} %collective-permute-done.8.refs_3_), channel_id=1, source_target_pairs={{0,4},{4,8},{8,12},{12,0},{1,5},{5,9},{9,13},{13,1},{2,6},{6,10},{... | collective-permute-start | bytes 1572872 | tf_op jit(solution)/shard_map/ppermute | solution.py:104
  42.9 0.8 copy-start.9
  50.2 25.4 %collective-permute-start.4 = (bf16[32,7168]{1,0:T(8,128)(2,1)S(1)}, bf16[32,7168]{1,0:T(8,128)(2,1)}, u32[]{:S(2)}, u32[]{:S(2)}) collective-permute-start(bf16[32,7168]{1,0:T(8,128)(2,1)S(1)} %collective-permute-done.2.refs_3_), channel_id=1, source_target_pairs={{0,4},{4,8},{8,12},{12,0},{1,5},{5,9},{9,13},{13,1},{2,6},{6,10},{... | collective-permute-start | bytes 1376264 | tf_op jit(solution)/shard_map/ppermute | solution.py:104
  50.2 25.9 %collective-permute-start.3 = (bf16[32,7168]{1,0:T(8,128)(2,1)S(1)}, bf16[32,7168]{1,0:T(8,128)(2,1)S(1)}, u32[]{:S(2)}, u32[]{:S(2)}) collective-permute-start(bf16[32,7168]{1,0:T(8,128)(2,1)S(1)} %collective-permute-done.2.refs_3_), channel_id=1, source_target_pairs={{0,16},{16,0},{1,17},{17,1},{2,18},{18,2},{3,19},{19,3},{4,20},{20... | collective-permute-start | bytes 1376264 | tf_op jit(solution)/shard_map/ppermute | solution.py:104
  51.9 0.8 copy-start.11
  52.7 20.5 %collective-permute-start.6 = (bf16[64,1024]{1,0:T(8,128)(2,1)S(1)}, bf16[64,1024]{1,0:T(8,128)(2,1)S(1)}, u32[]{:S(2)}, u32[]{:S(2)}) collective-permute-start(bf16[64,1024]{1,0:T(8,128)(2,1)S(1)} %slice.17), channel_id=1, source_target_pairs={{0,4},{4,8},{8,12},{12,0},{1,5},{5,9},{9,13},{13,1},{2,6},{6,10},{... | collective-permute-start | bytes 393224 | tf_op jit(solution)/shard_map/ppermute | solution.py:104
  73.2 0.8 copy-start.5
  74.0 6.8 %collective-permute-start.10 = (bf16[64,1024]{1,0:T(8,128)(2,1)S(1)}, bf16[64,1024]{1,0:T(8,128)(2,1)S(1)}, u32[]{:S(2)}, u32[]{:S(2)}) collective-permute-start(bf16[64,1024]{1,0:T(8,128)(2,1)S(1)} %collective-permute-done.6.refs_1_), channel_id=1, source_target_pairs={{0,4},{4,8},{8,12},{12,0},{1,5},{5,9},{9,13},{13,1},{2,6},{6,10},{... | collective-permute-start | bytes 393224 | tf_op jit(solution)/shard_map/ppermute | solution.py:104
  74.0 15.2 %collective-permute-start.14 = (bf16[32,8192]{1,0:T(8,128)(2,1)}, bf16[32,8192]{1,0:T(8,128)(2,1)}, u32[]{:S(2)}, u32[]{:S(2)}) collective-permute-start(bf16[32,8192]{1,0:T(8,128)(2,1)} %collective-permute-done.13.refs_5_), channel_id=1, source_target_pairs={{0,16},{16,0},{1,17},{17,1},{2,18},{18,2},{3,19},{19,3},{4,20},{20... | collective-permute-start | bytes 1572872 | tf_op jit(solution)/shard_map/ppermute | solution.py:104
  75.5 26.9 %collective-permute-start.5 = (bf16[32,7168]{1,0:T(8,128)(2,1)}, bf16[32,7168]{1,0:T(8,128)(2,1)}, u32[]{:S(2)}, u32[]{:S(2)}) collective-permute-start(bf16[32,7168]{1,0:T(8,128)(2,1)} %collective-permute-done.4.refs_5_), channel_id=1, source_target_pairs={{0,16},{16,0},{1,17},{17,1},{2,18},{18,2},{3,19},{19,3},{4,20},{20... | collective-permute-start | bytes 1376264 | tf_op jit(solution)/shard_map/ppermute | solution.py:104
  80.8 20.2 %collective-permute-start.11 = (bf16[64,1024]{1,0:T(8,128)(2,1)S(1)}, bf16[64,1024]{1,0:T(8,128)(2,1)}, u32[]{:S(2)}, u32[]{:S(2)}) collective-permute-start(bf16[64,1024]{1,0:T(8,128)(2,1)S(1)} %collective-permute-done.10.refs_2_), channel_id=1, source_target_pairs={{0,4},{4,8},{8,12},{12,0},{1,5},{5,9},{9,13},{13,1},{2,6},{6,10},{... | collective-permute-start | bytes 393224 | tf_op jit(solution)/shard_map/ppermute | solution.py:104
  89.2 3.4 %copy-start = (bf16[256,16384]{1,0:T(8,128)(2,1)S(1)}, bf16[256,16384]{1,0:T(8,128)(2,1)}, u32[]{:S(2)}) copy-start(bf16[256,16384]{1,0:T(8,128)(2,1)} %refs_8_.3) | copy-start | bytes 25165828
  92.6 1.0 copy-start.4
  93.6 1.0 copy-start.6
  94.7 6.3 %copy-start.1 = (bf16[256,16384]{1,0:T(8,128)(2,1)S(1)}, bf16[256,16384]{1,0:T(8,128)(2,1)}, u32[]{:S(2)}) copy-start(bf16[256,16384]{1,0:T(8,128)(2,1)} %refs_8_.3) | copy-start | bytes 25165828
  101.0 1.5 %copy-start.8 = (bf16[32,7168]{1,0:T(8,128)(2,1)S(1)}, bf16[32,7168]{1,0:T(8,128)(2,1)}, u32[]{:S(2)}) copy-start(bf16[32,7168]{1,0:T(8,128)(2,1)} %copy-done.7) | copy-start | bytes 1376260
  101.0 1.5 %copy-start.10 = (bf16[32,7168]{1,0:T(8,128)(2,1)S(1)}, bf16[32,7168]{1,0:T(8,128)(2,1)}, u32[]{:S(2)}) copy-start(bf16[32,7168]{1,0:T(8,128)(2,1)} %copy-done.9) | copy-start | bytes 1376260
  101.0 1.5 %copy-start.12 = (bf16[32,7168]{1,0:T(8,128)(2,1)S(1)}, bf16[32,7168]{1,0:T(8,128)(2,1)}, u32[]{:S(2)}) copy-start(bf16[32,7168]{1,0:T(8,128)(2,1)} %copy-done.11) | copy-start | bytes 1376260
  101.0 1.5 %copy-start.14 = (bf16[32,7168]{1,0:T(8,128)(2,1)S(1)}, bf16[32,7168]{1,0:T(8,128)(2,1)}, u32[]{:S(2)}) copy-start(bf16[32,7168]{1,0:T(8,128)(2,1)} %copy-done.13) | copy-start | bytes 1376260
  107.9 1.4 %collective-permute-start.15 = (f32[2,64,256]{2,1,0:T(8,128)S(1)}, f32[2,64,256]{2,1,0:T(8,128)S(1)}, u32[]{:S(2)}, u32[]{:S(2)}) collective-permute-start(f32[2,64,256]{2,1,0:T(8,128)S(1)} %dynamic-slice_bitcast_fusion), channel_id=1, source_target_pairs={{0,1},{1,0},{2,3},{3,2},{4,5},{5,4},{6,7},{7,6},{8,9},{9,8},{10,11... | collective-permute-start | bytes 393224 | tf_op jit(solution)/shard_map/ppermute | solution.py:104
  109.4 4.3 %collective-permute-start.16 = (f32[1,64,256]{2,1,0:T(8,128)S(1)}, f32[1,64,256]{2,1,0:T(8,128)S(1)}, u32[]{:S(2)}, u32[]{:S(2)}) collective-permute-start(f32[1,64,256]{2,1,0:T(8,128)S(1)} %constant_dynamic-slice_fusion), channel_id=1, source_target_pairs={{0,2},{1,3},{2,0},{3,1},{4,6},{5,7},{6,4},{7,5},{8,10},{9,11},{10,... | collective-permute-start | bytes 196616 | tf_op jit(solution)/shard_map/ppermute | solution.py:104
  (1 other events, 0.8 us)

commit v7 on v0

v7 whole, which is shorter than its diff:
```python
import jax
import jax.numpy as jnp
from jax import lax
from jax.sharding import PartitionSpec as P

CONTRACT = (((1,), (1,)), ((), ()))


def solution(mesh):
    n_grp, n_ex, n_feat = (mesh.shape[a] for a in ("grp", "ex", "feat"))

    def on_device(train, test, hess):
        docs, feats = train.shape
        queries = test.shape[0]
        grp, feat = lax.axis_index("grp"), lax.axis_index("feat")
        share = feats // n_grp
        inverse = 1.0 / (hess + jnp.float32(0.1))
        mine = lax.dynamic_slice_in_dim(test, grp * share, share, axis=1)
        scale = lax.dynamic_slice_in_dim(inverse, grp * share, share, axis=0)
        precond = (mine.astype(jnp.float32) * scale[None, :]).astype(jnp.bfloat16)
        gathered = lax.all_gather(precond, ("grp", "ex"), axis=0, tiled=True)

        sums = jnp.zeros((n_ex * queries, docs), jnp.float32)
        for g in range(n_grp):
            rows = gathered[g * n_ex * queries : (g + 1) * n_ex * queries]
            sums += lax.dot_general(
                rows, train[:, g * share : (g + 1) * share], CONTRACT, preferred_element_type=jnp.float32
            )

        held = sums.reshape(n_feat, -1, docs)
        bit = 1
        while bit < n_feat:
            pairs = held.reshape((-1, 2) + held.shape[1:])
            up = (feat // bit) % 2
            keep = lax.dynamic_index_in_dim(pairs, up, 1, keepdims=False)
            away = lax.dynamic_index_in_dim(pairs, 1 - up, 1, keepdims=False)
            held = keep + lax.ppermute(away, "feat", [(i, i ^ bit) for i in range(n_feat)])
            bit *= 2
        return held[0].T

    return jax.shard_map(
        on_device,
        mesh=mesh,
        in_specs=(P(("grp", "ex"), "feat"), P("ex", "feat"), P("feat")),
        out_specs=P(("grp", "ex"), "feat"),
        check_vma=False,
    )
```

time: 198 us -> 161 us (0.81)
  waiting for transfers between devices: 171 us -> 132 us
    all_gather x1, waiting for transfers between devices: 152 us -> 128 us  [on_device(): gathered = lax.all_gather(precond, ('grp', 'ex'), axis=0, tiled=True)]
    reduce_scatter x1 -> x0, waiting for transfers between devices: 18.4 us -> none  [on_device(): lax.psum_scatter(partial_sums, 'feat', scatter_dimension=1, tiled=True)]
    ppermute x0 -> x2, waiting for transfers between devices: none -> 4.09 us  [on_device(): lax.ppermute(away, 'feat', [(i, i ^ bit) for i in range(n_feat)])]
    dot_general x1 -> x2, matrix products: 8.85 us -> 8.81 us  [on_device(): lax.dot_general(rows, train[:, g * share:(g + 1) * share], CONTRACT, pref...]
  transfers between devices with their start and end apart: 2 -> 3, of which waited for: 2 -> 3; matrix products, arithmetic and copies ran while one was open for 0% -> 0% of each run, Pallas kernels for 0% -> 0%
where the time goes in v7:
time: 161 us
  waiting for transfers between devices  132 us (82%)
  between operations  13.5 us (8%)
  matrix products  8.81 us (5%)
  other arithmetic  3.89 us (2%)
    all_gather x1, waiting for transfers between devices, on_device(): gathered = lax.all_gather(precond, ('grp', 'ex'), axis=0, tiled=True)  128 us
    dot_general x2, matrix products, on_device(): lax.dot_general(rows, train[:, g * share:(g + 1) * share], CONTRACT, pref...  8.81 us
    ppermute x2, waiting for transfers between devices, on_device(): lax.ppermute(away, 'feat', [(i, i ^ bit) for i in range(n_feat)])  4.09 us
  transfers between devices with their start and end apart: 3, of which 3 were waited for; matrix products, arithmetic and copies ran while one was open for 0% of the time, Pallas kernels for 0%

profile of v7, /device:TPU:0, one launch (start us, length us, event | category | flops | bytes accessed | tf_op | source)
XLA Modules:
  0.0 160.7 jit_solution(5738949440205894683)
XLA Ops:
  6.5 0.0 all-gather.2.cloned.1.call-start
  6.5 0.8 fusion.11
  7.3 2.5 %multiply_convert_fusion = bf16[64,8192]{1,0:T(8,128)(2,1)} fusion(f32[8192]{0:T(1024)S(1)} %fusion.11, bf16[64,16384]{1,0:T(8,128)(2,1)} %param.4, s32[]{:T(128)S(6)} %select_n.34), kind=kLoop, calls=%fused_computation.6 | loop fusion | flops 1572864 | bytes 2129924 | tf_op jit(solution)/shard_map/convert_element_type | solution.py:20
  9.8 0.0 all-gather.2.cloned.1.call-update
  9.8 127.8 %all-gather.2.cloned.1.call-done = bf16[512,8192]{1,0:T(8,128)(2,1)} async-done(((bf16[64,8192]{1,0:T(8,128)(2,1)}), bf16[512,8192]{1,0:T(8,128)(2,1)}) %all-gather.2.cloned.1.call-update) | async-done | bytes 8388624 | tf_op jit(solution)/shard_map/all_gather | solution.py:21
  137.6 0.0 copy-start
  137.6 4.9 %fusion = f32[256,256]{1,0:T(8,128)S(1)} fusion(bf16[512,8192]{1,0:T(8,128)(2,1)} %all-gather.2.cloned.1.call-done, bf16[256,16384]{1,0:T(8,128)(2,1)} %param.3), kind=kOutput, calls=%fused_computation | convolution fusion | flops 1073741824 | bytes 8650752 | tf_op jit(solution)/shard_map/dot_general | solution.py:26
  142.5 1.0 copy-done
  143.4 3.9 %fusion.6 = f32[256,256]{1,0:T(8,128)S(1)} fusion(f32[256,256]{1,0:T(8,128)S(1)} %fusion, bf16[256,16384]{1,0:T(8,128)(2,1)S(1)} %copy-done, bf16[512,8192]{1,0:T(8,128)(2,1)} %all-gather.2.cloned.1.call-done), kind=kOutput, calls=%fused_computation.7 | convolution fusion | flops 1073807360 | bytes 8912896 | tf_op jit(solution)/shard_map/dot_general | solution.py:26
  147.4 0.1 collective-permute-start
  147.5 1.3 collective-permute-done
  148.8 1.5 collective-permute-start.1
  150.4 2.8 %collective-permute-done.1 = f32[1,64,256]{2,1,0:T(8,128)S(1)} collective-permute-done((f32[1,64,256]{2,1,0:T(8,128)S(1)}, f32[1,64,256]{2,1,0:T(8,128)S(1)}, u32[]{:S(2)}, u32[]{:S(2)}) %collective-permute-start.1) | collective-permute-done | bytes 65568 | tf_op jit(solution)/shard_map/ppermute | solution.py:37
  153.2 0.6 add_bitcast_fusion
  (3 shorter events, 0.0 us)
Async XLA Ops:
  6.5 131.0 %all-gather.2.cloned.1.call-start = ((), (), s32[]{:S(2)}) async-start(), calls=%async_computation | async-start | bytes 9437184 | tf_op jit(solution)/shard_map/all_gather | solution.py:21
  137.6 5.8 %copy-start = (bf16[256,16384]{1,0:T(8,128)(2,1)S(1)}, bf16[256,16384]{1,0:T(8,128)(2,1)}, u32[]{:S(2)}) copy-start(bf16[256,16384]{1,0:T(8,128)(2,1)} %param.3) | copy-start | bytes 25165828
  147.4 1.4 collective-permute-start
  148.8 4.3 %collective-permute-start.1 = (f32[1,64,256]{2,1,0:T(8,128)S(1)}, f32[1,64,256]{2,1,0:T(8,128)S(1)}, u32[]{:S(2)}, u32[]{:S(2)}) collective-permute-start(f32[1,64,256]{2,1,0:T(8,128)S(1)} %constant_dynamic-slice_fusion), channel_id=1, source_target_pairs={{0,2},{1,3},{2,0},{3,1},{4,6},{5,7},{6,4},{7,5},{8,10},{9,11},{10,... | collective-permute-start | bytes 196616 | tf_op jit(solution)/shard_map/ppermute | solution.py:37
Sparse Core Ops, SparseCore 0:
  9.9 127.6 all-gather.1

commit v8 on v0

v8 whole, which is shorter than its diff:
```python
import functools

import jax
import jax.numpy as jnp
from jax import lax
from jax.experimental import pallas as pl
from jax.experimental.pallas import tpu as pltpu
from jax.sharding import PartitionSpec as P

CONTRACT = (((1,), (1,)), ((), ()))
CHUNKS = (4, 4, 4, 4)


def scores_kernel(n_grp, n_ex, start, unit, n_rows, has_base, last, *refs):
    test, *received = refs[:n_rows]
    scale, train = refs[n_rows : n_rows + 2]
    out = refs[-2] if last else refs[-1]
    total = refs[-1]
    width = received[0].shape[1]
    sums = refs[n_rows + 2][...] if has_base else None
    for at in range(0, width, unit):
        here, there = slice(at, at + unit), slice(start + at, start + at + unit)
        block = jnp.concatenate([test[:, there]] + [r[:, here] for r in received], axis=0)
        precond = (block.astype(jnp.float32) * scale[:, there]).astype(jnp.bfloat16)
        part = lax.dot_general(
            precond, train[:, there], CONTRACT, preferred_element_type=jnp.float32
        )
        sums = part if sums is None else sums + part
    total[...] = sums
    if last:
        ex, grp = lax.axis_index("ex"), lax.axis_index("grp")
        queries = test.shape[0]
        half = queries // n_grp
        for b in range(n_ex):
            t = lax.rem(ex + (n_ex - b), n_ex)
            for h in range(n_grp):
                place = jnp.where(t == 0, h, lax.rem(h + n_grp - grp, n_grp))
                at = pl.multiple_of(t * queries + place * half, half)
                to = b * queries + h * half
                out[to : to + half, :] = total[pl.ds(at, half), :]


def scores(n_grp, n_ex, test, scale, train, start, unit, received, base, last):
    docs, width = train.shape[0], received[0].shape[1]
    queries = test.shape[0] * n_ex
    operands = [test, *received, scale, train] + ([] if base is None else [base])
    shape = (queries, docs)
    return pl.pallas_call(
        functools.partial(
            scores_kernel, n_grp, n_ex, start, unit, 1 + len(received), base is not None, last
        ),
        out_shape=jax.ShapeDtypeStruct(shape, jnp.float32),
        in_specs=[pl.BlockSpec(memory_space=pltpu.VMEM)] * len(operands),
        out_specs=pl.BlockSpec(memory_space=pltpu.VMEM),
        scratch_shapes=[pltpu.VMEM(shape, jnp.float32)] if last else [],
        cost_estimate=pl.CostEstimate(
            flops=2 * queries * docs * width,
            bytes_accessed=2 * (queries + docs) * width,
            transcendentals=0,
        ),
        compiler_params=pltpu.CompilerParams(vmem_limit_bytes=24 * 1024 * 1024),
    )(*operands)


def solution(mesh):
    n_grp, n_ex, n_feat = (mesh.shape[a] for a in ("grp", "ex", "feat"))
    assert n_grp <= 2

    def on_device(train, test, hess):
        docs, feats = train.shape
        queries = test.shape[0]
        half = queries // n_grp
        unit = feats // sum(CHUNKS)
        grp, feat = lax.axis_index("grp"), lax.axis_index("feat")
        ring = [(i, (i + 1) % n_ex) for i in range(n_ex)]
        hops, swaps = [], []

        def after(block, *waits):
            return lax.optimization_barrier((block, waits))[0] if waits else block

        def hop(block):
            hops.append(lax.ppermute(after(block, *hops[-2:-1], *swaps[-4:-3]), "ex", ring))
            return hops[-1]

        def swap(block):
            if n_grp == 1:
                return [block]
            swaps.append(lax.ppermute(after(block, *swaps[-2:-1]), "grp", [(0, 1), (1, 0)]))
            return [block, swaps[-1]]

        def sum_over_feat(sums):
            held = sums.reshape(n_feat, -1, docs)
            bit = 1
            while bit < n_feat:
                pairs = held.reshape((-1, 2) + held.shape[1:])
                mine = (feat // bit) % 2
                keep = lax.dynamic_index_in_dim(pairs, mine, 1, keepdims=False)
                away = lax.dynamic_index_in_dim(pairs, 1 - mine, 1, keepdims=False)
                held = keep + lax.ppermute(away, "feat", [(i, i ^ bit) for i in range(n_feat)])
                bit *= 2
            return held[0]

        def share(start, width):
            columns = slice(start, start + width)
            if n_grp == 1:
                return test[:, columns]
            return jnp.where(grp == 0, test[:half, columns], test[half:, columns])

        starts, at = [], 0
        for width in CHUNKS:
            starts.append(at)
            at += width * unit
        held = [share(start, width * unit) for start, width in zip(starts, CHUNKS)]
        got = [[] for _ in CHUNKS]
        for t in range(1, n_ex):
            for c in range(len(CHUNKS)):
                held[c] = hop(held[c])
                got[c] += swap(held[c])

        scale = (1.0 / (hess + jnp.float32(0.1))).reshape(1, feats)
        sums = None
        for c, start in enumerate(starts):
            sums = scores(
                n_grp, n_ex, test, scale, train, start, unit, got[c], sums, c == len(CHUNKS) - 1
            )
        return sum_over_feat(sums).T

    return jax.shard_map(
        on_device,
        mesh=mesh,
        in_specs=(P(("grp", "ex"), "feat"), P("ex", "feat"), P("feat")),
        out_specs=P(("grp", "ex"), "feat"),
        check_vma=False,
    )
```

time: 198 us -> 102 us (0.52)
  waiting for transfers between devices: 171 us -> 44.5 us
  starting transfers between devices: 0.04 us -> 28 us
  local copies, waits for them, and re-layouts: 0 us -> 21.1 us
  between operations: 13.4 us -> 0.28 us
  matrix products: 8.85 us -> 0 us
  Pallas kernels: 0 us -> 5.06 us
    all_gather x1 -> x0, waiting for transfers between devices: 152 us -> none  [on_device(): lax.all_gather(precond, 'ex', axis=0, tiled=True)]
    ppermute x0 -> x26, waiting for transfers between devices: none -> 44.5 us  [the longest x12 39.7 us: hop(): lax.ppermute(after(block, *hops[-2:-1], *swaps[-4:-3]), 'ex', ring)]
    ppermute x0 -> x26, starting transfers between devices: none -> 28 us  [the longest x12 19 us: swap(): lax.ppermute(after(block, *swaps[-2:-1]), 'grp', [(0, 1), (1, 0)])]
    unnamed x0 -> x68, local copies, waits for them, and re-layouts: none -> 21 us
    reduce_scatter x1 -> x0, waiting for transfers between devices: 18.4 us -> none  [on_device(): lax.psum_scatter(partial_sums, 'feat', scatter_dimension=1, tiled=True)]
    dot_general x1 -> x0, matrix products: 8.85 us -> none  [on_device(): lax.dot_general(train_grads, lax.all_gather(precond, 'ex', axis=0, tiled=...]
    pallas_call x0 -> x4, Pallas kernels: none -> 5.06 us  [scores(): pl.pallas_call(functools.partial(scores_kernel, n_grp, n_ex, start, unit,...]
    convert_element_type x1 -> x0, other arithmetic: 3.34 us -> none  [on_device(): (test_grads.astype(jnp.float32) * inverse[None, :]).astype(jnp.bfloat16)]
  transfers between devices with their start and end apart: 2 -> 26, of which waited for: 2 -> 15; matrix products, arithmetic and copies ran while one was open for 0% -> 0% of each run, Pallas kernels for 0% -> 3%
where the time goes in v8:
time: 102 us; the launch traced here: 101 us
  waiting for transfers between devices  44.5 us (44%)
  starting transfers between devices  28 us (27%)
  local copies, waits for them, and re-layouts  21.1 us (21%)
  Pallas kernels  5.06 us (5%)
  other arithmetic  2.45 us (2%)
    ppermute x12, waiting for transfers between devices, hop(): lax.ppermute(after(block, *hops[-2:-1], *swaps[-4:-3]), 'ex', ring)  39.7 us
    unnamed x68, local copies, waits for them, and re-layouts  21 us
    ppermute x12, starting transfers between devices, swap(): lax.ppermute(after(block, *swaps[-2:-1]), 'grp', [(0, 1), (1, 0)])  19 us
    ppermute x12, starting transfers between devices, hop(): lax.ppermute(after(block, *hops[-2:-1], *swaps[-4:-3]), 'ex', ring)  7.42 us
    pallas_call x4, Pallas kernels, scores(): pl.pallas_call(functools.partial(scores_kernel, n_grp, n_ex, start, unit,...  5.06 us
    ppermute x2, waiting for transfers between devices, sum_over_feat(): lax.ppermute(away, 'feat', [(i, i ^ bit) for i in range(n_feat)])  4.07 us
  transfers between devices with their start and end apart: 26, of which 15 were waited for; matrix products, arithmetic and copies ran while one was open for 0% of the time, Pallas kernels for 3%

profile of v8, /device:TPU:0, one launch (start us, length us, event | category | flops | bytes accessed | tf_op | source)
XLA Modules:
  0.0 101.4 jit_solution(10254593545719453340)
XLA Ops:
  0.0 1.8 %slice_select_fusion = (bf16[32,4096]{1,0:T(8,128)(2,1)S(1)}, bf16[32,4096]{1,0:T(8,128)(2,1)S(1)}, bf16[32,4096]{1,0:T(8,128)(2,1)S(1)}, bf16[32,4096]{1,0:T(8,128)(2,1)S(1)}) fusion(bf16[64,16384]{1,0:T(8,128)(2,1)} %refs_0_.7, pred[]{:T(512)S(6)} %eq.4), kind=kLoop, calls=%fused_computation | loop fusion | flops 524288 | bytes 3145729 | tf_op jit(solution)/shard_map/jit(_where)/select_n | solution.py:107
  1.8 3.1 %collective-permute-start.12 = (bf16[32,4096]{1,0:T(8,128)(2,1)S(1)}, bf16[32,4096]{1,0:T(8,128)(2,1)S(1)}, u32[]{:S(2)}, u32[]{:S(2)}) collective-permute-start(bf16[32,4096]{1,0:T(8,128)(2,1)S(1)} %get-tuple-element.45), channel_id=1, source_target_pairs={{0,4},{4,8},{8,12},{12,0},{1,5},{5,9},{9,13},{13,1},{2,6},{6,10},{... | collective-permute-start | bytes 786440 | tf_op jit(solution)/shard_map/ppermute | solution.py:82
  4.9 1.6 %collective-permute-start = (bf16[32,4096]{1,0:T(8,128)(2,1)S(1)}, bf16[32,4096]{1,0:T(8,128)(2,1)S(1)}, u32[]{:S(2)}, u32[]{:S(2)}) collective-permute-start(bf16[32,4096]{1,0:T(8,128)(2,1)S(1)} %get-tuple-element.47), channel_id=1, source_target_pairs={{0,4},{4,8},{8,12},{12,0},{1,5},{5,9},{9,13},{13,1},{2,6},{6,10},{... | collective-permute-start | bytes 786440 | tf_op jit(solution)/shard_map/ppermute | solution.py:82
  6.4 7.6 %collective-permute-done.12.refs_1_ = bf16[32,4096]{1,0:T(8,128)(2,1)S(1)} collective-permute-done((bf16[32,4096]{1,0:T(8,128)(2,1)S(1)}, bf16[32,4096]{1,0:T(8,128)(2,1)S(1)}, u32[]{:S(2)}, u32[]{:S(2)}) %collective-permute-start.12) | collective-permute-done | bytes 262176 | tf_op jit(solution)/shard_map/ppermute | solution.py:82
  14.1 1.7 %collective-permute-start.14 = (bf16[32,4096]{1,0:T(8,128)(2,1)S(1)}, bf16[32,4096]{1,0:T(8,128)(2,1)S(1)}, u32[]{:S(2)}, u32[]{:S(2)}) collective-permute-start(bf16[32,4096]{1,0:T(8,128)(2,1)S(1)} %collective-permute-done.12.refs_1_), channel_id=1, source_target_pairs={{0,16},{16,0},{1,17},{17,1},{2,18},{18,2},{3,19},{19,3},{4,20},{20... | collective-permute-start | bytes 786440 | tf_op jit(solution)/shard_map/ppermute | solution.py:88
  15.8 3.8 %collective-permute-done.refs_1_ = bf16[32,4096]{1,0:T(8,128)(2,1)S(1)} collective-permute-done((bf16[32,4096]{1,0:T(8,128)(2,1)S(1)}, bf16[32,4096]{1,0:T(8,128)(2,1)S(1)}, u32[]{:S(2)}, u32[]{:S(2)}) %collective-permute-start) | collective-permute-done | bytes 262176 | tf_op jit(solution)/shard_map/ppermute | solution.py:82
  19.7 1.7 %collective-permute-start.2 = (bf16[32,4096]{1,0:T(8,128)(2,1)S(1)}, bf16[32,4096]{1,0:T(8,128)(2,1)S(1)}, u32[]{:S(2)}, u32[]{:S(2)}) collective-permute-start(bf16[32,4096]{1,0:T(8,128)(2,1)S(1)} %collective-permute-done.refs_1_), channel_id=1, source_target_pairs={{0,16},{16,0},{1,17},{17,1},{2,18},{18,2},{3,19},{19,3},{4,20},{20... | collective-permute-start | bytes 786440 | tf_op jit(solution)/shard_map/ppermute | solution.py:88
  21.4 3.8 %collective-permute-done.13.refs_1_ = bf16[32,4096]{1,0:T(8,128)(2,1)S(1)} collective-permute-done((bf16[32,4096]{1,0:T(8,128)(2,1)S(1)}, bf16[32,4096]{1,0:T(8,128)(2,1)S(1)}, u32[]{:S(2)}, u32[]{:S(2)}) %collective-permute-start.13) | collective-permute-done | bytes 262176 | tf_op jit(solution)/shard_map/ppermute | solution.py:82
  25.3 1.7 %collective-permute-start.15 = (bf16[32,4096]{1,0:T(8,128)(2,1)S(1)}, bf16[32,4096]{1,0:T(8,128)(2,1)S(1)}, u32[]{:S(2)}, u32[]{:S(2)}) collective-permute-start(bf16[32,4096]{1,0:T(8,128)(2,1)S(1)} %collective-permute-done.13.refs_1_), channel_id=1, source_target_pairs={{0,16},{16,0},{1,17},{17,1},{2,18},{18,2},{3,19},{19,3},{4,20},{20... | collective-permute-start | bytes 786440 | tf_op jit(solution)/shard_map/ppermute | solution.py:88
  27.0 3.8 %collective-permute-done.1.refs_1_ = bf16[32,4096]{1,0:T(8,128)(2,1)S(1)} collective-permute-done((bf16[32,4096]{1,0:T(8,128)(2,1)S(1)}, bf16[32,4096]{1,0:T(8,128)(2,1)S(1)}, u32[]{:S(2)}, u32[]{:S(2)}) %collective-permute-start.1) | collective-permute-done | bytes 262176 | tf_op jit(solution)/shard_map/ppermute | solution.py:82
  31.6 1.7 %collective-permute-start.3 = (bf16[32,4096]{1,0:T(8,128)(2,1)S(1)}, bf16[32,4096]{1,0:T(8,128)(2,1)S(1)}, u32[]{:S(2)}, u32[]{:S(2)}) collective-permute-start(bf16[32,4096]{1,0:T(8,128)(2,1)S(1)} %collective-permute-done.1.refs_1_), channel_id=1, source_target_pairs={{0,16},{16,0},{1,17},{17,1},{2,18},{18,2},{3,19},{19,3},{4,20},{20... | collective-permute-start | bytes 786440 | tf_op jit(solution)/shard_map/ppermute | solution.py:88
  33.3 3.2 %collective-permute-done.16.refs_3_ = bf16[32,4096]{1,0:T(8,128)(2,1)S(1)} collective-permute-done((bf16[32,4096]{1,0:T(8,128)(2,1)S(1)}, bf16[32,4096]{1,0:T(8,128)(2,1)S(1)}, u32[]{:S(2)}, u32[]{:S(2)}) %collective-permute-start.16) | collective-permute-done | bytes 262176 | tf_op jit(solution)/shard_map/ppermute | solution.py:82
  37.2 1.7 %collective-permute-start.18 = (bf16[32,4096]{1,0:T(8,128)(2,1)S(1)}, bf16[32,4096]{1,0:T(8,128)(2,1)S(1)}, u32[]{:S(2)}, u32[]{:S(2)}) collective-permute-start(bf16[32,4096]{1,0:T(8,128)(2,1)S(1)} %collective-permute-done.16.refs_3_), channel_id=1, source_target_pairs={{0,16},{16,0},{1,17},{17,1},{2,18},{18,2},{3,19},{19,3},{4,20},{20... | collective-permute-start | bytes 786440 | tf_op jit(solution)/shard_map/ppermute | solution.py:88
  39.0 3.4 %collective-permute-done.4.refs_3_ = bf16[32,4096]{1,0:T(8,128)(2,1)S(1)} collective-permute-done((bf16[32,4096]{1,0:T(8,128)(2,1)S(1)}, bf16[32,4096]{1,0:T(8,128)(2,1)S(1)}, u32[]{:S(2)}, u32[]{:S(2)}) %collective-permute-start.4) | collective-permute-done | bytes 262176 | tf_op jit(solution)/shard_map/ppermute | solution.py:82
  43.2 1.8 %collective-permute-start.6 = (bf16[32,4096]{1,0:T(8,128)(2,1)S(1)}, bf16[32,4096]{1,0:T(8,128)(2,1)S(1)}, u32[]{:S(2)}, u32[]{:S(2)}) collective-permute-start(bf16[32,4096]{1,0:T(8,128)(2,1)S(1)} %collective-permute-done.4.refs_3_), channel_id=1, source_target_pairs={{0,16},{16,0},{1,17},{17,1},{2,18},{18,2},{3,19},{19,3},{4,20},{20... | collective-permute-start | bytes 786440 | tf_op jit(solution)/shard_map/ppermute | solution.py:88
  44.9 3.3 %collective-permute-done.17.refs_3_ = bf16[32,4096]{1,0:T(8,128)(2,1)S(1)} collective-permute-done((bf16[32,4096]{1,0:T(8,128)(2,1)S(1)}, bf16[32,4096]{1,0:T(8,128)(2,1)S(1)}, u32[]{:S(2)}, u32[]{:S(2)}) %collective-permute-start.17) | collective-permute-done | bytes 262176 | tf_op jit(solution)/shard_map/ppermute | solution.py:82
  49.7 1.8 %collective-permute-start.19 = (bf16[32,4096]{1,0:T(8,128)(2,1)S(1)}, bf16[32,4096]{1,0:T(8,128)(2,1)S(1)}, u32[]{:S(2)}, u32[]{:S(2)}) collective-permute-start(bf16[32,4096]{1,0:T(8,128)(2,1)S(1)} %collective-permute-done.17.refs_3_), channel_id=1, source_target_pairs={{0,16},{16,0},{1,17},{17,1},{2,18},{18,2},{3,19},{19,3},{4,20},{20... | collective-permute-start | bytes 786440 | tf_op jit(solution)/shard_map/ppermute | solution.py:88
  51.4 2.8 %collective-permute-done.5.refs_3_ = bf16[32,4096]{1,0:T(8,128)(2,1)S(1)} collective-permute-done((bf16[32,4096]{1,0:T(8,128)(2,1)S(1)}, bf16[32,4096]{1,0:T(8,128)(2,1)S(1)}, u32[]{:S(2)}, u32[]{:S(2)}) %collective-permute-start.5) | collective-permute-done | bytes 262176 | tf_op jit(solution)/shard_map/ppermute | solution.py:82
  55.7 1.8 %collective-permute-start.7 = (bf16[32,4096]{1,0:T(8,128)(2,1)S(1)}, bf16[32,4096]{1,0:T(8,128)(2,1)S(1)}, u32[]{:S(2)}, u32[]{:S(2)}) collective-permute-start(bf16[32,4096]{1,0:T(8,128)(2,1)S(1)} %collective-permute-done.5.refs_3_), channel_id=1, source_target_pairs={{0,16},{16,0},{1,17},{17,1},{2,18},{18,2},{3,19},{19,3},{4,20},{20... | collective-permute-start | bytes 786440 | tf_op jit(solution)/shard_map/ppermute | solution.py:88
  57.4 2.6 %collective-permute-done.20.refs_5_ = bf16[32,4096]{1,0:T(8,128)(2,1)S(1)} collective-permute-done((bf16[32,4096]{1,0:T(8,128)(2,1)S(1)}, bf16[32,4096]{1,0:T(8,128)(2,1)S(1)}, u32[]{:S(2)}, u32[]{:S(2)}) %collective-permute-start.20) | collective-permute-done | bytes 262176 | tf_op jit(solution)/shard_map/ppermute | solution.py:82
  60.7 1.8 %collective-permute-start.22 = (bf16[32,4096]{1,0:T(8,128)(2,1)S(1)}, bf16[32,4096]{1,0:T(8,128)(2,1)S(1)}, u32[]{:S(2)}, u32[]{:S(2)}) collective-permute-start(bf16[32,4096]{1,0:T(8,128)(2,1)S(1)} %collective-permute-done.20.refs_5_), channel_id=1, source_target_pairs={{0,16},{16,0},{1,17},{17,1},{2,18},{18,2},{3,19},{19,3},{4,20},{20... | collective-permute-start | bytes 786440 | tf_op jit(solution)/shard_map/ppermute | solution.py:88
  66.8 1.5 %collective-permute-start.10 = (bf16[32,4096]{1,0:T(8,128)(2,1)S(1)}, bf16[32,4096]{1,0:T(8,128)(2,1)S(1)}, u32[]{:S(2)}, u32[]{:S(2)}) collective-permute-start(bf16[32,4096]{1,0:T(8,128)(2,1)S(1)} %collective-permute-done.8.refs_5_), channel_id=1, source_target_pairs={{0,16},{16,0},{1,17},{17,1},{2,18},{18,2},{3,19},{19,3},{4,20},{20... | collective-permute-start | bytes 786440 | tf_op jit(solution)/shard_map/ppermute | solution.py:88
  69.1 1.6 %collective-permute-start.9 = (bf16[32,4096]{1,0:T(8,128)(2,1)S(1)}, bf16[32,4096]{1,0:T(8,128)(2,1)}, u32[]{:S(2)}, u32[]{:S(2)}) collective-permute-start(bf16[32,4096]{1,0:T(8,128)(2,1)S(1)} %collective-permute-done.5.refs_3_), channel_id=1, source_target_pairs={{0,4},{4,8},{8,12},{12,0},{1,5},{5,9},{9,13},{13,1},{2,6},{6,10},{... | collective-permute-start | bytes 786440 | tf_op jit(solution)/shard_map/ppermute | solution.py:82
  72.1 3.6 %collective-permute-done.21.refs_5_ = bf16[32,4096]{1,0:T(8,128)(2,1)} collective-permute-done((bf16[32,4096]{1,0:T(8,128)(2,1)S(1)}, bf16[32,4096]{1,0:T(8,128)(2,1)}, u32[]{:S(2)}, u32[]{:S(2)}) %collective-permute-start.21) | collective-permute-done | bytes 262176 | tf_op jit(solution)/shard_map/ppermute | solution.py:82
  77.3 1.2 %collective-permute-done.9.refs_5_ = bf16[32,4096]{1,0:T(8,128)(2,1)} collective-permute-done((bf16[32,4096]{1,0:T(8,128)(2,1)S(1)}, bf16[32,4096]{1,0:T(8,128)(2,1)}, u32[]{:S(2)}, u32[]{:S(2)}) %collective-permute-start.9) | collective-permute-done | bytes 262176 | tf_op jit(solution)/shard_map/ppermute | solution.py:82
  79.4 3.4 %copy-done = bf16[256,16384]{1,0:T(8,128)(2,1)S(1)} copy-done((bf16[256,16384]{1,0:T(8,128)(2,1)S(1)}, bf16[256,16384]{1,0:T(8,128)(2,1)}, u32[]{:S(2)}) %copy-start) | copy-done | bytes 8388632
  87.4 2.6 %copy-done.1 = bf16[256,16384]{1,0:T(8,128)(2,1)S(1)} copy-done((bf16[256,16384]{1,0:T(8,128)(2,1)S(1)}, bf16[256,16384]{1,0:T(8,128)(2,1)}, u32[]{:S(2)}) %copy-start.1) | copy-done | bytes 8388632
  91.3 1.8 %shard_map.39.refs_9_ = f32[256,256]{1,0:T(8,128)S(1)} custom-call(bf16[64,16384]{1,0:T(8,128)(2,1)S(1)} %copy-done.2, bf16[32,4096]{1,0:T(8,128)(2,1)S(1)} %collective-permute-done.13.refs_1_, bf16[32,4096]{1,0:T(8,128)(2,1)S(1)} %copy-done.6, bf16[32,4096]{1,0:T(8,128)(2,1)S(1)} %copy-done.14, bf16[32,4096]{1,0:T(8,128)(2,1)S(1)} %copy-done.22, ...), custom_call_target="tpu_custom_call" | custom-call | flops 536870912 | bytes 4194304 | tf_op jit(solution)/shard_map/pallas_call | solution.py:48
  93.1 1.8 %shard_map.40 = f32[256,256]{1,0:T(8,128)S(1)} custom-call(bf16[64,16384]{1,0:T(8,128)(2,1)S(1)} %copy-done.2, bf16[32,4096]{1,0:T(8,128)(2,1)S(1)} %collective-permute-done.1.refs_1_, bf16[32,4096]{1,0:T(8,128)(2,1)S(1)} %copy-done.8, bf16[32,4096]{1,0:T(8,128)(2,1)S(1)} %copy-done.16, bf16[32,4096]{1,0:T(8,128)(2,1)S(1)} %copy-done.24, ...), custom_call_target="tpu_custom_call" | custom-call | flops 536870912 | bytes 4194304 | tf_op jit(solution)/shard_map/pallas_call | solution.py:48
  95.1 1.3 %collective-permute-done.24 = f32[2,64,256]{2,1,0:T(8,128)S(1)} collective-permute-done((f32[2,64,256]{2,1,0:T(8,128)S(1)}, f32[2,64,256]{2,1,0:T(8,128)S(1)}, u32[]{:S(2)}, u32[]{:S(2)}) %collective-permute-start.24) | collective-permute-done | bytes 131104 | tf_op jit(solution)/shard_map/ppermute | solution.py:99
  96.4 1.6 %collective-permute-start.25 = (f32[1,64,256]{2,1,0:T(8,128)S(1)}, f32[1,64,256]{2,1,0:T(8,128)S(1)}, u32[]{:S(2)}, u32[]{:S(2)}) collective-permute-start(f32[1,64,256]{2,1,0:T(8,128)S(1)} %constant_dynamic-slice_fusion), channel_id=1, source_target_pairs={{0,2},{1,3},{2,0},{3,1},{4,6},{5,7},{6,4},{7,5},{8,10},{9,11},{10,... | collective-permute-start | bytes 196616 | tf_op jit(solution)/shard_map/ppermute | solution.py:99
  98.0 2.8 %collective-permute-done.25 = f32[1,64,256]{2,1,0:T(8,128)S(1)} collective-permute-done((f32[1,64,256]{2,1,0:T(8,128)S(1)}, f32[1,64,256]{2,1,0:T(8,128)S(1)}, u32[]{:S(2)}, u32[]{:S(2)}) %collective-permute-start.25) | collective-permute-done | bytes 65568 | tf_op jit(solution)/shard_map/ppermute | solution.py:99
  (98 shorter events, 21.5 us)
Async XLA Ops:
  0.0 79.4 %copy-start.2 = (bf16[64,16384]{1,0:T(8,128)(2,1)S(1)}, bf16[64,16384]{1,0:T(8,128)(2,1)}, u32[]{:S(2)}) copy-start(bf16[64,16384]{1,0:T(8,128)(2,1)} %refs_0_.7) | copy-start | bytes 6291460
  0.0 79.3 %copy-start.33 = (f32[16384]{0:T(1024)S(1)}, f32[16384]{0:T(1024)}, u32[]{:S(2)}) copy-start(f32[16384]{0:T(1024)} %param.5) | copy-start | bytes 196612
  1.8 12.2 %collective-permute-start.12 = (bf16[32,4096]{1,0:T(8,128)(2,1)S(1)}, bf16[32,4096]{1,0:T(8,128)(2,1)S(1)}, u32[]{:S(2)}, u32[]{:S(2)}) collective-permute-start(bf16[32,4096]{1,0:T(8,128)(2,1)S(1)} %get-tuple-element.45), channel_id=1, source_target_pairs={{0,4},{4,8},{8,12},{12,0},{1,5},{5,9},{9,13},{13,1},{2,6},{6,10},{... | collective-permute-start | bytes 786440 | tf_op jit(solution)/shard_map/ppermute | solution.py:82
  4.9 14.8 %collective-permute-start = (bf16[32,4096]{1,0:T(8,128)(2,1)S(1)}, bf16[32,4096]{1,0:T(8,128)(2,1)S(1)}, u32[]{:S(2)}, u32[]{:S(2)}) collective-permute-start(bf16[32,4096]{1,0:T(8,128)(2,1)S(1)} %get-tuple-element.47), channel_id=1, source_target_pairs={{0,4},{4,8},{8,12},{12,0},{1,5},{5,9},{9,13},{13,1},{2,6},{6,10},{... | collective-permute-start | bytes 786440 | tf_op jit(solution)/shard_map/ppermute | solution.py:82
  14.0 11.2 %collective-permute-start.13 = (bf16[32,4096]{1,0:T(8,128)(2,1)S(1)}, bf16[32,4096]{1,0:T(8,128)(2,1)S(1)}, u32[]{:S(2)}, u32[]{:S(2)}) collective-permute-start(bf16[32,4096]{1,0:T(8,128)(2,1)S(1)} %get-tuple-element.35), channel_id=1, source_target_pairs={{0,4},{4,8},{8,12},{12,0},{1,5},{5,9},{9,13},{13,1},{2,6},{6,10},{... | collective-permute-start | bytes 786440 | tf_op jit(solution)/shard_map/ppermute | solution.py:82
  14.1 11.2 %collective-permute-start.14 = (bf16[32,4096]{1,0:T(8,128)(2,1)S(1)}, bf16[32,4096]{1,0:T(8,128)(2,1)S(1)}, u32[]{:S(2)}, u32[]{:S(2)}) collective-permute-start(bf16[32,4096]{1,0:T(8,128)(2,1)S(1)} %collective-permute-done.12.refs_1_), channel_id=1, source_target_pairs={{0,16},{16,0},{1,17},{17,1},{2,18},{18,2},{3,19},{19,3},{4,20},{20... | collective-permute-start | bytes 786440 | tf_op jit(solution)/shard_map/ppermute | solution.py:88
  19.6 11.2 %collective-permute-start.1 = (bf16[32,4096]{1,0:T(8,128)(2,1)S(1)}, bf16[32,4096]{1,0:T(8,128)(2,1)S(1)}, u32[]{:S(2)}, u32[]{:S(2)}) collective-permute-start(bf16[32,4096]{1,0:T(8,128)(2,1)S(1)} %get-tuple-element.25), channel_id=1, source_target_pairs={{0,4},{4,8},{8,12},{12,0},{1,5},{5,9},{9,13},{13,1},{2,6},{6,10},{... | collective-permute-start | bytes 786440 | tf_op jit(solution)/shard_map/ppermute | solution.py:82
  19.7 11.2 %collective-permute-start.2 = (bf16[32,4096]{1,0:T(8,128)(2,1)S(1)}, bf16[32,4096]{1,0:T(8,128)(2,1)S(1)}, u32[]{:S(2)}, u32[]{:S(2)}) collective-permute-start(bf16[32,4096]{1,0:T(8,128)(2,1)S(1)} %collective-permute-done.refs_1_), channel_id=1, source_target_pairs={{0,16},{16,0},{1,17},{17,1},{2,18},{18,2},{3,19},{19,3},{4,20},{20... | collective-permute-start | bytes 786440 | tf_op jit(solution)/shard_map/ppermute | solution.py:88
  25.3 11.2 %collective-permute-start.16 = (bf16[32,4096]{1,0:T(8,128)(2,1)S(1)}, bf16[32,4096]{1,0:T(8,128)(2,1)S(1)}, u32[]{:S(2)}, u32[]{:S(2)}) collective-permute-start(bf16[32,4096]{1,0:T(8,128)(2,1)S(1)} %collective-permute-done.12.refs_1_), channel_id=1, source_target_pairs={{0,4},{4,8},{8,12},{12,0},{1,5},{5,9},{9,13},{13,1},{2,6},{6,10},{... | collective-permute-start | bytes 786440 | tf_op jit(solution)/shard_map/ppermute | solution.py:82
  25.3 11.2 %collective-permute-start.15 = (bf16[32,4096]{1,0:T(8,128)(2,1)S(1)}, bf16[32,4096]{1,0:T(8,128)(2,1)S(1)}, u32[]{:S(2)}, u32[]{:S(2)}) collective-permute-start(bf16[32,4096]{1,0:T(8,128)(2,1)S(1)} %collective-permute-done.13.refs_1_), channel_id=1, source_target_pairs={{0,16},{16,0},{1,17},{17,1},{2,18},{18,2},{3,19},{19,3},{4,20},{20... | collective-permute-start | bytes 786440 | tf_op jit(solution)/shard_map/ppermute | solution.py:88
  31.6 10.9 %collective-permute-start.4 = (bf16[32,4096]{1,0:T(8,128)(2,1)S(1)}, bf16[32,4096]{1,0:T(8,128)(2,1)S(1)}, u32[]{:S(2)}, u32[]{:S(2)}) collective-permute-start(bf16[32,4096]{1,0:T(8,128)(2,1)S(1)} %collective-permute-done.refs_1_), channel_id=1, source_target_pairs={{0,4},{4,8},{8,12},{12,0},{1,5},{5,9},{9,13},{13,1},{2,6},{6,10},{... | collective-permute-start | bytes 786440 | tf_op jit(solution)/shard_map/ppermute | solution.py:82
  31.6 10.8 %collective-permute-start.3 = (bf16[32,4096]{1,0:T(8,128)(2,1)S(1)}, bf16[32,4096]{1,0:T(8,128)(2,1)S(1)}, u32[]{:S(2)}, u32[]{:S(2)}) collective-permute-start(bf16[32,4096]{1,0:T(8,128)(2,1)S(1)} %collective-permute-done.1.refs_1_), channel_id=1, source_target_pairs={{0,16},{16,0},{1,17},{17,1},{2,18},{18,2},{3,19},{19,3},{4,20},{20... | collective-permute-start | bytes 786440 | tf_op jit(solution)/shard_map/ppermute | solution.py:88
  37.2 11.0 %collective-permute-start.17 = (bf16[32,4096]{1,0:T(8,128)(2,1)S(1)}, bf16[32,4096]{1,0:T(8,128)(2,1)S(1)}, u32[]{:S(2)}, u32[]{:S(2)}) collective-permute-start(bf16[32,4096]{1,0:T(8,128)(2,1)S(1)} %collective-permute-done.13.refs_1_), channel_id=1, source_target_pairs={{0,4},{4,8},{8,12},{12,0},{1,5},{5,9},{9,13},{13,1},{2,6},{6,10},{... | collective-permute-start | bytes 786440 | tf_op jit(solution)/shard_map/ppermute | solution.py:82
  37.2 11.0 %collective-permute-start.18 = (bf16[32,4096]{1,0:T(8,128)(2,1)S(1)}, bf16[32,4096]{1,0:T(8,128)(2,1)S(1)}, u32[]{:S(2)}, u32[]{:S(2)}) collective-permute-start(bf16[32,4096]{1,0:T(8,128)(2,1)S(1)} %collective-permute-done.16.refs_3_), channel_id=1, source_target_pairs={{0,16},{16,0},{1,17},{17,1},{2,18},{18,2},{3,19},{19,3},{4,20},{20... | collective-permute-start | bytes 786440 | tf_op jit(solution)/shard_map/ppermute | solution.py:88
  43.1 11.0 %collective-permute-start.5 = (bf16[32,4096]{1,0:T(8,128)(2,1)S(1)}, bf16[32,4096]{1,0:T(8,128)(2,1)S(1)}, u32[]{:S(2)}, u32[]{:S(2)}) collective-permute-start(bf16[32,4096]{1,0:T(8,128)(2,1)S(1)} %collective-permute-done.1.refs_1_), channel_id=1, source_target_pairs={{0,4},{4,8},{8,12},{12,0},{1,5},{5,9},{9,13},{13,1},{2,6},{6,10},{... | collective-permute-start | bytes 786440 | tf_op jit(solution)/shard_map/ppermute | solution.py:82
  43.2 11.0 %collective-permute-start.6 = (bf16[32,4096]{1,0:T(8,128)(2,1)S(1)}, bf16[32,4096]{1,0:T(8,128)(2,1)S(1)}, u32[]{:S(2)}, u32[]{:S(2)}) collective-permute-start(bf16[32,4096]{1,0:T(8,128)(2,1)S(1)} %collective-permute-done.4.refs_3_), channel_id=1, source_target_pairs={{0,16},{16,0},{1,17},{17,1},{2,18},{18,2},{3,19},{19,3},{4,20},{20... | collective-permute-start | bytes 786440 | tf_op jit(solution)/shard_map/ppermute | solution.py:88
  48.9 11.0 %collective-permute-start.20 = (bf16[32,4096]{1,0:T(8,128)(2,1)S(1)}, bf16[32,4096]{1,0:T(8,128)(2,1)S(1)}, u32[]{:S(2)}, u32[]{:S(2)}) collective-permute-start(bf16[32,4096]{1,0:T(8,128)(2,1)S(1)} %collective-permute-done.16.refs_3_), channel_id=1, source_target_pairs={{0,4},{4,8},{8,12},{12,0},{1,5},{5,9},{9,13},{13,1},{2,6},{6,10},{... | collective-permute-start | bytes 786440 | tf_op jit(solution)/shard_map/ppermute | solution.py:82
  49.7 10.3 %collective-permute-start.19 = (bf16[32,4096]{1,0:T(8,128)(2,1)S(1)}, bf16[32,4096]{1,0:T(8,128)(2,1)S(1)}, u32[]{:S(2)}, u32[]{:S(2)}) collective-permute-start(bf16[32,4096]{1,0:T(8,128)(2,1)S(1)} %collective-permute-done.17.refs_3_), channel_id=1, source_target_pairs={{0,16},{16,0},{1,17},{17,1},{2,18},{18,2},{3,19},{19,3},{4,20},{20... | collective-permute-start | bytes 786440 | tf_op jit(solution)/shard_map/ppermute | solution.py:88
  54.9 8.8 %collective-permute-start.8 = (bf16[32,4096]{1,0:T(8,128)(2,1)S(1)}, bf16[32,4096]{1,0:T(8,128)(2,1)S(1)}, u32[]{:S(2)}, u32[]{:S(2)}) collective-permute-start(bf16[32,4096]{1,0:T(8,128)(2,1)S(1)} %collective-permute-done.4.refs_3_), channel_id=1, source_target_pairs={{0,4},{4,8},{8,12},{12,0},{1,5},{5,9},{9,13},{13,1},{2,6},{6,10},{... | collective-permute-start | bytes 786440 | tf_op jit(solution)/shard_map/ppermute | solution.py:82
  55.7 8.8 %collective-permute-start.7 = (bf16[32,4096]{1,0:T(8,128)(2,1)S(1)}, bf16[32,4096]{1,0:T(8,128)(2,1)S(1)}, u32[]{:S(2)}, u32[]{:S(2)}) collective-permute-start(bf16[32,4096]{1,0:T(8,128)(2,1)S(1)} %collective-permute-done.5.refs_3_), channel_id=1, source_target_pairs={{0,16},{16,0},{1,17},{17,1},{2,18},{18,2},{3,19},{19,3},{4,20},{20... | collective-permute-start | bytes 786440 | tf_op jit(solution)/shard_map/ppermute | solution.py:88
  60.7 10.6 %collective-permute-start.22 = (bf16[32,4096]{1,0:T(8,128)(2,1)S(1)}, bf16[32,4096]{1,0:T(8,128)(2,1)S(1)}, u32[]{:S(2)}, u32[]{:S(2)}) collective-permute-start(bf16[32,4096]{1,0:T(8,128)(2,1)S(1)} %collective-permute-done.20.refs_5_), channel_id=1, source_target_pairs={{0,16},{16,0},{1,17},{17,1},{2,18},{18,2},{3,19},{19,3},{4,20},{20... | collective-permute-start | bytes 786440 | tf_op jit(solution)/shard_map/ppermute | solution.py:88
  65.1 10.5 %collective-permute-start.21 = (bf16[32,4096]{1,0:T(8,128)(2,1)S(1)}, bf16[32,4096]{1,0:T(8,128)(2,1)}, u32[]{:S(2)}, u32[]{:S(2)}) collective-permute-start(bf16[32,4096]{1,0:T(8,128)(2,1)S(1)} %collective-permute-done.17.refs_3_), channel_id=1, source_target_pairs={{0,4},{4,8},{8,12},{12,0},{1,5},{5,9},{9,13},{13,1},{2,6},{6,10},{... | collective-permute-start | bytes 786440 | tf_op jit(solution)/shard_map/ppermute | solution.py:82
  66.8 9.7 %collective-permute-start.10 = (bf16[32,4096]{1,0:T(8,128)(2,1)S(1)}, bf16[32,4096]{1,0:T(8,128)(2,1)S(1)}, u32[]{:S(2)}, u32[]{:S(2)}) collective-permute-start(bf16[32,4096]{1,0:T(8,128)(2,1)S(1)} %collective-permute-done.8.refs_5_), channel_id=1, source_target_pairs={{0,16},{16,0},{1,17},{17,1},{2,18},{18,2},{3,19},{19,3},{4,20},{20... | collective-permute-start | bytes 786440 | tf_op jit(solution)/shard_map/ppermute | solution.py:88
  69.1 9.4 %collective-permute-start.9 = (bf16[32,4096]{1,0:T(8,128)(2,1)S(1)}, bf16[32,4096]{1,0:T(8,128)(2,1)}, u32[]{:S(2)}, u32[]{:S(2)}) collective-permute-start(bf16[32,4096]{1,0:T(8,128)(2,1)S(1)} %collective-permute-done.5.refs_3_), channel_id=1, source_target_pairs={{0,4},{4,8},{8,12},{12,0},{1,5},{5,9},{9,13},{13,1},{2,6},{6,10},{... | collective-permute-start | bytes 786440 | tf_op jit(solution)/shard_map/ppermute | solution.py:82
  75.7 15.3 %collective-permute-start.23 = (bf16[32,4096]{1,0:T(8,128)(2,1)}, bf16[32,4096]{1,0:T(8,128)(2,1)}, u32[]{:S(2)}, u32[]{:S(2)}) collective-permute-start(bf16[32,4096]{1,0:T(8,128)(2,1)} %collective-permute-done.21.refs_5_), channel_id=1, source_target_pairs={{0,16},{16,0},{1,17},{17,1},{2,18},{18,2},{3,19},{19,3},{4,20},{20... | collective-permute-start | bytes 786440 | tf_op jit(solution)/shard_map/ppermute | solution.py:88
  78.5 14.6 %collective-permute-start.11 = (bf16[32,4096]{1,0:T(8,128)(2,1)}, bf16[32,4096]{1,0:T(8,128)(2,1)}, u32[]{:S(2)}, u32[]{:S(2)}) collective-permute-start(bf16[32,4096]{1,0:T(8,128)(2,1)} %collective-permute-done.9.refs_5_), channel_id=1, source_target_pairs={{0,16},{16,0},{1,17},{17,1},{2,18},{18,2},{3,19},{19,3},{4,20},{20... | collective-permute-start | bytes 786440 | tf_op jit(solution)/shard_map/ppermute | solution.py:88
  86.6 3.4 %copy-start.12 = (bf16[32,4096]{1,0:T(8,128)(2,1)S(1)}, bf16[32,4096]{1,0:T(8,128)(2,1)}, u32[]{:S(2)}) copy-start(bf16[32,4096]{1,0:T(8,128)(2,1)} %copy-done.11) | copy-start | bytes 786436
  86.6 3.5 %copy-start.20 = (bf16[32,4096]{1,0:T(8,128)(2,1)S(1)}, bf16[32,4096]{1,0:T(8,128)(2,1)}, u32[]{:S(2)}) copy-start(bf16[32,4096]{1,0:T(8,128)(2,1)} %copy-done.19) | copy-start | bytes 786436
  86.6 3.5 %copy-start.28 = (bf16[32,4096]{1,0:T(8,128)(2,1)S(1)}, bf16[32,4096]{1,0:T(8,128)(2,1)}, u32[]{:S(2)}) copy-start(bf16[32,4096]{1,0:T(8,128)(2,1)} %copy-done.27) | copy-start | bytes 786436
  86.6 3.6 %copy-start.32 = (bf16[32,4096]{1,0:T(8,128)(2,1)S(1)}, bf16[32,4096]{1,0:T(8,128)(2,1)}, u32[]{:S(2)}) copy-start(bf16[32,4096]{1,0:T(8,128)(2,1)} %copy-done.31) | copy-start | bytes 786436
  95.0 1.4 %collective-permute-start.24 = (f32[2,64,256]{2,1,0:T(8,128)S(1)}, f32[2,64,256]{2,1,0:T(8,128)S(1)}, u32[]{:S(2)}, u32[]{:S(2)}) collective-permute-start(f32[2,64,256]{2,1,0:T(8,128)S(1)} %dynamic-slice_bitcast_fusion), channel_id=1, source_target_pairs={{0,1},{1,0},{2,3},{3,2},{4,5},{5,4},{6,7},{7,6},{8,9},{9,8},{10,11... | collective-permute-start | bytes 393224 | tf_op jit(solution)/shard_map/ppermute | solution.py:99
  96.4 4.3 %collective-permute-start.25 = (f32[1,64,256]{2,1,0:T(8,128)S(1)}, f32[1,64,256]{2,1,0:T(8,128)S(1)}, u32[]{:S(2)}, u32[]{:S(2)}) collective-permute-start(f32[1,64,256]{2,1,0:T(8,128)S(1)} %constant_dynamic-slice_fusion), channel_id=1, source_target_pairs={{0,2},{1,3},{2,0},{3,1},{4,6},{5,7},{6,4},{7,5},{8,10},{9,11},{10,... | collective-permute-start | bytes 196616 | tf_op jit(solution)/shard_map/ppermute | solution.py:99
  (28 other events, 34.1 us)

commit v9 on v0

v9 whole, which is shorter than its diff:
```python
import functools

import jax
import jax.numpy as jnp
from jax import lax
from jax.experimental import pallas as pl
from jax.experimental.pallas import tpu as pltpu
from jax.sharding import PartitionSpec as P

CONTRACT = (((1,), (1,)), ((), ()))
CHUNKS = (4, 4, 4, 4)


def product(rows, scale, train, unit):
    total = None
    for at in range(0, train.shape[1], unit):
        here = slice(at, at + unit)
        precond = (rows(here).astype(jnp.float32) * scale(here)).astype(jnp.bfloat16)
        part = lax.dot_general(
            precond, train[:, here], CONTRACT, preferred_element_type=jnp.float32
        )
        total = part if total is None else total + part
    return total


def own_kernel(starts, unit, test, scale, *refs):
    trains, out = refs[:-1], refs[-1]
    total = None
    for start, train in zip(starts, trains):
        column = lambda here: slice(start + here.start, start + here.stop)
        part = product(lambda here: test[:, column(here)], lambda here: scale[:, column(here)], train, unit)
        total = part if total is None else total + part
    out[...] = total


def arrived_rows(parts):
    return lambda here: jnp.concatenate([p[:, here] for p in parts], axis=0)


def part_kernel(start, unit, n_parts, has_base, *refs):
    parts, (scale, train) = refs[:n_parts], refs[n_parts : n_parts + 2]
    column = lambda here: scale[:, start + here.start : start + here.stop]
    total = product(arrived_rows(parts), column, train, unit)
    refs[-1][...] = total + refs[n_parts + 2][...] if has_base else total


def last_kernel(n_grp, n_ex, start, unit, n_parts, *refs):
    parts, (scale, train) = refs[:n_parts], refs[n_parts : n_parts + 2]
    sums, (out, kept) = refs[n_parts + 2 : -2], refs[-2:]
    column = lambda here: scale[:, start + here.start : start + here.stop]
    total = product(arrived_rows(parts), column, train, unit) + sums[-1][...]
    queries = total.shape[0]
    half = queries // n_grp
    for t, value in enumerate([s[...] for s in sums[:-1]] + [total]):
        kept[t * queries : (t + 1) * queries, :] = value
    ex, grp = lax.axis_index("ex"), lax.axis_index("grp")
    for b in range(n_ex):
        t = lax.rem(ex + (n_ex - b), n_ex)
        for h in range(n_grp):
            place = jnp.where(t == 0, h, lax.rem(h + n_grp - grp, n_grp))
            at = pl.multiple_of(t * queries + place * half, half)
            to = b * queries + h * half
            out[to : to + half, :] = kept[pl.ds(at, half), :]


def call(kernel, rows, docs, width, operands, scratch=()):
    return pl.pallas_call(
        kernel,
        out_shape=jax.ShapeDtypeStruct((rows, docs), jnp.float32),
        in_specs=[pl.BlockSpec(memory_space=pltpu.VMEM)] * len(operands),
        out_specs=pl.BlockSpec(memory_space=pltpu.VMEM),
        scratch_shapes=scratch,
        cost_estimate=pl.CostEstimate(
            flops=2 * rows * docs * width, bytes_accessed=2 * (rows + docs) * width, transcendentals=0
        ),
        compiler_params=pltpu.CompilerParams(vmem_limit_bytes=16 * 1024 * 1024),
    )(*operands)


def solution(mesh):
    n_grp, n_ex, n_feat = (mesh.shape[a] for a in ("grp", "ex", "feat"))
    assert n_grp <= 2

    def on_device(train, test, hess):
        docs, feats = train.shape
        queries = test.shape[0]
        half = queries // n_grp
        unit = feats // sum(CHUNKS)
        grp, feat = lax.axis_index("grp"), lax.axis_index("feat")
        ring = [(i, (i + 1) % n_ex) for i in range(n_ex)]
        hops, swaps, made, first = [], [], [], []

        def after(block, *waits):
            return lax.optimization_barrier((block, waits))[0] if waits else block

        def hop(block):
            waits = hops[-2:-1] + swaps[-4:-3] + made[-6:-5] + (first if len(hops) == 3 else [])
            hops.append(lax.ppermute(after(block, *waits), "ex", ring))
            return hops[-1]

        def swap(block):
            if n_grp == 1:
                return [block]
            swaps.append(lax.ppermute(after(block, *swaps[-2:-1]), "grp", [(0, 1), (1, 0)]))
            return [block, swaps[-1]]

        def sum_over_feat(sums):
            held = sums.reshape(n_feat, -1, docs)
            bit = 1
            while bit < n_feat:
                pairs = held.reshape((-1, 2) + held.shape[1:])
                mine = (feat // bit) % 2
                keep = lax.dynamic_index_in_dim(pairs, mine, 1, keepdims=False)
                away = lax.dynamic_index_in_dim(pairs, 1 - mine, 1, keepdims=False)
                held = keep + lax.ppermute(away, "feat", [(i, i ^ bit) for i in range(n_feat)])
                bit *= 2
            return held[0]

        def share(rows, start, width):
            columns = slice(start, start + width)
            if n_grp == 1:
                return rows[:, columns]
            return jnp.where(grp == 0, rows[:half, columns], rows[half:, columns])

        scale = (1.0 / (hess + jnp.float32(0.1))).reshape(1, feats)
        widths = [width * unit for width in CHUNKS]
        starts = [sum(widths[:c]) for c in range(len(widths))]
        held = []
        for start, width in zip(starts, widths):
            held.append(share(after(test, *held[-1:]), start, width))
        trains = [train[:, start : start + width] for start, width in zip(starts, widths)]
        own = call(
            functools.partial(own_kernel, starts, unit), queries, docs, feats, [test, scale, *trains]
        )
        first.append(own)
        sums = [own]
        for t in range(1, n_ex):
            total = None
            for c, (start, width) in enumerate(zip(starts, widths)):
                held[c] = hop(held[c])
                parts = swap(held[c])
                operands = [*parts, scale, trains[c]]
                if t == n_ex - 1 and c == len(widths) - 1:
                    total = call(
                        functools.partial(last_kernel, n_grp, n_ex, start, unit, len(parts)),
                        n_ex * queries, docs, width, [*operands, *sums, total],
                        [pltpu.VMEM((n_ex * queries, docs), jnp.float32)],
                    )
                else:
                    total = call(
                        functools.partial(part_kernel, start, unit, len(parts), total is not None),
                        queries, docs, width, operands + ([] if total is None else [total]),
                    )
                made.append(total)
            sums.append(total)
        return sum_over_feat(sums[-1]).T


    return jax.shard_map(
        on_device,
        mesh=mesh,
        in_specs=(P(("grp", "ex"), "feat"), P("ex", "feat"), P("feat")),
        out_specs=P(("grp", "ex"), "feat"),
        check_vma=False,
    )
```

time: 198 us -> 94.2 us (0.48)
  waiting for transfers between devices: 171 us -> 41.3 us
  starting transfers between devices: 0.04 us -> 23.7 us
  between operations: 13.4 us -> 0.3 us
  Pallas kernels: 0 us -> 12.8 us
  local copies, waits for them, and re-layouts: 0 us -> 10.8 us
  matrix products: 8.85 us -> 0 us
    all_gather x1 -> x0, waiting for transfers between devices: 152 us -> none  [on_device(): lax.all_gather(precond, 'ex', axis=0, tiled=True)]
    ppermute x0 -> x26, waiting for transfers between devices: none -> 41.3 us  [the longest x12 27.6 us: hop(): hops.append(lax.ppermute(after(block, *waits), 'ex', ring))]
    ppermute x0 -> x26, starting transfers between devices: none -> 23.7 us  [the longest x12 15.8 us: swap(): lax.ppermute(after(block, *swaps[-2:-1]), 'grp', [(0, 1), (1, 0)])]
    reduce_scatter x1 -> x0, waiting for transfers between devices: 18.4 us -> none  [on_device(): lax.psum_scatter(partial_sums, 'feat', scatter_dimension=1, tiled=True)]
    pallas_call x0 -> x13, Pallas kernels: none -> 12.8 us  [call(): pl.pallas_call(kernel, out_shape=jax.ShapeDtypeStruct((rows, docs), jnp.f...]
    dot_general x1 -> x0, matrix products: 8.85 us -> none  [on_device(): lax.dot_general(train_grads, lax.all_gather(precond, 'ex', axis=0, tiled=...]
    unnamed x0 -> x46, local copies, waits for them, and re-layouts: none -> 6.76 us
    select_n x0 -> x4, other arithmetic: none -> 4.24 us  [share(): return jnp.where(grp == 0, rows[:half, columns], rows[half:, columns])]
  transfers between devices with their start and end apart: 2 -> 26, of which waited for: 2 -> 18; matrix products, arithmetic and copies ran while one was open for 0% -> 8% of each run, Pallas kernels for 0% -> 13%
where the time goes in v9:
time: 94.2 us; the launch traced here: 93.9 us
  waiting for transfers between devices  41.3 us (44%)
  starting transfers between devices  23.7 us (25%)
  Pallas kernels  12.8 us (14%)
  local copies, waits for them, and re-layouts  10.8 us (11%)
  other arithmetic  4.91 us (5%)
    ppermute x12, waiting for transfers between devices, hop(): hops.append(lax.ppermute(after(block, *waits), 'ex', ring))  27.6 us
    ppermute x12, starting transfers between devices, swap(): lax.ppermute(after(block, *swaps[-2:-1]), 'grp', [(0, 1), (1, 0)])  15.8 us
    pallas_call x13, Pallas kernels, call(): pl.pallas_call(kernel, out_shape=jax.ShapeDtypeStruct((rows, docs), jnp.f...  12.8 us
    ppermute x12, waiting for transfers between devices, swap(): lax.ppermute(after(block, *swaps[-2:-1]), 'grp', [(0, 1), (1, 0)])  9.83 us
    unnamed x46, local copies, waits for them, and re-layouts  6.76 us
    ppermute x12, starting transfers between devices, hop(): hops.append(lax.ppermute(after(block, *waits), 'ex', ring))  6.16 us
    select_n x4, other arithmetic, share(): return jnp.where(grp == 0, rows[:half, columns], rows[half:, columns])  4.24 us
    slice x1, local copies, waits for them, and re-layouts, on_device(): train[:, start:start + width]  4.03 us
  transfers between devices with their start and end apart: 26, of which 18 were waited for; matrix products, arithmetic and copies ran while one was open for 8% of the time, Pallas kernels for 13%

profile of v9, /device:TPU:0, one launch (start us, length us, event | category | flops | bytes accessed | tf_op | source)
XLA Modules:
  0.0 93.9 jit_solution(1045655203604444254)
XLA Ops:
  1.1 3.1 %collective-permute-start.5 = (bf16[32,4096]{1,0:T(8,128)(2,1)S(1)}, bf16[32,4096]{1,0:T(8,128)(2,1)S(1)}, u32[]{:S(2)}, u32[]{:S(2)}) collective-permute-start(bf16[32,4096]{1,0:T(8,128)(2,1)S(1)} %slice_select_fusion.3), channel_id=1, source_target_pairs={{0,4},{4,8},{8,12},{12,0},{1,5},{5,9},{9,13},{13,1},{2,6},{6,10},{... | collective-permute-start | bytes 786440 | tf_op jit(solution)/shard_map/ppermute | solution.py:98
  5.2 1.6 %collective-permute-start = (bf16[32,4096]{1,0:T(8,128)(2,1)S(1)}, bf16[32,4096]{1,0:T(8,128)(2,1)S(1)}, u32[]{:S(2)}, u32[]{:S(2)}) collective-permute-start(bf16[32,4096]{1,0:T(8,128)(2,1)S(1)} %slice_select_fusion.2), channel_id=1, source_target_pairs={{0,4},{4,8},{8,12},{12,0},{1,5},{5,9},{9,13},{13,1},{2,6},{6,10},{... | collective-permute-start | bytes 786440 | tf_op jit(solution)/shard_map/ppermute | solution.py:98
  9.0 4.0 %fusion = (bf16[256,4096]{1,0:T(8,128)(2,1)S(1)}, bf16[256,4096]{1,0:T(8,128)(2,1)S(1)}, bf16[256,4096]{1,0:T(8,128)(2,1)S(1)}, bf16[256,4096]{1,0:T(8,128)(2,1)S(1)}) fusion(bf16[256,16384]{1,0:T(8,128)(2,1)} %param.3), kind=kLoop, calls=%fused_computation.9 | loop fusion | bytes 16777216 | tf_op jit(solution)/shard_map/slice | solution.py:131
  13.3 1.4 %collective-permute-start.9 = (bf16[32,4096]{1,0:T(8,128)(2,1)S(1)}, bf16[32,4096]{1,0:T(8,128)(2,1)S(1)}, u32[]{:S(2)}, u32[]{:S(2)}) collective-permute-start(bf16[32,4096]{1,0:T(8,128)(2,1)S(1)} %slice_select_fusion.1), channel_id=1, source_target_pairs={{0,4},{4,8},{8,12},{12,0},{1,5},{5,9},{9,13},{13,1},{2,6},{6,10},{... | collective-permute-start | bytes 786440 | tf_op jit(solution)/shard_map/ppermute | solution.py:98
  14.7 1.5 %collective-permute-start.6 = (bf16[32,4096]{1,0:T(8,128)(2,1)S(1)}, bf16[32,4096]{1,0:T(8,128)(2,1)S(1)}, u32[]{:S(2)}, u32[]{:S(2)}) collective-permute-start(bf16[32,4096]{1,0:T(8,128)(2,1)S(1)} %collective-permute-done.5.refs_0_), channel_id=1, source_target_pairs={{0,16},{16,0},{1,17},{17,1},{2,18},{18,2},{3,19},{19,3},{4,20},{20... | collective-permute-start | bytes 786440 | tf_op jit(solution)/shard_map/ppermute | solution.py:104
  16.2 2.7 %shard_map.37.refs_4_ = f32[64,256]{1,0:T(8,128)S(1)} custom-call(bf16[64,16384]{1,0:T(8,128)(2,1)S(1)} %copy-done.7, f32[1,16384]{1,0:T(1,128)S(1)} %bitcast.10, bf16[256,4096]{1,0:T(8,128)(2,1)S(1)} %get-tuple-element.53.refs_0_.refs_3_, bf16[256,4096]{1,0:T(8,128)(2,1)S(1)} %get-tuple-element.52.refs_1_.refs_3_, ...), custom_call_target="tpu_custom_call" | custom-call | flops 536870912 | bytes 10485760 | tf_op jit(solution)/shard_map/pallas_call | solution.py:67
  18.9 1.8 %collective-permute-start.2 = (bf16[32,4096]{1,0:T(8,128)(2,1)S(1)}, bf16[32,4096]{1,0:T(8,128)(2,1)S(1)}, u32[]{:S(2)}, u32[]{:S(2)}) collective-permute-start(bf16[32,4096]{1,0:T(8,128)(2,1)S(1)} %collective-permute-done.refs_0_), channel_id=1, source_target_pairs={{0,16},{16,0},{1,17},{17,1},{2,18},{18,2},{3,19},{19,3},{4,20},{20... | collective-permute-start | bytes 786440 | tf_op jit(solution)/shard_map/ppermute | solution.py:104
  20.7 3.8 %collective-permute-done.9.refs_0_ = bf16[32,4096]{1,0:T(8,128)(2,1)S(1)} collective-permute-done((bf16[32,4096]{1,0:T(8,128)(2,1)S(1)}, bf16[32,4096]{1,0:T(8,128)(2,1)S(1)}, u32[]{:S(2)}, u32[]{:S(2)}) %collective-permute-start.9) | collective-permute-done | bytes 262176 | tf_op jit(solution)/shard_map/ppermute | solution.py:98
  24.5 1.8 %collective-permute-start.10 = (bf16[32,4096]{1,0:T(8,128)(2,1)S(1)}, bf16[32,4096]{1,0:T(8,128)(2,1)S(1)}, u32[]{:S(2)}, u32[]{:S(2)}) collective-permute-start(bf16[32,4096]{1,0:T(8,128)(2,1)S(1)} %collective-permute-done.9.refs_0_), channel_id=1, source_target_pairs={{0,16},{16,0},{1,17},{17,1},{2,18},{18,2},{3,19},{19,3},{4,20},{20... | collective-permute-start | bytes 786440 | tf_op jit(solution)/shard_map/ppermute | solution.py:104
  26.3 2.8 %collective-permute-done.2.refs_1_ = bf16[32,4096]{1,0:T(8,128)(2,1)S(1)} collective-permute-done((bf16[32,4096]{1,0:T(8,128)(2,1)S(1)}, bf16[32,4096]{1,0:T(8,128)(2,1)S(1)}, u32[]{:S(2)}, u32[]{:S(2)}) %collective-permute-start.2) | collective-permute-done | bytes 262176 | tf_op jit(solution)/shard_map/ppermute | solution.py:104
  29.1 1.1 %collective-permute-done.1.refs_0_ = bf16[32,4096]{1,0:T(8,128)(2,1)S(1)} collective-permute-done((bf16[32,4096]{1,0:T(8,128)(2,1)S(1)}, bf16[32,4096]{1,0:T(8,128)(2,1)S(1)}, u32[]{:S(2)}, u32[]{:S(2)}) %collective-permute-start.1) | collective-permute-done | bytes 262176 | tf_op jit(solution)/shard_map/ppermute | solution.py:98
  30.2 1.9 %collective-permute-start.4 = (bf16[32,4096]{1,0:T(8,128)(2,1)S(1)}, bf16[32,4096]{1,0:T(8,128)(2,1)S(1)}, u32[]{:S(2)}, u32[]{:S(2)}) collective-permute-start(bf16[32,4096]{1,0:T(8,128)(2,1)S(1)} %collective-permute-done.1.refs_0_), channel_id=1, source_target_pairs={{0,16},{16,0},{1,17},{17,1},{2,18},{18,2},{3,19},{19,3},{4,20},{20... | collective-permute-start | bytes 786440 | tf_op jit(solution)/shard_map/ppermute | solution.py:104
  32.8 1.9 %collective-permute-done.10.refs_1_ = bf16[32,4096]{1,0:T(8,128)(2,1)S(1)} collective-permute-done((bf16[32,4096]{1,0:T(8,128)(2,1)S(1)}, bf16[32,4096]{1,0:T(8,128)(2,1)S(1)}, u32[]{:S(2)}, u32[]{:S(2)}) %collective-permute-start.10) | collective-permute-done | bytes 262176 | tf_op jit(solution)/shard_map/ppermute | solution.py:104
  34.7 2.6 %collective-permute-done.13.refs_0_ = bf16[32,4096]{1,0:T(8,128)(2,1)S(1)} collective-permute-done((bf16[32,4096]{1,0:T(8,128)(2,1)S(1)}, bf16[32,4096]{1,0:T(8,128)(2,1)S(1)}, u32[]{:S(2)}, u32[]{:S(2)}) %collective-permute-start.13) | collective-permute-done | bytes 262176 | tf_op jit(solution)/shard_map/ppermute | solution.py:98
  38.5 3.1 %collective-permute-done.3.refs_0_ = bf16[32,4096]{1,0:T(8,128)(2,1)S(1)} collective-permute-done((bf16[32,4096]{1,0:T(8,128)(2,1)S(1)}, bf16[32,4096]{1,0:T(8,128)(2,1)S(1)}, u32[]{:S(2)}, u32[]{:S(2)}) %collective-permute-start.3) | collective-permute-done | bytes 262176 | tf_op jit(solution)/shard_map/ppermute | solution.py:98
  41.6 1.7 %collective-permute-start.8 = (bf16[32,4096]{1,0:T(8,128)(2,1)S(1)}, bf16[32,4096]{1,0:T(8,128)(2,1)S(1)}, u32[]{:S(2)}, u32[]{:S(2)}) collective-permute-start(bf16[32,4096]{1,0:T(8,128)(2,1)S(1)} %collective-permute-done.3.refs_0_), channel_id=1, source_target_pairs={{0,16},{16,0},{1,17},{17,1},{2,18},{18,2},{3,19},{19,3},{4,20},{20... | collective-permute-start | bytes 786440 | tf_op jit(solution)/shard_map/ppermute | solution.py:104
  44.1 2.5 %collective-permute-done.14.refs_1_ = bf16[32,4096]{1,0:T(8,128)(2,1)S(1)} collective-permute-done((bf16[32,4096]{1,0:T(8,128)(2,1)S(1)}, bf16[32,4096]{1,0:T(8,128)(2,1)S(1)}, u32[]{:S(2)}, u32[]{:S(2)}) %collective-permute-start.14) | collective-permute-done | bytes 262176 | tf_op jit(solution)/shard_map/ppermute | solution.py:104
  46.6 2.1 %collective-permute-done.18.refs_0_ = bf16[32,4096]{1,0:T(8,128)(2,1)S(1)} collective-permute-done((bf16[32,4096]{1,0:T(8,128)(2,1)S(1)}, bf16[32,4096]{1,0:T(8,128)(2,1)S(1)}, u32[]{:S(2)}, u32[]{:S(2)}) %collective-permute-start.18) | collective-permute-done | bytes 262176 | tf_op jit(solution)/shard_map/ppermute | solution.py:98
  48.7 1.4 %collective-permute-start.19 = (bf16[32,4096]{1,0:T(8,128)(2,1)S(1)}, bf16[32,4096]{1,0:T(8,128)(2,1)S(1)}, u32[]{:S(2)}, u32[]{:S(2)}) collective-permute-start(bf16[32,4096]{1,0:T(8,128)(2,1)S(1)} %collective-permute-done.18.refs_0_), channel_id=1, source_target_pairs={{0,16},{16,0},{1,17},{17,1},{2,18},{18,2},{3,19},{19,3},{4,20},{20... | collective-permute-start | bytes 786440 | tf_op jit(solution)/shard_map/ppermute | solution.py:104
  50.8 3.5 %collective-permute-done.7.refs_0_ = bf16[32,4096]{1,0:T(8,128)(2,1)S(1)} collective-permute-done((bf16[32,4096]{1,0:T(8,128)(2,1)S(1)}, bf16[32,4096]{1,0:T(8,128)(2,1)S(1)}, u32[]{:S(2)}, u32[]{:S(2)}) %collective-permute-start.7) | collective-permute-done | bytes 262176 | tf_op jit(solution)/shard_map/ppermute | solution.py:98
  54.3 1.4 %collective-permute-start.12 = (bf16[32,4096]{1,0:T(8,128)(2,1)S(1)}, bf16[32,4096]{1,0:T(8,128)(2,1)S(1)}, u32[]{:S(2)}, u32[]{:S(2)}) collective-permute-start(bf16[32,4096]{1,0:T(8,128)(2,1)S(1)} %collective-permute-done.7.refs_0_), channel_id=1, source_target_pairs={{0,16},{16,0},{1,17},{17,1},{2,18},{18,2},{3,19},{19,3},{4,20},{20... | collective-permute-start | bytes 786440 | tf_op jit(solution)/shard_map/ppermute | solution.py:104
  56.5 1.5 %collective-permute-done.19.refs_1_ = bf16[32,4096]{1,0:T(8,128)(2,1)S(1)} collective-permute-done((bf16[32,4096]{1,0:T(8,128)(2,1)S(1)}, bf16[32,4096]{1,0:T(8,128)(2,1)S(1)}, u32[]{:S(2)}, u32[]{:S(2)}) %collective-permute-start.19) | collective-permute-done | bytes 262176 | tf_op jit(solution)/shard_map/ppermute | solution.py:104
  58.0 3.2 %collective-permute-done.20.refs_0_ = bf16[32,4096]{1,0:T(8,128)(2,1)S(1)} collective-permute-done((bf16[32,4096]{1,0:T(8,128)(2,1)S(1)}, bf16[32,4096]{1,0:T(8,128)(2,1)S(1)}, u32[]{:S(2)}, u32[]{:S(2)}) %collective-permute-start.20) | collective-permute-done | bytes 262176 | tf_op jit(solution)/shard_map/ppermute | solution.py:98
  62.6 3.8 %collective-permute-done.11.refs_0_ = bf16[32,4096]{1,0:T(8,128)(2,1)S(1)} collective-permute-done((bf16[32,4096]{1,0:T(8,128)(2,1)S(1)}, bf16[32,4096]{1,0:T(8,128)(2,1)S(1)}, u32[]{:S(2)}, u32[]{:S(2)}) %collective-permute-start.11) | collective-permute-done | bytes 262176 | tf_op jit(solution)/shard_map/ppermute | solution.py:98
  68.8 2.7 %collective-permute-done.21.refs_0_ = bf16[32,4096]{1,0:T(8,128)(2,1)} collective-permute-done((bf16[32,4096]{1,0:T(8,128)(2,1)S(1)}, bf16[32,4096]{1,0:T(8,128)(2,1)}, u32[]{:S(2)}, u32[]{:S(2)}) %collective-permute-start.21) | collective-permute-done | bytes 262176 | tf_op jit(solution)/shard_map/ppermute | solution.py:98
  72.3 1.5 %collective-permute-start.23 = (bf16[32,4096]{1,0:T(8,128)(2,1)}, bf16[32,4096]{1,0:T(8,128)(2,1)}, u32[]{:S(2)}, u32[]{:S(2)}) collective-permute-start(bf16[32,4096]{1,0:T(8,128)(2,1)} %collective-permute-done.21.refs_0_), channel_id=1, source_target_pairs={{0,16},{16,0},{1,17},{17,1},{2,18},{18,2},{3,19},{19,3},{4,20},{20... | collective-permute-start | bytes 786440 | tf_op jit(solution)/shard_map/ppermute | solution.py:104
  73.8 1.4 %collective-permute-done.15.refs_0_ = bf16[32,4096]{1,0:T(8,128)(2,1)S(1)} collective-permute-done((bf16[32,4096]{1,0:T(8,128)(2,1)S(1)}, bf16[32,4096]{1,0:T(8,128)(2,1)S(1)}, u32[]{:S(2)}, u32[]{:S(2)}) %collective-permute-start.15) | collective-permute-done | bytes 262176 | tf_op jit(solution)/shard_map/ppermute | solution.py:98
  77.8 1.6 %copy-done.1 = bf16[256,4096]{1,0:T(8,128)(2,1)S(1)} copy-done((bf16[256,4096]{1,0:T(8,128)(2,1)S(1)}, bf16[256,4096]{1,0:T(8,128)(2,1)}, u32[]{:S(2)}) %copy-start.1) | copy-done | bytes 2097176
  84.8 1.8 %shard_map.48.refs_7_ = f32[64,256]{1,0:T(8,128)S(1)} custom-call(bf16[32,4096]{1,0:T(8,128)(2,1)} %collective-permute-done.21.refs_0_, bf16[32,4096]{1,0:T(8,128)(2,1)} %collective-permute-done.23.refs_1_, f32[1,16384]{1,0:T(1,128)S(1)} %bitcast.21, bf16[256,4096]{1,0:T(8,128)(2,1)S(1)} %copy-done.2, f32[64,256]{1,0:T(8,128)S(1)} %shard_map.47.refs_4_), custom_call_target="tpu_custom_call" | custom-call | flops 134217728 | bytes 2621440 | tf_op jit(solution)/shard_map/pallas_call | solution.py:67
  87.6 1.3 %collective-permute-done.24 = f32[2,64,256]{2,1,0:T(8,128)S(1)} collective-permute-done((f32[2,64,256]{2,1,0:T(8,128)S(1)}, f32[2,64,256]{2,1,0:T(8,128)S(1)}, u32[]{:S(2)}, u32[]{:S(2)}) %collective-permute-start.24) | collective-permute-done | bytes 131104 | tf_op jit(solution)/shard_map/ppermute | solution.py:115
  88.9 1.7 %collective-permute-start.25 = (f32[1,64,256]{2,1,0:T(8,128)S(1)}, f32[1,64,256]{2,1,0:T(8,128)S(1)}, u32[]{:S(2)}, u32[]{:S(2)}) collective-permute-start(f32[1,64,256]{2,1,0:T(8,128)S(1)} %constant_dynamic-slice_fusion), channel_id=1, source_target_pairs={{0,2},{1,3},{2,0},{3,1},{4,6},{5,7},{6,4},{7,5},{8,10},{9,11},{10,... | collective-permute-start | bytes 196616 | tf_op jit(solution)/shard_map/ppermute | solution.py:115
  90.6 2.6 %collective-permute-done.25 = f32[1,64,256]{2,1,0:T(8,128)S(1)} collective-permute-done((f32[1,64,256]{2,1,0:T(8,128)S(1)}, f32[1,64,256]{2,1,0:T(8,128)S(1)}, u32[]{:S(2)}, u32[]{:S(2)}) %collective-permute-start.25) | collective-permute-done | bytes 65568 | tf_op jit(solution)/shard_map/ppermute | solution.py:115
  (89 shorter events, 22.8 us)
Async XLA Ops:
  1.1 12.2 %collective-permute-start.5 = (bf16[32,4096]{1,0:T(8,128)(2,1)S(1)}, bf16[32,4096]{1,0:T(8,128)(2,1)S(1)}, u32[]{:S(2)}, u32[]{:S(2)}) collective-permute-start(bf16[32,4096]{1,0:T(8,128)(2,1)S(1)} %slice_select_fusion.3), channel_id=1, source_target_pairs={{0,4},{4,8},{8,12},{12,0},{1,5},{5,9},{9,13},{13,1},{2,6},{6,10},{... | collective-permute-start | bytes 786440 | tf_op jit(solution)/shard_map/ppermute | solution.py:98
  5.2 13.7 %collective-permute-start = (bf16[32,4096]{1,0:T(8,128)(2,1)S(1)}, bf16[32,4096]{1,0:T(8,128)(2,1)S(1)}, u32[]{:S(2)}, u32[]{:S(2)}) collective-permute-start(bf16[32,4096]{1,0:T(8,128)(2,1)S(1)} %slice_select_fusion.2), channel_id=1, source_target_pairs={{0,4},{4,8},{8,12},{12,0},{1,5},{5,9},{9,13},{13,1},{2,6},{6,10},{... | collective-permute-start | bytes 786440 | tf_op jit(solution)/shard_map/ppermute | solution.py:98
  13.0 30.3 %copy-start = (bf16[256,4096]{1,0:T(8,128)(2,1)}, bf16[256,4096]{1,0:T(8,128)(2,1)S(1)}, u32[]{:S(2)}) copy-start(bf16[256,4096]{1,0:T(8,128)(2,1)S(1)} %get-tuple-element.54.refs_2_.refs_3_) | copy-start | bytes 6291460
  13.0 42.7 %copy-start.5 = (bf16[256,4096]{1,0:T(8,128)(2,1)}, bf16[256,4096]{1,0:T(8,128)(2,1)S(1)}, u32[]{:S(2)}) copy-start(bf16[256,4096]{1,0:T(8,128)(2,1)S(1)} %get-tuple-element.53.refs_0_.refs_3_) | copy-start | bytes 6291460
  13.1 48.7 %copy-start.3 = (bf16[256,4096]{1,0:T(8,128)(2,1)}, bf16[256,4096]{1,0:T(8,128)(2,1)S(1)}, u32[]{:S(2)}) copy-start(bf16[256,4096]{1,0:T(8,128)(2,1)S(1)} %get-tuple-element.52.refs_1_.refs_3_) | copy-start | bytes 6291460
  13.3 11.2 %collective-permute-start.9 = (bf16[32,4096]{1,0:T(8,128)(2,1)S(1)}, bf16[32,4096]{1,0:T(8,128)(2,1)S(1)}, u32[]{:S(2)}, u32[]{:S(2)}) collective-permute-start(bf16[32,4096]{1,0:T(8,128)(2,1)S(1)} %slice_select_fusion.1), channel_id=1, source_target_pairs={{0,4},{4,8},{8,12},{12,0},{1,5},{5,9},{9,13},{13,1},{2,6},{6,10},{... | collective-permute-start | bytes 786440 | tf_op jit(solution)/shard_map/ppermute | solution.py:98
  14.7 9.8 %collective-permute-start.6 = (bf16[32,4096]{1,0:T(8,128)(2,1)S(1)}, bf16[32,4096]{1,0:T(8,128)(2,1)S(1)}, u32[]{:S(2)}, u32[]{:S(2)}) collective-permute-start(bf16[32,4096]{1,0:T(8,128)(2,1)S(1)} %collective-permute-done.5.refs_0_), channel_id=1, source_target_pairs={{0,16},{16,0},{1,17},{17,1},{2,18},{18,2},{3,19},{19,3},{4,20},{20... | collective-permute-start | bytes 786440 | tf_op jit(solution)/shard_map/ppermute | solution.py:104
  18.9 19.5 %copy-start.20 = (f32[64,256]{1,0:T(8,128)}, f32[64,256]{1,0:T(8,128)S(1)}, u32[]{:S(2)}) copy-start(f32[64,256]{1,0:T(8,128)S(1)} %shard_map.37.refs_4_) | copy-start | bytes 196612
  18.9 10.2 %collective-permute-start.2 = (bf16[32,4096]{1,0:T(8,128)(2,1)S(1)}, bf16[32,4096]{1,0:T(8,128)(2,1)S(1)}, u32[]{:S(2)}, u32[]{:S(2)}) collective-permute-start(bf16[32,4096]{1,0:T(8,128)(2,1)S(1)} %collective-permute-done.refs_0_), channel_id=1, source_target_pairs={{0,16},{16,0},{1,17},{17,1},{2,18},{18,2},{3,19},{19,3},{4,20},{20... | collective-permute-start | bytes 786440 | tf_op jit(solution)/shard_map/ppermute | solution.py:104
  20.7 9.5 %collective-permute-start.1 = (bf16[32,4096]{1,0:T(8,128)(2,1)S(1)}, bf16[32,4096]{1,0:T(8,128)(2,1)S(1)}, u32[]{:S(2)}, u32[]{:S(2)}) collective-permute-start(bf16[32,4096]{1,0:T(8,128)(2,1)S(1)} %slice_select_fusion), channel_id=1, source_target_pairs={{0,4},{4,8},{8,12},{12,0},{1,5},{5,9},{9,13},{13,1},{2,6},{6,10},{... | collective-permute-start | bytes 786440 | tf_op jit(solution)/shard_map/ppermute | solution.py:98
  24.5 10.2 %collective-permute-start.10 = (bf16[32,4096]{1,0:T(8,128)(2,1)S(1)}, bf16[32,4096]{1,0:T(8,128)(2,1)S(1)}, u32[]{:S(2)}, u32[]{:S(2)}) collective-permute-start(bf16[32,4096]{1,0:T(8,128)(2,1)S(1)} %collective-permute-done.9.refs_0_), channel_id=1, source_target_pairs={{0,16},{16,0},{1,17},{17,1},{2,18},{18,2},{3,19},{19,3},{4,20},{20... | collective-permute-start | bytes 786440 | tf_op jit(solution)/shard_map/ppermute | solution.py:104
  26.3 11.0 %collective-permute-start.13 = (bf16[32,4096]{1,0:T(8,128)(2,1)S(1)}, bf16[32,4096]{1,0:T(8,128)(2,1)S(1)}, u32[]{:S(2)}, u32[]{:S(2)}) collective-permute-start(bf16[32,4096]{1,0:T(8,128)(2,1)S(1)} %collective-permute-done.5.refs_0_), channel_id=1, source_target_pairs={{0,4},{4,8},{8,12},{12,0},{1,5},{5,9},{9,13},{13,1},{2,6},{6,10},{... | collective-permute-start | bytes 786440 | tf_op jit(solution)/shard_map/ppermute | solution.py:98
  30.2 11.4 %collective-permute-start.3 = (bf16[32,4096]{1,0:T(8,128)(2,1)S(1)}, bf16[32,4096]{1,0:T(8,128)(2,1)S(1)}, u32[]{:S(2)}, u32[]{:S(2)}) collective-permute-start(bf16[32,4096]{1,0:T(8,128)(2,1)S(1)} %collective-permute-done.refs_0_), channel_id=1, source_target_pairs={{0,4},{4,8},{8,12},{12,0},{1,5},{5,9},{9,13},{13,1},{2,6},{6,10},{... | collective-permute-start | bytes 786440 | tf_op jit(solution)/shard_map/ppermute | solution.py:98
  30.2 11.4 %collective-permute-start.4 = (bf16[32,4096]{1,0:T(8,128)(2,1)S(1)}, bf16[32,4096]{1,0:T(8,128)(2,1)S(1)}, u32[]{:S(2)}, u32[]{:S(2)}) collective-permute-start(bf16[32,4096]{1,0:T(8,128)(2,1)S(1)} %collective-permute-done.1.refs_0_), channel_id=1, source_target_pairs={{0,16},{16,0},{1,17},{17,1},{2,18},{18,2},{3,19},{19,3},{4,20},{20... | collective-permute-start | bytes 786440 | tf_op jit(solution)/shard_map/ppermute | solution.py:104
  37.3 9.2 %collective-permute-start.14 = (bf16[32,4096]{1,0:T(8,128)(2,1)S(1)}, bf16[32,4096]{1,0:T(8,128)(2,1)S(1)}, u32[]{:S(2)}, u32[]{:S(2)}) collective-permute-start(bf16[32,4096]{1,0:T(8,128)(2,1)S(1)} %collective-permute-done.13.refs_0_), channel_id=1, source_target_pairs={{0,16},{16,0},{1,17},{17,1},{2,18},{18,2},{3,19},{19,3},{4,20},{20... | collective-permute-start | bytes 786440 | tf_op jit(solution)/shard_map/ppermute | solution.py:104
  37.7 11.0 %collective-permute-start.18 = (bf16[32,4096]{1,0:T(8,128)(2,1)S(1)}, bf16[32,4096]{1,0:T(8,128)(2,1)S(1)}, u32[]{:S(2)}, u32[]{:S(2)}) collective-permute-start(bf16[32,4096]{1,0:T(8,128)(2,1)S(1)} %collective-permute-done.9.refs_0_), channel_id=1, source_target_pairs={{0,4},{4,8},{8,12},{12,0},{1,5},{5,9},{9,13},{13,1},{2,6},{6,10},{... | collective-permute-start | bytes 786440 | tf_op jit(solution)/shard_map/ppermute | solution.py:98
  41.6 12.8 %collective-permute-start.7 = (bf16[32,4096]{1,0:T(8,128)(2,1)S(1)}, bf16[32,4096]{1,0:T(8,128)(2,1)S(1)}, u32[]{:S(2)}, u32[]{:S(2)}) collective-permute-start(bf16[32,4096]{1,0:T(8,128)(2,1)S(1)} %collective-permute-done.1.refs_0_), channel_id=1, source_target_pairs={{0,4},{4,8},{8,12},{12,0},{1,5},{5,9},{9,13},{13,1},{2,6},{6,10},{... | collective-permute-start | bytes 786440 | tf_op jit(solution)/shard_map/ppermute | solution.py:98
  41.6 12.8 %collective-permute-start.8 = (bf16[32,4096]{1,0:T(8,128)(2,1)S(1)}, bf16[32,4096]{1,0:T(8,128)(2,1)S(1)}, u32[]{:S(2)}, u32[]{:S(2)}) collective-permute-start(bf16[32,4096]{1,0:T(8,128)(2,1)S(1)} %collective-permute-done.3.refs_0_), channel_id=1, source_target_pairs={{0,16},{16,0},{1,17},{17,1},{2,18},{18,2},{3,19},{19,3},{4,20},{20... | collective-permute-start | bytes 786440 | tf_op jit(solution)/shard_map/ppermute | solution.py:104
  48.7 9.2 %collective-permute-start.19 = (bf16[32,4096]{1,0:T(8,128)(2,1)S(1)}, bf16[32,4096]{1,0:T(8,128)(2,1)S(1)}, u32[]{:S(2)}, u32[]{:S(2)}) collective-permute-start(bf16[32,4096]{1,0:T(8,128)(2,1)S(1)} %collective-permute-done.18.refs_0_), channel_id=1, source_target_pairs={{0,16},{16,0},{1,17},{17,1},{2,18},{18,2},{3,19},{19,3},{4,20},{20... | collective-permute-start | bytes 786440 | tf_op jit(solution)/shard_map/ppermute | solution.py:104
  50.1 11.0 %collective-permute-start.20 = (bf16[32,4096]{1,0:T(8,128)(2,1)S(1)}, bf16[32,4096]{1,0:T(8,128)(2,1)S(1)}, u32[]{:S(2)}, u32[]{:S(2)}) collective-permute-start(bf16[32,4096]{1,0:T(8,128)(2,1)S(1)} %collective-permute-done.13.refs_0_), channel_id=1, source_target_pairs={{0,4},{4,8},{8,12},{12,0},{1,5},{5,9},{9,13},{13,1},{2,6},{6,10},{... | collective-permute-start | bytes 786440 | tf_op jit(solution)/shard_map/ppermute | solution.py:98
  54.3 12.0 %collective-permute-start.11 = (bf16[32,4096]{1,0:T(8,128)(2,1)S(1)}, bf16[32,4096]{1,0:T(8,128)(2,1)S(1)}, u32[]{:S(2)}, u32[]{:S(2)}) collective-permute-start(bf16[32,4096]{1,0:T(8,128)(2,1)S(1)} %collective-permute-done.3.refs_0_), channel_id=1, source_target_pairs={{0,4},{4,8},{8,12},{12,0},{1,5},{5,9},{9,13},{13,1},{2,6},{6,10},{... | collective-permute-start | bytes 786440 | tf_op jit(solution)/shard_map/ppermute | solution.py:98
  54.3 12.0 %collective-permute-start.12 = (bf16[32,4096]{1,0:T(8,128)(2,1)S(1)}, bf16[32,4096]{1,0:T(8,128)(2,1)S(1)}, u32[]{:S(2)}, u32[]{:S(2)}) collective-permute-start(bf16[32,4096]{1,0:T(8,128)(2,1)S(1)} %collective-permute-done.7.refs_0_), channel_id=1, source_target_pairs={{0,16},{16,0},{1,17},{17,1},{2,18},{18,2},{3,19},{19,3},{4,20},{20... | collective-permute-start | bytes 786440 | tf_op jit(solution)/shard_map/ppermute | solution.py:104
  58.0 8.4 %copy-start.10 = (bf16[32,4096]{1,0:T(8,128)(2,1)}, bf16[32,4096]{1,0:T(8,128)(2,1)S(1)}, u32[]{:S(2)}) copy-start(bf16[32,4096]{1,0:T(8,128)(2,1)S(1)} %collective-permute-done.19.refs_1_) | copy-start | bytes 786436
  61.1 14.1 %copy-start.8 = (bf16[32,4096]{1,0:T(8,128)(2,1)}, bf16[32,4096]{1,0:T(8,128)(2,1)S(1)}, u32[]{:S(2)}) copy-start(bf16[32,4096]{1,0:T(8,128)(2,1)S(1)} %collective-permute-done.20.refs_0_) | copy-start | bytes 786436
  61.1 10.4 %collective-permute-start.21 = (bf16[32,4096]{1,0:T(8,128)(2,1)S(1)}, bf16[32,4096]{1,0:T(8,128)(2,1)}, u32[]{:S(2)}, u32[]{:S(2)}) collective-permute-start(bf16[32,4096]{1,0:T(8,128)(2,1)S(1)} %collective-permute-done.18.refs_0_), channel_id=1, source_target_pairs={{0,4},{4,8},{8,12},{12,0},{1,5},{5,9},{9,13},{13,1},{2,6},{6,10},{... | collective-permute-start | bytes 786440 | tf_op jit(solution)/shard_map/ppermute | solution.py:98
  61.1 10.4 %collective-permute-start.22 = (bf16[32,4096]{1,0:T(8,128)(2,1)S(1)}, bf16[32,4096]{1,0:T(8,128)(2,1)S(1)}, u32[]{:S(2)}, u32[]{:S(2)}) collective-permute-start(bf16[32,4096]{1,0:T(8,128)(2,1)S(1)} %collective-permute-done.20.refs_0_), channel_id=1, source_target_pairs={{0,16},{16,0},{1,17},{17,1},{2,18},{18,2},{3,19},{19,3},{4,20},{20... | collective-permute-start | bytes 786440 | tf_op jit(solution)/shard_map/ppermute | solution.py:104
  67.0 8.2 %collective-permute-start.15 = (bf16[32,4096]{1,0:T(8,128)(2,1)S(1)}, bf16[32,4096]{1,0:T(8,128)(2,1)S(1)}, u32[]{:S(2)}, u32[]{:S(2)}) collective-permute-start(bf16[32,4096]{1,0:T(8,128)(2,1)S(1)} %collective-permute-done.7.refs_0_), channel_id=1, source_target_pairs={{0,4},{4,8},{8,12},{12,0},{1,5},{5,9},{9,13},{13,1},{2,6},{6,10},{... | collective-permute-start | bytes 786440 | tf_op jit(solution)/shard_map/ppermute | solution.py:98
  67.0 9.2 %collective-permute-start.16 = (bf16[32,4096]{1,0:T(8,128)(2,1)S(1)}, bf16[32,4096]{1,0:T(8,128)(2,1)S(1)}, u32[]{:S(2)}, u32[]{:S(2)}) collective-permute-start(bf16[32,4096]{1,0:T(8,128)(2,1)S(1)} %collective-permute-done.11.refs_0_), channel_id=1, source_target_pairs={{0,16},{16,0},{1,17},{17,1},{2,18},{18,2},{3,19},{19,3},{4,20},{20... | collective-permute-start | bytes 786440 | tf_op jit(solution)/shard_map/ppermute | solution.py:104
  72.3 11.7 %collective-permute-start.23 = (bf16[32,4096]{1,0:T(8,128)(2,1)}, bf16[32,4096]{1,0:T(8,128)(2,1)}, u32[]{:S(2)}, u32[]{:S(2)}) collective-permute-start(bf16[32,4096]{1,0:T(8,128)(2,1)} %collective-permute-done.21.refs_0_), channel_id=1, source_target_pairs={{0,16},{16,0},{1,17},{17,1},{2,18},{18,2},{3,19},{19,3},{4,20},{20... | collective-permute-start | bytes 786440 | tf_op jit(solution)/shard_map/ppermute | solution.py:104
  77.0 9.6 %collective-permute-start.17 = (bf16[32,4096]{1,0:T(8,128)(2,1)S(1)}, bf16[32,4096]{1,0:T(8,128)(2,1)S(1)}, u32[]{:S(2)}, u32[]{:S(2)}) collective-permute-start(bf16[32,4096]{1,0:T(8,128)(2,1)S(1)} %collective-permute-done.15.refs_0_), channel_id=1, source_target_pairs={{0,16},{16,0},{1,17},{17,1},{2,18},{18,2},{3,19},{19,3},{4,20},{20... | collective-permute-start | bytes 786440 | tf_op jit(solution)/shard_map/ppermute | solution.py:104
  87.5 1.4 %collective-permute-start.24 = (f32[2,64,256]{2,1,0:T(8,128)S(1)}, f32[2,64,256]{2,1,0:T(8,128)S(1)}, u32[]{:S(2)}, u32[]{:S(2)}) collective-permute-start(f32[2,64,256]{2,1,0:T(8,128)S(1)} %dynamic-slice_bitcast_fusion), channel_id=1, source_target_pairs={{0,1},{1,0},{2,3},{3,2},{4,5},{5,4},{6,7},{7,6},{8,9},{9,8},{10,11... | collective-permute-start | bytes 393224 | tf_op jit(solution)/shard_map/ppermute | solution.py:115
  88.9 4.3 %collective-permute-start.25 = (f32[1,64,256]{2,1,0:T(8,128)S(1)}, f32[1,64,256]{2,1,0:T(8,128)S(1)}, u32[]{:S(2)}, u32[]{:S(2)}) collective-permute-start(f32[1,64,256]{2,1,0:T(8,128)S(1)} %constant_dynamic-slice_fusion), channel_id=1, source_target_pairs={{0,2},{1,3},{2,0},{3,1},{4,6},{5,7},{6,4},{7,5},{8,10},{9,11},{10,... | collective-permute-start | bytes 196616 | tf_op jit(solution)/shard_map/ppermute | solution.py:115
  (17 other events, 32.2 us)

commit v10 on v9

--- a/solution.py
+++ b/solution.py
@@ -8,7 +8,7 @@
 from jax.sharding import PartitionSpec as P
 
 CONTRACT = (((1,), (1,)), ((), ()))
-CHUNKS = (4, 4, 4, 4)
+CHUNKS = (4, 4, 4, 3, 1)
 
 
 def product(rows, scale, train, unit):
@@ -33,25 +33,27 @@
     out[...] = total
 
 
-def arrived_rows(parts):
-    return lambda here: jnp.concatenate([p[:, here] for p in parts], axis=0)
+def arrived(groups, scale, refs):
+    refs, total = list(refs), None
+    for start, unit, count in groups:
+        parts, train, refs = refs[:count], refs[count], refs[count + 1 :]
+        rows = lambda here: jnp.concatenate([p[:, here] for p in parts], axis=0)
+        column = lambda here: scale[:, start + here.start : start + here.stop]
+        part = product(rows, column, train, unit)
+        total = part if total is None else total + part
+    return total, refs
 
 
-def part_kernel(start, unit, n_parts, has_base, *refs):
-    parts, (scale, train) = refs[:n_parts], refs[n_parts : n_parts + 2]
-    column = lambda here: scale[:, start + here.start : start + here.stop]
-    total = product(arrived_rows(parts), column, train, unit)
-    refs[-1][...] = total + refs[n_parts + 2][...] if has_base else total
+def part_kernel(groups, scale, *refs):
+    total, (*base, out) = arrived(groups, scale, refs)
+    out[...] = total + base[0][...] if base else total
 
 
-def last_kernel(n_grp, n_ex, start, unit, n_parts, *refs):
-    parts, (scale, train) = refs[:n_parts], refs[n_parts : n_parts + 2]
-    sums, (out, kept) = refs[n_parts + 2 : -2], refs[-2:]
-    column = lambda here: scale[:, start + here.start : start + here.stop]
-    total = product(arrived_rows(parts), column, train, unit) + sums[-1][...]
+def last_kernel(n_grp, n_ex, groups, scale, *refs):
+    total, (*sums, out, kept) = arrived(groups, scale, refs)
     queries = total.shape[0]
     half = queries // n_grp
-    for t, value in enumerate([s[...] for s in sums[:-1]] + [total]):
+    for t, value in enumerate([s[...] for s in sums[:-1]] + [total + sums[-1][...]]):
         kept[t * queries : (t + 1) * queries, :] = value
     ex, grp = lax.axis_index("ex"), lax.axis_index("grp")
     for b in range(n_ex):
@@ -73,7 +75,7 @@
         cost_estimate=pl.CostEstimate(
             flops=2 * rows * docs * width, bytes_accessed=2 * (rows + docs) * width, transcendentals=0
         ),
-        compiler_params=pltpu.CompilerParams(vmem_limit_bytes=16 * 1024 * 1024),
+        compiler_params=pltpu.CompilerParams(vmem_limit_bytes=4 * 1024 * 1024),
     )(*operands)
 
 
@@ -94,14 +96,15 @@
             return lax.optimization_barrier((block, waits))[0] if waits else block
 
         def hop(block):
-            waits = hops[-2:-1] + swaps[-4:-3] + made[-6:-5] + (first if len(hops) == 3 else [])
+            waits = hops[-2:-1] + swaps[-4:-3] + (first if len(hops) == 3 else [])
             hops.append(lax.ppermute(after(block, *waits), "ex", ring))
             return hops[-1]
 
         def swap(block):
             if n_grp == 1:
                 return [block]
-            swaps.append(lax.ppermute(after(block, *swaps[-2:-1]), "grp", [(0, 1), (1, 0)]))
+            waits = swaps[-2:-1] + made[-3:-2]
+            swaps.append(lax.ppermute(after(block, *waits), "grp", [(0, 1), (1, 0)]))
             return [block, swaps[-1]]
 
         def sum_over_feat(sums):
@@ -116,44 +119,54 @@
                 bit *= 2
             return held[0]
 
-        def share(rows, start, width):
+        def share(rows, start, width, other):
             columns = slice(start, start + width)
             if n_grp == 1:
                 return rows[:, columns]
-            return jnp.where(grp == 0, rows[:half, columns], rows[half:, columns])
+            return jnp.where(grp == other, rows[:half, columns], rows[half:, columns])
 
         scale = (1.0 / (hess + jnp.float32(0.1))).reshape(1, feats)
         widths = [width * unit for width in CHUNKS]
         starts = [sum(widths[:c]) for c in range(len(widths))]
         held = []
-        for start, width in zip(starts, widths):
-            held.append(share(after(test, *held[-1:]), start, width))
+        for c, (start, width) in enumerate(zip(starts, widths)):
+            rows = after(test, *held[-1:])
+            mine = share(rows, start, width, 0)
+            if c == len(widths) - 1 and n_grp > 1:
+                mine = jnp.concatenate([mine, share(rows, start, width, 1)])
+            held.append(mine)
         trains = [train[:, start : start + width] for start, width in zip(starts, widths)]
         own = call(
             functools.partial(own_kernel, starts, unit), queries, docs, feats, [test, scale, *trains]
         )
         first.append(own)
-        sums = [own]
-        for t in range(1, n_ex):
-            total = None
-            for c, (start, width) in enumerate(zip(starts, widths)):
-                held[c] = hop(held[c])
-                parts = swap(held[c])
-                operands = [*parts, scale, trains[c]]
-                if t == n_ex - 1 and c == len(widths) - 1:
-                    total = call(
-                        functools.partial(last_kernel, n_grp, n_ex, start, unit, len(parts)),
-                        n_ex * queries, docs, width, [*operands, *sums, total],
-                        [pltpu.VMEM((n_ex * queries, docs), jnp.float32)],
-                    )
-                else:
-                    total = call(
-                        functools.partial(part_kernel, start, unit, len(parts), total is not None),
-                        queries, docs, width, operands + ([] if total is None else [total]),
-                    )
-                made.append(total)
-            sums.append(total)
-        return sum_over_feat(sums[-1]).T
+        final, whole = n_ex - 1, len(widths) - 1
+        order = [(t, c) for t in range(1, final) for c in range(whole)]
+        waiting = [(t, whole) for t in range(1, n_ex)]
+        for c in range(whole):
+            order.append((final, c))
+            order += [waiting.pop(0) for _ in range(len(waiting) // (whole - c))]
+
+        sums, groups, operands = [own] + [None] * final, [], []
+        for t, c in order:
+            held[c] = hop(held[c])
+            parts = [held[c]] if c == whole else swap(held[c])
+            group, arrays = (starts[c], unit, len(parts)), [*parts, trains[c]]
+            if t == final and c >= whole - 1:
+                groups.append(group)
+                operands += arrays
+                continue
+            base = [] if sums[t] is None else [sums[t]]
+            sums[t] = call(
+                functools.partial(part_kernel, [group]), queries, docs, widths[c], [scale, *arrays, *base]
+            )
+            made.append(sums[t])
+        out = call(
+            functools.partial(last_kernel, n_grp, n_ex, groups),
+            n_ex * queries, docs, sum(widths[whole - 1 :]), [scale, *operands, *sums],
+            [pltpu.VMEM((n_ex * queries, docs), jnp.float32)],
+        )
+        return sum_over_feat(out).T
 
 
     return jax.shard_map(

time: 94.2 us -> 107 us (1.14)
  Pallas kernels: 12.8 us -> 19.2 us
  local copies, waits for them, and re-layouts: 10.8 us -> 15.9 us
  starting transfers between devices: 23.7 us -> 24.9 us
  other arithmetic: 4.91 us -> 3.74 us
    ppermute x12 -> x15, waiting for transfers between devices: 27.6 us -> 37.1 us  [hop(): hops.append(lax.ppermute(after(block, *waits), 'ex', ring))]
    ppermute x12, waiting for transfers between devices: 9.83 us -> 0.99 us  [swap(): swaps.append(lax.ppermute(after(block, *waits), 'grp', [(0, 1), (1, 0)]))]
    pallas_call x13 -> x15, Pallas kernels: 12.8 us -> 19.2 us  [call(): pl.pallas_call(kernel, out_shape=jax.ShapeDtypeStruct((rows, docs), jnp.f...]
    unnamed x46 -> x44, local copies, waits for them, and re-layouts: 6.76 us -> 9.37 us
    slice x1 -> x3, local copies, waits for them, and re-layouts: 4.03 us -> 6.49 us  [on_device(): train[:, start:start + width]]
    select_n x4 -> x5, other arithmetic: 4.24 us -> 3.06 us  [share(): return jnp.where(grp == other, rows[:half, columns], rows[half:, columns])]
    ppermute x12 -> x15, starting transfers between devices: 6.16 us -> 6.21 us  [hop(): hops.append(lax.ppermute(after(block, *waits), 'ex', ring))]
  transfers between devices with their start and end apart: 26 -> 29, of which waited for: 18 -> 13; matrix products, arithmetic and copies ran while one was open for 8% -> 8% of each run, Pallas kernels for 13% -> 16%
where the time goes in v10:
time: 107 us; the launch traced here: 106 us
  waiting for transfers between devices  41.7 us (39%)
  starting transfers between devices  24.9 us (23%)
  Pallas kernels  19.2 us (18%)
  local copies, waits for them, and re-layouts  15.9 us (15%)
  other arithmetic  3.74 us (3%)
    ppermute x15, waiting for transfers between devices, hop(): hops.append(lax.ppermute(after(block, *waits), 'ex', ring))  37.1 us
    pallas_call x15, Pallas kernels, call(): pl.pallas_call(kernel, out_shape=jax.ShapeDtypeStruct((rows, docs), jnp.f...  19.2 us
    ppermute x12, starting transfers between devices, swap(): swaps.append(lax.ppermute(after(block, *waits), 'grp', [(0, 1), (1, 0)]))  16.5 us
    unnamed x44, local copies, waits for them, and re-layouts  9.37 us
    slice x3, local copies, waits for them, and re-layouts, on_device(): train[:, start:start + width]  6.49 us
    ppermute x15, starting transfers between devices, hop(): hops.append(lax.ppermute(after(block, *waits), 'ex', ring))  6.21 us
    ppermute x2, waiting for transfers between devices, sum_over_feat(): lax.ppermute(away, 'feat', [(i, i ^ bit) for i in range(n_feat)])  3.7 us
    select_n x5, other arithmetic, share(): return jnp.where(grp == other, rows[:half, columns], rows[half:, columns])  3.06 us
  transfers between devices with their start and end apart: 29, of which 13 were waited for; matrix products, arithmetic and copies ran while one was open for 8% of the time, Pallas kernels for 16%

profile of v10, /device:TPU:0, one launch (start us, length us, event | category | flops | bytes accessed | tf_op | source)
XLA Modules:
  0.0 106.0 jit_solution(11282938934612503803)
XLA Ops:
  1.1 3.1 %collective-permute-start.4 = (bf16[32,4096]{1,0:T(8,128)(2,1)S(1)}, bf16[32,4096]{1,0:T(8,128)(2,1)S(1)}, u32[]{:S(2)}, u32[]{:S(2)}) collective-permute-start(bf16[32,4096]{1,0:T(8,128)(2,1)S(1)} %slice_select_fusion.2), channel_id=1, source_target_pairs={{0,4},{4,8},{8,12},{12,0},{1,5},{5,9},{9,13},{13,1},{2,6},{6,10},{... | collective-permute-start | bytes 786440 | tf_op jit(solution)/shard_map/ppermute | solution.py:100
  5.2 1.6 %collective-permute-start = (bf16[32,4096]{1,0:T(8,128)(2,1)S(1)}, bf16[32,4096]{1,0:T(8,128)(2,1)S(1)}, u32[]{:S(2)}, u32[]{:S(2)}) collective-permute-start(bf16[32,4096]{1,0:T(8,128)(2,1)S(1)} %slice_select_fusion.1), channel_id=1, source_target_pairs={{0,4},{4,8},{8,12},{12,0},{1,5},{5,9},{9,13},{13,1},{2,6},{6,10},{... | collective-permute-start | bytes 786440 | tf_op jit(solution)/shard_map/ppermute | solution.py:100
  6.9 3.5 %fusion = (bf16[256,4096]{1,0:T(8,128)(2,1)S(1)}, bf16[256,4096]{1,0:T(8,128)(2,1)S(1)}, bf16[256,4096]{1,0:T(8,128)(2,1)S(1)}) fusion(bf16[256,16384]{1,0:T(8,128)(2,1)} %param.3), kind=kLoop, calls=%fused_computation.12 | loop fusion | bytes 12582912 | tf_op jit(solution)/shard_map/slice | solution.py:138
  10.5 2.8 %collective-permute-done.4.refs_0_ = bf16[32,4096]{1,0:T(8,128)(2,1)S(1)} collective-permute-done((bf16[32,4096]{1,0:T(8,128)(2,1)S(1)}, bf16[32,4096]{1,0:T(8,128)(2,1)S(1)}, u32[]{:S(2)}, u32[]{:S(2)}) %collective-permute-start.4) | collective-permute-done | bytes 262176 | tf_op jit(solution)/shard_map/ppermute | solution.py:100
  13.3 1.7 %collective-permute-start.5 = (bf16[32,4096]{1,0:T(8,128)(2,1)S(1)}, bf16[32,4096]{1,0:T(8,128)(2,1)S(1)}, u32[]{:S(2)}, u32[]{:S(2)}) collective-permute-start(bf16[32,4096]{1,0:T(8,128)(2,1)S(1)} %collective-permute-done.4.refs_0_), channel_id=1, source_target_pairs={{0,16},{16,0},{1,17},{17,1},{2,18},{18,2},{3,19},{19,3},{4,20},{20... | collective-permute-start | bytes 786440 | tf_op jit(solution)/shard_map/ppermute | solution.py:107
  15.1 3.8 %collective-permute-done.refs_0_ = bf16[32,4096]{1,0:T(8,128)(2,1)S(1)} collective-permute-done((bf16[32,4096]{1,0:T(8,128)(2,1)S(1)}, bf16[32,4096]{1,0:T(8,128)(2,1)S(1)}, u32[]{:S(2)}, u32[]{:S(2)}) %collective-permute-start) | collective-permute-done | bytes 262176 | tf_op jit(solution)/shard_map/ppermute | solution.py:100
  18.9 1.8 %collective-permute-start.2 = (bf16[32,4096]{1,0:T(8,128)(2,1)S(1)}, bf16[32,4096]{1,0:T(8,128)(2,1)S(1)}, u32[]{:S(2)}, u32[]{:S(2)}) collective-permute-start(bf16[32,4096]{1,0:T(8,128)(2,1)S(1)} %collective-permute-done.refs_0_), channel_id=1, source_target_pairs={{0,16},{16,0},{1,17},{17,1},{2,18},{18,2},{3,19},{19,3},{4,20},{20... | collective-permute-start | bytes 786440 | tf_op jit(solution)/shard_map/ppermute | solution.py:107
  20.7 1.5 %slice.58.refs_3_.refs_2_ = bf16[256,3072]{1,0:T(8,128)(2,1)S(1)} slice(bf16[256,16384]{1,0:T(8,128)(2,1)} %param.3), slice={[0:256], [12288:15360]} | slice | bytes 3145728 | tf_op jit(solution)/shard_map/slice | solution.py:138
  22.2 1.5 %slice.59.refs_4_.refs_1_ = bf16[256,1024]{1,0:T(8,128)(2,1)S(1)} slice(bf16[256,16384]{1,0:T(8,128)(2,1)} %param.3), slice={[0:256], [15360:16384]} | slice | bytes 1048576 | tf_op jit(solution)/shard_map/slice | solution.py:138
  23.7 2.7 %shard_map.37.refs_5_ = f32[64,256]{1,0:T(8,128)S(1)} custom-call(bf16[64,16384]{1,0:T(8,128)(2,1)S(1)} %copy-done.9, f32[1,16384]{1,0:T(1,128)S(1)} %bitcast.10, bf16[256,4096]{1,0:T(8,128)(2,1)S(1)} %get-tuple-element.61.refs_0_.refs_2_, bf16[256,4096]{1,0:T(8,128)(2,1)S(1)} %get-tuple-element.60.refs_1_.refs_2_, ...), custom_call_target="tpu_custom_call" | custom-call | flops 536870912 | bytes 10485760 | tf_op jit(solution)/shard_map/pallas_call | solution.py:69
  26.4 1.3 %collective-permute-start.9 = (bf16[32,4096]{1,0:T(8,128)(2,1)S(1)}, bf16[32,4096]{1,0:T(8,128)(2,1)}, u32[]{:S(2)}, u32[]{:S(2)}) collective-permute-start(bf16[32,4096]{1,0:T(8,128)(2,1)S(1)} %collective-permute-done.4.refs_0_), channel_id=1, source_target_pairs={{0,4},{4,8},{8,12},{12,0},{1,5},{5,9},{9,13},{13,1},{2,6},{6,10},{... | collective-permute-start | bytes 786440 | tf_op jit(solution)/shard_map/ppermute | solution.py:100
  28.3 7.8 %collective-permute-done.1.refs_0_ = bf16[32,3072]{1,0:T(8,128)(2,1)S(1)} collective-permute-done((bf16[32,3072]{1,0:T(8,128)(2,1)S(1)}, bf16[32,3072]{1,0:T(8,128)(2,1)S(1)}, u32[]{:S(2)}, u32[]{:S(2)}) %collective-permute-start.1) | collective-permute-done | bytes 196640 | tf_op jit(solution)/shard_map/ppermute | solution.py:100
  37.9 3.9 %collective-permute-done.9.refs_0_ = bf16[32,4096]{1,0:T(8,128)(2,1)} collective-permute-done((bf16[32,4096]{1,0:T(8,128)(2,1)S(1)}, bf16[32,4096]{1,0:T(8,128)(2,1)}, u32[]{:S(2)}, u32[]{:S(2)}) %collective-permute-start.9) | collective-permute-done | bytes 262176 | tf_op jit(solution)/shard_map/ppermute | solution.py:100
  42.8 4.6 %collective-permute-done.3.refs_0_ = bf16[32,4096]{1,0:T(8,128)(2,1)} collective-permute-done((bf16[32,4096]{1,0:T(8,128)(2,1)S(1)}, bf16[32,4096]{1,0:T(8,128)(2,1)}, u32[]{:S(2)}, u32[]{:S(2)}) %collective-permute-start.3) | collective-permute-done | bytes 262176 | tf_op jit(solution)/shard_map/ppermute | solution.py:100
  49.9 2.4 %collective-permute-done.11.refs_0_ = bf16[32,4096]{1,0:T(8,128)(2,1)} collective-permute-done((bf16[32,4096]{1,0:T(8,128)(2,1)S(1)}, bf16[32,4096]{1,0:T(8,128)(2,1)}, u32[]{:S(2)}, u32[]{:S(2)}) %collective-permute-start.11) | collective-permute-done | bytes 262176 | tf_op jit(solution)/shard_map/ppermute | solution.py:100
  52.6 4.0 %collective-permute-done.7.refs_0_ = bf16[32,3072]{1,0:T(8,128)(2,1)S(1)} collective-permute-done((bf16[32,3072]{1,0:T(8,128)(2,1)S(1)}, bf16[32,3072]{1,0:T(8,128)(2,1)S(1)}, u32[]{:S(2)}, u32[]{:S(2)}) %collective-permute-start.7) | collective-permute-done | bytes 196640 | tf_op jit(solution)/shard_map/ppermute | solution.py:100
  58.0 1.6 %copy-done.4 = bf16[256,4096]{1,0:T(8,128)(2,1)S(1)} copy-done((bf16[256,4096]{1,0:T(8,128)(2,1)S(1)}, bf16[256,4096]{1,0:T(8,128)(2,1)}, u32[]{:S(2)}) %copy-start.4) | copy-done | bytes 2097176
  60.6 1.9 %shard_map.42.refs_3_ = f32[64,256]{1,0:T(8,128)S(1)} custom-call(f32[1,16384]{1,0:T(1,128)S(1)} %bitcast.15, bf16[32,4096]{1,0:T(8,128)(2,1)} %collective-permute-done.9.refs_0_, bf16[32,4096]{1,0:T(8,128)(2,1)S(1)} %copy-done.13, bf16[256,4096]{1,0:T(8,128)(2,1)S(1)} %copy-done.4), custom_call_target="tpu_custom_call" | custom-call | flops 134217728 | bytes 2621440 | tf_op jit(solution)/shard_map/pallas_call | solution.py:69
  62.4 1.8 %collective-permute-start.17 = (bf16[32,3072]{1,0:T(8,128)(2,1)S(1)}, bf16[32,3072]{1,0:T(8,128)(2,1)S(1)}, u32[]{:S(2)}, u32[]{:S(2)}) collective-permute-start(bf16[32,3072]{1,0:T(8,128)(2,1)S(1)} %copy-done.17), channel_id=1, source_target_pairs={{0,16},{16,0},{1,17},{17,1},{2,18},{18,2},{3,19},{19,3},{4,20},{20... | collective-permute-start | bytes 589832 | tf_op jit(solution)/shard_map/ppermute | solution.py:107
  64.3 1.7 %shard_map.43.refs_3_ = f32[64,256]{1,0:T(8,128)S(1)} custom-call(f32[1,16384]{1,0:T(1,128)S(1)} %bitcast.16, bf16[32,4096]{1,0:T(8,128)(2,1)} %collective-permute-done.3.refs_0_, bf16[32,4096]{1,0:T(8,128)(2,1)S(1)} %copy-done.15, bf16[256,4096]{1,0:T(8,128)(2,1)S(1)} %copy-done.1, f32[64,256]{1,0:T(8,128)S(1)} %shard_map.42.refs_3_), custom_call_target="tpu_custom_call" | custom-call | flops 134217728 | bytes 2621440 | tf_op jit(solution)/shard_map/pallas_call | solution.py:69
  68.0 1.8 %shard_map.44.refs_3_ = f32[64,256]{1,0:T(8,128)S(1)} custom-call(f32[1,16384]{1,0:T(1,128)S(1)} %bitcast.17, bf16[32,4096]{1,0:T(8,128)(2,1)} %collective-permute-done.11.refs_0_, bf16[32,4096]{1,0:T(8,128)(2,1)} %collective-permute-done.15.refs_1_, bf16[256,4096]{1,0:T(8,128)(2,1)S(1)} %get-tuple-element.59.refs_2_, f32[64,256]{1,0:T(8,128)S(1)} %shard_map.43.refs_3_), custom_call_target="tpu_custom_call" | custom-call | flops 134217728 | bytes 2621440 | tf_op jit(solution)/shard_map/pallas_call | solution.py:69
  70.5 2.4 %collective-permute-start.19 = (bf16[32,4096]{1,0:T(8,128)(2,1)S(1)}, bf16[32,4096]{1,0:T(8,128)(2,1)S(1)}, u32[]{:S(2)}, u32[]{:S(2)}) collective-permute-start(bf16[32,4096]{1,0:T(8,128)(2,1)S(1)} %collective-permute-done.13.refs_0_), channel_id=1, source_target_pairs={{0,16},{16,0},{1,17},{17,1},{2,18},{18,2},{3,19},{19,3},{4,20},{20... | collective-permute-start | bytes 786440 | tf_op jit(solution)/shard_map/ppermute | solution.py:107
  73.0 4.6 %collective-permute-done.16.refs_0_ = bf16[32,4096]{1,0:T(8,128)(2,1)S(1)} collective-permute-done((bf16[32,4096]{1,0:T(8,128)(2,1)}, bf16[32,4096]{1,0:T(8,128)(2,1)S(1)}, u32[]{:S(2)}, u32[]{:S(2)}) %collective-permute-start.16) | collective-permute-done | bytes 262176 | tf_op jit(solution)/shard_map/ppermute | solution.py:100
  77.6 1.7 %shard_map.48.refs_3_ = f32[64,256]{1,0:T(8,128)S(1)} custom-call(f32[1,16384]{1,0:T(1,128)S(1)} %bitcast.18, bf16[32,4096]{1,0:T(8,128)(2,1)} %collective-permute-done.20.refs_0_, bf16[32,4096]{1,0:T(8,128)(2,1)S(1)} %collective-permute-done.24.refs_1_, bf16[256,4096]{1,0:T(8,128)(2,1)S(1)} %copy-done.5), custom_call_target="tpu_custom_call" | custom-call | flops 134217728 | bytes 2621440 | tf_op jit(solution)/shard_map/pallas_call | solution.py:69
  79.3 3.1 %collective-permute-start.26 = (bf16[32,4096]{1,0:T(8,128)(2,1)S(1)}, bf16[32,4096]{1,0:T(8,128)(2,1)}, u32[]{:S(2)}, u32[]{:S(2)}) collective-permute-start(bf16[32,4096]{1,0:T(8,128)(2,1)S(1)} %collective-permute-done.16.refs_0_), channel_id=1, source_target_pairs={{0,16},{16,0},{1,17},{17,1},{2,18},{18,2},{3,19},{19,3},{4,20},{20... | collective-permute-start | bytes 786440 | tf_op jit(solution)/shard_map/ppermute | solution.py:107
  83.5 2.4 %collective-permute-done.18.refs_0_ = bf16[32,3072]{1,0:T(8,128)(2,1)} collective-permute-done((bf16[32,3072]{1,0:T(8,128)(2,1)S(1)}, bf16[32,3072]{1,0:T(8,128)(2,1)}, u32[]{:S(2)}, u32[]{:S(2)}) %collective-permute-start.18) | collective-permute-done | bytes 196640 | tf_op jit(solution)/shard_map/ppermute | solution.py:100
  85.9 3.6 %collective-permute-start.22 = (bf16[32,3072]{1,0:T(8,128)(2,1)}, bf16[32,3072]{1,0:T(8,128)(2,1)}, u32[]{:S(2)}, u32[]{:S(2)}) collective-permute-start(bf16[32,3072]{1,0:T(8,128)(2,1)} %collective-permute-done.18.refs_0_), channel_id=1, source_target_pairs={{0,16},{16,0},{1,17},{17,1},{2,18},{18,2},{3,19},{19,3},{4,20},{20... | collective-permute-start | bytes 589832 | tf_op jit(solution)/shard_map/ppermute | solution.py:107
  89.5 1.4 %copy-done.7 = bf16[256,3072]{1,0:T(8,128)(2,1)S(1)} copy-done((bf16[256,3072]{1,0:T(8,128)(2,1)S(1)}, bf16[256,3072]{1,0:T(8,128)(2,1)}, u32[]{:S(2)}) %copy-start.7) | copy-done | bytes 1572888
  95.5 1.8 %shard_map.50.refs_8_ = f32[64,256]{1,0:T(8,128)S(1)} custom-call(f32[1,16384]{1,0:T(1,128)S(1)} %bitcast.23, bf16[32,4096]{1,0:T(8,128)(2,1)S(1)} %collective-permute-done.16.refs_0_, bf16[32,4096]{1,0:T(8,128)(2,1)} %collective-permute-done.26.refs_1_, bf16[256,4096]{1,0:T(8,128)(2,1)S(1)} %get-tuple-element.59.refs_2_, f32[64,256]{1,0:T(8,128)S(1)} %shard_map.49.refs_3_), custom_call_target="tpu_custom_call" | custom-call | flops 134217728 | bytes 2621440 | tf_op jit(solution)/shard_map/pallas_call | solution.py:69
  97.3 1.9 %shard_map.51 = f32[256,256]{1,0:T(8,128)S(1)} custom-call(f32[1,16384]{1,0:T(1,128)S(1)} %bitcast.24, bf16[32,3072]{1,0:T(8,128)(2,1)} %collective-permute-done.18.refs_0_, bf16[32,3072]{1,0:T(8,128)(2,1)} %collective-permute-done.22.refs_1_, bf16[256,3072]{1,0:T(8,128)(2,1)S(1)} %copy-done.8, bf16[64,1024]{1,0:T(8,128)(2,1)} %collective-permute-done.25.refs_3_, ...), custom_call_target="tpu_custom_call" | custom-call | flops 536870912 | bytes 4194304 | tf_op jit(solution)/shard_map/pallas_call | solution.py:69
  100.7 2.2 %collective-permute-start.28 = (f32[1,64,256]{2,1,0:T(8,128)S(1)}, f32[1,64,256]{2,1,0:T(8,128)S(1)}, u32[]{:S(2)}, u32[]{:S(2)}) collective-permute-start(f32[1,64,256]{2,1,0:T(8,128)S(1)} %constant_dynamic-slice_fusion), channel_id=1, source_target_pairs={{0,2},{1,3},{2,0},{3,1},{4,6},{5,7},{6,4},{7,5},{8,10},{9,11},{10,... | collective-permute-start | bytes 196616 | tf_op jit(solution)/shard_map/ppermute | solution.py:118
  102.9 2.4 %collective-permute-done.28 = f32[1,64,256]{2,1,0:T(8,128)S(1)} collective-permute-done((f32[1,64,256]{2,1,0:T(8,128)S(1)}, f32[1,64,256]{2,1,0:T(8,128)S(1)}, u32[]{:S(2)}, u32[]{:S(2)}) %collective-permute-start.28) | collective-permute-done | bytes 65568 | tf_op jit(solution)/shard_map/ppermute | solution.py:118
  (99 shorter events, 21.2 us)
Async XLA Ops:
  1.1 12.2 %collective-permute-start.4 = (bf16[32,4096]{1,0:T(8,128)(2,1)S(1)}, bf16[32,4096]{1,0:T(8,128)(2,1)S(1)}, u32[]{:S(2)}, u32[]{:S(2)}) collective-permute-start(bf16[32,4096]{1,0:T(8,128)(2,1)S(1)} %slice_select_fusion.2), channel_id=1, source_target_pairs={{0,4},{4,8},{8,12},{12,0},{1,5},{5,9},{9,13},{13,1},{2,6},{6,10},{... | collective-permute-start | bytes 786440 | tf_op jit(solution)/shard_map/ppermute | solution.py:100
  5.2 13.7 %collective-permute-start = (bf16[32,4096]{1,0:T(8,128)(2,1)S(1)}, bf16[32,4096]{1,0:T(8,128)(2,1)S(1)}, u32[]{:S(2)}, u32[]{:S(2)}) collective-permute-start(bf16[32,4096]{1,0:T(8,128)(2,1)S(1)} %slice_select_fusion.1), channel_id=1, source_target_pairs={{0,4},{4,8},{8,12},{12,0},{1,5},{5,9},{9,13},{13,1},{2,6},{6,10},{... | collective-permute-start | bytes 786440 | tf_op jit(solution)/shard_map/ppermute | solution.py:100
  10.4 25.7 %copy-start.3 = (bf16[256,4096]{1,0:T(8,128)(2,1)}, bf16[256,4096]{1,0:T(8,128)(2,1)S(1)}, u32[]{:S(2)}) copy-start(bf16[256,4096]{1,0:T(8,128)(2,1)S(1)} %get-tuple-element.61.refs_0_.refs_2_) | copy-start | bytes 6291460
  10.4 26.8 %copy-start = (bf16[256,4096]{1,0:T(8,128)(2,1)}, bf16[256,4096]{1,0:T(8,128)(2,1)S(1)}, u32[]{:S(2)}) copy-start(bf16[256,4096]{1,0:T(8,128)(2,1)S(1)} %get-tuple-element.60.refs_1_.refs_2_) | copy-start | bytes 6291460
  13.3 13.1 %collective-permute-start.8 = (bf16[32,4096]{1,0:T(8,128)(2,1)S(1)}, bf16[32,4096]{1,0:T(8,128)(2,1)S(1)}, u32[]{:S(2)}, u32[]{:S(2)}) collective-permute-start(bf16[32,4096]{1,0:T(8,128)(2,1)S(1)} %slice_select_fusion), channel_id=1, source_target_pairs={{0,4},{4,8},{8,12},{12,0},{1,5},{5,9},{9,13},{13,1},{2,6},{6,10},{... | collective-permute-start | bytes 786440 | tf_op jit(solution)/shard_map/ppermute | solution.py:100
  13.3 13.1 %collective-permute-start.5 = (bf16[32,4096]{1,0:T(8,128)(2,1)S(1)}, bf16[32,4096]{1,0:T(8,128)(2,1)S(1)}, u32[]{:S(2)}, u32[]{:S(2)}) collective-permute-start(bf16[32,4096]{1,0:T(8,128)(2,1)S(1)} %collective-permute-done.4.refs_0_), channel_id=1, source_target_pairs={{0,16},{16,0},{1,17},{17,1},{2,18},{18,2},{3,19},{19,3},{4,20},{20... | collective-permute-start | bytes 786440 | tf_op jit(solution)/shard_map/ppermute | solution.py:107
  18.9 17.1 %collective-permute-start.2 = (bf16[32,4096]{1,0:T(8,128)(2,1)S(1)}, bf16[32,4096]{1,0:T(8,128)(2,1)S(1)}, u32[]{:S(2)}, u32[]{:S(2)}) collective-permute-start(bf16[32,4096]{1,0:T(8,128)(2,1)S(1)} %collective-permute-done.refs_0_), channel_id=1, source_target_pairs={{0,16},{16,0},{1,17},{17,1},{2,18},{18,2},{3,19},{19,3},{4,20},{20... | collective-permute-start | bytes 786440 | tf_op jit(solution)/shard_map/ppermute | solution.py:107
  22.2 25.4 %copy-start.6 = (bf16[256,3072]{1,0:T(8,128)(2,1)}, bf16[256,3072]{1,0:T(8,128)(2,1)S(1)}, u32[]{:S(2)}) copy-start(bf16[256,3072]{1,0:T(8,128)(2,1)S(1)} %slice.58.refs_3_.refs_2_) | copy-start | bytes 4718596
  26.4 9.7 %collective-permute-start.1 = (bf16[32,3072]{1,0:T(8,128)(2,1)S(1)}, bf16[32,3072]{1,0:T(8,128)(2,1)S(1)}, u32[]{:S(2)}, u32[]{:S(2)}) collective-permute-start(bf16[32,3072]{1,0:T(8,128)(2,1)S(1)} %slice_select_fusion.3), channel_id=1, source_target_pairs={{0,4},{4,8},{8,12},{12,0},{1,5},{5,9},{9,13},{13,1},{2,6},{6,10},{... | collective-permute-start | bytes 589832 | tf_op jit(solution)/shard_map/ppermute | solution.py:100
  26.4 15.3 %collective-permute-start.9 = (bf16[32,4096]{1,0:T(8,128)(2,1)S(1)}, bf16[32,4096]{1,0:T(8,128)(2,1)}, u32[]{:S(2)}, u32[]{:S(2)}) collective-permute-start(bf16[32,4096]{1,0:T(8,128)(2,1)S(1)} %collective-permute-done.4.refs_0_), channel_id=1, source_target_pairs={{0,4},{4,8},{8,12},{12,0},{1,5},{5,9},{9,13},{13,1},{2,6},{6,10},{... | collective-permute-start | bytes 786440 | tf_op jit(solution)/shard_map/ppermute | solution.py:100
  27.8 14.0 %collective-permute-start.10 = (bf16[32,4096]{1,0:T(8,128)(2,1)S(1)}, bf16[32,4096]{1,0:T(8,128)(2,1)S(1)}, u32[]{:S(2)}, u32[]{:S(2)}) collective-permute-start(bf16[32,4096]{1,0:T(8,128)(2,1)S(1)} %collective-permute-done.8.refs_0_), channel_id=1, source_target_pairs={{0,16},{16,0},{1,17},{17,1},{2,18},{18,2},{3,19},{19,3},{4,20},{20... | collective-permute-start | bytes 786440 | tf_op jit(solution)/shard_map/ppermute | solution.py:107
  36.0 11.3 %collective-permute-start.3 = (bf16[32,4096]{1,0:T(8,128)(2,1)S(1)}, bf16[32,4096]{1,0:T(8,128)(2,1)}, u32[]{:S(2)}, u32[]{:S(2)}) collective-permute-start(bf16[32,4096]{1,0:T(8,128)(2,1)S(1)} %collective-permute-done.refs_0_), channel_id=1, source_target_pairs={{0,4},{4,8},{8,12},{12,0},{1,5},{5,9},{9,13},{13,1},{2,6},{6,10},{... | collective-permute-start | bytes 786440 | tf_op jit(solution)/shard_map/ppermute | solution.py:100
  36.8 6.0 %collective-permute-start.6 = (bf16[32,3072]{1,0:T(8,128)(2,1)S(1)}, bf16[32,3072]{1,0:T(8,128)(2,1)S(1)}, u32[]{:S(2)}, u32[]{:S(2)}) collective-permute-start(bf16[32,3072]{1,0:T(8,128)(2,1)S(1)} %collective-permute-done.1.refs_0_), channel_id=1, source_target_pairs={{0,16},{16,0},{1,17},{17,1},{2,18},{18,2},{3,19},{19,3},{4,20},{20... | collective-permute-start | bytes 589832 | tf_op jit(solution)/shard_map/ppermute | solution.py:107
  41.8 7.4 %collective-permute-start.14 = (bf16[32,4096]{1,0:T(8,128)(2,1)}, bf16[32,4096]{1,0:T(8,128)(2,1)S(1)}, u32[]{:S(2)}, u32[]{:S(2)}) collective-permute-start(bf16[32,4096]{1,0:T(8,128)(2,1)} %collective-permute-done.9.refs_0_), channel_id=1, source_target_pairs={{0,16},{16,0},{1,17},{17,1},{2,18},{18,2},{3,19},{19,3},{4,20},{20... | collective-permute-start | bytes 786440 | tf_op jit(solution)/shard_map/ppermute | solution.py:107
  42.0 10.3 %collective-permute-start.11 = (bf16[32,4096]{1,0:T(8,128)(2,1)S(1)}, bf16[32,4096]{1,0:T(8,128)(2,1)}, u32[]{:S(2)}, u32[]{:S(2)}) collective-permute-start(bf16[32,4096]{1,0:T(8,128)(2,1)S(1)} %collective-permute-done.8.refs_0_), channel_id=1, source_target_pairs={{0,4},{4,8},{8,12},{12,0},{1,5},{5,9},{9,13},{13,1},{2,6},{6,10},{... | collective-permute-start | bytes 786440 | tf_op jit(solution)/shard_map/ppermute | solution.py:100
  47.4 9.2 %collective-permute-start.12 = (bf16[32,4096]{1,0:T(8,128)(2,1)}, bf16[32,4096]{1,0:T(8,128)(2,1)S(1)}, u32[]{:S(2)}, u32[]{:S(2)}) collective-permute-start(bf16[32,4096]{1,0:T(8,128)(2,1)} %collective-permute-done.3.refs_0_), channel_id=1, source_target_pairs={{0,16},{16,0},{1,17},{17,1},{2,18},{18,2},{3,19},{19,3},{4,20},{20... | collective-permute-start | bytes 786440 | tf_op jit(solution)/shard_map/ppermute | solution.py:107
  47.7 8.9 %collective-permute-start.7 = (bf16[32,3072]{1,0:T(8,128)(2,1)S(1)}, bf16[32,3072]{1,0:T(8,128)(2,1)S(1)}, u32[]{:S(2)}, u32[]{:S(2)}) collective-permute-start(bf16[32,3072]{1,0:T(8,128)(2,1)S(1)} %collective-permute-done.1.refs_0_), channel_id=1, source_target_pairs={{0,4},{4,8},{8,12},{12,0},{1,5},{5,9},{9,13},{13,1},{2,6},{6,10},{... | collective-permute-start | bytes 589832 | tf_op jit(solution)/shard_map/ppermute | solution.py:100
  52.3 13.7 %collective-permute-start.20 = (bf16[32,4096]{1,0:T(8,128)(2,1)}, bf16[32,4096]{1,0:T(8,128)(2,1)}, u32[]{:S(2)}, u32[]{:S(2)}) collective-permute-start(bf16[32,4096]{1,0:T(8,128)(2,1)} %collective-permute-done.9.refs_0_), channel_id=1, source_target_pairs={{0,4},{4,8},{8,12},{12,0},{1,5},{5,9},{9,13},{13,1},{2,6},{6,10},{... | collective-permute-start | bytes 786440 | tf_op jit(solution)/shard_map/ppermute | solution.py:100
  52.3 13.7 %collective-permute-start.15 = (bf16[32,4096]{1,0:T(8,128)(2,1)}, bf16[32,4096]{1,0:T(8,128)(2,1)}, u32[]{:S(2)}, u32[]{:S(2)}) collective-permute-start(bf16[32,4096]{1,0:T(8,128)(2,1)} %collective-permute-done.11.refs_0_), channel_id=1, source_target_pairs={{0,16},{16,0},{1,17},{17,1},{2,18},{18,2},{3,19},{19,3},{4,20},{20... | collective-permute-start | bytes 786440 | tf_op jit(solution)/shard_map/ppermute | solution.py:107
  58.0 9.1 %collective-permute-start.13 = (bf16[32,4096]{1,0:T(8,128)(2,1)}, bf16[32,4096]{1,0:T(8,128)(2,1)S(1)}, u32[]{:S(2)}, u32[]{:S(2)}) collective-permute-start(bf16[32,4096]{1,0:T(8,128)(2,1)} %collective-permute-done.3.refs_0_), channel_id=1, source_target_pairs={{0,4},{4,8},{8,12},{12,0},{1,5},{5,9},{9,13},{13,1},{2,6},{6,10},{... | collective-permute-start | bytes 786440 | tf_op jit(solution)/shard_map/ppermute | solution.py:100
  62.4 7.4 %collective-permute-start.17 = (bf16[32,3072]{1,0:T(8,128)(2,1)S(1)}, bf16[32,3072]{1,0:T(8,128)(2,1)S(1)}, u32[]{:S(2)}, u32[]{:S(2)}) collective-permute-start(bf16[32,3072]{1,0:T(8,128)(2,1)S(1)} %copy-done.17), channel_id=1, source_target_pairs={{0,16},{16,0},{1,17},{17,1},{2,18},{18,2},{3,19},{19,3},{4,20},{20... | collective-permute-start | bytes 589832 | tf_op jit(solution)/shard_map/ppermute | solution.py:107
  66.0 11.6 %collective-permute-start.24 = (bf16[32,4096]{1,0:T(8,128)(2,1)}, bf16[32,4096]{1,0:T(8,128)(2,1)S(1)}, u32[]{:S(2)}, u32[]{:S(2)}) collective-permute-start(bf16[32,4096]{1,0:T(8,128)(2,1)} %collective-permute-done.20.refs_0_), channel_id=1, source_target_pairs={{0,16},{16,0},{1,17},{17,1},{2,18},{18,2},{3,19},{19,3},{4,20},{20... | collective-permute-start | bytes 786440 | tf_op jit(solution)/shard_map/ppermute | solution.py:107
  67.1 10.5 %collective-permute-start.16 = (bf16[32,4096]{1,0:T(8,128)(2,1)}, bf16[32,4096]{1,0:T(8,128)(2,1)S(1)}, u32[]{:S(2)}, u32[]{:S(2)}) collective-permute-start(bf16[32,4096]{1,0:T(8,128)(2,1)} %collective-permute-done.11.refs_0_), channel_id=1, source_target_pairs={{0,4},{4,8},{8,12},{12,0},{1,5},{5,9},{9,13},{13,1},{2,6},{6,10},{... | collective-permute-start | bytes 786440 | tf_op jit(solution)/shard_map/ppermute | solution.py:100
  70.5 12.3 %collective-permute-start.19 = (bf16[32,4096]{1,0:T(8,128)(2,1)S(1)}, bf16[32,4096]{1,0:T(8,128)(2,1)S(1)}, u32[]{:S(2)}, u32[]{:S(2)}) collective-permute-start(bf16[32,4096]{1,0:T(8,128)(2,1)S(1)} %collective-permute-done.13.refs_0_), channel_id=1, source_target_pairs={{0,16},{16,0},{1,17},{17,1},{2,18},{18,2},{3,19},{19,3},{4,20},{20... | collective-permute-start | bytes 786440 | tf_op jit(solution)/shard_map/ppermute | solution.py:107
  73.0 9.5 %collective-permute-start.21 = (bf16[64,1024]{1,0:T(8,128)(2,1)S(1)}, bf16[64,1024]{1,0:T(8,128)(2,1)S(1)}, u32[]{:S(2)}, u32[]{:S(2)}) collective-permute-start(bf16[64,1024]{1,0:T(8,128)(2,1)S(1)} %pad_maximum_fusion), channel_id=1, source_target_pairs={{0,4},{4,8},{8,12},{12,0},{1,5},{5,9},{9,13},{13,1},{2,6},{6,10},{... | collective-permute-start | bytes 393224 | tf_op jit(solution)/shard_map/ppermute | solution.py:100
  77.6 8.3 %collective-permute-start.18 = (bf16[32,3072]{1,0:T(8,128)(2,1)S(1)}, bf16[32,3072]{1,0:T(8,128)(2,1)}, u32[]{:S(2)}, u32[]{:S(2)}) collective-permute-start(bf16[32,3072]{1,0:T(8,128)(2,1)S(1)} %copy-done.17), channel_id=1, source_target_pairs={{0,4},{4,8},{8,12},{12,0},{1,5},{5,9},{9,13},{13,1},{2,6},{6,10},{... | collective-permute-start | bytes 589832 | tf_op jit(solution)/shard_map/ppermute | solution.py:100
  79.3 16.1 %collective-permute-start.26 = (bf16[32,4096]{1,0:T(8,128)(2,1)S(1)}, bf16[32,4096]{1,0:T(8,128)(2,1)}, u32[]{:S(2)}, u32[]{:S(2)}) collective-permute-start(bf16[32,4096]{1,0:T(8,128)(2,1)S(1)} %collective-permute-done.16.refs_0_), channel_id=1, source_target_pairs={{0,16},{16,0},{1,17},{17,1},{2,18},{18,2},{3,19},{19,3},{4,20},{20... | collective-permute-start | bytes 786440 | tf_op jit(solution)/shard_map/ppermute | solution.py:107
  82.5 7.0 %collective-permute-start.23 = (bf16[64,1024]{1,0:T(8,128)(2,1)S(1)}, bf16[64,1024]{1,0:T(8,128)(2,1)}, u32[]{:S(2)}, u32[]{:S(2)}) collective-permute-start(bf16[64,1024]{1,0:T(8,128)(2,1)S(1)} %collective-permute-done.21.refs_0_), channel_id=1, source_target_pairs={{0,4},{4,8},{8,12},{12,0},{1,5},{5,9},{9,13},{13,1},{2,6},{6,10},{... | collective-permute-start | bytes 393224 | tf_op jit(solution)/shard_map/ppermute | solution.py:100
  85.9 11.4 %collective-permute-start.22 = (bf16[32,3072]{1,0:T(8,128)(2,1)}, bf16[32,3072]{1,0:T(8,128)(2,1)}, u32[]{:S(2)}, u32[]{:S(2)}) collective-permute-start(bf16[32,3072]{1,0:T(8,128)(2,1)} %collective-permute-done.18.refs_0_), channel_id=1, source_target_pairs={{0,16},{16,0},{1,17},{17,1},{2,18},{18,2},{3,19},{19,3},{4,20},{20... | collective-permute-start | bytes 589832 | tf_op jit(solution)/shard_map/ppermute | solution.py:107
  89.5 7.8 %collective-permute-start.25 = (bf16[64,1024]{1,0:T(8,128)(2,1)}, bf16[64,1024]{1,0:T(8,128)(2,1)}, u32[]{:S(2)}, u32[]{:S(2)}) collective-permute-start(bf16[64,1024]{1,0:T(8,128)(2,1)} %collective-permute-done.23.refs_0_), channel_id=1, source_target_pairs={{0,4},{4,8},{8,12},{12,0},{1,5},{5,9},{9,13},{13,1},{2,6},{6,10},{... | collective-permute-start | bytes 393224 | tf_op jit(solution)/shard_map/ppermute | solution.py:100
  99.3 1.4 %collective-permute-start.27 = (f32[2,64,256]{2,1,0:T(8,128)S(1)}, f32[2,64,256]{2,1,0:T(8,128)S(1)}, u32[]{:S(2)}, u32[]{:S(2)}) collective-permute-start(f32[2,64,256]{2,1,0:T(8,128)S(1)} %dynamic-slice_bitcast_fusion), channel_id=1, source_target_pairs={{0,1},{1,0},{2,3},{3,2},{4,5},{5,4},{6,7},{7,6},{8,9},{9,8},{10,11... | collective-permute-start | bytes 393224 | tf_op jit(solution)/shard_map/ppermute | solution.py:118
  100.7 4.6 %collective-permute-start.28 = (f32[1,64,256]{2,1,0:T(8,128)S(1)}, f32[1,64,256]{2,1,0:T(8,128)S(1)}, u32[]{:S(2)}, u32[]{:S(2)}) collective-permute-start(f32[1,64,256]{2,1,0:T(8,128)S(1)} %constant_dynamic-slice_fusion), channel_id=1, source_target_pairs={{0,2},{1,3},{2,0},{3,1},{4,6},{5,7},{6,4},{7,5},{8,10},{9,11},{10,... | collective-permute-start | bytes 196616 | tf_op jit(solution)/shard_map/ppermute | solution.py:118
  (19 other events, 56.6 us)

commit v11 on v8

v11 whole, which is shorter than its diff:
```python
import functools

import jax
import jax.numpy as jnp
from jax import lax
from jax.experimental import pallas as pl
from jax.experimental.pallas import tpu as pltpu
from jax.sharding import PartitionSpec as P

CONTRACT = (((1,), (1,)), ((), ()))
CHUNKS = (4, 4, 4, 3, 1)


def fetches(sems, rows, train, rows_buf, train_buf, start, unit):
    copies, at = [], 0
    for block in rows:
        copies.append((block, rows_buf.at[pl.ds(at, block.shape[0]), :]))
        at += block.shape[0]
    for col in range(0, train_buf.shape[1], unit):
        there = train_buf.at[:, pl.ds(col, unit)]
        copies.append((train.at[:, pl.ds(start + col, unit)], there))
    return [pltpu.make_async_copy(*copy, sems.at[i]) for i, copy in enumerate(copies)]


def scores_kernel(n_grp, n_ex, groups, unit, has_base, last, *refs):
    test, scale, train, *refs = refs
    blocks = []
    for start, width, count in groups:
        blocks.append([test.at[:, pl.ds(start, width)]] + refs[:count])
        refs = refs[count:]
    base, refs = (refs[0], refs[1:]) if has_base else (None, refs)
    out, refs = refs[0], refs[1:]
    kept, refs = (refs[0], refs[1:]) if last else (out, refs)
    pending = []
    for i, (start, width, _) in enumerate(groups):
        rows_buf, train_buf, sems = refs[3 * i : 3 * i + 3]
        pending.append(fetches(sems, blocks[i], train, rows_buf, train_buf, start, unit))
        for copy in pending[-1]:
            copy.start()
    total = None if base is None else base[...]
    for i, (start, width, _) in enumerate(groups):
        rows_buf, train_buf, _ = refs[3 * i : 3 * i + 3]
        count = len(blocks[i])
        for copy in pending[i][:count]:
            copy.wait()
        for step, col in enumerate(range(0, width, unit)):
            pending[i][count + step].wait()
            columns = scale[:, start + col : start + col + unit]
            here = slice(col, col + unit)
            precond = (rows_buf[:, here].astype(jnp.float32) * columns).astype(jnp.bfloat16)
            part = lax.dot_general(
                precond, train_buf[:, here], CONTRACT, preferred_element_type=jnp.float32
            )
            total = part if total is None else total + part
    kept[...] = total
    if last:
        ex, grp = lax.axis_index("ex"), lax.axis_index("grp")
        queries = test.shape[0]
        half = queries // n_grp
        for b in range(n_ex):
            t = lax.rem(ex + (n_ex - b), n_ex)
            for h in range(n_grp):
                place = jnp.where(t == 0, h, lax.rem(h + n_grp - grp, n_grp))
                at = pl.multiple_of(t * queries + place * half, half)
                to = b * queries + h * half
                out[to : to + half, :] = kept[pl.ds(at, half), :]


def scores(n_grp, n_ex, test, scale, train, unit, groups, base, last):
    docs = train.shape[0]
    queries = test.shape[0] * n_ex
    shape = jax.ShapeDtypeStruct((queries, docs), jnp.float32)
    hbm, vmem = pl.BlockSpec(memory_space=pltpu.HBM), pl.BlockSpec(memory_space=pltpu.VMEM)
    blocks = [block for _, _, received in groups for block in received]
    width = sum(w for _, w, _ in groups)
    scratch = [pltpu.VMEM(shape.shape, shape.dtype)] if last else []
    for _, w, received in groups:
        scratch += [
            pltpu.VMEM((queries, w), test.dtype),
            pltpu.VMEM((docs, w), train.dtype),
            pltpu.SemaphoreType.DMA((1 + len(received) + w // unit,)),
        ]
    kernel = functools.partial(
        scores_kernel, n_grp, n_ex, [(s, w, len(r)) for s, w, r in groups], unit, base is not None, last
    )
    return pl.pallas_call(
        kernel,
        out_shape=shape,
        in_specs=[hbm, vmem, hbm] + [hbm] * len(blocks) + ([] if base is None else [vmem]),
        out_specs=vmem,
        scratch_shapes=scratch,
        cost_estimate=pl.CostEstimate(
            flops=2 * queries * docs * width, bytes_accessed=2 * (queries + docs) * width, transcendentals=0
        ),
        compiler_params=pltpu.CompilerParams(vmem_limit_bytes=12 * 1024 * 1024),
    )(test, scale, train, *blocks, *([] if base is None else [base]))


def solution(mesh):
    n_grp, n_ex, n_feat = (mesh.shape[a] for a in ("grp", "ex", "feat"))
    assert n_grp <= 2

    def on_device(train, test, hess):
        docs, feats = train.shape
        queries = test.shape[0]
        half = queries // n_grp
        unit = feats // sum(CHUNKS)
        grp, feat = lax.axis_index("grp"), lax.axis_index("feat")
        ring = [(i, (i + 1) % n_ex) for i in range(n_ex)]
        hops, swaps = [], []

        def after(block, *waits):
            return lax.optimization_barrier((block, waits))[0] if waits else block

        def hop(block):
            hops.append(lax.ppermute(after(block, *hops[-2:-1], *swaps[-4:-3]), "ex", ring))
            return hops[-1]

        def swap(block):
            if n_grp == 1:
                return [block]
            swaps.append(lax.ppermute(after(block, *swaps[-2:-1]), "grp", [(0, 1), (1, 0)]))
            return [block, swaps[-1]]

        def sum_over_feat(sums):
            held = sums.reshape(n_feat, -1, docs)
            bit = 1
            while bit < n_feat:
                pairs = held.reshape((-1, 2) + held.shape[1:])
                mine = (feat // bit) % 2
                keep = lax.dynamic_index_in_dim(pairs, mine, 1, keepdims=False)
                away = lax.dynamic_index_in_dim(pairs, 1 - mine, 1, keepdims=False)
                held = keep + lax.ppermute(away, "feat", [(i, i ^ bit) for i in range(n_feat)])
                bit *= 2
            return held[0]

        def share(rows, start, width, other):
            columns = slice(start, start + width)
            if n_grp == 1:
                return rows[:, columns]
            return jnp.where(grp == other, rows[:half, columns], rows[half:, columns])

        scale = (1.0 / (hess + jnp.float32(0.1))).reshape(1, feats)
        widths = [width * unit for width in CHUNKS]
        starts = [sum(widths[:c]) for c in range(len(widths))]
        held = []
        for c, (start, width) in enumerate(zip(starts, widths)):
            rows = after(test, *held[-1:])
            mine = share(rows, start, width, 0)
            if c == len(widths) - 1 and n_grp > 1:
                mine = jnp.concatenate([mine, share(rows, start, width, 1)])
            held.append(mine)
        final, whole = n_ex - 1, len(widths) - 1
        order = [(t, c) for t in range(1, final) for c in range(whole)] + [(1, whole)]
        order += [(final, c) for c in range(whole - 1)] + [(t, whole) for t in range(2, final)]
        order += [(final, whole - 1), (final, whole)]

        got = [[] for _ in widths]
        for t, c in order:
            held[c] = hop(held[c])
            got[c] += [held[c]] if c == whole else swap(held[c])
        sums = None
        groups = list(zip(starts, widths, got))
        for group in [groups[c : c + 1] for c in range(whole - 1)] + [groups[whole - 1 :]]:
            sums = scores(n_grp, n_ex, test, scale, train, unit, group, sums, len(group) > 1)
        return sum_over_feat(sums).T

    return jax.shard_map(
        on_device,
        mesh=mesh,
        in_specs=(P(("grp", "ex"), "feat"), P("ex", "feat"), P("feat")),
        out_specs=P(("grp", "ex"), "feat"),
        check_vma=False,
    )
```

time: 102 us -> 107 us (1.049)
  waiting for transfers between devices: 44.5 us -> 56.6 us
  local copies, waits for them, and re-layouts: 21.1 us -> 11 us
  Pallas kernels: 5.06 us -> 12 us
  starting transfers between devices: 28 us -> 22.8 us
  other arithmetic: 2.45 us -> 4.04 us
    unnamed x68 -> x42, local copies, waits for them, and re-layouts: 21 us -> 11 us
    ppermute x12, waiting for transfers between devices: 0.7 us -> 8.47 us  [swap(): lax.ppermute(after(block, *swaps[-2:-1]), 'grp', [(0, 1), (1, 0)])]
    pallas_call x4, Pallas kernels: 5.06 us -> 12 us  [scores(): pl.pallas_call(kernel, out_shape=shape, in_specs=[hbm, vmem, hbm] + [hbm]...]
    ppermute x12, starting transfers between devices: 19 us -> 14.2 us  [swap(): lax.ppermute(after(block, *swaps[-2:-1]), 'grp', [(0, 1), (1, 0)])]
    ppermute x12 -> x15, waiting for transfers between devices: 39.7 us -> 44.1 us  [hop(): lax.ppermute(after(block, *hops[-2:-1], *swaps[-4:-3]), 'ex', ring)]
    select_n x1 -> x5, other arithmetic: 1.77 us -> 3.36 us  [share(): return jnp.where(grp == other, rows[:half, columns], rows[half:, columns])]
    ppermute x12 -> x15, starting transfers between devices: 7.42 us -> 6.95 us  [hop(): lax.ppermute(after(block, *hops[-2:-1], *swaps[-4:-3]), 'ex', ring)]
  transfers between devices with their start and end apart: 26 -> 29, of which waited for: 15 -> 18; matrix products, arithmetic and copies ran while one was open for 0% -> 2% of each run, Pallas kernels for 3% -> 8%
where the time goes in v11:
time: 107 us
  waiting for transfers between devices  56.6 us (53%)
  starting transfers between devices  22.8 us (21%)
  Pallas kernels  12 us (11%)
  local copies, waits for them, and re-layouts  11 us (10%)
  other arithmetic  4.04 us (4%)
    ppermute x15, waiting for transfers between devices, hop(): lax.ppermute(after(block, *hops[-2:-1], *swaps[-4:-3]), 'ex', ring)  44.1 us
    ppermute x12, starting transfers between devices, swap(): lax.ppermute(after(block, *swaps[-2:-1]), 'grp', [(0, 1), (1, 0)])  14.2 us
    pallas_call x4, Pallas kernels, scores(): pl.pallas_call(kernel, out_shape=shape, in_specs=[hbm, vmem, hbm] + [hbm]...  12 us
    unnamed x42, local copies, waits for them, and re-layouts  11 us
    ppermute x12, waiting for transfers between devices, swap(): lax.ppermute(after(block, *swaps[-2:-1]), 'grp', [(0, 1), (1, 0)])  8.47 us
    ppermute x15, starting transfers between devices, hop(): lax.ppermute(after(block, *hops[-2:-1], *swaps[-4:-3]), 'ex', ring)  6.95 us
    ppermute x2, waiting for transfers between devices, sum_over_feat(): lax.ppermute(away, 'feat', [(i, i ^ bit) for i in range(n_feat)])  4.04 us
    select_n x5, other arithmetic, share(): return jnp.where(grp == other, rows[:half, columns], rows[half:, columns])  3.36 us
  transfers between devices with their start and end apart: 29, of which 18 were waited for; matrix products, arithmetic and copies ran while one was open for 2% of the time, Pallas kernels for 8%

profile of v11, /device:TPU:0, one launch (start us, length us, event | category | flops | bytes accessed | tf_op | source)
XLA Modules:
  0.0 106.7 jit_solution(6050322068561108966)
XLA Ops:
  0.0 1.2 %slice_select_fusion.2 = bf16[32,4096]{1,0:T(8,128)(2,1)S(1)} fusion(bf16[64,16384]{1,0:T(8,128)(2,1)} %refs_0_.7, pred[]{:T(512)S(6)} %eq.6), kind=kLoop, calls=%fused_computation.2 | loop fusion | flops 131072 | bytes 786433 | tf_op jit(solution)/shard_map/jit(_where)/select_n | solution.py:141
  1.2 3.1 %collective-permute-start.8 = (bf16[32,4096]{1,0:T(8,128)(2,1)S(1)}, bf16[32,4096]{1,0:T(8,128)(2,1)S(1)}, u32[]{:S(2)}, u32[]{:S(2)}) collective-permute-start(bf16[32,4096]{1,0:T(8,128)(2,1)S(1)} %slice_select_fusion.2), channel_id=1, source_target_pairs={{0,4},{4,8},{8,12},{12,0},{1,5},{5,9},{9,13},{13,1},{2,6},{6,10},{... | collective-permute-start | bytes 786440 | tf_op jit(solution)/shard_map/ppermute | solution.py:116
  5.4 1.6 %collective-permute-start = (bf16[32,4096]{1,0:T(8,128)(2,1)S(1)}, bf16[32,4096]{1,0:T(8,128)(2,1)S(1)}, u32[]{:S(2)}, u32[]{:S(2)}) collective-permute-start(bf16[32,4096]{1,0:T(8,128)(2,1)S(1)} %slice_select_fusion.1), channel_id=1, source_target_pairs={{0,4},{4,8},{8,12},{12,0},{1,5},{5,9},{9,13},{13,1},{2,6},{6,10},{... | collective-permute-start | bytes 786440 | tf_op jit(solution)/shard_map/ppermute | solution.py:116
  8.0 5.4 %collective-permute-done.8.refs_3_ = bf16[32,4096]{1,0:T(8,128)(2,1)S(1)} collective-permute-done((bf16[32,4096]{1,0:T(8,128)(2,1)S(1)}, bf16[32,4096]{1,0:T(8,128)(2,1)S(1)}, u32[]{:S(2)}, u32[]{:S(2)}) %collective-permute-start.8) | collective-permute-done | bytes 262176 | tf_op jit(solution)/shard_map/ppermute | solution.py:116
  13.5 1.7 %collective-permute-start.10 = (bf16[32,4096]{1,0:T(8,128)(2,1)S(1)}, bf16[32,4096]{1,0:T(8,128)(2,1)S(1)}, u32[]{:S(2)}, u32[]{:S(2)}) collective-permute-start(bf16[32,4096]{1,0:T(8,128)(2,1)S(1)} %collective-permute-done.8.refs_3_), channel_id=1, source_target_pairs={{0,16},{16,0},{1,17},{17,1},{2,18},{18,2},{3,19},{19,3},{4,20},{20... | collective-permute-start | bytes 786440 | tf_op jit(solution)/shard_map/ppermute | solution.py:122
  15.2 3.8 %collective-permute-done.refs_3_ = bf16[32,4096]{1,0:T(8,128)(2,1)S(1)} collective-permute-done((bf16[32,4096]{1,0:T(8,128)(2,1)S(1)}, bf16[32,4096]{1,0:T(8,128)(2,1)S(1)}, u32[]{:S(2)}, u32[]{:S(2)}) %collective-permute-start) | collective-permute-done | bytes 262176 | tf_op jit(solution)/shard_map/ppermute | solution.py:116
  19.1 1.8 %collective-permute-start.2 = (bf16[32,4096]{1,0:T(8,128)(2,1)S(1)}, bf16[32,4096]{1,0:T(8,128)(2,1)S(1)}, u32[]{:S(2)}, u32[]{:S(2)}) collective-permute-start(bf16[32,4096]{1,0:T(8,128)(2,1)S(1)} %collective-permute-done.refs_3_), channel_id=1, source_target_pairs={{0,16},{16,0},{1,17},{17,1},{2,18},{18,2},{3,19},{19,3},{4,20},{20... | collective-permute-start | bytes 786440 | tf_op jit(solution)/shard_map/ppermute | solution.py:122
  20.9 3.8 %collective-permute-done.9.refs_3_ = bf16[32,4096]{1,0:T(8,128)(2,1)S(1)} collective-permute-done((bf16[32,4096]{1,0:T(8,128)(2,1)S(1)}, bf16[32,4096]{1,0:T(8,128)(2,1)S(1)}, u32[]{:S(2)}, u32[]{:S(2)}) %collective-permute-start.9) | collective-permute-done | bytes 262176 | tf_op jit(solution)/shard_map/ppermute | solution.py:116
  24.7 1.7 %collective-permute-start.12 = (bf16[32,4096]{1,0:T(8,128)(2,1)S(1)}, bf16[32,4096]{1,0:T(8,128)(2,1)S(1)}, u32[]{:S(2)}, u32[]{:S(2)}) collective-permute-start(bf16[32,4096]{1,0:T(8,128)(2,1)S(1)} %collective-permute-done.9.refs_3_), channel_id=1, source_target_pairs={{0,16},{16,0},{1,17},{17,1},{2,18},{18,2},{3,19},{19,3},{4,20},{20... | collective-permute-start | bytes 786440 | tf_op jit(solution)/shard_map/ppermute | solution.py:122
  26.5 2.8 %collective-permute-done.1.refs_3_ = bf16[32,3072]{1,0:T(8,128)(2,1)} collective-permute-done((bf16[32,3072]{1,0:T(8,128)(2,1)S(1)}, bf16[32,3072]{1,0:T(8,128)(2,1)}, u32[]{:S(2)}, u32[]{:S(2)}) %collective-permute-start.1) | collective-permute-done | bytes 196640 | tf_op jit(solution)/shard_map/ppermute | solution.py:116
  29.3 1.3 %collective-permute-start.3 = (bf16[32,3072]{1,0:T(8,128)(2,1)}, bf16[32,3072]{1,0:T(8,128)(2,1)}, u32[]{:S(2)}, u32[]{:S(2)}) collective-permute-start(bf16[32,3072]{1,0:T(8,128)(2,1)} %collective-permute-done.1.refs_3_), channel_id=1, source_target_pairs={{0,16},{16,0},{1,17},{17,1},{2,18},{18,2},{3,19},{19,3},{4,20},{20... | collective-permute-start | bytes 589832 | tf_op jit(solution)/shard_map/ppermute | solution.py:122
  30.6 5.3 %collective-permute-done.11.refs_5_ = bf16[32,4096]{1,0:T(8,128)(2,1)} collective-permute-done((bf16[32,4096]{1,0:T(8,128)(2,1)S(1)}, bf16[32,4096]{1,0:T(8,128)(2,1)}, u32[]{:S(2)}, u32[]{:S(2)}) %collective-permute-start.11) | collective-permute-done | bytes 262176 | tf_op jit(solution)/shard_map/ppermute | solution.py:116
  36.6 1.7 %collective-permute-start.14 = (bf16[32,4096]{1,0:T(8,128)(2,1)}, bf16[32,4096]{1,0:T(8,128)(2,1)}, u32[]{:S(2)}, u32[]{:S(2)}) collective-permute-start(bf16[32,4096]{1,0:T(8,128)(2,1)} %collective-permute-done.11.refs_5_), channel_id=1, source_target_pairs={{0,16},{16,0},{1,17},{17,1},{2,18},{18,2},{3,19},{19,3},{4,20},{20... | collective-permute-start | bytes 786440 | tf_op jit(solution)/shard_map/ppermute | solution.py:122
  38.2 3.2 %collective-permute-done.4.refs_5_ = bf16[32,4096]{1,0:T(8,128)(2,1)} collective-permute-done((bf16[32,4096]{1,0:T(8,128)(2,1)S(1)}, bf16[32,4096]{1,0:T(8,128)(2,1)}, u32[]{:S(2)}, u32[]{:S(2)}) %collective-permute-start.4) | collective-permute-done | bytes 262176 | tf_op jit(solution)/shard_map/ppermute | solution.py:116
  41.5 1.7 %collective-permute-start.6 = (bf16[32,4096]{1,0:T(8,128)(2,1)}, bf16[32,4096]{1,0:T(8,128)(2,1)S(1)}, u32[]{:S(2)}, u32[]{:S(2)}) collective-permute-start(bf16[32,4096]{1,0:T(8,128)(2,1)} %collective-permute-done.4.refs_5_), channel_id=1, source_target_pairs={{0,16},{16,0},{1,17},{17,1},{2,18},{18,2},{3,19},{19,3},{4,20},{20... | collective-permute-start | bytes 786440 | tf_op jit(solution)/shard_map/ppermute | solution.py:122
  43.2 4.3 %collective-permute-done.13.refs_5_ = bf16[32,4096]{1,0:T(8,128)(2,1)} collective-permute-done((bf16[32,4096]{1,0:T(8,128)(2,1)S(1)}, bf16[32,4096]{1,0:T(8,128)(2,1)}, u32[]{:S(2)}, u32[]{:S(2)}) %collective-permute-start.13) | collective-permute-done | bytes 262176 | tf_op jit(solution)/shard_map/ppermute | solution.py:116
  47.5 1.2 %collective-permute-start.16 = (bf16[32,4096]{1,0:T(8,128)(2,1)}, bf16[32,4096]{1,0:T(8,128)(2,1)S(1)}, u32[]{:S(2)}, u32[]{:S(2)}) collective-permute-start(bf16[32,4096]{1,0:T(8,128)(2,1)} %collective-permute-done.13.refs_5_), channel_id=1, source_target_pairs={{0,16},{16,0},{1,17},{17,1},{2,18},{18,2},{3,19},{19,3},{4,20},{20... | collective-permute-start | bytes 786440 | tf_op jit(solution)/shard_map/ppermute | solution.py:122
  51.7 8.7 %collective-permute-done.19.refs_9_ = bf16[64,1024]{1,0:T(8,128)(2,1)} collective-permute-done((bf16[64,1024]{1,0:T(8,128)(2,1)S(1)}, bf16[64,1024]{1,0:T(8,128)(2,1)}, u32[]{:S(2)}, u32[]{:S(2)}) %collective-permute-start.19) | collective-permute-done | bytes 131104 | tf_op jit(solution)/shard_map/ppermute | solution.py:116
  64.2 3.8 %collective-permute-done.7.refs_6_ = bf16[32,3072]{1,0:T(8,128)(2,1)S(1)} collective-permute-done((bf16[32,3072]{1,0:T(8,128)(2,1)S(1)}, bf16[32,3072]{1,0:T(8,128)(2,1)S(1)}, u32[]{:S(2)}, u32[]{:S(2)}) %collective-permute-start.7) | collective-permute-done | bytes 196640 | tf_op jit(solution)/shard_map/ppermute | solution.py:122
  68.7 1.6 %collective-permute-done.20.refs_7_ = bf16[32,4096]{1,0:T(8,128)(2,1)S(1)} collective-permute-done((bf16[32,4096]{1,0:T(8,128)(2,1)}, bf16[32,4096]{1,0:T(8,128)(2,1)S(1)}, u32[]{:S(2)}, u32[]{:S(2)}) %collective-permute-start.20) | collective-permute-done | bytes 262176 | tf_op jit(solution)/shard_map/ppermute | solution.py:116
  71.1 2.1 %collective-permute-done.17.refs_7_ = bf16[32,4096]{1,0:T(8,128)(2,1)} collective-permute-done((bf16[32,4096]{1,0:T(8,128)(2,1)}, bf16[32,4096]{1,0:T(8,128)(2,1)}, u32[]{:S(2)}, u32[]{:S(2)}) %collective-permute-start.17) | collective-permute-done | bytes 262176 | tf_op jit(solution)/shard_map/ppermute | solution.py:116
  74.0 1.4 %collective-permute-start.26 = (bf16[32,4096]{1,0:T(8,128)(2,1)}, bf16[32,4096]{1,0:T(8,128)(2,1)}, u32[]{:S(2)}, u32[]{:S(2)}) collective-permute-start(bf16[32,4096]{1,0:T(8,128)(2,1)} %collective-permute-done.17.refs_7_), channel_id=1, source_target_pairs={{0,16},{16,0},{1,17},{17,1},{2,18},{18,2},{3,19},{19,3},{4,20},{20... | collective-permute-start | bytes 786440 | tf_op jit(solution)/shard_map/ppermute | solution.py:122
  75.4 4.1 %collective-permute-done.21.refs_8_ = bf16[32,4096]{1,0:T(8,128)(2,1)S(1)} collective-permute-done((bf16[32,4096]{1,0:T(8,128)(2,1)S(1)}, bf16[32,4096]{1,0:T(8,128)(2,1)S(1)}, u32[]{:S(2)}, u32[]{:S(2)}) %collective-permute-start.21) | collective-permute-done | bytes 262176 | tf_op jit(solution)/shard_map/ppermute | solution.py:122
  81.2 1.6 %collective-permute-done.23.refs_10_ = bf16[64,1024]{1,0:T(8,128)(2,1)} collective-permute-done((bf16[64,1024]{1,0:T(8,128)(2,1)}, bf16[64,1024]{1,0:T(8,128)(2,1)}, u32[]{:S(2)}, u32[]{:S(2)}) %collective-permute-start.23) | collective-permute-done | bytes 131104 | tf_op jit(solution)/shard_map/ppermute | solution.py:116
  82.8 3.4 %copy-done = bf16[256,16384]{1,0:T(8,128)(2,1)S(1)} copy-done((bf16[256,16384]{1,0:T(8,128)(2,1)S(1)}, bf16[256,16384]{1,0:T(8,128)(2,1)}, u32[]{:S(2)}) %copy-start) | copy-done | bytes 8388632
  88.1 2.9 %shard_map.37.refs_9_ = f32[256,256]{1,0:T(8,128)S(1)} custom-call(bf16[64,16384]{1,0:T(8,128)(2,1)S(1)} %copy-done.1, f32[1,16384]{1,0:T(1,128)S(1)} %bitcast.10, bf16[256,16384]{1,0:T(8,128)(2,1)S(1)} %copy-done, bf16[32,4096]{1,0:T(8,128)(2,1)S(1)} %collective-permute-done.8.refs_3_, bf16[32,4096]{1,0:T(8,128)(2,1)S(1)} %collective-permute-done.10.refs_4_, ...), custom_call_target="tpu_custom_call" | custom-call | flops 536870912 | bytes 4194304 | tf_op jit(solution)/shard_map/pallas_call | solution.py:86
  91.1 2.8 %shard_map.38.refs_9_ = f32[256,256]{1,0:T(8,128)S(1)} custom-call(bf16[64,16384]{1,0:T(8,128)(2,1)S(1)} %copy-done.1, f32[1,16384]{1,0:T(1,128)S(1)} %bitcast.11, bf16[256,16384]{1,0:T(8,128)(2,1)S(1)} %copy-done, bf16[32,4096]{1,0:T(8,128)(2,1)S(1)} %collective-permute-done.refs_3_, bf16[32,4096]{1,0:T(8,128)(2,1)S(1)} %collective-permute-done.2.refs_4_, ...), custom_call_target="tpu_custom_call" | custom-call | flops 536870912 | bytes 4194304 | tf_op jit(solution)/shard_map/pallas_call | solution.py:86
  93.9 2.9 %shard_map.39.refs_12_ = f32[256,256]{1,0:T(8,128)S(1)} custom-call(bf16[64,16384]{1,0:T(8,128)(2,1)S(1)} %copy-done.1, f32[1,16384]{1,0:T(1,128)S(1)} %bitcast.12, bf16[256,16384]{1,0:T(8,128)(2,1)S(1)} %copy-done, bf16[32,4096]{1,0:T(8,128)(2,1)S(1)} %collective-permute-done.9.refs_3_, bf16[32,4096]{1,0:T(8,128)(2,1)S(1)} %copy-done.3, ...), custom_call_target="tpu_custom_call" | custom-call | flops 536870912 | bytes 4194304 | tf_op jit(solution)/shard_map/pallas_call | solution.py:86
  96.9 3.4 %shard_map.40 = f32[256,256]{1,0:T(8,128)S(1)} custom-call(bf16[64,16384]{1,0:T(8,128)(2,1)S(1)} %copy-done.1, f32[1,16384]{1,0:T(1,128)S(1)} %bitcast.13, bf16[256,16384]{1,0:T(8,128)(2,1)S(1)} %copy-done, bf16[32,3072]{1,0:T(8,128)(2,1)} %collective-permute-done.1.refs_3_, bf16[32,3072]{1,0:T(8,128)(2,1)} %collective-permute-done.3.refs_4_, ...), custom_call_target="tpu_custom_call" | custom-call | flops 536870912 | bytes 4194304 | tf_op jit(solution)/shard_map/pallas_call | solution.py:86
  100.4 1.3 %collective-permute-done.27 = f32[2,64,256]{2,1,0:T(8,128)S(1)} collective-permute-done((f32[2,64,256]{2,1,0:T(8,128)S(1)}, f32[2,64,256]{2,1,0:T(8,128)S(1)}, u32[]{:S(2)}, u32[]{:S(2)}) %collective-permute-start.27) | collective-permute-done | bytes 131104 | tf_op jit(solution)/shard_map/ppermute | solution.py:133
  101.7 1.6 %collective-permute-start.28 = (f32[1,64,256]{2,1,0:T(8,128)S(1)}, f32[1,64,256]{2,1,0:T(8,128)S(1)}, u32[]{:S(2)}, u32[]{:S(2)}) collective-permute-start(f32[1,64,256]{2,1,0:T(8,128)S(1)} %constant_dynamic-slice_fusion), channel_id=1, source_target_pairs={{0,2},{1,3},{2,0},{3,1},{4,6},{5,7},{6,4},{7,5},{8,10},{9,11},{10,... | collective-permute-start | bytes 196616 | tf_op jit(solution)/shard_map/ppermute | solution.py:133
  103.3 2.7 %collective-permute-done.28 = f32[1,64,256]{2,1,0:T(8,128)S(1)} collective-permute-done((f32[1,64,256]{2,1,0:T(8,128)S(1)}, f32[1,64,256]{2,1,0:T(8,128)S(1)}, u32[]{:S(2)}, u32[]{:S(2)}) %collective-permute-start.28) | collective-permute-done | bytes 65568 | tf_op jit(solution)/shard_map/ppermute | solution.py:133
  (83 shorter events, 16.4 us)
Async XLA Ops:
  0.0 20.8 %copy-start.1 = (bf16[64,16384]{1,0:T(8,128)(2,1)S(1)}, bf16[64,16384]{1,0:T(8,128)(2,1)}, u32[]{:S(2)}) copy-start(bf16[64,16384]{1,0:T(8,128)(2,1)} %refs_0_.7) | copy-start | bytes 6291460
  0.0 81.2 %copy-start.20 = (f32[16384]{0:T(1024)S(1)}, f32[16384]{0:T(1024)}, u32[]{:S(2)}) copy-start(f32[16384]{0:T(1024)} %param.5) | copy-start | bytes 196612
  1.2 12.2 %collective-permute-start.8 = (bf16[32,4096]{1,0:T(8,128)(2,1)S(1)}, bf16[32,4096]{1,0:T(8,128)(2,1)S(1)}, u32[]{:S(2)}, u32[]{:S(2)}) collective-permute-start(bf16[32,4096]{1,0:T(8,128)(2,1)S(1)} %slice_select_fusion.2), channel_id=1, source_target_pairs={{0,4},{4,8},{8,12},{12,0},{1,5},{5,9},{9,13},{13,1},{2,6},{6,10},{... | collective-permute-start | bytes 786440 | tf_op jit(solution)/shard_map/ppermute | solution.py:116
  5.4 13.7 %collective-permute-start = (bf16[32,4096]{1,0:T(8,128)(2,1)S(1)}, bf16[32,4096]{1,0:T(8,128)(2,1)S(1)}, u32[]{:S(2)}, u32[]{:S(2)}) collective-permute-start(bf16[32,4096]{1,0:T(8,128)(2,1)S(1)} %slice_select_fusion.1), channel_id=1, source_target_pairs={{0,4},{4,8},{8,12},{12,0},{1,5},{5,9},{9,13},{13,1},{2,6},{6,10},{... | collective-permute-start | bytes 786440 | tf_op jit(solution)/shard_map/ppermute | solution.py:116
  13.5 11.2 %collective-permute-start.9 = (bf16[32,4096]{1,0:T(8,128)(2,1)S(1)}, bf16[32,4096]{1,0:T(8,128)(2,1)S(1)}, u32[]{:S(2)}, u32[]{:S(2)}) collective-permute-start(bf16[32,4096]{1,0:T(8,128)(2,1)S(1)} %slice_select_fusion), channel_id=1, source_target_pairs={{0,4},{4,8},{8,12},{12,0},{1,5},{5,9},{9,13},{13,1},{2,6},{6,10},{... | collective-permute-start | bytes 786440 | tf_op jit(solution)/shard_map/ppermute | solution.py:116
  13.5 11.2 %collective-permute-start.10 = (bf16[32,4096]{1,0:T(8,128)(2,1)S(1)}, bf16[32,4096]{1,0:T(8,128)(2,1)S(1)}, u32[]{:S(2)}, u32[]{:S(2)}) collective-permute-start(bf16[32,4096]{1,0:T(8,128)(2,1)S(1)} %collective-permute-done.8.refs_3_), channel_id=1, source_target_pairs={{0,16},{16,0},{1,17},{17,1},{2,18},{18,2},{3,19},{19,3},{4,20},{20... | collective-permute-start | bytes 786440 | tf_op jit(solution)/shard_map/ppermute | solution.py:122
  19.1 10.2 %collective-permute-start.2 = (bf16[32,4096]{1,0:T(8,128)(2,1)S(1)}, bf16[32,4096]{1,0:T(8,128)(2,1)S(1)}, u32[]{:S(2)}, u32[]{:S(2)}) collective-permute-start(bf16[32,4096]{1,0:T(8,128)(2,1)S(1)} %collective-permute-done.refs_3_), channel_id=1, source_target_pairs={{0,16},{16,0},{1,17},{17,1},{2,18},{18,2},{3,19},{19,3},{4,20},{20... | collective-permute-start | bytes 786440 | tf_op jit(solution)/shard_map/ppermute | solution.py:122
  20.9 8.4 %collective-permute-start.1 = (bf16[32,3072]{1,0:T(8,128)(2,1)S(1)}, bf16[32,3072]{1,0:T(8,128)(2,1)}, u32[]{:S(2)}, u32[]{:S(2)}) collective-permute-start(bf16[32,3072]{1,0:T(8,128)(2,1)S(1)} %slice_select_fusion.3), channel_id=1, source_target_pairs={{0,4},{4,8},{8,12},{12,0},{1,5},{5,9},{9,13},{13,1},{2,6},{6,10},{... | collective-permute-start | bytes 589832 | tf_op jit(solution)/shard_map/ppermute | solution.py:116
  24.7 11.1 %collective-permute-start.11 = (bf16[32,4096]{1,0:T(8,128)(2,1)S(1)}, bf16[32,4096]{1,0:T(8,128)(2,1)}, u32[]{:S(2)}, u32[]{:S(2)}) collective-permute-start(bf16[32,4096]{1,0:T(8,128)(2,1)S(1)} %collective-permute-done.8.refs_3_), channel_id=1, source_target_pairs={{0,4},{4,8},{8,12},{12,0},{1,5},{5,9},{9,13},{13,1},{2,6},{6,10},{... | collective-permute-start | bytes 786440 | tf_op jit(solution)/shard_map/ppermute | solution.py:116
  24.7 11.1 %collective-permute-start.12 = (bf16[32,4096]{1,0:T(8,128)(2,1)S(1)}, bf16[32,4096]{1,0:T(8,128)(2,1)S(1)}, u32[]{:S(2)}, u32[]{:S(2)}) collective-permute-start(bf16[32,4096]{1,0:T(8,128)(2,1)S(1)} %collective-permute-done.9.refs_3_), channel_id=1, source_target_pairs={{0,16},{16,0},{1,17},{17,1},{2,18},{18,2},{3,19},{19,3},{4,20},{20... | collective-permute-start | bytes 786440 | tf_op jit(solution)/shard_map/ppermute | solution.py:122
  29.3 12.1 %collective-permute-start.4 = (bf16[32,4096]{1,0:T(8,128)(2,1)S(1)}, bf16[32,4096]{1,0:T(8,128)(2,1)}, u32[]{:S(2)}, u32[]{:S(2)}) collective-permute-start(bf16[32,4096]{1,0:T(8,128)(2,1)S(1)} %collective-permute-done.refs_3_), channel_id=1, source_target_pairs={{0,4},{4,8},{8,12},{12,0},{1,5},{5,9},{9,13},{13,1},{2,6},{6,10},{... | collective-permute-start | bytes 786440 | tf_op jit(solution)/shard_map/ppermute | solution.py:116
  29.3 8.9 %collective-permute-start.3 = (bf16[32,3072]{1,0:T(8,128)(2,1)}, bf16[32,3072]{1,0:T(8,128)(2,1)}, u32[]{:S(2)}, u32[]{:S(2)}) collective-permute-start(bf16[32,3072]{1,0:T(8,128)(2,1)} %collective-permute-done.1.refs_3_), channel_id=1, source_target_pairs={{0,16},{16,0},{1,17},{17,1},{2,18},{18,2},{3,19},{19,3},{4,20},{20... | collective-permute-start | bytes 589832 | tf_op jit(solution)/shard_map/ppermute | solution.py:122
  36.6 10.9 %collective-permute-start.13 = (bf16[32,4096]{1,0:T(8,128)(2,1)S(1)}, bf16[32,4096]{1,0:T(8,128)(2,1)}, u32[]{:S(2)}, u32[]{:S(2)}) collective-permute-start(bf16[32,4096]{1,0:T(8,128)(2,1)S(1)} %collective-permute-done.9.refs_3_), channel_id=1, source_target_pairs={{0,4},{4,8},{8,12},{12,0},{1,5},{5,9},{9,13},{13,1},{2,6},{6,10},{... | collective-permute-start | bytes 786440 | tf_op jit(solution)/shard_map/ppermute | solution.py:116
  36.6 10.9 %collective-permute-start.14 = (bf16[32,4096]{1,0:T(8,128)(2,1)}, bf16[32,4096]{1,0:T(8,128)(2,1)}, u32[]{:S(2)}, u32[]{:S(2)}) collective-permute-start(bf16[32,4096]{1,0:T(8,128)(2,1)} %collective-permute-done.11.refs_5_), channel_id=1, source_target_pairs={{0,16},{16,0},{1,17},{17,1},{2,18},{18,2},{3,19},{19,3},{4,20},{20... | collective-permute-start | bytes 786440 | tf_op jit(solution)/shard_map/ppermute | solution.py:122
  41.5 8.0 %collective-permute-start.5 = (bf16[32,3072]{1,0:T(8,128)(2,1)}, bf16[32,3072]{1,0:T(8,128)(2,1)S(1)}, u32[]{:S(2)}, u32[]{:S(2)}) collective-permute-start(bf16[32,3072]{1,0:T(8,128)(2,1)} %collective-permute-done.1.refs_3_), channel_id=1, source_target_pairs={{0,4},{4,8},{8,12},{12,0},{1,5},{5,9},{9,13},{13,1},{2,6},{6,10},{... | collective-permute-start | bytes 589832 | tf_op jit(solution)/shard_map/ppermute | solution.py:116
  41.5 9.6 %collective-permute-start.6 = (bf16[32,4096]{1,0:T(8,128)(2,1)}, bf16[32,4096]{1,0:T(8,128)(2,1)S(1)}, u32[]{:S(2)}, u32[]{:S(2)}) collective-permute-start(bf16[32,4096]{1,0:T(8,128)(2,1)} %collective-permute-done.4.refs_5_), channel_id=1, source_target_pairs={{0,16},{16,0},{1,17},{17,1},{2,18},{18,2},{3,19},{19,3},{4,20},{20... | collective-permute-start | bytes 786440 | tf_op jit(solution)/shard_map/ppermute | solution.py:122
  47.5 13.7 %collective-permute-start.16 = (bf16[32,4096]{1,0:T(8,128)(2,1)}, bf16[32,4096]{1,0:T(8,128)(2,1)S(1)}, u32[]{:S(2)}, u32[]{:S(2)}) collective-permute-start(bf16[32,4096]{1,0:T(8,128)(2,1)} %collective-permute-done.13.refs_5_), channel_id=1, source_target_pairs={{0,16},{16,0},{1,17},{17,1},{2,18},{18,2},{3,19},{19,3},{4,20},{20... | collective-permute-start | bytes 786440 | tf_op jit(solution)/shard_map/ppermute | solution.py:122
  49.5 31.4 %copy-start.16 = (bf16[32,3072]{1,0:T(8,128)(2,1)}, bf16[32,3072]{1,0:T(8,128)(2,1)S(1)}, u32[]{:S(2)}) copy-start(bf16[32,3072]{1,0:T(8,128)(2,1)S(1)} %collective-permute-done.5.refs_5_) | copy-start | bytes 589828
  49.5 12.5 %collective-permute-start.15 = (bf16[32,4096]{1,0:T(8,128)(2,1)}, bf16[32,4096]{1,0:T(8,128)(2,1)S(1)}, u32[]{:S(2)}, u32[]{:S(2)}) collective-permute-start(bf16[32,4096]{1,0:T(8,128)(2,1)} %collective-permute-done.11.refs_5_), channel_id=1, source_target_pairs={{0,4},{4,8},{8,12},{12,0},{1,5},{5,9},{9,13},{13,1},{2,6},{6,10},{... | collective-permute-start | bytes 786440 | tf_op jit(solution)/shard_map/ppermute | solution.py:116
  49.5 11.0 %collective-permute-start.19 = (bf16[64,1024]{1,0:T(8,128)(2,1)S(1)}, bf16[64,1024]{1,0:T(8,128)(2,1)}, u32[]{:S(2)}, u32[]{:S(2)}) collective-permute-start(bf16[64,1024]{1,0:T(8,128)(2,1)S(1)} %pad_maximum_fusion), channel_id=1, source_target_pairs={{0,4},{4,8},{8,12},{12,0},{1,5},{5,9},{9,13},{13,1},{2,6},{6,10},{... | collective-permute-start | bytes 393224 | tf_op jit(solution)/shard_map/ppermute | solution.py:116
  60.5 9.9 %collective-permute-start.20 = (bf16[32,4096]{1,0:T(8,128)(2,1)}, bf16[32,4096]{1,0:T(8,128)(2,1)S(1)}, u32[]{:S(2)}, u32[]{:S(2)}) collective-permute-start(bf16[32,4096]{1,0:T(8,128)(2,1)} %collective-permute-done.4.refs_5_), channel_id=1, source_target_pairs={{0,4},{4,8},{8,12},{12,0},{1,5},{5,9},{9,13},{13,1},{2,6},{6,10},{... | collective-permute-start | bytes 786440 | tf_op jit(solution)/shard_map/ppermute | solution.py:116
  60.5 7.5 %collective-permute-start.7 = (bf16[32,3072]{1,0:T(8,128)(2,1)S(1)}, bf16[32,3072]{1,0:T(8,128)(2,1)S(1)}, u32[]{:S(2)}, u32[]{:S(2)}) collective-permute-start(bf16[32,3072]{1,0:T(8,128)(2,1)S(1)} %collective-permute-done.5.refs_5_), channel_id=1, source_target_pairs={{0,16},{16,0},{1,17},{17,1},{2,18},{18,2},{3,19},{19,3},{4,20},{20... | collective-permute-start | bytes 589832 | tf_op jit(solution)/shard_map/ppermute | solution.py:122
  61.9 11.3 %collective-permute-start.17 = (bf16[32,4096]{1,0:T(8,128)(2,1)}, bf16[32,4096]{1,0:T(8,128)(2,1)}, u32[]{:S(2)}, u32[]{:S(2)}) collective-permute-start(bf16[32,4096]{1,0:T(8,128)(2,1)} %collective-permute-done.13.refs_5_), channel_id=1, source_target_pairs={{0,4},{4,8},{8,12},{12,0},{1,5},{5,9},{9,13},{13,1},{2,6},{6,10},{... | collective-permute-start | bytes 786440 | tf_op jit(solution)/shard_map/ppermute | solution.py:116
  63.0 10.3 %collective-permute-start.24 = (bf16[32,4096]{1,0:T(8,128)(2,1)S(1)}, bf16[32,4096]{1,0:T(8,128)(2,1)S(1)}, u32[]{:S(2)}, u32[]{:S(2)}) collective-permute-start(bf16[32,4096]{1,0:T(8,128)(2,1)S(1)} %collective-permute-done.15.refs_7_), channel_id=1, source_target_pairs={{0,16},{16,0},{1,17},{17,1},{2,18},{18,2},{3,19},{19,3},{4,20},{20... | collective-permute-start | bytes 786440 | tf_op jit(solution)/shard_map/ppermute | solution.py:122
  70.3 9.2 %collective-permute-start.21 = (bf16[32,4096]{1,0:T(8,128)(2,1)S(1)}, bf16[32,4096]{1,0:T(8,128)(2,1)S(1)}, u32[]{:S(2)}, u32[]{:S(2)}) collective-permute-start(bf16[32,4096]{1,0:T(8,128)(2,1)S(1)} %collective-permute-done.20.refs_7_), channel_id=1, source_target_pairs={{0,16},{16,0},{1,17},{17,1},{2,18},{18,2},{3,19},{19,3},{4,20},{20... | collective-permute-start | bytes 786440 | tf_op jit(solution)/shard_map/ppermute | solution.py:122
  73.2 7.6 %collective-permute-start.18 = (bf16[32,3072]{1,0:T(8,128)(2,1)S(1)}, bf16[32,3072]{1,0:T(8,128)(2,1)}, u32[]{:S(2)}, u32[]{:S(2)}) collective-permute-start(bf16[32,3072]{1,0:T(8,128)(2,1)S(1)} %collective-permute-done.5.refs_5_), channel_id=1, source_target_pairs={{0,4},{4,8},{8,12},{12,0},{1,5},{5,9},{9,13},{13,1},{2,6},{6,10},{... | collective-permute-start | bytes 589832 | tf_op jit(solution)/shard_map/ppermute | solution.py:116
  73.2 9.5 %collective-permute-start.23 = (bf16[64,1024]{1,0:T(8,128)(2,1)}, bf16[64,1024]{1,0:T(8,128)(2,1)}, u32[]{:S(2)}, u32[]{:S(2)}) collective-permute-start(bf16[64,1024]{1,0:T(8,128)(2,1)} %collective-permute-done.19.refs_9_), channel_id=1, source_target_pairs={{0,4},{4,8},{8,12},{12,0},{1,5},{5,9},{9,13},{13,1},{2,6},{6,10},{... | collective-permute-start | bytes 393224 | tf_op jit(solution)/shard_map/ppermute | solution.py:116
  74.0 19.9 %collective-permute-start.26 = (bf16[32,4096]{1,0:T(8,128)(2,1)}, bf16[32,4096]{1,0:T(8,128)(2,1)}, u32[]{:S(2)}, u32[]{:S(2)}) collective-permute-start(bf16[32,4096]{1,0:T(8,128)(2,1)} %collective-permute-done.17.refs_7_), channel_id=1, source_target_pairs={{0,16},{16,0},{1,17},{17,1},{2,18},{18,2},{3,19},{19,3},{4,20},{20... | collective-permute-start | bytes 786440 | tf_op jit(solution)/shard_map/ppermute | solution.py:122
  80.8 16.0 %collective-permute-start.22 = (bf16[32,3072]{1,0:T(8,128)(2,1)}, bf16[32,3072]{1,0:T(8,128)(2,1)}, u32[]{:S(2)}, u32[]{:S(2)}) collective-permute-start(bf16[32,3072]{1,0:T(8,128)(2,1)} %collective-permute-done.18.refs_7_), channel_id=1, source_target_pairs={{0,16},{16,0},{1,17},{17,1},{2,18},{18,2},{3,19},{19,3},{4,20},{20... | collective-permute-start | bytes 589832 | tf_op jit(solution)/shard_map/ppermute | solution.py:122
  82.8 14.0 %collective-permute-start.25 = (bf16[64,1024]{1,0:T(8,128)(2,1)}, bf16[64,1024]{1,0:T(8,128)(2,1)S(1)}, u32[]{:S(2)}, u32[]{:S(2)}) collective-permute-start(bf16[64,1024]{1,0:T(8,128)(2,1)} %collective-permute-done.23.refs_10_), channel_id=1, source_target_pairs={{0,4},{4,8},{8,12},{12,0},{1,5},{5,9},{9,13},{13,1},{2,6},{6,10},{... | collective-permute-start | bytes 393224 | tf_op jit(solution)/shard_map/ppermute | solution.py:116
  100.2 1.4 %collective-permute-start.27 = (f32[2,64,256]{2,1,0:T(8,128)S(1)}, f32[2,64,256]{2,1,0:T(8,128)S(1)}, u32[]{:S(2)}, u32[]{:S(2)}) collective-permute-start(f32[2,64,256]{2,1,0:T(8,128)S(1)} %dynamic-slice_bitcast_fusion), channel_id=1, source_target_pairs={{0,1},{1,0},{2,3},{3,2},{4,5},{5,4},{6,7},{7,6},{8,9},{9,8},{10,11... | collective-permute-start | bytes 393224 | tf_op jit(solution)/shard_map/ppermute | solution.py:133
  101.7 4.3 %collective-permute-start.28 = (f32[1,64,256]{2,1,0:T(8,128)S(1)}, f32[1,64,256]{2,1,0:T(8,128)S(1)}, u32[]{:S(2)}, u32[]{:S(2)}) collective-permute-start(f32[1,64,256]{2,1,0:T(8,128)S(1)} %constant_dynamic-slice_fusion), channel_id=1, source_target_pairs={{0,2},{1,3},{2,0},{3,1},{4,6},{5,7},{6,4},{7,5},{8,10},{9,11},{10,... | collective-permute-start | bytes 196616 | tf_op jit(solution)/shard_map/ppermute | solution.py:133
  (18 other events, 31.5 us)

commit v12 on v0

v12 whole, which is shorter than its diff:
```python
import functools

import jax
import jax.numpy as jnp
from jax import lax
from jax.experimental import pallas as pl
from jax.experimental.pallas import tpu as pltpu
from jax.sharding import PartitionSpec as P

CONTRACT = (((1,), (1,)), ((), ()))
CHUNKS = (4, 4, 4, 3, 1)


def rounds(n_ex):
    if n_ex == 4:
        near, far = ([(i, i ^ x) for i in range(4)] for x in (1, 3))
        return [(0, near), (0, far), (2, near)], lambda ex, b: _select(ex ^ b, (0, 1, 3, 2))
    ring = [(i, (i + 1) % n_ex) for i in range(n_ex)]
    return [(t, ring) for t in range(n_ex - 1)], lambda ex, b: lax.rem(ex + (n_ex - b), n_ex)


def _select(index, values):
    found = jnp.int32(values[0])
    for i, value in enumerate(values[1:], 1):
        found = jnp.where(index == i, value, found)
    return found


def scores_kernel(n_grp, n_ex, groups, unit, has_base, last, *refs):
    test, scale, *refs = refs
    total = None
    for start, count in groups:
        blocks, train, refs = refs[:count], refs[count], refs[count + 1 :]
        for at in range(0, train.shape[1], unit):
            here, there = slice(at, at + unit), slice(start + at, start + at + unit)
            rows = jnp.concatenate([test[:, there]] + [r[:, here] for r in blocks], axis=0)
            precond = (rows.astype(jnp.float32) * scale[:, there]).astype(jnp.bfloat16)
            part = lax.dot_general(
                precond, train[:, here], CONTRACT, preferred_element_type=jnp.float32
            )
            total = part if total is None else total + part
    if has_base:
        total += refs[0][...]
    if not last:
        refs[-1][...] = total
        return
    out, kept = refs[-2:]
    kept[...] = total
    ex, grp = lax.axis_index("ex"), lax.axis_index("grp")
    queries = test.shape[0]
    half = queries // n_grp
    for b in range(n_ex):
        t = rounds(n_ex)[1](ex, b)
        for h in range(n_grp):
            place = jnp.where(t == 0, h, lax.rem(h + n_grp - grp, n_grp))
            at = pl.multiple_of(t * queries + place * half, half)
            to = b * queries + h * half
            out[to : to + half, :] = kept[pl.ds(at, half), :]


def scores(n_grp, n_ex, test, scale, unit, groups, base, last):
    docs = groups[0][2].shape[0]
    shape = (test.shape[0] * n_ex, docs)
    operands = [test, scale]
    for _, blocks, train in groups:
        operands += [*blocks, train]
    operands += [] if base is None else [base]
    width = sum(train.shape[1] for _, _, train in groups)
    return pl.pallas_call(
        functools.partial(
            scores_kernel, n_grp, n_ex, [(s, len(r)) for s, r, _ in groups], unit, base is not None, last
        ),
        out_shape=jax.ShapeDtypeStruct(shape, jnp.float32),
        in_specs=[pl.BlockSpec(memory_space=pltpu.VMEM)] * len(operands),
        out_specs=pl.BlockSpec(memory_space=pltpu.VMEM),
        scratch_shapes=[pltpu.VMEM(shape, jnp.float32)] if last else [],
        cost_estimate=pl.CostEstimate(
            flops=2 * shape[0] * docs * width,
            bytes_accessed=2 * (shape[0] + docs) * width,
            transcendentals=0,
        ),
        compiler_params=pltpu.CompilerParams(vmem_limit_bytes=12 * 1024 * 1024),
    )(*operands)


def solution(mesh):
    n_grp, n_ex, n_feat = (mesh.shape[a] for a in ("grp", "ex", "feat"))
    assert n_grp <= 2

    def on_device(train, test, hess):
        docs, feats = train.shape
        queries = test.shape[0]
        half = queries // n_grp
        unit = feats // sum(CHUNKS)
        grp, feat = lax.axis_index("grp"), lax.axis_index("feat")
        plan, _ = rounds(n_ex)
        hops, swaps = [], []

        def after(block, *waits):
            return lax.optimization_barrier((block, waits))[0] if waits else block

        def hop(block, pairs, *ahead):
            waits = [*hops[-2:-1], *swaps[-4:-3], *ahead]
            hops.append(lax.ppermute(after(block, *waits), "ex", pairs))
            return hops[-1]

        def swap(block):
            if n_grp == 1:
                return [block]
            swaps.append(lax.ppermute(after(block, *swaps[-2:-1]), "grp", [(0, 1), (1, 0)]))
            return [block, swaps[-1]]

        def sum_over_feat(sums):
            held = sums.reshape(n_feat, -1, docs)
            bit = 1
            while bit < n_feat:
                pairs = held.reshape((-1, 2) + held.shape[1:])
                mine = (feat // bit) % 2
                keep = lax.dynamic_index_in_dim(pairs, mine, 1, keepdims=False)
                away = lax.dynamic_index_in_dim(pairs, 1 - mine, 1, keepdims=False)
                held = keep + lax.ppermute(away, "feat", [(i, i ^ bit) for i in range(n_feat)])
                bit *= 2
            return held[0]

        def share(rows, start, width, other):
            columns = slice(start, start + width)
            if n_grp == 1:
                return rows[:, columns]
            return jnp.where(grp == other, rows[:half, columns], rows[half:, columns])

        scale = (1.0 / (hess + jnp.float32(0.1))).reshape(1, feats)
        widths = [width * unit for width in CHUNKS]
        starts = [sum(widths[:c]) for c in range(len(widths))]
        whole, final = len(widths) - 1, n_ex - 1
        held = []
        for c, (start, width) in enumerate(zip(starts, widths)):
            rows = after(test, *[h[0] for h in held[-1:]])
            mine = share(rows, start, width, 0)
            if c == whole and n_grp > 1:
                mine = jnp.concatenate([mine, share(rows, start, width, 1)])
            held.append({0: mine})
        trains = [train[:, start : start + width] for start, width in zip(starts, widths)]

        if n_ex == 4:
            order = [(0, 1), (0, 2)]
            for c in range(1, whole):
                order += [(c, 1), (c - 1, 3), (c, 2)]
            order += [(whole, 2), (whole - 1, 3), (whole, 1), (whole, 3)]
        else:
            order = [(c, t) for t in range(1, n_ex) for c in range(whole + 1)]

        got = [[None] * final for _ in widths]
        sums, made = None, []
        for j, (c, t) in enumerate(order):
            source, pairs = plan[t - 1]
            ahead = [m for at, m in made if at == j - 5]
            ahead += trains[whole - 1 :] if j == len(order) - 3 else []
            held[c][t] = hop(held[c][source], pairs, *ahead)
            got[c][t - 1] = [held[c][t]] if c == whole else swap(held[c][t])
            if t == final and c < whole - 1:
                group = (starts[c], sum(got[c], []), trains[c])
                sums = scores(n_grp, n_ex, test, scale, unit, [group], sums, False)
                made.append((j, sums))
        blocks = [sum(parts, []) for parts in got]
        groups = list(zip(starts, blocks, trains))[whole - 1 :]
        return sum_over_feat(scores(n_grp, n_ex, test, scale, unit, groups, sums, True)).T

    return jax.shard_map(
        on_device,
        mesh=mesh,
        in_specs=(P(("grp", "ex"), "feat"), P("ex", "feat"), P("feat")),
        out_specs=P(("grp", "ex"), "feat"),
        check_vma=False,
    )
```

time: 198 us -> 107 us (0.54)
  waiting for transfers between devices: 171 us -> 38.8 us
  starting transfers between devices: 0.04 us -> 37.8 us
  local copies, waits for them, and re-layouts: 0 us -> 19.2 us
  between operations: 13.4 us -> 0.23 us
  matrix products: 8.85 us -> 0 us
  Pallas kernels: 0 us -> 6.58 us
    all_gather x1 -> x0, waiting for transfers between devices: 152 us -> none  [on_device(): lax.all_gather(precond, 'ex', axis=0, tiled=True)]
    ppermute x0 -> x29, waiting for transfers between devices: none -> 38.8 us  [the longest x15 34.4 us: hop(): hops.append(lax.ppermute(after(block, *waits), 'ex', pairs))]
    ppermute x0 -> x29, starting transfers between devices: none -> 37.8 us  [the longest x15 21.5 us: hop(): hops.append(lax.ppermute(after(block, *waits), 'ex', pairs))]
    reduce_scatter x1 -> x0, waiting for transfers between devices: 18.4 us -> none  [on_device(): lax.psum_scatter(partial_sums, 'feat', scatter_dimension=1, tiled=True)]
    unnamed x0 -> x34, local copies, waits for them, and re-layouts: none -> 9.82 us
    slice x0 -> x3, local copies, waits for them, and re-layouts: none -> 9.39 us  [on_device(): train[:, start:start + width]]
    dot_general x1 -> x0, matrix products: 8.85 us -> none  [on_device(): lax.dot_general(train_grads, lax.all_gather(precond, 'ex', axis=0, tiled=...]
    pallas_call x0 -> x4, Pallas kernels: none -> 6.58 us  [scores(): pl.pallas_call(functools.partial(scores_kernel, n_grp, n_ex, [(s, len(r))...]
  transfers between devices with their start and end apart: 2 -> 29, of which waited for: 2 -> 16; matrix products, arithmetic and copies ran while one was open for 0% -> 11% of each run, Pallas kernels for 0% -> 4%
where the time goes in v12:
time: 107 us
  waiting for transfers between devices  38.8 us (36%)
  starting transfers between devices  37.8 us (35%)
  local copies, waits for them, and re-layouts  19.2 us (18%)
  Pallas kernels  6.58 us (6%)
  other arithmetic  4.2 us (4%)
    ppermute x15, waiting for transfers between devices, hop(): hops.append(lax.ppermute(after(block, *waits), 'ex', pairs))  34.4 us
    ppermute x15, starting transfers between devices, hop(): hops.append(lax.ppermute(after(block, *waits), 'ex', pairs))  21.5 us
    ppermute x12, starting transfers between devices, swap(): lax.ppermute(after(block, *swaps[-2:-1]), 'grp', [(0, 1), (1, 0)])  14.6 us
    unnamed x34, local copies, waits for them, and re-layouts  9.82 us
    slice x3, local copies, waits for them, and re-layouts, on_device(): train[:, start:start + width]  9.39 us
    pallas_call x4, Pallas kernels, scores(): pl.pallas_call(functools.partial(scores_kernel, n_grp, n_ex, [(s, len(r))...  6.58 us
    ppermute x2, waiting for transfers between devices, sum_over_feat(): lax.ppermute(away, 'feat', [(i, i ^ bit) for i in range(n_feat)])  3.98 us
    select_n x5, other arithmetic, share(): return jnp.where(grp == other, rows[:half, columns], rows[half:, columns])  2.87 us
  transfers between devices with their start and end apart: 29, of which 16 were waited for; matrix products, arithmetic and copies ran while one was open for 11% of the time, Pallas kernels for 4%

profile of v12, /device:TPU:0, one launch (start us, length us, event | category | flops | bytes accessed | tf_op | source)
XLA Modules:
  0.0 106.9 jit_solution(14325955497440512247)
XLA Ops:
  1.1 3.1 %collective-permute-start = (bf16[32,4096]{1,0:T(8,128)(2,1)S(1)}, bf16[32,4096]{1,0:T(8,128)(2,1)S(1)}, u32[]{:S(2)}, u32[]{:S(2)}) collective-permute-start(bf16[32,4096]{1,0:T(8,128)(2,1)S(1)} %slice_select_fusion.2), channel_id=1, source_target_pairs={{0,4},{4,0},{8,12},{12,8},{1,5},{5,1},{9,13},{13,9},{2,6},{6,2},{1... | collective-permute-start | bytes 786440 | tf_op jit(solution)/shard_map/ppermute | solution.py:104
  4.2 2.5 %collective-permute-start.7 = (bf16[32,4096]{1,0:T(8,128)(2,1)S(1)}, bf16[32,4096]{1,0:T(8,128)(2,1)S(1)}, u32[]{:S(2)}, u32[]{:S(2)}) collective-permute-start(bf16[32,4096]{1,0:T(8,128)(2,1)S(1)} %slice_select_fusion.2), channel_id=1, source_target_pairs={{0,12},{4,8},{8,4},{12,0},{1,13},{5,9},{9,5},{13,1},{2,14},{6,10},... | collective-permute-start | bytes 786440 | tf_op jit(solution)/shard_map/ppermute | solution.py:104
  7.7 3.1 %collective-permute-done.refs_2_ = bf16[32,4096]{1,0:T(8,128)(2,1)S(1)} collective-permute-done((bf16[32,4096]{1,0:T(8,128)(2,1)S(1)}, bf16[32,4096]{1,0:T(8,128)(2,1)S(1)}, u32[]{:S(2)}, u32[]{:S(2)}) %collective-permute-start) | collective-permute-done | bytes 262176 | tf_op jit(solution)/shard_map/ppermute | solution.py:104
  10.9 2.5 %collective-permute-start.1 = (bf16[32,4096]{1,0:T(8,128)(2,1)S(1)}, bf16[32,4096]{1,0:T(8,128)(2,1)S(1)}, u32[]{:S(2)}, u32[]{:S(2)}) collective-permute-start(bf16[32,4096]{1,0:T(8,128)(2,1)S(1)} %slice_select_fusion.1), channel_id=1, source_target_pairs={{0,4},{4,0},{8,12},{12,8},{1,5},{5,1},{9,13},{13,9},{2,6},{6,2},{1... | collective-permute-start | bytes 786440 | tf_op jit(solution)/shard_map/ppermute | solution.py:104
  13.3 1.5 %collective-permute-start.2 = (bf16[32,4096]{1,0:T(8,128)(2,1)S(1)}, bf16[32,4096]{1,0:T(8,128)(2,1)S(1)}, u32[]{:S(2)}, u32[]{:S(2)}) collective-permute-start(bf16[32,4096]{1,0:T(8,128)(2,1)S(1)} %collective-permute-done.refs_2_), channel_id=1, source_target_pairs={{0,16},{16,0},{1,17},{17,1},{2,18},{18,2},{3,19},{19,3},{4,20},{20... | collective-permute-start | bytes 786440 | tf_op jit(solution)/shard_map/ppermute | solution.py:110
  14.9 5.6 %fusion = (bf16[256,4096]{1,0:T(8,128)(2,1)}, bf16[256,4096]{1,0:T(8,128)(2,1)S(1)}, bf16[256,4096]{1,0:T(8,128)(2,1)}) fusion(bf16[256,16384]{1,0:T(8,128)(2,1)} %param.3), kind=kLoop, calls=%fused_computation.12 | loop fusion | bytes 12582912 | tf_op jit(solution)/shard_map/slice | solution.py:142
  21.1 3.0 %collective-permute-done.1.refs_2_ = bf16[32,4096]{1,0:T(8,128)(2,1)S(1)} collective-permute-done((bf16[32,4096]{1,0:T(8,128)(2,1)S(1)}, bf16[32,4096]{1,0:T(8,128)(2,1)S(1)}, u32[]{:S(2)}, u32[]{:S(2)}) %collective-permute-start.1) | collective-permute-done | bytes 262176 | tf_op jit(solution)/shard_map/ppermute | solution.py:104
  24.1 4.5 %collective-permute-start.3 = (bf16[32,4096]{1,0:T(8,128)(2,1)S(1)}, bf16[32,4096]{1,0:T(8,128)(2,1)S(1)}, u32[]{:S(2)}, u32[]{:S(2)}) collective-permute-start(bf16[32,4096]{1,0:T(8,128)(2,1)S(1)} %slice_select_fusion.1), channel_id=1, source_target_pairs={{0,12},{4,8},{8,4},{12,0},{1,13},{5,9},{9,5},{13,1},{2,14},{6,10},... | collective-permute-start | bytes 786440 | tf_op jit(solution)/shard_map/ppermute | solution.py:104
  28.6 1.5 %collective-permute-start.4 = (bf16[32,4096]{1,0:T(8,128)(2,1)S(1)}, bf16[32,4096]{1,0:T(8,128)(2,1)S(1)}, u32[]{:S(2)}, u32[]{:S(2)}) collective-permute-start(bf16[32,4096]{1,0:T(8,128)(2,1)S(1)} %collective-permute-done.1.refs_2_), channel_id=1, source_target_pairs={{0,16},{16,0},{1,17},{17,1},{2,18},{18,2},{3,19},{19,3},{4,20},{20... | collective-permute-start | bytes 786440 | tf_op jit(solution)/shard_map/ppermute | solution.py:110
  30.2 1.4 %collective-permute-done.9.refs_6_ = bf16[32,4096]{1,0:T(8,128)(2,1)S(1)} collective-permute-done((bf16[32,4096]{1,0:T(8,128)(2,1)S(1)}, bf16[32,4096]{1,0:T(8,128)(2,1)S(1)}, u32[]{:S(2)}, u32[]{:S(2)}) %collective-permute-start.9) | collective-permute-done | bytes 262176 | tf_op jit(solution)/shard_map/ppermute | solution.py:104
  31.6 1.4 %collective-permute-start.10 = (bf16[32,4096]{1,0:T(8,128)(2,1)S(1)}, bf16[32,4096]{1,0:T(8,128)(2,1)S(1)}, u32[]{:S(2)}, u32[]{:S(2)}) collective-permute-start(bf16[32,4096]{1,0:T(8,128)(2,1)S(1)} %collective-permute-done.9.refs_6_), channel_id=1, source_target_pairs={{0,16},{16,0},{1,17},{17,1},{2,18},{18,2},{3,19},{19,3},{4,20},{20... | collective-permute-start | bytes 786440 | tf_op jit(solution)/shard_map/ppermute | solution.py:110
  33.0 6.7 %collective-permute-done.3.refs_4_ = bf16[32,4096]{1,0:T(8,128)(2,1)S(1)} collective-permute-done((bf16[32,4096]{1,0:T(8,128)(2,1)S(1)}, bf16[32,4096]{1,0:T(8,128)(2,1)S(1)}, u32[]{:S(2)}, u32[]{:S(2)}) %collective-permute-start.3) | collective-permute-done | bytes 262176 | tf_op jit(solution)/shard_map/ppermute | solution.py:104
  42.2 1.7 %collective-permute-done.16.refs_2_ = bf16[32,4096]{1,0:T(8,128)(2,1)S(1)} collective-permute-done((bf16[32,4096]{1,0:T(8,128)(2,1)S(1)}, bf16[32,4096]{1,0:T(8,128)(2,1)S(1)}, u32[]{:S(2)}, u32[]{:S(2)}) %collective-permute-start.16) | collective-permute-done | bytes 262176 | tf_op jit(solution)/shard_map/ppermute | solution.py:104
  43.9 3.0 %collective-permute-start.17 = (bf16[32,4096]{1,0:T(8,128)(2,1)S(1)}, bf16[32,4096]{1,0:T(8,128)(2,1)}, u32[]{:S(2)}, u32[]{:S(2)}) collective-permute-start(bf16[32,4096]{1,0:T(8,128)(2,1)S(1)} %slice_select_fusion), channel_id=1, source_target_pairs={{0,12},{4,8},{8,4},{12,0},{1,13},{5,9},{9,5},{13,1},{2,14},{6,10},... | collective-permute-start | bytes 786440 | tf_op jit(solution)/shard_map/ppermute | solution.py:104
  46.8 2.1 %collective-permute-start.18 = (bf16[32,4096]{1,0:T(8,128)(2,1)S(1)}, bf16[32,4096]{1,0:T(8,128)(2,1)S(1)}, u32[]{:S(2)}, u32[]{:S(2)}) collective-permute-start(bf16[32,4096]{1,0:T(8,128)(2,1)S(1)} %collective-permute-done.16.refs_2_), channel_id=1, source_target_pairs={{0,16},{16,0},{1,17},{17,1},{2,18},{18,2},{3,19},{19,3},{4,20},{20... | collective-permute-start | bytes 786440 | tf_op jit(solution)/shard_map/ppermute | solution.py:110
  49.6 3.0 %collective-permute-done.5.refs_6_ = bf16[32,4096]{1,0:T(8,128)(2,1)} collective-permute-done((bf16[32,4096]{1,0:T(8,128)(2,1)S(1)}, bf16[32,4096]{1,0:T(8,128)(2,1)}, u32[]{:S(2)}, u32[]{:S(2)}) %collective-permute-start.5) | collective-permute-done | bytes 262176 | tf_op jit(solution)/shard_map/ppermute | solution.py:104
  53.5 2.2 %collective-permute-done.17.refs_4_ = bf16[32,4096]{1,0:T(8,128)(2,1)} collective-permute-done((bf16[32,4096]{1,0:T(8,128)(2,1)S(1)}, bf16[32,4096]{1,0:T(8,128)(2,1)}, u32[]{:S(2)}, u32[]{:S(2)}) %collective-permute-start.17) | collective-permute-done | bytes 262176 | tf_op jit(solution)/shard_map/ppermute | solution.py:104
  56.4 2.1 %collective-permute-start.19 = (bf16[32,4096]{1,0:T(8,128)(2,1)}, bf16[32,4096]{1,0:T(8,128)(2,1)}, u32[]{:S(2)}, u32[]{:S(2)}) collective-permute-start(bf16[32,4096]{1,0:T(8,128)(2,1)} %collective-permute-done.17.refs_4_), channel_id=1, source_target_pairs={{0,16},{16,0},{1,17},{17,1},{2,18},{18,2},{3,19},{19,3},{4,20},{20... | collective-permute-start | bytes 786440 | tf_op jit(solution)/shard_map/ppermute | solution.py:110
  58.5 2.7 %slice.56.refs_8_ = bf16[256,3072]{1,0:T(8,128)(2,1)} slice(bf16[256,16384]{1,0:T(8,128)(2,1)} %param.3), slice={[0:256], [12288:15360]} | slice | bytes 3145728 | tf_op jit(solution)/shard_map/slice | solution.py:142
  62.3 1.9 %collective-permute-start.14 = (bf16[32,3072]{1,0:T(8,128)(2,1)}, bf16[32,3072]{1,0:T(8,128)(2,1)}, u32[]{:S(2)}, u32[]{:S(2)}) collective-permute-start(bf16[32,3072]{1,0:T(8,128)(2,1)} %slice_select_fusion.3), channel_id=1, source_target_pairs={{0,12},{4,8},{8,4},{12,0},{1,13},{5,9},{9,5},{13,1},{2,14},{6,10},... | collective-permute-start | bytes 589832 | tf_op jit(solution)/shard_map/ppermute | solution.py:104
  64.3 2.3 %collective-permute-done.21.refs_6_ = bf16[32,4096]{1,0:T(8,128)(2,1)} collective-permute-done((bf16[32,4096]{1,0:T(8,128)(2,1)}, bf16[32,4096]{1,0:T(8,128)(2,1)}, u32[]{:S(2)}, u32[]{:S(2)}) %collective-permute-start.21) | collective-permute-done | bytes 262176 | tf_op jit(solution)/shard_map/ppermute | solution.py:104
  68.6 3.5 %collective-permute-done.14.refs_4_ = bf16[32,3072]{1,0:T(8,128)(2,1)} collective-permute-done((bf16[32,3072]{1,0:T(8,128)(2,1)}, bf16[32,3072]{1,0:T(8,128)(2,1)}, u32[]{:S(2)}, u32[]{:S(2)}) %collective-permute-start.14) | collective-permute-done | bytes 196640 | tf_op jit(solution)/shard_map/ppermute | solution.py:104
  72.8 1.6 %copy-done.2 = bf16[256,4096]{1,0:T(8,128)(2,1)S(1)} copy-done((bf16[256,4096]{1,0:T(8,128)(2,1)S(1)}, bf16[256,4096]{1,0:T(8,128)(2,1)}, u32[]{:S(2)}) %copy-start.2) | copy-done | bytes 2097176
  77.2 1.9 %shard_map.38.refs_9_ = f32[256,256]{1,0:T(8,128)S(1)} custom-call(bf16[64,16384]{1,0:T(8,128)(2,1)S(1)} %copy-done, f32[1,16384]{1,0:T(1,128)S(1)} %bitcast.11, bf16[32,4096]{1,0:T(8,128)(2,1)S(1)} %collective-permute-done.1.refs_2_, bf16[32,4096]{1,0:T(8,128)(2,1)S(1)} %copy-done.7, bf16[32,4096]{1,0:T(8,128)(2,1)S(1)} %copy-done.5, ...), custom_call_target="tpu_custom_call" | custom-call | flops 536870912 | bytes 4194304 | tf_op jit(solution)/shard_map/pallas_call | solution.py:69
  79.2 1.9 %collective-permute-start.24 = (bf16[64,1024]{1,0:T(8,128)(2,1)}, bf16[64,1024]{1,0:T(8,128)(2,1)}, u32[]{:S(2)}, u32[]{:S(2)}) collective-permute-start(bf16[64,1024]{1,0:T(8,128)(2,1)} %pad_maximum_fusion), channel_id=1, source_target_pairs={{0,12},{4,8},{8,4},{12,0},{1,13},{5,9},{9,5},{13,1},{2,14},{6,10},... | collective-permute-start | bytes 393224 | tf_op jit(solution)/shard_map/ppermute | solution.py:104
  81.6 1.5 %collective-permute-start.23 = (bf16[32,3072]{1,0:T(8,128)(2,1)}, bf16[32,3072]{1,0:T(8,128)(2,1)}, u32[]{:S(2)}, u32[]{:S(2)}) collective-permute-start(bf16[32,3072]{1,0:T(8,128)(2,1)} %collective-permute-done.20.refs_6_), channel_id=1, source_target_pairs={{0,16},{16,0},{1,17},{17,1},{2,18},{18,2},{3,19},{19,3},{4,20},{20... | collective-permute-start | bytes 589832 | tf_op jit(solution)/shard_map/ppermute | solution.py:110
  83.1 3.9 %collective-permute-done.24.refs_10_ = bf16[64,1024]{1,0:T(8,128)(2,1)} collective-permute-done((bf16[64,1024]{1,0:T(8,128)(2,1)}, bf16[64,1024]{1,0:T(8,128)(2,1)}, u32[]{:S(2)}, u32[]{:S(2)}) %collective-permute-start.24) | collective-permute-done | bytes 131104 | tf_op jit(solution)/shard_map/ppermute | solution.py:104
  88.0 1.9 %shard_map.39.refs_13_ = f32[256,256]{1,0:T(8,128)S(1)} custom-call(bf16[64,16384]{1,0:T(8,128)(2,1)S(1)} %copy-done, f32[1,16384]{1,0:T(1,128)S(1)} %bitcast.12, bf16[32,4096]{1,0:T(8,128)(2,1)S(1)} %collective-permute-done.16.refs_2_, bf16[32,4096]{1,0:T(8,128)(2,1)S(1)} %copy-done.9, bf16[32,4096]{1,0:T(8,128)(2,1)} %collective-permute-done.17.refs_4_, ...), custom_call_target="tpu_custom_call" | custom-call | flops 536870912 | bytes 4194304 | tf_op jit(solution)/shard_map/pallas_call | solution.py:69
  92.9 2.1 %collective-permute-done.26.refs_11_ = bf16[64,1024]{1,0:T(8,128)(2,1)S(1)} collective-permute-done((bf16[64,1024]{1,0:T(8,128)(2,1)}, bf16[64,1024]{1,0:T(8,128)(2,1)S(1)}, u32[]{:S(2)}, u32[]{:S(2)}) %collective-permute-start.26) | collective-permute-done | bytes 131104 | tf_op jit(solution)/shard_map/ppermute | solution.py:104
  98.3 2.1 %shard_map.40 = f32[256,256]{1,0:T(8,128)S(1)} custom-call(bf16[64,16384]{1,0:T(8,128)(2,1)S(1)} %copy-done, f32[1,16384]{1,0:T(1,128)S(1)} %bitcast.13, bf16[32,3072]{1,0:T(8,128)(2,1)} %collective-permute-done.11.refs_2_, bf16[32,3072]{1,0:T(8,128)(2,1)S(1)} %copy-done.13, bf16[32,3072]{1,0:T(8,128)(2,1)} %collective-permute-done.14.refs_4_, ...), custom_call_target="tpu_custom_call" | custom-call | flops 536870912 | bytes 4194304 | tf_op jit(solution)/shard_map/pallas_call | solution.py:69
  101.9 1.6 %collective-permute-start.28 = (f32[1,64,256]{2,1,0:T(8,128)S(1)}, f32[1,64,256]{2,1,0:T(8,128)S(1)}, u32[]{:S(2)}, u32[]{:S(2)}) collective-permute-start(f32[1,64,256]{2,1,0:T(8,128)S(1)} %constant_dynamic-slice_fusion), channel_id=1, source_target_pairs={{0,2},{1,3},{2,0},{3,1},{4,6},{5,7},{6,4},{7,5},{8,10},{9,11},{10,... | collective-permute-start | bytes 196616 | tf_op jit(solution)/shard_map/ppermute | solution.py:121
  103.5 2.7 %collective-permute-done.28 = f32[1,64,256]{2,1,0:T(8,128)S(1)} collective-permute-done((f32[1,64,256]{2,1,0:T(8,128)S(1)}, f32[1,64,256]{2,1,0:T(8,128)S(1)}, u32[]{:S(2)}, u32[]{:S(2)}) %collective-permute-start.28) | collective-permute-done | bytes 65568 | tf_op jit(solution)/shard_map/ppermute | solution.py:121
  (78 shorter events, 24.1 us)
Async XLA Ops:
  1.1 9.8 %collective-permute-start = (bf16[32,4096]{1,0:T(8,128)(2,1)S(1)}, bf16[32,4096]{1,0:T(8,128)(2,1)S(1)}, u32[]{:S(2)}, u32[]{:S(2)}) collective-permute-start(bf16[32,4096]{1,0:T(8,128)(2,1)S(1)} %slice_select_fusion.2), channel_id=1, source_target_pairs={{0,4},{4,0},{8,12},{12,8},{1,5},{5,1},{9,13},{13,9},{2,6},{6,2},{1... | collective-permute-start | bytes 786440 | tf_op jit(solution)/shard_map/ppermute | solution.py:104
  4.2 16.3 %collective-permute-start.7 = (bf16[32,4096]{1,0:T(8,128)(2,1)S(1)}, bf16[32,4096]{1,0:T(8,128)(2,1)S(1)}, u32[]{:S(2)}, u32[]{:S(2)}) collective-permute-start(bf16[32,4096]{1,0:T(8,128)(2,1)S(1)} %slice_select_fusion.2), channel_id=1, source_target_pairs={{0,12},{4,8},{8,4},{12,0},{1,13},{5,9},{9,5},{13,1},{2,14},{6,10},... | collective-permute-start | bytes 786440 | tf_op jit(solution)/shard_map/ppermute | solution.py:104
  7.7 22.4 %copy-start = (bf16[64,16384]{1,0:T(8,128)(2,1)S(1)}, bf16[64,16384]{1,0:T(8,128)(2,1)}, u32[]{:S(2)}) copy-start(bf16[64,16384]{1,0:T(8,128)(2,1)} %refs_0_.7) | copy-start | bytes 6291460
  7.7 44.9 %copy-start.16 = (f32[16384]{0:T(1024)S(1)}, f32[16384]{0:T(1024)}, u32[]{:S(2)}) copy-start(f32[16384]{0:T(1024)} %param.5) | copy-start | bytes 196612
  10.9 13.2 %collective-permute-start.1 = (bf16[32,4096]{1,0:T(8,128)(2,1)S(1)}, bf16[32,4096]{1,0:T(8,128)(2,1)S(1)}, u32[]{:S(2)}, u32[]{:S(2)}) collective-permute-start(bf16[32,4096]{1,0:T(8,128)(2,1)S(1)} %slice_select_fusion.1), channel_id=1, source_target_pairs={{0,4},{4,0},{8,12},{12,8},{1,5},{5,1},{9,13},{13,9},{2,6},{6,2},{1... | collective-permute-start | bytes 786440 | tf_op jit(solution)/shard_map/ppermute | solution.py:104
  13.3 10.8 %collective-permute-start.2 = (bf16[32,4096]{1,0:T(8,128)(2,1)S(1)}, bf16[32,4096]{1,0:T(8,128)(2,1)S(1)}, u32[]{:S(2)}, u32[]{:S(2)}) collective-permute-start(bf16[32,4096]{1,0:T(8,128)(2,1)S(1)} %collective-permute-done.refs_2_), channel_id=1, source_target_pairs={{0,16},{16,0},{1,17},{17,1},{2,18},{18,2},{3,19},{19,3},{4,20},{20... | collective-permute-start | bytes 786440 | tf_op jit(solution)/shard_map/ppermute | solution.py:110
  20.5 11.1 %collective-permute-start.9 = (bf16[32,4096]{1,0:T(8,128)(2,1)S(1)}, bf16[32,4096]{1,0:T(8,128)(2,1)S(1)}, u32[]{:S(2)}, u32[]{:S(2)}) collective-permute-start(bf16[32,4096]{1,0:T(8,128)(2,1)S(1)} %collective-permute-done.7.refs_4_), channel_id=1, source_target_pairs={{0,4},{4,0},{8,12},{12,8},{1,5},{5,1},{9,13},{13,9},{2,6},{6,2},{1... | collective-permute-start | bytes 786440 | tf_op jit(solution)/shard_map/ppermute | solution.py:104
  20.5 11.1 %collective-permute-start.8 = (bf16[32,4096]{1,0:T(8,128)(2,1)S(1)}, bf16[32,4096]{1,0:T(8,128)(2,1)S(1)}, u32[]{:S(2)}, u32[]{:S(2)}) collective-permute-start(bf16[32,4096]{1,0:T(8,128)(2,1)S(1)} %collective-permute-done.7.refs_4_), channel_id=1, source_target_pairs={{0,16},{16,0},{1,17},{17,1},{2,18},{18,2},{3,19},{19,3},{4,20},{20... | collective-permute-start | bytes 786440 | tf_op jit(solution)/shard_map/ppermute | solution.py:110
  24.1 15.7 %collective-permute-start.3 = (bf16[32,4096]{1,0:T(8,128)(2,1)S(1)}, bf16[32,4096]{1,0:T(8,128)(2,1)S(1)}, u32[]{:S(2)}, u32[]{:S(2)}) collective-permute-start(bf16[32,4096]{1,0:T(8,128)(2,1)S(1)} %slice_select_fusion.1), channel_id=1, source_target_pairs={{0,12},{4,8},{8,4},{12,0},{1,13},{5,9},{9,5},{13,1},{2,14},{6,10},... | collective-permute-start | bytes 786440 | tf_op jit(solution)/shard_map/ppermute | solution.py:104
  28.6 11.2 %collective-permute-start.4 = (bf16[32,4096]{1,0:T(8,128)(2,1)S(1)}, bf16[32,4096]{1,0:T(8,128)(2,1)S(1)}, u32[]{:S(2)}, u32[]{:S(2)}) collective-permute-start(bf16[32,4096]{1,0:T(8,128)(2,1)S(1)} %collective-permute-done.1.refs_2_), channel_id=1, source_target_pairs={{0,16},{16,0},{1,17},{17,1},{2,18},{18,2},{3,19},{19,3},{4,20},{20... | collective-permute-start | bytes 786440 | tf_op jit(solution)/shard_map/ppermute | solution.py:110
  31.6 10.6 %collective-permute-start.10 = (bf16[32,4096]{1,0:T(8,128)(2,1)S(1)}, bf16[32,4096]{1,0:T(8,128)(2,1)S(1)}, u32[]{:S(2)}, u32[]{:S(2)}) collective-permute-start(bf16[32,4096]{1,0:T(8,128)(2,1)S(1)} %collective-permute-done.9.refs_6_), channel_id=1, source_target_pairs={{0,16},{16,0},{1,17},{17,1},{2,18},{18,2},{3,19},{19,3},{4,20},{20... | collective-permute-start | bytes 786440 | tf_op jit(solution)/shard_map/ppermute | solution.py:110
  33.0 10.8 %collective-permute-start.16 = (bf16[32,4096]{1,0:T(8,128)(2,1)S(1)}, bf16[32,4096]{1,0:T(8,128)(2,1)S(1)}, u32[]{:S(2)}, u32[]{:S(2)}) collective-permute-start(bf16[32,4096]{1,0:T(8,128)(2,1)S(1)} %slice_select_fusion), channel_id=1, source_target_pairs={{0,4},{4,0},{8,12},{12,8},{1,5},{5,1},{9,13},{13,9},{2,6},{6,2},{1... | collective-permute-start | bytes 786440 | tf_op jit(solution)/shard_map/ppermute | solution.py:104
  39.8 13.6 %copy-start.6 = (bf16[32,4096]{1,0:T(8,128)(2,1)}, bf16[32,4096]{1,0:T(8,128)(2,1)S(1)}, u32[]{:S(2)}) copy-start(bf16[32,4096]{1,0:T(8,128)(2,1)S(1)} %collective-permute-done.4.refs_3_) | copy-start | bytes 786436
  39.8 9.1 %collective-permute-start.6 = (bf16[32,4096]{1,0:T(8,128)(2,1)S(1)}, bf16[32,4096]{1,0:T(8,128)(2,1)S(1)}, u32[]{:S(2)}, u32[]{:S(2)}) collective-permute-start(bf16[32,4096]{1,0:T(8,128)(2,1)S(1)} %collective-permute-done.3.refs_4_), channel_id=1, source_target_pairs={{0,16},{16,0},{1,17},{17,1},{2,18},{18,2},{3,19},{19,3},{4,20},{20... | collective-permute-start | bytes 786440 | tf_op jit(solution)/shard_map/ppermute | solution.py:110
  41.1 11.5 %collective-permute-start.5 = (bf16[32,4096]{1,0:T(8,128)(2,1)S(1)}, bf16[32,4096]{1,0:T(8,128)(2,1)}, u32[]{:S(2)}, u32[]{:S(2)}) collective-permute-start(bf16[32,4096]{1,0:T(8,128)(2,1)S(1)} %collective-permute-done.3.refs_4_), channel_id=1, source_target_pairs={{0,4},{4,0},{8,12},{12,8},{1,5},{5,1},{9,13},{13,9},{2,6},{6,2},{1... | collective-permute-start | bytes 786440 | tf_op jit(solution)/shard_map/ppermute | solution.py:104
  43.9 11.8 %collective-permute-start.17 = (bf16[32,4096]{1,0:T(8,128)(2,1)S(1)}, bf16[32,4096]{1,0:T(8,128)(2,1)}, u32[]{:S(2)}, u32[]{:S(2)}) collective-permute-start(bf16[32,4096]{1,0:T(8,128)(2,1)S(1)} %slice_select_fusion), channel_id=1, source_target_pairs={{0,12},{4,8},{8,4},{12,0},{1,13},{5,9},{9,5},{13,1},{2,14},{6,10},... | collective-permute-start | bytes 786440 | tf_op jit(solution)/shard_map/ppermute | solution.py:104
  46.8 8.9 %collective-permute-start.18 = (bf16[32,4096]{1,0:T(8,128)(2,1)S(1)}, bf16[32,4096]{1,0:T(8,128)(2,1)S(1)}, u32[]{:S(2)}, u32[]{:S(2)}) collective-permute-start(bf16[32,4096]{1,0:T(8,128)(2,1)S(1)} %collective-permute-done.16.refs_2_), channel_id=1, source_target_pairs={{0,16},{16,0},{1,17},{17,1},{2,18},{18,2},{3,19},{19,3},{4,20},{20... | collective-permute-start | bytes 786440 | tf_op jit(solution)/shard_map/ppermute | solution.py:110
  52.6 9.6 %collective-permute-start.12 = (bf16[32,4096]{1,0:T(8,128)(2,1)}, bf16[32,4096]{1,0:T(8,128)(2,1)}, u32[]{:S(2)}, u32[]{:S(2)}) collective-permute-start(bf16[32,4096]{1,0:T(8,128)(2,1)} %collective-permute-done.5.refs_6_), channel_id=1, source_target_pairs={{0,16},{16,0},{1,17},{17,1},{2,18},{18,2},{3,19},{19,3},{4,20},{20... | collective-permute-start | bytes 786440 | tf_op jit(solution)/shard_map/ppermute | solution.py:110
  53.4 8.8 %collective-permute-start.11 = (bf16[32,3072]{1,0:T(8,128)(2,1)}, bf16[32,3072]{1,0:T(8,128)(2,1)}, u32[]{:S(2)}, u32[]{:S(2)}) collective-permute-start(bf16[32,3072]{1,0:T(8,128)(2,1)} %slice_select_fusion.3), channel_id=1, source_target_pairs={{0,4},{4,0},{8,12},{12,8},{1,5},{5,1},{9,13},{13,9},{2,6},{6,2},{1... | collective-permute-start | bytes 589832 | tf_op jit(solution)/shard_map/ppermute | solution.py:104
  56.4 7.9 %collective-permute-start.19 = (bf16[32,4096]{1,0:T(8,128)(2,1)}, bf16[32,4096]{1,0:T(8,128)(2,1)}, u32[]{:S(2)}, u32[]{:S(2)}) collective-permute-start(bf16[32,4096]{1,0:T(8,128)(2,1)} %collective-permute-done.17.refs_4_), channel_id=1, source_target_pairs={{0,16},{16,0},{1,17},{17,1},{2,18},{18,2},{3,19},{19,3},{4,20},{20... | collective-permute-start | bytes 786440 | tf_op jit(solution)/shard_map/ppermute | solution.py:110
  58.5 8.1 %collective-permute-start.21 = (bf16[32,4096]{1,0:T(8,128)(2,1)}, bf16[32,4096]{1,0:T(8,128)(2,1)}, u32[]{:S(2)}, u32[]{:S(2)}) collective-permute-start(bf16[32,4096]{1,0:T(8,128)(2,1)} %collective-permute-done.17.refs_4_), channel_id=1, source_target_pairs={{0,4},{4,0},{8,12},{12,8},{1,5},{5,1},{9,13},{13,9},{2,6},{6,2},{1... | collective-permute-start | bytes 786440 | tf_op jit(solution)/shard_map/ppermute | solution.py:104
  62.3 9.9 %collective-permute-start.14 = (bf16[32,3072]{1,0:T(8,128)(2,1)}, bf16[32,3072]{1,0:T(8,128)(2,1)}, u32[]{:S(2)}, u32[]{:S(2)}) collective-permute-start(bf16[32,3072]{1,0:T(8,128)(2,1)} %slice_select_fusion.3), channel_id=1, source_target_pairs={{0,12},{4,8},{8,4},{12,0},{1,13},{5,9},{9,5},{13,1},{2,14},{6,10},... | collective-permute-start | bytes 589832 | tf_op jit(solution)/shard_map/ppermute | solution.py:104
  66.6 15.0 %collective-permute-start.22 = (bf16[32,4096]{1,0:T(8,128)(2,1)}, bf16[32,4096]{1,0:T(8,128)(2,1)S(1)}, u32[]{:S(2)}, u32[]{:S(2)}) collective-permute-start(bf16[32,4096]{1,0:T(8,128)(2,1)} %collective-permute-done.21.refs_6_), channel_id=1, source_target_pairs={{0,16},{16,0},{1,17},{17,1},{2,18},{18,2},{3,19},{19,3},{4,20},{20... | collective-permute-start | bytes 786440 | tf_op jit(solution)/shard_map/ppermute | solution.py:110
  67.3 13.7 %collective-permute-start.13 = (bf16[32,3072]{1,0:T(8,128)(2,1)}, bf16[32,3072]{1,0:T(8,128)(2,1)S(1)}, u32[]{:S(2)}, u32[]{:S(2)}) collective-permute-start(bf16[32,3072]{1,0:T(8,128)(2,1)} %collective-permute-done.11.refs_2_), channel_id=1, source_target_pairs={{0,16},{16,0},{1,17},{17,1},{2,18},{18,2},{3,19},{19,3},{4,20},{20... | collective-permute-start | bytes 589832 | tf_op jit(solution)/shard_map/ppermute | solution.py:110
  72.1 9.5 %collective-permute-start.20 = (bf16[32,3072]{1,0:T(8,128)(2,1)}, bf16[32,3072]{1,0:T(8,128)(2,1)}, u32[]{:S(2)}, u32[]{:S(2)}) collective-permute-start(bf16[32,3072]{1,0:T(8,128)(2,1)} %collective-permute-done.14.refs_4_), channel_id=1, source_target_pairs={{0,4},{4,0},{8,12},{12,8},{1,5},{5,1},{9,13},{13,9},{2,6},{6,2},{1... | collective-permute-start | bytes 589832 | tf_op jit(solution)/shard_map/ppermute | solution.py:104
  79.2 7.8 %collective-permute-start.24 = (bf16[64,1024]{1,0:T(8,128)(2,1)}, bf16[64,1024]{1,0:T(8,128)(2,1)}, u32[]{:S(2)}, u32[]{:S(2)}) collective-permute-start(bf16[64,1024]{1,0:T(8,128)(2,1)} %pad_maximum_fusion), channel_id=1, source_target_pairs={{0,12},{4,8},{8,4},{12,0},{1,13},{5,9},{9,5},{13,1},{2,14},{6,10},... | collective-permute-start | bytes 393224 | tf_op jit(solution)/shard_map/ppermute | solution.py:104
  81.1 11.2 %collective-permute-start.15 = (bf16[32,3072]{1,0:T(8,128)(2,1)}, bf16[32,3072]{1,0:T(8,128)(2,1)S(1)}, u32[]{:S(2)}, u32[]{:S(2)}) collective-permute-start(bf16[32,3072]{1,0:T(8,128)(2,1)} %collective-permute-done.14.refs_4_), channel_id=1, source_target_pairs={{0,16},{16,0},{1,17},{17,1},{2,18},{18,2},{3,19},{19,3},{4,20},{20... | collective-permute-start | bytes 589832 | tf_op jit(solution)/shard_map/ppermute | solution.py:110
  81.6 13.4 %collective-permute-start.23 = (bf16[32,3072]{1,0:T(8,128)(2,1)}, bf16[32,3072]{1,0:T(8,128)(2,1)}, u32[]{:S(2)}, u32[]{:S(2)}) collective-permute-start(bf16[32,3072]{1,0:T(8,128)(2,1)} %collective-permute-done.20.refs_6_), channel_id=1, source_target_pairs={{0,16},{16,0},{1,17},{17,1},{2,18},{18,2},{3,19},{19,3},{4,20},{20... | collective-permute-start | bytes 589832 | tf_op jit(solution)/shard_map/ppermute | solution.py:110
  87.0 5.3 %collective-permute-start.25 = (bf16[64,1024]{1,0:T(8,128)(2,1)}, bf16[64,1024]{1,0:T(8,128)(2,1)}, u32[]{:S(2)}, u32[]{:S(2)}) collective-permute-start(bf16[64,1024]{1,0:T(8,128)(2,1)} %pad_maximum_fusion), channel_id=1, source_target_pairs={{0,4},{4,0},{8,12},{12,8},{1,5},{5,1},{9,13},{13,9},{2,6},{6,2},{1... | collective-permute-start | bytes 393224 | tf_op jit(solution)/shard_map/ppermute | solution.py:104
  89.8 5.2 %collective-permute-start.26 = (bf16[64,1024]{1,0:T(8,128)(2,1)}, bf16[64,1024]{1,0:T(8,128)(2,1)S(1)}, u32[]{:S(2)}, u32[]{:S(2)}) collective-permute-start(bf16[64,1024]{1,0:T(8,128)(2,1)} %collective-permute-done.24.refs_10_), channel_id=1, source_target_pairs={{0,4},{4,0},{8,12},{12,8},{1,5},{5,1},{9,13},{13,9},{2,6},{6,2},{1... | collective-permute-start | bytes 393224 | tf_op jit(solution)/shard_map/ppermute | solution.py:104
  100.4 1.4 %collective-permute-start.27 = (f32[2,64,256]{2,1,0:T(8,128)S(1)}, f32[2,64,256]{2,1,0:T(8,128)S(1)}, u32[]{:S(2)}, u32[]{:S(2)}) collective-permute-start(f32[2,64,256]{2,1,0:T(8,128)S(1)} %dynamic-slice_bitcast_fusion), channel_id=1, source_target_pairs={{0,1},{1,0},{2,3},{3,2},{4,5},{5,4},{6,7},{7,6},{8,9},{9,8},{10,11... | collective-permute-start | bytes 393224 | tf_op jit(solution)/shard_map/ppermute | solution.py:121
  101.9 4.3 %collective-permute-start.28 = (f32[1,64,256]{2,1,0:T(8,128)S(1)}, f32[1,64,256]{2,1,0:T(8,128)S(1)}, u32[]{:S(2)}, u32[]{:S(2)}) collective-permute-start(f32[1,64,256]{2,1,0:T(8,128)S(1)} %constant_dynamic-slice_fusion), channel_id=1, source_target_pairs={{0,2},{1,3},{2,0},{3,1},{4,6},{5,7},{6,4},{7,5},{8,10},{9,11},{10,... | collective-permute-start | bytes 196616 | tf_op jit(solution)/shard_map/ppermute | solution.py:121
  (14 other events, 53.6 us)

commit v13 on v10

--- a/solution.py
+++ b/solution.py
@@ -33,27 +33,30 @@
     out[...] = total
 
 
-def arrived(groups, scale, refs):
-    refs, total = list(refs), None
-    for start, unit, count in groups:
-        parts, train, refs = refs[:count], refs[count], refs[count + 1 :]
-        rows = lambda here: jnp.concatenate([p[:, here] for p in parts], axis=0)
-        column = lambda here: scale[:, start + here.start : start + here.stop]
-        part = product(rows, column, train, unit)
-        total = part if total is None else total + part
-    return total, refs
+def arrived_rows(parts):
+    return lambda here: jnp.concatenate([p[:, here] for p in parts], axis=0)
 
 
-def part_kernel(groups, scale, *refs):
-    total, (*base, out) = arrived(groups, scale, refs)
-    out[...] = total + base[0][...] if base else total
+def part_kernel(start, unit, n_parts, has_base, *refs):
+    parts, (scale, train) = refs[:n_parts], refs[n_parts : n_parts + 2]
+    column = lambda here: scale[:, start + here.start : start + here.stop]
+    total = product(arrived_rows(parts), column, train, unit)
+    refs[-1][...] = total + refs[n_parts + 2][...] if has_base else total
 
 
-def last_kernel(n_grp, n_ex, groups, scale, *refs):
-    total, (*sums, out, kept) = arrived(groups, scale, refs)
+def last_kernel(n_grp, n_ex, starts, unit, n_parts, *refs):
+    parts, (scale, train), refs = refs[:n_parts], refs[n_parts : n_parts + 2], refs[n_parts + 2 :]
+    wholes, (whole_train, *sums), (out, kept) = refs[: n_ex - 1], refs[n_ex - 1 : -2], refs[-2:]
+    columns = lambda start: lambda here: scale[:, start + here.start : start + here.stop]
+    total = product(arrived_rows(parts), columns(starts[0]), train, unit)
     queries = total.shape[0]
     half = queries // n_grp
-    for t, value in enumerate([s[...] for s in sums[:-1]] + [total + sums[-1][...]]):
+    for t, value in enumerate(sums):
+        value = value[...]
+        if t > 0:
+            value += product(arrived_rows([wholes[t - 1]]), columns(starts[1]), whole_train, unit)
+        if t == n_ex - 1:
+            value += total
         kept[t * queries : (t + 1) * queries, :] = value
     ex, grp = lax.axis_index("ex"), lax.axis_index("grp")
     for b in range(n_ex):
@@ -75,7 +78,7 @@
         cost_estimate=pl.CostEstimate(
             flops=2 * rows * docs * width, bytes_accessed=2 * (rows + docs) * width, transcendentals=0
         ),
-        compiler_params=pltpu.CompilerParams(vmem_limit_bytes=4 * 1024 * 1024),
+        compiler_params=pltpu.CompilerParams(vmem_limit_bytes=16 * 1024 * 1024),
     )(*operands)
 
 
@@ -96,15 +99,14 @@
             return lax.optimization_barrier((block, waits))[0] if waits else block
 
         def hop(block):
-            waits = hops[-2:-1] + swaps[-4:-3] + (first if len(hops) == 3 else [])
+            waits = hops[-2:-1] + swaps[-4:-3] + made[-5:-4] + (first if len(hops) == 3 else [])
             hops.append(lax.ppermute(after(block, *waits), "ex", ring))
             return hops[-1]
 
         def swap(block):
             if n_grp == 1:
                 return [block]
-            waits = swaps[-2:-1] + made[-3:-2]
-            swaps.append(lax.ppermute(after(block, *waits), "grp", [(0, 1), (1, 0)]))
+            swaps.append(lax.ppermute(after(block, *swaps[-2:-1]), "grp", [(0, 1), (1, 0)]))
             return [block, swaps[-1]]
 
         def sum_over_feat(sums):
@@ -119,7 +121,7 @@
                 bit *= 2
             return held[0]
 
-        def share(rows, start, width, other):
+        def share(rows, start, width, other=0):
             columns = slice(start, start + width)
             if n_grp == 1:
                 return rows[:, columns]
@@ -129,10 +131,11 @@
         widths = [width * unit for width in CHUNKS]
         starts = [sum(widths[:c]) for c in range(len(widths))]
         held = []
+        final, whole = n_ex - 1, len(widths) - 1
         for c, (start, width) in enumerate(zip(starts, widths)):
             rows = after(test, *held[-1:])
-            mine = share(rows, start, width, 0)
-            if c == len(widths) - 1 and n_grp > 1:
+            mine = share(rows, start, width)
+            if c == whole and n_grp > 1:
                 mine = jnp.concatenate([mine, share(rows, start, width, 1)])
             held.append(mine)
         trains = [train[:, start : start + width] for start, width in zip(starts, widths)]
@@ -140,34 +143,32 @@
             functools.partial(own_kernel, starts, unit), queries, docs, feats, [test, scale, *trains]
         )
         first.append(own)
-        final, whole = n_ex - 1, len(widths) - 1
-        order = [(t, c) for t in range(1, final) for c in range(whole)]
-        waiting = [(t, whole) for t in range(1, n_ex)]
-        for c in range(whole):
-            order.append((final, c))
-            order += [waiting.pop(0) for _ in range(len(waiting) // (whole - c))]
-
-        sums, groups, operands = [own] + [None] * final, [], []
+        order = [(t, c) for t in range(1, n_ex) for c in range(whole)]
+        order[-whole + 1 : -whole + 1] = [(t, whole) for t in range(1, final - 1)]
+        order += [(t, whole) for t in range(max(final - 1, 1), n_ex)]
+        sums, wholes = [own] + [None] * final, []
         for t, c in order:
             held[c] = hop(held[c])
-            parts = [held[c]] if c == whole else swap(held[c])
-            group, arrays = (starts[c], unit, len(parts)), [*parts, trains[c]]
-            if t == final and c >= whole - 1:
-                groups.append(group)
-                operands += arrays
+            if c == whole:
+                wholes.append(held[c])
+                continue
+            parts = swap(held[c])
+            operands = [*parts, scale, trains[c]]
+            if (t, c) == (final, whole - 1):
+                last = operands
                 continue
             base = [] if sums[t] is None else [sums[t]]
             sums[t] = call(
-                functools.partial(part_kernel, [group]), queries, docs, widths[c], [scale, *arrays, *base]
+                functools.partial(part_kernel, starts[c], unit, len(parts), len(base)),
+                queries, docs, widths[c], operands + base,
             )
             made.append(sums[t])
-        out = call(
-            functools.partial(last_kernel, n_grp, n_ex, groups),
-            n_ex * queries, docs, sum(widths[whole - 1 :]), [scale, *operands, *sums],
+        total = call(
+            functools.partial(last_kernel, n_grp, n_ex, starts[-2:], unit, len(last) - 2),
+            n_ex * queries, docs, sum(widths[-2:]), [*last, *wholes, trains[whole], *sums],
             [pltpu.VMEM((n_ex * queries, docs), jnp.float32)],
         )
-        return sum_over_feat(out).T
-
+        return sum_over_feat(total).T
 
     return jax.shard_map(
         on_device,

time: 107 us -> 112 us (1.047)
  starting transfers between devices: 24.9 us -> 28.8 us
  Pallas kernels: 19.2 us -> 17 us
  waiting for transfers between devices: 41.7 us -> 43 us
  local copies, waits for them, and re-layouts: 15.9 us -> 17.1 us
    ppermute x12, waiting for transfers between devices: 0.99 us -> 9.16 us  [swap(): lax.ppermute(after(block, *swaps[-2:-1]), 'grp', [(0, 1), (1, 0)])]
    ppermute x15, waiting for transfers between devices: 37.1 us -> 29.2 us  [hop(): hops.append(lax.ppermute(after(block, *waits), 'ex', ring))]
    ppermute x15, starting transfers between devices: 6.21 us -> 12.4 us  [hop(): hops.append(lax.ppermute(after(block, *waits), 'ex', ring))]
    pallas_call x15 -> x13, Pallas kernels: 19.2 us -> 17 us  [call(): pl.pallas_call(kernel, out_shape=jax.ShapeDtypeStruct((rows, docs), jnp.f...]
    unnamed x44 -> x46, local copies, waits for them, and re-layouts: 9.37 us -> 10.7 us
    ppermute x2, starting transfers between devices: 2.26 us -> 1.03 us  [sum_over_feat(): lax.ppermute(away, 'feat', [(i, i ^ bit) for i in range(n_feat)])]
  transfers between devices with their start and end apart: 29 -> 29, of which waited for: 13 -> 14; matrix products, arithmetic and copies ran while one was open for 8% -> 9% of each run, Pallas kernels for 16% -> 13%
where the time goes in v13:
time: 112 us; the launch traced here: 111 us
  waiting for transfers between devices  43 us (38%)
  starting transfers between devices  28.8 us (26%)
  local copies, waits for them, and re-layouts  17.1 us (15%)
  Pallas kernels  17 us (15%)
  other arithmetic  4.76 us (4%)
    ppermute x15, waiting for transfers between devices, hop(): hops.append(lax.ppermute(after(block, *waits), 'ex', ring))  29.2 us
    pallas_call x13, Pallas kernels, call(): pl.pallas_call(kernel, out_shape=jax.ShapeDtypeStruct((rows, docs), jnp.f...  17 us
    ppermute x12, starting transfers between devices, swap(): lax.ppermute(after(block, *swaps[-2:-1]), 'grp', [(0, 1), (1, 0)])  15.4 us
    ppermute x15, starting transfers between devices, hop(): hops.append(lax.ppermute(after(block, *waits), 'ex', ring))  12.4 us
    unnamed x46, local copies, waits for them, and re-layouts  10.7 us
    ppermute x12, waiting for transfers between devices, swap(): lax.ppermute(after(block, *swaps[-2:-1]), 'grp', [(0, 1), (1, 0)])  9.16 us
    slice x3, local copies, waits for them, and re-layouts, on_device(): train[:, start:start + width]  6.39 us
    ppermute x2, waiting for transfers between devices, sum_over_feat(): lax.ppermute(away, 'feat', [(i, i ^ bit) for i in range(n_feat)])  4.67 us
  transfers between devices with their start and end apart: 29, of which 14 were waited for; matrix products, arithmetic and copies ran while one was open for 9% of the time, Pallas kernels for 13%

profile of v13, /device:TPU:0, one launch (start us, length us, event | category | flops | bytes accessed | tf_op | source)
XLA Modules:
  0.0 111.0 jit_solution(190528756736838000)
XLA Ops:
  1.1 3.1 %collective-permute-start.3 = (bf16[32,4096]{1,0:T(8,128)(2,1)S(1)}, bf16[32,4096]{1,0:T(8,128)(2,1)S(1)}, u32[]{:S(2)}, u32[]{:S(2)}) collective-permute-start(bf16[32,4096]{1,0:T(8,128)(2,1)S(1)} %slice_select_fusion.2), channel_id=1, source_target_pairs={{0,4},{4,8},{8,12},{12,0},{1,5},{5,9},{9,13},{13,1},{2,6},{6,10},{... | collective-permute-start | bytes 786440 | tf_op jit(solution)/shard_map/ppermute | solution.py:103
  5.2 1.6 %collective-permute-start = (bf16[32,4096]{1,0:T(8,128)(2,1)S(1)}, bf16[32,4096]{1,0:T(8,128)(2,1)S(1)}, u32[]{:S(2)}, u32[]{:S(2)}) collective-permute-start(bf16[32,4096]{1,0:T(8,128)(2,1)S(1)} %slice_select_fusion.1), channel_id=1, source_target_pairs={{0,4},{4,8},{8,12},{12,0},{1,5},{5,9},{9,13},{13,1},{2,6},{6,10},{... | collective-permute-start | bytes 786440 | tf_op jit(solution)/shard_map/ppermute | solution.py:103
  7.9 3.8 %fusion = (bf16[256,4096]{1,0:T(8,128)(2,1)S(1)}, bf16[256,4096]{1,0:T(8,128)(2,1)S(1)}, bf16[256,4096]{1,0:T(8,128)(2,1)S(1)}) fusion(bf16[256,16384]{1,0:T(8,128)(2,1)} %param.3), kind=kLoop, calls=%fused_computation.12 | loop fusion | bytes 12582912 | tf_op jit(solution)/shard_map/slice | solution.py:141
  11.8 1.5 %collective-permute-done.3.refs_0_ = bf16[32,4096]{1,0:T(8,128)(2,1)S(1)} collective-permute-done((bf16[32,4096]{1,0:T(8,128)(2,1)S(1)}, bf16[32,4096]{1,0:T(8,128)(2,1)S(1)}, u32[]{:S(2)}, u32[]{:S(2)}) %collective-permute-start.3) | collective-permute-done | bytes 262176 | tf_op jit(solution)/shard_map/ppermute | solution.py:103
  13.4 1.6 %collective-permute-start.4 = (bf16[32,4096]{1,0:T(8,128)(2,1)S(1)}, bf16[32,4096]{1,0:T(8,128)(2,1)S(1)}, u32[]{:S(2)}, u32[]{:S(2)}) collective-permute-start(bf16[32,4096]{1,0:T(8,128)(2,1)S(1)} %collective-permute-done.3.refs_0_), channel_id=1, source_target_pairs={{0,16},{16,0},{1,17},{17,1},{2,18},{18,2},{3,19},{19,3},{4,20},{20... | collective-permute-start | bytes 786440 | tf_op jit(solution)/shard_map/ppermute | solution.py:109
  15.1 3.8 %collective-permute-done.refs_0_ = bf16[32,4096]{1,0:T(8,128)(2,1)S(1)} collective-permute-done((bf16[32,4096]{1,0:T(8,128)(2,1)S(1)}, bf16[32,4096]{1,0:T(8,128)(2,1)S(1)}, u32[]{:S(2)}, u32[]{:S(2)}) %collective-permute-start) | collective-permute-done | bytes 262176 | tf_op jit(solution)/shard_map/ppermute | solution.py:103
  18.9 1.8 %collective-permute-start.2 = (bf16[32,4096]{1,0:T(8,128)(2,1)S(1)}, bf16[32,4096]{1,0:T(8,128)(2,1)S(1)}, u32[]{:S(2)}, u32[]{:S(2)}) collective-permute-start(bf16[32,4096]{1,0:T(8,128)(2,1)S(1)} %collective-permute-done.refs_0_), channel_id=1, source_target_pairs={{0,16},{16,0},{1,17},{17,1},{2,18},{18,2},{3,19},{19,3},{4,20},{20... | collective-permute-start | bytes 786440 | tf_op jit(solution)/shard_map/ppermute | solution.py:109
  21.8 1.5 %slice.58.refs_3_ = bf16[256,3072]{1,0:T(8,128)(2,1)S(1)} slice(bf16[256,16384]{1,0:T(8,128)(2,1)} %param.3), slice={[0:256], [12288:15360]} | slice | bytes 3145728 | tf_op jit(solution)/shard_map/slice | solution.py:141
  23.7 1.5 %collective-permute-start.8 = (bf16[32,4096]{1,0:T(8,128)(2,1)S(1)}, bf16[32,4096]{1,0:T(8,128)(2,1)S(1)}, u32[]{:S(2)}, u32[]{:S(2)}) collective-permute-start(bf16[32,4096]{1,0:T(8,128)(2,1)S(1)} %collective-permute-done.7.refs_0_), channel_id=1, source_target_pairs={{0,16},{16,0},{1,17},{17,1},{2,18},{18,2},{3,19},{19,3},{4,20},{20... | collective-permute-start | bytes 786440 | tf_op jit(solution)/shard_map/ppermute | solution.py:109
  25.2 2.7 %shard_map.37.refs_8_ = f32[64,256]{1,0:T(8,128)S(1)} custom-call(bf16[64,16384]{1,0:T(8,128)(2,1)S(1)} %copy-done.9, f32[1,16384]{1,0:T(1,128)S(1)} %bitcast.10, bf16[256,4096]{1,0:T(8,128)(2,1)S(1)} %get-tuple-element.61.refs_0_.refs_3_, bf16[256,4096]{1,0:T(8,128)(2,1)S(1)} %get-tuple-element.60.refs_1_.refs_3_, ...), custom_call_target="tpu_custom_call" | custom-call | flops 536870912 | bytes 10485760 | tf_op jit(solution)/shard_map/pallas_call | solution.py:72
  27.9 1.3 %collective-permute-start.1 = (bf16[32,3072]{1,0:T(8,128)(2,1)S(1)}, bf16[32,3072]{1,0:T(8,128)(2,1)S(1)}, u32[]{:S(2)}, u32[]{:S(2)}) collective-permute-start(bf16[32,3072]{1,0:T(8,128)(2,1)S(1)} %slice_select_fusion.3), channel_id=1, source_target_pairs={{0,4},{4,8},{8,12},{12,0},{1,5},{5,9},{9,13},{13,1},{2,6},{6,10},{... | collective-permute-start | bytes 589832 | tf_op jit(solution)/shard_map/ppermute | solution.py:103
  30.0 8.2 %collective-permute-done.1.refs_0_ = bf16[32,3072]{1,0:T(8,128)(2,1)S(1)} collective-permute-done((bf16[32,3072]{1,0:T(8,128)(2,1)S(1)}, bf16[32,3072]{1,0:T(8,128)(2,1)S(1)}, u32[]{:S(2)}, u32[]{:S(2)}) %collective-permute-start.1) | collective-permute-done | bytes 196640 | tf_op jit(solution)/shard_map/ppermute | solution.py:103
  39.8 1.3 %collective-permute-start.6 = (bf16[32,3072]{1,0:T(8,128)(2,1)S(1)}, bf16[32,3072]{1,0:T(8,128)(2,1)S(1)}, u32[]{:S(2)}, u32[]{:S(2)}) collective-permute-start(bf16[32,3072]{1,0:T(8,128)(2,1)S(1)} %collective-permute-done.1.refs_0_), channel_id=1, source_target_pairs={{0,16},{16,0},{1,17},{17,1},{2,18},{18,2},{3,19},{19,3},{4,20},{20... | collective-permute-start | bytes 589832 | tf_op jit(solution)/shard_map/ppermute | solution.py:109
  41.1 8.9 %collective-permute-done.6.refs_1_ = bf16[32,3072]{1,0:T(8,128)(2,1)S(1)} collective-permute-done((bf16[32,3072]{1,0:T(8,128)(2,1)S(1)}, bf16[32,3072]{1,0:T(8,128)(2,1)S(1)}, u32[]{:S(2)}, u32[]{:S(2)}) %collective-permute-start.6) | collective-permute-done | bytes 196640 | tf_op jit(solution)/shard_map/ppermute | solution.py:109
  53.8 1.7 %collective-permute-start.17 = (bf16[32,4096]{1,0:T(8,128)(2,1)}, bf16[32,4096]{1,0:T(8,128)(2,1)S(1)}, u32[]{:S(2)}, u32[]{:S(2)}) collective-permute-start(bf16[32,4096]{1,0:T(8,128)(2,1)} %collective-permute-done.11.refs_0_), channel_id=1, source_target_pairs={{0,16},{16,0},{1,17},{17,1},{2,18},{18,2},{3,19},{19,3},{4,20},{20... | collective-permute-start | bytes 786440 | tf_op jit(solution)/shard_map/ppermute | solution.py:109
  56.4 1.6 %copy-done.4 = bf16[256,4096]{1,0:T(8,128)(2,1)S(1)} copy-done((bf16[256,4096]{1,0:T(8,128)(2,1)S(1)}, bf16[256,4096]{1,0:T(8,128)(2,1)}, u32[]{:S(2)}) %copy-start.4) | copy-done | bytes 2097176
  59.0 1.8 %shard_map.42.refs_4_ = f32[64,256]{1,0:T(8,128)S(1)} custom-call(bf16[32,4096]{1,0:T(8,128)(2,1)} %collective-permute-done.10.refs_0_, bf16[32,4096]{1,0:T(8,128)(2,1)S(1)} %copy-done.17, f32[1,16384]{1,0:T(1,128)S(1)} %bitcast.15, bf16[256,4096]{1,0:T(8,128)(2,1)S(1)} %copy-done.4), custom_call_target="tpu_custom_call" | custom-call | flops 134217728 | bytes 2621440 | tf_op jit(solution)/shard_map/pallas_call | solution.py:72
  61.9 2.3 %collective-permute-start.15 = (bf16[32,4096]{1,0:T(8,128)(2,1)S(1)}, bf16[32,4096]{1,0:T(8,128)(2,1)S(1)}, u32[]{:S(2)}, u32[]{:S(2)}) collective-permute-start(bf16[32,4096]{1,0:T(8,128)(2,1)S(1)} %copy-done.11), channel_id=1, source_target_pairs={{0,4},{4,8},{8,12},{12,0},{1,5},{5,9},{9,13},{13,1},{2,6},{6,10},{... | collective-permute-start | bytes 786440 | tf_op jit(solution)/shard_map/ppermute | solution.py:103
  64.2 1.9 %collective-permute-done.9.refs_0_ = bf16[32,3072]{1,0:T(8,128)(2,1)S(1)} collective-permute-done((bf16[32,3072]{1,0:T(8,128)(2,1)S(1)}, bf16[32,3072]{1,0:T(8,128)(2,1)S(1)}, u32[]{:S(2)}, u32[]{:S(2)}) %collective-permute-start.9) | collective-permute-done | bytes 196640 | tf_op jit(solution)/shard_map/ppermute | solution.py:103
  67.3 1.7 %shard_map.43.refs_4_ = f32[64,256]{1,0:T(8,128)S(1)} custom-call(bf16[32,4096]{1,0:T(8,128)(2,1)S(1)} %copy-done.11, bf16[32,4096]{1,0:T(8,128)(2,1)} %collective-permute-done.14.refs_1_, f32[1,16384]{1,0:T(1,128)S(1)} %bitcast.16, bf16[256,4096]{1,0:T(8,128)(2,1)S(1)} %copy-done.1, f32[64,256]{1,0:T(8,128)S(1)} %shard_map.42.refs_4_), custom_call_target="tpu_custom_call" | custom-call | flops 134217728 | bytes 2621440 | tf_op jit(solution)/shard_map/pallas_call | solution.py:72
  69.1 3.8 %collective-permute-done.21.refs_4_ = bf16[64,1024]{1,0:T(8,128)(2,1)S(1)} collective-permute-done((bf16[64,1024]{1,0:T(8,128)(2,1)S(1)}, bf16[64,1024]{1,0:T(8,128)(2,1)S(1)}, u32[]{:S(2)}, u32[]{:S(2)}) %collective-permute-start.21) | collective-permute-done | bytes 131104 | tf_op jit(solution)/shard_map/ppermute | solution.py:103
  74.9 1.7 %shard_map.44.refs_4_ = f32[64,256]{1,0:T(8,128)S(1)} custom-call(bf16[32,4096]{1,0:T(8,128)(2,1)} %collective-permute-done.11.refs_0_, bf16[32,4096]{1,0:T(8,128)(2,1)S(1)} %collective-permute-done.17.refs_1_, f32[1,16384]{1,0:T(1,128)S(1)} %bitcast.17, bf16[256,4096]{1,0:T(8,128)(2,1)S(1)} %get-tuple-element.59.refs_2_.refs_3_, ...), custom_call_target="tpu_custom_call" | custom-call | flops 134217728 | bytes 2621440 | tf_op jit(solution)/shard_map/pallas_call | solution.py:72
  77.9 4.0 %collective-permute-done.22.refs_0_ = bf16[32,4096]{1,0:T(8,128)(2,1)} collective-permute-done((bf16[32,4096]{1,0:T(8,128)(2,1)}, bf16[32,4096]{1,0:T(8,128)(2,1)}, u32[]{:S(2)}, u32[]{:S(2)}) %collective-permute-start.22) | collective-permute-done | bytes 262176 | tf_op jit(solution)/shard_map/ppermute | solution.py:103
  83.3 1.6 %collective-permute-start.24 = (bf16[64,1024]{1,0:T(8,128)(2,1)S(1)}, bf16[64,1024]{1,0:T(8,128)(2,1)}, u32[]{:S(2)}, u32[]{:S(2)}) collective-permute-start(bf16[64,1024]{1,0:T(8,128)(2,1)S(1)} %collective-permute-done.21.refs_4_), channel_id=1, source_target_pairs={{0,4},{4,8},{8,12},{12,0},{1,5},{5,9},{9,13},{13,1},{2,6},{6,10},{... | collective-permute-start | bytes 393224 | tf_op jit(solution)/shard_map/ppermute | solution.py:103
  86.6 1.8 %collective-permute-start.20 = (bf16[32,3072]{1,0:T(8,128)(2,1)}, bf16[32,3072]{1,0:T(8,128)(2,1)}, u32[]{:S(2)}, u32[]{:S(2)}) collective-permute-start(bf16[32,3072]{1,0:T(8,128)(2,1)} %collective-permute-done.18.refs_0_), channel_id=1, source_target_pairs={{0,16},{16,0},{1,17},{17,1},{2,18},{18,2},{3,19},{19,3},{4,20},{20... | collective-permute-start | bytes 589832 | tf_op jit(solution)/shard_map/ppermute | solution.py:109
  88.4 3.8 %collective-permute-done.24.refs_5_ = bf16[64,1024]{1,0:T(8,128)(2,1)} collective-permute-done((bf16[64,1024]{1,0:T(8,128)(2,1)S(1)}, bf16[64,1024]{1,0:T(8,128)(2,1)}, u32[]{:S(2)}, u32[]{:S(2)}) %collective-permute-start.24) | collective-permute-done | bytes 131104 | tf_op jit(solution)/shard_map/ppermute | solution.py:103
  92.2 1.4 %copy-done.7 = bf16[256,3072]{1,0:T(8,128)(2,1)S(1)} copy-done((bf16[256,3072]{1,0:T(8,128)(2,1)S(1)}, bf16[256,3072]{1,0:T(8,128)(2,1)}, u32[]{:S(2)}) %copy-start.7) | copy-done | bytes 1572888
  96.1 1.6 %copy-done.5 = bf16[256,4096]{1,0:T(8,128)(2,1)S(1)} copy-done((bf16[256,4096]{1,0:T(8,128)(2,1)S(1)}, bf16[256,4096]{1,0:T(8,128)(2,1)}, u32[]{:S(2)}) %copy-start.5) | copy-done | bytes 2097176
  100.4 1.9 %shard_map.48.refs_11_ = f32[64,256]{1,0:T(8,128)S(1)} custom-call(bf16[32,4096]{1,0:T(8,128)(2,1)} %collective-permute-done.22.refs_0_, bf16[32,4096]{1,0:T(8,128)(2,1)} %collective-permute-done.26.refs_1_, f32[1,16384]{1,0:T(1,128)S(1)} %bitcast.21, bf16[256,4096]{1,0:T(8,128)(2,1)S(1)} %get-tuple-element.59.refs_2_.refs_3_, f32[64,256]{1,0:T(8,128)S(1)} %shard_map.47.refs_4_), custom_call_target="tpu_custom_call" | custom-call | flops 134217728 | bytes 2621440 | tf_op jit(solution)/shard_map/pallas_call | solution.py:72
  102.3 2.3 %shard_map.49 = f32[256,256]{1,0:T(8,128)S(1)} custom-call(bf16[32,3072]{1,0:T(8,128)(2,1)} %collective-permute-done.18.refs_0_, bf16[32,3072]{1,0:T(8,128)(2,1)} %collective-permute-done.20.refs_1_, f32[1,16384]{1,0:T(1,128)S(1)} %bitcast.22, bf16[256,3072]{1,0:T(8,128)(2,1)S(1)} %copy-done.8, bf16[64,1024]{1,0:T(8,128)(2,1)S(1)} %collective-permute-done.21.refs_4_, ...), custom_call_target="tpu_custom_call" | custom-call | flops 536870912 | bytes 4194304 | tf_op jit(solution)/shard_map/pallas_call | solution.py:72
  104.7 1.3 %collective-permute-done.27 = f32[2,64,256]{2,1,0:T(8,128)S(1)} collective-permute-done((f32[2,64,256]{2,1,0:T(8,128)S(1)}, f32[2,64,256]{2,1,0:T(8,128)S(1)}, u32[]{:S(2)}, u32[]{:S(2)}) %collective-permute-start.27) | collective-permute-done | bytes 131104 | tf_op jit(solution)/shard_map/ppermute | solution.py:120
  107.0 3.4 %collective-permute-done.28 = f32[1,64,256]{2,1,0:T(8,128)S(1)} collective-permute-done((f32[1,64,256]{2,1,0:T(8,128)S(1)}, f32[1,64,256]{2,1,0:T(8,128)S(1)}, u32[]{:S(2)}, u32[]{:S(2)}) %collective-permute-start.28) | collective-permute-done | bytes 65568 | tf_op jit(solution)/shard_map/ppermute | solution.py:120
  (99 shorter events, 28.5 us)
Async XLA Ops:
  1.1 12.2 %collective-permute-start.3 = (bf16[32,4096]{1,0:T(8,128)(2,1)S(1)}, bf16[32,4096]{1,0:T(8,128)(2,1)S(1)}, u32[]{:S(2)}, u32[]{:S(2)}) collective-permute-start(bf16[32,4096]{1,0:T(8,128)(2,1)S(1)} %slice_select_fusion.2), channel_id=1, source_target_pairs={{0,4},{4,8},{8,12},{12,0},{1,5},{5,9},{9,13},{13,1},{2,6},{6,10},{... | collective-permute-start | bytes 786440 | tf_op jit(solution)/shard_map/ppermute | solution.py:103
  5.2 13.7 %collective-permute-start = (bf16[32,4096]{1,0:T(8,128)(2,1)S(1)}, bf16[32,4096]{1,0:T(8,128)(2,1)S(1)}, u32[]{:S(2)}, u32[]{:S(2)}) collective-permute-start(bf16[32,4096]{1,0:T(8,128)(2,1)S(1)} %slice_select_fusion.1), channel_id=1, source_target_pairs={{0,4},{4,8},{8,12},{12,0},{1,5},{5,9},{9,13},{13,1},{2,6},{6,10},{... | collective-permute-start | bytes 786440 | tf_op jit(solution)/shard_map/ppermute | solution.py:103
  11.7 17.5 %copy-start.3 = (bf16[256,4096]{1,0:T(8,128)(2,1)}, bf16[256,4096]{1,0:T(8,128)(2,1)S(1)}, u32[]{:S(2)}) copy-start(bf16[256,4096]{1,0:T(8,128)(2,1)S(1)} %get-tuple-element.61.refs_0_.refs_3_) | copy-start | bytes 6291460
  11.7 26.5 %copy-start = (bf16[256,4096]{1,0:T(8,128)(2,1)}, bf16[256,4096]{1,0:T(8,128)(2,1)S(1)}, u32[]{:S(2)}) copy-start(bf16[256,4096]{1,0:T(8,128)(2,1)S(1)} %get-tuple-element.60.refs_1_.refs_3_) | copy-start | bytes 6291460
  13.3 10.4 %collective-permute-start.7 = (bf16[32,4096]{1,0:T(8,128)(2,1)S(1)}, bf16[32,4096]{1,0:T(8,128)(2,1)S(1)}, u32[]{:S(2)}, u32[]{:S(2)}) collective-permute-start(bf16[32,4096]{1,0:T(8,128)(2,1)S(1)} %slice_select_fusion), channel_id=1, source_target_pairs={{0,4},{4,8},{8,12},{12,0},{1,5},{5,9},{9,13},{13,1},{2,6},{6,10},{... | collective-permute-start | bytes 786440 | tf_op jit(solution)/shard_map/ppermute | solution.py:103
  13.4 10.3 %collective-permute-start.4 = (bf16[32,4096]{1,0:T(8,128)(2,1)S(1)}, bf16[32,4096]{1,0:T(8,128)(2,1)S(1)}, u32[]{:S(2)}, u32[]{:S(2)}) collective-permute-start(bf16[32,4096]{1,0:T(8,128)(2,1)S(1)} %collective-permute-done.3.refs_0_), channel_id=1, source_target_pairs={{0,16},{16,0},{1,17},{17,1},{2,18},{18,2},{3,19},{19,3},{4,20},{20... | collective-permute-start | bytes 786440 | tf_op jit(solution)/shard_map/ppermute | solution.py:109
  18.9 19.3 %collective-permute-start.2 = (bf16[32,4096]{1,0:T(8,128)(2,1)S(1)}, bf16[32,4096]{1,0:T(8,128)(2,1)S(1)}, u32[]{:S(2)}, u32[]{:S(2)}) collective-permute-start(bf16[32,4096]{1,0:T(8,128)(2,1)S(1)} %collective-permute-done.refs_0_), channel_id=1, source_target_pairs={{0,16},{16,0},{1,17},{17,1},{2,18},{18,2},{3,19},{19,3},{4,20},{20... | collective-permute-start | bytes 786440 | tf_op jit(solution)/shard_map/ppermute | solution.py:109
  23.3 28.2 %copy-start.6 = (bf16[256,3072]{1,0:T(8,128)(2,1)}, bf16[256,3072]{1,0:T(8,128)(2,1)S(1)}, u32[]{:S(2)}) copy-start(bf16[256,3072]{1,0:T(8,128)(2,1)S(1)} %slice.58.refs_3_) | copy-start | bytes 4718596
  23.7 15.3 %collective-permute-start.8 = (bf16[32,4096]{1,0:T(8,128)(2,1)S(1)}, bf16[32,4096]{1,0:T(8,128)(2,1)S(1)}, u32[]{:S(2)}, u32[]{:S(2)}) collective-permute-start(bf16[32,4096]{1,0:T(8,128)(2,1)S(1)} %collective-permute-done.7.refs_0_), channel_id=1, source_target_pairs={{0,16},{16,0},{1,17},{17,1},{2,18},{18,2},{3,19},{19,3},{4,20},{20... | collective-permute-start | bytes 786440 | tf_op jit(solution)/shard_map/ppermute | solution.py:109
  25.2 13.8 %collective-permute-start.10 = (bf16[32,4096]{1,0:T(8,128)(2,1)S(1)}, bf16[32,4096]{1,0:T(8,128)(2,1)}, u32[]{:S(2)}, u32[]{:S(2)}) collective-permute-start(bf16[32,4096]{1,0:T(8,128)(2,1)S(1)} %collective-permute-done.3.refs_0_), channel_id=1, source_target_pairs={{0,4},{4,8},{8,12},{12,0},{1,5},{5,9},{9,13},{13,1},{2,6},{6,10},{... | collective-permute-start | bytes 786440 | tf_op jit(solution)/shard_map/ppermute | solution.py:103
  27.9 10.3 %collective-permute-start.1 = (bf16[32,3072]{1,0:T(8,128)(2,1)S(1)}, bf16[32,3072]{1,0:T(8,128)(2,1)S(1)}, u32[]{:S(2)}, u32[]{:S(2)}) collective-permute-start(bf16[32,3072]{1,0:T(8,128)(2,1)S(1)} %slice_select_fusion.3), channel_id=1, source_target_pairs={{0,4},{4,8},{8,12},{12,0},{1,5},{5,9},{9,13},{13,1},{2,6},{6,10},{... | collective-permute-start | bytes 589832 | tf_op jit(solution)/shard_map/ppermute | solution.py:103
  38.2 11.8 %collective-permute-start.5 = (bf16[32,4096]{1,0:T(8,128)(2,1)S(1)}, bf16[32,4096]{1,0:T(8,128)(2,1)S(1)}, u32[]{:S(2)}, u32[]{:S(2)}) collective-permute-start(bf16[32,4096]{1,0:T(8,128)(2,1)S(1)} %collective-permute-done.refs_0_), channel_id=1, source_target_pairs={{0,4},{4,8},{8,12},{12,0},{1,5},{5,9},{9,13},{13,1},{2,6},{6,10},{... | collective-permute-start | bytes 786440 | tf_op jit(solution)/shard_map/ppermute | solution.py:103
  39.0 13.1 %collective-permute-start.12 = (bf16[32,4096]{1,0:T(8,128)(2,1)}, bf16[32,4096]{1,0:T(8,128)(2,1)S(1)}, u32[]{:S(2)}, u32[]{:S(2)}) collective-permute-start(bf16[32,4096]{1,0:T(8,128)(2,1)} %collective-permute-done.10.refs_0_), channel_id=1, source_target_pairs={{0,16},{16,0},{1,17},{17,1},{2,18},{18,2},{3,19},{19,3},{4,20},{20... | collective-permute-start | bytes 786440 | tf_op jit(solution)/shard_map/ppermute | solution.py:109
  39.8 13.0 %collective-permute-start.11 = (bf16[32,4096]{1,0:T(8,128)(2,1)S(1)}, bf16[32,4096]{1,0:T(8,128)(2,1)}, u32[]{:S(2)}, u32[]{:S(2)}) collective-permute-start(bf16[32,4096]{1,0:T(8,128)(2,1)S(1)} %collective-permute-done.7.refs_0_), channel_id=1, source_target_pairs={{0,4},{4,8},{8,12},{12,0},{1,5},{5,9},{9,13},{13,1},{2,6},{6,10},{... | collective-permute-start | bytes 786440 | tf_op jit(solution)/shard_map/ppermute | solution.py:103
  39.8 10.1 %collective-permute-start.6 = (bf16[32,3072]{1,0:T(8,128)(2,1)S(1)}, bf16[32,3072]{1,0:T(8,128)(2,1)S(1)}, u32[]{:S(2)}, u32[]{:S(2)}) collective-permute-start(bf16[32,3072]{1,0:T(8,128)(2,1)S(1)} %collective-permute-done.1.refs_0_), channel_id=1, source_target_pairs={{0,16},{16,0},{1,17},{17,1},{2,18},{18,2},{3,19},{19,3},{4,20},{20... | collective-permute-start | bytes 589832 | tf_op jit(solution)/shard_map/ppermute | solution.py:109
  50.0 10.7 %collective-permute-start.14 = (bf16[32,4096]{1,0:T(8,128)(2,1)S(1)}, bf16[32,4096]{1,0:T(8,128)(2,1)}, u32[]{:S(2)}, u32[]{:S(2)}) collective-permute-start(bf16[32,4096]{1,0:T(8,128)(2,1)S(1)} %collective-permute-done.5.refs_0_), channel_id=1, source_target_pairs={{0,16},{16,0},{1,17},{17,1},{2,18},{18,2},{3,19},{19,3},{4,20},{20... | collective-permute-start | bytes 786440 | tf_op jit(solution)/shard_map/ppermute | solution.py:109
  52.8 9.1 %collective-permute-start.13 = (bf16[32,4096]{1,0:T(8,128)(2,1)}, bf16[32,4096]{1,0:T(8,128)(2,1)S(1)}, u32[]{:S(2)}, u32[]{:S(2)}) collective-permute-start(bf16[32,4096]{1,0:T(8,128)(2,1)} %collective-permute-done.10.refs_0_), channel_id=1, source_target_pairs={{0,4},{4,8},{8,12},{12,0},{1,5},{5,9},{9,13},{13,1},{2,6},{6,10},{... | collective-permute-start | bytes 786440 | tf_op jit(solution)/shard_map/ppermute | solution.py:103
  52.8 13.3 %collective-permute-start.9 = (bf16[32,3072]{1,0:T(8,128)(2,1)S(1)}, bf16[32,3072]{1,0:T(8,128)(2,1)S(1)}, u32[]{:S(2)}, u32[]{:S(2)}) collective-permute-start(bf16[32,3072]{1,0:T(8,128)(2,1)S(1)} %collective-permute-done.1.refs_0_), channel_id=1, source_target_pairs={{0,4},{4,8},{8,12},{12,0},{1,5},{5,9},{9,13},{13,1},{2,6},{6,10},{... | collective-permute-start | bytes 589832 | tf_op jit(solution)/shard_map/ppermute | solution.py:103
  53.8 15.2 %collective-permute-start.17 = (bf16[32,4096]{1,0:T(8,128)(2,1)}, bf16[32,4096]{1,0:T(8,128)(2,1)S(1)}, u32[]{:S(2)}, u32[]{:S(2)}) collective-permute-start(bf16[32,4096]{1,0:T(8,128)(2,1)} %collective-permute-done.11.refs_0_), channel_id=1, source_target_pairs={{0,16},{16,0},{1,17},{17,1},{2,18},{18,2},{3,19},{19,3},{4,20},{20... | collective-permute-start | bytes 786440 | tf_op jit(solution)/shard_map/ppermute | solution.py:109
  61.9 12.3 %collective-permute-start.15 = (bf16[32,4096]{1,0:T(8,128)(2,1)S(1)}, bf16[32,4096]{1,0:T(8,128)(2,1)S(1)}, u32[]{:S(2)}, u32[]{:S(2)}) collective-permute-start(bf16[32,4096]{1,0:T(8,128)(2,1)S(1)} %copy-done.11), channel_id=1, source_target_pairs={{0,4},{4,8},{8,12},{12,0},{1,5},{5,9},{9,13},{13,1},{2,6},{6,10},{... | collective-permute-start | bytes 786440 | tf_op jit(solution)/shard_map/ppermute | solution.py:103
  66.1 6.8 %collective-permute-start.21 = (bf16[64,1024]{1,0:T(8,128)(2,1)S(1)}, bf16[64,1024]{1,0:T(8,128)(2,1)S(1)}, u32[]{:S(2)}, u32[]{:S(2)}) collective-permute-start(bf16[64,1024]{1,0:T(8,128)(2,1)S(1)} %pad_maximum_fusion), channel_id=1, source_target_pairs={{0,4},{4,8},{8,12},{12,0},{1,5},{5,9},{9,13},{13,1},{2,6},{6,10},{... | collective-permute-start | bytes 393224 | tf_op jit(solution)/shard_map/ppermute | solution.py:103
  66.1 8.0 %collective-permute-start.16 = (bf16[32,3072]{1,0:T(8,128)(2,1)S(1)}, bf16[32,3072]{1,0:T(8,128)(2,1)S(1)}, u32[]{:S(2)}, u32[]{:S(2)}) collective-permute-start(bf16[32,3072]{1,0:T(8,128)(2,1)S(1)} %collective-permute-done.9.refs_0_), channel_id=1, source_target_pairs={{0,16},{16,0},{1,17},{17,1},{2,18},{18,2},{3,19},{19,3},{4,20},{20... | collective-permute-start | bytes 589832 | tf_op jit(solution)/shard_map/ppermute | solution.py:109
  72.8 9.0 %collective-permute-start.22 = (bf16[32,4096]{1,0:T(8,128)(2,1)}, bf16[32,4096]{1,0:T(8,128)(2,1)}, u32[]{:S(2)}, u32[]{:S(2)}) collective-permute-start(bf16[32,4096]{1,0:T(8,128)(2,1)} %collective-permute-done.11.refs_0_), channel_id=1, source_target_pairs={{0,4},{4,8},{8,12},{12,0},{1,5},{5,9},{9,13},{13,1},{2,6},{6,10},{... | collective-permute-start | bytes 786440 | tf_op jit(solution)/shard_map/ppermute | solution.py:103
  72.8 9.0 %collective-permute-start.23 = (bf16[32,4096]{1,0:T(8,128)(2,1)S(1)}, bf16[32,4096]{1,0:T(8,128)(2,1)S(1)}, u32[]{:S(2)}, u32[]{:S(2)}) collective-permute-start(bf16[32,4096]{1,0:T(8,128)(2,1)S(1)} %collective-permute-done.13.refs_0_), channel_id=1, source_target_pairs={{0,16},{16,0},{1,17},{17,1},{2,18},{18,2},{3,19},{19,3},{4,20},{20... | collective-permute-start | bytes 786440 | tf_op jit(solution)/shard_map/ppermute | solution.py:109
  74.1 11.8 %collective-permute-start.19 = (bf16[32,4096]{1,0:T(8,128)(2,1)S(1)}, bf16[32,4096]{1,0:T(8,128)(2,1)S(1)}, u32[]{:S(2)}, u32[]{:S(2)}) collective-permute-start(bf16[32,4096]{1,0:T(8,128)(2,1)S(1)} %collective-permute-done.15.refs_0_), channel_id=1, source_target_pairs={{0,16},{16,0},{1,17},{17,1},{2,18},{18,2},{3,19},{19,3},{4,20},{20... | collective-permute-start | bytes 786440 | tf_op jit(solution)/shard_map/ppermute | solution.py:109
  76.7 9.0 %collective-permute-start.18 = (bf16[32,3072]{1,0:T(8,128)(2,1)S(1)}, bf16[32,3072]{1,0:T(8,128)(2,1)}, u32[]{:S(2)}, u32[]{:S(2)}) collective-permute-start(bf16[32,3072]{1,0:T(8,128)(2,1)S(1)} %collective-permute-done.9.refs_0_), channel_id=1, source_target_pairs={{0,4},{4,8},{8,12},{12,0},{1,5},{5,9},{9,13},{13,1},{2,6},{6,10},{... | collective-permute-start | bytes 589832 | tf_op jit(solution)/shard_map/ppermute | solution.py:103
  82.6 17.8 %collective-permute-start.26 = (bf16[32,4096]{1,0:T(8,128)(2,1)}, bf16[32,4096]{1,0:T(8,128)(2,1)}, u32[]{:S(2)}, u32[]{:S(2)}) collective-permute-start(bf16[32,4096]{1,0:T(8,128)(2,1)} %collective-permute-done.22.refs_0_), channel_id=1, source_target_pairs={{0,16},{16,0},{1,17},{17,1},{2,18},{18,2},{3,19},{19,3},{4,20},{20... | collective-permute-start | bytes 786440 | tf_op jit(solution)/shard_map/ppermute | solution.py:109
  83.3 8.9 %collective-permute-start.24 = (bf16[64,1024]{1,0:T(8,128)(2,1)S(1)}, bf16[64,1024]{1,0:T(8,128)(2,1)}, u32[]{:S(2)}, u32[]{:S(2)}) collective-permute-start(bf16[64,1024]{1,0:T(8,128)(2,1)S(1)} %collective-permute-done.21.refs_4_), channel_id=1, source_target_pairs={{0,4},{4,8},{8,12},{12,0},{1,5},{5,9},{9,13},{13,1},{2,6},{6,10},{... | collective-permute-start | bytes 393224 | tf_op jit(solution)/shard_map/ppermute | solution.py:103
  86.6 15.7 %collective-permute-start.20 = (bf16[32,3072]{1,0:T(8,128)(2,1)}, bf16[32,3072]{1,0:T(8,128)(2,1)}, u32[]{:S(2)}, u32[]{:S(2)}) collective-permute-start(bf16[32,3072]{1,0:T(8,128)(2,1)} %collective-permute-done.18.refs_0_), channel_id=1, source_target_pairs={{0,16},{16,0},{1,17},{17,1},{2,18},{18,2},{3,19},{19,3},{4,20},{20... | collective-permute-start | bytes 589832 | tf_op jit(solution)/shard_map/ppermute | solution.py:109
  92.2 10.1 %collective-permute-start.25 = (bf16[64,1024]{1,0:T(8,128)(2,1)}, bf16[64,1024]{1,0:T(8,128)(2,1)}, u32[]{:S(2)}, u32[]{:S(2)}) collective-permute-start(bf16[64,1024]{1,0:T(8,128)(2,1)} %collective-permute-done.24.refs_5_), channel_id=1, source_target_pairs={{0,4},{4,8},{8,12},{12,0},{1,5},{5,9},{9,13},{13,1},{2,6},{6,10},{... | collective-permute-start | bytes 393224 | tf_op jit(solution)/shard_map/ppermute | solution.py:103
  104.6 1.4 %collective-permute-start.27 = (f32[2,64,256]{2,1,0:T(8,128)S(1)}, f32[2,64,256]{2,1,0:T(8,128)S(1)}, u32[]{:S(2)}, u32[]{:S(2)}) collective-permute-start(f32[2,64,256]{2,1,0:T(8,128)S(1)} %dynamic-slice_bitcast_fusion), channel_id=1, source_target_pairs={{0,1},{1,0},{2,3},{3,2},{4,5},{5,4},{6,7},{7,6},{8,9},{9,8},{10,11... | collective-permute-start | bytes 393224 | tf_op jit(solution)/shard_map/ppermute | solution.py:120
  106.0 4.3 %collective-permute-start.28 = (f32[1,64,256]{2,1,0:T(8,128)S(1)}, f32[1,64,256]{2,1,0:T(8,128)S(1)}, u32[]{:S(2)}, u32[]{:S(2)}) collective-permute-start(f32[1,64,256]{2,1,0:T(8,128)S(1)} %constant_dynamic-slice_fusion), channel_id=1, source_target_pairs={{0,2},{1,3},{2,0},{3,1},{4,6},{5,7},{6,4},{7,5},{8,10},{9,11},{10,... | collective-permute-start | bytes 196616 | tf_op jit(solution)/shard_map/ppermute | solution.py:120
  (20 other events, 75.9 us)

commit v14 on v9

--- a/solution.py
+++ b/solution.py
@@ -94,7 +94,7 @@
             return lax.optimization_barrier((block, waits))[0] if waits else block
 
         def hop(block):
-            waits = hops[-2:-1] + swaps[-4:-3] + made[-6:-5] + (first if len(hops) == 3 else [])
+            waits = hops[-2:-1] + swaps[-4:-3] + made[-5:-4] + (first if len(hops) == 3 else [])
             hops.append(lax.ppermute(after(block, *waits), "ex", ring))
             return hops[-1]
 

time: 94.2 us -> 93.5 us (level)
  local copies, waits for them, and re-layouts: 10.8 us -> 9.25 us
    unnamed x46 -> x36, local copies, waits for them, and re-layouts: 6.76 us -> 5.19 us
    ppermute x12, waiting for transfers between devices: 27.6 us -> 28.6 us  [hop(): hops.append(lax.ppermute(after(block, *waits), 'ex', ring))]
  transfers between devices with their start and end apart: 26 -> 26, of which waited for: 18 -> 19; matrix products, arithmetic and copies ran while one was open for 8% -> 8% of each run, Pallas kernels for 13% -> 13%
where the time goes in v14:
time: 93.5 us; the launch traced here: 93.1 us
  waiting for transfers between devices  41.5 us (44%)
  starting transfers between devices  24.3 us (26%)
  Pallas kernels  12.8 us (14%)
  local copies, waits for them, and re-layouts  9.25 us (10%)
  other arithmetic  4.91 us (5%)
    ppermute x12, waiting for transfers between devices, hop(): hops.append(lax.ppermute(after(block, *waits), 'ex', ring))  28.6 us
    ppermute x12, starting transfers between devices, swap(): lax.ppermute(after(block, *swaps[-2:-1]), 'grp', [(0, 1), (1, 0)])  16.4 us
    pallas_call x13, Pallas kernels, call(): pl.pallas_call(kernel, out_shape=jax.ShapeDtypeStruct((rows, docs), jnp.f...  12.8 us
    ppermute x12, waiting for transfers between devices, swap(): lax.ppermute(after(block, *swaps[-2:-1]), 'grp', [(0, 1), (1, 0)])  8.91 us
    ppermute x12, starting transfers between devices, hop(): hops.append(lax.ppermute(after(block, *waits), 'ex', ring))  6.26 us
    unnamed x36, local copies, waits for them, and re-layouts  5.19 us
    select_n x4, other arithmetic, share(): return jnp.where(grp == 0, rows[:half, columns], rows[half:, columns])  4.24 us
    ppermute x2, waiting for transfers between devices, sum_over_feat(): lax.ppermute(away, 'feat', [(i, i ^ bit) for i in range(n_feat)])  4.04 us
  transfers between devices with their start and end apart: 26, of which 19 were waited for; matrix products, arithmetic and copies ran while one was open for 8% of the time, Pallas kernels for 13%

profile of v14, /device:TPU:0, one launch (start us, length us, event | category | flops | bytes accessed | tf_op | source)
XLA Modules:
  0.0 93.1 jit_solution(7538524910220028800)
XLA Ops:
  1.1 3.1 %collective-permute-start.3 = (bf16[32,4096]{1,0:T(8,128)(2,1)S(1)}, bf16[32,4096]{1,0:T(8,128)(2,1)S(1)}, u32[]{:S(2)}, u32[]{:S(2)}) collective-permute-start(bf16[32,4096]{1,0:T(8,128)(2,1)S(1)} %slice_select_fusion.3), channel_id=1, source_target_pairs={{0,4},{4,8},{8,12},{12,0},{1,5},{5,9},{9,13},{13,1},{2,6},{6,10},{... | collective-permute-start | bytes 786440 | tf_op jit(solution)/shard_map/ppermute | solution.py:98
  5.2 1.6 %collective-permute-start = (bf16[32,4096]{1,0:T(8,128)(2,1)S(1)}, bf16[32,4096]{1,0:T(8,128)(2,1)S(1)}, u32[]{:S(2)}, u32[]{:S(2)}) collective-permute-start(bf16[32,4096]{1,0:T(8,128)(2,1)S(1)} %slice_select_fusion.2), channel_id=1, source_target_pairs={{0,4},{4,8},{8,12},{12,0},{1,5},{5,9},{9,13},{13,1},{2,6},{6,10},{... | collective-permute-start | bytes 786440 | tf_op jit(solution)/shard_map/ppermute | solution.py:98
  9.0 4.0 %fusion = (bf16[256,4096]{1,0:T(8,128)(2,1)S(1)}, bf16[256,4096]{1,0:T(8,128)(2,1)S(1)}, bf16[256,4096]{1,0:T(8,128)(2,1)S(1)}, bf16[256,4096]{1,0:T(8,128)(2,1)S(1)}) fusion(bf16[256,16384]{1,0:T(8,128)(2,1)} %param.3), kind=kLoop, calls=%fused_computation.9 | loop fusion | bytes 16777216 | tf_op jit(solution)/shard_map/slice | solution.py:131
  13.3 1.4 %collective-permute-start.7 = (bf16[32,4096]{1,0:T(8,128)(2,1)S(1)}, bf16[32,4096]{1,0:T(8,128)(2,1)S(1)}, u32[]{:S(2)}, u32[]{:S(2)}) collective-permute-start(bf16[32,4096]{1,0:T(8,128)(2,1)S(1)} %slice_select_fusion.1), channel_id=1, source_target_pairs={{0,4},{4,8},{8,12},{12,0},{1,5},{5,9},{9,13},{13,1},{2,6},{6,10},{... | collective-permute-start | bytes 786440 | tf_op jit(solution)/shard_map/ppermute | solution.py:98
  14.7 1.5 %collective-permute-start.4 = (bf16[32,4096]{1,0:T(8,128)(2,1)S(1)}, bf16[32,4096]{1,0:T(8,128)(2,1)S(1)}, u32[]{:S(2)}, u32[]{:S(2)}) collective-permute-start(bf16[32,4096]{1,0:T(8,128)(2,1)S(1)} %collective-permute-done.3.refs_0_), channel_id=1, source_target_pairs={{0,16},{16,0},{1,17},{17,1},{2,18},{18,2},{3,19},{19,3},{4,20},{20... | collective-permute-start | bytes 786440 | tf_op jit(solution)/shard_map/ppermute | solution.py:104
  16.2 2.7 %shard_map.37.refs_4_ = f32[64,256]{1,0:T(8,128)S(1)} custom-call(bf16[64,16384]{1,0:T(8,128)(2,1)S(1)} %copy-done.6, f32[1,16384]{1,0:T(1,128)S(1)} %bitcast.10, bf16[256,4096]{1,0:T(8,128)(2,1)S(1)} %get-tuple-element.53.refs_0_.refs_3_, bf16[256,4096]{1,0:T(8,128)(2,1)S(1)} %get-tuple-element.52.refs_1_.refs_3_, ...), custom_call_target="tpu_custom_call" | custom-call | flops 536870912 | bytes 10485760 | tf_op jit(solution)/shard_map/pallas_call | solution.py:67
  18.9 1.8 %collective-permute-start.2 = (bf16[32,4096]{1,0:T(8,128)(2,1)S(1)}, bf16[32,4096]{1,0:T(8,128)(2,1)S(1)}, u32[]{:S(2)}, u32[]{:S(2)}) collective-permute-start(bf16[32,4096]{1,0:T(8,128)(2,1)S(1)} %collective-permute-done.refs_0_), channel_id=1, source_target_pairs={{0,16},{16,0},{1,17},{17,1},{2,18},{18,2},{3,19},{19,3},{4,20},{20... | collective-permute-start | bytes 786440 | tf_op jit(solution)/shard_map/ppermute | solution.py:104
  20.7 3.8 %collective-permute-done.7.refs_0_ = bf16[32,4096]{1,0:T(8,128)(2,1)S(1)} collective-permute-done((bf16[32,4096]{1,0:T(8,128)(2,1)S(1)}, bf16[32,4096]{1,0:T(8,128)(2,1)S(1)}, u32[]{:S(2)}, u32[]{:S(2)}) %collective-permute-start.7) | collective-permute-done | bytes 262176 | tf_op jit(solution)/shard_map/ppermute | solution.py:98
  24.5 1.8 %collective-permute-start.8 = (bf16[32,4096]{1,0:T(8,128)(2,1)S(1)}, bf16[32,4096]{1,0:T(8,128)(2,1)S(1)}, u32[]{:S(2)}, u32[]{:S(2)}) collective-permute-start(bf16[32,4096]{1,0:T(8,128)(2,1)S(1)} %collective-permute-done.7.refs_0_), channel_id=1, source_target_pairs={{0,16},{16,0},{1,17},{17,1},{2,18},{18,2},{3,19},{19,3},{4,20},{20... | collective-permute-start | bytes 786440 | tf_op jit(solution)/shard_map/ppermute | solution.py:104
  27.1 2.0 %collective-permute-done.2.refs_1_ = bf16[32,4096]{1,0:T(8,128)(2,1)S(1)} collective-permute-done((bf16[32,4096]{1,0:T(8,128)(2,1)S(1)}, bf16[32,4096]{1,0:T(8,128)(2,1)S(1)}, u32[]{:S(2)}, u32[]{:S(2)}) %collective-permute-start.2) | collective-permute-done | bytes 262176 | tf_op jit(solution)/shard_map/ppermute | solution.py:104
  30.2 1.9 %collective-permute-start.6 = (bf16[32,4096]{1,0:T(8,128)(2,1)S(1)}, bf16[32,4096]{1,0:T(8,128)(2,1)S(1)}, u32[]{:S(2)}, u32[]{:S(2)}) collective-permute-start(bf16[32,4096]{1,0:T(8,128)(2,1)S(1)} %collective-permute-done.1.refs_0_), channel_id=1, source_target_pairs={{0,16},{16,0},{1,17},{17,1},{2,18},{18,2},{3,19},{19,3},{4,20},{20... | collective-permute-start | bytes 786440 | tf_op jit(solution)/shard_map/ppermute | solution.py:104
  32.8 1.9 %collective-permute-done.8.refs_1_ = bf16[32,4096]{1,0:T(8,128)(2,1)S(1)} collective-permute-done((bf16[32,4096]{1,0:T(8,128)(2,1)S(1)}, bf16[32,4096]{1,0:T(8,128)(2,1)S(1)}, u32[]{:S(2)}, u32[]{:S(2)}) %collective-permute-start.8) | collective-permute-done | bytes 262176 | tf_op jit(solution)/shard_map/ppermute | solution.py:104
  34.7 2.6 %collective-permute-done.11.refs_0_ = bf16[32,4096]{1,0:T(8,128)(2,1)S(1)} collective-permute-done((bf16[32,4096]{1,0:T(8,128)(2,1)S(1)}, bf16[32,4096]{1,0:T(8,128)(2,1)S(1)}, u32[]{:S(2)}, u32[]{:S(2)}) %collective-permute-start.11) | collective-permute-done | bytes 262176 | tf_op jit(solution)/shard_map/ppermute | solution.py:98
  37.7 3.9 %collective-permute-done.5.refs_0_ = bf16[32,4096]{1,0:T(8,128)(2,1)S(1)} collective-permute-done((bf16[32,4096]{1,0:T(8,128)(2,1)S(1)}, bf16[32,4096]{1,0:T(8,128)(2,1)S(1)}, u32[]{:S(2)}, u32[]{:S(2)}) %collective-permute-start.5) | collective-permute-done | bytes 262176 | tf_op jit(solution)/shard_map/ppermute | solution.py:98
  42.4 1.8 %collective-permute-start.10 = (bf16[32,4096]{1,0:T(8,128)(2,1)S(1)}, bf16[32,4096]{1,0:T(8,128)(2,1)S(1)}, u32[]{:S(2)}, u32[]{:S(2)}) collective-permute-start(bf16[32,4096]{1,0:T(8,128)(2,1)S(1)} %collective-permute-done.5.refs_0_), channel_id=1, source_target_pairs={{0,16},{16,0},{1,17},{17,1},{2,18},{18,2},{3,19},{19,3},{4,20},{20... | collective-permute-start | bytes 786440 | tf_op jit(solution)/shard_map/ppermute | solution.py:104
  46.0 2.7 %collective-permute-done.15.refs_0_ = bf16[32,4096]{1,0:T(8,128)(2,1)S(1)} collective-permute-done((bf16[32,4096]{1,0:T(8,128)(2,1)S(1)}, bf16[32,4096]{1,0:T(8,128)(2,1)S(1)}, u32[]{:S(2)}, u32[]{:S(2)}) %collective-permute-start.15) | collective-permute-done | bytes 262176 | tf_op jit(solution)/shard_map/ppermute | solution.py:98
  49.9 4.4 %collective-permute-done.9.refs_0_ = bf16[32,4096]{1,0:T(8,128)(2,1)S(1)} collective-permute-done((bf16[32,4096]{1,0:T(8,128)(2,1)S(1)}, bf16[32,4096]{1,0:T(8,128)(2,1)S(1)}, u32[]{:S(2)}, u32[]{:S(2)}) %collective-permute-start.9) | collective-permute-done | bytes 262176 | tf_op jit(solution)/shard_map/ppermute | solution.py:98
  55.9 2.0 %collective-permute-done.16.refs_1_ = bf16[32,4096]{1,0:T(8,128)(2,1)S(1)} collective-permute-done((bf16[32,4096]{1,0:T(8,128)(2,1)S(1)}, bf16[32,4096]{1,0:T(8,128)(2,1)S(1)}, u32[]{:S(2)}, u32[]{:S(2)}) %collective-permute-start.16) | collective-permute-done | bytes 262176 | tf_op jit(solution)/shard_map/ppermute | solution.py:104
  58.0 2.2 %collective-permute-done.20.refs_0_ = bf16[32,4096]{1,0:T(8,128)(2,1)S(1)} collective-permute-done((bf16[32,4096]{1,0:T(8,128)(2,1)S(1)}, bf16[32,4096]{1,0:T(8,128)(2,1)S(1)}, u32[]{:S(2)}, u32[]{:S(2)}) %collective-permute-start.20) | collective-permute-done | bytes 262176 | tf_op jit(solution)/shard_map/ppermute | solution.py:98
  60.2 1.6 %collective-permute-start.22 = (bf16[32,4096]{1,0:T(8,128)(2,1)S(1)}, bf16[32,4096]{1,0:T(8,128)(2,1)S(1)}, u32[]{:S(2)}, u32[]{:S(2)}) collective-permute-start(bf16[32,4096]{1,0:T(8,128)(2,1)S(1)} %collective-permute-done.20.refs_0_), channel_id=1, source_target_pairs={{0,16},{16,0},{1,17},{17,1},{2,18},{18,2},{3,19},{19,3},{4,20},{20... | collective-permute-start | bytes 786440 | tf_op jit(solution)/shard_map/ppermute | solution.py:104
  61.8 4.0 %collective-permute-done.13.refs_0_ = bf16[32,4096]{1,0:T(8,128)(2,1)S(1)} collective-permute-done((bf16[32,4096]{1,0:T(8,128)(2,1)S(1)}, bf16[32,4096]{1,0:T(8,128)(2,1)S(1)}, u32[]{:S(2)}, u32[]{:S(2)}) %collective-permute-start.13) | collective-permute-done | bytes 262176 | tf_op jit(solution)/shard_map/ppermute | solution.py:98
  66.7 1.7 %collective-permute-start.18 = (bf16[32,4096]{1,0:T(8,128)(2,1)S(1)}, bf16[32,4096]{1,0:T(8,128)(2,1)S(1)}, u32[]{:S(2)}, u32[]{:S(2)}) collective-permute-start(bf16[32,4096]{1,0:T(8,128)(2,1)S(1)} %collective-permute-done.13.refs_0_), channel_id=1, source_target_pairs={{0,16},{16,0},{1,17},{17,1},{2,18},{18,2},{3,19},{19,3},{4,20},{20... | collective-permute-start | bytes 786440 | tf_op jit(solution)/shard_map/ppermute | solution.py:104
  69.7 1.8 %collective-permute-done.21.refs_0_ = bf16[32,4096]{1,0:T(8,128)(2,1)} collective-permute-done((bf16[32,4096]{1,0:T(8,128)(2,1)S(1)}, bf16[32,4096]{1,0:T(8,128)(2,1)}, u32[]{:S(2)}, u32[]{:S(2)}) %collective-permute-start.21) | collective-permute-done | bytes 262176 | tf_op jit(solution)/shard_map/ppermute | solution.py:98
  71.6 1.5 %collective-permute-start.23 = (bf16[32,4096]{1,0:T(8,128)(2,1)}, bf16[32,4096]{1,0:T(8,128)(2,1)}, u32[]{:S(2)}, u32[]{:S(2)}) collective-permute-start(bf16[32,4096]{1,0:T(8,128)(2,1)} %collective-permute-done.21.refs_0_), channel_id=1, source_target_pairs={{0,16},{16,0},{1,17},{17,1},{2,18},{18,2},{3,19},{19,3},{4,20},{20... | collective-permute-start | bytes 786440 | tf_op jit(solution)/shard_map/ppermute | solution.py:104
  73.1 1.7 %collective-permute-done.17.refs_0_ = bf16[32,4096]{1,0:T(8,128)(2,1)S(1)} collective-permute-done((bf16[32,4096]{1,0:T(8,128)(2,1)S(1)}, bf16[32,4096]{1,0:T(8,128)(2,1)S(1)}, u32[]{:S(2)}, u32[]{:S(2)}) %collective-permute-start.17) | collective-permute-done | bytes 262176 | tf_op jit(solution)/shard_map/ppermute | solution.py:98
  74.8 1.2 %collective-permute-done.18.refs_1_ = bf16[32,4096]{1,0:T(8,128)(2,1)S(1)} collective-permute-done((bf16[32,4096]{1,0:T(8,128)(2,1)S(1)}, bf16[32,4096]{1,0:T(8,128)(2,1)S(1)}, u32[]{:S(2)}, u32[]{:S(2)}) %collective-permute-start.18) | collective-permute-done | bytes 262176 | tf_op jit(solution)/shard_map/ppermute | solution.py:104
  76.7 1.4 %collective-permute-start.19 = (bf16[32,4096]{1,0:T(8,128)(2,1)S(1)}, bf16[32,4096]{1,0:T(8,128)(2,1)S(1)}, u32[]{:S(2)}, u32[]{:S(2)}) collective-permute-start(bf16[32,4096]{1,0:T(8,128)(2,1)S(1)} %collective-permute-done.17.refs_0_), channel_id=1, source_target_pairs={{0,16},{16,0},{1,17},{17,1},{2,18},{18,2},{3,19},{19,3},{4,20},{20... | collective-permute-start | bytes 786440 | tf_op jit(solution)/shard_map/ppermute | solution.py:104
  80.0 1.6 %copy-done.5 = bf16[256,4096]{1,0:T(8,128)(2,1)S(1)} copy-done((bf16[256,4096]{1,0:T(8,128)(2,1)S(1)}, bf16[256,4096]{1,0:T(8,128)(2,1)}, u32[]{:S(2)}) %copy-start.5) | copy-done | bytes 2097176
  84.1 1.8 %shard_map.48.refs_7_ = f32[64,256]{1,0:T(8,128)S(1)} custom-call(bf16[32,4096]{1,0:T(8,128)(2,1)} %collective-permute-done.21.refs_0_, bf16[32,4096]{1,0:T(8,128)(2,1)} %collective-permute-done.23.refs_1_, f32[1,16384]{1,0:T(1,128)S(1)} %bitcast.21, bf16[256,4096]{1,0:T(8,128)(2,1)S(1)} %copy-done.1, f32[64,256]{1,0:T(8,128)S(1)} %shard_map.47.refs_4_), custom_call_target="tpu_custom_call" | custom-call | flops 134217728 | bytes 2621440 | tf_op jit(solution)/shard_map/pallas_call | solution.py:67
  86.8 1.3 %collective-permute-done.24 = f32[2,64,256]{2,1,0:T(8,128)S(1)} collective-permute-done((f32[2,64,256]{2,1,0:T(8,128)S(1)}, f32[2,64,256]{2,1,0:T(8,128)S(1)}, u32[]{:S(2)}, u32[]{:S(2)}) %collective-permute-start.24) | collective-permute-done | bytes 131104 | tf_op jit(solution)/shard_map/ppermute | solution.py:115
  88.2 1.6 %collective-permute-start.25 = (f32[1,64,256]{2,1,0:T(8,128)S(1)}, f32[1,64,256]{2,1,0:T(8,128)S(1)}, u32[]{:S(2)}, u32[]{:S(2)}) collective-permute-start(f32[1,64,256]{2,1,0:T(8,128)S(1)} %constant_dynamic-slice_fusion), channel_id=1, source_target_pairs={{0,2},{1,3},{2,0},{3,1},{4,6},{5,7},{6,4},{7,5},{8,10},{9,11},{10,... | collective-permute-start | bytes 196616 | tf_op jit(solution)/shard_map/ppermute | solution.py:115
  89.8 2.7 %collective-permute-done.25 = f32[1,64,256]{2,1,0:T(8,128)S(1)} collective-permute-done((f32[1,64,256]{2,1,0:T(8,128)S(1)}, f32[1,64,256]{2,1,0:T(8,128)S(1)}, u32[]{:S(2)}, u32[]{:S(2)}) %collective-permute-start.25) | collective-permute-done | bytes 65568 | tf_op jit(solution)/shard_map/ppermute | solution.py:115
  (79 shorter events, 21.8 us)
Async XLA Ops:
  1.1 12.2 %collective-permute-start.3 = (bf16[32,4096]{1,0:T(8,128)(2,1)S(1)}, bf16[32,4096]{1,0:T(8,128)(2,1)S(1)}, u32[]{:S(2)}, u32[]{:S(2)}) collective-permute-start(bf16[32,4096]{1,0:T(8,128)(2,1)S(1)} %slice_select_fusion.3), channel_id=1, source_target_pairs={{0,4},{4,8},{8,12},{12,0},{1,5},{5,9},{9,13},{13,1},{2,6},{6,10},{... | collective-permute-start | bytes 786440 | tf_op jit(solution)/shard_map/ppermute | solution.py:98
  5.2 13.7 %collective-permute-start = (bf16[32,4096]{1,0:T(8,128)(2,1)S(1)}, bf16[32,4096]{1,0:T(8,128)(2,1)S(1)}, u32[]{:S(2)}, u32[]{:S(2)}) collective-permute-start(bf16[32,4096]{1,0:T(8,128)(2,1)S(1)} %slice_select_fusion.2), channel_id=1, source_target_pairs={{0,4},{4,8},{8,12},{12,0},{1,5},{5,9},{9,13},{13,1},{2,6},{6,10},{... | collective-permute-start | bytes 786440 | tf_op jit(solution)/shard_map/ppermute | solution.py:98
  13.0 36.1 %copy-start.4 = (bf16[256,4096]{1,0:T(8,128)(2,1)}, bf16[256,4096]{1,0:T(8,128)(2,1)S(1)}, u32[]{:S(2)}) copy-start(bf16[256,4096]{1,0:T(8,128)(2,1)S(1)} %get-tuple-element.53.refs_0_.refs_3_) | copy-start | bytes 6291460
  13.0 42.1 %copy-start.2 = (bf16[256,4096]{1,0:T(8,128)(2,1)}, bf16[256,4096]{1,0:T(8,128)(2,1)S(1)}, u32[]{:S(2)}) copy-start(bf16[256,4096]{1,0:T(8,128)(2,1)S(1)} %get-tuple-element.52.refs_1_.refs_3_) | copy-start | bytes 6291460
  13.1 52.8 %copy-start = (bf16[256,4096]{1,0:T(8,128)(2,1)}, bf16[256,4096]{1,0:T(8,128)(2,1)S(1)}, u32[]{:S(2)}) copy-start(bf16[256,4096]{1,0:T(8,128)(2,1)S(1)} %get-tuple-element.54.refs_2_.refs_3_) | copy-start | bytes 6291460
  13.3 11.2 %collective-permute-start.7 = (bf16[32,4096]{1,0:T(8,128)(2,1)S(1)}, bf16[32,4096]{1,0:T(8,128)(2,1)S(1)}, u32[]{:S(2)}, u32[]{:S(2)}) collective-permute-start(bf16[32,4096]{1,0:T(8,128)(2,1)S(1)} %slice_select_fusion.1), channel_id=1, source_target_pairs={{0,4},{4,8},{8,12},{12,0},{1,5},{5,9},{9,13},{13,1},{2,6},{6,10},{... | collective-permute-start | bytes 786440 | tf_op jit(solution)/shard_map/ppermute | solution.py:98
  14.7 9.8 %collective-permute-start.4 = (bf16[32,4096]{1,0:T(8,128)(2,1)S(1)}, bf16[32,4096]{1,0:T(8,128)(2,1)S(1)}, u32[]{:S(2)}, u32[]{:S(2)}) collective-permute-start(bf16[32,4096]{1,0:T(8,128)(2,1)S(1)} %collective-permute-done.3.refs_0_), channel_id=1, source_target_pairs={{0,16},{16,0},{1,17},{17,1},{2,18},{18,2},{3,19},{19,3},{4,20},{20... | collective-permute-start | bytes 786440 | tf_op jit(solution)/shard_map/ppermute | solution.py:104
  18.9 11.3 %copy-start.15 = (f32[64,256]{1,0:T(8,128)}, f32[64,256]{1,0:T(8,128)S(1)}, u32[]{:S(2)}) copy-start(f32[64,256]{1,0:T(8,128)S(1)} %shard_map.37.refs_4_) | copy-start | bytes 196612
  18.9 10.2 %collective-permute-start.2 = (bf16[32,4096]{1,0:T(8,128)(2,1)S(1)}, bf16[32,4096]{1,0:T(8,128)(2,1)S(1)}, u32[]{:S(2)}, u32[]{:S(2)}) collective-permute-start(bf16[32,4096]{1,0:T(8,128)(2,1)S(1)} %collective-permute-done.refs_0_), channel_id=1, source_target_pairs={{0,16},{16,0},{1,17},{17,1},{2,18},{18,2},{3,19},{19,3},{4,20},{20... | collective-permute-start | bytes 786440 | tf_op jit(solution)/shard_map/ppermute | solution.py:104
  20.7 9.5 %collective-permute-start.1 = (bf16[32,4096]{1,0:T(8,128)(2,1)S(1)}, bf16[32,4096]{1,0:T(8,128)(2,1)S(1)}, u32[]{:S(2)}, u32[]{:S(2)}) collective-permute-start(bf16[32,4096]{1,0:T(8,128)(2,1)S(1)} %slice_select_fusion), channel_id=1, source_target_pairs={{0,4},{4,8},{8,12},{12,0},{1,5},{5,9},{9,13},{13,1},{2,6},{6,10},{... | collective-permute-start | bytes 786440 | tf_op jit(solution)/shard_map/ppermute | solution.py:98
  24.5 10.2 %collective-permute-start.8 = (bf16[32,4096]{1,0:T(8,128)(2,1)S(1)}, bf16[32,4096]{1,0:T(8,128)(2,1)S(1)}, u32[]{:S(2)}, u32[]{:S(2)}) collective-permute-start(bf16[32,4096]{1,0:T(8,128)(2,1)S(1)} %collective-permute-done.7.refs_0_), channel_id=1, source_target_pairs={{0,16},{16,0},{1,17},{17,1},{2,18},{18,2},{3,19},{19,3},{4,20},{20... | collective-permute-start | bytes 786440 | tf_op jit(solution)/shard_map/ppermute | solution.py:104
  26.3 11.0 %collective-permute-start.11 = (bf16[32,4096]{1,0:T(8,128)(2,1)S(1)}, bf16[32,4096]{1,0:T(8,128)(2,1)S(1)}, u32[]{:S(2)}, u32[]{:S(2)}) collective-permute-start(bf16[32,4096]{1,0:T(8,128)(2,1)S(1)} %collective-permute-done.3.refs_0_), channel_id=1, source_target_pairs={{0,4},{4,8},{8,12},{12,0},{1,5},{5,9},{9,13},{13,1},{2,6},{6,10},{... | collective-permute-start | bytes 786440 | tf_op jit(solution)/shard_map/ppermute | solution.py:98
  30.2 11.4 %collective-permute-start.5 = (bf16[32,4096]{1,0:T(8,128)(2,1)S(1)}, bf16[32,4096]{1,0:T(8,128)(2,1)S(1)}, u32[]{:S(2)}, u32[]{:S(2)}) collective-permute-start(bf16[32,4096]{1,0:T(8,128)(2,1)S(1)} %collective-permute-done.refs_0_), channel_id=1, source_target_pairs={{0,4},{4,8},{8,12},{12,0},{1,5},{5,9},{9,13},{13,1},{2,6},{6,10},{... | collective-permute-start | bytes 786440 | tf_op jit(solution)/shard_map/ppermute | solution.py:98
  30.2 11.4 %collective-permute-start.6 = (bf16[32,4096]{1,0:T(8,128)(2,1)S(1)}, bf16[32,4096]{1,0:T(8,128)(2,1)S(1)}, u32[]{:S(2)}, u32[]{:S(2)}) collective-permute-start(bf16[32,4096]{1,0:T(8,128)(2,1)S(1)} %collective-permute-done.1.refs_0_), channel_id=1, source_target_pairs={{0,16},{16,0},{1,17},{17,1},{2,18},{18,2},{3,19},{19,3},{4,20},{20... | collective-permute-start | bytes 786440 | tf_op jit(solution)/shard_map/ppermute | solution.py:104
  37.3 8.7 %collective-permute-start.12 = (bf16[32,4096]{1,0:T(8,128)(2,1)S(1)}, bf16[32,4096]{1,0:T(8,128)(2,1)S(1)}, u32[]{:S(2)}, u32[]{:S(2)}) collective-permute-start(bf16[32,4096]{1,0:T(8,128)(2,1)S(1)} %collective-permute-done.11.refs_0_), channel_id=1, source_target_pairs={{0,16},{16,0},{1,17},{17,1},{2,18},{18,2},{3,19},{19,3},{4,20},{20... | collective-permute-start | bytes 786440 | tf_op jit(solution)/shard_map/ppermute | solution.py:104
  37.7 11.0 %collective-permute-start.15 = (bf16[32,4096]{1,0:T(8,128)(2,1)S(1)}, bf16[32,4096]{1,0:T(8,128)(2,1)S(1)}, u32[]{:S(2)}, u32[]{:S(2)}) collective-permute-start(bf16[32,4096]{1,0:T(8,128)(2,1)S(1)} %collective-permute-done.7.refs_0_), channel_id=1, source_target_pairs={{0,4},{4,8},{8,12},{12,0},{1,5},{5,9},{9,13},{13,1},{2,6},{6,10},{... | collective-permute-start | bytes 786440 | tf_op jit(solution)/shard_map/ppermute | solution.py:98
  42.3 12.0 %collective-permute-start.9 = (bf16[32,4096]{1,0:T(8,128)(2,1)S(1)}, bf16[32,4096]{1,0:T(8,128)(2,1)S(1)}, u32[]{:S(2)}, u32[]{:S(2)}) collective-permute-start(bf16[32,4096]{1,0:T(8,128)(2,1)S(1)} %collective-permute-done.1.refs_0_), channel_id=1, source_target_pairs={{0,4},{4,8},{8,12},{12,0},{1,5},{5,9},{9,13},{13,1},{2,6},{6,10},{... | collective-permute-start | bytes 786440 | tf_op jit(solution)/shard_map/ppermute | solution.py:98
  42.4 11.9 %collective-permute-start.10 = (bf16[32,4096]{1,0:T(8,128)(2,1)S(1)}, bf16[32,4096]{1,0:T(8,128)(2,1)S(1)}, u32[]{:S(2)}, u32[]{:S(2)}) collective-permute-start(bf16[32,4096]{1,0:T(8,128)(2,1)S(1)} %collective-permute-done.5.refs_0_), channel_id=1, source_target_pairs={{0,16},{16,0},{1,17},{17,1},{2,18},{18,2},{3,19},{19,3},{4,20},{20... | collective-permute-start | bytes 786440 | tf_op jit(solution)/shard_map/ppermute | solution.py:104
  48.7 9.2 %collective-permute-start.16 = (bf16[32,4096]{1,0:T(8,128)(2,1)S(1)}, bf16[32,4096]{1,0:T(8,128)(2,1)S(1)}, u32[]{:S(2)}, u32[]{:S(2)}) collective-permute-start(bf16[32,4096]{1,0:T(8,128)(2,1)S(1)} %collective-permute-done.15.refs_0_), channel_id=1, source_target_pairs={{0,16},{16,0},{1,17},{17,1},{2,18},{18,2},{3,19},{19,3},{4,20},{20... | collective-permute-start | bytes 786440 | tf_op jit(solution)/shard_map/ppermute | solution.py:104
  49.1 11.0 %collective-permute-start.20 = (bf16[32,4096]{1,0:T(8,128)(2,1)S(1)}, bf16[32,4096]{1,0:T(8,128)(2,1)S(1)}, u32[]{:S(2)}, u32[]{:S(2)}) collective-permute-start(bf16[32,4096]{1,0:T(8,128)(2,1)S(1)} %collective-permute-done.11.refs_0_), channel_id=1, source_target_pairs={{0,4},{4,8},{8,12},{12,0},{1,5},{5,9},{9,13},{13,1},{2,6},{6,10},{... | collective-permute-start | bytes 786440 | tf_op jit(solution)/shard_map/ppermute | solution.py:98
  54.3 11.5 %collective-permute-start.13 = (bf16[32,4096]{1,0:T(8,128)(2,1)S(1)}, bf16[32,4096]{1,0:T(8,128)(2,1)S(1)}, u32[]{:S(2)}, u32[]{:S(2)}) collective-permute-start(bf16[32,4096]{1,0:T(8,128)(2,1)S(1)} %collective-permute-done.5.refs_0_), channel_id=1, source_target_pairs={{0,4},{4,8},{8,12},{12,0},{1,5},{5,9},{9,13},{13,1},{2,6},{6,10},{... | collective-permute-start | bytes 786440 | tf_op jit(solution)/shard_map/ppermute | solution.py:98
  54.3 11.5 %collective-permute-start.14 = (bf16[32,4096]{1,0:T(8,128)(2,1)S(1)}, bf16[32,4096]{1,0:T(8,128)(2,1)S(1)}, u32[]{:S(2)}, u32[]{:S(2)}) collective-permute-start(bf16[32,4096]{1,0:T(8,128)(2,1)S(1)} %collective-permute-done.9.refs_0_), channel_id=1, source_target_pairs={{0,16},{16,0},{1,17},{17,1},{2,18},{18,2},{3,19},{19,3},{4,20},{20... | collective-permute-start | bytes 786440 | tf_op jit(solution)/shard_map/ppermute | solution.py:104
  60.2 8.8 %collective-permute-start.22 = (bf16[32,4096]{1,0:T(8,128)(2,1)S(1)}, bf16[32,4096]{1,0:T(8,128)(2,1)S(1)}, u32[]{:S(2)}, u32[]{:S(2)}) collective-permute-start(bf16[32,4096]{1,0:T(8,128)(2,1)S(1)} %collective-permute-done.20.refs_0_), channel_id=1, source_target_pairs={{0,16},{16,0},{1,17},{17,1},{2,18},{18,2},{3,19},{19,3},{4,20},{20... | collective-permute-start | bytes 786440 | tf_op jit(solution)/shard_map/ppermute | solution.py:104
  61.8 9.8 %collective-permute-start.21 = (bf16[32,4096]{1,0:T(8,128)(2,1)S(1)}, bf16[32,4096]{1,0:T(8,128)(2,1)}, u32[]{:S(2)}, u32[]{:S(2)}) collective-permute-start(bf16[32,4096]{1,0:T(8,128)(2,1)S(1)} %collective-permute-done.15.refs_0_), channel_id=1, source_target_pairs={{0,4},{4,8},{8,12},{12,0},{1,5},{5,9},{9,13},{13,1},{2,6},{6,10},{... | collective-permute-start | bytes 786440 | tf_op jit(solution)/shard_map/ppermute | solution.py:98
  65.8 9.0 %copy-start.7 = (bf16[32,4096]{1,0:T(8,128)(2,1)}, bf16[32,4096]{1,0:T(8,128)(2,1)S(1)}, u32[]{:S(2)}) copy-start(bf16[32,4096]{1,0:T(8,128)(2,1)S(1)} %collective-permute-done.13.refs_0_) | copy-start | bytes 786436
  65.8 10.2 %copy-start.9 = (bf16[32,4096]{1,0:T(8,128)(2,1)}, bf16[32,4096]{1,0:T(8,128)(2,1)S(1)}, u32[]{:S(2)}) copy-start(bf16[32,4096]{1,0:T(8,128)(2,1)S(1)} %collective-permute-done.14.refs_1_) | copy-start | bytes 786436
  66.6 8.2 %collective-permute-start.17 = (bf16[32,4096]{1,0:T(8,128)(2,1)S(1)}, bf16[32,4096]{1,0:T(8,128)(2,1)S(1)}, u32[]{:S(2)}, u32[]{:S(2)}) collective-permute-start(bf16[32,4096]{1,0:T(8,128)(2,1)S(1)} %collective-permute-done.9.refs_0_), channel_id=1, source_target_pairs={{0,4},{4,8},{8,12},{12,0},{1,5},{5,9},{9,13},{13,1},{2,6},{6,10},{... | collective-permute-start | bytes 786440 | tf_op jit(solution)/shard_map/ppermute | solution.py:98
  66.7 9.3 %collective-permute-start.18 = (bf16[32,4096]{1,0:T(8,128)(2,1)S(1)}, bf16[32,4096]{1,0:T(8,128)(2,1)S(1)}, u32[]{:S(2)}, u32[]{:S(2)}) collective-permute-start(bf16[32,4096]{1,0:T(8,128)(2,1)S(1)} %collective-permute-done.13.refs_0_), channel_id=1, source_target_pairs={{0,16},{16,0},{1,17},{17,1},{2,18},{18,2},{3,19},{19,3},{4,20},{20... | collective-permute-start | bytes 786440 | tf_op jit(solution)/shard_map/ppermute | solution.py:104
  71.6 11.7 %collective-permute-start.23 = (bf16[32,4096]{1,0:T(8,128)(2,1)}, bf16[32,4096]{1,0:T(8,128)(2,1)}, u32[]{:S(2)}, u32[]{:S(2)}) collective-permute-start(bf16[32,4096]{1,0:T(8,128)(2,1)} %collective-permute-done.21.refs_0_), channel_id=1, source_target_pairs={{0,16},{16,0},{1,17},{17,1},{2,18},{18,2},{3,19},{19,3},{4,20},{20... | collective-permute-start | bytes 786440 | tf_op jit(solution)/shard_map/ppermute | solution.py:104
  76.7 9.2 %collective-permute-start.19 = (bf16[32,4096]{1,0:T(8,128)(2,1)S(1)}, bf16[32,4096]{1,0:T(8,128)(2,1)S(1)}, u32[]{:S(2)}, u32[]{:S(2)}) collective-permute-start(bf16[32,4096]{1,0:T(8,128)(2,1)S(1)} %collective-permute-done.17.refs_0_), channel_id=1, source_target_pairs={{0,16},{16,0},{1,17},{17,1},{2,18},{18,2},{3,19},{19,3},{4,20},{20... | collective-permute-start | bytes 786440 | tf_op jit(solution)/shard_map/ppermute | solution.py:104
  86.7 1.4 %collective-permute-start.24 = (f32[2,64,256]{2,1,0:T(8,128)S(1)}, f32[2,64,256]{2,1,0:T(8,128)S(1)}, u32[]{:S(2)}, u32[]{:S(2)}) collective-permute-start(f32[2,64,256]{2,1,0:T(8,128)S(1)} %dynamic-slice_bitcast_fusion), channel_id=1, source_target_pairs={{0,1},{1,0},{2,3},{3,2},{4,5},{5,4},{6,7},{7,6},{8,9},{9,8},{10,11... | collective-permute-start | bytes 393224 | tf_op jit(solution)/shard_map/ppermute | solution.py:115
  88.2 4.3 %collective-permute-start.25 = (f32[1,64,256]{2,1,0:T(8,128)S(1)}, f32[1,64,256]{2,1,0:T(8,128)S(1)}, u32[]{:S(2)}, u32[]{:S(2)}) collective-permute-start(f32[1,64,256]{2,1,0:T(8,128)S(1)} %constant_dynamic-slice_fusion), channel_id=1, source_target_pairs={{0,2},{1,3},{2,0},{3,1},{4,6},{5,7},{6,4},{7,5},{8,10},{9,11},{10,... | collective-permute-start | bytes 196616 | tf_op jit(solution)/shard_map/ppermute | solution.py:115
  (12 other events, 28.0 us)

commit v15 on v13

v15 whole, which is shorter than its diff:
```python
import functools

import jax
import jax.numpy as jnp
from jax import lax
from jax.experimental import pallas as pl
from jax.experimental.pallas import tpu as pltpu
from jax.sharding import PartitionSpec as P

CONTRACT = (((1,), (1,)), ((), ()))
LANES = 128
CHUNKS, SHARE = 4, 15 / 64


def product(rows, scale, train, unit, width, skip=0):
    total = None
    for at in range(0, width, unit):
        here = slice(at, min(at + unit, width))
        precond = (rows(here).astype(jnp.float32) * scale(here)).astype(jnp.bfloat16)
        there = train[:, skip + here.start : skip + here.stop]
        part = lax.dot_general(precond, there, CONTRACT, preferred_element_type=jnp.float32)
        total = part if total is None else total + part
    return total


def own_kernel(starts, unit, test, scale, *refs):
    trains, out = refs[:-1], refs[-1]
    total = None
    for start, train in zip(starts, trains):
        column = lambda here: slice(start + here.start, start + here.stop)
        rows, scales = (lambda here, a=a: a[:, column(here)] for a in (test, scale))
        part = product(rows, scales, train, unit, train.shape[1])
        total = part if total is None else total + part
    out[...] = total


def arrived_rows(parts):
    return lambda here: jnp.concatenate([p[:, here] for p in parts], axis=0)


def part_kernel(start, unit, n_parts, has_base, *refs):
    parts, (scale, train) = refs[:n_parts], refs[n_parts : n_parts + 2]
    column = lambda here: scale[:, start + here.start : start + here.stop]
    total = product(arrived_rows(parts), column, train, unit, parts[0].shape[1])
    refs[-1][...] = total + refs[n_parts + 2][...] if has_base else total


def last_kernel(n_grp, n_ex, starts, unit, n_parts, *refs):
    parts, (scale, train), refs = refs[:n_parts], refs[n_parts : n_parts + 2], refs[n_parts + 2 :]
    wholes, sums, (out, kept) = refs[: n_ex - 1], refs[n_ex - 1 : -2], refs[-2:]
    width, left = parts[0].shape[1], wholes[0].shape[1]
    columns = lambda start: lambda here: scale[:, start + here.start : start + here.stop]
    total = product(arrived_rows(parts), columns(starts[0]), train, unit, width)
    queries = total.shape[0]
    half = queries // n_grp
    for t, value in enumerate(sums):
        value = value[...]
        if t > 0:
            rows = arrived_rows(wholes[t - 1 : t])
            value += product(rows, columns(starts[1]), train, unit, left, width)
        if t == n_ex - 1:
            value += total
        kept[t * queries : (t + 1) * queries, :] = value
    ex, grp = lax.axis_index("ex"), lax.axis_index("grp")
    for b in range(n_ex):
        t = lax.rem(ex + (n_ex - b), n_ex)
        for h in range(n_grp):
            place = jnp.where(t == 0, h, lax.rem(h + n_grp - grp, n_grp))
            at = pl.multiple_of(t * queries + place * half, half)
            to = b * queries + h * half
            out[to : to + half, :] = kept[pl.ds(at, half), :]


def call(kernel, rows, docs, width, operands, scratch=()):
    return pl.pallas_call(
        kernel,
        out_shape=jax.ShapeDtypeStruct((rows, docs), jnp.float32),
        in_specs=[pl.BlockSpec(memory_space=pltpu.VMEM)] * len(operands),
        out_specs=pl.BlockSpec(memory_space=pltpu.VMEM),
        scratch_shapes=scratch,
        cost_estimate=pl.CostEstimate(
            flops=2 * rows * docs * width, bytes_accessed=2 * (rows + docs) * width, transcendentals=0
        ),
        compiler_params=pltpu.CompilerParams(vmem_limit_bytes=16 * 1024 * 1024),
    )(*operands)


def solution(mesh):
    n_grp, n_ex, n_feat = (mesh.shape[a] for a in ("grp", "ex", "feat"))
    assert n_grp <= 2

    def on_device(train, test, hess):
        docs, feats = train.shape
        queries = test.shape[0]
        half = queries // n_grp
        unit = 8 * LANES
        width = int(feats * SHARE) // LANES * LANES
        grp, feat = lax.axis_index("grp"), lax.axis_index("feat")
        ring = [(i, (i + 1) % n_ex) for i in range(n_ex)]
        hops, swaps, made, first = [], [], [], []

        def after(block, *waits):
            return lax.optimization_barrier((block, waits))[0] if waits else block

        def hop(block, *ahead):
            waits = hops[-2:-1] + swaps[-4:-3] + made[-5:-4] + (first if len(hops) == 3 else [])
            hops.append(lax.ppermute(after(block, *waits, *ahead), "ex", ring))
            return hops[-1]

        def swap(block):
            if n_grp == 1:
                return [block]
            swaps.append(lax.ppermute(after(block, *swaps[-2:-1]), "grp", [(0, 1), (1, 0)]))
            return [block, swaps[-1]]

        def sum_over_feat(sums):
            held = sums.reshape(n_feat, -1, docs)
            bit = 1
            while bit < n_feat:
                pairs = held.reshape((-1, 2) + held.shape[1:])
                mine = (feat // bit) % 2
                keep = lax.dynamic_index_in_dim(pairs, mine, 1, keepdims=False)
                away = lax.dynamic_index_in_dim(pairs, 1 - mine, 1, keepdims=False)
                held = keep + lax.ppermute(away, "feat", [(i, i ^ bit) for i in range(n_feat)])
                bit *= 2
            return held[0]

        def share(rows, columns, other=0):
            if n_grp == 1:
                return rows[:, columns]
            return jnp.where(grp == other, rows[:half, columns], rows[half:, columns])

        scale = (1.0 / (hess + jnp.float32(0.1))).reshape(1, feats)
        starts = [c * width for c in range(CHUNKS)]
        rest = CHUNKS * width
        held = []
        for start in starts:
            held.append(share(after(test, *held[-1:]), slice(start, start + width)))
        late = after(test, *held[-1:])
        sides = [share(late, slice(rest, feats), other) for other in range(n_grp)]
        whole = [jnp.concatenate(sides, axis=0)]
        cuts = [*starts, feats]
        trains = [train[:, a:b] for a, b in zip(cuts[:-1], cuts[1:])]
        own = call(
            functools.partial(own_kernel, starts, unit), queries, docs, feats, [test, scale, *trains]
        )
        first.append(own)
        final = n_ex - 1
        sums = [own] + [None] * final
        def whole_hop(gate):
            whole.append(lax.ppermute(after(whole[-1], hops[gate]), "ex", ring))

        for t in range(1, n_ex):
            for c, start in enumerate(starts):
                held[c] = hop(held[c], *(whole[-1:] if t > 2 and c == 1 else []))
                if 1 < t < final and c == 1:
                    whole_hop(-2)
                parts = swap(held[c])
                operands = [*parts, scale, trains[c]]
                if (t, c) == (final, CHUNKS - 1):
                    continue
                base = [] if sums[t] is None else [sums[t]]
                sums[t] = call(
                    functools.partial(part_kernel, start, unit, len(parts), len(base)),
                    queries, docs, width, operands + base,
                )
                made.append(sums[t])
        while len(whole) < n_ex:
            whole_hop(-2)
        total = call(
            functools.partial(last_kernel, n_grp, n_ex, [starts[-1], rest], unit, len(operands) - 2),
            n_ex * queries, docs, feats - starts[-1], [*operands, *whole[1:], *sums],
            [pltpu.VMEM((n_ex * queries, docs), jnp.float32)],
        )
        return sum_over_feat(total).T

    return jax.shard_map(
        on_device,
        mesh=mesh,
        in_specs=(P(("grp", "ex"), "feat"), P("ex", "feat"), P("feat")),
        out_specs=P(("grp", "ex"), "feat"),
        check_vma=False,
    )
```

time: 112 us -> 98.4 us (0.88)
  waiting for transfers between devices: 43 us -> 24.8 us
  starting transfers between devices: 28.8 us -> 34.8 us
  local copies, waits for them, and re-layouts: 17.1 us -> 13.6 us
  other arithmetic: 4.76 us -> 6.07 us
    ppermute x15, waiting for transfers between devices: 29.2 us -> 18.2 us  [the longest x12 14.3 us: hop(): hops.append(lax.ppermute(after(block, *waits, *ahead), 'ex', ring))]
    ppermute x12, waiting for transfers between devices: 9.16 us -> 2.49 us  [swap(): lax.ppermute(after(block, *swaps[-2:-1]), 'grp', [(0, 1), (1, 0)])]
    ppermute x12, starting transfers between devices: 15.4 us -> 21.8 us  [swap(): lax.ppermute(after(block, *swaps[-2:-1]), 'grp', [(0, 1), (1, 0)])]
    unnamed x46 -> x44, local copies, waits for them, and re-layouts: 10.7 us -> 6.51 us
    select_n x5, other arithmetic: 4.08 us -> 5.39 us  [share(): return jnp.where(grp == other, rows[:half, columns], rows[half:, columns])]
    slice x3 -> x2, local copies, waits for them, and re-layouts: 6.39 us -> 7.04 us  [on_device(): trains = [train[:, a:b] for a, b in zip(cuts[:-1], cuts[1:])]]
  transfers between devices with their start and end apart: 29 -> 29, of which waited for: 14 -> 15; matrix products, arithmetic and copies ran while one was open for 9% -> 12% of each run, Pallas kernels for 13% -> 16%
where the time goes in v15:
time: 98.4 us; the launch traced here: 97.6 us
  starting transfers between devices  34.8 us (35%)
  waiting for transfers between devices  24.8 us (25%)
  Pallas kernels  18 us (18%)
  local copies, waits for them, and re-layouts  13.6 us (14%)
  other arithmetic  6.07 us (6%)
    ppermute x12, starting transfers between devices, swap(): lax.ppermute(after(block, *swaps[-2:-1]), 'grp', [(0, 1), (1, 0)])  21.8 us
    pallas_call x13, Pallas kernels, call(): pl.pallas_call(kernel, out_shape=jax.ShapeDtypeStruct((rows, docs), jnp.f...  18 us
    ppermute x12, waiting for transfers between devices, hop(): hops.append(lax.ppermute(after(block, *waits, *ahead), 'ex', ring))  14.3 us
    ppermute x12, starting transfers between devices, hop(): hops.append(lax.ppermute(after(block, *waits, *ahead), 'ex', ring))  9.21 us
    slice x2, local copies, waits for them, and re-layouts, on_device(): trains = [train[:, a:b] for a, b in zip(cuts[:-1], cuts[1:])]  7.04 us
    unnamed x44, local copies, waits for them, and re-layouts  6.51 us
    select_n x5, other arithmetic, share(): return jnp.where(grp == other, rows[:half, columns], rows[half:, columns])  5.39 us
    ppermute x2, waiting for transfers between devices, sum_over_feat(): lax.ppermute(away, 'feat', [(i, i ^ bit) for i in range(n_feat)])  4.08 us
  transfers between devices with their start and end apart: 29, of which 15 were waited for; matrix products, arithmetic and copies ran while one was open for 12% of the time, Pallas kernels for 16%

profile of v15, /device:TPU:0, one launch (start us, length us, event | category | flops | bytes accessed | tf_op | source)
XLA Modules:
  0.0 97.6 jit_solution(9800767733747068135)
XLA Ops:
  1.1 3.1 %collective-permute-start.3 = (bf16[32,3840]{1,0:T(8,128)(2,1)S(1)}, bf16[32,3840]{1,0:T(8,128)(2,1)S(1)}, u32[]{:S(2)}, u32[]{:S(2)}) collective-permute-start(bf16[32,3840]{1,0:T(8,128)(2,1)S(1)} %slice_select_fusion.3), channel_id=1, source_target_pairs={{0,4},{4,8},{8,12},{12,0},{1,5},{5,9},{9,13},{13,1},{2,6},{6,10},{... | collective-permute-start | bytes 737288 | tf_op jit(solution)/shard_map/ppermute | solution.py:107
  5.3 1.6 %collective-permute-start = (bf16[32,3840]{1,0:T(8,128)(2,1)S(1)}, bf16[32,3840]{1,0:T(8,128)(2,1)}, u32[]{:S(2)}, u32[]{:S(2)}) collective-permute-start(bf16[32,3840]{1,0:T(8,128)(2,1)S(1)} %slice_select_fusion.2), channel_id=1, source_target_pairs={{0,4},{4,8},{8,12},{12,0},{1,5},{5,9},{9,13},{13,1},{2,6},{6,10},{... | collective-permute-start | bytes 737288 | tf_op jit(solution)/shard_map/ppermute | solution.py:107
  9.1 3.1 %fusion = (bf16[256,3840]{1,0:T(8,128)(2,1)S(1)}, bf16[256,3840]{1,0:T(8,128)(2,1)S(1)}, bf16[256,3840]{1,0:T(8,128)(2,1)S(1)}) fusion(bf16[256,16384]{1,0:T(8,128)(2,1)} %param.3), kind=kLoop, calls=%fused_computation.12 | loop fusion | bytes 11796480 | tf_op jit(solution)/shard_map/slice | solution.py:143
  12.3 3.9 %slice.55.refs_3_ = bf16[256,4864]{1,0:T(8,128)(2,1)S(1)} slice(bf16[256,16384]{1,0:T(8,128)(2,1)} %param.3), slice={[0:256], [11520:16384]} | slice | bytes 4980736 | tf_op jit(solution)/shard_map/slice | solution.py:143
  16.2 1.6 %collective-permute-start.7 = (bf16[32,3840]{1,0:T(8,128)(2,1)S(1)}, bf16[32,3840]{1,0:T(8,128)(2,1)}, u32[]{:S(2)}, u32[]{:S(2)}) collective-permute-start(bf16[32,3840]{1,0:T(8,128)(2,1)S(1)} %slice_select_fusion.1), channel_id=1, source_target_pairs={{0,4},{4,8},{8,12},{12,0},{1,5},{5,9},{9,13},{13,1},{2,6},{6,10},{... | collective-permute-start | bytes 737288 | tf_op jit(solution)/shard_map/ppermute | solution.py:107
  19.4 2.6 %shard_map.37.refs_7_ = f32[64,256]{1,0:T(8,128)S(1)} custom-call(bf16[64,16384]{1,0:T(8,128)(2,1)S(1)} %copy-done.10, f32[1,16384]{1,0:T(1,128)S(1)} %bitcast.10, bf16[256,3840]{1,0:T(8,128)(2,1)S(1)} %get-tuple-element.61.refs_0_.refs_3_, bf16[256,3840]{1,0:T(8,128)(2,1)S(1)} %get-tuple-element.60.refs_1_.refs_3_, ...), custom_call_target="tpu_custom_call" | custom-call | flops 536870912 | bytes 10485760 | tf_op jit(solution)/shard_map/pallas_call | solution.py:75
  22.7 2.6 %collective-permute-done.7.refs_0_ = bf16[32,3840]{1,0:T(8,128)(2,1)} collective-permute-done((bf16[32,3840]{1,0:T(8,128)(2,1)S(1)}, bf16[32,3840]{1,0:T(8,128)(2,1)}, u32[]{:S(2)}, u32[]{:S(2)}) %collective-permute-start.7) | collective-permute-done | bytes 245792 | tf_op jit(solution)/shard_map/ppermute | solution.py:107
  25.8 2.5 %collective-permute-start.8 = (bf16[32,3840]{1,0:T(8,128)(2,1)}, bf16[32,3840]{1,0:T(8,128)(2,1)}, u32[]{:S(2)}, u32[]{:S(2)}) collective-permute-start(bf16[32,3840]{1,0:T(8,128)(2,1)} %collective-permute-done.7.refs_0_), channel_id=1, source_target_pairs={{0,16},{16,0},{1,17},{17,1},{2,18},{18,2},{3,19},{19,3},{4,20},{20... | collective-permute-start | bytes 737288 | tf_op jit(solution)/shard_map/ppermute | solution.py:113
  29.2 2.0 %collective-permute-done.2.refs_1_ = bf16[32,3840]{1,0:T(8,128)(2,1)S(1)} collective-permute-done((bf16[32,3840]{1,0:T(8,128)(2,1)}, bf16[32,3840]{1,0:T(8,128)(2,1)S(1)}, u32[]{:S(2)}, u32[]{:S(2)}) %collective-permute-start.2) | collective-permute-done | bytes 245792 | tf_op jit(solution)/shard_map/ppermute | solution.py:113
  32.2 2.6 %collective-permute-start.6 = (bf16[32,3840]{1,0:T(8,128)(2,1)}, bf16[32,3840]{1,0:T(8,128)(2,1)S(1)}, u32[]{:S(2)}, u32[]{:S(2)}) collective-permute-start(bf16[32,3840]{1,0:T(8,128)(2,1)} %collective-permute-done.1.refs_0_), channel_id=1, source_target_pairs={{0,16},{16,0},{1,17},{17,1},{2,18},{18,2},{3,19},{19,3},{4,20},{20... | collective-permute-start | bytes 737288 | tf_op jit(solution)/shard_map/ppermute | solution.py:113
  35.8 1.5 %copy-done.4 = bf16[256,3840]{1,0:T(8,128)(2,1)S(1)} copy-done((bf16[256,3840]{1,0:T(8,128)(2,1)S(1)}, bf16[256,3840]{1,0:T(8,128)(2,1)}, u32[]{:S(2)}) %copy-start.4) | copy-done | bytes 1966104
  38.3 1.7 %shard_map.39.refs_4_ = f32[64,256]{1,0:T(8,128)S(1)} custom-call(bf16[32,3840]{1,0:T(8,128)(2,1)} %collective-permute-done.refs_0_, bf16[32,3840]{1,0:T(8,128)(2,1)S(1)} %copy-done.18, f32[1,16384]{1,0:T(1,128)S(1)} %bitcast.12, bf16[256,3840]{1,0:T(8,128)(2,1)S(1)} %copy-done.4, f32[64,256]{1,0:T(8,128)S(1)} %shard_map.38.refs_4_), custom_call_target="tpu_custom_call" | custom-call | flops 125829120 | bytes 2457600 | tf_op jit(solution)/shard_map/pallas_call | solution.py:75
  41.9 1.8 %shard_map.40.refs_4_ = f32[64,256]{1,0:T(8,128)S(1)} custom-call(bf16[32,3840]{1,0:T(8,128)(2,1)} %collective-permute-done.7.refs_0_, bf16[32,3840]{1,0:T(8,128)(2,1)} %collective-permute-done.8.refs_1_, f32[1,16384]{1,0:T(1,128)S(1)} %bitcast.13, bf16[256,3840]{1,0:T(8,128)(2,1)S(1)} %copy-done.1, f32[64,256]{1,0:T(8,128)S(1)} %shard_map.39.refs_4_), custom_call_target="tpu_custom_call" | custom-call | flops 125829120 | bytes 2457600 | tf_op jit(solution)/shard_map/pallas_call | solution.py:75
  44.9 2.0 %collective-permute-start.10 = (bf16[32,3840]{1,0:T(8,128)(2,1)}, bf16[32,3840]{1,0:T(8,128)(2,1)S(1)}, u32[]{:S(2)}, u32[]{:S(2)}) collective-permute-start(bf16[32,3840]{1,0:T(8,128)(2,1)} %collective-permute-done.5.refs_0_), channel_id=1, source_target_pairs={{0,16},{16,0},{1,17},{17,1},{2,18},{18,2},{3,19},{19,3},{4,20},{20... | collective-permute-start | bytes 737288 | tf_op jit(solution)/shard_map/ppermute | solution.py:113
  46.8 2.1 %collective-permute-start.13 = (bf16[64,1024]{1,0:T(8,128)(2,1)S(1)}, bf16[64,1024]{1,0:T(8,128)(2,1)S(1)}, u32[]{:S(2)}, u32[]{:S(2)}) collective-permute-start(bf16[64,1024]{1,0:T(8,128)(2,1)S(1)} %pad_maximum_fusion), channel_id=1, source_target_pairs={{0,4},{4,8},{8,12},{12,0},{1,5},{5,9},{9,13},{13,1},{2,6},{6,10},{... | collective-permute-start | bytes 393224 | tf_op jit(solution)/shard_map/ppermute | solution.py:151
  49.0 1.7 %shard_map.44.refs_8_ = f32[64,256]{1,0:T(8,128)S(1)} custom-call(bf16[32,3840]{1,0:T(8,128)(2,1)} %collective-permute-done.1.refs_0_, bf16[32,3840]{1,0:T(8,128)(2,1)S(1)} %collective-permute-done.6.refs_1_, f32[1,16384]{1,0:T(1,128)S(1)} %bitcast.14, bf16[256,4864]{1,0:T(8,128)(2,1)S(1)} %slice.55.refs_3_, f32[64,256]{1,0:T(8,128)S(1)} %shard_map.40.refs_4_), custom_call_target="tpu_custom_call" | custom-call | flops 125829120 | bytes 2457600 | tf_op jit(solution)/shard_map/pallas_call | solution.py:75
  50.7 2.2 %collective-permute-start.17 = (bf16[32,3840]{1,0:T(8,128)(2,1)S(1)}, bf16[32,3840]{1,0:T(8,128)(2,1)S(1)}, u32[]{:S(2)}, u32[]{:S(2)}) collective-permute-start(bf16[32,3840]{1,0:T(8,128)(2,1)S(1)} %collective-permute-done.16.refs_0_), channel_id=1, source_target_pairs={{0,16},{16,0},{1,17},{17,1},{2,18},{18,2},{3,19},{19,3},{4,20},{20... | collective-permute-start | bytes 737288 | tf_op jit(solution)/shard_map/ppermute | solution.py:113
  53.6 2.2 %collective-permute-done.9.refs_0_ = bf16[32,3840]{1,0:T(8,128)(2,1)S(1)} collective-permute-done((bf16[32,3840]{1,0:T(8,128)(2,1)}, bf16[32,3840]{1,0:T(8,128)(2,1)S(1)}, u32[]{:S(2)}, u32[]{:S(2)}) %collective-permute-start.9) | collective-permute-done | bytes 245792 | tf_op jit(solution)/shard_map/ppermute | solution.py:107
  55.8 2.8 %collective-permute-done.13.refs_4_ = bf16[64,1024]{1,0:T(8,128)(2,1)S(1)} collective-permute-done((bf16[64,1024]{1,0:T(8,128)(2,1)S(1)}, bf16[64,1024]{1,0:T(8,128)(2,1)S(1)}, u32[]{:S(2)}, u32[]{:S(2)}) %collective-permute-start.13) | collective-permute-done | bytes 131104 | tf_op jit(solution)/shard_map/ppermute | solution.py:151
  58.6 2.4 %collective-permute-start.15 = (bf16[32,3840]{1,0:T(8,128)(2,1)S(1)}, bf16[32,3840]{1,0:T(8,128)(2,1)S(1)}, u32[]{:S(2)}, u32[]{:S(2)}) collective-permute-start(bf16[32,3840]{1,0:T(8,128)(2,1)S(1)} %collective-permute-done.9.refs_0_), channel_id=1, source_target_pairs={{0,16},{16,0},{1,17},{17,1},{2,18},{18,2},{3,19},{19,3},{4,20},{20... | collective-permute-start | bytes 737288 | tf_op jit(solution)/shard_map/ppermute | solution.py:113
  61.0 1.7 %shard_map.42.refs_4_ = f32[64,256]{1,0:T(8,128)S(1)} custom-call(bf16[32,3840]{1,0:T(8,128)(2,1)} %collective-permute-done.5.refs_0_, bf16[32,3840]{1,0:T(8,128)(2,1)S(1)} %collective-permute-done.10.refs_1_, f32[1,16384]{1,0:T(1,128)S(1)} %bitcast.16, bf16[256,3840]{1,0:T(8,128)(2,1)S(1)} %copy-done.5, f32[64,256]{1,0:T(8,128)S(1)} %shard_map.41.refs_4_), custom_call_target="tpu_custom_call" | custom-call | flops 125829120 | bytes 2457600 | tf_op jit(solution)/shard_map/pallas_call | solution.py:75
  63.9 2.4 %collective-permute-start.25 = (bf16[32,3840]{1,0:T(8,128)(2,1)S(1)}, bf16[32,3840]{1,0:T(8,128)(2,1)S(1)}, u32[]{:S(2)}, u32[]{:S(2)}) collective-permute-start(bf16[32,3840]{1,0:T(8,128)(2,1)S(1)} %collective-permute-done.21.refs_0_), channel_id=1, source_target_pairs={{0,16},{16,0},{1,17},{17,1},{2,18},{18,2},{3,19},{19,3},{4,20},{20... | collective-permute-start | bytes 737288 | tf_op jit(solution)/shard_map/ppermute | solution.py:113
  66.3 3.3 %collective-permute-done.14.refs_0_ = bf16[32,3840]{1,0:T(8,128)(2,1)S(1)} collective-permute-done((bf16[32,3840]{1,0:T(8,128)(2,1)}, bf16[32,3840]{1,0:T(8,128)(2,1)S(1)}, u32[]{:S(2)}, u32[]{:S(2)}) %collective-permute-start.14) | collective-permute-done | bytes 245792 | tf_op jit(solution)/shard_map/ppermute | solution.py:107
  70.3 2.0 %collective-permute-start.19 = (bf16[32,3840]{1,0:T(8,128)(2,1)S(1)}, bf16[32,3840]{1,0:T(8,128)(2,1)S(1)}, u32[]{:S(2)}, u32[]{:S(2)}) collective-permute-start(bf16[32,3840]{1,0:T(8,128)(2,1)S(1)} %collective-permute-done.14.refs_0_), channel_id=1, source_target_pairs={{0,16},{16,0},{1,17},{17,1},{2,18},{18,2},{3,19},{19,3},{4,20},{20... | collective-permute-start | bytes 737288 | tf_op jit(solution)/shard_map/ppermute | solution.py:113
  72.3 2.5 %collective-permute-done.22.refs_0_ = bf16[32,3840]{1,0:T(8,128)(2,1)} collective-permute-done((bf16[32,3840]{1,0:T(8,128)(2,1)S(1)}, bf16[32,3840]{1,0:T(8,128)(2,1)}, u32[]{:S(2)}, u32[]{:S(2)}) %collective-permute-start.22) | collective-permute-done | bytes 245792 | tf_op jit(solution)/shard_map/ppermute | solution.py:107
  74.8 2.3 %collective-permute-start.26 = (bf16[32,3840]{1,0:T(8,128)(2,1)}, bf16[32,3840]{1,0:T(8,128)(2,1)}, u32[]{:S(2)}, u32[]{:S(2)}) collective-permute-start(bf16[32,3840]{1,0:T(8,128)(2,1)} %collective-permute-done.22.refs_0_), channel_id=1, source_target_pairs={{0,16},{16,0},{1,17},{17,1},{2,18},{18,2},{3,19},{19,3},{4,20},{20... | collective-permute-start | bytes 737288 | tf_op jit(solution)/shard_map/ppermute | solution.py:113
  77.1 1.8 %collective-permute-done.18.refs_0_ = bf16[32,3840]{1,0:T(8,128)(2,1)} collective-permute-done((bf16[32,3840]{1,0:T(8,128)(2,1)S(1)}, bf16[32,3840]{1,0:T(8,128)(2,1)}, u32[]{:S(2)}, u32[]{:S(2)}) %collective-permute-start.18) | collective-permute-done | bytes 245792 | tf_op jit(solution)/shard_map/ppermute | solution.py:107
  83.4 1.5 %copy-done.9 = bf16[256,3840]{1,0:T(8,128)(2,1)S(1)} copy-done((bf16[256,3840]{1,0:T(8,128)(2,1)S(1)}, bf16[256,3840]{1,0:T(8,128)(2,1)}, u32[]{:S(2)}) %copy-start.9) | copy-done | bytes 1966104
  86.5 1.8 %shard_map.48.refs_10_ = f32[64,256]{1,0:T(8,128)S(1)} custom-call(bf16[32,3840]{1,0:T(8,128)(2,1)} %collective-permute-done.22.refs_0_, bf16[32,3840]{1,0:T(8,128)(2,1)} %collective-permute-done.26.refs_1_, f32[1,16384]{1,0:T(1,128)S(1)} %bitcast.21, bf16[256,3840]{1,0:T(8,128)(2,1)S(1)} %copy-done.2, f32[64,256]{1,0:T(8,128)S(1)} %shard_map.47.refs_4_), custom_call_target="tpu_custom_call" | custom-call | flops 125829120 | bytes 2457600 | tf_op jit(solution)/shard_map/pallas_call | solution.py:75
  88.8 2.4 %shard_map.49 = f32[256,256]{1,0:T(8,128)S(1)} custom-call(bf16[32,3840]{1,0:T(8,128)(2,1)} %collective-permute-done.18.refs_0_, bf16[32,3840]{1,0:T(8,128)(2,1)} %collective-permute-done.20.refs_1_, f32[1,16384]{1,0:T(1,128)S(1)} %bitcast.22, bf16[256,4864]{1,0:T(8,128)(2,1)S(1)} %slice.55.refs_3_, bf16[64,1024]{1,0:T(8,128)(2,1)S(1)} %copy-done.20, ...), custom_call_target="tpu_custom_call" | custom-call | flops 637534208 | bytes 4980736 | tf_op jit(solution)/shard_map/pallas_call | solution.py:75
  92.7 1.5 %collective-permute-start.28 = (f32[1,64,256]{2,1,0:T(8,128)S(1)}, f32[1,64,256]{2,1,0:T(8,128)S(1)}, u32[]{:S(2)}, u32[]{:S(2)}) collective-permute-start(f32[1,64,256]{2,1,0:T(8,128)S(1)} %constant_dynamic-slice_fusion), channel_id=1, source_target_pairs={{0,2},{1,3},{2,0},{3,1},{4,6},{5,7},{6,4},{7,5},{8,10},{9,11},{10,... | collective-permute-start | bytes 196616 | tf_op jit(solution)/shard_map/ppermute | solution.py:124
  94.2 2.8 %collective-permute-done.28 = f32[1,64,256]{2,1,0:T(8,128)S(1)} collective-permute-done((f32[1,64,256]{2,1,0:T(8,128)S(1)}, f32[1,64,256]{2,1,0:T(8,128)S(1)}, u32[]{:S(2)}, u32[]{:S(2)}) %collective-permute-start.28) | collective-permute-done | bytes 65568 | tf_op jit(solution)/shard_map/ppermute | solution.py:124
  (96 shorter events, 25.1 us)
Async XLA Ops:
  1.1 15.1 %collective-permute-start.3 = (bf16[32,3840]{1,0:T(8,128)(2,1)S(1)}, bf16[32,3840]{1,0:T(8,128)(2,1)S(1)}, u32[]{:S(2)}, u32[]{:S(2)}) collective-permute-start(bf16[32,3840]{1,0:T(8,128)(2,1)S(1)} %slice_select_fusion.3), channel_id=1, source_target_pairs={{0,4},{4,8},{8,12},{12,0},{1,5},{5,9},{9,13},{13,1},{2,6},{6,10},{... | collective-permute-start | bytes 737288 | tf_op jit(solution)/shard_map/ppermute | solution.py:107
  5.3 16.8 %collective-permute-start = (bf16[32,3840]{1,0:T(8,128)(2,1)S(1)}, bf16[32,3840]{1,0:T(8,128)(2,1)}, u32[]{:S(2)}, u32[]{:S(2)}) collective-permute-start(bf16[32,3840]{1,0:T(8,128)(2,1)S(1)} %slice_select_fusion.2), channel_id=1, source_target_pairs={{0,4},{4,8},{8,12},{12,0},{1,5},{5,9},{9,13},{13,1},{2,6},{6,10},{... | collective-permute-start | bytes 737288 | tf_op jit(solution)/shard_map/ppermute | solution.py:107
  12.3 16.2 %copy-start.7 = (bf16[256,3840]{1,0:T(8,128)(2,1)}, bf16[256,3840]{1,0:T(8,128)(2,1)S(1)}, u32[]{:S(2)}) copy-start(bf16[256,3840]{1,0:T(8,128)(2,1)S(1)} %get-tuple-element.61.refs_0_.refs_3_) | copy-start | bytes 5898244
  16.2 9.1 %collective-permute-start.7 = (bf16[32,3840]{1,0:T(8,128)(2,1)S(1)}, bf16[32,3840]{1,0:T(8,128)(2,1)}, u32[]{:S(2)}, u32[]{:S(2)}) collective-permute-start(bf16[32,3840]{1,0:T(8,128)(2,1)S(1)} %slice_select_fusion.1), channel_id=1, source_target_pairs={{0,4},{4,8},{8,12},{12,0},{1,5},{5,9},{9,13},{13,1},{2,6},{6,10},{... | collective-permute-start | bytes 737288 | tf_op jit(solution)/shard_map/ppermute | solution.py:107
  17.9 7.9 %collective-permute-start.4 = (bf16[32,3840]{1,0:T(8,128)(2,1)S(1)}, bf16[32,3840]{1,0:T(8,128)(2,1)S(1)}, u32[]{:S(2)}, u32[]{:S(2)}) collective-permute-start(bf16[32,3840]{1,0:T(8,128)(2,1)S(1)} %collective-permute-done.3.refs_0_), channel_id=1, source_target_pairs={{0,16},{16,0},{1,17},{17,1},{2,18},{18,2},{3,19},{19,3},{4,20},{20... | collective-permute-start | bytes 737288 | tf_op jit(solution)/shard_map/ppermute | solution.py:113
  22.0 9.2 %collective-permute-start.2 = (bf16[32,3840]{1,0:T(8,128)(2,1)}, bf16[32,3840]{1,0:T(8,128)(2,1)S(1)}, u32[]{:S(2)}, u32[]{:S(2)}) collective-permute-start(bf16[32,3840]{1,0:T(8,128)(2,1)} %collective-permute-done.refs_0_), channel_id=1, source_target_pairs={{0,16},{16,0},{1,17},{17,1},{2,18},{18,2},{3,19},{19,3},{4,20},{20... | collective-permute-start | bytes 737288 | tf_op jit(solution)/shard_map/ppermute | solution.py:113
  22.6 9.6 %collective-permute-start.1 = (bf16[32,3840]{1,0:T(8,128)(2,1)S(1)}, bf16[32,3840]{1,0:T(8,128)(2,1)}, u32[]{:S(2)}, u32[]{:S(2)}) collective-permute-start(bf16[32,3840]{1,0:T(8,128)(2,1)S(1)} %slice_select_fusion), channel_id=1, source_target_pairs={{0,4},{4,8},{8,12},{12,0},{1,5},{5,9},{9,13},{13,1},{2,6},{6,10},{... | collective-permute-start | bytes 737288 | tf_op jit(solution)/shard_map/ppermute | solution.py:107
  25.8 14.2 %collective-permute-start.8 = (bf16[32,3840]{1,0:T(8,128)(2,1)}, bf16[32,3840]{1,0:T(8,128)(2,1)}, u32[]{:S(2)}, u32[]{:S(2)}) collective-permute-start(bf16[32,3840]{1,0:T(8,128)(2,1)} %collective-permute-done.7.refs_0_), channel_id=1, source_target_pairs={{0,16},{16,0},{1,17},{17,1},{2,18},{18,2},{3,19},{19,3},{4,20},{20... | collective-permute-start | bytes 737288 | tf_op jit(solution)/shard_map/ppermute | solution.py:113
  28.3 11.7 %collective-permute-start.11 = (bf16[32,3840]{1,0:T(8,128)(2,1)S(1)}, bf16[32,3840]{1,0:T(8,128)(2,1)S(1)}, u32[]{:S(2)}, u32[]{:S(2)}) collective-permute-start(bf16[32,3840]{1,0:T(8,128)(2,1)S(1)} %collective-permute-done.3.refs_0_), channel_id=1, source_target_pairs={{0,4},{4,8},{8,12},{12,0},{1,5},{5,9},{9,13},{13,1},{2,6},{6,10},{... | collective-permute-start | bytes 737288 | tf_op jit(solution)/shard_map/ppermute | solution.py:107
  32.2 9.7 %collective-permute-start.5 = (bf16[32,3840]{1,0:T(8,128)(2,1)}, bf16[32,3840]{1,0:T(8,128)(2,1)}, u32[]{:S(2)}, u32[]{:S(2)}) collective-permute-start(bf16[32,3840]{1,0:T(8,128)(2,1)} %collective-permute-done.refs_0_), channel_id=1, source_target_pairs={{0,4},{4,8},{8,12},{12,0},{1,5},{5,9},{9,13},{13,1},{2,6},{6,10},{... | collective-permute-start | bytes 737288 | tf_op jit(solution)/shard_map/ppermute | solution.py:107
  32.2 9.7 %collective-permute-start.6 = (bf16[32,3840]{1,0:T(8,128)(2,1)}, bf16[32,3840]{1,0:T(8,128)(2,1)S(1)}, u32[]{:S(2)}, u32[]{:S(2)}) collective-permute-start(bf16[32,3840]{1,0:T(8,128)(2,1)} %collective-permute-done.1.refs_0_), channel_id=1, source_target_pairs={{0,16},{16,0},{1,17},{17,1},{2,18},{18,2},{3,19},{19,3},{4,20},{20... | collective-permute-start | bytes 737288 | tf_op jit(solution)/shard_map/ppermute | solution.py:113
  40.0 10.7 %collective-permute-start.12 = (bf16[32,3840]{1,0:T(8,128)(2,1)S(1)}, bf16[32,3840]{1,0:T(8,128)(2,1)S(1)}, u32[]{:S(2)}, u32[]{:S(2)}) collective-permute-start(bf16[32,3840]{1,0:T(8,128)(2,1)S(1)} %collective-permute-done.11.refs_0_), channel_id=1, source_target_pairs={{0,16},{16,0},{1,17},{17,1},{2,18},{18,2},{3,19},{19,3},{4,20},{20... | collective-permute-start | bytes 737288 | tf_op jit(solution)/shard_map/ppermute | solution.py:113
  40.1 10.6 %collective-permute-start.16 = (bf16[32,3840]{1,0:T(8,128)(2,1)}, bf16[32,3840]{1,0:T(8,128)(2,1)S(1)}, u32[]{:S(2)}, u32[]{:S(2)}) collective-permute-start(bf16[32,3840]{1,0:T(8,128)(2,1)} %collective-permute-done.7.refs_0_), channel_id=1, source_target_pairs={{0,4},{4,8},{8,12},{12,0},{1,5},{5,9},{9,13},{13,1},{2,6},{6,10},{... | collective-permute-start | bytes 737288 | tf_op jit(solution)/shard_map/ppermute | solution.py:107
  43.7 12.1 %collective-permute-start.9 = (bf16[32,3840]{1,0:T(8,128)(2,1)}, bf16[32,3840]{1,0:T(8,128)(2,1)S(1)}, u32[]{:S(2)}, u32[]{:S(2)}) collective-permute-start(bf16[32,3840]{1,0:T(8,128)(2,1)} %collective-permute-done.1.refs_0_), channel_id=1, source_target_pairs={{0,4},{4,8},{8,12},{12,0},{1,5},{5,9},{9,13},{13,1},{2,6},{6,10},{... | collective-permute-start | bytes 737288 | tf_op jit(solution)/shard_map/ppermute | solution.py:107
  44.9 11.0 %collective-permute-start.10 = (bf16[32,3840]{1,0:T(8,128)(2,1)}, bf16[32,3840]{1,0:T(8,128)(2,1)S(1)}, u32[]{:S(2)}, u32[]{:S(2)}) collective-permute-start(bf16[32,3840]{1,0:T(8,128)(2,1)} %collective-permute-done.5.refs_0_), channel_id=1, source_target_pairs={{0,16},{16,0},{1,17},{17,1},{2,18},{18,2},{3,19},{19,3},{4,20},{20... | collective-permute-start | bytes 737288 | tf_op jit(solution)/shard_map/ppermute | solution.py:113
  46.8 14.2 %copy-start.5 = (bf16[256,3840]{1,0:T(8,128)(2,1)S(1)}, bf16[256,3840]{1,0:T(8,128)(2,1)}, u32[]{:S(2)}) copy-start(bf16[256,3840]{1,0:T(8,128)(2,1)} %copy-done.3) | copy-start | bytes 5898244
  46.8 11.8 %collective-permute-start.13 = (bf16[64,1024]{1,0:T(8,128)(2,1)S(1)}, bf16[64,1024]{1,0:T(8,128)(2,1)S(1)}, u32[]{:S(2)}, u32[]{:S(2)}) collective-permute-start(bf16[64,1024]{1,0:T(8,128)(2,1)S(1)} %pad_maximum_fusion), channel_id=1, source_target_pairs={{0,4},{4,8},{8,12},{12,0},{1,5},{5,9},{9,13},{13,1},{2,6},{6,10},{... | collective-permute-start | bytes 393224 | tf_op jit(solution)/shard_map/ppermute | solution.py:151
  50.7 12.0 %collective-permute-start.17 = (bf16[32,3840]{1,0:T(8,128)(2,1)S(1)}, bf16[32,3840]{1,0:T(8,128)(2,1)S(1)}, u32[]{:S(2)}, u32[]{:S(2)}) collective-permute-start(bf16[32,3840]{1,0:T(8,128)(2,1)S(1)} %collective-permute-done.16.refs_0_), channel_id=1, source_target_pairs={{0,16},{16,0},{1,17},{17,1},{2,18},{18,2},{3,19},{19,3},{4,20},{20... | collective-permute-start | bytes 737288 | tf_op jit(solution)/shard_map/ppermute | solution.py:113
  52.9 11.0 %collective-permute-start.21 = (bf16[32,3840]{1,0:T(8,128)(2,1)S(1)}, bf16[32,3840]{1,0:T(8,128)(2,1)S(1)}, u32[]{:S(2)}, u32[]{:S(2)}) collective-permute-start(bf16[32,3840]{1,0:T(8,128)(2,1)S(1)} %collective-permute-done.11.refs_0_), channel_id=1, source_target_pairs={{0,4},{4,8},{8,12},{12,0},{1,5},{5,9},{9,13},{13,1},{2,6},{6,10},{... | collective-permute-start | bytes 737288 | tf_op jit(solution)/shard_map/ppermute | solution.py:107
  58.6 16.2 %copy-start.19 = (bf16[64,1024]{1,0:T(8,128)(2,1)}, bf16[64,1024]{1,0:T(8,128)(2,1)S(1)}, u32[]{:S(2)}) copy-start(bf16[64,1024]{1,0:T(8,128)(2,1)S(1)} %collective-permute-done.13.refs_4_) | copy-start | bytes 393220
  58.6 10.9 %collective-permute-start.14 = (bf16[32,3840]{1,0:T(8,128)(2,1)}, bf16[32,3840]{1,0:T(8,128)(2,1)S(1)}, u32[]{:S(2)}, u32[]{:S(2)}) collective-permute-start(bf16[32,3840]{1,0:T(8,128)(2,1)} %collective-permute-done.5.refs_0_), channel_id=1, source_target_pairs={{0,4},{4,8},{8,12},{12,0},{1,5},{5,9},{9,13},{13,1},{2,6},{6,10},{... | collective-permute-start | bytes 737288 | tf_op jit(solution)/shard_map/ppermute | solution.py:107
  58.6 10.9 %collective-permute-start.15 = (bf16[32,3840]{1,0:T(8,128)(2,1)S(1)}, bf16[32,3840]{1,0:T(8,128)(2,1)S(1)}, u32[]{:S(2)}, u32[]{:S(2)}) collective-permute-start(bf16[32,3840]{1,0:T(8,128)(2,1)S(1)} %collective-permute-done.9.refs_0_), channel_id=1, source_target_pairs={{0,16},{16,0},{1,17},{17,1},{2,18},{18,2},{3,19},{19,3},{4,20},{20... | collective-permute-start | bytes 737288 | tf_op jit(solution)/shard_map/ppermute | solution.py:113
  63.9 10.9 %collective-permute-start.22 = (bf16[32,3840]{1,0:T(8,128)(2,1)S(1)}, bf16[32,3840]{1,0:T(8,128)(2,1)}, u32[]{:S(2)}, u32[]{:S(2)}) collective-permute-start(bf16[32,3840]{1,0:T(8,128)(2,1)S(1)} %collective-permute-done.16.refs_0_), channel_id=1, source_target_pairs={{0,4},{4,8},{8,12},{12,0},{1,5},{5,9},{9,13},{13,1},{2,6},{6,10},{... | collective-permute-start | bytes 737288 | tf_op jit(solution)/shard_map/ppermute | solution.py:107
  63.9 10.9 %collective-permute-start.25 = (bf16[32,3840]{1,0:T(8,128)(2,1)S(1)}, bf16[32,3840]{1,0:T(8,128)(2,1)S(1)}, u32[]{:S(2)}, u32[]{:S(2)}) collective-permute-start(bf16[32,3840]{1,0:T(8,128)(2,1)S(1)} %collective-permute-done.21.refs_0_), channel_id=1, source_target_pairs={{0,16},{16,0},{1,17},{17,1},{2,18},{18,2},{3,19},{19,3},{4,20},{20... | collective-permute-start | bytes 737288 | tf_op jit(solution)/shard_map/ppermute | solution.py:113
  70.3 8.7 %collective-permute-start.18 = (bf16[32,3840]{1,0:T(8,128)(2,1)S(1)}, bf16[32,3840]{1,0:T(8,128)(2,1)}, u32[]{:S(2)}, u32[]{:S(2)}) collective-permute-start(bf16[32,3840]{1,0:T(8,128)(2,1)S(1)} %collective-permute-done.9.refs_0_), channel_id=1, source_target_pairs={{0,4},{4,8},{8,12},{12,0},{1,5},{5,9},{9,13},{13,1},{2,6},{6,10},{... | collective-permute-start | bytes 737288 | tf_op jit(solution)/shard_map/ppermute | solution.py:107
  70.3 8.6 %collective-permute-start.19 = (bf16[32,3840]{1,0:T(8,128)(2,1)S(1)}, bf16[32,3840]{1,0:T(8,128)(2,1)S(1)}, u32[]{:S(2)}, u32[]{:S(2)}) collective-permute-start(bf16[32,3840]{1,0:T(8,128)(2,1)S(1)} %collective-permute-done.14.refs_0_), channel_id=1, source_target_pairs={{0,16},{16,0},{1,17},{17,1},{2,18},{18,2},{3,19},{19,3},{4,20},{20... | collective-permute-start | bytes 737288 | tf_op jit(solution)/shard_map/ppermute | solution.py:113
  74.8 6.9 %collective-permute-start.23 = (bf16[64,1024]{1,0:T(8,128)(2,1)S(1)}, bf16[64,1024]{1,0:T(8,128)(2,1)}, u32[]{:S(2)}, u32[]{:S(2)}) collective-permute-start(bf16[64,1024]{1,0:T(8,128)(2,1)S(1)} %collective-permute-done.13.refs_4_), channel_id=1, source_target_pairs={{0,4},{4,8},{8,12},{12,0},{1,5},{5,9},{9,13},{13,1},{2,6},{6,10},{... | collective-permute-start | bytes 393224 | tf_op jit(solution)/shard_map/ppermute | solution.py:151
  74.8 11.6 %collective-permute-start.26 = (bf16[32,3840]{1,0:T(8,128)(2,1)}, bf16[32,3840]{1,0:T(8,128)(2,1)}, u32[]{:S(2)}, u32[]{:S(2)}) collective-permute-start(bf16[32,3840]{1,0:T(8,128)(2,1)} %collective-permute-done.22.refs_0_), channel_id=1, source_target_pairs={{0,16},{16,0},{1,17},{17,1},{2,18},{18,2},{3,19},{19,3},{4,20},{20... | collective-permute-start | bytes 737288 | tf_op jit(solution)/shard_map/ppermute | solution.py:113
  79.7 8.5 %collective-permute-start.20 = (bf16[32,3840]{1,0:T(8,128)(2,1)}, bf16[32,3840]{1,0:T(8,128)(2,1)}, u32[]{:S(2)}, u32[]{:S(2)}) collective-permute-start(bf16[32,3840]{1,0:T(8,128)(2,1)} %collective-permute-done.18.refs_0_), channel_id=1, source_target_pairs={{0,16},{16,0},{1,17},{17,1},{2,18},{18,2},{3,19},{19,3},{4,20},{20... | collective-permute-start | bytes 737288 | tf_op jit(solution)/shard_map/ppermute | solution.py:113
  81.7 7.1 %collective-permute-start.24 = (bf16[64,1024]{1,0:T(8,128)(2,1)}, bf16[64,1024]{1,0:T(8,128)(2,1)}, u32[]{:S(2)}, u32[]{:S(2)}) collective-permute-start(bf16[64,1024]{1,0:T(8,128)(2,1)} %collective-permute-done.23.refs_5_), channel_id=1, source_target_pairs={{0,4},{4,8},{8,12},{12,0},{1,5},{5,9},{9,13},{13,1},{2,6},{6,10},{... | collective-permute-start | bytes 393224 | tf_op jit(solution)/shard_map/ppermute | solution.py:151
  91.2 1.4 %collective-permute-start.27 = (f32[2,64,256]{2,1,0:T(8,128)S(1)}, f32[2,64,256]{2,1,0:T(8,128)S(1)}, u32[]{:S(2)}, u32[]{:S(2)}) collective-permute-start(f32[2,64,256]{2,1,0:T(8,128)S(1)} %dynamic-slice_bitcast_fusion), channel_id=1, source_target_pairs={{0,1},{1,0},{2,3},{3,2},{4,5},{5,4},{6,7},{7,6},{8,9},{9,8},{10,11... | collective-permute-start | bytes 393224 | tf_op jit(solution)/shard_map/ppermute | solution.py:124
  92.7 4.3 %collective-permute-start.28 = (f32[1,64,256]{2,1,0:T(8,128)S(1)}, f32[1,64,256]{2,1,0:T(8,128)S(1)}, u32[]{:S(2)}, u32[]{:S(2)}) collective-permute-start(f32[1,64,256]{2,1,0:T(8,128)S(1)} %constant_dynamic-slice_fusion), channel_id=1, source_target_pairs={{0,2},{1,3},{2,0},{3,1},{4,6},{5,7},{6,4},{7,5},{8,10},{9,11},{10,... | collective-permute-start | bytes 196616 | tf_op jit(solution)/shard_map/ppermute | solution.py:124
  (19 other events, 79.9 us)

commit v16 on v15

--- a/solution.py
+++ b/solution.py
@@ -9,7 +9,7 @@
 
 CONTRACT = (((1,), (1,)), ((), ()))
 LANES = 128
-CHUNKS, SHARE = 4, 15 / 64
+QUARTERS, SHARE = 4, 15 / 16
 
 
 def product(rows, scale, train, unit, width, skip=0):
@@ -46,18 +46,21 @@
 
 
 def last_kernel(n_grp, n_ex, starts, unit, n_parts, *refs):
-    parts, (scale, train), refs = refs[:n_parts], refs[n_parts : n_parts + 2], refs[n_parts + 2 :]
+    parts, (scale, train, end_train), refs = refs[:n_parts], refs[n_parts : n_parts + 3], refs[n_parts + 3 :]
     wholes, sums, (out, kept) = refs[: n_ex - 1], refs[n_ex - 1 : -2], refs[-2:]
-    width, left = parts[0].shape[1], wholes[0].shape[1]
-    columns = lambda start: lambda here: scale[:, start + here.start : start + here.stop]
-    total = product(arrived_rows(parts), columns(starts[0]), train, unit, width)
+    width = parts[0].shape[1]
+    column = lambda here: scale[:, starts[-1] + here.start : starts[-1] + here.stop]
+    total = product(arrived_rows(parts), column, train, unit, width)
     queries = total.shape[0]
     half = queries // n_grp
+    left = end_train.shape[1] // len(starts)
+    block = jnp.concatenate([w[...] for w in wholes], axis=0)
+    end_scale = jnp.concatenate([scale[:, s + width : s + width + left] for s in starts], axis=1)
+    rest = product(lambda here: block[:, here], lambda here: end_scale[:, here], end_train, unit, len(starts) * left)
     for t, value in enumerate(sums):
         value = value[...]
         if t > 0:
-            rows = arrived_rows(wholes[t - 1 : t])
-            value += product(rows, columns(starts[1]), train, unit, left, width)
+            value += rest[(t - 1) * queries : t * queries]
         if t == n_ex - 1:
             value += total
         kept[t * queries : (t + 1) * queries, :] = value
@@ -94,7 +97,8 @@
         queries = test.shape[0]
         half = queries // n_grp
         unit = 8 * LANES
-        width = int(feats * SHARE) // LANES * LANES
+        quarter = feats // QUARTERS
+        width = int(quarter * SHARE) // LANES * LANES
         grp, feat = lax.axis_index("grp"), lax.axis_index("feat")
         ring = [(i, (i + 1) % n_ex) for i in range(n_ex)]
         hops, swaps, made, first = [], [], [], []
@@ -131,16 +135,18 @@
             return jnp.where(grp == other, rows[:half, columns], rows[half:, columns])
 
         scale = (1.0 / (hess + jnp.float32(0.1))).reshape(1, feats)
-        starts = [c * width for c in range(CHUNKS)]
-        rest = CHUNKS * width
+        starts = [c * quarter for c in range(QUARTERS)]
         held = []
         for start in starts:
             held.append(share(after(test, *held[-1:]), slice(start, start + width)))
         late = after(test, *held[-1:])
-        sides = [share(late, slice(rest, feats), other) for other in range(n_grp)]
+        ends = [slice(start + width, start + quarter) for start in starts]
+        sides = [
+            jnp.concatenate([share(late, end, other) for end in ends], axis=1) for other in range(n_grp)
+        ]
         whole = [jnp.concatenate(sides, axis=0)]
-        cuts = [*starts, feats]
-        trains = [train[:, a:b] for a, b in zip(cuts[:-1], cuts[1:])]
+        trains = [train[:, start : start + quarter] for start in starts]
+        end_train = jnp.concatenate([train[:, end] for end in ends], axis=1)
         own = call(
             functools.partial(own_kernel, starts, unit), queries, docs, feats, [test, scale, *trains]
         )
@@ -152,12 +158,13 @@
 
         for t in range(1, n_ex):
             for c, start in enumerate(starts):
-                held[c] = hop(held[c], *(whole[-1:] if t > 2 and c == 1 else []))
+                ahead = whole[-1:] if t > 2 and c == 1 else [end_train] if (t, c) == (2, 2) else []
+                held[c] = hop(held[c], *ahead)
                 if 1 < t < final and c == 1:
                     whole_hop(-2)
                 parts = swap(held[c])
                 operands = [*parts, scale, trains[c]]
-                if (t, c) == (final, CHUNKS - 1):
+                if (t, c) == (final, QUARTERS - 1):
                     continue
                 base = [] if sums[t] is None else [sums[t]]
                 sums[t] = call(
@@ -168,8 +175,8 @@
         while len(whole) < n_ex:
             whole_hop(-2)
         total = call(
-            functools.partial(last_kernel, n_grp, n_ex, [starts[-1], rest], unit, len(operands) - 2),
-            n_ex * queries, docs, feats - starts[-1], [*operands, *whole[1:], *sums],
+            functools.partial(last_kernel, n_grp, n_ex, starts, unit, len(operands) - 2),
+            n_ex * queries, docs, 2 * width, [*operands, end_train, *whole[1:], *sums],
             [pltpu.VMEM((n_ex * queries, docs), jnp.float32)],
         )
         return sum_over_feat(total).T

time: 98.4 us -> 98.3 us (level)
  local copies, waits for them, and re-layouts: 13.6 us -> 15 us
    unnamed x44 -> x56, local copies, waits for them, and re-layouts: 6.51 us -> 9.72 us
    ppermute x12, waiting for transfers between devices: 14.3 us -> 12.2 us  [hop(): hops.append(lax.ppermute(after(block, *waits, *ahead), 'ex', ring))]
    slice x2, local copies, waits for them, and re-layouts: 7.04 us -> 5.22 us  [the longest x1 4.08 us: on_device(): trains = [train[:, start:start + quarter] for start in starts]]
    ppermute x12, starting transfers between devices: 21.8 us -> 20 us  [swap(): lax.ppermute(after(block, *swaps[-2:-1]), 'grp', [(0, 1), (1, 0)])]
    ppermute x12, starting transfers between devices: 9.21 us -> 10.8 us  [hop(): hops.append(lax.ppermute(after(block, *waits, *ahead), 'ex', ring))]
    ppermute x12, waiting for transfers between devices: 2.49 us -> 3.93 us  [swap(): lax.ppermute(after(block, *swaps[-2:-1]), 'grp', [(0, 1), (1, 0)])]
  transfers between devices with their start and end apart: 29 -> 29, of which waited for: 15 -> 13; matrix products, arithmetic and copies ran while one was open for 12% -> 10% of each run, Pallas kernels for 16% -> 16%
where the time goes in v16:
time: 98.3 us; the launch traced here: 97.8 us
  starting transfers between devices  34.2 us (35%)
  waiting for transfers between devices  24.5 us (25%)
  Pallas kernels  17.5 us (18%)
  local copies, waits for them, and re-layouts  15 us (15%)
  other arithmetic  6.09 us (6%)
    ppermute x12, starting transfers between devices, swap(): lax.ppermute(after(block, *swaps[-2:-1]), 'grp', [(0, 1), (1, 0)])  20 us
    pallas_call x13, Pallas kernels, call(): pl.pallas_call(kernel, out_shape=jax.ShapeDtypeStruct((rows, docs), jnp.f...  17.5 us
    ppermute x12, waiting for transfers between devices, hop(): hops.append(lax.ppermute(after(block, *waits, *ahead), 'ex', ring))  12.2 us
    ppermute x12, starting transfers between devices, hop(): hops.append(lax.ppermute(after(block, *waits, *ahead), 'ex', ring))  10.8 us
    unnamed x56, local copies, waits for them, and re-layouts  9.72 us
    select_n x5, other arithmetic, share(): return jnp.where(grp == other, rows[:half, columns], rows[half:, columns])  5.36 us
    ppermute x3, waiting for transfers between devices, whole_hop(): whole.append(lax.ppermute(after(whole[-1], hops[gate]), 'ex', ring))  4.34 us
    slice x1, local copies, waits for them, and re-layouts, on_device(): trains = [train[:, start:start + quarter] for start in starts]  4.08 us
  transfers between devices with their start and end apart: 29, of which 13 were waited for; matrix products, arithmetic and copies ran while one was open for 10% of the time, Pallas kernels for 16%

profile of v16, /device:TPU:0, one launch (start us, length us, event | category | flops | bytes accessed | tf_op | source)
XLA Modules:
  0.0 97.8 jit_solution(13268908546193320384)
XLA Ops:
  1.1 3.1 %collective-permute-start.3 = (bf16[32,3840]{1,0:T(8,128)(2,1)S(1)}, bf16[32,3840]{1,0:T(8,128)(2,1)}, u32[]{:S(2)}, u32[]{:S(2)}) collective-permute-start(bf16[32,3840]{1,0:T(8,128)(2,1)S(1)} %slice_select_fusion.3), channel_id=1, source_target_pairs={{0,4},{4,8},{8,12},{12,0},{1,5},{5,9},{9,13},{13,1},{2,6},{6,10},{... | collective-permute-start | bytes 737288 | tf_op jit(solution)/shard_map/ppermute | solution.py:111
  5.3 1.6 %collective-permute-start = (bf16[32,3840]{1,0:T(8,128)(2,1)S(1)}, bf16[32,3840]{1,0:T(8,128)(2,1)S(1)}, u32[]{:S(2)}, u32[]{:S(2)}) collective-permute-start(bf16[32,3840]{1,0:T(8,128)(2,1)S(1)} %slice_select_fusion.2), channel_id=1, source_target_pairs={{0,4},{4,8},{8,12},{12,0},{1,5},{5,9},{9,13},{13,1},{2,6},{6,10},{... | collective-permute-start | bytes 737288 | tf_op jit(solution)/shard_map/ppermute | solution.py:111
  9.1 4.1 %fusion.1 = (bf16[256,4096]{1,0:T(8,128)(2,1)S(1)}, bf16[256,4096]{1,0:T(8,128)(2,1)S(1)}, bf16[256,4096]{1,0:T(8,128)(2,1)S(1)}, bf16[256,4096]{1,0:T(8,128)(2,1)S(1)}) fusion(bf16[256,16384]{1,0:T(8,128)(2,1)} %param.3), kind=kLoop, calls=%fused_computation.20 | loop fusion | bytes 16777216 | tf_op jit(solution)/shard_map/slice | solution.py:148
  13.3 1.6 %collective-permute-start.7 = (bf16[32,3840]{1,0:T(8,128)(2,1)S(1)}, bf16[32,3840]{1,0:T(8,128)(2,1)}, u32[]{:S(2)}, u32[]{:S(2)}) collective-permute-start(bf16[32,3840]{1,0:T(8,128)(2,1)S(1)} %slice_select_fusion.1), channel_id=1, source_target_pairs={{0,4},{4,8},{8,12},{12,0},{1,5},{5,9},{9,13},{13,1},{2,6},{6,10},{... | collective-permute-start | bytes 737288 | tf_op jit(solution)/shard_map/ppermute | solution.py:111
  16.4 2.7 %shard_map.37.refs_8_ = f32[64,256]{1,0:T(8,128)S(1)} custom-call(bf16[64,16384]{1,0:T(8,128)(2,1)S(1)} %copy-done.10, f32[1,16384]{1,0:T(1,128)S(1)} %bitcast.10, bf16[256,4096]{1,0:T(8,128)(2,1)S(1)} %get-tuple-element.66.refs_0_.refs_3_, bf16[256,4096]{1,0:T(8,128)(2,1)S(1)} %get-tuple-element.65.refs_1_.refs_3_, ...), custom_call_target="tpu_custom_call" | custom-call | flops 536870912 | bytes 10485760 | tf_op jit(solution)/shard_map/pallas_call | solution.py:78
  20.9 2.0 %collective-permute-done.7.refs_0_ = bf16[32,3840]{1,0:T(8,128)(2,1)} collective-permute-done((bf16[32,3840]{1,0:T(8,128)(2,1)S(1)}, bf16[32,3840]{1,0:T(8,128)(2,1)}, u32[]{:S(2)}, u32[]{:S(2)}) %collective-permute-start.7) | collective-permute-done | bytes 245792 | tf_op jit(solution)/shard_map/ppermute | solution.py:111
  23.4 2.1 %collective-permute-start.8 = (bf16[32,3840]{1,0:T(8,128)(2,1)}, bf16[32,3840]{1,0:T(8,128)(2,1)}, u32[]{:S(2)}, u32[]{:S(2)}) collective-permute-start(bf16[32,3840]{1,0:T(8,128)(2,1)} %collective-permute-done.7.refs_0_), channel_id=1, source_target_pairs={{0,16},{16,0},{1,17},{17,1},{2,18},{18,2},{3,19},{19,3},{4,20},{20... | collective-permute-start | bytes 737288 | tf_op jit(solution)/shard_map/ppermute | solution.py:117
  25.8 2.9 %collective-permute-done.2.refs_1_ = bf16[32,3840]{1,0:T(8,128)(2,1)S(1)} collective-permute-done((bf16[32,3840]{1,0:T(8,128)(2,1)S(1)}, bf16[32,3840]{1,0:T(8,128)(2,1)S(1)}, u32[]{:S(2)}, u32[]{:S(2)}) %collective-permute-start.2) | collective-permute-done | bytes 245792 | tf_op jit(solution)/shard_map/ppermute | solution.py:117
  29.4 1.6 %shard_map.38.refs_4_ = f32[64,256]{1,0:T(8,128)S(1)} custom-call(bf16[32,3840]{1,0:T(8,128)(2,1)} %collective-permute-done.3.refs_0_, bf16[32,3840]{1,0:T(8,128)(2,1)S(1)} %collective-permute-done.4.refs_1_, f32[1,16384]{1,0:T(1,128)S(1)} %bitcast.11, bf16[256,4096]{1,0:T(8,128)(2,1)S(1)} %get-tuple-element.66.refs_0_.refs_3_), custom_call_target="tpu_custom_call" | custom-call | flops 125829120 | bytes 2457600 | tf_op jit(solution)/shard_map/pallas_call | solution.py:78
  31.4 2.0 %collective-permute-start.6 = (bf16[32,3840]{1,0:T(8,128)(2,1)}, bf16[32,3840]{1,0:T(8,128)(2,1)}, u32[]{:S(2)}, u32[]{:S(2)}) collective-permute-start(bf16[32,3840]{1,0:T(8,128)(2,1)} %collective-permute-done.1.refs_0_), channel_id=1, source_target_pairs={{0,16},{16,0},{1,17},{17,1},{2,18},{18,2},{3,19},{19,3},{4,20},{20... | collective-permute-start | bytes 737288 | tf_op jit(solution)/shard_map/ppermute | solution.py:117
  34.5 1.6 %copy-done.4 = bf16[256,4096]{1,0:T(8,128)(2,1)S(1)} copy-done((bf16[256,4096]{1,0:T(8,128)(2,1)S(1)}, bf16[256,4096]{1,0:T(8,128)(2,1)}, u32[]{:S(2)}) %copy-start.4) | copy-done | bytes 2097176
  37.9 1.6 %collective-permute-start.16 = (bf16[32,3840]{1,0:T(8,128)(2,1)}, bf16[32,3840]{1,0:T(8,128)(2,1)S(1)}, u32[]{:S(2)}, u32[]{:S(2)}) collective-permute-start(bf16[32,3840]{1,0:T(8,128)(2,1)} %collective-permute-done.7.refs_0_), channel_id=1, source_target_pairs={{0,4},{4,8},{8,12},{12,0},{1,5},{5,9},{9,13},{13,1},{2,6},{6,10},{... | collective-permute-start | bytes 737288 | tf_op jit(solution)/shard_map/ppermute | solution.py:111
  40.0 1.8 %shard_map.40.refs_4_ = f32[64,256]{1,0:T(8,128)S(1)} custom-call(bf16[32,3840]{1,0:T(8,128)(2,1)} %collective-permute-done.7.refs_0_, bf16[32,3840]{1,0:T(8,128)(2,1)} %collective-permute-done.8.refs_1_, f32[1,16384]{1,0:T(1,128)S(1)} %bitcast.13, bf16[256,4096]{1,0:T(8,128)(2,1)S(1)} %copy-done.1, f32[64,256]{1,0:T(8,128)S(1)} %shard_map.39.refs_4_), custom_call_target="tpu_custom_call" | custom-call | flops 125829120 | bytes 2457600 | tf_op jit(solution)/shard_map/pallas_call | solution.py:78
  41.8 1.7 %collective-permute-start.9 = (bf16[32,3840]{1,0:T(8,128)(2,1)}, bf16[32,3840]{1,0:T(8,128)(2,1)S(1)}, u32[]{:S(2)}, u32[]{:S(2)}) collective-permute-start(bf16[32,3840]{1,0:T(8,128)(2,1)} %collective-permute-done.1.refs_0_), channel_id=1, source_target_pairs={{0,4},{4,8},{8,12},{12,0},{1,5},{5,9},{9,13},{13,1},{2,6},{6,10},{... | collective-permute-start | bytes 737288 | tf_op jit(solution)/shard_map/ppermute | solution.py:111
  43.5 2.5 %collective-permute-start.10 = (bf16[32,3840]{1,0:T(8,128)(2,1)}, bf16[32,3840]{1,0:T(8,128)(2,1)S(1)}, u32[]{:S(2)}, u32[]{:S(2)}) collective-permute-start(bf16[32,3840]{1,0:T(8,128)(2,1)} %collective-permute-done.5.refs_0_), channel_id=1, source_target_pairs={{0,16},{16,0},{1,17},{17,1},{2,18},{18,2},{3,19},{19,3},{4,20},{20... | collective-permute-start | bytes 737288 | tf_op jit(solution)/shard_map/ppermute | solution.py:117
  46.0 1.7 %collective-permute-start.13 = (bf16[64,1024]{1,0:T(8,128)(2,1)S(1)}, bf16[64,1024]{1,0:T(8,128)(2,1)S(1)}, u32[]{:S(2)}, u32[]{:S(2)}) collective-permute-start(bf16[64,1024]{1,0:T(8,128)(2,1)S(1)} %maximum_maximum_fusion), channel_id=1, source_target_pairs={{0,4},{4,8},{8,12},{12,0},{1,5},{5,9},{9,13},{13,1},{2,6},{6,10},{... | collective-permute-start | bytes 393224 | tf_op jit(solution)/shard_map/ppermute | solution.py:157
  47.7 1.8 %shard_map.44.refs_9_ = f32[64,256]{1,0:T(8,128)S(1)} custom-call(bf16[32,3840]{1,0:T(8,128)(2,1)} %collective-permute-done.1.refs_0_, bf16[32,3840]{1,0:T(8,128)(2,1)} %collective-permute-done.6.refs_1_, f32[1,16384]{1,0:T(1,128)S(1)} %bitcast.14, bf16[256,4096]{1,0:T(8,128)(2,1)S(1)} %get-tuple-element.63.refs_3_, f32[64,256]{1,0:T(8,128)S(1)} %shard_map.40.refs_4_), custom_call_target="tpu_custom_call" | custom-call | flops 125829120 | bytes 2457600 | tf_op jit(solution)/shard_map/pallas_call | solution.py:78
  51.9 2.1 %collective-permute-done.9.refs_0_ = bf16[32,3840]{1,0:T(8,128)(2,1)S(1)} collective-permute-done((bf16[32,3840]{1,0:T(8,128)(2,1)}, bf16[32,3840]{1,0:T(8,128)(2,1)S(1)}, u32[]{:S(2)}, u32[]{:S(2)}) %collective-permute-start.9) | collective-permute-done | bytes 245792 | tf_op jit(solution)/shard_map/ppermute | solution.py:111
  54.0 2.8 %collective-permute-done.13.refs_5_ = bf16[64,1024]{1,0:T(8,128)(2,1)S(1)} collective-permute-done((bf16[64,1024]{1,0:T(8,128)(2,1)S(1)}, bf16[64,1024]{1,0:T(8,128)(2,1)S(1)}, u32[]{:S(2)}, u32[]{:S(2)}) %collective-permute-start.13) | collective-permute-done | bytes 131104 | tf_op jit(solution)/shard_map/ppermute | solution.py:157
  56.8 2.1 %collective-permute-start.15 = (bf16[32,3840]{1,0:T(8,128)(2,1)S(1)}, bf16[32,3840]{1,0:T(8,128)(2,1)S(1)}, u32[]{:S(2)}, u32[]{:S(2)}) collective-permute-start(bf16[32,3840]{1,0:T(8,128)(2,1)S(1)} %collective-permute-done.9.refs_0_), channel_id=1, source_target_pairs={{0,16},{16,0},{1,17},{17,1},{2,18},{18,2},{3,19},{19,3},{4,20},{20... | collective-permute-start | bytes 737288 | tf_op jit(solution)/shard_map/ppermute | solution.py:117
  58.9 1.6 %shard_map.42.refs_4_ = f32[64,256]{1,0:T(8,128)S(1)} custom-call(bf16[32,3840]{1,0:T(8,128)(2,1)} %collective-permute-done.5.refs_0_, bf16[32,3840]{1,0:T(8,128)(2,1)S(1)} %collective-permute-done.10.refs_1_, f32[1,16384]{1,0:T(1,128)S(1)} %bitcast.16, bf16[256,4096]{1,0:T(8,128)(2,1)S(1)} %copy-done.5, f32[64,256]{1,0:T(8,128)S(1)} %shard_map.41.refs_4_), custom_call_target="tpu_custom_call" | custom-call | flops 125829120 | bytes 2457600 | tf_op jit(solution)/shard_map/pallas_call | solution.py:78
  62.1 2.1 %collective-permute-start.25 = (bf16[32,3840]{1,0:T(8,128)(2,1)S(1)}, bf16[32,3840]{1,0:T(8,128)(2,1)S(1)}, u32[]{:S(2)}, u32[]{:S(2)}) collective-permute-start(bf16[32,3840]{1,0:T(8,128)(2,1)S(1)} %collective-permute-done.21.refs_0_), channel_id=1, source_target_pairs={{0,16},{16,0},{1,17},{17,1},{2,18},{18,2},{3,19},{19,3},{4,20},{20... | collective-permute-start | bytes 737288 | tf_op jit(solution)/shard_map/ppermute | solution.py:117
  64.1 3.1 %collective-permute-done.14.refs_0_ = bf16[32,3840]{1,0:T(8,128)(2,1)S(1)} collective-permute-done((bf16[32,3840]{1,0:T(8,128)(2,1)}, bf16[32,3840]{1,0:T(8,128)(2,1)S(1)}, u32[]{:S(2)}, u32[]{:S(2)}) %collective-permute-start.14) | collective-permute-done | bytes 245792 | tf_op jit(solution)/shard_map/ppermute | solution.py:111
  68.0 2.1 %collective-permute-start.19 = (bf16[32,3840]{1,0:T(8,128)(2,1)S(1)}, bf16[32,3840]{1,0:T(8,128)(2,1)S(1)}, u32[]{:S(2)}, u32[]{:S(2)}) collective-permute-start(bf16[32,3840]{1,0:T(8,128)(2,1)S(1)} %collective-permute-done.14.refs_0_), channel_id=1, source_target_pairs={{0,16},{16,0},{1,17},{17,1},{2,18},{18,2},{3,19},{19,3},{4,20},{20... | collective-permute-start | bytes 737288 | tf_op jit(solution)/shard_map/ppermute | solution.py:117
  70.2 2.7 %collective-permute-done.22.refs_0_ = bf16[32,3840]{1,0:T(8,128)(2,1)} collective-permute-done((bf16[32,3840]{1,0:T(8,128)(2,1)S(1)}, bf16[32,3840]{1,0:T(8,128)(2,1)}, u32[]{:S(2)}, u32[]{:S(2)}) %collective-permute-start.22) | collective-permute-done | bytes 245792 | tf_op jit(solution)/shard_map/ppermute | solution.py:111
  73.6 1.6 %collective-permute-start.26 = (bf16[32,3840]{1,0:T(8,128)(2,1)}, bf16[32,3840]{1,0:T(8,128)(2,1)}, u32[]{:S(2)}, u32[]{:S(2)}) collective-permute-start(bf16[32,3840]{1,0:T(8,128)(2,1)} %collective-permute-done.22.refs_0_), channel_id=1, source_target_pairs={{0,16},{16,0},{1,17},{17,1},{2,18},{18,2},{3,19},{19,3},{4,20},{20... | collective-permute-start | bytes 737288 | tf_op jit(solution)/shard_map/ppermute | solution.py:117
  76.7 2.1 %collective-permute-start.20 = (bf16[32,3840]{1,0:T(8,128)(2,1)S(1)}, bf16[32,3840]{1,0:T(8,128)(2,1)}, u32[]{:S(2)}, u32[]{:S(2)}) collective-permute-start(bf16[32,3840]{1,0:T(8,128)(2,1)S(1)} %collective-permute-done.18.refs_0_), channel_id=1, source_target_pairs={{0,16},{16,0},{1,17},{17,1},{2,18},{18,2},{3,19},{19,3},{4,20},{20... | collective-permute-start | bytes 737288 | tf_op jit(solution)/shard_map/ppermute | solution.py:117
  83.2 1.6 %copy-done.9 = bf16[256,4096]{1,0:T(8,128)(2,1)S(1)} copy-done((bf16[256,4096]{1,0:T(8,128)(2,1)S(1)}, bf16[256,4096]{1,0:T(8,128)(2,1)}, u32[]{:S(2)}) %copy-start.9) | copy-done | bytes 2097176
  87.5 1.8 %shard_map.48.refs_11_ = f32[64,256]{1,0:T(8,128)S(1)} custom-call(bf16[32,3840]{1,0:T(8,128)(2,1)} %collective-permute-done.22.refs_0_, bf16[32,3840]{1,0:T(8,128)(2,1)} %collective-permute-done.26.refs_1_, f32[1,16384]{1,0:T(1,128)S(1)} %bitcast.21, bf16[256,4096]{1,0:T(8,128)(2,1)S(1)} %copy-done.2, f32[64,256]{1,0:T(8,128)S(1)} %shard_map.47.refs_4_), custom_call_target="tpu_custom_call" | custom-call | flops 125829120 | bytes 2457600 | tf_op jit(solution)/shard_map/pallas_call | solution.py:78
  89.3 2.0 %shard_map.49 = f32[256,256]{1,0:T(8,128)S(1)} custom-call(bf16[32,3840]{1,0:T(8,128)(2,1)S(1)} %collective-permute-done.18.refs_0_, bf16[32,3840]{1,0:T(8,128)(2,1)} %collective-permute-done.20.refs_1_, f32[1,16384]{1,0:T(1,128)S(1)} %bitcast.22, bf16[256,4096]{1,0:T(8,128)(2,1)S(1)} %get-tuple-element.63.refs_3_, ...), custom_call_target="tpu_custom_call" | custom-call | flops 1006632960 | bytes 7864320 | tf_op jit(solution)/shard_map/pallas_call | solution.py:78
  92.8 1.6 %collective-permute-start.28 = (f32[1,64,256]{2,1,0:T(8,128)S(1)}, f32[1,64,256]{2,1,0:T(8,128)S(1)}, u32[]{:S(2)}, u32[]{:S(2)}) collective-permute-start(f32[1,64,256]{2,1,0:T(8,128)S(1)} %constant_dynamic-slice_fusion), channel_id=1, source_target_pairs={{0,2},{1,3},{2,0},{3,1},{4,6},{5,7},{6,4},{7,5},{8,10},{9,11},{10,... | collective-permute-start | bytes 196616 | tf_op jit(solution)/shard_map/ppermute | solution.py:128
  94.3 2.8 %collective-permute-done.28 = f32[1,64,256]{2,1,0:T(8,128)S(1)} collective-permute-done((f32[1,64,256]{2,1,0:T(8,128)S(1)}, f32[1,64,256]{2,1,0:T(8,128)S(1)}, u32[]{:S(2)}, u32[]{:S(2)}) %collective-permute-start.28) | collective-permute-done | bytes 65568 | tf_op jit(solution)/shard_map/ppermute | solution.py:128
  (109 shorter events, 28.9 us)
Async XLA Ops:
  1.1 12.2 %collective-permute-start.3 = (bf16[32,3840]{1,0:T(8,128)(2,1)S(1)}, bf16[32,3840]{1,0:T(8,128)(2,1)}, u32[]{:S(2)}, u32[]{:S(2)}) collective-permute-start(bf16[32,3840]{1,0:T(8,128)(2,1)S(1)} %slice_select_fusion.3), channel_id=1, source_target_pairs={{0,4},{4,8},{8,12},{12,0},{1,5},{5,9},{9,13},{13,1},{2,6},{6,10},{... | collective-permute-start | bytes 737288 | tf_op jit(solution)/shard_map/ppermute | solution.py:111
  5.3 13.8 %collective-permute-start = (bf16[32,3840]{1,0:T(8,128)(2,1)S(1)}, bf16[32,3840]{1,0:T(8,128)(2,1)S(1)}, u32[]{:S(2)}, u32[]{:S(2)}) collective-permute-start(bf16[32,3840]{1,0:T(8,128)(2,1)S(1)} %slice_select_fusion.2), channel_id=1, source_target_pairs={{0,4},{4,8},{8,12},{12,0},{1,5},{5,9},{9,13},{13,1},{2,6},{6,10},{... | collective-permute-start | bytes 737288 | tf_op jit(solution)/shard_map/ppermute | solution.py:111
  13.2 16.1 %copy-start.7 = (bf16[256,4096]{1,0:T(8,128)(2,1)}, bf16[256,4096]{1,0:T(8,128)(2,1)S(1)}, u32[]{:S(2)}) copy-start(bf16[256,4096]{1,0:T(8,128)(2,1)S(1)} %get-tuple-element.66.refs_0_.refs_3_) | copy-start | bytes 6291460
  13.3 9.6 %collective-permute-start.7 = (bf16[32,3840]{1,0:T(8,128)(2,1)S(1)}, bf16[32,3840]{1,0:T(8,128)(2,1)}, u32[]{:S(2)}, u32[]{:S(2)}) collective-permute-start(bf16[32,3840]{1,0:T(8,128)(2,1)S(1)} %slice_select_fusion.1), channel_id=1, source_target_pairs={{0,4},{4,8},{8,12},{12,0},{1,5},{5,9},{9,13},{13,1},{2,6},{6,10},{... | collective-permute-start | bytes 737288 | tf_op jit(solution)/shard_map/ppermute | solution.py:111
  14.9 8.5 %collective-permute-start.4 = (bf16[32,3840]{1,0:T(8,128)(2,1)}, bf16[32,3840]{1,0:T(8,128)(2,1)S(1)}, u32[]{:S(2)}, u32[]{:S(2)}) collective-permute-start(bf16[32,3840]{1,0:T(8,128)(2,1)} %collective-permute-done.3.refs_0_), channel_id=1, source_target_pairs={{0,16},{16,0},{1,17},{17,1},{2,18},{18,2},{3,19},{19,3},{4,20},{20... | collective-permute-start | bytes 737288 | tf_op jit(solution)/shard_map/ppermute | solution.py:117
  19.1 9.5 %collective-permute-start.2 = (bf16[32,3840]{1,0:T(8,128)(2,1)S(1)}, bf16[32,3840]{1,0:T(8,128)(2,1)S(1)}, u32[]{:S(2)}, u32[]{:S(2)}) collective-permute-start(bf16[32,3840]{1,0:T(8,128)(2,1)S(1)} %collective-permute-done.refs_0_), channel_id=1, source_target_pairs={{0,16},{16,0},{1,17},{17,1},{2,18},{18,2},{3,19},{19,3},{4,20},{20... | collective-permute-start | bytes 737288 | tf_op jit(solution)/shard_map/ppermute | solution.py:117
  19.7 9.7 %collective-permute-start.1 = (bf16[32,3840]{1,0:T(8,128)(2,1)S(1)}, bf16[32,3840]{1,0:T(8,128)(2,1)}, u32[]{:S(2)}, u32[]{:S(2)}) collective-permute-start(bf16[32,3840]{1,0:T(8,128)(2,1)S(1)} %slice_select_fusion), channel_id=1, source_target_pairs={{0,4},{4,8},{8,12},{12,0},{1,5},{5,9},{9,13},{13,1},{2,6},{6,10},{... | collective-permute-start | bytes 737288 | tf_op jit(solution)/shard_map/ppermute | solution.py:111
  23.4 14.4 %collective-permute-start.8 = (bf16[32,3840]{1,0:T(8,128)(2,1)}, bf16[32,3840]{1,0:T(8,128)(2,1)}, u32[]{:S(2)}, u32[]{:S(2)}) collective-permute-start(bf16[32,3840]{1,0:T(8,128)(2,1)} %collective-permute-done.7.refs_0_), channel_id=1, source_target_pairs={{0,16},{16,0},{1,17},{17,1},{2,18},{18,2},{3,19},{19,3},{4,20},{20... | collective-permute-start | bytes 737288 | tf_op jit(solution)/shard_map/ppermute | solution.py:117
  25.5 12.3 %collective-permute-start.11 = (bf16[32,3840]{1,0:T(8,128)(2,1)}, bf16[32,3840]{1,0:T(8,128)(2,1)S(1)}, u32[]{:S(2)}, u32[]{:S(2)}) collective-permute-start(bf16[32,3840]{1,0:T(8,128)(2,1)} %collective-permute-done.3.refs_0_), channel_id=1, source_target_pairs={{0,4},{4,8},{8,12},{12,0},{1,5},{5,9},{9,13},{13,1},{2,6},{6,10},{... | collective-permute-start | bytes 737288 | tf_op jit(solution)/shard_map/ppermute | solution.py:111
  31.0 8.5 %collective-permute-start.5 = (bf16[32,3840]{1,0:T(8,128)(2,1)S(1)}, bf16[32,3840]{1,0:T(8,128)(2,1)}, u32[]{:S(2)}, u32[]{:S(2)}) collective-permute-start(bf16[32,3840]{1,0:T(8,128)(2,1)S(1)} %collective-permute-done.refs_0_), channel_id=1, source_target_pairs={{0,4},{4,8},{8,12},{12,0},{1,5},{5,9},{9,13},{13,1},{2,6},{6,10},{... | collective-permute-start | bytes 737288 | tf_op jit(solution)/shard_map/ppermute | solution.py:111
  31.4 8.6 %collective-permute-start.6 = (bf16[32,3840]{1,0:T(8,128)(2,1)}, bf16[32,3840]{1,0:T(8,128)(2,1)}, u32[]{:S(2)}, u32[]{:S(2)}) collective-permute-start(bf16[32,3840]{1,0:T(8,128)(2,1)} %collective-permute-done.1.refs_0_), channel_id=1, source_target_pairs={{0,16},{16,0},{1,17},{17,1},{2,18},{18,2},{3,19},{19,3},{4,20},{20... | collective-permute-start | bytes 737288 | tf_op jit(solution)/shard_map/ppermute | solution.py:117
  37.8 11.7 %collective-permute-start.12 = (bf16[32,3840]{1,0:T(8,128)(2,1)S(1)}, bf16[32,3840]{1,0:T(8,128)(2,1)S(1)}, u32[]{:S(2)}, u32[]{:S(2)}) collective-permute-start(bf16[32,3840]{1,0:T(8,128)(2,1)S(1)} %collective-permute-done.11.refs_0_), channel_id=1, source_target_pairs={{0,16},{16,0},{1,17},{17,1},{2,18},{18,2},{3,19},{19,3},{4,20},{20... | collective-permute-start | bytes 737288 | tf_op jit(solution)/shard_map/ppermute | solution.py:117
  37.9 11.6 %collective-permute-start.16 = (bf16[32,3840]{1,0:T(8,128)(2,1)}, bf16[32,3840]{1,0:T(8,128)(2,1)S(1)}, u32[]{:S(2)}, u32[]{:S(2)}) collective-permute-start(bf16[32,3840]{1,0:T(8,128)(2,1)} %collective-permute-done.7.refs_0_), channel_id=1, source_target_pairs={{0,4},{4,8},{8,12},{12,0},{1,5},{5,9},{9,13},{13,1},{2,6},{6,10},{... | collective-permute-start | bytes 737288 | tf_op jit(solution)/shard_map/ppermute | solution.py:111
  41.8 12.2 %collective-permute-start.9 = (bf16[32,3840]{1,0:T(8,128)(2,1)}, bf16[32,3840]{1,0:T(8,128)(2,1)S(1)}, u32[]{:S(2)}, u32[]{:S(2)}) collective-permute-start(bf16[32,3840]{1,0:T(8,128)(2,1)} %collective-permute-done.1.refs_0_), channel_id=1, source_target_pairs={{0,4},{4,8},{8,12},{12,0},{1,5},{5,9},{9,13},{13,1},{2,6},{6,10},{... | collective-permute-start | bytes 737288 | tf_op jit(solution)/shard_map/ppermute | solution.py:111
  43.5 10.5 %collective-permute-start.10 = (bf16[32,3840]{1,0:T(8,128)(2,1)}, bf16[32,3840]{1,0:T(8,128)(2,1)S(1)}, u32[]{:S(2)}, u32[]{:S(2)}) collective-permute-start(bf16[32,3840]{1,0:T(8,128)(2,1)} %collective-permute-done.5.refs_0_), channel_id=1, source_target_pairs={{0,16},{16,0},{1,17},{17,1},{2,18},{18,2},{3,19},{19,3},{4,20},{20... | collective-permute-start | bytes 737288 | tf_op jit(solution)/shard_map/ppermute | solution.py:117
  46.0 10.8 %collective-permute-start.13 = (bf16[64,1024]{1,0:T(8,128)(2,1)S(1)}, bf16[64,1024]{1,0:T(8,128)(2,1)S(1)}, u32[]{:S(2)}, u32[]{:S(2)}) collective-permute-start(bf16[64,1024]{1,0:T(8,128)(2,1)S(1)} %maximum_maximum_fusion), channel_id=1, source_target_pairs={{0,4},{4,8},{8,12},{12,0},{1,5},{5,9},{9,13},{13,1},{2,6},{6,10},{... | collective-permute-start | bytes 393224 | tf_op jit(solution)/shard_map/ppermute | solution.py:157
  49.5 11.1 %collective-permute-start.17 = (bf16[32,3840]{1,0:T(8,128)(2,1)S(1)}, bf16[32,3840]{1,0:T(8,128)(2,1)S(1)}, u32[]{:S(2)}, u32[]{:S(2)}) collective-permute-start(bf16[32,3840]{1,0:T(8,128)(2,1)S(1)} %collective-permute-done.16.refs_0_), channel_id=1, source_target_pairs={{0,16},{16,0},{1,17},{17,1},{2,18},{18,2},{3,19},{19,3},{4,20},{20... | collective-permute-start | bytes 737288 | tf_op jit(solution)/shard_map/ppermute | solution.py:117
  50.8 11.3 %collective-permute-start.21 = (bf16[32,3840]{1,0:T(8,128)(2,1)S(1)}, bf16[32,3840]{1,0:T(8,128)(2,1)S(1)}, u32[]{:S(2)}, u32[]{:S(2)}) collective-permute-start(bf16[32,3840]{1,0:T(8,128)(2,1)S(1)} %collective-permute-done.11.refs_0_), channel_id=1, source_target_pairs={{0,4},{4,8},{8,12},{12,0},{1,5},{5,9},{9,13},{13,1},{2,6},{6,10},{... | collective-permute-start | bytes 737288 | tf_op jit(solution)/shard_map/ppermute | solution.py:111
  54.0 14.0 %copy-start.11 = (bf16[32,3840]{1,0:T(8,128)(2,1)}, bf16[32,3840]{1,0:T(8,128)(2,1)S(1)}, u32[]{:S(2)}) copy-start(bf16[32,3840]{1,0:T(8,128)(2,1)S(1)} %collective-permute-done.9.refs_0_) | copy-start | bytes 737284
  56.8 10.4 %collective-permute-start.14 = (bf16[32,3840]{1,0:T(8,128)(2,1)}, bf16[32,3840]{1,0:T(8,128)(2,1)S(1)}, u32[]{:S(2)}, u32[]{:S(2)}) collective-permute-start(bf16[32,3840]{1,0:T(8,128)(2,1)} %collective-permute-done.5.refs_0_), channel_id=1, source_target_pairs={{0,4},{4,8},{8,12},{12,0},{1,5},{5,9},{9,13},{13,1},{2,6},{6,10},{... | collective-permute-start | bytes 737288 | tf_op jit(solution)/shard_map/ppermute | solution.py:111
  56.8 10.4 %collective-permute-start.15 = (bf16[32,3840]{1,0:T(8,128)(2,1)S(1)}, bf16[32,3840]{1,0:T(8,128)(2,1)S(1)}, u32[]{:S(2)}, u32[]{:S(2)}) collective-permute-start(bf16[32,3840]{1,0:T(8,128)(2,1)S(1)} %collective-permute-done.9.refs_0_), channel_id=1, source_target_pairs={{0,16},{16,0},{1,17},{17,1},{2,18},{18,2},{3,19},{19,3},{4,20},{20... | collective-permute-start | bytes 737288 | tf_op jit(solution)/shard_map/ppermute | solution.py:117
  62.1 14.0 %copy-start.13 = (bf16[32,3840]{1,0:T(8,128)(2,1)}, bf16[32,3840]{1,0:T(8,128)(2,1)S(1)}, u32[]{:S(2)}) copy-start(bf16[32,3840]{1,0:T(8,128)(2,1)S(1)} %collective-permute-done.21.refs_0_) | copy-start | bytes 737284
  62.1 10.8 %collective-permute-start.22 = (bf16[32,3840]{1,0:T(8,128)(2,1)S(1)}, bf16[32,3840]{1,0:T(8,128)(2,1)}, u32[]{:S(2)}, u32[]{:S(2)}) collective-permute-start(bf16[32,3840]{1,0:T(8,128)(2,1)S(1)} %collective-permute-done.16.refs_0_), channel_id=1, source_target_pairs={{0,4},{4,8},{8,12},{12,0},{1,5},{5,9},{9,13},{13,1},{2,6},{6,10},{... | collective-permute-start | bytes 737288 | tf_op jit(solution)/shard_map/ppermute | solution.py:111
  62.1 10.8 %collective-permute-start.25 = (bf16[32,3840]{1,0:T(8,128)(2,1)S(1)}, bf16[32,3840]{1,0:T(8,128)(2,1)S(1)}, u32[]{:S(2)}, u32[]{:S(2)}) collective-permute-start(bf16[32,3840]{1,0:T(8,128)(2,1)S(1)} %collective-permute-done.21.refs_0_), channel_id=1, source_target_pairs={{0,16},{16,0},{1,17},{17,1},{2,18},{18,2},{3,19},{19,3},{4,20},{20... | collective-permute-start | bytes 737288 | tf_op jit(solution)/shard_map/ppermute | solution.py:117
  68.0 8.0 %collective-permute-start.18 = (bf16[32,3840]{1,0:T(8,128)(2,1)S(1)}, bf16[32,3840]{1,0:T(8,128)(2,1)S(1)}, u32[]{:S(2)}, u32[]{:S(2)}) collective-permute-start(bf16[32,3840]{1,0:T(8,128)(2,1)S(1)} %collective-permute-done.9.refs_0_), channel_id=1, source_target_pairs={{0,4},{4,8},{8,12},{12,0},{1,5},{5,9},{9,13},{13,1},{2,6},{6,10},{... | collective-permute-start | bytes 737288 | tf_op jit(solution)/shard_map/ppermute | solution.py:111
  68.0 8.0 %collective-permute-start.19 = (bf16[32,3840]{1,0:T(8,128)(2,1)S(1)}, bf16[32,3840]{1,0:T(8,128)(2,1)S(1)}, u32[]{:S(2)}, u32[]{:S(2)}) collective-permute-start(bf16[32,3840]{1,0:T(8,128)(2,1)S(1)} %collective-permute-done.14.refs_0_), channel_id=1, source_target_pairs={{0,16},{16,0},{1,17},{17,1},{2,18},{18,2},{3,19},{19,3},{4,20},{20... | collective-permute-start | bytes 737288 | tf_op jit(solution)/shard_map/ppermute | solution.py:117
  72.9 7.5 %collective-permute-start.23 = (bf16[64,1024]{1,0:T(8,128)(2,1)S(1)}, bf16[64,1024]{1,0:T(8,128)(2,1)S(1)}, u32[]{:S(2)}, u32[]{:S(2)}) collective-permute-start(bf16[64,1024]{1,0:T(8,128)(2,1)S(1)} %collective-permute-done.13.refs_5_), channel_id=1, source_target_pairs={{0,4},{4,8},{8,12},{12,0},{1,5},{5,9},{9,13},{13,1},{2,6},{6,10},{... | collective-permute-start | bytes 393224 | tf_op jit(solution)/shard_map/ppermute | solution.py:157
  73.6 13.9 %collective-permute-start.26 = (bf16[32,3840]{1,0:T(8,128)(2,1)}, bf16[32,3840]{1,0:T(8,128)(2,1)}, u32[]{:S(2)}, u32[]{:S(2)}) collective-permute-start(bf16[32,3840]{1,0:T(8,128)(2,1)} %collective-permute-done.22.refs_0_), channel_id=1, source_target_pairs={{0,16},{16,0},{1,17},{17,1},{2,18},{18,2},{3,19},{19,3},{4,20},{20... | collective-permute-start | bytes 737288 | tf_op jit(solution)/shard_map/ppermute | solution.py:117
  76.7 12.6 %collective-permute-start.20 = (bf16[32,3840]{1,0:T(8,128)(2,1)S(1)}, bf16[32,3840]{1,0:T(8,128)(2,1)}, u32[]{:S(2)}, u32[]{:S(2)}) collective-permute-start(bf16[32,3840]{1,0:T(8,128)(2,1)S(1)} %collective-permute-done.18.refs_0_), channel_id=1, source_target_pairs={{0,16},{16,0},{1,17},{17,1},{2,18},{18,2},{3,19},{19,3},{4,20},{20... | collective-permute-start | bytes 737288 | tf_op jit(solution)/shard_map/ppermute | solution.py:117
  80.3 9.0 %collective-permute-start.24 = (bf16[64,1024]{1,0:T(8,128)(2,1)S(1)}, bf16[64,1024]{1,0:T(8,128)(2,1)}, u32[]{:S(2)}, u32[]{:S(2)}) collective-permute-start(bf16[64,1024]{1,0:T(8,128)(2,1)S(1)} %collective-permute-done.23.refs_6_), channel_id=1, source_target_pairs={{0,4},{4,8},{8,12},{12,0},{1,5},{5,9},{9,13},{13,1},{2,6},{6,10},{... | collective-permute-start | bytes 393224 | tf_op jit(solution)/shard_map/ppermute | solution.py:157
  91.3 1.4 %collective-permute-start.27 = (f32[2,64,256]{2,1,0:T(8,128)S(1)}, f32[2,64,256]{2,1,0:T(8,128)S(1)}, u32[]{:S(2)}, u32[]{:S(2)}) collective-permute-start(f32[2,64,256]{2,1,0:T(8,128)S(1)} %dynamic-slice_bitcast_fusion), channel_id=1, source_target_pairs={{0,1},{1,0},{2,3},{3,2},{4,5},{5,4},{6,7},{7,6},{8,9},{9,8},{10,11... | collective-permute-start | bytes 393224 | tf_op jit(solution)/shard_map/ppermute | solution.py:128
  92.8 4.3 %collective-permute-start.28 = (f32[1,64,256]{2,1,0:T(8,128)S(1)}, f32[1,64,256]{2,1,0:T(8,128)S(1)}, u32[]{:S(2)}, u32[]{:S(2)}) collective-permute-start(f32[1,64,256]{2,1,0:T(8,128)S(1)} %constant_dynamic-slice_fusion), channel_id=1, source_target_pairs={{0,2},{1,3},{2,0},{3,1},{4,6},{5,7},{6,4},{7,5},{8,10},{9,11},{10,... | collective-permute-start | bytes 196616 | tf_op jit(solution)/shard_map/ppermute | solution.py:128
  (25 other events, 101.7 us)

commit v17 on v16

--- a/solution.py
+++ b/solution.py
@@ -107,14 +107,17 @@
             return lax.optimization_barrier((block, waits))[0] if waits else block
 
         def hop(block, *ahead):
-            waits = hops[-2:-1] + swaps[-4:-3] + made[-5:-4] + (first if len(hops) == 3 else [])
+            waits = hops[-2:-1] + swaps[-4:-3] + made[-4:-3] + (first if len(hops) == 3 else [])
             hops.append(lax.ppermute(after(block, *waits, *ahead), "ex", ring))
             return hops[-1]
 
         def swap(block):
             if n_grp == 1:
                 return [block]
-            swaps.append(lax.ppermute(after(block, *swaps[-2:-1]), "grp", [(0, 1), (1, 0)]))
+            waits = swaps[-2:-1]
+            if len(swaps) > (n_ex - 2) * QUARTERS:
+                waits += made[-3:-2]
+            swaps.append(lax.ppermute(after(block, *waits), "grp", [(0, 1), (1, 0)]))
             return [block, swaps[-1]]
 
         def sum_over_feat(sums):

time: 98.3 us -> 98.6 us (level)
  waiting for transfers between devices: 24.5 us -> 37.6 us
  starting transfers between devices: 34.2 us -> 24.8 us
  local copies, waits for them, and re-layouts: 15 us -> 12.8 us
  other arithmetic: 6.09 us -> 4.88 us
    ppermute x12, waiting for transfers between devices: 12.2 us -> 27.4 us  [hop(): hops.append(lax.ppermute(after(block, *waits, *ahead), 'ex', ring))]
    ppermute x12, starting transfers between devices: 20 us -> 14.1 us  [swap(): swaps.append(lax.ppermute(after(block, *waits), 'grp', [(0, 1), (1, 0)]))]
    ppermute x12, starting transfers between devices: 10.8 us -> 7.51 us  [hop(): hops.append(lax.ppermute(after(block, *waits, *ahead), 'ex', ring))]
    ppermute x12, waiting for transfers between devices: 3.93 us -> 1.13 us  [swap(): swaps.append(lax.ppermute(after(block, *waits), 'grp', [(0, 1), (1, 0)]))]
    unnamed x56 -> x34, local copies, waits for them, and re-layouts: 9.72 us -> 7.65 us
    select_n x5, other arithmetic: 5.36 us -> 4.15 us  [share(): return jnp.where(grp == other, rows[:half, columns], rows[half:, columns])]
    ppermute x3, waiting for transfers between devices: 4.34 us -> 5.36 us  [whole_hop(): whole.append(lax.ppermute(after(whole[-1], hops[gate]), 'ex', ring))]
  transfers between devices with their start and end apart: 29 -> 29, of which waited for: 13 -> 17; matrix products, arithmetic and copies ran while one was open for 10% -> 8% of each run, Pallas kernels for 16% -> 16%
where the time goes in v17:
time: 98.6 us; the launch traced here: 98 us
  waiting for transfers between devices  37.6 us (38%)
  starting transfers between devices  24.8 us (25%)
  Pallas kernels  17.5 us (18%)
  local copies, waits for them, and re-layouts  12.8 us (13%)
  other arithmetic  4.88 us (5%)
    ppermute x12, waiting for transfers between devices, hop(): hops.append(lax.ppermute(after(block, *waits, *ahead), 'ex', ring))  27.4 us
    pallas_call x13, Pallas kernels, call(): pl.pallas_call(kernel, out_shape=jax.ShapeDtypeStruct((rows, docs), jnp.f...  17.5 us
    ppermute x12, starting transfers between devices, swap(): swaps.append(lax.ppermute(after(block, *waits), 'grp', [(0, 1), (1, 0)]))  14.1 us
    unnamed x34, local copies, waits for them, and re-layouts  7.65 us
    ppermute x12, starting transfers between devices, hop(): hops.append(lax.ppermute(after(block, *waits, *ahead), 'ex', ring))  7.51 us
    ppermute x3, waiting for transfers between devices, whole_hop(): whole.append(lax.ppermute(after(whole[-1], hops[gate]), 'ex', ring))  5.36 us
    select_n x5, other arithmetic, share(): return jnp.where(grp == other, rows[:half, columns], rows[half:, columns])  4.15 us
    slice x1, local copies, waits for them, and re-layouts, on_device(): trains = [train[:, start:start + quarter] for start in starts]  4.03 us
  transfers between devices with their start and end apart: 29, of which 17 were waited for; matrix products, arithmetic and copies ran while one was open for 8% of the time, Pallas kernels for 16%

profile of v17, /device:TPU:0, one launch (start us, length us, event | category | flops | bytes accessed | tf_op | source)
XLA Modules:
  0.0 98.0 jit_solution(9145422801173023875)
XLA Ops:
  1.1 3.1 %collective-permute-start.3 = (bf16[32,3840]{1,0:T(8,128)(2,1)S(1)}, bf16[32,3840]{1,0:T(8,128)(2,1)}, u32[]{:S(2)}, u32[]{:S(2)}) collective-permute-start(bf16[32,3840]{1,0:T(8,128)(2,1)S(1)} %slice_select_fusion.3), channel_id=1, source_target_pairs={{0,4},{4,8},{8,12},{12,0},{1,5},{5,9},{9,13},{13,1},{2,6},{6,10},{... | collective-permute-start | bytes 737288 | tf_op jit(solution)/shard_map/ppermute | solution.py:111
  5.3 1.6 %collective-permute-start = (bf16[32,3840]{1,0:T(8,128)(2,1)S(1)}, bf16[32,3840]{1,0:T(8,128)(2,1)S(1)}, u32[]{:S(2)}, u32[]{:S(2)}) collective-permute-start(bf16[32,3840]{1,0:T(8,128)(2,1)S(1)} %slice_select_fusion.2), channel_id=1, source_target_pairs={{0,4},{4,8},{8,12},{12,0},{1,5},{5,9},{9,13},{13,1},{2,6},{6,10},{... | collective-permute-start | bytes 737288 | tf_op jit(solution)/shard_map/ppermute | solution.py:111
  8.0 4.0 %fusion.1 = (bf16[256,4096]{1,0:T(8,128)(2,1)S(1)}, bf16[256,4096]{1,0:T(8,128)(2,1)S(1)}, bf16[256,4096]{1,0:T(8,128)(2,1)S(1)}, bf16[256,4096]{1,0:T(8,128)(2,1)S(1)}) fusion(bf16[256,16384]{1,0:T(8,128)(2,1)} %param.3), kind=kLoop, calls=%fused_computation.20 | loop fusion | bytes 16777216 | tf_op jit(solution)/shard_map/slice | solution.py:151
  13.8 1.5 %collective-permute-start.4 = (bf16[32,3840]{1,0:T(8,128)(2,1)}, bf16[32,3840]{1,0:T(8,128)(2,1)S(1)}, u32[]{:S(2)}, u32[]{:S(2)}) collective-permute-start(bf16[32,3840]{1,0:T(8,128)(2,1)} %collective-permute-done.3.refs_0_), channel_id=1, source_target_pairs={{0,16},{16,0},{1,17},{17,1},{2,18},{18,2},{3,19},{19,3},{4,20},{20... | collective-permute-start | bytes 737288 | tf_op jit(solution)/shard_map/ppermute | solution.py:120
  15.3 2.7 %shard_map.37.refs_8_ = f32[64,256]{1,0:T(8,128)S(1)} custom-call(bf16[64,16384]{1,0:T(8,128)(2,1)S(1)} %copy-done.9, f32[1,16384]{1,0:T(1,128)S(1)} %bitcast.10, bf16[256,4096]{1,0:T(8,128)(2,1)S(1)} %get-tuple-element.66.refs_0_.refs_3_, bf16[256,4096]{1,0:T(8,128)(2,1)S(1)} %get-tuple-element.65.refs_1_.refs_3_, ...), custom_call_target="tpu_custom_call" | custom-call | flops 536870912 | bytes 10485760 | tf_op jit(solution)/shard_map/pallas_call | solution.py:78
  20.0 3.9 %collective-permute-done.7.refs_0_ = bf16[32,3840]{1,0:T(8,128)(2,1)} collective-permute-done((bf16[32,3840]{1,0:T(8,128)(2,1)S(1)}, bf16[32,3840]{1,0:T(8,128)(2,1)}, u32[]{:S(2)}, u32[]{:S(2)}) %collective-permute-start.7) | collective-permute-done | bytes 245792 | tf_op jit(solution)/shard_map/ppermute | solution.py:111
  23.9 1.8 %collective-permute-start.8 = (bf16[32,3840]{1,0:T(8,128)(2,1)}, bf16[32,3840]{1,0:T(8,128)(2,1)}, u32[]{:S(2)}, u32[]{:S(2)}) collective-permute-start(bf16[32,3840]{1,0:T(8,128)(2,1)} %collective-permute-done.7.refs_0_), channel_id=1, source_target_pairs={{0,16},{16,0},{1,17},{17,1},{2,18},{18,2},{3,19},{19,3},{4,20},{20... | collective-permute-start | bytes 737288 | tf_op jit(solution)/shard_map/ppermute | solution.py:120
  25.7 1.6 %shard_map.38.refs_4_ = f32[64,256]{1,0:T(8,128)S(1)} custom-call(bf16[32,3840]{1,0:T(8,128)(2,1)} %collective-permute-done.3.refs_0_, bf16[32,3840]{1,0:T(8,128)(2,1)S(1)} %collective-permute-done.4.refs_1_, f32[1,16384]{1,0:T(1,128)S(1)} %bitcast.11, bf16[256,4096]{1,0:T(8,128)(2,1)S(1)} %get-tuple-element.66.refs_0_.refs_3_), custom_call_target="tpu_custom_call" | custom-call | flops 125829120 | bytes 2457600 | tf_op jit(solution)/shard_map/pallas_call | solution.py:78
  27.4 1.1 %fusion = (bf16[256,256]{1,0:T(8,128)(2,1)S(1)}, bf16[256,256]{1,0:T(8,128)(2,1)S(1)}, bf16[256,256]{1,0:T(8,128)(2,1)S(1)}, bf16[256,256]{1,0:T(8,128)(2,1)S(1)}) fusion(bf16[256,16384]{1,0:T(8,128)(2,1)} %param.3), kind=kLoop, calls=%fused_computation.19 | loop fusion | bytes 1048576 | tf_op jit(solution)/shard_map/slice | solution.py:152
  29.2 1.2 %collective-permute-start.5 = (bf16[32,3840]{1,0:T(8,128)(2,1)S(1)}, bf16[32,3840]{1,0:T(8,128)(2,1)}, u32[]{:S(2)}, u32[]{:S(2)}) collective-permute-start(bf16[32,3840]{1,0:T(8,128)(2,1)S(1)} %collective-permute-done.refs_0_), channel_id=1, source_target_pairs={{0,4},{4,8},{8,12},{12,0},{1,5},{5,9},{9,13},{13,1},{2,6},{6,10},{... | collective-permute-start | bytes 737288 | tf_op jit(solution)/shard_map/ppermute | solution.py:111
  32.0 1.6 %copy-done.1 = bf16[256,4096]{1,0:T(8,128)(2,1)S(1)} copy-done((bf16[256,4096]{1,0:T(8,128)(2,1)S(1)}, bf16[256,4096]{1,0:T(8,128)(2,1)}, u32[]{:S(2)}) %copy-start.1) | copy-done | bytes 2097176
  33.6 1.8 %shard_map.40.refs_4_ = f32[64,256]{1,0:T(8,128)S(1)} custom-call(bf16[32,3840]{1,0:T(8,128)(2,1)} %collective-permute-done.7.refs_0_, bf16[32,3840]{1,0:T(8,128)(2,1)} %collective-permute-done.8.refs_1_, f32[1,16384]{1,0:T(1,128)S(1)} %bitcast.13, bf16[256,4096]{1,0:T(8,128)(2,1)S(1)} %copy-done.1, f32[64,256]{1,0:T(8,128)S(1)} %shard_map.39.refs_4_), custom_call_target="tpu_custom_call" | custom-call | flops 125829120 | bytes 2457600 | tf_op jit(solution)/shard_map/pallas_call | solution.py:78
  35.4 2.1 %collective-permute-done.11.refs_0_ = bf16[32,3840]{1,0:T(8,128)(2,1)S(1)} collective-permute-done((bf16[32,3840]{1,0:T(8,128)(2,1)}, bf16[32,3840]{1,0:T(8,128)(2,1)S(1)}, u32[]{:S(2)}, u32[]{:S(2)}) %collective-permute-start.11) | collective-permute-done | bytes 245792 | tf_op jit(solution)/shard_map/ppermute | solution.py:111
  39.0 2.3 %collective-permute-done.5.refs_0_ = bf16[32,3840]{1,0:T(8,128)(2,1)} collective-permute-done((bf16[32,3840]{1,0:T(8,128)(2,1)S(1)}, bf16[32,3840]{1,0:T(8,128)(2,1)}, u32[]{:S(2)}, u32[]{:S(2)}) %collective-permute-start.5) | collective-permute-done | bytes 245792 | tf_op jit(solution)/shard_map/ppermute | solution.py:111
  41.3 1.1 %collective-permute-start.10 = (bf16[32,3840]{1,0:T(8,128)(2,1)}, bf16[32,3840]{1,0:T(8,128)(2,1)S(1)}, u32[]{:S(2)}, u32[]{:S(2)}) collective-permute-start(bf16[32,3840]{1,0:T(8,128)(2,1)} %collective-permute-done.5.refs_0_), channel_id=1, source_target_pairs={{0,16},{16,0},{1,17},{17,1},{2,18},{18,2},{3,19},{19,3},{4,20},{20... | collective-permute-start | bytes 737288 | tf_op jit(solution)/shard_map/ppermute | solution.py:120
  42.4 1.8 %shard_map.41.refs_9_ = f32[64,256]{1,0:T(8,128)S(1)} custom-call(bf16[32,3840]{1,0:T(8,128)(2,1)} %collective-permute-done.1.refs_0_, bf16[32,3840]{1,0:T(8,128)(2,1)} %collective-permute-done.6.refs_1_, f32[1,16384]{1,0:T(1,128)S(1)} %bitcast.14, bf16[256,4096]{1,0:T(8,128)(2,1)S(1)} %get-tuple-element.63.refs_3_, f32[64,256]{1,0:T(8,128)S(1)} %shard_map.40.refs_4_), custom_call_target="tpu_custom_call" | custom-call | flops 125829120 | bytes 2457600 | tf_op jit(solution)/shard_map/pallas_call | solution.py:78
  45.4 1.9 %collective-permute-done.16.refs_0_ = bf16[32,3840]{1,0:T(8,128)(2,1)S(1)} collective-permute-done((bf16[32,3840]{1,0:T(8,128)(2,1)}, bf16[32,3840]{1,0:T(8,128)(2,1)S(1)}, u32[]{:S(2)}, u32[]{:S(2)}) %collective-permute-start.16) | collective-permute-done | bytes 245792 | tf_op jit(solution)/shard_map/ppermute | solution.py:111
  47.4 2.7 %collective-permute-start.17 = (bf16[32,3840]{1,0:T(8,128)(2,1)S(1)}, bf16[32,3840]{1,0:T(8,128)(2,1)S(1)}, u32[]{:S(2)}, u32[]{:S(2)}) collective-permute-start(bf16[32,3840]{1,0:T(8,128)(2,1)S(1)} %collective-permute-done.16.refs_0_), channel_id=1, source_target_pairs={{0,16},{16,0},{1,17},{17,1},{2,18},{18,2},{3,19},{19,3},{4,20},{20... | collective-permute-start | bytes 737288 | tf_op jit(solution)/shard_map/ppermute | solution.py:120
  50.9 1.6 %shard_map.43.refs_4_ = f32[64,256]{1,0:T(8,128)S(1)} custom-call(bf16[32,3840]{1,0:T(8,128)(2,1)} %collective-permute-done.5.refs_0_, bf16[32,3840]{1,0:T(8,128)(2,1)S(1)} %collective-permute-done.10.refs_1_, f32[1,16384]{1,0:T(1,128)S(1)} %bitcast.16, bf16[256,4096]{1,0:T(8,128)(2,1)S(1)} %copy-done.5, f32[64,256]{1,0:T(8,128)S(1)} %shard_map.42.refs_4_), custom_call_target="tpu_custom_call" | custom-call | flops 125829120 | bytes 2457600 | tf_op jit(solution)/shard_map/pallas_call | solution.py:78
  52.5 2.6 %collective-permute-done.9.refs_0_ = bf16[32,3840]{1,0:T(8,128)(2,1)S(1)} collective-permute-done((bf16[32,3840]{1,0:T(8,128)(2,1)}, bf16[32,3840]{1,0:T(8,128)(2,1)S(1)}, u32[]{:S(2)}, u32[]{:S(2)}) %collective-permute-start.9) | collective-permute-done | bytes 245792 | tf_op jit(solution)/shard_map/ppermute | solution.py:111
  55.2 2.8 %collective-permute-done.13.refs_5_ = bf16[64,1024]{1,0:T(8,128)(2,1)S(1)} collective-permute-done((bf16[64,1024]{1,0:T(8,128)(2,1)S(1)}, bf16[64,1024]{1,0:T(8,128)(2,1)S(1)}, u32[]{:S(2)}, u32[]{:S(2)}) %collective-permute-start.13) | collective-permute-done | bytes 131104 | tf_op jit(solution)/shard_map/ppermute | solution.py:160
  59.6 3.6 %collective-permute-done.20.refs_0_ = bf16[32,3840]{1,0:T(8,128)(2,1)S(1)} collective-permute-done((bf16[32,3840]{1,0:T(8,128)(2,1)S(1)}, bf16[32,3840]{1,0:T(8,128)(2,1)S(1)}, u32[]{:S(2)}, u32[]{:S(2)}) %collective-permute-start.20) | collective-permute-done | bytes 245792 | tf_op jit(solution)/shard_map/ppermute | solution.py:111
  64.2 4.3 %collective-permute-done.14.refs_0_ = bf16[32,3840]{1,0:T(8,128)(2,1)S(1)} collective-permute-done((bf16[32,3840]{1,0:T(8,128)(2,1)}, bf16[32,3840]{1,0:T(8,128)(2,1)S(1)}, u32[]{:S(2)}, u32[]{:S(2)}) %collective-permute-start.14) | collective-permute-done | bytes 245792 | tf_op jit(solution)/shard_map/ppermute | solution.py:111
  70.2 3.8 %collective-permute-done.23.refs_0_ = bf16[32,3840]{1,0:T(8,128)(2,1)} collective-permute-done((bf16[32,3840]{1,0:T(8,128)(2,1)S(1)}, bf16[32,3840]{1,0:T(8,128)(2,1)}, u32[]{:S(2)}, u32[]{:S(2)}) %collective-permute-start.23) | collective-permute-done | bytes 245792 | tf_op jit(solution)/shard_map/ppermute | solution.py:111
  75.7 1.6 %collective-permute-done.18.refs_0_ = bf16[32,3840]{1,0:T(8,128)(2,1)S(1)} collective-permute-done((bf16[32,3840]{1,0:T(8,128)(2,1)S(1)}, bf16[32,3840]{1,0:T(8,128)(2,1)S(1)}, u32[]{:S(2)}, u32[]{:S(2)}) %collective-permute-start.18) | collective-permute-done | bytes 245792 | tf_op jit(solution)/shard_map/ppermute | solution.py:111
  79.0 2.5 %collective-permute-done.24.refs_6_ = bf16[64,1024]{1,0:T(8,128)(2,1)S(1)} collective-permute-done((bf16[64,1024]{1,0:T(8,128)(2,1)S(1)}, bf16[64,1024]{1,0:T(8,128)(2,1)S(1)}, u32[]{:S(2)}, u32[]{:S(2)}) %collective-permute-start.24) | collective-permute-done | bytes 131104 | tf_op jit(solution)/shard_map/ppermute | solution.py:160
  81.6 1.6 %copy-done.6 = bf16[256,4096]{1,0:T(8,128)(2,1)S(1)} copy-done((bf16[256,4096]{1,0:T(8,128)(2,1)S(1)}, bf16[256,4096]{1,0:T(8,128)(2,1)}, u32[]{:S(2)}) %copy-start.6) | copy-done | bytes 2097176
  86.7 1.8 %shard_map.48.refs_11_ = f32[64,256]{1,0:T(8,128)S(1)} custom-call(bf16[32,3840]{1,0:T(8,128)(2,1)} %collective-permute-done.23.refs_0_, bf16[32,3840]{1,0:T(8,128)(2,1)} %collective-permute-done.26.refs_1_, f32[1,16384]{1,0:T(1,128)S(1)} %bitcast.21, bf16[256,4096]{1,0:T(8,128)(2,1)S(1)} %copy-done.3, f32[64,256]{1,0:T(8,128)S(1)} %shard_map.47.refs_4_), custom_call_target="tpu_custom_call" | custom-call | flops 125829120 | bytes 2457600 | tf_op jit(solution)/shard_map/pallas_call | solution.py:78
  89.4 1.9 %shard_map.49 = f32[256,256]{1,0:T(8,128)S(1)} custom-call(bf16[32,3840]{1,0:T(8,128)(2,1)S(1)} %collective-permute-done.18.refs_0_, bf16[32,3840]{1,0:T(8,128)(2,1)} %collective-permute-done.22.refs_1_, f32[1,16384]{1,0:T(1,128)S(1)} %bitcast.22, bf16[256,4096]{1,0:T(8,128)(2,1)S(1)} %get-tuple-element.63.refs_3_, ...), custom_call_target="tpu_custom_call" | custom-call | flops 1006632960 | bytes 7864320 | tf_op jit(solution)/shard_map/pallas_call | solution.py:78
  91.5 1.3 %collective-permute-done.27 = f32[2,64,256]{2,1,0:T(8,128)S(1)} collective-permute-done((f32[2,64,256]{2,1,0:T(8,128)S(1)}, f32[2,64,256]{2,1,0:T(8,128)S(1)}, u32[]{:S(2)}, u32[]{:S(2)}) %collective-permute-start.27) | collective-permute-done | bytes 131104 | tf_op jit(solution)/shard_map/ppermute | solution.py:131
  92.9 2.1 %collective-permute-start.28 = (f32[1,64,256]{2,1,0:T(8,128)S(1)}, f32[1,64,256]{2,1,0:T(8,128)S(1)}, u32[]{:S(2)}, u32[]{:S(2)}) collective-permute-start(f32[1,64,256]{2,1,0:T(8,128)S(1)} %constant_dynamic-slice_fusion), channel_id=1, source_target_pairs={{0,2},{1,3},{2,0},{3,1},{4,6},{5,7},{6,4},{7,5},{8,10},{9,11},{10,... | collective-permute-start | bytes 196616 | tf_op jit(solution)/shard_map/ppermute | solution.py:131
  95.0 2.4 %collective-permute-done.28 = f32[1,64,256]{2,1,0:T(8,128)S(1)} collective-permute-done((f32[1,64,256]{2,1,0:T(8,128)S(1)}, f32[1,64,256]{2,1,0:T(8,128)S(1)}, u32[]{:S(2)}, u32[]{:S(2)}) %collective-permute-start.28) | collective-permute-done | bytes 65568 | tf_op jit(solution)/shard_map/ppermute | solution.py:131
  (87 shorter events, 25.6 us)
Async XLA Ops:
  1.1 12.0 %collective-permute-start.3 = (bf16[32,3840]{1,0:T(8,128)(2,1)S(1)}, bf16[32,3840]{1,0:T(8,128)(2,1)}, u32[]{:S(2)}, u32[]{:S(2)}) collective-permute-start(bf16[32,3840]{1,0:T(8,128)(2,1)S(1)} %slice_select_fusion.3), channel_id=1, source_target_pairs={{0,4},{4,8},{8,12},{12,0},{1,5},{5,9},{9,13},{13,1},{2,6},{6,10},{... | collective-permute-start | bytes 737288 | tf_op jit(solution)/shard_map/ppermute | solution.py:111
  5.3 13.0 %collective-permute-start = (bf16[32,3840]{1,0:T(8,128)(2,1)S(1)}, bf16[32,3840]{1,0:T(8,128)(2,1)S(1)}, u32[]{:S(2)}, u32[]{:S(2)}) collective-permute-start(bf16[32,3840]{1,0:T(8,128)(2,1)S(1)} %slice_select_fusion.2), channel_id=1, source_target_pairs={{0,4},{4,8},{8,12},{12,0},{1,5},{5,9},{9,13},{13,1},{2,6},{6,10},{... | collective-permute-start | bytes 737288 | tf_op jit(solution)/shard_map/ppermute | solution.py:111
  12.1 16.5 %copy-start.4 = (bf16[256,4096]{1,0:T(8,128)(2,1)}, bf16[256,4096]{1,0:T(8,128)(2,1)S(1)}, u32[]{:S(2)}) copy-start(bf16[256,4096]{1,0:T(8,128)(2,1)S(1)} %get-tuple-element.65.refs_1_.refs_3_) | copy-start | bytes 6291460
  13.1 10.8 %collective-permute-start.7 = (bf16[32,3840]{1,0:T(8,128)(2,1)S(1)}, bf16[32,3840]{1,0:T(8,128)(2,1)}, u32[]{:S(2)}, u32[]{:S(2)}) collective-permute-start(bf16[32,3840]{1,0:T(8,128)(2,1)S(1)} %slice_select_fusion.1), channel_id=1, source_target_pairs={{0,4},{4,8},{8,12},{12,0},{1,5},{5,9},{9,13},{13,1},{2,6},{6,10},{... | collective-permute-start | bytes 737288 | tf_op jit(solution)/shard_map/ppermute | solution.py:111
  13.8 10.1 %collective-permute-start.4 = (bf16[32,3840]{1,0:T(8,128)(2,1)}, bf16[32,3840]{1,0:T(8,128)(2,1)S(1)}, u32[]{:S(2)}, u32[]{:S(2)}) collective-permute-start(bf16[32,3840]{1,0:T(8,128)(2,1)} %collective-permute-done.3.refs_0_), channel_id=1, source_target_pairs={{0,16},{16,0},{1,17},{17,1},{2,18},{18,2},{3,19},{19,3},{4,20},{20... | collective-permute-start | bytes 737288 | tf_op jit(solution)/shard_map/ppermute | solution.py:120
  18.2 10.3 %collective-permute-start.1 = (bf16[32,3840]{1,0:T(8,128)(2,1)S(1)}, bf16[32,3840]{1,0:T(8,128)(2,1)}, u32[]{:S(2)}, u32[]{:S(2)}) collective-permute-start(bf16[32,3840]{1,0:T(8,128)(2,1)S(1)} %slice_select_fusion), channel_id=1, source_target_pairs={{0,4},{4,8},{8,12},{12,0},{1,5},{5,9},{9,13},{13,1},{2,6},{6,10},{... | collective-permute-start | bytes 737288 | tf_op jit(solution)/shard_map/ppermute | solution.py:111
  19.0 9.5 %collective-permute-start.2 = (bf16[32,3840]{1,0:T(8,128)(2,1)S(1)}, bf16[32,3840]{1,0:T(8,128)(2,1)S(1)}, u32[]{:S(2)}, u32[]{:S(2)}) collective-permute-start(bf16[32,3840]{1,0:T(8,128)(2,1)S(1)} %collective-permute-done.refs_0_), channel_id=1, source_target_pairs={{0,16},{16,0},{1,17},{17,1},{2,18},{18,2},{3,19},{19,3},{4,20},{20... | collective-permute-start | bytes 737288 | tf_op jit(solution)/shard_map/ppermute | solution.py:120
  23.9 8.1 %collective-permute-start.8 = (bf16[32,3840]{1,0:T(8,128)(2,1)}, bf16[32,3840]{1,0:T(8,128)(2,1)}, u32[]{:S(2)}, u32[]{:S(2)}) collective-permute-start(bf16[32,3840]{1,0:T(8,128)(2,1)} %collective-permute-done.7.refs_0_), channel_id=1, source_target_pairs={{0,16},{16,0},{1,17},{17,1},{2,18},{18,2},{3,19},{19,3},{4,20},{20... | collective-permute-start | bytes 737288 | tf_op jit(solution)/shard_map/ppermute | solution.py:120
  27.3 10.2 %collective-permute-start.11 = (bf16[32,3840]{1,0:T(8,128)(2,1)}, bf16[32,3840]{1,0:T(8,128)(2,1)S(1)}, u32[]{:S(2)}, u32[]{:S(2)}) collective-permute-start(bf16[32,3840]{1,0:T(8,128)(2,1)} %collective-permute-done.3.refs_0_), channel_id=1, source_target_pairs={{0,4},{4,8},{8,12},{12,0},{1,5},{5,9},{9,13},{13,1},{2,6},{6,10},{... | collective-permute-start | bytes 737288 | tf_op jit(solution)/shard_map/ppermute | solution.py:111
  29.2 12.1 %collective-permute-start.5 = (bf16[32,3840]{1,0:T(8,128)(2,1)S(1)}, bf16[32,3840]{1,0:T(8,128)(2,1)}, u32[]{:S(2)}, u32[]{:S(2)}) collective-permute-start(bf16[32,3840]{1,0:T(8,128)(2,1)S(1)} %collective-permute-done.refs_0_), channel_id=1, source_target_pairs={{0,4},{4,8},{8,12},{12,0},{1,5},{5,9},{9,13},{13,1},{2,6},{6,10},{... | collective-permute-start | bytes 737288 | tf_op jit(solution)/shard_map/ppermute | solution.py:111
  30.4 10.9 %collective-permute-start.6 = (bf16[32,3840]{1,0:T(8,128)(2,1)}, bf16[32,3840]{1,0:T(8,128)(2,1)}, u32[]{:S(2)}, u32[]{:S(2)}) collective-permute-start(bf16[32,3840]{1,0:T(8,128)(2,1)} %collective-permute-done.1.refs_0_), channel_id=1, source_target_pairs={{0,16},{16,0},{1,17},{17,1},{2,18},{18,2},{3,19},{19,3},{4,20},{20... | collective-permute-start | bytes 737288 | tf_op jit(solution)/shard_map/ppermute | solution.py:120
  35.4 14.7 %copy-start.8 = (bf16[256,4096]{1,0:T(8,128)(2,1)S(1)}, bf16[256,4096]{1,0:T(8,128)(2,1)}, u32[]{:S(2)}) copy-start(bf16[256,4096]{1,0:T(8,128)(2,1)} %copy-done.7) | copy-start | bytes 6291460
  37.5 7.9 %collective-permute-start.12 = (bf16[32,3840]{1,0:T(8,128)(2,1)S(1)}, bf16[32,3840]{1,0:T(8,128)(2,1)S(1)}, u32[]{:S(2)}, u32[]{:S(2)}) collective-permute-start(bf16[32,3840]{1,0:T(8,128)(2,1)S(1)} %collective-permute-done.11.refs_0_), channel_id=1, source_target_pairs={{0,16},{16,0},{1,17},{17,1},{2,18},{18,2},{3,19},{19,3},{4,20},{20... | collective-permute-start | bytes 737288 | tf_op jit(solution)/shard_map/ppermute | solution.py:120
  38.1 9.2 %collective-permute-start.16 = (bf16[32,3840]{1,0:T(8,128)(2,1)}, bf16[32,3840]{1,0:T(8,128)(2,1)S(1)}, u32[]{:S(2)}, u32[]{:S(2)}) collective-permute-start(bf16[32,3840]{1,0:T(8,128)(2,1)} %collective-permute-done.7.refs_0_), channel_id=1, source_target_pairs={{0,4},{4,8},{8,12},{12,0},{1,5},{5,9},{9,13},{13,1},{2,6},{6,10},{... | collective-permute-start | bytes 737288 | tf_op jit(solution)/shard_map/ppermute | solution.py:111
  41.3 9.5 %collective-permute-start.10 = (bf16[32,3840]{1,0:T(8,128)(2,1)}, bf16[32,3840]{1,0:T(8,128)(2,1)S(1)}, u32[]{:S(2)}, u32[]{:S(2)}) collective-permute-start(bf16[32,3840]{1,0:T(8,128)(2,1)} %collective-permute-done.5.refs_0_), channel_id=1, source_target_pairs={{0,16},{16,0},{1,17},{17,1},{2,18},{18,2},{3,19},{19,3},{4,20},{20... | collective-permute-start | bytes 737288 | tf_op jit(solution)/shard_map/ppermute | solution.py:120
  44.2 11.0 %collective-permute-start.9 = (bf16[32,3840]{1,0:T(8,128)(2,1)}, bf16[32,3840]{1,0:T(8,128)(2,1)S(1)}, u32[]{:S(2)}, u32[]{:S(2)}) collective-permute-start(bf16[32,3840]{1,0:T(8,128)(2,1)} %collective-permute-done.1.refs_0_), channel_id=1, source_target_pairs={{0,4},{4,8},{8,12},{12,0},{1,5},{5,9},{9,13},{13,1},{2,6},{6,10},{... | collective-permute-start | bytes 737288 | tf_op jit(solution)/shard_map/ppermute | solution.py:111
  44.3 14.6 %copy-start.2 = (bf16[256,4096]{1,0:T(8,128)(2,1)S(1)}, bf16[256,4096]{1,0:T(8,128)(2,1)}, u32[]{:S(2)}) copy-start(bf16[256,4096]{1,0:T(8,128)(2,1)} %copy-done) | copy-start | bytes 6291460
  44.3 13.7 %collective-permute-start.13 = (bf16[64,1024]{1,0:T(8,128)(2,1)S(1)}, bf16[64,1024]{1,0:T(8,128)(2,1)S(1)}, u32[]{:S(2)}, u32[]{:S(2)}) collective-permute-start(bf16[64,1024]{1,0:T(8,128)(2,1)S(1)} %maximum_maximum_fusion), channel_id=1, source_target_pairs={{0,4},{4,8},{8,12},{12,0},{1,5},{5,9},{9,13},{13,1},{2,6},{6,10},{... | collective-permute-start | bytes 393224 | tf_op jit(solution)/shard_map/ppermute | solution.py:160
  47.4 11.6 %collective-permute-start.17 = (bf16[32,3840]{1,0:T(8,128)(2,1)S(1)}, bf16[32,3840]{1,0:T(8,128)(2,1)S(1)}, u32[]{:S(2)}, u32[]{:S(2)}) collective-permute-start(bf16[32,3840]{1,0:T(8,128)(2,1)S(1)} %collective-permute-done.16.refs_0_), channel_id=1, source_target_pairs={{0,16},{16,0},{1,17},{17,1},{2,18},{18,2},{3,19},{19,3},{4,20},{20... | collective-permute-start | bytes 737288 | tf_op jit(solution)/shard_map/ppermute | solution.py:120
  50.8 12.5 %collective-permute-start.20 = (bf16[32,3840]{1,0:T(8,128)(2,1)S(1)}, bf16[32,3840]{1,0:T(8,128)(2,1)S(1)}, u32[]{:S(2)}, u32[]{:S(2)}) collective-permute-start(bf16[32,3840]{1,0:T(8,128)(2,1)S(1)} %collective-permute-done.11.refs_0_), channel_id=1, source_target_pairs={{0,4},{4,8},{8,12},{12,0},{1,5},{5,9},{9,13},{13,1},{2,6},{6,10},{... | collective-permute-start | bytes 737288 | tf_op jit(solution)/shard_map/ppermute | solution.py:111
  58.0 10.4 %collective-permute-start.14 = (bf16[32,3840]{1,0:T(8,128)(2,1)}, bf16[32,3840]{1,0:T(8,128)(2,1)S(1)}, u32[]{:S(2)}, u32[]{:S(2)}) collective-permute-start(bf16[32,3840]{1,0:T(8,128)(2,1)} %collective-permute-done.5.refs_0_), channel_id=1, source_target_pairs={{0,4},{4,8},{8,12},{12,0},{1,5},{5,9},{9,13},{13,1},{2,6},{6,10},{... | collective-permute-start | bytes 737288 | tf_op jit(solution)/shard_map/ppermute | solution.py:111
  58.0 10.4 %collective-permute-start.15 = (bf16[32,3840]{1,0:T(8,128)(2,1)S(1)}, bf16[32,3840]{1,0:T(8,128)(2,1)S(1)}, u32[]{:S(2)}, u32[]{:S(2)}) collective-permute-start(bf16[32,3840]{1,0:T(8,128)(2,1)S(1)} %collective-permute-done.9.refs_0_), channel_id=1, source_target_pairs={{0,16},{16,0},{1,17},{17,1},{2,18},{18,2},{3,19},{19,3},{4,20},{20... | collective-permute-start | bytes 737288 | tf_op jit(solution)/shard_map/ppermute | solution.py:120
  63.3 10.8 %collective-permute-start.23 = (bf16[32,3840]{1,0:T(8,128)(2,1)S(1)}, bf16[32,3840]{1,0:T(8,128)(2,1)}, u32[]{:S(2)}, u32[]{:S(2)}) collective-permute-start(bf16[32,3840]{1,0:T(8,128)(2,1)S(1)} %collective-permute-done.16.refs_0_), channel_id=1, source_target_pairs={{0,4},{4,8},{8,12},{12,0},{1,5},{5,9},{9,13},{13,1},{2,6},{6,10},{... | collective-permute-start | bytes 737288 | tf_op jit(solution)/shard_map/ppermute | solution.py:111
  63.3 10.8 %collective-permute-start.21 = (bf16[32,3840]{1,0:T(8,128)(2,1)S(1)}, bf16[32,3840]{1,0:T(8,128)(2,1)S(1)}, u32[]{:S(2)}, u32[]{:S(2)}) collective-permute-start(bf16[32,3840]{1,0:T(8,128)(2,1)S(1)} %collective-permute-done.20.refs_0_), channel_id=1, source_target_pairs={{0,16},{16,0},{1,17},{17,1},{2,18},{18,2},{3,19},{19,3},{4,20},{20... | collective-permute-start | bytes 737288 | tf_op jit(solution)/shard_map/ppermute | solution.py:120
  69.2 8.1 %collective-permute-start.18 = (bf16[32,3840]{1,0:T(8,128)(2,1)S(1)}, bf16[32,3840]{1,0:T(8,128)(2,1)S(1)}, u32[]{:S(2)}, u32[]{:S(2)}) collective-permute-start(bf16[32,3840]{1,0:T(8,128)(2,1)S(1)} %collective-permute-done.9.refs_0_), channel_id=1, source_target_pairs={{0,4},{4,8},{8,12},{12,0},{1,5},{5,9},{9,13},{13,1},{2,6},{6,10},{... | collective-permute-start | bytes 737288 | tf_op jit(solution)/shard_map/ppermute | solution.py:111
  69.2 8.0 %collective-permute-start.19 = (bf16[32,3840]{1,0:T(8,128)(2,1)S(1)}, bf16[32,3840]{1,0:T(8,128)(2,1)S(1)}, u32[]{:S(2)}, u32[]{:S(2)}) collective-permute-start(bf16[32,3840]{1,0:T(8,128)(2,1)S(1)} %collective-permute-done.14.refs_0_), channel_id=1, source_target_pairs={{0,16},{16,0},{1,17},{17,1},{2,18},{18,2},{3,19},{19,3},{4,20},{20... | collective-permute-start | bytes 737288 | tf_op jit(solution)/shard_map/ppermute | solution.py:120
  74.1 7.5 %collective-permute-start.24 = (bf16[64,1024]{1,0:T(8,128)(2,1)S(1)}, bf16[64,1024]{1,0:T(8,128)(2,1)S(1)}, u32[]{:S(2)}, u32[]{:S(2)}) collective-permute-start(bf16[64,1024]{1,0:T(8,128)(2,1)S(1)} %collective-permute-done.13.refs_5_), channel_id=1, source_target_pairs={{0,4},{4,8},{8,12},{12,0},{1,5},{5,9},{9,13},{13,1},{2,6},{6,10},{... | collective-permute-start | bytes 393224 | tf_op jit(solution)/shard_map/ppermute | solution.py:160
  74.1 11.8 %collective-permute-start.26 = (bf16[32,3840]{1,0:T(8,128)(2,1)}, bf16[32,3840]{1,0:T(8,128)(2,1)}, u32[]{:S(2)}, u32[]{:S(2)}) collective-permute-start(bf16[32,3840]{1,0:T(8,128)(2,1)} %collective-permute-done.23.refs_0_), channel_id=1, source_target_pairs={{0,16},{16,0},{1,17},{17,1},{2,18},{18,2},{3,19},{19,3},{4,20},{20... | collective-permute-start | bytes 737288 | tf_op jit(solution)/shard_map/ppermute | solution.py:120
  77.9 10.6 %collective-permute-start.22 = (bf16[32,3840]{1,0:T(8,128)(2,1)S(1)}, bf16[32,3840]{1,0:T(8,128)(2,1)}, u32[]{:S(2)}, u32[]{:S(2)}) collective-permute-start(bf16[32,3840]{1,0:T(8,128)(2,1)S(1)} %collective-permute-done.18.refs_0_), channel_id=1, source_target_pairs={{0,16},{16,0},{1,17},{17,1},{2,18},{18,2},{3,19},{19,3},{4,20},{20... | collective-permute-start | bytes 737288 | tf_op jit(solution)/shard_map/ppermute | solution.py:120
  81.6 7.0 %collective-permute-start.25 = (bf16[64,1024]{1,0:T(8,128)(2,1)S(1)}, bf16[64,1024]{1,0:T(8,128)(2,1)}, u32[]{:S(2)}, u32[]{:S(2)}) collective-permute-start(bf16[64,1024]{1,0:T(8,128)(2,1)S(1)} %collective-permute-done.24.refs_6_), channel_id=1, source_target_pairs={{0,4},{4,8},{8,12},{12,0},{1,5},{5,9},{9,13},{13,1},{2,6},{6,10},{... | collective-permute-start | bytes 393224 | tf_op jit(solution)/shard_map/ppermute | solution.py:160
  91.4 1.4 %collective-permute-start.27 = (f32[2,64,256]{2,1,0:T(8,128)S(1)}, f32[2,64,256]{2,1,0:T(8,128)S(1)}, u32[]{:S(2)}, u32[]{:S(2)}) collective-permute-start(f32[2,64,256]{2,1,0:T(8,128)S(1)} %dynamic-slice_bitcast_fusion), channel_id=1, source_target_pairs={{0,1},{1,0},{2,3},{3,2},{4,5},{5,4},{6,7},{7,6},{8,9},{9,8},{10,11... | collective-permute-start | bytes 393224 | tf_op jit(solution)/shard_map/ppermute | solution.py:131
  92.9 4.5 %collective-permute-start.28 = (f32[1,64,256]{2,1,0:T(8,128)S(1)}, f32[1,64,256]{2,1,0:T(8,128)S(1)}, u32[]{:S(2)}, u32[]{:S(2)}) collective-permute-start(f32[1,64,256]{2,1,0:T(8,128)S(1)} %constant_dynamic-slice_fusion), channel_id=1, source_target_pairs={{0,2},{1,3},{2,0},{3,1},{4,6},{5,7},{6,4},{7,5},{8,10},{9,11},{10,... | collective-permute-start | bytes 196616 | tf_op jit(solution)/shard_map/ppermute | solution.py:131
  (14 other events, 60.0 us)

commit v18 on v17

--- a/solution.py
+++ b/solution.py
@@ -45,7 +45,7 @@
     refs[-1][...] = total + refs[n_parts + 2][...] if has_base else total
 
 
-def last_kernel(n_grp, n_ex, starts, unit, n_parts, *refs):
+def last_kernel(n_grp, n_ex, n_feat, starts, unit, n_parts, *refs):
     parts, (scale, train, end_train), refs = refs[:n_parts], refs[n_parts : n_parts + 3], refs[n_parts + 3 :]
     wholes, sums, (out, kept) = refs[: n_ex - 1], refs[n_ex - 1 : -2], refs[-2:]
     width = parts[0].shape[1]
@@ -64,14 +64,16 @@
         if t == n_ex - 1:
             value += total
         kept[t * queries : (t + 1) * queries, :] = value
-    ex, grp = lax.axis_index("ex"), lax.axis_index("grp")
-    for b in range(n_ex):
-        t = lax.rem(ex + (n_ex - b), n_ex)
-        for h in range(n_grp):
-            place = jnp.where(t == 0, h, lax.rem(h + n_grp - grp, n_grp))
-            at = pl.multiple_of(t * queries + place * half, half)
-            to = b * queries + h * half
-            out[to : to + half, :] = kept[pl.ds(at, half), :]
+    ex, grp, feat = (lax.axis_index(a) for a in ("ex", "grp", "feat"))
+    units = n_ex * n_grp
+    each = units // n_feat
+    for to in range(units):
+        unit_of = (feat ^ (to // each)) * each + to % each
+        t = lax.rem(ex + (n_ex - lax.div(unit_of, n_grp)), n_ex)
+        h = lax.rem(unit_of, n_grp)
+        place = jnp.where(t == 0, h, lax.rem(h + n_grp - grp, n_grp))
+        at = pl.multiple_of(t * queries + place * half, half)
+        out[to * half : (to + 1) * half, :] = kept[pl.ds(at, half), :]
 
 
 def call(kernel, rows, docs, width, operands, scratch=()):
@@ -99,7 +101,7 @@
         unit = 8 * LANES
         quarter = feats // QUARTERS
         width = int(quarter * SHARE) // LANES * LANES
-        grp, feat = lax.axis_index("grp"), lax.axis_index("feat")
+        first_grp = lax.axis_index("grp") == 0
         ring = [(i, (i + 1) % n_ex) for i in range(n_ex)]
         hops, swaps, made, first = [], [], [], []
 
@@ -125,17 +127,16 @@
             bit = 1
             while bit < n_feat:
                 pairs = held.reshape((-1, 2) + held.shape[1:])
-                mine = (feat // bit) % 2
-                keep = lax.dynamic_index_in_dim(pairs, mine, 1, keepdims=False)
-                away = lax.dynamic_index_in_dim(pairs, 1 - mine, 1, keepdims=False)
-                held = keep + lax.ppermute(away, "feat", [(i, i ^ bit) for i in range(n_feat)])
+                partner = [(i, i ^ bit) for i in range(n_feat)]
+                held = pairs[:, 0] + lax.ppermute(pairs[:, 1], "feat", partner)
                 bit *= 2
             return held[0]
 
         def share(rows, columns, other=0):
             if n_grp == 1:
                 return rows[:, columns]
-            return jnp.where(grp == other, rows[:half, columns], rows[half:, columns])
+            low, high = rows[:half, columns], rows[half:, columns]
+            return jnp.where(first_grp, high, low) if other else jnp.where(first_grp, low, high)
 
         scale = (1.0 / (hess + jnp.float32(0.1))).reshape(1, feats)
         starts = [c * quarter for c in range(QUARTERS)]
@@ -178,7 +179,7 @@
         while len(whole) < n_ex:
             whole_hop(-2)
         total = call(
-            functools.partial(last_kernel, n_grp, n_ex, starts, unit, len(operands) - 2),
+            functools.partial(last_kernel, n_grp, n_ex, n_feat, starts, unit, len(operands) - 2),
             n_ex * queries, docs, 2 * width, [*operands, end_train, *whole[1:], *sums],
             [pltpu.VMEM((n_ex * queries, docs), jnp.float32)],
         )

time: 98.6 us -> 94.3 us (0.956)
  waiting for transfers between devices: 37.6 us -> 46.3 us
  local copies, waits for them, and re-layouts: 12.8 us -> 5.25 us
  Pallas kernels: 17.5 us -> 11.3 us
  starting transfers between devices: 24.8 us -> 27 us
    unnamed x34 -> x4, local copies, waits for them, and re-layouts: 7.65 us -> 0.01 us
    pallas_call x13, Pallas kernels: 17.5 us -> 11.3 us  [call(): pl.pallas_call(kernel, out_shape=jax.ShapeDtypeStruct((rows, docs), jnp.f...]
    ppermute x3, waiting for transfers between devices: 5.36 us -> 10.4 us  [whole_hop(): whole.append(lax.ppermute(after(whole[-1], hops[gate]), 'ex', ring))]
    ppermute x12, starting transfers between devices: 14.1 us -> 16.7 us  [swap(): swaps.append(lax.ppermute(after(block, *waits), 'grp', [(0, 1), (1, 0)]))]
    ppermute x12, waiting for transfers between devices: 1.13 us -> 3.69 us  [swap(): swaps.append(lax.ppermute(after(block, *waits), 'grp', [(0, 1), (1, 0)]))]
  transfers between devices with their start and end apart: 29 -> 29, of which waited for: 17 -> 21; matrix products, arithmetic and copies ran while one was open for 8% -> 8% of each run, Pallas kernels for 16% -> 11%
where the time goes in v18:
time: 94.3 us; the launch traced here: 94.1 us
  waiting for transfers between devices  46.3 us (49%)
  starting transfers between devices  27 us (29%)
  Pallas kernels  11.3 us (12%)
  local copies, waits for them, and re-layouts  5.25 us (6%)
  other arithmetic  4.05 us (4%)
    ppermute x12, waiting for transfers between devices, hop(): hops.append(lax.ppermute(after(block, *waits, *ahead), 'ex', ring))  27.8 us
    ppermute x12, starting transfers between devices, swap(): swaps.append(lax.ppermute(after(block, *waits), 'grp', [(0, 1), (1, 0)]))  16.7 us
    pallas_call x13, Pallas kernels, call(): pl.pallas_call(kernel, out_shape=jax.ShapeDtypeStruct((rows, docs), jnp.f...  11.3 us
    ppermute x3, waiting for transfers between devices, whole_hop(): whole.append(lax.ppermute(after(whole[-1], hops[gate]), 'ex', ring))  10.4 us
    ppermute x12, starting transfers between devices, hop(): hops.append(lax.ppermute(after(block, *waits, *ahead), 'ex', ring))  7.72 us
    ppermute x2, waiting for transfers between devices, sum_over_feat(): held = pairs[:, 0] + lax.ppermute(pairs[:, 1], 'feat', partner)  4.45 us
    slice x1, local copies, waits for them, and re-layouts, on_device(): trains = [train[:, start:start + quarter] for start in starts]  4.08 us
    ppermute x12, waiting for transfers between devices, swap(): swaps.append(lax.ppermute(after(block, *waits), 'grp', [(0, 1), (1, 0)]))  3.69 us
  transfers between devices with their start and end apart: 29, of which 21 were waited for; matrix products, arithmetic and copies ran while one was open for 8% of the time, Pallas kernels for 11%

profile of v18, /device:TPU:0, one launch (start us, length us, event | category | flops | bytes accessed | tf_op | source)
XLA Modules:
  0.0 94.1 jit_solution(11342878102408608485)
XLA Ops:
  1.1 3.1 %collective-permute-start.3 = (bf16[32,3840]{1,0:T(8,128)(2,1)S(1)}, bf16[32,3840]{1,0:T(8,128)(2,1)S(1)}, u32[]{:S(2)}, u32[]{:S(2)}) collective-permute-start(bf16[32,3840]{1,0:T(8,128)(2,1)S(1)} %slice_select_fusion.3), channel_id=1, source_target_pairs={{0,4},{4,8},{8,12},{12,0},{1,5},{5,9},{9,13},{13,1},{2,6},{6,10},{... | collective-permute-start | bytes 737288 | tf_op jit(solution)/shard_map/ppermute | solution.py:113
  5.3 1.6 %collective-permute-start = (bf16[32,3840]{1,0:T(8,128)(2,1)S(1)}, bf16[32,3840]{1,0:T(8,128)(2,1)S(1)}, u32[]{:S(2)}, u32[]{:S(2)}) collective-permute-start(bf16[32,3840]{1,0:T(8,128)(2,1)S(1)} %slice_select_fusion.2), channel_id=1, source_target_pairs={{0,4},{4,8},{8,12},{12,0},{1,5},{5,9},{9,13},{13,1},{2,6},{6,10},{... | collective-permute-start | bytes 737288 | tf_op jit(solution)/shard_map/ppermute | solution.py:113
  8.0 4.1 %fusion.5 = (bf16[256,4096]{1,0:T(8,128)(2,1)S(1)}, bf16[256,4096]{1,0:T(8,128)(2,1)S(1)}, bf16[256,4096]{1,0:T(8,128)(2,1)S(1)}, bf16[256,4096]{1,0:T(8,128)(2,1)S(1)}) fusion(bf16[256,16384]{1,0:T(8,128)(2,1)} %param.3), kind=kLoop, calls=%fused_computation.24 | loop fusion | bytes 16777216 | tf_op jit(solution)/shard_map/slice | solution.py:152
  13.8 1.5 %collective-permute-start.4 = (bf16[32,3840]{1,0:T(8,128)(2,1)S(1)}, bf16[32,3840]{1,0:T(8,128)(2,1)S(1)}, u32[]{:S(2)}, u32[]{:S(2)}) collective-permute-start(bf16[32,3840]{1,0:T(8,128)(2,1)S(1)} %collective-permute-done.3.refs_0_), channel_id=1, source_target_pairs={{0,16},{16,0},{1,17},{17,1},{2,18},{18,2},{3,19},{19,3},{4,20},{20... | collective-permute-start | bytes 737288 | tf_op jit(solution)/shard_map/ppermute | solution.py:122
  15.3 2.7 %shard_map.37.refs_8_ = f32[64,256]{1,0:T(8,128)S(1)} custom-call(bf16[64,16384]{1,0:T(8,128)(2,1)S(1)} %copy-done, f32[1,16384]{1,0:T(1,128)S(1)} %bitcast.28, bf16[256,4096]{1,0:T(8,128)(2,1)S(1)} %get-tuple-element.66.refs_0_.refs_3_, bf16[256,4096]{1,0:T(8,128)(2,1)S(1)} %get-tuple-element.65.refs_1_.refs_3_, ...), custom_call_target="tpu_custom_call" | custom-call | flops 536870912 | bytes 10485760 | tf_op jit(solution)/shard_map/pallas_call | solution.py:80
  18.9 1.2 %collective-permute-start.2 = (bf16[32,3840]{1,0:T(8,128)(2,1)S(1)}, bf16[32,3840]{1,0:T(8,128)(2,1)S(1)}, u32[]{:S(2)}, u32[]{:S(2)}) collective-permute-start(bf16[32,3840]{1,0:T(8,128)(2,1)S(1)} %collective-permute-done.refs_0_), channel_id=1, source_target_pairs={{0,16},{16,0},{1,17},{17,1},{2,18},{18,2},{3,19},{19,3},{4,20},{20... | collective-permute-start | bytes 737288 | tf_op jit(solution)/shard_map/ppermute | solution.py:122
  20.0 3.7 %collective-permute-done.7.refs_0_ = bf16[32,3840]{1,0:T(8,128)(2,1)S(1)} collective-permute-done((bf16[32,3840]{1,0:T(8,128)(2,1)S(1)}, bf16[32,3840]{1,0:T(8,128)(2,1)S(1)}, u32[]{:S(2)}, u32[]{:S(2)}) %collective-permute-start.7) | collective-permute-done | bytes 245792 | tf_op jit(solution)/shard_map/ppermute | solution.py:113
  23.7 1.8 %collective-permute-start.8 = (bf16[32,3840]{1,0:T(8,128)(2,1)S(1)}, bf16[32,3840]{1,0:T(8,128)(2,1)S(1)}, u32[]{:S(2)}, u32[]{:S(2)}) collective-permute-start(bf16[32,3840]{1,0:T(8,128)(2,1)S(1)} %collective-permute-done.7.refs_0_), channel_id=1, source_target_pairs={{0,16},{16,0},{1,17},{17,1},{2,18},{18,2},{3,19},{19,3},{4,20},{20... | collective-permute-start | bytes 737288 | tf_op jit(solution)/shard_map/ppermute | solution.py:122
  26.2 1.1 %fusion.4 = (bf16[256,256]{1,0:T(8,128)(2,1)S(1)}, bf16[256,256]{1,0:T(8,128)(2,1)S(1)}, bf16[256,256]{1,0:T(8,128)(2,1)S(1)}, bf16[256,256]{1,0:T(8,128)(2,1)S(1)}) fusion(bf16[256,16384]{1,0:T(8,128)(2,1)} %param.3), kind=kLoop, calls=%fused_computation.23 | loop fusion | bytes 1048576 | tf_op jit(solution)/shard_map/slice | solution.py:153
  28.7 1.4 %collective-permute-start.5 = (bf16[32,3840]{1,0:T(8,128)(2,1)S(1)}, bf16[32,3840]{1,0:T(8,128)(2,1)S(1)}, u32[]{:S(2)}, u32[]{:S(2)}) collective-permute-start(bf16[32,3840]{1,0:T(8,128)(2,1)S(1)} %collective-permute-done.refs_0_), channel_id=1, source_target_pairs={{0,4},{4,8},{8,12},{12,0},{1,5},{5,9},{9,13},{13,1},{2,6},{6,10},{... | collective-permute-start | bytes 737288 | tf_op jit(solution)/shard_map/ppermute | solution.py:113
  30.0 1.1 %collective-permute-start.6 = (bf16[32,3840]{1,0:T(8,128)(2,1)S(1)}, bf16[32,3840]{1,0:T(8,128)(2,1)S(1)}, u32[]{:S(2)}, u32[]{:S(2)}) collective-permute-start(bf16[32,3840]{1,0:T(8,128)(2,1)S(1)} %collective-permute-done.1.refs_0_), channel_id=1, source_target_pairs={{0,16},{16,0},{1,17},{17,1},{2,18},{18,2},{3,19},{19,3},{4,20},{20... | collective-permute-start | bytes 737288 | tf_op jit(solution)/shard_map/ppermute | solution.py:122
  32.5 3.7 %collective-permute-done.11.refs_0_ = bf16[32,3840]{1,0:T(8,128)(2,1)S(1)} collective-permute-done((bf16[32,3840]{1,0:T(8,128)(2,1)S(1)}, bf16[32,3840]{1,0:T(8,128)(2,1)S(1)}, u32[]{:S(2)}, u32[]{:S(2)}) %collective-permute-start.11) | collective-permute-done | bytes 245792 | tf_op jit(solution)/shard_map/ppermute | solution.py:113
  36.2 5.2 %collective-permute-done.5.refs_0_ = bf16[32,3840]{1,0:T(8,128)(2,1)S(1)} collective-permute-done((bf16[32,3840]{1,0:T(8,128)(2,1)S(1)}, bf16[32,3840]{1,0:T(8,128)(2,1)S(1)}, u32[]{:S(2)}, u32[]{:S(2)}) %collective-permute-start.5) | collective-permute-done | bytes 245792 | tf_op jit(solution)/shard_map/ppermute | solution.py:113
  42.5 1.2 %collective-permute-start.13 = (bf16[64,1024]{1,0:T(8,128)(2,1)S(1)}, bf16[64,1024]{1,0:T(8,128)(2,1)S(1)}, u32[]{:S(2)}, u32[]{:S(2)}) collective-permute-start(bf16[64,1024]{1,0:T(8,128)(2,1)S(1)} %maximum_maximum_fusion), channel_id=1, source_target_pairs={{0,4},{4,8},{8,12},{12,0},{1,5},{5,9},{9,13},{13,1},{2,6},{6,10},{... | collective-permute-start | bytes 393224 | tf_op jit(solution)/shard_map/ppermute | solution.py:161
  44.6 1.4 %collective-permute-done.16.refs_0_ = bf16[32,3840]{1,0:T(8,128)(2,1)S(1)} collective-permute-done((bf16[32,3840]{1,0:T(8,128)(2,1)S(1)}, bf16[32,3840]{1,0:T(8,128)(2,1)S(1)}, u32[]{:S(2)}, u32[]{:S(2)}) %collective-permute-start.16) | collective-permute-done | bytes 245792 | tf_op jit(solution)/shard_map/ppermute | solution.py:113
  46.0 1.9 %collective-permute-start.17 = (bf16[32,3840]{1,0:T(8,128)(2,1)S(1)}, bf16[32,3840]{1,0:T(8,128)(2,1)S(1)}, u32[]{:S(2)}, u32[]{:S(2)}) collective-permute-start(bf16[32,3840]{1,0:T(8,128)(2,1)S(1)} %collective-permute-done.16.refs_0_), channel_id=1, source_target_pairs={{0,16},{16,0},{1,17},{17,1},{2,18},{18,2},{3,19},{19,3},{4,20},{20... | collective-permute-start | bytes 737288 | tf_op jit(solution)/shard_map/ppermute | solution.py:122
  48.6 1.4 %collective-permute-done.10.refs_1_ = bf16[32,3840]{1,0:T(8,128)(2,1)S(1)} collective-permute-done((bf16[32,3840]{1,0:T(8,128)(2,1)S(1)}, bf16[32,3840]{1,0:T(8,128)(2,1)S(1)}, u32[]{:S(2)}, u32[]{:S(2)}) %collective-permute-start.10) | collective-permute-done | bytes 245792 | tf_op jit(solution)/shard_map/ppermute | solution.py:122
  50.7 2.4 %collective-permute-done.9.refs_0_ = bf16[32,3840]{1,0:T(8,128)(2,1)S(1)} collective-permute-done((bf16[32,3840]{1,0:T(8,128)(2,1)S(1)}, bf16[32,3840]{1,0:T(8,128)(2,1)S(1)}, u32[]{:S(2)}, u32[]{:S(2)}) %collective-permute-start.9) | collective-permute-done | bytes 245792 | tf_op jit(solution)/shard_map/ppermute | solution.py:113
  53.1 2.8 %collective-permute-done.13.refs_5_ = bf16[64,1024]{1,0:T(8,128)(2,1)S(1)} collective-permute-done((bf16[64,1024]{1,0:T(8,128)(2,1)S(1)}, bf16[64,1024]{1,0:T(8,128)(2,1)S(1)}, u32[]{:S(2)}, u32[]{:S(2)}) %collective-permute-start.13) | collective-permute-done | bytes 131104 | tf_op jit(solution)/shard_map/ppermute | solution.py:161
  55.9 1.8 %collective-permute-start.15 = (bf16[32,3840]{1,0:T(8,128)(2,1)S(1)}, bf16[32,3840]{1,0:T(8,128)(2,1)S(1)}, u32[]{:S(2)}, u32[]{:S(2)}) collective-permute-start(bf16[32,3840]{1,0:T(8,128)(2,1)S(1)} %collective-permute-done.9.refs_0_), channel_id=1, source_target_pairs={{0,16},{16,0},{1,17},{17,1},{2,18},{18,2},{3,19},{19,3},{4,20},{20... | collective-permute-start | bytes 737288 | tf_op jit(solution)/shard_map/ppermute | solution.py:122
  58.4 2.7 %collective-permute-done.20.refs_0_ = bf16[32,3840]{1,0:T(8,128)(2,1)S(1)} collective-permute-done((bf16[32,3840]{1,0:T(8,128)(2,1)S(1)}, bf16[32,3840]{1,0:T(8,128)(2,1)S(1)}, u32[]{:S(2)}, u32[]{:S(2)}) %collective-permute-start.20) | collective-permute-done | bytes 245792 | tf_op jit(solution)/shard_map/ppermute | solution.py:113
  61.2 1.8 %collective-permute-start.21 = (bf16[32,3840]{1,0:T(8,128)(2,1)S(1)}, bf16[32,3840]{1,0:T(8,128)(2,1)S(1)}, u32[]{:S(2)}, u32[]{:S(2)}) collective-permute-start(bf16[32,3840]{1,0:T(8,128)(2,1)S(1)} %collective-permute-done.20.refs_0_), channel_id=1, source_target_pairs={{0,16},{16,0},{1,17},{17,1},{2,18},{18,2},{3,19},{19,3},{4,20},{20... | collective-permute-start | bytes 737288 | tf_op jit(solution)/shard_map/ppermute | solution.py:122
  63.0 3.4 %collective-permute-done.14.refs_0_ = bf16[32,3840]{1,0:T(8,128)(2,1)S(1)} collective-permute-done((bf16[32,3840]{1,0:T(8,128)(2,1)S(1)}, bf16[32,3840]{1,0:T(8,128)(2,1)S(1)}, u32[]{:S(2)}, u32[]{:S(2)}) %collective-permute-start.14) | collective-permute-done | bytes 245792 | tf_op jit(solution)/shard_map/ppermute | solution.py:113
  67.2 1.9 %collective-permute-start.19 = (bf16[32,3840]{1,0:T(8,128)(2,1)S(1)}, bf16[32,3840]{1,0:T(8,128)(2,1)S(1)}, u32[]{:S(2)}, u32[]{:S(2)}) collective-permute-start(bf16[32,3840]{1,0:T(8,128)(2,1)S(1)} %collective-permute-done.14.refs_0_), channel_id=1, source_target_pairs={{0,16},{16,0},{1,17},{17,1},{2,18},{18,2},{3,19},{19,3},{4,20},{20... | collective-permute-start | bytes 737288 | tf_op jit(solution)/shard_map/ppermute | solution.py:122
  69.0 2.8 %collective-permute-done.23.refs_0_ = bf16[32,3840]{1,0:T(8,128)(2,1)S(1)} collective-permute-done((bf16[32,3840]{1,0:T(8,128)(2,1)S(1)}, bf16[32,3840]{1,0:T(8,128)(2,1)S(1)}, u32[]{:S(2)}, u32[]{:S(2)}) %collective-permute-start.23) | collective-permute-done | bytes 245792 | tf_op jit(solution)/shard_map/ppermute | solution.py:113
  71.8 1.9 %collective-permute-start.26 = (bf16[32,3840]{1,0:T(8,128)(2,1)S(1)}, bf16[32,3840]{1,0:T(8,128)(2,1)S(1)}, u32[]{:S(2)}, u32[]{:S(2)}) collective-permute-start(bf16[32,3840]{1,0:T(8,128)(2,1)S(1)} %collective-permute-done.23.refs_0_), channel_id=1, source_target_pairs={{0,16},{16,0},{1,17},{17,1},{2,18},{18,2},{3,19},{19,3},{4,20},{20... | collective-permute-start | bytes 737288 | tf_op jit(solution)/shard_map/ppermute | solution.py:122
  75.3 1.7 %collective-permute-start.22 = (bf16[32,3840]{1,0:T(8,128)(2,1)S(1)}, bf16[32,3840]{1,0:T(8,128)(2,1)S(1)}, u32[]{:S(2)}, u32[]{:S(2)}) collective-permute-start(bf16[32,3840]{1,0:T(8,128)(2,1)S(1)} %collective-permute-done.18.refs_0_), channel_id=1, source_target_pairs={{0,16},{16,0},{1,17},{17,1},{2,18},{18,2},{3,19},{19,3},{4,20},{20... | collective-permute-start | bytes 737288 | tf_op jit(solution)/shard_map/ppermute | solution.py:122
  77.0 3.0 %collective-permute-done.24.refs_6_ = bf16[64,1024]{1,0:T(8,128)(2,1)S(1)} collective-permute-done((bf16[64,1024]{1,0:T(8,128)(2,1)S(1)}, bf16[64,1024]{1,0:T(8,128)(2,1)S(1)}, u32[]{:S(2)}, u32[]{:S(2)}) %collective-permute-start.24) | collective-permute-done | bytes 131104 | tf_op jit(solution)/shard_map/ppermute | solution.py:161
  82.2 4.6 %collective-permute-done.25.refs_7_ = bf16[64,1024]{1,0:T(8,128)(2,1)S(1)} collective-permute-done((bf16[64,1024]{1,0:T(8,128)(2,1)S(1)}, bf16[64,1024]{1,0:T(8,128)(2,1)S(1)}, u32[]{:S(2)}, u32[]{:S(2)}) %collective-permute-start.25) | collective-permute-done | bytes 131104 | tf_op jit(solution)/shard_map/ppermute | solution.py:161
  87.8 1.3 %collective-permute-done.27 = f32[2,64,256]{2,1,0:T(8,128)S(1)} collective-permute-done((f32[2,64,256]{2,1,0:T(8,128)S(1)}, f32[2,64,256]{2,1,0:T(8,128)S(1)}, u32[]{:S(2)}, u32[]{:S(2)}) %collective-permute-start.27) | collective-permute-done | bytes 131104 | tf_op jit(solution)/shard_map/ppermute | solution.py:131
  89.1 1.2 %collective-permute-start.28 = (f32[1,64,256]{2,1,0:T(8,128)S(1)}, f32[1,64,256]{2,1,0:T(8,128)S(1)}, u32[]{:S(2)}, u32[]{:S(2)}) collective-permute-start(f32[1,64,256]{2,1,0:T(8,128)S(1)} %slice_bitcast_fusion.2), channel_id=1, source_target_pairs={{0,2},{1,3},{2,0},{3,1},{4,6},{5,7},{6,4},{7,5},{8,10},{9,11},{10,... | collective-permute-start | bytes 196616 | tf_op jit(solution)/shard_map/ppermute | solution.py:131
  90.4 3.1 %collective-permute-done.28 = f32[1,64,256]{2,1,0:T(8,128)S(1)} collective-permute-done((f32[1,64,256]{2,1,0:T(8,128)S(1)}, f32[1,64,256]{2,1,0:T(8,128)S(1)}, u32[]{:S(2)}, u32[]{:S(2)}) %collective-permute-start.28) | collective-permute-done | bytes 65568 | tf_op jit(solution)/shard_map/ppermute | solution.py:131
  (57 shorter events, 19.6 us)
Async XLA Ops:
  1.1 11.9 %collective-permute-start.3 = (bf16[32,3840]{1,0:T(8,128)(2,1)S(1)}, bf16[32,3840]{1,0:T(8,128)(2,1)S(1)}, u32[]{:S(2)}, u32[]{:S(2)}) collective-permute-start(bf16[32,3840]{1,0:T(8,128)(2,1)S(1)} %slice_select_fusion.3), channel_id=1, source_target_pairs={{0,4},{4,8},{8,12},{12,0},{1,5},{5,9},{9,13},{13,1},{2,6},{6,10},{... | collective-permute-start | bytes 737288 | tf_op jit(solution)/shard_map/ppermute | solution.py:113
  5.3 13.0 %collective-permute-start = (bf16[32,3840]{1,0:T(8,128)(2,1)S(1)}, bf16[32,3840]{1,0:T(8,128)(2,1)S(1)}, u32[]{:S(2)}, u32[]{:S(2)}) collective-permute-start(bf16[32,3840]{1,0:T(8,128)(2,1)S(1)} %slice_select_fusion.2), channel_id=1, source_target_pairs={{0,4},{4,8},{8,12},{12,0},{1,5},{5,9},{9,13},{13,1},{2,6},{6,10},{... | collective-permute-start | bytes 737288 | tf_op jit(solution)/shard_map/ppermute | solution.py:113
  8.0 4.1 %copy-start = (bf16[64,16384]{1,0:T(8,128)(2,1)S(1)}, bf16[64,16384]{1,0:T(8,128)(2,1)}, u32[]{:S(2)}) copy-start(bf16[64,16384]{1,0:T(8,128)(2,1)} %test.1) | copy-start | bytes 6291460
  8.0 7.3 %copy-start.1 = (f32[16384]{0:T(1024)S(1)}, f32[16384]{0:T(1024)}, u32[]{:S(2)}) copy-start(f32[16384]{0:T(1024)} %param.5) | copy-start | bytes 196612
  13.0 10.7 %collective-permute-start.7 = (bf16[32,3840]{1,0:T(8,128)(2,1)S(1)}, bf16[32,3840]{1,0:T(8,128)(2,1)S(1)}, u32[]{:S(2)}, u32[]{:S(2)}) collective-permute-start(bf16[32,3840]{1,0:T(8,128)(2,1)S(1)} %slice_select_fusion.1), channel_id=1, source_target_pairs={{0,4},{4,8},{8,12},{12,0},{1,5},{5,9},{9,13},{13,1},{2,6},{6,10},{... | collective-permute-start | bytes 737288 | tf_op jit(solution)/shard_map/ppermute | solution.py:113
  13.8 9.9 %collective-permute-start.4 = (bf16[32,3840]{1,0:T(8,128)(2,1)S(1)}, bf16[32,3840]{1,0:T(8,128)(2,1)S(1)}, u32[]{:S(2)}, u32[]{:S(2)}) collective-permute-start(bf16[32,3840]{1,0:T(8,128)(2,1)S(1)} %collective-permute-done.3.refs_0_), channel_id=1, source_target_pairs={{0,16},{16,0},{1,17},{17,1},{2,18},{18,2},{3,19},{19,3},{4,20},{20... | collective-permute-start | bytes 737288 | tf_op jit(solution)/shard_map/ppermute | solution.py:122
  18.2 9.7 %collective-permute-start.1 = (bf16[32,3840]{1,0:T(8,128)(2,1)S(1)}, bf16[32,3840]{1,0:T(8,128)(2,1)S(1)}, u32[]{:S(2)}, u32[]{:S(2)}) collective-permute-start(bf16[32,3840]{1,0:T(8,128)(2,1)S(1)} %slice_select_fusion), channel_id=1, source_target_pairs={{0,4},{4,8},{8,12},{12,0},{1,5},{5,9},{9,13},{13,1},{2,6},{6,10},{... | collective-permute-start | bytes 737288 | tf_op jit(solution)/shard_map/ppermute | solution.py:113
  18.9 8.5 %collective-permute-start.2 = (bf16[32,3840]{1,0:T(8,128)(2,1)S(1)}, bf16[32,3840]{1,0:T(8,128)(2,1)S(1)}, u32[]{:S(2)}, u32[]{:S(2)}) collective-permute-start(bf16[32,3840]{1,0:T(8,128)(2,1)S(1)} %collective-permute-done.refs_0_), channel_id=1, source_target_pairs={{0,16},{16,0},{1,17},{17,1},{2,18},{18,2},{3,19},{19,3},{4,20},{20... | collective-permute-start | bytes 737288 | tf_op jit(solution)/shard_map/ppermute | solution.py:122
  23.7 8.1 %collective-permute-start.8 = (bf16[32,3840]{1,0:T(8,128)(2,1)S(1)}, bf16[32,3840]{1,0:T(8,128)(2,1)S(1)}, u32[]{:S(2)}, u32[]{:S(2)}) collective-permute-start(bf16[32,3840]{1,0:T(8,128)(2,1)S(1)} %collective-permute-done.7.refs_0_), channel_id=1, source_target_pairs={{0,16},{16,0},{1,17},{17,1},{2,18},{18,2},{3,19},{19,3},{4,20},{20... | collective-permute-start | bytes 737288 | tf_op jit(solution)/shard_map/ppermute | solution.py:122
  26.1 10.0 %collective-permute-start.11 = (bf16[32,3840]{1,0:T(8,128)(2,1)S(1)}, bf16[32,3840]{1,0:T(8,128)(2,1)S(1)}, u32[]{:S(2)}, u32[]{:S(2)}) collective-permute-start(bf16[32,3840]{1,0:T(8,128)(2,1)S(1)} %collective-permute-done.3.refs_0_), channel_id=1, source_target_pairs={{0,4},{4,8},{8,12},{12,0},{1,5},{5,9},{9,13},{13,1},{2,6},{6,10},{... | collective-permute-start | bytes 737288 | tf_op jit(solution)/shard_map/ppermute | solution.py:113
  28.7 12.8 %collective-permute-start.5 = (bf16[32,3840]{1,0:T(8,128)(2,1)S(1)}, bf16[32,3840]{1,0:T(8,128)(2,1)S(1)}, u32[]{:S(2)}, u32[]{:S(2)}) collective-permute-start(bf16[32,3840]{1,0:T(8,128)(2,1)S(1)} %collective-permute-done.refs_0_), channel_id=1, source_target_pairs={{0,4},{4,8},{8,12},{12,0},{1,5},{5,9},{9,13},{13,1},{2,6},{6,10},{... | collective-permute-start | bytes 737288 | tf_op jit(solution)/shard_map/ppermute | solution.py:113
  30.0 11.4 %collective-permute-start.6 = (bf16[32,3840]{1,0:T(8,128)(2,1)S(1)}, bf16[32,3840]{1,0:T(8,128)(2,1)S(1)}, u32[]{:S(2)}, u32[]{:S(2)}) collective-permute-start(bf16[32,3840]{1,0:T(8,128)(2,1)S(1)} %collective-permute-done.1.refs_0_), channel_id=1, source_target_pairs={{0,16},{16,0},{1,17},{17,1},{2,18},{18,2},{3,19},{19,3},{4,20},{20... | collective-permute-start | bytes 737288 | tf_op jit(solution)/shard_map/ppermute | solution.py:122
  36.2 8.5 %collective-permute-start.12 = (bf16[32,3840]{1,0:T(8,128)(2,1)S(1)}, bf16[32,3840]{1,0:T(8,128)(2,1)S(1)}, u32[]{:S(2)}, u32[]{:S(2)}) collective-permute-start(bf16[32,3840]{1,0:T(8,128)(2,1)S(1)} %collective-permute-done.11.refs_0_), channel_id=1, source_target_pairs={{0,16},{16,0},{1,17},{17,1},{2,18},{18,2},{3,19},{19,3},{4,20},{20... | collective-permute-start | bytes 737288 | tf_op jit(solution)/shard_map/ppermute | solution.py:122
  36.2 9.8 %collective-permute-start.16 = (bf16[32,3840]{1,0:T(8,128)(2,1)S(1)}, bf16[32,3840]{1,0:T(8,128)(2,1)S(1)}, u32[]{:S(2)}, u32[]{:S(2)}) collective-permute-start(bf16[32,3840]{1,0:T(8,128)(2,1)S(1)} %collective-permute-done.7.refs_0_), channel_id=1, source_target_pairs={{0,4},{4,8},{8,12},{12,0},{1,5},{5,9},{9,13},{13,1},{2,6},{6,10},{... | collective-permute-start | bytes 737288 | tf_op jit(solution)/shard_map/ppermute | solution.py:113
  41.4 8.6 %collective-permute-start.10 = (bf16[32,3840]{1,0:T(8,128)(2,1)S(1)}, bf16[32,3840]{1,0:T(8,128)(2,1)S(1)}, u32[]{:S(2)}, u32[]{:S(2)}) collective-permute-start(bf16[32,3840]{1,0:T(8,128)(2,1)S(1)} %collective-permute-done.5.refs_0_), channel_id=1, source_target_pairs={{0,16},{16,0},{1,17},{17,1},{2,18},{18,2},{3,19},{19,3},{4,20},{20... | collective-permute-start | bytes 737288 | tf_op jit(solution)/shard_map/ppermute | solution.py:122
  42.3 10.8 %collective-permute-start.9 = (bf16[32,3840]{1,0:T(8,128)(2,1)S(1)}, bf16[32,3840]{1,0:T(8,128)(2,1)S(1)}, u32[]{:S(2)}, u32[]{:S(2)}) collective-permute-start(bf16[32,3840]{1,0:T(8,128)(2,1)S(1)} %collective-permute-done.1.refs_0_), channel_id=1, source_target_pairs={{0,4},{4,8},{8,12},{12,0},{1,5},{5,9},{9,13},{13,1},{2,6},{6,10},{... | collective-permute-start | bytes 737288 | tf_op jit(solution)/shard_map/ppermute | solution.py:113
  42.5 13.5 %collective-permute-start.13 = (bf16[64,1024]{1,0:T(8,128)(2,1)S(1)}, bf16[64,1024]{1,0:T(8,128)(2,1)S(1)}, u32[]{:S(2)}, u32[]{:S(2)}) collective-permute-start(bf16[64,1024]{1,0:T(8,128)(2,1)S(1)} %maximum_maximum_fusion), channel_id=1, source_target_pairs={{0,4},{4,8},{8,12},{12,0},{1,5},{5,9},{9,13},{13,1},{2,6},{6,10},{... | collective-permute-start | bytes 393224 | tf_op jit(solution)/shard_map/ppermute | solution.py:161
  46.0 11.8 %collective-permute-start.17 = (bf16[32,3840]{1,0:T(8,128)(2,1)S(1)}, bf16[32,3840]{1,0:T(8,128)(2,1)S(1)}, u32[]{:S(2)}, u32[]{:S(2)}) collective-permute-start(bf16[32,3840]{1,0:T(8,128)(2,1)S(1)} %collective-permute-done.16.refs_0_), channel_id=1, source_target_pairs={{0,16},{16,0},{1,17},{17,1},{2,18},{18,2},{3,19},{19,3},{4,20},{20... | collective-permute-start | bytes 737288 | tf_op jit(solution)/shard_map/ppermute | solution.py:122
  48.6 12.6 %collective-permute-start.20 = (bf16[32,3840]{1,0:T(8,128)(2,1)S(1)}, bf16[32,3840]{1,0:T(8,128)(2,1)S(1)}, u32[]{:S(2)}, u32[]{:S(2)}) collective-permute-start(bf16[32,3840]{1,0:T(8,128)(2,1)S(1)} %collective-permute-done.11.refs_0_), channel_id=1, source_target_pairs={{0,4},{4,8},{8,12},{12,0},{1,5},{5,9},{9,13},{13,1},{2,6},{6,10},{... | collective-permute-start | bytes 737288 | tf_op jit(solution)/shard_map/ppermute | solution.py:113
  55.9 10.5 %collective-permute-start.14 = (bf16[32,3840]{1,0:T(8,128)(2,1)S(1)}, bf16[32,3840]{1,0:T(8,128)(2,1)S(1)}, u32[]{:S(2)}, u32[]{:S(2)}) collective-permute-start(bf16[32,3840]{1,0:T(8,128)(2,1)S(1)} %collective-permute-done.5.refs_0_), channel_id=1, source_target_pairs={{0,4},{4,8},{8,12},{12,0},{1,5},{5,9},{9,13},{13,1},{2,6},{6,10},{... | collective-permute-start | bytes 737288 | tf_op jit(solution)/shard_map/ppermute | solution.py:113
  55.9 10.5 %collective-permute-start.15 = (bf16[32,3840]{1,0:T(8,128)(2,1)S(1)}, bf16[32,3840]{1,0:T(8,128)(2,1)S(1)}, u32[]{:S(2)}, u32[]{:S(2)}) collective-permute-start(bf16[32,3840]{1,0:T(8,128)(2,1)S(1)} %collective-permute-done.9.refs_0_), channel_id=1, source_target_pairs={{0,16},{16,0},{1,17},{17,1},{2,18},{18,2},{3,19},{19,3},{4,20},{20... | collective-permute-start | bytes 737288 | tf_op jit(solution)/shard_map/ppermute | solution.py:122
  61.2 10.6 %collective-permute-start.23 = (bf16[32,3840]{1,0:T(8,128)(2,1)S(1)}, bf16[32,3840]{1,0:T(8,128)(2,1)S(1)}, u32[]{:S(2)}, u32[]{:S(2)}) collective-permute-start(bf16[32,3840]{1,0:T(8,128)(2,1)S(1)} %collective-permute-done.16.refs_0_), channel_id=1, source_target_pairs={{0,4},{4,8},{8,12},{12,0},{1,5},{5,9},{9,13},{13,1},{2,6},{6,10},{... | collective-permute-start | bytes 737288 | tf_op jit(solution)/shard_map/ppermute | solution.py:113
  61.2 10.6 %collective-permute-start.21 = (bf16[32,3840]{1,0:T(8,128)(2,1)S(1)}, bf16[32,3840]{1,0:T(8,128)(2,1)S(1)}, u32[]{:S(2)}, u32[]{:S(2)}) collective-permute-start(bf16[32,3840]{1,0:T(8,128)(2,1)S(1)} %collective-permute-done.20.refs_0_), channel_id=1, source_target_pairs={{0,16},{16,0},{1,17},{17,1},{2,18},{18,2},{3,19},{19,3},{4,20},{20... | collective-permute-start | bytes 737288 | tf_op jit(solution)/shard_map/ppermute | solution.py:122
  67.1 8.2 %collective-permute-start.18 = (bf16[32,3840]{1,0:T(8,128)(2,1)S(1)}, bf16[32,3840]{1,0:T(8,128)(2,1)S(1)}, u32[]{:S(2)}, u32[]{:S(2)}) collective-permute-start(bf16[32,3840]{1,0:T(8,128)(2,1)S(1)} %collective-permute-done.9.refs_0_), channel_id=1, source_target_pairs={{0,4},{4,8},{8,12},{12,0},{1,5},{5,9},{9,13},{13,1},{2,6},{6,10},{... | collective-permute-start | bytes 737288 | tf_op jit(solution)/shard_map/ppermute | solution.py:113
  67.2 8.1 %collective-permute-start.19 = (bf16[32,3840]{1,0:T(8,128)(2,1)S(1)}, bf16[32,3840]{1,0:T(8,128)(2,1)S(1)}, u32[]{:S(2)}, u32[]{:S(2)}) collective-permute-start(bf16[32,3840]{1,0:T(8,128)(2,1)S(1)} %collective-permute-done.14.refs_0_), channel_id=1, source_target_pairs={{0,16},{16,0},{1,17},{17,1},{2,18},{18,2},{3,19},{19,3},{4,20},{20... | collective-permute-start | bytes 737288 | tf_op jit(solution)/shard_map/ppermute | solution.py:122
  71.8 8.2 %collective-permute-start.24 = (bf16[64,1024]{1,0:T(8,128)(2,1)S(1)}, bf16[64,1024]{1,0:T(8,128)(2,1)S(1)}, u32[]{:S(2)}, u32[]{:S(2)}) collective-permute-start(bf16[64,1024]{1,0:T(8,128)(2,1)S(1)} %collective-permute-done.13.refs_5_), channel_id=1, source_target_pairs={{0,4},{4,8},{8,12},{12,0},{1,5},{5,9},{9,13},{13,1},{2,6},{6,10},{... | collective-permute-start | bytes 393224 | tf_op jit(solution)/shard_map/ppermute | solution.py:161
  71.8 8.9 %collective-permute-start.26 = (bf16[32,3840]{1,0:T(8,128)(2,1)S(1)}, bf16[32,3840]{1,0:T(8,128)(2,1)S(1)}, u32[]{:S(2)}, u32[]{:S(2)}) collective-permute-start(bf16[32,3840]{1,0:T(8,128)(2,1)S(1)} %collective-permute-done.23.refs_0_), channel_id=1, source_target_pairs={{0,16},{16,0},{1,17},{17,1},{2,18},{18,2},{3,19},{19,3},{4,20},{20... | collective-permute-start | bytes 737288 | tf_op jit(solution)/shard_map/ppermute | solution.py:122
  75.3 6.9 %collective-permute-start.22 = (bf16[32,3840]{1,0:T(8,128)(2,1)S(1)}, bf16[32,3840]{1,0:T(8,128)(2,1)S(1)}, u32[]{:S(2)}, u32[]{:S(2)}) collective-permute-start(bf16[32,3840]{1,0:T(8,128)(2,1)S(1)} %collective-permute-done.18.refs_0_), channel_id=1, source_target_pairs={{0,16},{16,0},{1,17},{17,1},{2,18},{18,2},{3,19},{19,3},{4,20},{20... | collective-permute-start | bytes 737288 | tf_op jit(solution)/shard_map/ppermute | solution.py:122
  80.0 6.8 %collective-permute-start.25 = (bf16[64,1024]{1,0:T(8,128)(2,1)S(1)}, bf16[64,1024]{1,0:T(8,128)(2,1)S(1)}, u32[]{:S(2)}, u32[]{:S(2)}) collective-permute-start(bf16[64,1024]{1,0:T(8,128)(2,1)S(1)} %collective-permute-done.24.refs_6_), channel_id=1, source_target_pairs={{0,4},{4,8},{8,12},{12,0},{1,5},{5,9},{9,13},{13,1},{2,6},{6,10},{... | collective-permute-start | bytes 393224 | tf_op jit(solution)/shard_map/ppermute | solution.py:161
  87.7 1.4 %collective-permute-start.27 = (f32[2,64,256]{2,1,0:T(8,128)S(1)}, f32[2,64,256]{2,1,0:T(8,128)S(1)}, u32[]{:S(2)}, u32[]{:S(2)}) collective-permute-start(f32[2,64,256]{2,1,0:T(8,128)S(1)} %slice_bitcast_fusion), channel_id=1, source_target_pairs={{0,1},{1,0},{2,3},{3,2},{4,5},{5,4},{6,7},{7,6},{8,9},{9,8},{10,11... | collective-permute-start | bytes 393224 | tf_op jit(solution)/shard_map/ppermute | solution.py:131
  89.1 4.3 %collective-permute-start.28 = (f32[1,64,256]{2,1,0:T(8,128)S(1)}, f32[1,64,256]{2,1,0:T(8,128)S(1)}, u32[]{:S(2)}, u32[]{:S(2)}) collective-permute-start(f32[1,64,256]{2,1,0:T(8,128)S(1)} %slice_bitcast_fusion.2), channel_id=1, source_target_pairs={{0,2},{1,3},{2,0},{3,1},{4,6},{5,7},{6,4},{7,5},{8,10},{9,11},{10,... | collective-permute-start | bytes 196616 | tf_op jit(solution)/shard_map/ppermute | solution.py:131

commit v19 on v18

--- a/solution.py
+++ b/solution.py
@@ -9,7 +9,7 @@
 
 CONTRACT = (((1,), (1,)), ((), ()))
 LANES = 128
-QUARTERS, SHARE = 4, 15 / 16
+QUARTERS, SHARE = 4, 31 / 32
 
 
 def product(rows, scale, train, unit, width, skip=0):
@@ -103,6 +103,7 @@
         width = int(quarter * SHARE) // LANES * LANES
         first_grp = lax.axis_index("grp") == 0
         ring = [(i, (i + 1) % n_ex) for i in range(n_ex)]
+        back = [(d, s) for s, d in ring]
         hops, swaps, made, first = [], [], [], []
 
         def after(block, *waits):
@@ -148,7 +149,7 @@
         sides = [
             jnp.concatenate([share(late, end, other) for end in ends], axis=1) for other in range(n_grp)
         ]
-        whole = [jnp.concatenate(sides, axis=0)]
+        whole = jnp.concatenate(sides, axis=0)
         trains = [train[:, start : start + quarter] for start in starts]
         end_train = jnp.concatenate([train[:, end] for end in ends], axis=1)
         own = call(
@@ -157,12 +158,21 @@
         first.append(own)
         final = n_ex - 1
         sums = [own] + [None] * final
+        turns = []
+        for away in range(1, n_ex // 2 + 1):
+            turns += [(away, away - 1, ring), (n_ex - away, (n_ex + 1 - away) % n_ex, back)]
+        turns = turns[: n_ex - 1]
+        rest = {0: whole}
+        latest = []
+
         def whole_hop(gate):
-            whole.append(lax.ppermute(after(whole[-1], hops[gate]), "ex", ring))
+            to, source, pairs = turns.pop(0)
+            rest[to] = lax.ppermute(after(rest[source], hops[gate]), "ex", pairs)
+            latest[:] = [rest[to]]
 
         for t in range(1, n_ex):
             for c, start in enumerate(starts):
-                ahead = whole[-1:] if t > 2 and c == 1 else [end_train] if (t, c) == (2, 2) else []
+                ahead = latest if t > 2 and c == 1 else [end_train] if (t, c) == (2, 2) else []
                 held[c] = hop(held[c], *ahead)
                 if 1 < t < final and c == 1:
                     whole_hop(-2)
@@ -176,11 +186,11 @@
                     queries, docs, width, operands + base,
                 )
                 made.append(sums[t])
-        while len(whole) < n_ex:
+        while turns:
             whole_hop(-2)
         total = call(
             functools.partial(last_kernel, n_grp, n_ex, n_feat, starts, unit, len(operands) - 2),
-            n_ex * queries, docs, 2 * width, [*operands, end_train, *whole[1:], *sums],
+            n_ex * queries, docs, 2 * width, [*operands, end_train, *(rest[t] for t in range(1, n_ex)), *sums],
             [pltpu.VMEM((n_ex * queries, docs), jnp.float32)],
         )
         return sum_over_feat(total).T

time: 94.3 us -> 91.1 us (0.966)
  waiting for transfers between devices: 46.3 us -> 33.9 us
  starting transfers between devices: 27 us -> 35.7 us
    ppermute x3, waiting for transfers between devices: 10.4 us -> 1.34 us  [whole_hop(): rest[to] = lax.ppermute(after(rest[source], hops[gate]), 'ex', pairs)]
    ppermute x12, waiting for transfers between devices: 27.8 us -> 20.6 us  [hop(): hops.append(lax.ppermute(after(block, *waits, *ahead), 'ex', ring))]
    ppermute x12, starting transfers between devices: 16.7 us -> 21.6 us  [swap(): swaps.append(lax.ppermute(after(block, *waits), 'grp', [(0, 1), (1, 0)]))]
    ppermute x3, starting transfers between devices: 1.24 us -> 5.45 us  [whole_hop(): rest[to] = lax.ppermute(after(rest[source], hops[gate]), 'ex', pairs)]
    ppermute x12, waiting for transfers between devices: 3.69 us -> 7.69 us  [swap(): swaps.append(lax.ppermute(after(block, *waits), 'grp', [(0, 1), (1, 0)]))]
  transfers between devices with their start and end apart: 29 -> 29, of which waited for: 21 -> 21; matrix products, arithmetic and copies ran while one was open for 8% -> 8% of each run, Pallas kernels for 11% -> 12%
where the time goes in v19:
time: 91.1 us; the launch traced here: 90.9 us
  starting transfers between devices  35.7 us (39%)
  waiting for transfers between devices  33.9 us (37%)
  Pallas kernels  11.8 us (13%)
  local copies, waits for them, and re-layouts  4.95 us (5%)
  other arithmetic  4.22 us (5%)
    ppermute x12, starting transfers between devices, swap(): swaps.append(lax.ppermute(after(block, *waits), 'grp', [(0, 1), (1, 0)]))  21.6 us
    ppermute x12, waiting for transfers between devices, hop(): hops.append(lax.ppermute(after(block, *waits, *ahead), 'ex', ring))  20.6 us
    pallas_call x13, Pallas kernels, call(): pl.pallas_call(kernel, out_shape=jax.ShapeDtypeStruct((rows, docs), jnp.f...  11.8 us
    ppermute x12, waiting for transfers between devices, swap(): swaps.append(lax.ppermute(after(block, *waits), 'grp', [(0, 1), (1, 0)]))  7.69 us
    ppermute x12, starting transfers between devices, hop(): hops.append(lax.ppermute(after(block, *waits, *ahead), 'ex', ring))  7.21 us
    ppermute x3, starting transfers between devices, whole_hop(): rest[to] = lax.ppermute(after(rest[source], hops[gate]), 'ex', pairs)  5.45 us
    ppermute x2, waiting for transfers between devices, sum_over_feat(): held = pairs[:, 0] + lax.ppermute(pairs[:, 1], 'feat', partner)  4.28 us
    slice x1, local copies, waits for them, and re-layouts, on_device(): trains = [train[:, start:start + quarter] for start in starts]  3.97 us
  transfers between devices with their start and end apart: 29, of which 21 were waited for; matrix products, arithmetic and copies ran while one was open for 8% of the time, Pallas kernels for 12%

profile of v19, /device:TPU:0, one launch (start us, length us, event | category | flops | bytes accessed | tf_op | source)
XLA Modules:
  0.0 90.9 jit_solution(7209185977661745626)
XLA Ops:
  0.0 1.2 %slice_select_fusion.3 = bf16[32,3968]{1,0:T(8,128)(2,1)S(1)} fusion(bf16[64,16384]{1,0:T(8,128)(2,1)} %test.1, pred[]{:T(512)S(6)} %eq.3), kind=kLoop, calls=%fused_computation.4 | loop fusion | flops 126976 | bytes 761857 | tf_op jit(solution)/shard_map/jit(_where)/select_n | solution.py:140
  1.3 3.1 %collective-permute-start.3 = (bf16[32,3968]{1,0:T(8,128)(2,1)S(1)}, bf16[32,3968]{1,0:T(8,128)(2,1)S(1)}, u32[]{:S(2)}, u32[]{:S(2)}) collective-permute-start(bf16[32,3968]{1,0:T(8,128)(2,1)S(1)} %slice_select_fusion.3), channel_id=1, source_target_pairs={{0,4},{4,8},{8,12},{12,0},{1,5},{5,9},{9,13},{13,1},{2,6},{6,10},{... | collective-permute-start | bytes 761864 | tf_op jit(solution)/shard_map/ppermute | solution.py:114
  5.4 1.6 %collective-permute-start = (bf16[32,3968]{1,0:T(8,128)(2,1)S(1)}, bf16[32,3968]{1,0:T(8,128)(2,1)S(1)}, u32[]{:S(2)}, u32[]{:S(2)}) collective-permute-start(bf16[32,3968]{1,0:T(8,128)(2,1)S(1)} %slice_select_fusion.2), channel_id=1, source_target_pairs={{0,4},{4,8},{8,12},{12,0},{1,5},{5,9},{9,13},{13,1},{2,6},{6,10},{... | collective-permute-start | bytes 761864 | tf_op jit(solution)/shard_map/ppermute | solution.py:114
  8.2 4.0 %fusion.5 = (bf16[256,4096]{1,0:T(8,128)(2,1)S(1)}, bf16[256,4096]{1,0:T(8,128)(2,1)S(1)}, bf16[256,4096]{1,0:T(8,128)(2,1)S(1)}, bf16[256,4096]{1,0:T(8,128)(2,1)S(1)}) fusion(bf16[256,16384]{1,0:T(8,128)(2,1)} %param.3), kind=kLoop, calls=%fused_computation.24 | loop fusion | bytes 16777216 | tf_op jit(solution)/shard_map/slice | solution.py:153
  13.9 1.5 %collective-permute-start.4 = (bf16[32,3968]{1,0:T(8,128)(2,1)S(1)}, bf16[32,3968]{1,0:T(8,128)(2,1)S(1)}, u32[]{:S(2)}, u32[]{:S(2)}) collective-permute-start(bf16[32,3968]{1,0:T(8,128)(2,1)S(1)} %collective-permute-done.3.refs_0_), channel_id=1, source_target_pairs={{0,16},{16,0},{1,17},{17,1},{2,18},{18,2},{3,19},{19,3},{4,20},{20... | collective-permute-start | bytes 761864 | tf_op jit(solution)/shard_map/ppermute | solution.py:123
  15.4 2.7 %shard_map.37.refs_8_ = f32[64,256]{1,0:T(8,128)S(1)} custom-call(bf16[64,16384]{1,0:T(8,128)(2,1)S(1)} %copy-done, f32[1,16384]{1,0:T(1,128)S(1)} %bitcast.28, bf16[256,4096]{1,0:T(8,128)(2,1)S(1)} %get-tuple-element.66.refs_0_.refs_3_, bf16[256,4096]{1,0:T(8,128)(2,1)S(1)} %get-tuple-element.65.refs_1_.refs_3_, ...), custom_call_target="tpu_custom_call" | custom-call | flops 536870912 | bytes 10485760 | tf_op jit(solution)/shard_map/pallas_call | solution.py:80
  18.8 1.8 %collective-permute-start.2 = (bf16[32,3968]{1,0:T(8,128)(2,1)S(1)}, bf16[32,3968]{1,0:T(8,128)(2,1)S(1)}, u32[]{:S(2)}, u32[]{:S(2)}) collective-permute-start(bf16[32,3968]{1,0:T(8,128)(2,1)S(1)} %collective-permute-done.refs_0_), channel_id=1, source_target_pairs={{0,16},{16,0},{1,17},{17,1},{2,18},{18,2},{3,19},{19,3},{4,20},{20... | collective-permute-start | bytes 761864 | tf_op jit(solution)/shard_map/ppermute | solution.py:123
  20.5 3.6 %collective-permute-done.7.refs_0_ = bf16[32,3968]{1,0:T(8,128)(2,1)S(1)} collective-permute-done((bf16[32,3968]{1,0:T(8,128)(2,1)S(1)}, bf16[32,3968]{1,0:T(8,128)(2,1)S(1)}, u32[]{:S(2)}, u32[]{:S(2)}) %collective-permute-start.7) | collective-permute-done | bytes 253984 | tf_op jit(solution)/shard_map/ppermute | solution.py:114
  24.1 1.9 %collective-permute-start.8 = (bf16[32,3968]{1,0:T(8,128)(2,1)S(1)}, bf16[32,3968]{1,0:T(8,128)(2,1)S(1)}, u32[]{:S(2)}, u32[]{:S(2)}) collective-permute-start(bf16[32,3968]{1,0:T(8,128)(2,1)S(1)} %collective-permute-done.7.refs_0_), channel_id=1, source_target_pairs={{0,16},{16,0},{1,17},{17,1},{2,18},{18,2},{3,19},{19,3},{4,20},{20... | collective-permute-start | bytes 761864 | tf_op jit(solution)/shard_map/ppermute | solution.py:123
  27.4 1.4 %collective-permute-done.1.refs_0_ = bf16[32,3968]{1,0:T(8,128)(2,1)S(1)} collective-permute-done((bf16[32,3968]{1,0:T(8,128)(2,1)S(1)}, bf16[32,3968]{1,0:T(8,128)(2,1)S(1)}, u32[]{:S(2)}, u32[]{:S(2)}) %collective-permute-start.1) | collective-permute-done | bytes 253984 | tf_op jit(solution)/shard_map/ppermute | solution.py:114
  30.5 1.5 %collective-permute-start.6 = (bf16[32,3968]{1,0:T(8,128)(2,1)S(1)}, bf16[32,3968]{1,0:T(8,128)(2,1)S(1)}, u32[]{:S(2)}, u32[]{:S(2)}) collective-permute-start(bf16[32,3968]{1,0:T(8,128)(2,1)S(1)} %collective-permute-done.1.refs_0_), channel_id=1, source_target_pairs={{0,16},{16,0},{1,17},{17,1},{2,18},{18,2},{3,19},{19,3},{4,20},{20... | collective-permute-start | bytes 761864 | tf_op jit(solution)/shard_map/ppermute | solution.py:123
  33.8 3.2 %collective-permute-done.11.refs_0_ = bf16[32,3968]{1,0:T(8,128)(2,1)S(1)} collective-permute-done((bf16[32,3968]{1,0:T(8,128)(2,1)S(1)}, bf16[32,3968]{1,0:T(8,128)(2,1)S(1)}, u32[]{:S(2)}, u32[]{:S(2)}) %collective-permute-start.11) | collective-permute-done | bytes 253984 | tf_op jit(solution)/shard_map/ppermute | solution.py:114
  37.2 2.4 %collective-permute-done.6.refs_1_ = bf16[32,3968]{1,0:T(8,128)(2,1)S(1)} collective-permute-done((bf16[32,3968]{1,0:T(8,128)(2,1)S(1)}, bf16[32,3968]{1,0:T(8,128)(2,1)S(1)}, u32[]{:S(2)}, u32[]{:S(2)}) %collective-permute-start.6) | collective-permute-done | bytes 253984 | tf_op jit(solution)/shard_map/ppermute | solution.py:123
  40.3 1.1 %collective-permute-done.5.refs_0_ = bf16[32,3968]{1,0:T(8,128)(2,1)S(1)} collective-permute-done((bf16[32,3968]{1,0:T(8,128)(2,1)S(1)}, bf16[32,3968]{1,0:T(8,128)(2,1)S(1)}, u32[]{:S(2)}, u32[]{:S(2)}) %collective-permute-start.5) | collective-permute-done | bytes 253984 | tf_op jit(solution)/shard_map/ppermute | solution.py:114
  41.4 1.2 %collective-permute-start.10 = (bf16[32,3968]{1,0:T(8,128)(2,1)S(1)}, bf16[32,3968]{1,0:T(8,128)(2,1)S(1)}, u32[]{:S(2)}, u32[]{:S(2)}) collective-permute-start(bf16[32,3968]{1,0:T(8,128)(2,1)S(1)} %collective-permute-done.5.refs_0_), channel_id=1, source_target_pairs={{0,16},{16,0},{1,17},{17,1},{2,18},{18,2},{3,19},{19,3},{4,20},{20... | collective-permute-start | bytes 761864 | tf_op jit(solution)/shard_map/ppermute | solution.py:123
  43.4 1.6 %collective-permute-start.13 = (bf16[64,512]{1,0:T(8,128)(2,1)S(1)}, bf16[64,512]{1,0:T(8,128)(2,1)S(1)}, u32[]{:S(2)}, u32[]{:S(2)}) collective-permute-start(bf16[64,512]{1,0:T(8,128)(2,1)S(1)} %maximum_maximum_fusion), channel_id=1, source_target_pairs={{0,4},{4,8},{8,12},{12,0},{1,5},{5,9},{9,13},{13,1},{2,6},{6,10},{... | collective-permute-start | bytes 196616 | tf_op jit(solution)/shard_map/ppermute | solution.py:170
  46.7 3.2 %collective-permute-start.17 = (bf16[32,3968]{1,0:T(8,128)(2,1)S(1)}, bf16[32,3968]{1,0:T(8,128)(2,1)S(1)}, u32[]{:S(2)}, u32[]{:S(2)}) collective-permute-start(bf16[32,3968]{1,0:T(8,128)(2,1)S(1)} %collective-permute-done.16.refs_0_), channel_id=1, source_target_pairs={{0,16},{16,0},{1,17},{17,1},{2,18},{18,2},{3,19},{19,3},{4,20},{20... | collective-permute-start | bytes 761864 | tf_op jit(solution)/shard_map/ppermute | solution.py:123
  49.9 1.5 %collective-permute-done.10.refs_1_ = bf16[32,3968]{1,0:T(8,128)(2,1)S(1)} collective-permute-done((bf16[32,3968]{1,0:T(8,128)(2,1)S(1)}, bf16[32,3968]{1,0:T(8,128)(2,1)S(1)}, u32[]{:S(2)}, u32[]{:S(2)}) %collective-permute-start.10) | collective-permute-done | bytes 253984 | tf_op jit(solution)/shard_map/ppermute | solution.py:123
  51.3 2.2 %collective-permute-done.9.refs_0_ = bf16[32,3968]{1,0:T(8,128)(2,1)S(1)} collective-permute-done((bf16[32,3968]{1,0:T(8,128)(2,1)S(1)}, bf16[32,3968]{1,0:T(8,128)(2,1)S(1)}, u32[]{:S(2)}, u32[]{:S(2)}) %collective-permute-start.9) | collective-permute-done | bytes 253984 | tf_op jit(solution)/shard_map/ppermute | solution.py:114
  54.9 1.8 %collective-permute-start.15 = (bf16[32,3968]{1,0:T(8,128)(2,1)S(1)}, bf16[32,3968]{1,0:T(8,128)(2,1)S(1)}, u32[]{:S(2)}, u32[]{:S(2)}) collective-permute-start(bf16[32,3968]{1,0:T(8,128)(2,1)S(1)} %collective-permute-done.9.refs_0_), channel_id=1, source_target_pairs={{0,16},{16,0},{1,17},{17,1},{2,18},{18,2},{3,19},{19,3},{4,20},{20... | collective-permute-start | bytes 761864 | tf_op jit(solution)/shard_map/ppermute | solution.py:123
  56.7 3.5 %collective-permute-done.20.refs_0_ = bf16[32,3968]{1,0:T(8,128)(2,1)S(1)} collective-permute-done((bf16[32,3968]{1,0:T(8,128)(2,1)S(1)}, bf16[32,3968]{1,0:T(8,128)(2,1)S(1)}, u32[]{:S(2)}, u32[]{:S(2)}) %collective-permute-start.20) | collective-permute-done | bytes 253984 | tf_op jit(solution)/shard_map/ppermute | solution.py:114
  60.2 1.9 %collective-permute-start.21 = (bf16[32,3968]{1,0:T(8,128)(2,1)S(1)}, bf16[32,3968]{1,0:T(8,128)(2,1)S(1)}, u32[]{:S(2)}, u32[]{:S(2)}) collective-permute-start(bf16[32,3968]{1,0:T(8,128)(2,1)S(1)} %collective-permute-done.20.refs_0_), channel_id=1, source_target_pairs={{0,16},{16,0},{1,17},{17,1},{2,18},{18,2},{3,19},{19,3},{4,20},{20... | collective-permute-start | bytes 761864 | tf_op jit(solution)/shard_map/ppermute | solution.py:123
  63.0 1.6 %collective-permute-done.14.refs_0_ = bf16[32,3968]{1,0:T(8,128)(2,1)S(1)} collective-permute-done((bf16[32,3968]{1,0:T(8,128)(2,1)S(1)}, bf16[32,3968]{1,0:T(8,128)(2,1)S(1)}, u32[]{:S(2)}, u32[]{:S(2)}) %collective-permute-start.14) | collective-permute-done | bytes 253984 | tf_op jit(solution)/shard_map/ppermute | solution.py:114
  65.5 3.0 %collective-permute-start.19 = (bf16[32,3968]{1,0:T(8,128)(2,1)S(1)}, bf16[32,3968]{1,0:T(8,128)(2,1)S(1)}, u32[]{:S(2)}, u32[]{:S(2)}) collective-permute-start(bf16[32,3968]{1,0:T(8,128)(2,1)S(1)} %collective-permute-done.14.refs_0_), channel_id=1, source_target_pairs={{0,16},{16,0},{1,17},{17,1},{2,18},{18,2},{3,19},{19,3},{4,20},{20... | collective-permute-start | bytes 761864 | tf_op jit(solution)/shard_map/ppermute | solution.py:123
  69.2 2.0 %collective-permute-done.23.refs_0_ = bf16[32,3968]{1,0:T(8,128)(2,1)S(1)} collective-permute-done((bf16[32,3968]{1,0:T(8,128)(2,1)S(1)}, bf16[32,3968]{1,0:T(8,128)(2,1)S(1)}, u32[]{:S(2)}, u32[]{:S(2)}) %collective-permute-start.23) | collective-permute-done | bytes 253984 | tf_op jit(solution)/shard_map/ppermute | solution.py:114
  71.2 1.7 %collective-permute-start.26 = (bf16[32,3968]{1,0:T(8,128)(2,1)S(1)}, bf16[32,3968]{1,0:T(8,128)(2,1)S(1)}, u32[]{:S(2)}, u32[]{:S(2)}) collective-permute-start(bf16[32,3968]{1,0:T(8,128)(2,1)S(1)} %collective-permute-done.23.refs_0_), channel_id=1, source_target_pairs={{0,16},{16,0},{1,17},{17,1},{2,18},{18,2},{3,19},{19,3},{4,20},{20... | collective-permute-start | bytes 761864 | tf_op jit(solution)/shard_map/ppermute | solution.py:123
  73.9 1.6 %collective-permute-done.19.refs_1_ = bf16[32,3968]{1,0:T(8,128)(2,1)S(1)} collective-permute-done((bf16[32,3968]{1,0:T(8,128)(2,1)S(1)}, bf16[32,3968]{1,0:T(8,128)(2,1)S(1)}, u32[]{:S(2)}, u32[]{:S(2)}) %collective-permute-start.19) | collective-permute-done | bytes 253984 | tf_op jit(solution)/shard_map/ppermute | solution.py:123
  75.5 2.0 %collective-permute-start.22 = (bf16[32,3968]{1,0:T(8,128)(2,1)S(1)}, bf16[32,3968]{1,0:T(8,128)(2,1)S(1)}, u32[]{:S(2)}, u32[]{:S(2)}) collective-permute-start(bf16[32,3968]{1,0:T(8,128)(2,1)S(1)} %collective-permute-done.18.refs_0_), channel_id=1, source_target_pairs={{0,16},{16,0},{1,17},{17,1},{2,18},{18,2},{3,19},{19,3},{4,20},{20... | collective-permute-start | bytes 761864 | tf_op jit(solution)/shard_map/ppermute | solution.py:123
  77.6 3.8 %collective-permute-start.25 = (bf16[64,512]{1,0:T(8,128)(2,1)S(1)}, bf16[64,512]{1,0:T(8,128)(2,1)S(1)}, u32[]{:S(2)}, u32[]{:S(2)}) collective-permute-start(bf16[64,512]{1,0:T(8,128)(2,1)S(1)} %maximum_maximum_fusion), channel_id=1, source_target_pairs={{4,0},{8,4},{12,8},{0,12},{5,1},{9,5},{13,9},{1,13},{6,2},{10,6},{... | collective-permute-start | bytes 196616 | tf_op jit(solution)/shard_map/ppermute | solution.py:170
  84.6 1.3 %collective-permute-done.27 = f32[2,64,256]{2,1,0:T(8,128)S(1)} collective-permute-done((f32[2,64,256]{2,1,0:T(8,128)S(1)}, f32[2,64,256]{2,1,0:T(8,128)S(1)}, u32[]{:S(2)}, u32[]{:S(2)}) %collective-permute-start.27) | collective-permute-done | bytes 131104 | tf_op jit(solution)/shard_map/ppermute | solution.py:132
  85.9 1.4 %collective-permute-start.28 = (f32[1,64,256]{2,1,0:T(8,128)S(1)}, f32[1,64,256]{2,1,0:T(8,128)S(1)}, u32[]{:S(2)}, u32[]{:S(2)}) collective-permute-start(f32[1,64,256]{2,1,0:T(8,128)S(1)} %slice_bitcast_fusion.2), channel_id=1, source_target_pairs={{0,2},{1,3},{2,0},{3,1},{4,6},{5,7},{6,4},{7,5},{8,10},{9,11},{10,... | collective-permute-start | bytes 196616 | tf_op jit(solution)/shard_map/ppermute | solution.py:132
  87.3 2.9 %collective-permute-done.28 = f32[1,64,256]{2,1,0:T(8,128)S(1)} collective-permute-done((f32[1,64,256]{2,1,0:T(8,128)S(1)}, f32[1,64,256]{2,1,0:T(8,128)S(1)}, u32[]{:S(2)}, u32[]{:S(2)}) %collective-permute-start.28) | collective-permute-done | bytes 65568 | tf_op jit(solution)/shard_map/ppermute | solution.py:132
  (57 shorter events, 21.4 us)
Async XLA Ops:
  0.0 8.2 %copy-start = (bf16[64,16384]{1,0:T(8,128)(2,1)S(1)}, bf16[64,16384]{1,0:T(8,128)(2,1)}, u32[]{:S(2)}) copy-start(bf16[64,16384]{1,0:T(8,128)(2,1)} %test.1) | copy-start | bytes 6291460
  1.3 12.1 %collective-permute-start.3 = (bf16[32,3968]{1,0:T(8,128)(2,1)S(1)}, bf16[32,3968]{1,0:T(8,128)(2,1)S(1)}, u32[]{:S(2)}, u32[]{:S(2)}) collective-permute-start(bf16[32,3968]{1,0:T(8,128)(2,1)S(1)} %slice_select_fusion.3), channel_id=1, source_target_pairs={{0,4},{4,8},{8,12},{12,0},{1,5},{5,9},{9,13},{13,1},{2,6},{6,10},{... | collective-permute-start | bytes 761864 | tf_op jit(solution)/shard_map/ppermute | solution.py:114
  5.4 13.3 %collective-permute-start = (bf16[32,3968]{1,0:T(8,128)(2,1)S(1)}, bf16[32,3968]{1,0:T(8,128)(2,1)S(1)}, u32[]{:S(2)}, u32[]{:S(2)}) collective-permute-start(bf16[32,3968]{1,0:T(8,128)(2,1)S(1)} %slice_select_fusion.2), channel_id=1, source_target_pairs={{0,4},{4,8},{8,12},{12,0},{1,5},{5,9},{9,13},{13,1},{2,6},{6,10},{... | collective-permute-start | bytes 761864 | tf_op jit(solution)/shard_map/ppermute | solution.py:114
  8.2 4.0 %copy-start.1 = (f32[16384]{0:T(1024)S(1)}, f32[16384]{0:T(1024)}, u32[]{:S(2)}) copy-start(f32[16384]{0:T(1024)} %param.5) | copy-start | bytes 196612
  13.3 10.8 %collective-permute-start.7 = (bf16[32,3968]{1,0:T(8,128)(2,1)S(1)}, bf16[32,3968]{1,0:T(8,128)(2,1)S(1)}, u32[]{:S(2)}, u32[]{:S(2)}) collective-permute-start(bf16[32,3968]{1,0:T(8,128)(2,1)S(1)} %slice_select_fusion.1), channel_id=1, source_target_pairs={{0,4},{4,8},{8,12},{12,0},{1,5},{5,9},{9,13},{13,1},{2,6},{6,10},{... | collective-permute-start | bytes 761864 | tf_op jit(solution)/shard_map/ppermute | solution.py:114
  13.9 10.2 %collective-permute-start.4 = (bf16[32,3968]{1,0:T(8,128)(2,1)S(1)}, bf16[32,3968]{1,0:T(8,128)(2,1)S(1)}, u32[]{:S(2)}, u32[]{:S(2)}) collective-permute-start(bf16[32,3968]{1,0:T(8,128)(2,1)S(1)} %collective-permute-done.3.refs_0_), channel_id=1, source_target_pairs={{0,16},{16,0},{1,17},{17,1},{2,18},{18,2},{3,19},{19,3},{4,20},{20... | collective-permute-start | bytes 761864 | tf_op jit(solution)/shard_map/ppermute | solution.py:123
  18.8 8.6 %collective-permute-start.2 = (bf16[32,3968]{1,0:T(8,128)(2,1)S(1)}, bf16[32,3968]{1,0:T(8,128)(2,1)S(1)}, u32[]{:S(2)}, u32[]{:S(2)}) collective-permute-start(bf16[32,3968]{1,0:T(8,128)(2,1)S(1)} %collective-permute-done.refs_0_), channel_id=1, source_target_pairs={{0,16},{16,0},{1,17},{17,1},{2,18},{18,2},{3,19},{19,3},{4,20},{20... | collective-permute-start | bytes 761864 | tf_op jit(solution)/shard_map/ppermute | solution.py:123
  20.5 8.3 %collective-permute-start.1 = (bf16[32,3968]{1,0:T(8,128)(2,1)S(1)}, bf16[32,3968]{1,0:T(8,128)(2,1)S(1)}, u32[]{:S(2)}, u32[]{:S(2)}) collective-permute-start(bf16[32,3968]{1,0:T(8,128)(2,1)S(1)} %slice_select_fusion), channel_id=1, source_target_pairs={{0,4},{4,8},{8,12},{12,0},{1,5},{5,9},{9,13},{13,1},{2,6},{6,10},{... | collective-permute-start | bytes 761864 | tf_op jit(solution)/shard_map/ppermute | solution.py:114
  24.1 8.9 %collective-permute-start.8 = (bf16[32,3968]{1,0:T(8,128)(2,1)S(1)}, bf16[32,3968]{1,0:T(8,128)(2,1)S(1)}, u32[]{:S(2)}, u32[]{:S(2)}) collective-permute-start(bf16[32,3968]{1,0:T(8,128)(2,1)S(1)} %collective-permute-done.7.refs_0_), channel_id=1, source_target_pairs={{0,16},{16,0},{1,17},{17,1},{2,18},{18,2},{3,19},{19,3},{4,20},{20... | collective-permute-start | bytes 761864 | tf_op jit(solution)/shard_map/ppermute | solution.py:123
  26.7 10.3 %collective-permute-start.11 = (bf16[32,3968]{1,0:T(8,128)(2,1)S(1)}, bf16[32,3968]{1,0:T(8,128)(2,1)S(1)}, u32[]{:S(2)}, u32[]{:S(2)}) collective-permute-start(bf16[32,3968]{1,0:T(8,128)(2,1)S(1)} %collective-permute-done.3.refs_0_), channel_id=1, source_target_pairs={{0,4},{4,8},{8,12},{12,0},{1,5},{5,9},{9,13},{13,1},{2,6},{6,10},{... | collective-permute-start | bytes 761864 | tf_op jit(solution)/shard_map/ppermute | solution.py:114
  29.6 11.9 %collective-permute-start.5 = (bf16[32,3968]{1,0:T(8,128)(2,1)S(1)}, bf16[32,3968]{1,0:T(8,128)(2,1)S(1)}, u32[]{:S(2)}, u32[]{:S(2)}) collective-permute-start(bf16[32,3968]{1,0:T(8,128)(2,1)S(1)} %collective-permute-done.refs_0_), channel_id=1, source_target_pairs={{0,4},{4,8},{8,12},{12,0},{1,5},{5,9},{9,13},{13,1},{2,6},{6,10},{... | collective-permute-start | bytes 761864 | tf_op jit(solution)/shard_map/ppermute | solution.py:114
  30.5 9.1 %collective-permute-start.6 = (bf16[32,3968]{1,0:T(8,128)(2,1)S(1)}, bf16[32,3968]{1,0:T(8,128)(2,1)S(1)}, u32[]{:S(2)}, u32[]{:S(2)}) collective-permute-start(bf16[32,3968]{1,0:T(8,128)(2,1)S(1)} %collective-permute-done.1.refs_0_), channel_id=1, source_target_pairs={{0,16},{16,0},{1,17},{17,1},{2,18},{18,2},{3,19},{19,3},{4,20},{20... | collective-permute-start | bytes 761864 | tf_op jit(solution)/shard_map/ppermute | solution.py:123
  37.0 8.9 %collective-permute-start.12 = (bf16[32,3968]{1,0:T(8,128)(2,1)S(1)}, bf16[32,3968]{1,0:T(8,128)(2,1)S(1)}, u32[]{:S(2)}, u32[]{:S(2)}) collective-permute-start(bf16[32,3968]{1,0:T(8,128)(2,1)S(1)} %collective-permute-done.11.refs_0_), channel_id=1, source_target_pairs={{0,16},{16,0},{1,17},{17,1},{2,18},{18,2},{3,19},{19,3},{4,20},{20... | collective-permute-start | bytes 761864 | tf_op jit(solution)/shard_map/ppermute | solution.py:123
  37.2 9.5 %collective-permute-start.16 = (bf16[32,3968]{1,0:T(8,128)(2,1)S(1)}, bf16[32,3968]{1,0:T(8,128)(2,1)S(1)}, u32[]{:S(2)}, u32[]{:S(2)}) collective-permute-start(bf16[32,3968]{1,0:T(8,128)(2,1)S(1)} %collective-permute-done.7.refs_0_), channel_id=1, source_target_pairs={{0,4},{4,8},{8,12},{12,0},{1,5},{5,9},{9,13},{13,1},{2,6},{6,10},{... | collective-permute-start | bytes 761864 | tf_op jit(solution)/shard_map/ppermute | solution.py:114
  41.4 9.9 %collective-permute-start.10 = (bf16[32,3968]{1,0:T(8,128)(2,1)S(1)}, bf16[32,3968]{1,0:T(8,128)(2,1)S(1)}, u32[]{:S(2)}, u32[]{:S(2)}) collective-permute-start(bf16[32,3968]{1,0:T(8,128)(2,1)S(1)} %collective-permute-done.5.refs_0_), channel_id=1, source_target_pairs={{0,16},{16,0},{1,17},{17,1},{2,18},{18,2},{3,19},{19,3},{4,20},{20... | collective-permute-start | bytes 761864 | tf_op jit(solution)/shard_map/ppermute | solution.py:123
  42.7 10.9 %collective-permute-start.9 = (bf16[32,3968]{1,0:T(8,128)(2,1)S(1)}, bf16[32,3968]{1,0:T(8,128)(2,1)S(1)}, u32[]{:S(2)}, u32[]{:S(2)}) collective-permute-start(bf16[32,3968]{1,0:T(8,128)(2,1)S(1)} %collective-permute-done.1.refs_0_), channel_id=1, source_target_pairs={{0,4},{4,8},{8,12},{12,0},{1,5},{5,9},{9,13},{13,1},{2,6},{6,10},{... | collective-permute-start | bytes 761864 | tf_op jit(solution)/shard_map/ppermute | solution.py:114
  43.4 11.6 %collective-permute-start.13 = (bf16[64,512]{1,0:T(8,128)(2,1)S(1)}, bf16[64,512]{1,0:T(8,128)(2,1)S(1)}, u32[]{:S(2)}, u32[]{:S(2)}) collective-permute-start(bf16[64,512]{1,0:T(8,128)(2,1)S(1)} %maximum_maximum_fusion), channel_id=1, source_target_pairs={{0,4},{4,8},{8,12},{12,0},{1,5},{5,9},{9,13},{13,1},{2,6},{6,10},{... | collective-permute-start | bytes 196616 | tf_op jit(solution)/shard_map/ppermute | solution.py:170
  46.7 10.0 %collective-permute-start.17 = (bf16[32,3968]{1,0:T(8,128)(2,1)S(1)}, bf16[32,3968]{1,0:T(8,128)(2,1)S(1)}, u32[]{:S(2)}, u32[]{:S(2)}) collective-permute-start(bf16[32,3968]{1,0:T(8,128)(2,1)S(1)} %collective-permute-done.16.refs_0_), channel_id=1, source_target_pairs={{0,16},{16,0},{1,17},{17,1},{2,18},{18,2},{3,19},{19,3},{4,20},{20... | collective-permute-start | bytes 761864 | tf_op jit(solution)/shard_map/ppermute | solution.py:123
  49.9 10.4 %collective-permute-start.20 = (bf16[32,3968]{1,0:T(8,128)(2,1)S(1)}, bf16[32,3968]{1,0:T(8,128)(2,1)S(1)}, u32[]{:S(2)}, u32[]{:S(2)}) collective-permute-start(bf16[32,3968]{1,0:T(8,128)(2,1)S(1)} %collective-permute-done.11.refs_0_), channel_id=1, source_target_pairs={{0,4},{4,8},{8,12},{12,0},{1,5},{5,9},{9,13},{13,1},{2,6},{6,10},{... | collective-permute-start | bytes 761864 | tf_op jit(solution)/shard_map/ppermute | solution.py:114
  54.9 9.6 %collective-permute-start.14 = (bf16[32,3968]{1,0:T(8,128)(2,1)S(1)}, bf16[32,3968]{1,0:T(8,128)(2,1)S(1)}, u32[]{:S(2)}, u32[]{:S(2)}) collective-permute-start(bf16[32,3968]{1,0:T(8,128)(2,1)S(1)} %collective-permute-done.5.refs_0_), channel_id=1, source_target_pairs={{0,4},{4,8},{8,12},{12,0},{1,5},{5,9},{9,13},{13,1},{2,6},{6,10},{... | collective-permute-start | bytes 761864 | tf_op jit(solution)/shard_map/ppermute | solution.py:114
  54.9 9.6 %collective-permute-start.15 = (bf16[32,3968]{1,0:T(8,128)(2,1)S(1)}, bf16[32,3968]{1,0:T(8,128)(2,1)S(1)}, u32[]{:S(2)}, u32[]{:S(2)}) collective-permute-start(bf16[32,3968]{1,0:T(8,128)(2,1)S(1)} %collective-permute-done.9.refs_0_), channel_id=1, source_target_pairs={{0,16},{16,0},{1,17},{17,1},{2,18},{18,2},{3,19},{19,3},{4,20},{20... | collective-permute-start | bytes 761864 | tf_op jit(solution)/shard_map/ppermute | solution.py:123
  60.2 8.9 %collective-permute-start.21 = (bf16[32,3968]{1,0:T(8,128)(2,1)S(1)}, bf16[32,3968]{1,0:T(8,128)(2,1)S(1)}, u32[]{:S(2)}, u32[]{:S(2)}) collective-permute-start(bf16[32,3968]{1,0:T(8,128)(2,1)S(1)} %collective-permute-done.20.refs_0_), channel_id=1, source_target_pairs={{0,16},{16,0},{1,17},{17,1},{2,18},{18,2},{3,19},{19,3},{4,20},{20... | collective-permute-start | bytes 761864 | tf_op jit(solution)/shard_map/ppermute | solution.py:123
  62.9 8.3 %collective-permute-start.23 = (bf16[32,3968]{1,0:T(8,128)(2,1)S(1)}, bf16[32,3968]{1,0:T(8,128)(2,1)S(1)}, u32[]{:S(2)}, u32[]{:S(2)}) collective-permute-start(bf16[32,3968]{1,0:T(8,128)(2,1)S(1)} %collective-permute-done.16.refs_0_), channel_id=1, source_target_pairs={{0,4},{4,8},{8,12},{12,0},{1,5},{5,9},{9,13},{13,1},{2,6},{6,10},{... | collective-permute-start | bytes 761864 | tf_op jit(solution)/shard_map/ppermute | solution.py:114
  65.3 8.6 %collective-permute-start.18 = (bf16[32,3968]{1,0:T(8,128)(2,1)S(1)}, bf16[32,3968]{1,0:T(8,128)(2,1)S(1)}, u32[]{:S(2)}, u32[]{:S(2)}) collective-permute-start(bf16[32,3968]{1,0:T(8,128)(2,1)S(1)} %collective-permute-done.9.refs_0_), channel_id=1, source_target_pairs={{0,4},{4,8},{8,12},{12,0},{1,5},{5,9},{9,13},{13,1},{2,6},{6,10},{... | collective-permute-start | bytes 761864 | tf_op jit(solution)/shard_map/ppermute | solution.py:114
  65.5 10.0 %collective-permute-start.19 = (bf16[32,3968]{1,0:T(8,128)(2,1)S(1)}, bf16[32,3968]{1,0:T(8,128)(2,1)S(1)}, u32[]{:S(2)}, u32[]{:S(2)}) collective-permute-start(bf16[32,3968]{1,0:T(8,128)(2,1)S(1)} %collective-permute-done.14.refs_0_), channel_id=1, source_target_pairs={{0,16},{16,0},{1,17},{17,1},{2,18},{18,2},{3,19},{19,3},{4,20},{20... | collective-permute-start | bytes 761864 | tf_op jit(solution)/shard_map/ppermute | solution.py:123
  71.2 11.0 %collective-permute-start.26 = (bf16[32,3968]{1,0:T(8,128)(2,1)S(1)}, bf16[32,3968]{1,0:T(8,128)(2,1)S(1)}, u32[]{:S(2)}, u32[]{:S(2)}) collective-permute-start(bf16[32,3968]{1,0:T(8,128)(2,1)S(1)} %collective-permute-done.23.refs_0_), channel_id=1, source_target_pairs={{0,16},{16,0},{1,17},{17,1},{2,18},{18,2},{3,19},{19,3},{4,20},{20... | collective-permute-start | bytes 761864 | tf_op jit(solution)/shard_map/ppermute | solution.py:123
  75.5 8.1 %collective-permute-start.22 = (bf16[32,3968]{1,0:T(8,128)(2,1)S(1)}, bf16[32,3968]{1,0:T(8,128)(2,1)S(1)}, u32[]{:S(2)}, u32[]{:S(2)}) collective-permute-start(bf16[32,3968]{1,0:T(8,128)(2,1)S(1)} %collective-permute-done.18.refs_0_), channel_id=1, source_target_pairs={{0,16},{16,0},{1,17},{17,1},{2,18},{18,2},{3,19},{19,3},{4,20},{20... | collective-permute-start | bytes 761864 | tf_op jit(solution)/shard_map/ppermute | solution.py:123
  77.6 6.1 %collective-permute-start.24 = (bf16[64,512]{1,0:T(8,128)(2,1)S(1)}, bf16[64,512]{1,0:T(8,128)(2,1)S(1)}, u32[]{:S(2)}, u32[]{:S(2)}) collective-permute-start(bf16[64,512]{1,0:T(8,128)(2,1)S(1)} %collective-permute-done.13.refs_5_), channel_id=1, source_target_pairs={{0,4},{4,8},{8,12},{12,0},{1,5},{5,9},{9,13},{13,1},{2,6},{6,10},{... | collective-permute-start | bytes 196616 | tf_op jit(solution)/shard_map/ppermute | solution.py:170
  77.6 6.1 %collective-permute-start.25 = (bf16[64,512]{1,0:T(8,128)(2,1)S(1)}, bf16[64,512]{1,0:T(8,128)(2,1)S(1)}, u32[]{:S(2)}, u32[]{:S(2)}) collective-permute-start(bf16[64,512]{1,0:T(8,128)(2,1)S(1)} %maximum_maximum_fusion), channel_id=1, source_target_pairs={{4,0},{8,4},{12,8},{0,12},{5,1},{9,5},{13,9},{1,13},{6,2},{10,6},{... | collective-permute-start | bytes 196616 | tf_op jit(solution)/shard_map/ppermute | solution.py:170
  84.5 1.4 %collective-permute-start.27 = (f32[2,64,256]{2,1,0:T(8,128)S(1)}, f32[2,64,256]{2,1,0:T(8,128)S(1)}, u32[]{:S(2)}, u32[]{:S(2)}) collective-permute-start(f32[2,64,256]{2,1,0:T(8,128)S(1)} %slice_bitcast_fusion), channel_id=1, source_target_pairs={{0,1},{1,0},{2,3},{3,2},{4,5},{5,4},{6,7},{7,6},{8,9},{9,8},{10,11... | collective-permute-start | bytes 393224 | tf_op jit(solution)/shard_map/ppermute | solution.py:132
  85.9 4.3 %collective-permute-start.28 = (f32[1,64,256]{2,1,0:T(8,128)S(1)}, f32[1,64,256]{2,1,0:T(8,128)S(1)}, u32[]{:S(2)}, u32[]{:S(2)}) collective-permute-start(f32[1,64,256]{2,1,0:T(8,128)S(1)} %slice_bitcast_fusion.2), channel_id=1, source_target_pairs={{0,2},{1,3},{2,0},{3,1},{4,6},{5,7},{6,4},{7,5},{8,10},{9,11},{10,... | collective-permute-start | bytes 196616 | tf_op jit(solution)/shard_map/ppermute | solution.py:132

commit v20 on v18

v20 whole, which is shorter than its diff:
```python
import functools

import jax
import jax.numpy as jnp
from jax import lax
from jax.experimental import pallas as pl
from jax.experimental.pallas import tpu as pltpu
from jax.sharding import PartitionSpec as P

CONTRACT = (((1,), (1,)), ((), ()))
LANES = 128
CHUNKS = 4


def product(rows, scale, train, unit):
    width, total = train.shape[1], None
    for at in range(0, width, unit):
        here = slice(at, min(at + unit, width))
        precond = (rows(here).astype(jnp.float32) * scale(here)).astype(jnp.bfloat16)
        part = lax.dot_general(
            precond, train[:, here], CONTRACT, preferred_element_type=jnp.float32
        )
        total = part if total is None else total + part
    return total


def own_kernel(starts, unit, test, scale, *refs):
    trains, out = refs[:-1], refs[-1]
    total = None
    for start, train in zip(starts, trains):
        column = lambda here: slice(start + here.start, start + here.stop)
        rows, scales = (lambda here, a=a: a[:, column(here)] for a in (test, scale))
        part = product(rows, scales, train, unit)
        total = part if total is None else total + part
    out[...] = total


def arrived_rows(parts):
    return lambda here: jnp.concatenate([p[:, here] for p in parts], axis=0)


def part_kernel(start, unit, n_parts, has_base, *refs):
    parts, (scale, train) = refs[:n_parts], refs[n_parts : n_parts + 2]
    column = lambda here: scale[:, start + here.start : start + here.stop]
    total = product(arrived_rows(parts), column, train, unit)
    refs[-1][...] = total + refs[n_parts + 2][...] if has_base else total


def last_kernel(n_grp, n_ex, n_feat, start, unit, n_parts, *refs):
    parts, (scale, train) = refs[:n_parts], refs[n_parts : n_parts + 2]
    sums, (out, kept) = refs[n_parts + 2 : -2], refs[-2:]
    column = lambda here: scale[:, start + here.start : start + here.stop]
    total = product(arrived_rows(parts), column, train, unit) + sums[-1][...]
    queries = total.shape[0]
    half = queries // n_grp
    for t, value in enumerate([s[...] for s in sums[:-1]] + [total]):
        kept[t * queries : (t + 1) * queries, :] = value
    ex, grp, feat = (lax.axis_index(a) for a in ("ex", "grp", "feat"))
    units = n_ex * n_grp
    each = units // n_feat
    for to in range(units):
        unit_of = (feat ^ (to // each)) * each + to % each
        t = lax.rem(ex + (n_ex - lax.div(unit_of, n_grp)), n_ex)
        h = lax.rem(unit_of, n_grp)
        place = jnp.where(t == 0, h, lax.rem(h + n_grp - grp, n_grp))
        at = pl.multiple_of(t * queries + place * half, half)
        out[to * half : (to + 1) * half, :] = kept[pl.ds(at, half), :]


def call(kernel, rows, docs, width, operands, scratch=()):
    return pl.pallas_call(
        kernel,
        out_shape=jax.ShapeDtypeStruct((rows, docs), jnp.float32),
        in_specs=[pl.BlockSpec(memory_space=pltpu.VMEM)] * len(operands),
        out_specs=pl.BlockSpec(memory_space=pltpu.VMEM),
        scratch_shapes=scratch,
        cost_estimate=pl.CostEstimate(
            flops=2 * rows * docs * width, bytes_accessed=2 * (rows + docs) * width, transcendentals=0
        ),
        compiler_params=pltpu.CompilerParams(vmem_limit_bytes=16 * 1024 * 1024),
    )(*operands)


def solution(mesh):
    n_grp, n_ex, n_feat = (mesh.shape[a] for a in ("grp", "ex", "feat"))
    assert n_grp <= 2

    def on_device(train, test, hess):
        docs, feats = train.shape
        queries = test.shape[0]
        half = queries // n_grp
        unit = 8 * LANES
        lanes = feats // LANES
        cuts = [c * lanes // CHUNKS * LANES for c in range(CHUNKS + 1)]
        starts, columns = cuts[:-1], [slice(*ends) for ends in zip(cuts[:-1], cuts[1:])]
        first_grp = lax.axis_index("grp") == 0
        ring = [(i, (i + 1) % n_ex) for i in range(n_ex)]
        hops, swaps, made, first = [], [], [], []

        def after(block, *waits):
            return lax.optimization_barrier((block, waits))[0] if waits else block

        def hop(block):
            waits = hops[-2:-1] + swaps[-4:-3] + made[-4:-3] + (first if len(hops) == 3 else [])
            hops.append(lax.ppermute(after(block, *waits), "ex", ring))
            return hops[-1]

        def swap(block):
            if n_grp == 1:
                return [block]
            waits = swaps[-2:-1]
            if len(swaps) > (n_ex - 2) * CHUNKS:
                waits = swaps[-3:-2] + made[-3:-2]
            swaps.append(lax.ppermute(after(block, *waits), "grp", [(0, 1), (1, 0)]))
            return [block, swaps[-1]]

        def sum_over_feat(sums):
            held = sums.reshape(n_feat, -1, docs)
            bit = 1
            while bit < n_feat:
                pairs = held.reshape((-1, 2) + held.shape[1:])
                partner = [(i, i ^ bit) for i in range(n_feat)]
                held = pairs[:, 0] + lax.ppermute(pairs[:, 1], "feat", partner)
                bit *= 2
            return held[0]

        def share(rows, columns):
            if n_grp == 1:
                return rows[:, columns]
            return jnp.where(first_grp, rows[:half, columns], rows[half:, columns])

        scale = (1.0 / (hess + jnp.float32(0.1))).reshape(1, feats)
        held = []
        for here in columns:
            held.append(share(after(test, *held[-1:]), here))
        trains = [train[:, here] for here in columns]
        own = call(
            functools.partial(own_kernel, starts, unit), queries, docs, feats, [test, scale, *trains]
        )
        first.append(own)
        final = n_ex - 1
        sums = [own] + [None] * final
        for t in range(1, n_ex):
            for c, (start, here) in enumerate(zip(starts, columns)):
                held[c] = hop(held[c])
                parts = swap(held[c])
                operands = [*parts, scale, trains[c]]
                if (t, c) == (final, CHUNKS - 1):
                    continue
                base = [] if sums[t] is None else [sums[t]]
                sums[t] = call(
                    functools.partial(part_kernel, start, unit, len(parts), len(base)),
                    queries, docs, here.stop - here.start, operands + base,
                )
                made.append(sums[t])
        total = call(
            functools.partial(last_kernel, n_grp, n_ex, n_feat, start, unit, len(parts)),
            n_ex * queries, docs, here.stop - here.start, [*operands, *sums],
            [pltpu.VMEM((n_ex * queries, docs), jnp.float32)],
        )
        return sum_over_feat(total).T

    return jax.shard_map(
        on_device,
        mesh=mesh,
        in_specs=(P(("grp", "ex"), "feat"), P("ex", "feat"), P("feat")),
        out_specs=P(("grp", "ex"), "feat"),
        check_vma=False,
    )
```

time: 94.3 us -> 90.9 us (0.964)
  starting transfers between devices: 27 us -> 24.5 us
  local copies, waits for them, and re-layouts: 5.25 us -> 4 us
    ppermute x12, waiting for transfers between devices: 3.69 us -> 13 us  [swap(): swaps.append(lax.ppermute(after(block, *waits), 'grp', [(0, 1), (1, 0)]))]
    ppermute x15 -> x12, waiting for transfers between devices: 38.2 us -> 29.5 us  [hop(): hops.append(lax.ppermute(after(block, *waits), 'ex', ring))]
    ppermute x15 -> x12, starting transfers between devices: 8.96 us -> 5.33 us  [hop(): hops.append(lax.ppermute(after(block, *waits), 'ex', ring))]
    slice x2 -> x1, local copies, waits for them, and re-layouts: 5.22 us -> 3.97 us  [on_device(): trains = [train[:, here] for here in columns]]
    select_n x5 -> x4, other arithmetic: 3.32 us -> 3.36 us  [share(): return jnp.where(first_grp, rows[:half, columns], rows[half:, columns])]
  transfers between devices with their start and end apart: 29 -> 26, of which waited for: 21 -> 23; matrix products, arithmetic and copies ran while one was open for 8% -> 7% of each run, Pallas kernels for 11% -> 12%
where the time goes in v20:
time: 90.9 us; the launch traced here: 90.7 us
  waiting for transfers between devices  46.2 us (51%)
  starting transfers between devices  24.5 us (27%)
  Pallas kernels  11.8 us (13%)
  other arithmetic  4.03 us (4%)
  local copies, waits for them, and re-layouts  4 us (4%)
    ppermute x12, waiting for transfers between devices, hop(): hops.append(lax.ppermute(after(block, *waits), 'ex', ring))  29.5 us
    ppermute x12, starting transfers between devices, swap(): swaps.append(lax.ppermute(after(block, *waits), 'grp', [(0, 1), (1, 0)]))  17.2 us
    ppermute x12, waiting for transfers between devices, swap(): swaps.append(lax.ppermute(after(block, *waits), 'grp', [(0, 1), (1, 0)]))  13 us
    pallas_call x13, Pallas kernels, call(): pl.pallas_call(kernel, out_shape=jax.ShapeDtypeStruct((rows, docs), jnp.f...  11.8 us
    ppermute x12, starting transfers between devices, hop(): hops.append(lax.ppermute(after(block, *waits), 'ex', ring))  5.33 us
    slice x1, local copies, waits for them, and re-layouts, on_device(): trains = [train[:, here] for here in columns]  3.97 us
    ppermute x2, waiting for transfers between devices, sum_over_feat(): held = pairs[:, 0] + lax.ppermute(pairs[:, 1], 'feat', partner)  3.74 us
    select_n x4, other arithmetic, share(): return jnp.where(first_grp, rows[:half, columns], rows[half:, columns])  3.36 us
  transfers between devices with their start and end apart: 26, of which 23 were waited for; matrix products, arithmetic and copies ran while one was open for 7% of the time, Pallas kernels for 12%

profile of v20, /device:TPU:0, one launch (start us, length us, event | category | flops | bytes accessed | tf_op | source)
XLA Modules:
  0.0 90.7 jit_solution(10653414401948372917)
XLA Ops:
  1.2 3.1 %collective-permute-start.3 = (bf16[32,4096]{1,0:T(8,128)(2,1)S(1)}, bf16[32,4096]{1,0:T(8,128)(2,1)S(1)}, u32[]{:S(2)}, u32[]{:S(2)}) collective-permute-start(bf16[32,4096]{1,0:T(8,128)(2,1)S(1)} %slice_select_fusion.3), channel_id=1, source_target_pairs={{0,4},{4,8},{8,12},{12,0},{1,5},{5,9},{9,13},{13,1},{2,6},{6,10},{... | collective-permute-start | bytes 786440 | tf_op jit(solution)/shard_map/ppermute | solution.py:105
  5.4 1.6 %collective-permute-start = (bf16[32,4096]{1,0:T(8,128)(2,1)S(1)}, bf16[32,4096]{1,0:T(8,128)(2,1)S(1)}, u32[]{:S(2)}, u32[]{:S(2)}) collective-permute-start(bf16[32,4096]{1,0:T(8,128)(2,1)S(1)} %slice_select_fusion.2), channel_id=1, source_target_pairs={{0,4},{4,8},{8,12},{12,0},{1,5},{5,9},{9,13},{13,1},{2,6},{6,10},{... | collective-permute-start | bytes 786440 | tf_op jit(solution)/shard_map/ppermute | solution.py:105
  8.1 4.0 %fusion.4 = (bf16[256,4096]{1,0:T(8,128)(2,1)S(1)}, bf16[256,4096]{1,0:T(8,128)(2,1)S(1)}, bf16[256,4096]{1,0:T(8,128)(2,1)S(1)}, bf16[256,4096]{1,0:T(8,128)(2,1)S(1)}) fusion(bf16[256,16384]{1,0:T(8,128)(2,1)} %param.3), kind=kLoop, calls=%fused_computation.13 | loop fusion | bytes 16777216 | tf_op jit(solution)/shard_map/slice | solution.py:136
  12.1 1.3 %collective-permute-done.3.refs_0_ = bf16[32,4096]{1,0:T(8,128)(2,1)S(1)} collective-permute-done((bf16[32,4096]{1,0:T(8,128)(2,1)S(1)}, bf16[32,4096]{1,0:T(8,128)(2,1)S(1)}, u32[]{:S(2)}, u32[]{:S(2)}) %collective-permute-start.3) | collective-permute-done | bytes 262176 | tf_op jit(solution)/shard_map/ppermute | solution.py:105
  13.8 1.5 %collective-permute-start.4 = (bf16[32,4096]{1,0:T(8,128)(2,1)S(1)}, bf16[32,4096]{1,0:T(8,128)(2,1)S(1)}, u32[]{:S(2)}, u32[]{:S(2)}) collective-permute-start(bf16[32,4096]{1,0:T(8,128)(2,1)S(1)} %collective-permute-done.3.refs_0_), channel_id=1, source_target_pairs={{0,16},{16,0},{1,17},{17,1},{2,18},{18,2},{3,19},{19,3},{4,20},{20... | collective-permute-start | bytes 786440 | tf_op jit(solution)/shard_map/ppermute | solution.py:114
  15.3 2.7 %shard_map.37.refs_4_ = f32[64,256]{1,0:T(8,128)S(1)} custom-call(bf16[64,16384]{1,0:T(8,128)(2,1)S(1)} %copy-done, f32[1,16384]{1,0:T(1,128)S(1)} %bitcast.28, bf16[256,4096]{1,0:T(8,128)(2,1)S(1)} %get-tuple-element.53.refs_0_.refs_3_, bf16[256,4096]{1,0:T(8,128)(2,1)S(1)} %get-tuple-element.52.refs_1_.refs_3_, ...), custom_call_target="tpu_custom_call" | custom-call | flops 536870912 | bytes 10485760 | tf_op jit(solution)/shard_map/pallas_call | solution.py:71
  19.1 1.8 %collective-permute-start.2 = (bf16[32,4096]{1,0:T(8,128)(2,1)S(1)}, bf16[32,4096]{1,0:T(8,128)(2,1)S(1)}, u32[]{:S(2)}, u32[]{:S(2)}) collective-permute-start(bf16[32,4096]{1,0:T(8,128)(2,1)S(1)} %collective-permute-done.refs_0_), channel_id=1, source_target_pairs={{0,16},{16,0},{1,17},{17,1},{2,18},{18,2},{3,19},{19,3},{4,20},{20... | collective-permute-start | bytes 786440 | tf_op jit(solution)/shard_map/ppermute | solution.py:114
  20.8 3.8 %collective-permute-done.7.refs_0_ = bf16[32,4096]{1,0:T(8,128)(2,1)S(1)} collective-permute-done((bf16[32,4096]{1,0:T(8,128)(2,1)S(1)}, bf16[32,4096]{1,0:T(8,128)(2,1)S(1)}, u32[]{:S(2)}, u32[]{:S(2)}) %collective-permute-start.7) | collective-permute-done | bytes 262176 | tf_op jit(solution)/shard_map/ppermute | solution.py:105
  24.7 1.8 %collective-permute-start.8 = (bf16[32,4096]{1,0:T(8,128)(2,1)S(1)}, bf16[32,4096]{1,0:T(8,128)(2,1)S(1)}, u32[]{:S(2)}, u32[]{:S(2)}) collective-permute-start(bf16[32,4096]{1,0:T(8,128)(2,1)S(1)} %collective-permute-done.7.refs_0_), channel_id=1, source_target_pairs={{0,16},{16,0},{1,17},{17,1},{2,18},{18,2},{3,19},{19,3},{4,20},{20... | collective-permute-start | bytes 786440 | tf_op jit(solution)/shard_map/ppermute | solution.py:114
  27.4 2.2 %collective-permute-done.1.refs_0_ = bf16[32,4096]{1,0:T(8,128)(2,1)S(1)} collective-permute-done((bf16[32,4096]{1,0:T(8,128)(2,1)S(1)}, bf16[32,4096]{1,0:T(8,128)(2,1)S(1)}, u32[]{:S(2)}, u32[]{:S(2)}) %collective-permute-start.1) | collective-permute-done | bytes 262176 | tf_op jit(solution)/shard_map/ppermute | solution.py:105
  29.5 2.3 %collective-permute-start.6 = (bf16[32,4096]{1,0:T(8,128)(2,1)S(1)}, bf16[32,4096]{1,0:T(8,128)(2,1)S(1)}, u32[]{:S(2)}, u32[]{:S(2)}) collective-permute-start(bf16[32,4096]{1,0:T(8,128)(2,1)S(1)} %collective-permute-done.1.refs_0_), channel_id=1, source_target_pairs={{0,16},{16,0},{1,17},{17,1},{2,18},{18,2},{3,19},{19,3},{4,20},{20... | collective-permute-start | bytes 786440 | tf_op jit(solution)/shard_map/ppermute | solution.py:114
  33.5 2.4 %collective-permute-done.11.refs_0_ = bf16[32,4096]{1,0:T(8,128)(2,1)S(1)} collective-permute-done((bf16[32,4096]{1,0:T(8,128)(2,1)S(1)}, bf16[32,4096]{1,0:T(8,128)(2,1)S(1)}, u32[]{:S(2)}, u32[]{:S(2)}) %collective-permute-start.11) | collective-permute-done | bytes 262176 | tf_op jit(solution)/shard_map/ppermute | solution.py:105
  35.9 2.1 %collective-permute-start.12 = (bf16[32,4096]{1,0:T(8,128)(2,1)S(1)}, bf16[32,4096]{1,0:T(8,128)(2,1)S(1)}, u32[]{:S(2)}, u32[]{:S(2)}) collective-permute-start(bf16[32,4096]{1,0:T(8,128)(2,1)S(1)} %collective-permute-done.11.refs_0_), channel_id=1, source_target_pairs={{0,16},{16,0},{1,17},{17,1},{2,18},{18,2},{3,19},{19,3},{4,20},{20... | collective-permute-start | bytes 786440 | tf_op jit(solution)/shard_map/ppermute | solution.py:114
  39.9 2.5 %collective-permute-done.5.refs_0_ = bf16[32,4096]{1,0:T(8,128)(2,1)S(1)} collective-permute-done((bf16[32,4096]{1,0:T(8,128)(2,1)S(1)}, bf16[32,4096]{1,0:T(8,128)(2,1)S(1)}, u32[]{:S(2)}, u32[]{:S(2)}) %collective-permute-start.5) | collective-permute-done | bytes 262176 | tf_op jit(solution)/shard_map/ppermute | solution.py:105
  42.4 1.3 %collective-permute-start.10 = (bf16[32,4096]{1,0:T(8,128)(2,1)S(1)}, bf16[32,4096]{1,0:T(8,128)(2,1)S(1)}, u32[]{:S(2)}, u32[]{:S(2)}) collective-permute-start(bf16[32,4096]{1,0:T(8,128)(2,1)S(1)} %collective-permute-done.5.refs_0_), channel_id=1, source_target_pairs={{0,16},{16,0},{1,17},{17,1},{2,18},{18,2},{3,19},{19,3},{4,20},{20... | collective-permute-start | bytes 786440 | tf_op jit(solution)/shard_map/ppermute | solution.py:114
  43.7 1.4 %collective-permute-done.12.refs_1_ = bf16[32,4096]{1,0:T(8,128)(2,1)S(1)} collective-permute-done((bf16[32,4096]{1,0:T(8,128)(2,1)S(1)}, bf16[32,4096]{1,0:T(8,128)(2,1)S(1)}, u32[]{:S(2)}, u32[]{:S(2)}) %collective-permute-start.12) | collective-permute-done | bytes 262176 | tf_op jit(solution)/shard_map/ppermute | solution.py:114
  45.8 3.1 %collective-permute-done.15.refs_0_ = bf16[32,4096]{1,0:T(8,128)(2,1)S(1)} collective-permute-done((bf16[32,4096]{1,0:T(8,128)(2,1)S(1)}, bf16[32,4096]{1,0:T(8,128)(2,1)S(1)}, u32[]{:S(2)}, u32[]{:S(2)}) %collective-permute-start.15) | collective-permute-done | bytes 262176 | tf_op jit(solution)/shard_map/ppermute | solution.py:105
  49.8 1.5 %collective-permute-done.10.refs_1_ = bf16[32,4096]{1,0:T(8,128)(2,1)S(1)} collective-permute-done((bf16[32,4096]{1,0:T(8,128)(2,1)S(1)}, bf16[32,4096]{1,0:T(8,128)(2,1)S(1)}, u32[]{:S(2)}, u32[]{:S(2)}) %collective-permute-start.10) | collective-permute-done | bytes 262176 | tf_op jit(solution)/shard_map/ppermute | solution.py:114
  51.3 3.4 %collective-permute-done.9.refs_0_ = bf16[32,4096]{1,0:T(8,128)(2,1)S(1)} collective-permute-done((bf16[32,4096]{1,0:T(8,128)(2,1)S(1)}, bf16[32,4096]{1,0:T(8,128)(2,1)S(1)}, u32[]{:S(2)}, u32[]{:S(2)}) %collective-permute-start.9) | collective-permute-done | bytes 262176 | tf_op jit(solution)/shard_map/ppermute | solution.py:105
  56.3 1.3 %collective-permute-done.16.refs_1_ = bf16[32,4096]{1,0:T(8,128)(2,1)S(1)} collective-permute-done((bf16[32,4096]{1,0:T(8,128)(2,1)S(1)}, bf16[32,4096]{1,0:T(8,128)(2,1)S(1)}, u32[]{:S(2)}, u32[]{:S(2)}) %collective-permute-start.16) | collective-permute-done | bytes 262176 | tf_op jit(solution)/shard_map/ppermute | solution.py:114
  57.6 2.3 %collective-permute-done.18.refs_0_ = bf16[32,4096]{1,0:T(8,128)(2,1)S(1)} collective-permute-done((bf16[32,4096]{1,0:T(8,128)(2,1)S(1)}, bf16[32,4096]{1,0:T(8,128)(2,1)S(1)}, u32[]{:S(2)}, u32[]{:S(2)}) %collective-permute-start.18) | collective-permute-done | bytes 262176 | tf_op jit(solution)/shard_map/ppermute | solution.py:105
  61.6 2.3 %collective-permute-done.14.refs_1_ = bf16[32,4096]{1,0:T(8,128)(2,1)S(1)} collective-permute-done((bf16[32,4096]{1,0:T(8,128)(2,1)S(1)}, bf16[32,4096]{1,0:T(8,128)(2,1)S(1)}, u32[]{:S(2)}, u32[]{:S(2)}) %collective-permute-start.14) | collective-permute-done | bytes 262176 | tf_op jit(solution)/shard_map/ppermute | solution.py:114
  64.7 2.5 %collective-permute-done.13.refs_0_ = bf16[32,4096]{1,0:T(8,128)(2,1)S(1)} collective-permute-done((bf16[32,4096]{1,0:T(8,128)(2,1)S(1)}, bf16[32,4096]{1,0:T(8,128)(2,1)S(1)}, u32[]{:S(2)}, u32[]{:S(2)}) %collective-permute-start.13) | collective-permute-done | bytes 262176 | tf_op jit(solution)/shard_map/ppermute | solution.py:105
  67.2 1.3 %collective-permute-start.23 = (bf16[32,4096]{1,0:T(8,128)(2,1)S(1)}, bf16[32,4096]{1,0:T(8,128)(2,1)S(1)}, u32[]{:S(2)}, u32[]{:S(2)}) collective-permute-start(bf16[32,4096]{1,0:T(8,128)(2,1)S(1)} %collective-permute-done.13.refs_0_), channel_id=1, source_target_pairs={{0,16},{16,0},{1,17},{17,1},{2,18},{18,2},{3,19},{19,3},{4,20},{20... | collective-permute-start | bytes 786440 | tf_op jit(solution)/shard_map/ppermute | solution.py:114
  68.5 4.0 %collective-permute-done.21.refs_0_ = bf16[32,4096]{1,0:T(8,128)(2,1)S(1)} collective-permute-done((bf16[32,4096]{1,0:T(8,128)(2,1)S(1)}, bf16[32,4096]{1,0:T(8,128)(2,1)S(1)}, u32[]{:S(2)}, u32[]{:S(2)}) %collective-permute-start.21) | collective-permute-done | bytes 262176 | tf_op jit(solution)/shard_map/ppermute | solution.py:105
  72.4 1.4 %collective-permute-start.22 = (bf16[32,4096]{1,0:T(8,128)(2,1)S(1)}, bf16[32,4096]{1,0:T(8,128)(2,1)S(1)}, u32[]{:S(2)}, u32[]{:S(2)}) collective-permute-start(bf16[32,4096]{1,0:T(8,128)(2,1)S(1)} %collective-permute-done.21.refs_0_), channel_id=1, source_target_pairs={{0,16},{16,0},{1,17},{17,1},{2,18},{18,2},{3,19},{19,3},{4,20},{20... | collective-permute-start | bytes 786440 | tf_op jit(solution)/shard_map/ppermute | solution.py:114
  75.4 1.3 %collective-permute-start.20 = (bf16[32,4096]{1,0:T(8,128)(2,1)S(1)}, bf16[32,4096]{1,0:T(8,128)(2,1)S(1)}, u32[]{:S(2)}, u32[]{:S(2)}) collective-permute-start(bf16[32,4096]{1,0:T(8,128)(2,1)S(1)} %collective-permute-done.17.refs_0_), channel_id=1, source_target_pairs={{0,16},{16,0},{1,17},{17,1},{2,18},{18,2},{3,19},{19,3},{4,20},{20... | collective-permute-start | bytes 786440 | tf_op jit(solution)/shard_map/ppermute | solution.py:114
  77.4 3.3 %collective-permute-done.22.refs_1_ = bf16[32,4096]{1,0:T(8,128)(2,1)S(1)} collective-permute-done((bf16[32,4096]{1,0:T(8,128)(2,1)S(1)}, bf16[32,4096]{1,0:T(8,128)(2,1)S(1)}, u32[]{:S(2)}, u32[]{:S(2)}) %collective-permute-start.22) | collective-permute-done | bytes 262176 | tf_op jit(solution)/shard_map/ppermute | solution.py:114
  81.5 2.0 %collective-permute-done.20.refs_1_ = bf16[32,4096]{1,0:T(8,128)(2,1)S(1)} collective-permute-done((bf16[32,4096]{1,0:T(8,128)(2,1)S(1)}, bf16[32,4096]{1,0:T(8,128)(2,1)S(1)}, u32[]{:S(2)}, u32[]{:S(2)}) %collective-permute-start.20) | collective-permute-done | bytes 262176 | tf_op jit(solution)/shard_map/ppermute | solution.py:114
  84.4 1.3 %collective-permute-done.24 = f32[2,64,256]{2,1,0:T(8,128)S(1)} collective-permute-done((f32[2,64,256]{2,1,0:T(8,128)S(1)}, f32[2,64,256]{2,1,0:T(8,128)S(1)}, u32[]{:S(2)}, u32[]{:S(2)}) %collective-permute-start.24) | collective-permute-done | bytes 131104 | tf_op jit(solution)/shard_map/ppermute | solution.py:123
  85.8 1.9 %collective-permute-start.25 = (f32[1,64,256]{2,1,0:T(8,128)S(1)}, f32[1,64,256]{2,1,0:T(8,128)S(1)}, u32[]{:S(2)}, u32[]{:S(2)}) collective-permute-start(f32[1,64,256]{2,1,0:T(8,128)S(1)} %slice_bitcast_fusion.2), channel_id=1, source_target_pairs={{0,2},{1,3},{2,0},{3,1},{4,6},{5,7},{6,4},{7,5},{8,10},{9,11},{10,... | collective-permute-start | bytes 196616 | tf_op jit(solution)/shard_map/ppermute | solution.py:123
  87.7 2.4 %collective-permute-done.25 = f32[1,64,256]{2,1,0:T(8,128)S(1)} collective-permute-done((f32[1,64,256]{2,1,0:T(8,128)S(1)}, f32[1,64,256]{2,1,0:T(8,128)S(1)}, u32[]{:S(2)}, u32[]{:S(2)}) %collective-permute-start.25) | collective-permute-done | bytes 65568 | tf_op jit(solution)/shard_map/ppermute | solution.py:123
  (47 shorter events, 19.6 us)
Async XLA Ops:
  0.0 8.0 %copy-start = (bf16[64,16384]{1,0:T(8,128)(2,1)S(1)}, bf16[64,16384]{1,0:T(8,128)(2,1)}, u32[]{:S(2)}) copy-start(bf16[64,16384]{1,0:T(8,128)(2,1)} %test.1) | copy-start | bytes 6291460
  1.2 12.2 %collective-permute-start.3 = (bf16[32,4096]{1,0:T(8,128)(2,1)S(1)}, bf16[32,4096]{1,0:T(8,128)(2,1)S(1)}, u32[]{:S(2)}, u32[]{:S(2)}) collective-permute-start(bf16[32,4096]{1,0:T(8,128)(2,1)S(1)} %slice_select_fusion.3), channel_id=1, source_target_pairs={{0,4},{4,8},{8,12},{12,0},{1,5},{5,9},{9,13},{13,1},{2,6},{6,10},{... | collective-permute-start | bytes 786440 | tf_op jit(solution)/shard_map/ppermute | solution.py:105
  5.4 13.7 %collective-permute-start = (bf16[32,4096]{1,0:T(8,128)(2,1)S(1)}, bf16[32,4096]{1,0:T(8,128)(2,1)S(1)}, u32[]{:S(2)}, u32[]{:S(2)}) collective-permute-start(bf16[32,4096]{1,0:T(8,128)(2,1)S(1)} %slice_select_fusion.2), channel_id=1, source_target_pairs={{0,4},{4,8},{8,12},{12,0},{1,5},{5,9},{9,13},{13,1},{2,6},{6,10},{... | collective-permute-start | bytes 786440 | tf_op jit(solution)/shard_map/ppermute | solution.py:105
  8.1 4.0 %copy-start.1 = (f32[16384]{0:T(1024)S(1)}, f32[16384]{0:T(1024)}, u32[]{:S(2)}) copy-start(f32[16384]{0:T(1024)} %param.5) | copy-start | bytes 196612
  13.4 11.2 %collective-permute-start.7 = (bf16[32,4096]{1,0:T(8,128)(2,1)S(1)}, bf16[32,4096]{1,0:T(8,128)(2,1)S(1)}, u32[]{:S(2)}, u32[]{:S(2)}) collective-permute-start(bf16[32,4096]{1,0:T(8,128)(2,1)S(1)} %slice_select_fusion.1), channel_id=1, source_target_pairs={{0,4},{4,8},{8,12},{12,0},{1,5},{5,9},{9,13},{13,1},{2,6},{6,10},{... | collective-permute-start | bytes 786440 | tf_op jit(solution)/shard_map/ppermute | solution.py:105
  13.8 10.9 %collective-permute-start.4 = (bf16[32,4096]{1,0:T(8,128)(2,1)S(1)}, bf16[32,4096]{1,0:T(8,128)(2,1)S(1)}, u32[]{:S(2)}, u32[]{:S(2)}) collective-permute-start(bf16[32,4096]{1,0:T(8,128)(2,1)S(1)} %collective-permute-done.3.refs_0_), channel_id=1, source_target_pairs={{0,16},{16,0},{1,17},{17,1},{2,18},{18,2},{3,19},{19,3},{4,20},{20... | collective-permute-start | bytes 786440 | tf_op jit(solution)/shard_map/ppermute | solution.py:114
  19.1 8.3 %collective-permute-start.2 = (bf16[32,4096]{1,0:T(8,128)(2,1)S(1)}, bf16[32,4096]{1,0:T(8,128)(2,1)S(1)}, u32[]{:S(2)}, u32[]{:S(2)}) collective-permute-start(bf16[32,4096]{1,0:T(8,128)(2,1)S(1)} %collective-permute-done.refs_0_), channel_id=1, source_target_pairs={{0,16},{16,0},{1,17},{17,1},{2,18},{18,2},{3,19},{19,3},{4,20},{20... | collective-permute-start | bytes 786440 | tf_op jit(solution)/shard_map/ppermute | solution.py:114
  20.8 8.7 %collective-permute-start.1 = (bf16[32,4096]{1,0:T(8,128)(2,1)S(1)}, bf16[32,4096]{1,0:T(8,128)(2,1)S(1)}, u32[]{:S(2)}, u32[]{:S(2)}) collective-permute-start(bf16[32,4096]{1,0:T(8,128)(2,1)S(1)} %slice_select_fusion), channel_id=1, source_target_pairs={{0,4},{4,8},{8,12},{12,0},{1,5},{5,9},{9,13},{13,1},{2,6},{6,10},{... | collective-permute-start | bytes 786440 | tf_op jit(solution)/shard_map/ppermute | solution.py:105
  24.7 8.8 %collective-permute-start.8 = (bf16[32,4096]{1,0:T(8,128)(2,1)S(1)}, bf16[32,4096]{1,0:T(8,128)(2,1)S(1)}, u32[]{:S(2)}, u32[]{:S(2)}) collective-permute-start(bf16[32,4096]{1,0:T(8,128)(2,1)S(1)} %collective-permute-done.7.refs_0_), channel_id=1, source_target_pairs={{0,16},{16,0},{1,17},{17,1},{2,18},{18,2},{3,19},{19,3},{4,20},{20... | collective-permute-start | bytes 786440 | tf_op jit(solution)/shard_map/ppermute | solution.py:114
  27.2 8.7 %collective-permute-start.11 = (bf16[32,4096]{1,0:T(8,128)(2,1)S(1)}, bf16[32,4096]{1,0:T(8,128)(2,1)S(1)}, u32[]{:S(2)}, u32[]{:S(2)}) collective-permute-start(bf16[32,4096]{1,0:T(8,128)(2,1)S(1)} %collective-permute-done.3.refs_0_), channel_id=1, source_target_pairs={{0,4},{4,8},{8,12},{12,0},{1,5},{5,9},{9,13},{13,1},{2,6},{6,10},{... | collective-permute-start | bytes 786440 | tf_op jit(solution)/shard_map/ppermute | solution.py:105
  29.5 9.6 %collective-permute-start.6 = (bf16[32,4096]{1,0:T(8,128)(2,1)S(1)}, bf16[32,4096]{1,0:T(8,128)(2,1)S(1)}, u32[]{:S(2)}, u32[]{:S(2)}) collective-permute-start(bf16[32,4096]{1,0:T(8,128)(2,1)S(1)} %collective-permute-done.1.refs_0_), channel_id=1, source_target_pairs={{0,16},{16,0},{1,17},{17,1},{2,18},{18,2},{3,19},{19,3},{4,20},{20... | collective-permute-start | bytes 786440 | tf_op jit(solution)/shard_map/ppermute | solution.py:114
  32.6 9.8 %collective-permute-start.5 = (bf16[32,4096]{1,0:T(8,128)(2,1)S(1)}, bf16[32,4096]{1,0:T(8,128)(2,1)S(1)}, u32[]{:S(2)}, u32[]{:S(2)}) collective-permute-start(bf16[32,4096]{1,0:T(8,128)(2,1)S(1)} %collective-permute-done.refs_0_), channel_id=1, source_target_pairs={{0,4},{4,8},{8,12},{12,0},{1,5},{5,9},{9,13},{13,1},{2,6},{6,10},{... | collective-permute-start | bytes 786440 | tf_op jit(solution)/shard_map/ppermute | solution.py:105
  35.9 9.1 %collective-permute-start.12 = (bf16[32,4096]{1,0:T(8,128)(2,1)S(1)}, bf16[32,4096]{1,0:T(8,128)(2,1)S(1)}, u32[]{:S(2)}, u32[]{:S(2)}) collective-permute-start(bf16[32,4096]{1,0:T(8,128)(2,1)S(1)} %collective-permute-done.11.refs_0_), channel_id=1, source_target_pairs={{0,16},{16,0},{1,17},{17,1},{2,18},{18,2},{3,19},{19,3},{4,20},{20... | collective-permute-start | bytes 786440 | tf_op jit(solution)/shard_map/ppermute | solution.py:114
  38.7 10.2 %collective-permute-start.15 = (bf16[32,4096]{1,0:T(8,128)(2,1)S(1)}, bf16[32,4096]{1,0:T(8,128)(2,1)S(1)}, u32[]{:S(2)}, u32[]{:S(2)}) collective-permute-start(bf16[32,4096]{1,0:T(8,128)(2,1)S(1)} %collective-permute-done.7.refs_0_), channel_id=1, source_target_pairs={{0,4},{4,8},{8,12},{12,0},{1,5},{5,9},{9,13},{13,1},{2,6},{6,10},{... | collective-permute-start | bytes 786440 | tf_op jit(solution)/shard_map/ppermute | solution.py:105
  42.4 8.9 %collective-permute-start.10 = (bf16[32,4096]{1,0:T(8,128)(2,1)S(1)}, bf16[32,4096]{1,0:T(8,128)(2,1)S(1)}, u32[]{:S(2)}, u32[]{:S(2)}) collective-permute-start(bf16[32,4096]{1,0:T(8,128)(2,1)S(1)} %collective-permute-done.5.refs_0_), channel_id=1, source_target_pairs={{0,16},{16,0},{1,17},{17,1},{2,18},{18,2},{3,19},{19,3},{4,20},{20... | collective-permute-start | bytes 786440 | tf_op jit(solution)/shard_map/ppermute | solution.py:114
  43.7 11.0 %collective-permute-start.9 = (bf16[32,4096]{1,0:T(8,128)(2,1)S(1)}, bf16[32,4096]{1,0:T(8,128)(2,1)S(1)}, u32[]{:S(2)}, u32[]{:S(2)}) collective-permute-start(bf16[32,4096]{1,0:T(8,128)(2,1)S(1)} %collective-permute-done.1.refs_0_), channel_id=1, source_target_pairs={{0,4},{4,8},{8,12},{12,0},{1,5},{5,9},{9,13},{13,1},{2,6},{6,10},{... | collective-permute-start | bytes 786440 | tf_op jit(solution)/shard_map/ppermute | solution.py:105
  49.0 8.6 %collective-permute-start.16 = (bf16[32,4096]{1,0:T(8,128)(2,1)S(1)}, bf16[32,4096]{1,0:T(8,128)(2,1)S(1)}, u32[]{:S(2)}, u32[]{:S(2)}) collective-permute-start(bf16[32,4096]{1,0:T(8,128)(2,1)S(1)} %collective-permute-done.15.refs_0_), channel_id=1, source_target_pairs={{0,16},{16,0},{1,17},{17,1},{2,18},{18,2},{3,19},{19,3},{4,20},{20... | collective-permute-start | bytes 786440 | tf_op jit(solution)/shard_map/ppermute | solution.py:114
  49.8 10.0 %collective-permute-start.18 = (bf16[32,4096]{1,0:T(8,128)(2,1)S(1)}, bf16[32,4096]{1,0:T(8,128)(2,1)S(1)}, u32[]{:S(2)}, u32[]{:S(2)}) collective-permute-start(bf16[32,4096]{1,0:T(8,128)(2,1)S(1)} %collective-permute-done.11.refs_0_), channel_id=1, source_target_pairs={{0,4},{4,8},{8,12},{12,0},{1,5},{5,9},{9,13},{13,1},{2,6},{6,10},{... | collective-permute-start | bytes 786440 | tf_op jit(solution)/shard_map/ppermute | solution.py:105
  54.7 9.2 %collective-permute-start.14 = (bf16[32,4096]{1,0:T(8,128)(2,1)S(1)}, bf16[32,4096]{1,0:T(8,128)(2,1)S(1)}, u32[]{:S(2)}, u32[]{:S(2)}) collective-permute-start(bf16[32,4096]{1,0:T(8,128)(2,1)S(1)} %collective-permute-done.9.refs_0_), channel_id=1, source_target_pairs={{0,16},{16,0},{1,17},{17,1},{2,18},{18,2},{3,19},{19,3},{4,20},{20... | collective-permute-start | bytes 786440 | tf_op jit(solution)/shard_map/ppermute | solution.py:114
  56.2 11.0 %collective-permute-start.13 = (bf16[32,4096]{1,0:T(8,128)(2,1)S(1)}, bf16[32,4096]{1,0:T(8,128)(2,1)S(1)}, u32[]{:S(2)}, u32[]{:S(2)}) collective-permute-start(bf16[32,4096]{1,0:T(8,128)(2,1)S(1)} %collective-permute-done.5.refs_0_), channel_id=1, source_target_pairs={{0,4},{4,8},{8,12},{12,0},{1,5},{5,9},{9,13},{13,1},{2,6},{6,10},{... | collective-permute-start | bytes 786440 | tf_op jit(solution)/shard_map/ppermute | solution.py:105
  59.9 14.0 %collective-permute-start.19 = (bf16[32,4096]{1,0:T(8,128)(2,1)S(1)}, bf16[32,4096]{1,0:T(8,128)(2,1)S(1)}, u32[]{:S(2)}, u32[]{:S(2)}) collective-permute-start(bf16[32,4096]{1,0:T(8,128)(2,1)S(1)} %collective-permute-done.18.refs_0_), channel_id=1, source_target_pairs={{0,16},{16,0},{1,17},{17,1},{2,18},{18,2},{3,19},{19,3},{4,20},{20... | collective-permute-start | bytes 786440 | tf_op jit(solution)/shard_map/ppermute | solution.py:114
  61.5 10.9 %collective-permute-start.21 = (bf16[32,4096]{1,0:T(8,128)(2,1)S(1)}, bf16[32,4096]{1,0:T(8,128)(2,1)S(1)}, u32[]{:S(2)}, u32[]{:S(2)}) collective-permute-start(bf16[32,4096]{1,0:T(8,128)(2,1)S(1)} %collective-permute-done.15.refs_0_), channel_id=1, source_target_pairs={{0,4},{4,8},{8,12},{12,0},{1,5},{5,9},{9,13},{13,1},{2,6},{6,10},{... | collective-permute-start | bytes 786440 | tf_op jit(solution)/shard_map/ppermute | solution.py:105
  67.2 8.2 %collective-permute-start.17 = (bf16[32,4096]{1,0:T(8,128)(2,1)S(1)}, bf16[32,4096]{1,0:T(8,128)(2,1)S(1)}, u32[]{:S(2)}, u32[]{:S(2)}) collective-permute-start(bf16[32,4096]{1,0:T(8,128)(2,1)S(1)} %collective-permute-done.9.refs_0_), channel_id=1, source_target_pairs={{0,4},{4,8},{8,12},{12,0},{1,5},{5,9},{9,13},{13,1},{2,6},{6,10},{... | collective-permute-start | bytes 786440 | tf_op jit(solution)/shard_map/ppermute | solution.py:105
  67.2 9.4 %collective-permute-start.23 = (bf16[32,4096]{1,0:T(8,128)(2,1)S(1)}, bf16[32,4096]{1,0:T(8,128)(2,1)S(1)}, u32[]{:S(2)}, u32[]{:S(2)}) collective-permute-start(bf16[32,4096]{1,0:T(8,128)(2,1)S(1)} %collective-permute-done.13.refs_0_), channel_id=1, source_target_pairs={{0,16},{16,0},{1,17},{17,1},{2,18},{18,2},{3,19},{19,3},{4,20},{20... | collective-permute-start | bytes 786440 | tf_op jit(solution)/shard_map/ppermute | solution.py:114
  72.4 8.3 %collective-permute-start.22 = (bf16[32,4096]{1,0:T(8,128)(2,1)S(1)}, bf16[32,4096]{1,0:T(8,128)(2,1)S(1)}, u32[]{:S(2)}, u32[]{:S(2)}) collective-permute-start(bf16[32,4096]{1,0:T(8,128)(2,1)S(1)} %collective-permute-done.21.refs_0_), channel_id=1, source_target_pairs={{0,16},{16,0},{1,17},{17,1},{2,18},{18,2},{3,19},{19,3},{4,20},{20... | collective-permute-start | bytes 786440 | tf_op jit(solution)/shard_map/ppermute | solution.py:114
  75.4 8.1 %collective-permute-start.20 = (bf16[32,4096]{1,0:T(8,128)(2,1)S(1)}, bf16[32,4096]{1,0:T(8,128)(2,1)S(1)}, u32[]{:S(2)}, u32[]{:S(2)}) collective-permute-start(bf16[32,4096]{1,0:T(8,128)(2,1)S(1)} %collective-permute-done.17.refs_0_), channel_id=1, source_target_pairs={{0,16},{16,0},{1,17},{17,1},{2,18},{18,2},{3,19},{19,3},{4,20},{20... | collective-permute-start | bytes 786440 | tf_op jit(solution)/shard_map/ppermute | solution.py:114
  84.3 1.4 %collective-permute-start.24 = (f32[2,64,256]{2,1,0:T(8,128)S(1)}, f32[2,64,256]{2,1,0:T(8,128)S(1)}, u32[]{:S(2)}, u32[]{:S(2)}) collective-permute-start(f32[2,64,256]{2,1,0:T(8,128)S(1)} %slice_bitcast_fusion), channel_id=1, source_target_pairs={{0,1},{1,0},{2,3},{3,2},{4,5},{5,4},{6,7},{7,6},{8,9},{9,8},{10,11... | collective-permute-start | bytes 393224 | tf_op jit(solution)/shard_map/ppermute | solution.py:123
  85.8 4.3 %collective-permute-start.25 = (f32[1,64,256]{2,1,0:T(8,128)S(1)}, f32[1,64,256]{2,1,0:T(8,128)S(1)}, u32[]{:S(2)}, u32[]{:S(2)}) collective-permute-start(f32[1,64,256]{2,1,0:T(8,128)S(1)} %slice_bitcast_fusion.2), channel_id=1, source_target_pairs={{0,2},{1,3},{2,0},{3,1},{4,6},{5,7},{6,4},{7,5},{8,10},{9,11},{10,... | collective-permute-start | bytes 196616 | tf_op jit(solution)/shard_map/ppermute | solution.py:123

commit v21 on v20

--- a/solution.py
+++ b/solution.py
@@ -9,7 +9,8 @@
 
 CONTRACT = (((1,), (1,)), ((), ()))
 LANES = 128
-CHUNKS = 4
+SHARES = (34, 34, 34, 26)
+CHUNKS = len(SHARES)
 
 
 def product(rows, scale, train, unit):
@@ -91,7 +92,7 @@
         half = queries // n_grp
         unit = 8 * LANES
         lanes = feats // LANES
-        cuts = [c * lanes // CHUNKS * LANES for c in range(CHUNKS + 1)]
+        cuts = [sum(SHARES[:c]) * lanes // sum(SHARES) * LANES for c in range(CHUNKS + 1)]
         starts, columns = cuts[:-1], [slice(*ends) for ends in zip(cuts[:-1], cuts[1:])]
         first_grp = lax.axis_index("grp") == 0
         ring = [(i, (i + 1) % n_ex) for i in range(n_ex)]

time: 90.9 us -> 93.5 us (1.029)
  waiting for transfers between devices: 46.2 us -> 51.4 us
  starting transfers between devices: 24.5 us -> 20.9 us
  local copies, waits for them, and re-layouts: 4 us -> 5.15 us
    ppermute x12, waiting for transfers between devices: 29.5 us -> 35.8 us  [hop(): hops.append(lax.ppermute(after(block, *waits), 'ex', ring))]
    ppermute x12, starting transfers between devices: 17.2 us -> 13 us  [swap(): swaps.append(lax.ppermute(after(block, *waits), 'grp', [(0, 1), (1, 0)]))]
    ppermute x12, waiting for transfers between devices: 13 us -> 11.5 us  [swap(): swaps.append(lax.ppermute(after(block, *waits), 'grp', [(0, 1), (1, 0)]))]
    slice x1 -> x2, local copies, waits for them, and re-layouts: 3.97 us -> 5.12 us  [on_device(): trains = [train[:, here] for here in columns]]
  transfers between devices with their start and end apart: 26 -> 26, of which waited for: 23 -> 20; matrix products, arithmetic and copies ran while one was open for 7% -> 8% of each run, Pallas kernels for 12% -> 12%
where the time goes in v21:
time: 93.5 us; the launch traced here: 93.3 us
  waiting for transfers between devices  51.4 us (55%)
  starting transfers between devices  20.9 us (22%)
  Pallas kernels  11.8 us (13%)
  local copies, waits for them, and re-layouts  5.15 us (6%)
  other arithmetic  3.91 us (4%)
    ppermute x12, waiting for transfers between devices, hop(): hops.append(lax.ppermute(after(block, *waits), 'ex', ring))  35.8 us
    ppermute x12, starting transfers between devices, swap(): swaps.append(lax.ppermute(after(block, *waits), 'grp', [(0, 1), (1, 0)]))  13 us
    pallas_call x13, Pallas kernels, call(): pl.pallas_call(kernel, out_shape=jax.ShapeDtypeStruct((rows, docs), jnp.f...  11.8 us
    ppermute x12, waiting for transfers between devices, swap(): swaps.append(lax.ppermute(after(block, *waits), 'grp', [(0, 1), (1, 0)]))  11.5 us
    ppermute x12, starting transfers between devices, hop(): hops.append(lax.ppermute(after(block, *waits), 'ex', ring))  6.23 us
    slice x2, local copies, waits for them, and re-layouts, on_device(): trains = [train[:, here] for here in columns]  5.12 us
    ppermute x2, waiting for transfers between devices, sum_over_feat(): held = pairs[:, 0] + lax.ppermute(pairs[:, 1], 'feat', partner)  4.11 us
    select_n x4, other arithmetic, share(): return jnp.where(first_grp, rows[:half, columns], rows[half:, columns])  3.24 us
  transfers between devices with their start and end apart: 26, of which 20 were waited for; matrix products, arithmetic and copies ran while one was open for 8% of the time, Pallas kernels for 12%

profile of v21, /device:TPU:0, one launch (start us, length us, event | category | flops | bytes accessed | tf_op | source)
XLA Modules:
  0.0 93.3 jit_solution(11177234930961133962)
XLA Ops:
  1.1 3.1 %collective-permute-start.3 = (bf16[32,4352]{1,0:T(8,128)(2,1)S(1)}, bf16[32,4352]{1,0:T(8,128)(2,1)S(1)}, u32[]{:S(2)}, u32[]{:S(2)}) collective-permute-start(bf16[32,4352]{1,0:T(8,128)(2,1)S(1)} %slice_select_fusion.2), channel_id=1, source_target_pairs={{0,4},{4,8},{8,12},{12,0},{1,5},{5,9},{9,13},{13,1},{2,6},{6,10},{... | collective-permute-start | bytes 835592 | tf_op jit(solution)/shard_map/ppermute | solution.py:106
  5.2 1.6 %collective-permute-start = (bf16[32,4352]{1,0:T(8,128)(2,1)S(1)}, bf16[32,4352]{1,0:T(8,128)(2,1)S(1)}, u32[]{:S(2)}, u32[]{:S(2)}) collective-permute-start(bf16[32,4352]{1,0:T(8,128)(2,1)S(1)} %slice_select_fusion.1), channel_id=1, source_target_pairs={{0,4},{4,8},{8,12},{12,0},{1,5},{5,9},{9,13},{13,1},{2,6},{6,10},{... | collective-permute-start | bytes 835592 | tf_op jit(solution)/shard_map/ppermute | solution.py:106
  8.0 3.6 %fusion.4 = (bf16[256,4352]{1,0:T(8,128)(2,1)S(1)}, bf16[256,4352]{1,0:T(8,128)(2,1)S(1)}, bf16[256,4352]{1,0:T(8,128)(2,1)S(1)}) fusion(bf16[256,16384]{1,0:T(8,128)(2,1)} %param.3), kind=kLoop, calls=%fused_computation.13 | loop fusion | bytes 13369344 | tf_op jit(solution)/shard_map/slice | solution.py:137
  11.6 2.1 %collective-permute-done.3.refs_0_ = bf16[32,4352]{1,0:T(8,128)(2,1)S(1)} collective-permute-done((bf16[32,4352]{1,0:T(8,128)(2,1)S(1)}, bf16[32,4352]{1,0:T(8,128)(2,1)S(1)}, u32[]{:S(2)}, u32[]{:S(2)}) %collective-permute-start.3) | collective-permute-done | bytes 278560 | tf_op jit(solution)/shard_map/ppermute | solution.py:106
  13.7 1.7 %collective-permute-start.4 = (bf16[32,4352]{1,0:T(8,128)(2,1)S(1)}, bf16[32,4352]{1,0:T(8,128)(2,1)S(1)}, u32[]{:S(2)}, u32[]{:S(2)}) collective-permute-start(bf16[32,4352]{1,0:T(8,128)(2,1)S(1)} %collective-permute-done.3.refs_0_), channel_id=1, source_target_pairs={{0,16},{16,0},{1,17},{17,1},{2,18},{18,2},{3,19},{19,3},{4,20},{20... | collective-permute-start | bytes 835592 | tf_op jit(solution)/shard_map/ppermute | solution.py:115
  15.4 4.2 %collective-permute-done.refs_0_ = bf16[32,4352]{1,0:T(8,128)(2,1)S(1)} collective-permute-done((bf16[32,4352]{1,0:T(8,128)(2,1)S(1)}, bf16[32,4352]{1,0:T(8,128)(2,1)S(1)}, u32[]{:S(2)}, u32[]{:S(2)}) %collective-permute-start) | collective-permute-done | bytes 278560 | tf_op jit(solution)/shard_map/ppermute | solution.py:106
  19.6 1.8 %collective-permute-start.2 = (bf16[32,4352]{1,0:T(8,128)(2,1)S(1)}, bf16[32,4352]{1,0:T(8,128)(2,1)S(1)}, u32[]{:S(2)}, u32[]{:S(2)}) collective-permute-start(bf16[32,4352]{1,0:T(8,128)(2,1)S(1)} %collective-permute-done.refs_0_), channel_id=1, source_target_pairs={{0,16},{16,0},{1,17},{17,1},{2,18},{18,2},{3,19},{19,3},{4,20},{20... | collective-permute-start | bytes 835592 | tf_op jit(solution)/shard_map/ppermute | solution.py:115
  21.4 1.6 %slice.59.refs_3_ = bf16[256,3328]{1,0:T(8,128)(2,1)S(1)} slice(bf16[256,16384]{1,0:T(8,128)(2,1)} %param.3), slice={[0:256], [13056:16384]} | slice | bytes 3407872 | tf_op jit(solution)/shard_map/slice | solution.py:137
  23.0 2.6 %shard_map.37.refs_4_ = f32[64,256]{1,0:T(8,128)S(1)} custom-call(bf16[64,16384]{1,0:T(8,128)(2,1)S(1)} %copy-done, f32[1,16384]{1,0:T(1,128)S(1)} %bitcast.28, bf16[256,4352]{1,0:T(8,128)(2,1)S(1)} %get-tuple-element.53.refs_0_.refs_3_, bf16[256,4352]{1,0:T(8,128)(2,1)S(1)} %get-tuple-element.52.refs_1_.refs_3_, ...), custom_call_target="tpu_custom_call" | custom-call | flops 536870912 | bytes 10485760 | tf_op jit(solution)/shard_map/pallas_call | solution.py:72
  27.1 1.3 %collective-permute-start.11 = (bf16[32,4352]{1,0:T(8,128)(2,1)S(1)}, bf16[32,4352]{1,0:T(8,128)(2,1)S(1)}, u32[]{:S(2)}, u32[]{:S(2)}) collective-permute-start(bf16[32,4352]{1,0:T(8,128)(2,1)S(1)} %collective-permute-done.3.refs_0_), channel_id=1, source_target_pairs={{0,4},{4,8},{8,12},{12,0},{1,5},{5,9},{9,13},{13,1},{2,6},{6,10},{... | collective-permute-start | bytes 835592 | tf_op jit(solution)/shard_map/ppermute | solution.py:106
  29.2 6.4 %collective-permute-done.1.refs_0_ = bf16[32,3328]{1,0:T(8,128)(2,1)S(1)} collective-permute-done((bf16[32,3328]{1,0:T(8,128)(2,1)S(1)}, bf16[32,3328]{1,0:T(8,128)(2,1)S(1)}, u32[]{:S(2)}, u32[]{:S(2)}) %collective-permute-start.1) | collective-permute-done | bytes 213024 | tf_op jit(solution)/shard_map/ppermute | solution.py:106
  36.7 4.8 %collective-permute-done.11.refs_0_ = bf16[32,4352]{1,0:T(8,128)(2,1)S(1)} collective-permute-done((bf16[32,4352]{1,0:T(8,128)(2,1)S(1)}, bf16[32,4352]{1,0:T(8,128)(2,1)S(1)}, u32[]{:S(2)}, u32[]{:S(2)}) %collective-permute-start.11) | collective-permute-done | bytes 278560 | tf_op jit(solution)/shard_map/ppermute | solution.py:106
  41.8 1.7 %collective-permute-done.6.refs_1_ = bf16[32,3328]{1,0:T(8,128)(2,1)S(1)} collective-permute-done((bf16[32,3328]{1,0:T(8,128)(2,1)S(1)}, bf16[32,3328]{1,0:T(8,128)(2,1)S(1)}, u32[]{:S(2)}, u32[]{:S(2)}) %collective-permute-start.6) | collective-permute-done | bytes 213024 | tf_op jit(solution)/shard_map/ppermute | solution.py:115
  43.5 4.0 %collective-permute-done.5.refs_0_ = bf16[32,4352]{1,0:T(8,128)(2,1)S(1)} collective-permute-done((bf16[32,4352]{1,0:T(8,128)(2,1)S(1)}, bf16[32,4352]{1,0:T(8,128)(2,1)S(1)}, u32[]{:S(2)}, u32[]{:S(2)}) %collective-permute-start.5) | collective-permute-done | bytes 278560 | tf_op jit(solution)/shard_map/ppermute | solution.py:106
  48.5 1.7 %collective-permute-done.12.refs_1_ = bf16[32,4352]{1,0:T(8,128)(2,1)S(1)} collective-permute-done((bf16[32,4352]{1,0:T(8,128)(2,1)S(1)}, bf16[32,4352]{1,0:T(8,128)(2,1)S(1)}, u32[]{:S(2)}, u32[]{:S(2)}) %collective-permute-start.12) | collective-permute-done | bytes 278560 | tf_op jit(solution)/shard_map/ppermute | solution.py:115
  50.2 2.6 %collective-permute-done.15.refs_0_ = bf16[32,4352]{1,0:T(8,128)(2,1)S(1)} collective-permute-done((bf16[32,4352]{1,0:T(8,128)(2,1)S(1)}, bf16[32,4352]{1,0:T(8,128)(2,1)S(1)}, u32[]{:S(2)}, u32[]{:S(2)}) %collective-permute-start.15) | collective-permute-done | bytes 278560 | tf_op jit(solution)/shard_map/ppermute | solution.py:106
  54.6 2.4 %collective-permute-done.10.refs_1_ = bf16[32,4352]{1,0:T(8,128)(2,1)S(1)} collective-permute-done((bf16[32,4352]{1,0:T(8,128)(2,1)S(1)}, bf16[32,4352]{1,0:T(8,128)(2,1)S(1)}, u32[]{:S(2)}, u32[]{:S(2)}) %collective-permute-start.10) | collective-permute-done | bytes 278560 | tf_op jit(solution)/shard_map/ppermute | solution.py:115
  58.4 1.7 %collective-permute-start.14 = (bf16[32,3328]{1,0:T(8,128)(2,1)S(1)}, bf16[32,3328]{1,0:T(8,128)(2,1)S(1)}, u32[]{:S(2)}, u32[]{:S(2)}) collective-permute-start(bf16[32,3328]{1,0:T(8,128)(2,1)S(1)} %collective-permute-done.9.refs_0_), channel_id=1, source_target_pairs={{0,16},{16,0},{1,17},{17,1},{2,18},{18,2},{3,19},{19,3},{4,20},{20... | collective-permute-start | bytes 638984 | tf_op jit(solution)/shard_map/ppermute | solution.py:115
  60.1 1.8 %collective-permute-done.16.refs_1_ = bf16[32,4352]{1,0:T(8,128)(2,1)S(1)} collective-permute-done((bf16[32,4352]{1,0:T(8,128)(2,1)S(1)}, bf16[32,4352]{1,0:T(8,128)(2,1)S(1)}, u32[]{:S(2)}, u32[]{:S(2)}) %collective-permute-start.16) | collective-permute-done | bytes 278560 | tf_op jit(solution)/shard_map/ppermute | solution.py:115
  62.7 3.1 %collective-permute-done.18.refs_0_ = bf16[32,4352]{1,0:T(8,128)(2,1)S(1)} collective-permute-done((bf16[32,4352]{1,0:T(8,128)(2,1)S(1)}, bf16[32,4352]{1,0:T(8,128)(2,1)S(1)}, u32[]{:S(2)}, u32[]{:S(2)}) %collective-permute-start.18) | collective-permute-done | bytes 278560 | tf_op jit(solution)/shard_map/ppermute | solution.py:106
  65.8 1.3 %collective-permute-start.19 = (bf16[32,4352]{1,0:T(8,128)(2,1)S(1)}, bf16[32,4352]{1,0:T(8,128)(2,1)S(1)}, u32[]{:S(2)}, u32[]{:S(2)}) collective-permute-start(bf16[32,4352]{1,0:T(8,128)(2,1)S(1)} %collective-permute-done.18.refs_0_), channel_id=1, source_target_pairs={{0,16},{16,0},{1,17},{17,1},{2,18},{18,2},{3,19},{19,3},{4,20},{20... | collective-permute-start | bytes 835592 | tf_op jit(solution)/shard_map/ppermute | solution.py:115
  67.7 4.1 %collective-permute-done.13.refs_0_ = bf16[32,4352]{1,0:T(8,128)(2,1)S(1)} collective-permute-done((bf16[32,4352]{1,0:T(8,128)(2,1)S(1)}, bf16[32,4352]{1,0:T(8,128)(2,1)S(1)}, u32[]{:S(2)}, u32[]{:S(2)}) %collective-permute-start.13) | collective-permute-done | bytes 278560 | tf_op jit(solution)/shard_map/ppermute | solution.py:106
  71.7 1.3 %collective-permute-start.23 = (bf16[32,4352]{1,0:T(8,128)(2,1)S(1)}, bf16[32,4352]{1,0:T(8,128)(2,1)S(1)}, u32[]{:S(2)}, u32[]{:S(2)}) collective-permute-start(bf16[32,4352]{1,0:T(8,128)(2,1)S(1)} %collective-permute-done.13.refs_0_), channel_id=1, source_target_pairs={{0,16},{16,0},{1,17},{17,1},{2,18},{18,2},{3,19},{19,3},{4,20},{20... | collective-permute-start | bytes 835592 | tf_op jit(solution)/shard_map/ppermute | solution.py:115
  73.0 2.5 %collective-permute-done.21.refs_0_ = bf16[32,4352]{1,0:T(8,128)(2,1)S(1)} collective-permute-done((bf16[32,4352]{1,0:T(8,128)(2,1)S(1)}, bf16[32,4352]{1,0:T(8,128)(2,1)S(1)}, u32[]{:S(2)}, u32[]{:S(2)}) %collective-permute-start.21) | collective-permute-done | bytes 278560 | tf_op jit(solution)/shard_map/ppermute | solution.py:106
  75.5 1.6 %collective-permute-start.22 = (bf16[32,4352]{1,0:T(8,128)(2,1)S(1)}, bf16[32,4352]{1,0:T(8,128)(2,1)S(1)}, u32[]{:S(2)}, u32[]{:S(2)}) collective-permute-start(bf16[32,4352]{1,0:T(8,128)(2,1)S(1)} %collective-permute-done.21.refs_0_), channel_id=1, source_target_pairs={{0,16},{16,0},{1,17},{17,1},{2,18},{18,2},{3,19},{19,3},{4,20},{20... | collective-permute-start | bytes 835592 | tf_op jit(solution)/shard_map/ppermute | solution.py:115
  77.8 1.5 %collective-permute-done.17.refs_0_ = bf16[32,3328]{1,0:T(8,128)(2,1)S(1)} collective-permute-done((bf16[32,3328]{1,0:T(8,128)(2,1)S(1)}, bf16[32,3328]{1,0:T(8,128)(2,1)S(1)}, u32[]{:S(2)}, u32[]{:S(2)}) %collective-permute-start.17) | collective-permute-done | bytes 213024 | tf_op jit(solution)/shard_map/ppermute | solution.py:106
  79.4 1.3 %collective-permute-start.20 = (bf16[32,3328]{1,0:T(8,128)(2,1)S(1)}, bf16[32,3328]{1,0:T(8,128)(2,1)S(1)}, u32[]{:S(2)}, u32[]{:S(2)}) collective-permute-start(bf16[32,3328]{1,0:T(8,128)(2,1)S(1)} %collective-permute-done.17.refs_0_), channel_id=1, source_target_pairs={{0,16},{16,0},{1,17},{17,1},{2,18},{18,2},{3,19},{19,3},{4,20},{20... | collective-permute-start | bytes 638984 | tf_op jit(solution)/shard_map/ppermute | solution.py:115
  81.7 2.2 %collective-permute-done.22.refs_1_ = bf16[32,4352]{1,0:T(8,128)(2,1)S(1)} collective-permute-done((bf16[32,4352]{1,0:T(8,128)(2,1)S(1)}, bf16[32,4352]{1,0:T(8,128)(2,1)S(1)}, u32[]{:S(2)}, u32[]{:S(2)}) %collective-permute-start.22) | collective-permute-done | bytes 278560 | tf_op jit(solution)/shard_map/ppermute | solution.py:115
  84.7 1.5 %collective-permute-done.20.refs_1_ = bf16[32,3328]{1,0:T(8,128)(2,1)S(1)} collective-permute-done((bf16[32,3328]{1,0:T(8,128)(2,1)S(1)}, bf16[32,3328]{1,0:T(8,128)(2,1)S(1)}, u32[]{:S(2)}, u32[]{:S(2)}) %collective-permute-start.20) | collective-permute-done | bytes 213024 | tf_op jit(solution)/shard_map/ppermute | solution.py:115
  87.0 1.3 %collective-permute-done.24 = f32[2,64,256]{2,1,0:T(8,128)S(1)} collective-permute-done((f32[2,64,256]{2,1,0:T(8,128)S(1)}, f32[2,64,256]{2,1,0:T(8,128)S(1)}, u32[]{:S(2)}, u32[]{:S(2)}) %collective-permute-start.24) | collective-permute-done | bytes 131104 | tf_op jit(solution)/shard_map/ppermute | solution.py:124
  88.3 1.6 %collective-permute-start.25 = (f32[1,64,256]{2,1,0:T(8,128)S(1)}, f32[1,64,256]{2,1,0:T(8,128)S(1)}, u32[]{:S(2)}, u32[]{:S(2)}) collective-permute-start(f32[1,64,256]{2,1,0:T(8,128)S(1)} %slice_bitcast_fusion.2), channel_id=1, source_target_pairs={{0,2},{1,3},{2,0},{3,1},{4,6},{5,7},{6,4},{7,5},{8,10},{9,11},{10,... | collective-permute-start | bytes 196616 | tf_op jit(solution)/shard_map/ppermute | solution.py:124
  89.9 2.8 %collective-permute-done.25 = f32[1,64,256]{2,1,0:T(8,128)S(1)} collective-permute-done((f32[1,64,256]{2,1,0:T(8,128)S(1)}, f32[1,64,256]{2,1,0:T(8,128)S(1)}, u32[]{:S(2)}, u32[]{:S(2)}) %collective-permute-start.25) | collective-permute-done | bytes 65568 | tf_op jit(solution)/shard_map/ppermute | solution.py:124
  (48 shorter events, 16.7 us)
Async XLA Ops:
  1.1 12.6 %collective-permute-start.3 = (bf16[32,4352]{1,0:T(8,128)(2,1)S(1)}, bf16[32,4352]{1,0:T(8,128)(2,1)S(1)}, u32[]{:S(2)}, u32[]{:S(2)}) collective-permute-start(bf16[32,4352]{1,0:T(8,128)(2,1)S(1)} %slice_select_fusion.2), channel_id=1, source_target_pairs={{0,4},{4,8},{8,12},{12,0},{1,5},{5,9},{9,13},{13,1},{2,6},{6,10},{... | collective-permute-start | bytes 835592 | tf_op jit(solution)/shard_map/ppermute | solution.py:106
  5.2 14.4 %collective-permute-start = (bf16[32,4352]{1,0:T(8,128)(2,1)S(1)}, bf16[32,4352]{1,0:T(8,128)(2,1)S(1)}, u32[]{:S(2)}, u32[]{:S(2)}) collective-permute-start(bf16[32,4352]{1,0:T(8,128)(2,1)S(1)} %slice_select_fusion.1), channel_id=1, source_target_pairs={{0,4},{4,8},{8,12},{12,0},{1,5},{5,9},{9,13},{13,1},{2,6},{6,10},{... | collective-permute-start | bytes 835592 | tf_op jit(solution)/shard_map/ppermute | solution.py:106
  7.9 3.6 %copy-start = (bf16[64,16384]{1,0:T(8,128)(2,1)S(1)}, bf16[64,16384]{1,0:T(8,128)(2,1)}, u32[]{:S(2)}) copy-start(bf16[64,16384]{1,0:T(8,128)(2,1)} %test.1) | copy-start | bytes 6291460
  7.9 13.5 %copy-start.1 = (f32[16384]{0:T(1024)S(1)}, f32[16384]{0:T(1024)}, u32[]{:S(2)}) copy-start(f32[16384]{0:T(1024)} %param.5) | copy-start | bytes 196612
  13.7 12.0 %collective-permute-start.7 = (bf16[32,4352]{1,0:T(8,128)(2,1)S(1)}, bf16[32,4352]{1,0:T(8,128)(2,1)S(1)}, u32[]{:S(2)}, u32[]{:S(2)}) collective-permute-start(bf16[32,4352]{1,0:T(8,128)(2,1)S(1)} %slice_select_fusion), channel_id=1, source_target_pairs={{0,4},{4,8},{8,12},{12,0},{1,5},{5,9},{9,13},{13,1},{2,6},{6,10},{... | collective-permute-start | bytes 835592 | tf_op jit(solution)/shard_map/ppermute | solution.py:106
  13.7 12.0 %collective-permute-start.4 = (bf16[32,4352]{1,0:T(8,128)(2,1)S(1)}, bf16[32,4352]{1,0:T(8,128)(2,1)S(1)}, u32[]{:S(2)}, u32[]{:S(2)}) collective-permute-start(bf16[32,4352]{1,0:T(8,128)(2,1)S(1)} %collective-permute-done.3.refs_0_), channel_id=1, source_target_pairs={{0,16},{16,0},{1,17},{17,1},{2,18},{18,2},{3,19},{19,3},{4,20},{20... | collective-permute-start | bytes 835592 | tf_op jit(solution)/shard_map/ppermute | solution.py:115
  19.6 8.8 %collective-permute-start.2 = (bf16[32,4352]{1,0:T(8,128)(2,1)S(1)}, bf16[32,4352]{1,0:T(8,128)(2,1)S(1)}, u32[]{:S(2)}, u32[]{:S(2)}) collective-permute-start(bf16[32,4352]{1,0:T(8,128)(2,1)S(1)} %collective-permute-done.refs_0_), channel_id=1, source_target_pairs={{0,16},{16,0},{1,17},{17,1},{2,18},{18,2},{3,19},{19,3},{4,20},{20... | collective-permute-start | bytes 835592 | tf_op jit(solution)/shard_map/ppermute | solution.py:115
  25.6 9.9 %collective-permute-start.1 = (bf16[32,3328]{1,0:T(8,128)(2,1)S(1)}, bf16[32,3328]{1,0:T(8,128)(2,1)S(1)}, u32[]{:S(2)}, u32[]{:S(2)}) collective-permute-start(bf16[32,3328]{1,0:T(8,128)(2,1)S(1)} %slice_select_fusion.3), channel_id=1, source_target_pairs={{0,4},{4,8},{8,12},{12,0},{1,5},{5,9},{9,13},{13,1},{2,6},{6,10},{... | collective-permute-start | bytes 638984 | tf_op jit(solution)/shard_map/ppermute | solution.py:106
  25.7 10.2 %collective-permute-start.8 = (bf16[32,4352]{1,0:T(8,128)(2,1)S(1)}, bf16[32,4352]{1,0:T(8,128)(2,1)S(1)}, u32[]{:S(2)}, u32[]{:S(2)}) collective-permute-start(bf16[32,4352]{1,0:T(8,128)(2,1)S(1)} %collective-permute-done.7.refs_0_), channel_id=1, source_target_pairs={{0,16},{16,0},{1,17},{17,1},{2,18},{18,2},{3,19},{19,3},{4,20},{20... | collective-permute-start | bytes 835592 | tf_op jit(solution)/shard_map/ppermute | solution.py:115
  27.1 14.4 %collective-permute-start.11 = (bf16[32,4352]{1,0:T(8,128)(2,1)S(1)}, bf16[32,4352]{1,0:T(8,128)(2,1)S(1)}, u32[]{:S(2)}, u32[]{:S(2)}) collective-permute-start(bf16[32,4352]{1,0:T(8,128)(2,1)S(1)} %collective-permute-done.3.refs_0_), channel_id=1, source_target_pairs={{0,4},{4,8},{8,12},{12,0},{1,5},{5,9},{9,13},{13,1},{2,6},{6,10},{... | collective-permute-start | bytes 835592 | tf_op jit(solution)/shard_map/ppermute | solution.py:106
  35.6 11.9 %collective-permute-start.5 = (bf16[32,4352]{1,0:T(8,128)(2,1)S(1)}, bf16[32,4352]{1,0:T(8,128)(2,1)S(1)}, u32[]{:S(2)}, u32[]{:S(2)}) collective-permute-start(bf16[32,4352]{1,0:T(8,128)(2,1)S(1)} %collective-permute-done.refs_0_), channel_id=1, source_target_pairs={{0,4},{4,8},{8,12},{12,0},{1,5},{5,9},{9,13},{13,1},{2,6},{6,10},{... | collective-permute-start | bytes 835592 | tf_op jit(solution)/shard_map/ppermute | solution.py:106
  35.6 7.9 %collective-permute-start.6 = (bf16[32,3328]{1,0:T(8,128)(2,1)S(1)}, bf16[32,3328]{1,0:T(8,128)(2,1)S(1)}, u32[]{:S(2)}, u32[]{:S(2)}) collective-permute-start(bf16[32,3328]{1,0:T(8,128)(2,1)S(1)} %collective-permute-done.1.refs_0_), channel_id=1, source_target_pairs={{0,16},{16,0},{1,17},{17,1},{2,18},{18,2},{3,19},{19,3},{4,20},{20... | collective-permute-start | bytes 638984 | tf_op jit(solution)/shard_map/ppermute | solution.py:115
  41.5 8.6 %collective-permute-start.12 = (bf16[32,4352]{1,0:T(8,128)(2,1)S(1)}, bf16[32,4352]{1,0:T(8,128)(2,1)S(1)}, u32[]{:S(2)}, u32[]{:S(2)}) collective-permute-start(bf16[32,4352]{1,0:T(8,128)(2,1)S(1)} %collective-permute-done.11.refs_0_), channel_id=1, source_target_pairs={{0,16},{16,0},{1,17},{17,1},{2,18},{18,2},{3,19},{19,3},{4,20},{20... | collective-permute-start | bytes 835592 | tf_op jit(solution)/shard_map/ppermute | solution.py:115
  41.8 10.9 %collective-permute-start.15 = (bf16[32,4352]{1,0:T(8,128)(2,1)S(1)}, bf16[32,4352]{1,0:T(8,128)(2,1)S(1)}, u32[]{:S(2)}, u32[]{:S(2)}) collective-permute-start(bf16[32,4352]{1,0:T(8,128)(2,1)S(1)} %collective-permute-done.7.refs_0_), channel_id=1, source_target_pairs={{0,4},{4,8},{8,12},{12,0},{1,5},{5,9},{9,13},{13,1},{2,6},{6,10},{... | collective-permute-start | bytes 835592 | tf_op jit(solution)/shard_map/ppermute | solution.py:106
  47.5 9.5 %collective-permute-start.10 = (bf16[32,4352]{1,0:T(8,128)(2,1)S(1)}, bf16[32,4352]{1,0:T(8,128)(2,1)S(1)}, u32[]{:S(2)}, u32[]{:S(2)}) collective-permute-start(bf16[32,4352]{1,0:T(8,128)(2,1)S(1)} %collective-permute-done.5.refs_0_), channel_id=1, source_target_pairs={{0,16},{16,0},{1,17},{17,1},{2,18},{18,2},{3,19},{19,3},{4,20},{20... | collective-permute-start | bytes 835592 | tf_op jit(solution)/shard_map/ppermute | solution.py:115
  48.4 10.0 %collective-permute-start.9 = (bf16[32,3328]{1,0:T(8,128)(2,1)S(1)}, bf16[32,3328]{1,0:T(8,128)(2,1)S(1)}, u32[]{:S(2)}, u32[]{:S(2)}) collective-permute-start(bf16[32,3328]{1,0:T(8,128)(2,1)S(1)} %collective-permute-done.1.refs_0_), channel_id=1, source_target_pairs={{0,4},{4,8},{8,12},{12,0},{1,5},{5,9},{9,13},{13,1},{2,6},{6,10},{... | collective-permute-start | bytes 638984 | tf_op jit(solution)/shard_map/ppermute | solution.py:106
  52.8 9.1 %collective-permute-start.16 = (bf16[32,4352]{1,0:T(8,128)(2,1)S(1)}, bf16[32,4352]{1,0:T(8,128)(2,1)S(1)}, u32[]{:S(2)}, u32[]{:S(2)}) collective-permute-start(bf16[32,4352]{1,0:T(8,128)(2,1)S(1)} %collective-permute-done.15.refs_0_), channel_id=1, source_target_pairs={{0,16},{16,0},{1,17},{17,1},{2,18},{18,2},{3,19},{19,3},{4,20},{20... | collective-permute-start | bytes 835592 | tf_op jit(solution)/shard_map/ppermute | solution.py:115
  54.5 11.2 %collective-permute-start.18 = (bf16[32,4352]{1,0:T(8,128)(2,1)S(1)}, bf16[32,4352]{1,0:T(8,128)(2,1)S(1)}, u32[]{:S(2)}, u32[]{:S(2)}) collective-permute-start(bf16[32,4352]{1,0:T(8,128)(2,1)S(1)} %collective-permute-done.11.refs_0_), channel_id=1, source_target_pairs={{0,4},{4,8},{8,12},{12,0},{1,5},{5,9},{9,13},{13,1},{2,6},{6,10},{... | collective-permute-start | bytes 835592 | tf_op jit(solution)/shard_map/ppermute | solution.py:106
  58.4 13.3 %collective-permute-start.13 = (bf16[32,4352]{1,0:T(8,128)(2,1)S(1)}, bf16[32,4352]{1,0:T(8,128)(2,1)S(1)}, u32[]{:S(2)}, u32[]{:S(2)}) collective-permute-start(bf16[32,4352]{1,0:T(8,128)(2,1)S(1)} %collective-permute-done.5.refs_0_), channel_id=1, source_target_pairs={{0,4},{4,8},{8,12},{12,0},{1,5},{5,9},{9,13},{13,1},{2,6},{6,10},{... | collective-permute-start | bytes 835592 | tf_op jit(solution)/shard_map/ppermute | solution.py:106
  58.4 8.6 %collective-permute-start.14 = (bf16[32,3328]{1,0:T(8,128)(2,1)S(1)}, bf16[32,3328]{1,0:T(8,128)(2,1)S(1)}, u32[]{:S(2)}, u32[]{:S(2)}) collective-permute-start(bf16[32,3328]{1,0:T(8,128)(2,1)S(1)} %collective-permute-done.9.refs_0_), channel_id=1, source_target_pairs={{0,16},{16,0},{1,17},{17,1},{2,18},{18,2},{3,19},{19,3},{4,20},{20... | collective-permute-start | bytes 638984 | tf_op jit(solution)/shard_map/ppermute | solution.py:115
  65.8 9.7 %collective-permute-start.21 = (bf16[32,4352]{1,0:T(8,128)(2,1)S(1)}, bf16[32,4352]{1,0:T(8,128)(2,1)S(1)}, u32[]{:S(2)}, u32[]{:S(2)}) collective-permute-start(bf16[32,4352]{1,0:T(8,128)(2,1)S(1)} %collective-permute-done.15.refs_0_), channel_id=1, source_target_pairs={{0,4},{4,8},{8,12},{12,0},{1,5},{5,9},{9,13},{13,1},{2,6},{6,10},{... | collective-permute-start | bytes 835592 | tf_op jit(solution)/shard_map/ppermute | solution.py:106
  65.8 11.3 %collective-permute-start.19 = (bf16[32,4352]{1,0:T(8,128)(2,1)S(1)}, bf16[32,4352]{1,0:T(8,128)(2,1)S(1)}, u32[]{:S(2)}, u32[]{:S(2)}) collective-permute-start(bf16[32,4352]{1,0:T(8,128)(2,1)S(1)} %collective-permute-done.18.refs_0_), channel_id=1, source_target_pairs={{0,16},{16,0},{1,17},{17,1},{2,18},{18,2},{3,19},{19,3},{4,20},{20... | collective-permute-start | bytes 835592 | tf_op jit(solution)/shard_map/ppermute | solution.py:115
  71.7 7.6 %collective-permute-start.17 = (bf16[32,3328]{1,0:T(8,128)(2,1)S(1)}, bf16[32,3328]{1,0:T(8,128)(2,1)S(1)}, u32[]{:S(2)}, u32[]{:S(2)}) collective-permute-start(bf16[32,3328]{1,0:T(8,128)(2,1)S(1)} %collective-permute-done.9.refs_0_), channel_id=1, source_target_pairs={{0,4},{4,8},{8,12},{12,0},{1,5},{5,9},{9,13},{13,1},{2,6},{6,10},{... | collective-permute-start | bytes 638984 | tf_op jit(solution)/shard_map/ppermute | solution.py:106
  71.7 9.2 %collective-permute-start.23 = (bf16[32,4352]{1,0:T(8,128)(2,1)S(1)}, bf16[32,4352]{1,0:T(8,128)(2,1)S(1)}, u32[]{:S(2)}, u32[]{:S(2)}) collective-permute-start(bf16[32,4352]{1,0:T(8,128)(2,1)S(1)} %collective-permute-done.13.refs_0_), channel_id=1, source_target_pairs={{0,16},{16,0},{1,17},{17,1},{2,18},{18,2},{3,19},{19,3},{4,20},{20... | collective-permute-start | bytes 835592 | tf_op jit(solution)/shard_map/ppermute | solution.py:115
  75.5 8.4 %collective-permute-start.22 = (bf16[32,4352]{1,0:T(8,128)(2,1)S(1)}, bf16[32,4352]{1,0:T(8,128)(2,1)S(1)}, u32[]{:S(2)}, u32[]{:S(2)}) collective-permute-start(bf16[32,4352]{1,0:T(8,128)(2,1)S(1)} %collective-permute-done.21.refs_0_), channel_id=1, source_target_pairs={{0,16},{16,0},{1,17},{17,1},{2,18},{18,2},{3,19},{19,3},{4,20},{20... | collective-permute-start | bytes 835592 | tf_op jit(solution)/shard_map/ppermute | solution.py:115
  79.4 6.8 %collective-permute-start.20 = (bf16[32,3328]{1,0:T(8,128)(2,1)S(1)}, bf16[32,3328]{1,0:T(8,128)(2,1)S(1)}, u32[]{:S(2)}, u32[]{:S(2)}) collective-permute-start(bf16[32,3328]{1,0:T(8,128)(2,1)S(1)} %collective-permute-done.17.refs_0_), channel_id=1, source_target_pairs={{0,16},{16,0},{1,17},{17,1},{2,18},{18,2},{3,19},{19,3},{4,20},{20... | collective-permute-start | bytes 638984 | tf_op jit(solution)/shard_map/ppermute | solution.py:115
  86.9 1.4 %collective-permute-start.24 = (f32[2,64,256]{2,1,0:T(8,128)S(1)}, f32[2,64,256]{2,1,0:T(8,128)S(1)}, u32[]{:S(2)}, u32[]{:S(2)}) collective-permute-start(f32[2,64,256]{2,1,0:T(8,128)S(1)} %slice_bitcast_fusion), channel_id=1, source_target_pairs={{0,1},{1,0},{2,3},{3,2},{4,5},{5,4},{6,7},{7,6},{8,9},{9,8},{10,11... | collective-permute-start | bytes 393224 | tf_op jit(solution)/shard_map/ppermute | solution.py:124
  88.3 4.3 %collective-permute-start.25 = (f32[1,64,256]{2,1,0:T(8,128)S(1)}, f32[1,64,256]{2,1,0:T(8,128)S(1)}, u32[]{:S(2)}, u32[]{:S(2)}) collective-permute-start(f32[1,64,256]{2,1,0:T(8,128)S(1)} %slice_bitcast_fusion.2), channel_id=1, source_target_pairs={{0,2},{1,3},{2,0},{3,1},{4,6},{5,7},{6,4},{7,5},{8,10},{9,11},{10,... | collective-permute-start | bytes 196616 | tf_op jit(solution)/shard_map/ppermute | solution.py:124

commit v22 on v20

--- a/solution.py
+++ b/solution.py
@@ -67,12 +67,132 @@
         out[to * half : (to + 1) * half, :] = kept[pl.ds(at, half), :]
 
 
-def call(kernel, rows, docs, width, operands, scratch=()):
+LINE, SHIP = (5, 5, 4), 2
+KEPT = ((0, 1, 2, 3), (1, 0, 2, 3), (2, 3, 1, 0), (3, 2, 1, 0))
+
+
+def line_rows(n_grp, n_feat, halved):
+    ex, grp, feat = (lax.axis_index(a) for a in ("ex", "grp", "feat"))
+    units = len(KEPT) * n_grp
+    each = units // n_feat
+    found = []
+    for to in range(units):
+        unit_of = (feat ^ (to // each)) * each + to % each
+        block, h = lax.div(unit_of, n_grp), lax.rem(unit_of, n_grp)
+        t = jnp.int32(0)
+        for i, kept in enumerate(KEPT):
+            for b in kept[1:]:
+                t = jnp.where((ex == i) & (block == b), kept.index(b), t)
+        place = jnp.where(t == 0, h, lax.rem(h + n_grp - grp, n_grp)) if halved else h
+        found.append(t * n_grp + place)
+    return found
+
+
+def units_product(rows, scale, trains, unit, first, count):
+    total = None
+    for k in range(count):
+        j = first + k
+        column = scale[:, j * unit : (j + 1) * unit]
+        precond = (rows(k).astype(jnp.float32) * column).astype(jnp.bfloat16)
+        here = trains[j // 4][:, (j % 4) * unit : (j % 4 + 1) * unit]
+        part = lax.dot_general(precond, here, CONTRACT, preferred_element_type=jnp.float32)
+        total = part if total is None else total + part
+    return total
+
+
+def line_own_kernel(unit, test, scale, *refs):
+    rows = lambda k: test[:, k * unit : (k + 1) * unit]
+    refs[-1][...] = units_product(rows, scale, refs[:-1], unit, 0, sum(LINE))
+
+
+def line_part_kernel(unit, first, count, quarters, n_parts, *refs):
+    parts, scale = refs[:n_parts], refs[n_parts]
+    trains = dict(zip(quarters, refs[n_parts + 1 :]))
+    base = refs[n_parts + 1 + len(quarters) : -1]
+    rows = lambda k: jnp.concatenate([p[:, k * unit : (k + 1) * unit] for p in parts], axis=0)
+    total = units_product(rows, scale, trains, unit, first, count)
+    refs[-1][...] = total + base[0][...] if base else total
+
+
+def line_last_kernel(n_grp, n_feat, unit, first, count, quarters, n_parts, *refs):
+    parts, scale = refs[:n_parts], refs[n_parts]
+    trains = dict(zip(quarters, refs[n_parts + 1 :]))
+    near, *sums = refs[n_parts + 1 + len(quarters) : -2]
+    out, kept = refs[-2:]
+    rows = lambda k: jnp.concatenate([p[:, k * unit : (k + 1) * unit] for p in parts], axis=0)
+    total = units_product(rows, scale, trains, unit, first, count) + sums[-1][...]
+    queries = total.shape[0]
+    half = queries // n_grp
+    for t, value in enumerate([s[...] for s in sums[:-1]] + [total]):
+        kept[t * queries : (t + 1) * queries, :] = value
+    for to, place in enumerate(line_rows(n_grp, n_feat, True)):
+        at = pl.multiple_of(place * half, half)
+        here = slice(to * half, (to + 1) * half)
+        out[here, :] = kept[pl.ds(at, half), :] + near[here, :]
+
+
+def crate_kernel(unit, n_grp, test, train, *outs):
+    half = test.shape[0] // n_grp
+    base = sum(LINE)
+    blocks = []
+    for h in range(n_grp):
+        for x in range(SHIP):
+            cols = slice((base + x) * unit, (base + x + 1) * unit)
+            blocks.append(test[h * half : (h + 1) * half, cols])
+    n_tests = len(blocks)
+    for x in range(SHIP):
+        at = ((base + x) % 4) * unit
+        for g in range(train.shape[0] // half):
+            blocks.append(train[g * half : (g + 1) * half, at : at + unit])
+    for i, block in enumerate(blocks[:n_tests]):
+        outs[-1][:, i * unit : (i + 1) * unit] = block
+    for out in outs[:-1]:
+        for i in range(out.shape[1] // unit):
+            out[:, i * unit : (i + 1) * unit] = blocks.pop(0) if len(blocks) > 1 else blocks[0]
+
+
+def shipped_kernel(n_grp, n_feat, unit, n_cargo, test, scale, train, other, *refs):
+    cargo, (near, far, kept) = refs[:n_cargo], refs[n_cargo:]
+    base = sum(LINE)
+    half = test.shape[0] // n_grp
+    blocks = [(c, i * unit) for c in cargo for i in range(c.shape[1] // unit)]
+    tests, rows_of = blocks[: n_grp * SHIP], blocks[n_grp * SHIP :]
+    groups = train.shape[0] // half
+    sums = [None, None]
+    for x in range(SHIP):
+        parts = [test[:, (base + x) * unit : (base + x + 1) * unit]]
+        for h in range(n_grp):
+            ref, at = tests[h * SHIP + x]
+            parts.append(ref[:, at : at + unit])
+        for k in range(2):
+            for h in range(n_grp):
+                at = (h * SHIP + x) * unit
+                parts.append(other[k * half : (k + 1) * half, at : at + unit])
+        rows = jnp.concatenate(parts, axis=0)
+        column = scale[:, (base + x) * unit : (base + x + 1) * unit]
+        precond = (rows.astype(jnp.float32) * column).astype(jnp.bfloat16)
+        at = ((base + x) % 4) * unit
+        away = [ref[:, c : c + unit] for ref, c in rows_of[x * groups : (x + 1) * groups]]
+        for i, docs in enumerate((train[:, at : at + unit], jnp.concatenate(away, axis=0))):
+            part = lax.dot_general(precond, docs, CONTRACT, preferred_element_type=jnp.float32)
+            sums[i] = part if sums[i] is None else sums[i] + part
+    ex = lax.axis_index("ex")
+    inner = (ex > 0) & (ex < len(KEPT) - 1)
+    places = line_rows(n_grp, n_feat, False)
+    for value, out in zip((jnp.where(inner, sums[0], 0.0), sums[1]), (near, far)):
+        kept[...] = value
+        for to, place in enumerate(places):
+            at = pl.multiple_of(place * half, half)
+            out[to * half : (to + 1) * half, :] = kept[pl.ds(at, half), :]
+
+
+def call(kernel, rows, docs, width, operands, scratch=(), shapes=None):
+    vmem = pl.BlockSpec(memory_space=pltpu.VMEM)
     return pl.pallas_call(
         kernel,
-        out_shape=jax.ShapeDtypeStruct((rows, docs), jnp.float32),
-        in_specs=[pl.BlockSpec(memory_space=pltpu.VMEM)] * len(operands),
-        out_specs=pl.BlockSpec(memory_space=pltpu.VMEM),
+        out_shape=shapes or jax.ShapeDtypeStruct((rows, docs), jnp.float32),
+        in_specs=[vmem] * len(operands),
+        out_specs=[vmem] * len(shapes) if shapes else vmem,
         scratch_shapes=scratch,
         cost_estimate=pl.CostEstimate(
             flops=2 * rows * docs * width, bytes_accessed=2 * (rows + docs) * width, transcendentals=0
@@ -84,6 +204,133 @@
 def solution(mesh):
     n_grp, n_ex, n_feat = (mesh.shape[a] for a in ("grp", "ex", "feat"))
     assert n_grp <= 2
+
+    def after(block, *waits):
+        return lax.optimization_barrier((block, waits))[0] if waits else block
+
+    def line(train, test, scale):
+        docs, feats = train.shape
+        queries = test.shape[0]
+        half = queries // n_grp
+        unit = feats // (sum(LINE) + SHIP)
+        ex = lax.axis_index("ex")
+        is_end, first_grp = (ex == 0) | (ex == n_ex - 1), lax.axis_index("grp") == 0
+        test, is_end, first_grp = lax.optimization_barrier((test, is_end, first_grp))
+        done, outs, swaps, middles, made = {}, [], [], [], []
+
+        outer_pairs = [(i, i ^ 1) for i in range(n_ex)]
+        middle_pairs = []
+        for i in range(n_ex):
+            for f in range(n_feat):
+                to = (i, f ^ 1) if i in (0, n_ex - 1) else (n_ex - 1 - i, f)
+                middle_pairs.append((i * n_feat + f, to[0] * n_feat + to[1]))
+
+        def outer(name, block):
+            waits = outs[-2:-1] + swaps[-4:-3] + made[-4:-3] + (first if len(outs) == 3 else [])
+            outs.append(lax.ppermute(after(block, *waits), "ex", outer_pairs))
+            done[name] = outs[-1]
+
+        def middle(name, block):
+            middles.append(lax.ppermute(after(block, *middles[-1:]), ("ex", "feat"), middle_pairs))
+            done[name] = middles[-1]
+
+        def swap(block):
+            if n_grp == 1:
+                return [block]
+            waits = swaps[-2:-1]
+            if len(swaps) > 2 * len(LINE):
+                waits = swaps[-3:-2] + made[-3:-2]
+            swaps.append(lax.ppermute(after(block, *waits), "grp", [(0, 1), (1, 0)]))
+            return [block, swaps[-1]]
+
+        def sum_over_feat(sums, *waits):
+            held = sums.reshape(n_feat, -1, docs)
+            bit = 1
+            while bit < n_feat:
+                pairs = held.reshape((-1, 2) + held.shape[1:])
+                partner = [(i, i ^ bit) for i in range(n_feat)]
+                send = after(pairs[:, 1], *waits)
+                held, waits = pairs[:, 0] + lax.ppermute(send, "feat", partner), ()
+                bit *= 2
+            return held[0]
+
+        def share(rows, start, count):
+            here = slice(start * unit, (start + count) * unit)
+            if n_grp == 1:
+                return rows[:, here]
+            return jnp.where(first_grp, rows[:half, here], rows[half:, here])
+
+        firsts = [sum(LINE[:c]) for c in range(len(LINE))]
+        columns = [slice(f * unit, (f + n) * unit) for f, n in zip(firsts, LINE)]
+        mine = []
+        for start, count in zip(firsts, LINE):
+            mine.append(share(after(test, *mine[-1:]), start, count))
+        every = share(after(test, mine[0]), 0, sum(LINE))
+        trains = [train[:, q * 4 * unit : (q + 1) * 4 * unit] for q in range(4)]
+        own = call(
+            functools.partial(line_own_kernel, unit), queries, docs, feats, [test, scale, *trains]
+        )
+        first = [own]
+        widths = [*LINE, *LINE[:2]]
+        shapes = [jax.ShapeDtypeStruct((half, w * unit), test.dtype) for w in widths]
+        shapes.append(jax.ShapeDtypeStruct((half, n_grp * SHIP * unit), test.dtype))
+        *cargo, own_tests = call(
+            functools.partial(crate_kernel, unit, n_grp), docs, SHIP * unit, 1,
+            [test, trains[3]], shapes=shapes,
+        )
+
+        sums = [own, None, None, None]
+        n = len(LINE)
+
+        def finish(t, c, block):
+            parts = swap(block)
+            quarters = sorted({j // 4 for j in range(firsts[c], firsts[c] + LINE[c])})
+            operands = [*parts, scale, *(trains[q] for q in quarters)]
+            sizes = (unit, firsts[c], LINE[c], quarters, len(parts))
+            if (t, c) == (3, n - 1):
+                return sizes, operands
+            base = [] if sums[t] is None else [sums[t]]
+            kernel = functools.partial(line_part_kernel, *sizes)
+            sums[t] = call(kernel, queries, docs, LINE[c] * unit, operands + base)
+            made.append(sums[t])
+
+        for c in range(n):
+            outer(f"E1{c}", mine[c])
+            if c == 0:
+                middle("O1", every)
+            finish(1, c, done[f"E1{c}"])
+        middle("O20", done["E10"])
+        for c in range(n):
+            inner = done["O1"][:, columns[c]]
+            outer(f"E2{c}", jnp.where(is_end, cargo[c], inner))
+            if c == 0:
+                middle("O21", jnp.concatenate([done["E11"], done["E12"]], axis=1))
+            finish(2, c, jnp.where(is_end, done[f"E2{c}"], inner))
+        end_tests = done["E20"][:, : own_tests.shape[1]]
+        middle("OS", jnp.concatenate([own_tests, end_tests], axis=0))
+        for c in range(n):
+            inner = done["O20"] if c == 0 else done["O21"]
+            if c > 0:
+                inner = inner[:, columns[c].start - columns[1].start : columns[c].stop - columns[1].start]
+            outer(f"E3{c}", jnp.where(is_end, cargo[3 + c], inner) if c < 2 else inner)
+            last = finish(3, c, jnp.where(is_end, done[f"E3{c}"], inner))
+        shape = jax.ShapeDtypeStruct((n_ex * queries, docs), jnp.float32)
+        landed = [done[name] for name in ("E20", "E21", "E22", "E30", "E31")]
+        near, far = call(
+            functools.partial(shipped_kernel, n_grp, n_feat, unit, len(landed)),
+            n_ex * queries, docs, 2 * SHIP * unit,
+            [test, scale, trains[3], done["OS"], *landed],
+            [pltpu.VMEM(shape.shape, jnp.float32)], shapes=[shape, shape],
+        )
+        back = lax.ppermute(sum_over_feat(far), "ex", outer_pairs)
+        sizes, operands = last
+        total = call(
+            functools.partial(line_last_kernel, n_grp, n_feat, *sizes),
+            n_ex * queries, docs, LINE[-1] * unit, [*operands, near, *sums],
+            [pltpu.VMEM(shape.shape, jnp.float32)],
+        )
+        out = sum_over_feat(total, back) + jnp.where(is_end, back, 0.0)
+        return out.T
 
     def on_device(train, test, hess):
         docs, feats = train.shape
@@ -130,6 +377,8 @@
             return jnp.where(first_grp, rows[:half, columns], rows[half:, columns])
 
         scale = (1.0 / (hess + jnp.float32(0.1))).reshape(1, feats)
+        if n_ex == len(KEPT):
+            return line(train, test, scale)
         held = []
         for here in columns:
             held.append(share(after(test, *held[-1:]), here))

time: 90.9 us -> 107 us (1.18)
  waiting for transfers between devices: 46.2 us -> 56.6 us
  starting transfers between devices: 24.5 us -> 29.5 us
    ppermute x12 -> x9, waiting for transfers between devices: 13 us -> 24.6 us  [swap(): swaps.append(lax.ppermute(after(block, *waits), 'grp', [(0, 1), (1, 0)]))]
    ppermute x14 -> x18, starting transfers between devices: 7.34 us -> 16.6 us  [the longest x9 12.2 us: outer(): outs.append(lax.ppermute(after(block, *waits), 'ex', outer_pairs))]
    ppermute x12 -> x9, starting transfers between devices: 17.2 us -> 12.8 us  [swap(): swaps.append(lax.ppermute(after(block, *waits), 'grp', [(0, 1), (1, 0)]))]
    ppermute x14 -> x18, waiting for transfers between devices: 33.2 us -> 32.1 us  [the longest x9 24.8 us: outer(): outs.append(lax.ppermute(after(block, *waits), 'ex', outer_pairs))]
    select_n x4 -> x14, other arithmetic: 3.36 us -> 4.17 us  [the longest x4 3.8 us: share(): return jnp.where(first_grp, rows[:half, here], rows[half:, here])]
    pallas_call x13 -> x12, Pallas kernels: 11.8 us -> 11 us  [call(): pl.pallas_call(kernel, out_shape=shapes or jax.ShapeDtypeStruct((rows, do...]
    slice x1 -> x3, local copies, waits for them, and re-layouts: 3.97 us -> 4.1 us  [the longest x1 4.07 us: line(): trains = [train[:, q * 4 * unit:(q + 1) * 4 * unit] for q in range(4)]]
  transfers between devices with their start and end apart: 26 -> 27, of which waited for: 23 -> 16; matrix products, arithmetic and copies ran while one was open for 7% -> 7% of each run, Pallas kernels for 12% -> 10%
where the time goes in v22:
time: 107 us
  waiting for transfers between devices  56.6 us (53%)
  starting transfers between devices  29.5 us (28%)
  Pallas kernels  11 us (10%)
  other arithmetic  4.95 us (5%)
  local copies, waits for them, and re-layouts  4.15 us (4%)
    ppermute x9, waiting for transfers between devices, outer(): outs.append(lax.ppermute(after(block, *waits), 'ex', outer_pairs))  24.8 us
    ppermute x9, waiting for transfers between devices, swap(): swaps.append(lax.ppermute(after(block, *waits), 'grp', [(0, 1), (1, 0)]))  24.6 us
    ppermute x9, starting transfers between devices, swap(): swaps.append(lax.ppermute(after(block, *waits), 'grp', [(0, 1), (1, 0)]))  12.8 us
    ppermute x9, starting transfers between devices, outer(): outs.append(lax.ppermute(after(block, *waits), 'ex', outer_pairs))  12.2 us
    pallas_call x12, Pallas kernels, call(): pl.pallas_call(kernel, out_shape=shapes or jax.ShapeDtypeStruct((rows, do...  11 us
    slice x1, local copies, waits for them, and re-layouts, line(): trains = [train[:, q * 4 * unit:(q + 1) * 4 * unit] for q in range(4)]  4.07 us
    ppermute x4, waiting for transfers between devices, sum_over_feat(): held, waits = (pairs[:, 0] + lax.ppermute(send, 'feat', partner), ())  4.04 us
    select_n x4, other arithmetic, share(): return jnp.where(first_grp, rows[:half, here], rows[half:, here])  3.8 us
  transfers between devices with their start and end apart: 27, of which 16 were waited for; matrix products, arithmetic and copies ran while one was open for 7% of the time, Pallas kernels for 10%

profile of v22, /device:TPU:0, one launch (start us, length us, event | category | flops | bytes accessed | tf_op | source)
XLA Modules:
  0.0 106.6 jit_solution(5536909652154562195)
XLA Ops:
  1.1 3.1 %collective-permute-start.1 = (bf16[32,5120]{1,0:T(8,128)(2,1)S(1)}, bf16[32,5120]{1,0:T(8,128)(2,1)S(1)}, u32[]{:S(2)}, u32[]{:S(2)}) collective-permute-start(bf16[32,5120]{1,0:T(8,128)(2,1)S(1)} %slice_select_fusion.2), channel_id=1, source_target_pairs={{0,4},{4,0},{8,12},{12,8},{1,5},{5,1},{9,13},{13,9},{2,6},{6,2},{1... | collective-permute-start | bytes 983048 | tf_op jit(solution)/shard_map/ppermute | solution.py:230
  5.4 1.6 %slice_select_fusion = bf16[32,14336]{1,0:T(8,128)(2,1)S(1)} fusion(bf16[64,16384]{1,0:T(8,128)(2,1)} %test.2, pred[]{:T(512)S(6)} %eq.11), kind=kLoop, calls=%fused_computation | loop fusion | flops 458752 | bytes 2752513 | tf_op jit(solution)/shard_map/jit(_where)/select_n | solution.py:261
  7.1 4.1 %fusion.10 = (bf16[256,4096]{1,0:T(8,128)(2,1)S(1)}, bf16[256,4096]{1,0:T(8,128)(2,1)S(1)}, bf16[256,4096]{1,0:T(8,128)(2,1)S(1)}, bf16[256,4096]{1,0:T(8,128)(2,1)S(1)}) fusion(bf16[256,16384]{1,0:T(8,128)(2,1)} %param.3), kind=kLoop, calls=%fused_computation.36 | loop fusion | bytes 16777216 | tf_op jit(solution)/shard_map/slice | solution.py:269
  11.2 1.6 %collective-permute-done.1.refs_0_ = bf16[32,5120]{1,0:T(8,128)(2,1)S(1)} collective-permute-done((bf16[32,5120]{1,0:T(8,128)(2,1)S(1)}, bf16[32,5120]{1,0:T(8,128)(2,1)S(1)}, u32[]{:S(2)}, u32[]{:S(2)}) %collective-permute-start.1) | collective-permute-done | bytes 327712 | tf_op jit(solution)/shard_map/ppermute | solution.py:230
  12.7 2.1 %collective-permute-start.2 = (bf16[32,4096]{1,0:T(8,128)(2,1)S(1)}, bf16[32,4096]{1,0:T(8,128)(2,1)S(1)}, u32[]{:S(2)}, u32[]{:S(2)}) collective-permute-start(bf16[32,4096]{1,0:T(8,128)(2,1)S(1)} %slice_select_fusion.3), channel_id=1, source_target_pairs={{0,4},{4,0},{8,12},{12,8},{1,5},{5,1},{9,13},{13,9},{2,6},{6,2},{1... | collective-permute-start | bytes 786440 | tf_op jit(solution)/shard_map/ppermute | solution.py:230
  14.9 2.3 %shard_map.41.refs_6_ = f32[64,256]{1,0:T(8,128)S(1)} custom-call(bf16[64,16384]{1,0:T(8,128)(2,1)S(1)} %copy-done, f32[1,16384]{1,0:T(1,128)S(1)} %bitcast.61, bf16[256,4096]{1,0:T(8,128)(2,1)S(1)} %get-tuple-element.68.refs_3_.refs_0_, bf16[256,4096]{1,0:T(8,128)(2,1)S(1)} %get-tuple-element.70.refs_4_.refs_3_.refs_1_, ...), custom_call_target="tpu_custom_call" | custom-call | flops 536870912 | bytes 10485760 | tf_op jit(solution)/shard_map/pallas_call | solution.py:191
  17.3 1.6 %collective-permute-start.6 = (bf16[32,5120]{1,0:T(8,128)(2,1)S(1)}, bf16[32,5120]{1,0:T(8,128)(2,1)S(1)}, u32[]{:S(2)}, u32[]{:S(2)}) collective-permute-start(bf16[32,5120]{1,0:T(8,128)(2,1)S(1)} %collective-permute-done.1.refs_0_), channel_id=1, source_target_pairs={{0,16},{16,0},{1,17},{17,1},{2,18},{18,2},{3,19},{19,3},{4,20},{20... | collective-permute-start | bytes 983048 | tf_op jit(solution)/shard_map/ppermute | solution.py:243
  19.8 2.0 %collective-permute-start.9 = (bf16[32,5120]{1,0:T(8,128)(2,1)S(1)}, bf16[32,5120]{1,0:T(8,128)(2,1)S(1)}, u32[]{:S(2)}, u32[]{:S(2)}) collective-permute-start(bf16[32,5120]{1,0:T(8,128)(2,1)S(1)} %collective-permute-done.refs_0_), channel_id=1, source_target_pairs={{0,16},{16,0},{1,17},{17,1},{2,18},{18,2},{3,19},{19,3},{4,20},{20... | collective-permute-start | bytes 983048 | tf_op jit(solution)/shard_map/ppermute | solution.py:243
  21.8 2.8 %collective-permute-done.2.refs_0_ = bf16[32,4096]{1,0:T(8,128)(2,1)S(1)} collective-permute-done((bf16[32,4096]{1,0:T(8,128)(2,1)S(1)}, bf16[32,4096]{1,0:T(8,128)(2,1)S(1)}, u32[]{:S(2)}, u32[]{:S(2)}) %collective-permute-start.2) | collective-permute-done | bytes 262176 | tf_op jit(solution)/shard_map/ppermute | solution.py:230
  24.6 3.4 %collective-permute-done.6.refs_1_ = bf16[32,5120]{1,0:T(8,128)(2,1)S(1)} collective-permute-done((bf16[32,5120]{1,0:T(8,128)(2,1)S(1)}, bf16[32,5120]{1,0:T(8,128)(2,1)S(1)}, u32[]{:S(2)}, u32[]{:S(2)}) %collective-permute-start.6) | collective-permute-done | bytes 327712 | tf_op jit(solution)/shard_map/ppermute | solution.py:243
  28.0 1.5 %collective-permute-start.8 = (bf16[32,4096]{1,0:T(8,128)(2,1)S(1)}, bf16[32,4096]{1,0:T(8,128)(2,1)S(1)}, u32[]{:S(2)}, u32[]{:S(2)}) collective-permute-start(bf16[32,4096]{1,0:T(8,128)(2,1)S(1)} %collective-permute-done.2.refs_0_), channel_id=1, source_target_pairs={{0,16},{16,0},{1,17},{17,1},{2,18},{18,2},{3,19},{19,3},{4,20},{20... | collective-permute-start | bytes 786440 | tf_op jit(solution)/shard_map/ppermute | solution.py:243
  30.4 4.6 %collective-permute-done.9.refs_1_ = bf16[32,5120]{1,0:T(8,128)(2,1)S(1)} collective-permute-done((bf16[32,5120]{1,0:T(8,128)(2,1)S(1)}, bf16[32,5120]{1,0:T(8,128)(2,1)S(1)}, u32[]{:S(2)}, u32[]{:S(2)}) %collective-permute-start.9) | collective-permute-done | bytes 327712 | tf_op jit(solution)/shard_map/ppermute | solution.py:243
  36.2 2.0 %collective-permute-done.8.refs_1_ = bf16[32,4096]{1,0:T(8,128)(2,1)S(1)} collective-permute-done((bf16[32,4096]{1,0:T(8,128)(2,1)S(1)}, bf16[32,4096]{1,0:T(8,128)(2,1)S(1)}, u32[]{:S(2)}, u32[]{:S(2)}) %collective-permute-start.8) | collective-permute-done | bytes 262176 | tf_op jit(solution)/shard_map/ppermute | solution.py:243
  39.0 7.0 %collective-permute-done.12.refs_0_ = bf16[32,5120]{1,0:T(8,128)(2,1)S(1)} collective-permute-done((bf16[32,5120]{1,0:T(8,128)(2,1)S(1)}, bf16[32,5120]{1,0:T(8,128)(2,1)S(1)}, u32[]{:S(2)}, u32[]{:S(2)}) %collective-permute-start.12) | collective-permute-done | bytes 327712 | tf_op jit(solution)/shard_map/ppermute | solution.py:230
  46.0 2.0 %collective-permute-start.13 = (bf16[32,5120]{1,0:T(8,128)(2,1)S(1)}, bf16[32,5120]{1,0:T(8,128)(2,1)S(1)}, u32[]{:S(2)}, u32[]{:S(2)}) collective-permute-start(bf16[32,5120]{1,0:T(8,128)(2,1)S(1)} %get-tuple-element.52.refs_0_), channel_id=1, source_target_pairs={{0,16},{16,0},{1,17},{17,1},{2,18},{18,2},{3,19},{19,3},{4,20},{20... | collective-permute-start | bytes 983048 | tf_op jit(solution)/shard_map/ppermute | solution.py:243
  48.1 2.7 %collective-permute-start.7 = (bf16[32,5120]{1,0:T(8,128)(2,1)S(1)}, bf16[32,5120]{1,0:T(8,128)(2,1)S(1)}, u32[]{:S(2)}, u32[]{:S(2)}) collective-permute-start(bf16[32,5120]{1,0:T(8,128)(2,1)S(1)} %get-tuple-element.46), channel_id=1, source_target_pairs={{0,4},{4,0},{8,12},{12,8},{1,5},{5,1},{9,13},{13,9},{2,6},{6,2},{1... | collective-permute-start | bytes 983048 | tf_op jit(solution)/shard_map/ppermute | solution.py:230
  50.9 2.5 %collective-permute-done.15.refs_2_ = bf16[32,4096]{1,0:T(8,128)(2,1)S(1)} collective-permute-done((bf16[32,4096]{1,0:T(8,128)(2,1)S(1)}, bf16[32,4096]{1,0:T(8,128)(2,1)S(1)}, u32[]{:S(2)}, u32[]{:S(2)}) %collective-permute-start.15) | collective-permute-done | bytes 262176 | tf_op jit(solution)/shard_map/ppermute | solution.py:230
  53.4 5.9 %collective-permute-done.7.refs_1_ = bf16[32,5120]{1,0:T(8,128)(2,1)S(1)} collective-permute-done((bf16[32,5120]{1,0:T(8,128)(2,1)S(1)}, bf16[32,5120]{1,0:T(8,128)(2,1)S(1)}, u32[]{:S(2)}, u32[]{:S(2)}) %collective-permute-start.7) | collective-permute-done | bytes 327712 | tf_op jit(solution)/shard_map/ppermute | solution.py:230
  59.4 2.0 %collective-permute-start.11 = (bf16[32,5120]{1,0:T(8,128)(2,1)S(1)}, bf16[32,5120]{1,0:T(8,128)(2,1)S(1)}, u32[]{:S(2)}, u32[]{:S(2)}) collective-permute-start(bf16[32,5120]{1,0:T(8,128)(2,1)S(1)} %broadcast_select_fusion.5.refs_0_), channel_id=1, source_target_pairs={{0,16},{16,0},{1,17},{17,1},{2,18},{18,2},{3,19},{19,3},{4,20},{20... | collective-permute-start | bytes 983048 | tf_op jit(solution)/shard_map/ppermute | solution.py:243
  62.5 2.1 %collective-permute-start.19 = (bf16[32,5120]{1,0:T(8,128)(2,1)S(1)}, bf16[32,5120]{1,0:T(8,128)(2,1)S(1)}, u32[]{:S(2)}, u32[]{:S(2)}) collective-permute-start(bf16[32,5120]{1,0:T(8,128)(2,1)S(1)} %broadcast_select_fusion.2), channel_id=1, source_target_pairs={{0,4},{4,0},{8,12},{12,8},{1,5},{5,1},{9,13},{13,9},{2,6},{6,2},{1... | collective-permute-start | bytes 983048 | tf_op jit(solution)/shard_map/ppermute | solution.py:230
  64.5 5.5 %collective-permute-done.11.refs_1_ = bf16[32,5120]{1,0:T(8,128)(2,1)S(1)} collective-permute-done((bf16[32,5120]{1,0:T(8,128)(2,1)S(1)}, bf16[32,5120]{1,0:T(8,128)(2,1)S(1)}, u32[]{:S(2)}, u32[]{:S(2)}) %collective-permute-start.11) | collective-permute-done | bytes 327712 | tf_op jit(solution)/shard_map/ppermute | solution.py:243
  71.0 2.1 %collective-permute-start.14 = (bf16[32,4096]{1,0:T(8,128)(2,1)S(1)}, bf16[32,4096]{1,0:T(8,128)(2,1)S(1)}, u32[]{:S(2)}, u32[]{:S(2)}) collective-permute-start(bf16[32,4096]{1,0:T(8,128)(2,1)S(1)} %slice.104), channel_id=1, source_target_pairs={{0,4},{4,0},{8,12},{12,8},{1,5},{5,1},{9,13},{13,9},{2,6},{6,2},{1... | collective-permute-start | bytes 786440 | tf_op jit(solution)/shard_map/ppermute | solution.py:230
  73.1 1.4 %collective-permute-start.21 = (bf16[32,5120]{1,0:T(8,128)(2,1)S(1)}, bf16[32,5120]{1,0:T(8,128)(2,1)S(1)}, u32[]{:S(2)}, u32[]{:S(2)}) collective-permute-start(bf16[32,5120]{1,0:T(8,128)(2,1)S(1)} %broadcast_select_fusion.refs_0_), channel_id=1, source_target_pairs={{0,16},{16,0},{1,17},{17,1},{2,18},{18,2},{3,19},{19,3},{4,20},{20... | collective-permute-start | bytes 983048 | tf_op jit(solution)/shard_map/ppermute | solution.py:243
  74.6 1.1 %collective-permute-done.16.refs_1_ = bf16[32,4096]{1,0:T(8,128)(2,1)S(1)} collective-permute-done((bf16[32,4096]{1,0:T(8,128)(2,1)S(1)}, bf16[32,4096]{1,0:T(8,128)(2,1)S(1)}, u32[]{:S(2)}, u32[]{:S(2)}) %collective-permute-start.16) | collective-permute-done | bytes 262176 | tf_op jit(solution)/shard_map/ppermute | solution.py:243
  76.5 4.1 %collective-permute-done.14 = bf16[32,4096]{1,0:T(8,128)(2,1)S(1)} collective-permute-done((bf16[32,4096]{1,0:T(8,128)(2,1)S(1)}, bf16[32,4096]{1,0:T(8,128)(2,1)S(1)}, u32[]{:S(2)}, u32[]{:S(2)}) %collective-permute-start.14) | collective-permute-done | bytes 262176 | tf_op jit(solution)/shard_map/ppermute | solution.py:230
  81.7 2.1 %collective-permute-start.20 = (bf16[32,5120]{1,0:T(8,128)(2,1)S(1)}, bf16[32,5120]{1,0:T(8,128)(2,1)S(1)}, u32[]{:S(2)}, u32[]{:S(2)}) collective-permute-start(bf16[32,5120]{1,0:T(8,128)(2,1)S(1)} %broadcast_select_fusion.1.refs_0_), channel_id=1, source_target_pairs={{0,16},{16,0},{1,17},{17,1},{2,18},{18,2},{3,19},{19,3},{4,20},{20... | collective-permute-start | bytes 983048 | tf_op jit(solution)/shard_map/ppermute | solution.py:243
  84.7 1.6 %collective-permute-start.23 = (f32[1,64,256]{2,1,0:T(8,128)S(1)}, f32[1,64,256]{2,1,0:T(8,128)S(1)}, u32[]{:S(2)}, u32[]{:S(2)}) collective-permute-start(f32[1,64,256]{2,1,0:T(8,128)S(1)} %slice_bitcast_fusion.6), channel_id=1, source_target_pairs={{0,2},{1,3},{2,0},{3,1},{4,6},{5,7},{6,4},{7,5},{8,10},{9,11},{10,... | collective-permute-start | bytes 196616 | tf_op jit(solution)/shard_map/ppermute | solution.py:253
  86.3 7.8 %collective-permute-done.20.refs_1_ = bf16[32,5120]{1,0:T(8,128)(2,1)S(1)} collective-permute-done((bf16[32,5120]{1,0:T(8,128)(2,1)S(1)}, bf16[32,5120]{1,0:T(8,128)(2,1)S(1)}, u32[]{:S(2)}, u32[]{:S(2)}) %collective-permute-start.20) | collective-permute-done | bytes 327712 | tf_op jit(solution)/shard_map/ppermute | solution.py:243
  96.9 3.3 %collective-permute-done.24 = f32[64,256]{1,0:T(8,128)S(1)} collective-permute-done((f32[64,256]{1,0:T(8,128)S(1)}, f32[64,256]{1,0:T(8,128)S(1)}, u32[]{:S(2)}, u32[]{:S(2)}) %collective-permute-start.24) | collective-permute-done | bytes 65568 | tf_op jit(solution)/shard_map/ppermute | solution.py:325
  100.2 1.3 %collective-permute-done.25 = f32[2,64,256]{2,1,0:T(8,128)S(1)} collective-permute-done((f32[2,64,256]{2,1,0:T(8,128)S(1)}, f32[2,64,256]{2,1,0:T(8,128)S(1)}, u32[]{:S(2)}, u32[]{:S(2)}) %collective-permute-start.25) | collective-permute-done | bytes 131104 | tf_op jit(solution)/shard_map/ppermute | solution.py:253
  101.6 1.6 %collective-permute-start.26 = (f32[1,64,256]{2,1,0:T(8,128)S(1)}, f32[1,64,256]{2,1,0:T(8,128)S(1)}, u32[]{:S(2)}, u32[]{:S(2)}) collective-permute-start(f32[1,64,256]{2,1,0:T(8,128)S(1)} %slice_bitcast_fusion.4), channel_id=1, source_target_pairs={{0,2},{1,3},{2,0},{3,1},{4,6},{5,7},{6,4},{7,5},{8,10},{9,11},{10,... | collective-permute-start | bytes 196616 | tf_op jit(solution)/shard_map/ppermute | solution.py:253
  103.2 2.7 %collective-permute-done.26 = f32[1,64,256]{2,1,0:T(8,128)S(1)} collective-permute-done((f32[1,64,256]{2,1,0:T(8,128)S(1)}, f32[1,64,256]{2,1,0:T(8,128)S(1)}, u32[]{:S(2)}, u32[]{:S(2)}) %collective-permute-start.26) | collective-permute-done | bytes 65568 | tf_op jit(solution)/shard_map/ppermute | solution.py:253
  (66 shorter events, 14.7 us)
Async XLA Ops:
  1.1 11.6 %collective-permute-start.1 = (bf16[32,5120]{1,0:T(8,128)(2,1)S(1)}, bf16[32,5120]{1,0:T(8,128)(2,1)S(1)}, u32[]{:S(2)}, u32[]{:S(2)}) collective-permute-start(bf16[32,5120]{1,0:T(8,128)(2,1)S(1)} %slice_select_fusion.2), channel_id=1, source_target_pairs={{0,4},{4,0},{8,12},{12,8},{1,5},{5,1},{9,13},{13,9},{2,6},{6,2},{1... | collective-permute-start | bytes 983048 | tf_op jit(solution)/shard_map/ppermute | solution.py:230
  5.3 14.4 %collective-permute-start = (bf16[32,5120]{1,0:T(8,128)(2,1)S(1)}, bf16[32,5120]{1,0:T(8,128)(2,1)S(1)}, u32[]{:S(2)}, u32[]{:S(2)}) collective-permute-start(bf16[32,5120]{1,0:T(8,128)(2,1)S(1)} %slice_select_fusion.1), channel_id=1, source_target_pairs={{0,4},{4,0},{8,12},{12,8},{1,5},{5,1},{9,13},{13,9},{2,6},{6,2},{1... | collective-permute-start | bytes 983048 | tf_op jit(solution)/shard_map/ppermute | solution.py:230
  6.9 4.2 %copy-start = (bf16[64,16384]{1,0:T(8,128)(2,1)S(1)}, bf16[64,16384]{1,0:T(8,128)(2,1)}, u32[]{:S(2)}) copy-start(bf16[64,16384]{1,0:T(8,128)(2,1)} %test.2) | copy-start | bytes 6291460
  7.0 7.8 %copy-start.1 = (f32[16384]{0:T(1024)S(1)}, f32[16384]{0:T(1024)}, u32[]{:S(2)}) copy-start(f32[16384]{0:T(1024)} %param.5) | copy-start | bytes 196612
  7.0 29.0 %collective-permute-start.3 = (bf16[32,14336]{1,0:T(8,128)(2,1)S(1)}, bf16[32,14336]{1,0:T(8,128)(2,1)S(1)}, u32[]{:S(2)}, u32[]{:S(2)}) collective-permute-start(bf16[32,14336]{1,0:T(8,128)(2,1)S(1)} %slice_select_fusion), channel_id=1, source_target_pairs={{0,1},{1,0},{2,3},{3,2},{4,8},{5,9},{6,10},{7,11},{8,4},{9,5},{10,... | collective-permute-start | bytes 2752520 | tf_op jit(solution)/shard_map/ppermute | solution.py:234
  12.7 11.8 %collective-permute-start.2 = (bf16[32,4096]{1,0:T(8,128)(2,1)S(1)}, bf16[32,4096]{1,0:T(8,128)(2,1)S(1)}, u32[]{:S(2)}, u32[]{:S(2)}) collective-permute-start(bf16[32,4096]{1,0:T(8,128)(2,1)S(1)} %slice_select_fusion.3), channel_id=1, source_target_pairs={{0,4},{4,0},{8,12},{12,8},{1,5},{5,1},{9,13},{13,9},{2,6},{6,2},{1... | collective-permute-start | bytes 786440 | tf_op jit(solution)/shard_map/ppermute | solution.py:230
  17.3 10.7 %collective-permute-start.6 = (bf16[32,5120]{1,0:T(8,128)(2,1)S(1)}, bf16[32,5120]{1,0:T(8,128)(2,1)S(1)}, u32[]{:S(2)}, u32[]{:S(2)}) collective-permute-start(bf16[32,5120]{1,0:T(8,128)(2,1)S(1)} %collective-permute-done.1.refs_0_), channel_id=1, source_target_pairs={{0,16},{16,0},{1,17},{17,1},{2,18},{18,2},{3,19},{19,3},{4,20},{20... | collective-permute-start | bytes 983048 | tf_op jit(solution)/shard_map/ppermute | solution.py:243
  19.8 15.3 %collective-permute-start.9 = (bf16[32,5120]{1,0:T(8,128)(2,1)S(1)}, bf16[32,5120]{1,0:T(8,128)(2,1)S(1)}, u32[]{:S(2)}, u32[]{:S(2)}) collective-permute-start(bf16[32,5120]{1,0:T(8,128)(2,1)S(1)} %collective-permute-done.refs_0_), channel_id=1, source_target_pairs={{0,16},{16,0},{1,17},{17,1},{2,18},{18,2},{3,19},{19,3},{4,20},{20... | collective-permute-start | bytes 983048 | tf_op jit(solution)/shard_map/ppermute | solution.py:243
  28.0 10.2 %collective-permute-start.8 = (bf16[32,4096]{1,0:T(8,128)(2,1)S(1)}, bf16[32,4096]{1,0:T(8,128)(2,1)S(1)}, u32[]{:S(2)}, u32[]{:S(2)}) collective-permute-start(bf16[32,4096]{1,0:T(8,128)(2,1)S(1)} %collective-permute-done.2.refs_0_), channel_id=1, source_target_pairs={{0,16},{16,0},{1,17},{17,1},{2,18},{18,2},{3,19},{19,3},{4,20},{20... | collective-permute-start | bytes 786440 | tf_op jit(solution)/shard_map/ppermute | solution.py:243
  36.0 9.9 %collective-permute-start.12 = (bf16[32,5120]{1,0:T(8,128)(2,1)S(1)}, bf16[32,5120]{1,0:T(8,128)(2,1)S(1)}, u32[]{:S(2)}, u32[]{:S(2)}) collective-permute-start(bf16[32,5120]{1,0:T(8,128)(2,1)S(1)} %broadcast_select_fusion.4), channel_id=1, source_target_pairs={{0,4},{4,0},{8,12},{12,8},{1,5},{5,1},{9,13},{13,9},{2,6},{6,2},{1... | collective-permute-start | bytes 983048 | tf_op jit(solution)/shard_map/ppermute | solution.py:230
  36.1 12.0 %collective-permute-start.4 = (bf16[32,5120]{1,0:T(8,128)(2,1)S(1)}, bf16[32,5120]{1,0:T(8,128)(2,1)S(1)}, u32[]{:S(2)}, u32[]{:S(2)}) collective-permute-start(bf16[32,5120]{1,0:T(8,128)(2,1)S(1)} %collective-permute-done.1.refs_0_), channel_id=1, source_target_pairs={{0,1},{1,0},{2,3},{3,2},{4,8},{5,9},{6,10},{7,11},{8,4},{9,5},{10,... | collective-permute-start | bytes 983048 | tf_op jit(solution)/shard_map/ppermute | solution.py:234
  45.9 7.5 %collective-permute-start.15 = (bf16[32,4096]{1,0:T(8,128)(2,1)S(1)}, bf16[32,4096]{1,0:T(8,128)(2,1)S(1)}, u32[]{:S(2)}, u32[]{:S(2)}) collective-permute-start(bf16[32,4096]{1,0:T(8,128)(2,1)S(1)} %broadcast_select_fusion.9), channel_id=1, source_target_pairs={{0,4},{4,0},{8,12},{12,8},{1,5},{5,1},{9,13},{13,9},{2,6},{6,2},{1... | collective-permute-start | bytes 786440 | tf_op jit(solution)/shard_map/ppermute | solution.py:230
  46.0 15.4 %collective-permute-start.13 = (bf16[32,5120]{1,0:T(8,128)(2,1)S(1)}, bf16[32,5120]{1,0:T(8,128)(2,1)S(1)}, u32[]{:S(2)}, u32[]{:S(2)}) collective-permute-start(bf16[32,5120]{1,0:T(8,128)(2,1)S(1)} %get-tuple-element.52.refs_0_), channel_id=1, source_target_pairs={{0,16},{16,0},{1,17},{17,1},{2,18},{18,2},{3,19},{19,3},{4,20},{20... | collective-permute-start | bytes 983048 | tf_op jit(solution)/shard_map/ppermute | solution.py:243
  48.0 14.4 %collective-permute-start.5 = (bf16[32,9216]{1,0:T(8,128)(2,1)S(1)}, bf16[32,9216]{1,0:T(8,128)(2,1)S(1)}, u32[]{:S(2)}, u32[]{:S(2)}) collective-permute-start(bf16[32,9216]{1,0:T(8,128)(2,1)S(1)} %pad_maximum_fusion), channel_id=1, source_target_pairs={{0,1},{1,0},{2,3},{3,2},{4,8},{5,9},{6,10},{7,11},{8,4},{9,5},{10,... | collective-permute-start | bytes 1769480 | tf_op jit(solution)/shard_map/ppermute | solution.py:234
  48.1 11.3 %collective-permute-start.7 = (bf16[32,5120]{1,0:T(8,128)(2,1)S(1)}, bf16[32,5120]{1,0:T(8,128)(2,1)S(1)}, u32[]{:S(2)}, u32[]{:S(2)}) collective-permute-start(bf16[32,5120]{1,0:T(8,128)(2,1)S(1)} %get-tuple-element.46), channel_id=1, source_target_pairs={{0,4},{4,0},{8,12},{12,8},{1,5},{5,1},{9,13},{13,9},{2,6},{6,2},{1... | collective-permute-start | bytes 983048 | tf_op jit(solution)/shard_map/ppermute | solution.py:230
  59.3 11.7 %collective-permute-start.10 = (bf16[32,5120]{1,0:T(8,128)(2,1)S(1)}, bf16[32,5120]{1,0:T(8,128)(2,1)S(1)}, u32[]{:S(2)}, u32[]{:S(2)}) collective-permute-start(bf16[32,5120]{1,0:T(8,128)(2,1)S(1)} %broadcast_select_fusion.7), channel_id=1, source_target_pairs={{0,4},{4,0},{8,12},{12,8},{1,5},{5,1},{9,13},{13,9},{2,6},{6,2},{1... | collective-permute-start | bytes 983048 | tf_op jit(solution)/shard_map/ppermute | solution.py:230
  59.4 10.7 %collective-permute-start.11 = (bf16[32,5120]{1,0:T(8,128)(2,1)S(1)}, bf16[32,5120]{1,0:T(8,128)(2,1)S(1)}, u32[]{:S(2)}, u32[]{:S(2)}) collective-permute-start(bf16[32,5120]{1,0:T(8,128)(2,1)S(1)} %broadcast_select_fusion.5.refs_0_), channel_id=1, source_target_pairs={{0,16},{16,0},{1,17},{17,1},{2,18},{18,2},{3,19},{19,3},{4,20},{20... | collective-permute-start | bytes 983048 | tf_op jit(solution)/shard_map/ppermute | solution.py:243
  61.4 14.3 %collective-permute-start.16 = (bf16[32,4096]{1,0:T(8,128)(2,1)S(1)}, bf16[32,4096]{1,0:T(8,128)(2,1)S(1)}, u32[]{:S(2)}, u32[]{:S(2)}) collective-permute-start(bf16[32,4096]{1,0:T(8,128)(2,1)S(1)} %broadcast_select_fusion.8.refs_0_), channel_id=1, source_target_pairs={{0,16},{16,0},{1,17},{17,1},{2,18},{18,2},{3,19},{19,3},{4,20},{20... | collective-permute-start | bytes 786440 | tf_op jit(solution)/shard_map/ppermute | solution.py:243
  62.5 18.3 %collective-permute-start.19 = (bf16[32,5120]{1,0:T(8,128)(2,1)S(1)}, bf16[32,5120]{1,0:T(8,128)(2,1)S(1)}, u32[]{:S(2)}, u32[]{:S(2)}) collective-permute-start(bf16[32,5120]{1,0:T(8,128)(2,1)S(1)} %broadcast_select_fusion.2), channel_id=1, source_target_pairs={{0,4},{4,0},{8,12},{12,8},{1,5},{5,1},{9,13},{13,9},{2,6},{6,2},{1... | collective-permute-start | bytes 983048 | tf_op jit(solution)/shard_map/ppermute | solution.py:230
  64.5 16.2 %collective-permute-start.18 = (bf16[64,4096]{1,0:T(8,128)(2,1)S(1)}, bf16[64,4096]{1,0:T(8,128)(2,1)S(1)}, u32[]{:S(2)}, u32[]{:S(2)}) collective-permute-start(bf16[64,4096]{1,0:T(8,128)(2,1)S(1)} %pad_maximum_fusion.1), channel_id=1, source_target_pairs={{0,1},{1,0},{2,3},{3,2},{4,8},{5,9},{6,10},{7,11},{8,4},{9,5},{10,... | collective-permute-start | bytes 1572872 | tf_op jit(solution)/shard_map/ppermute | solution.py:234
  71.0 9.6 %collective-permute-start.14 = (bf16[32,4096]{1,0:T(8,128)(2,1)S(1)}, bf16[32,4096]{1,0:T(8,128)(2,1)S(1)}, u32[]{:S(2)}, u32[]{:S(2)}) collective-permute-start(bf16[32,4096]{1,0:T(8,128)(2,1)S(1)} %slice.104), channel_id=1, source_target_pairs={{0,4},{4,0},{8,12},{12,8},{1,5},{5,1},{9,13},{13,9},{2,6},{6,2},{1... | collective-permute-start | bytes 786440 | tf_op jit(solution)/shard_map/ppermute | solution.py:230
  73.1 10.6 %collective-permute-start.21 = (bf16[32,5120]{1,0:T(8,128)(2,1)S(1)}, bf16[32,5120]{1,0:T(8,128)(2,1)S(1)}, u32[]{:S(2)}, u32[]{:S(2)}) collective-permute-start(bf16[32,5120]{1,0:T(8,128)(2,1)S(1)} %broadcast_select_fusion.refs_0_), channel_id=1, source_target_pairs={{0,16},{16,0},{1,17},{17,1},{2,18},{18,2},{3,19},{19,3},{4,20},{20... | collective-permute-start | bytes 983048 | tf_op jit(solution)/shard_map/ppermute | solution.py:243
  80.6 14.4 %collective-permute-start.17 = (bf16[32,4096]{1,0:T(8,128)(2,1)S(1)}, bf16[32,4096]{1,0:T(8,128)(2,1)S(1)}, u32[]{:S(2)}, u32[]{:S(2)}) collective-permute-start(bf16[32,4096]{1,0:T(8,128)(2,1)S(1)} %broadcast_select_fusion.10.refs_0_), channel_id=1, source_target_pairs={{0,16},{16,0},{1,17},{17,1},{2,18},{18,2},{3,19},{19,3},{4,20},{20... | collective-permute-start | bytes 786440 | tf_op jit(solution)/shard_map/ppermute | solution.py:243
  81.6 3.1 %collective-permute-start.22 = (f32[2,64,256]{2,1,0:T(8,128)S(1)}, f32[2,64,256]{2,1,0:T(8,128)S(1)}, u32[]{:S(2)}, u32[]{:S(2)}) collective-permute-start(f32[2,64,256]{2,1,0:T(8,128)S(1)} %slice_bitcast_fusion), channel_id=1, source_target_pairs={{0,1},{1,0},{2,3},{3,2},{4,5},{5,4},{6,7},{7,6},{8,9},{9,8},{10,11... | collective-permute-start | bytes 393224 | tf_op jit(solution)/shard_map/ppermute | solution.py:253
  81.7 12.4 %collective-permute-start.20 = (bf16[32,5120]{1,0:T(8,128)(2,1)S(1)}, bf16[32,5120]{1,0:T(8,128)(2,1)S(1)}, u32[]{:S(2)}, u32[]{:S(2)}) collective-permute-start(bf16[32,5120]{1,0:T(8,128)(2,1)S(1)} %broadcast_select_fusion.1.refs_0_), channel_id=1, source_target_pairs={{0,16},{16,0},{1,17},{17,1},{2,18},{18,2},{3,19},{19,3},{4,20},{20... | collective-permute-start | bytes 983048 | tf_op jit(solution)/shard_map/ppermute | solution.py:243
  84.7 11.1 %collective-permute-start.23 = (f32[1,64,256]{2,1,0:T(8,128)S(1)}, f32[1,64,256]{2,1,0:T(8,128)S(1)}, u32[]{:S(2)}, u32[]{:S(2)}) collective-permute-start(f32[1,64,256]{2,1,0:T(8,128)S(1)} %slice_bitcast_fusion.6), channel_id=1, source_target_pairs={{0,2},{1,3},{2,0},{3,1},{4,6},{5,7},{6,4},{7,5},{8,10},{9,11},{10,... | collective-permute-start | bytes 196616 | tf_op jit(solution)/shard_map/ppermute | solution.py:253
  95.9 4.3 %collective-permute-start.24 = (f32[64,256]{1,0:T(8,128)S(1)}, f32[64,256]{1,0:T(8,128)S(1)}, u32[]{:S(2)}, u32[]{:S(2)}) collective-permute-start(f32[64,256]{1,0:T(8,128)S(1)} %fusion.9), channel_id=1, source_target_pairs={{0,4},{4,0},{8,12},{12,8},{1,5},{5,1},{9,13},{13,9},{2,6},{6,2},{1... | collective-permute-start | bytes 196616 | tf_op jit(solution)/shard_map/ppermute | solution.py:325
  100.2 1.3 %collective-permute-start.25 = (f32[2,64,256]{2,1,0:T(8,128)S(1)}, f32[2,64,256]{2,1,0:T(8,128)S(1)}, u32[]{:S(2)}, u32[]{:S(2)}) collective-permute-start(f32[2,64,256]{2,1,0:T(8,128)S(1)} %slice_bitcast_fusion.2), channel_id=1, source_target_pairs={{0,1},{1,0},{2,3},{3,2},{4,5},{5,4},{6,7},{7,6},{8,9},{9,8},{10,11... | collective-permute-start | bytes 393224 | tf_op jit(solution)/shard_map/ppermute | solution.py:253
  101.6 4.3 %collective-permute-start.26 = (f32[1,64,256]{2,1,0:T(8,128)S(1)}, f32[1,64,256]{2,1,0:T(8,128)S(1)}, u32[]{:S(2)}, u32[]{:S(2)}) collective-permute-start(f32[1,64,256]{2,1,0:T(8,128)S(1)} %slice_bitcast_fusion.4), channel_id=1, source_target_pairs={{0,2},{1,3},{2,0},{3,1},{4,6},{5,7},{6,4},{7,5},{8,10},{9,11},{10,... | collective-permute-start | bytes 196616 | tf_op jit(solution)/shard_map/ppermute | solution.py:253

commit v23 on v22

--- a/solution.py
+++ b/solution.py
@@ -67,7 +67,7 @@
         out[to * half : (to + 1) * half, :] = kept[pl.ds(at, half), :]
 
 
-LINE, SHIP = (5, 5, 4), 2
+LINE, SHIP = (5, 5, 5), 1
 KEPT = ((0, 1, 2, 3), (1, 0, 2, 3), (2, 3, 1, 0), (3, 2, 1, 0))
 
 
@@ -226,7 +226,7 @@
                 middle_pairs.append((i * n_feat + f, to[0] * n_feat + to[1]))
 
         def outer(name, block):
-            waits = outs[-2:-1] + swaps[-4:-3] + made[-4:-3] + (first if len(outs) == 3 else [])
+            waits = outs[-2:-1] + swaps[-3:-2] + made[-4:-3] + (first if len(outs) == 3 else [])
             outs.append(lax.ppermute(after(block, *waits), "ex", outer_pairs))
             done[name] = outs[-1]
 
@@ -265,13 +265,12 @@
         mine = []
         for start, count in zip(firsts, LINE):
             mine.append(share(after(test, *mine[-1:]), start, count))
-        every = share(after(test, mine[0]), 0, sum(LINE))
         trains = [train[:, q * 4 * unit : (q + 1) * 4 * unit] for q in range(4)]
         own = call(
             functools.partial(line_own_kernel, unit), queries, docs, feats, [test, scale, *trains]
         )
         first = [own]
-        widths = [*LINE, *LINE[:2]]
+        widths = LINE[:2]
         shapes = [jax.ShapeDtypeStruct((half, w * unit), test.dtype) for w in widths]
         shapes.append(jax.ShapeDtypeStruct((half, n_grp * SHIP * unit), test.dtype))
         *cargo, own_tests = call(
@@ -296,26 +295,21 @@
 
         for c in range(n):
             outer(f"E1{c}", mine[c])
-            if c == 0:
-                middle("O1", every)
+            middle(f"O1{c}", mine[c])
             finish(1, c, done[f"E1{c}"])
-        middle("O20", done["E10"])
         for c in range(n):
-            inner = done["O1"][:, columns[c]]
-            outer(f"E2{c}", jnp.where(is_end, cargo[c], inner))
-            if c == 0:
-                middle("O21", jnp.concatenate([done["E11"], done["E12"]], axis=1))
+            inner = done[f"O1{c}"]
+            outer(f"E2{c}", jnp.where(is_end, cargo[c], inner) if c < len(cargo) else inner)
+            middle(f"O2{c}", done[f"E1{c}"])
             finish(2, c, jnp.where(is_end, done[f"E2{c}"], inner))
         end_tests = done["E20"][:, : own_tests.shape[1]]
         middle("OS", jnp.concatenate([own_tests, end_tests], axis=0))
         for c in range(n):
-            inner = done["O20"] if c == 0 else done["O21"]
-            if c > 0:
-                inner = inner[:, columns[c].start - columns[1].start : columns[c].stop - columns[1].start]
-            outer(f"E3{c}", jnp.where(is_end, cargo[3 + c], inner) if c < 2 else inner)
+            inner = done[f"O2{c}"]
+            outer(f"E3{c}", inner)
             last = finish(3, c, jnp.where(is_end, done[f"E3{c}"], inner))
         shape = jax.ShapeDtypeStruct((n_ex * queries, docs), jnp.float32)
-        landed = [done[name] for name in ("E20", "E21", "E22", "E30", "E31")]
+        landed = [done["E20"], done["E21"]]
         near, far = call(
             functools.partial(shipped_kernel, n_grp, n_feat, unit, len(landed)),
             n_ex * queries, docs, 2 * SHIP * unit,

time: 107 us -> 94.5 us (0.88)
  waiting for transfers between devices: 56.6 us -> 38.6 us
  starting transfers between devices: 29.5 us -> 34.9 us
    ppermute x9, waiting for transfers between devices: 24.8 us -> 5.98 us  [outer(): outs.append(lax.ppermute(after(block, *waits), 'ex', outer_pairs))]
    ppermute x9, starting transfers between devices: 12.2 us -> 17.2 us  [outer(): outs.append(lax.ppermute(after(block, *waits), 'ex', outer_pairs))]
    ppermute x1, waiting for transfers between devices: 3.26 us -> 0.01 us  [line(): back = lax.ppermute(sum_over_feat(far), 'ex', outer_pairs)]
    ppermute x9, waiting for transfers between devices: 24.6 us -> 27.5 us  [swap(): swaps.append(lax.ppermute(after(block, *waits), 'grp', [(0, 1), (1, 0)]))]
    select_n x4 -> x3, other arithmetic: 3.8 us -> 3.32 us  [share(): return jnp.where(first_grp, rows[:half, here], rows[half:, here])]
  transfers between devices with their start and end apart: 27 -> 30, of which waited for: 16 -> 13; matrix products, arithmetic and copies ran while one was open for 7% -> 7% of each run, Pallas kernels for 10% -> 12%
where the time goes in v23:
time: 94.5 us; the launch traced here: 94.3 us
  waiting for transfers between devices  38.6 us (41%)
  starting transfers between devices  34.9 us (37%)
  Pallas kernels  11.3 us (12%)
  local copies, waits for them, and re-layouts  4.9 us (5%)
  other arithmetic  4.33 us (5%)
    ppermute x9, waiting for transfers between devices, swap(): swaps.append(lax.ppermute(after(block, *waits), 'grp', [(0, 1), (1, 0)]))  27.5 us
    ppermute x9, starting transfers between devices, outer(): outs.append(lax.ppermute(after(block, *waits), 'ex', outer_pairs))  17.2 us
    ppermute x9, starting transfers between devices, swap(): swaps.append(lax.ppermute(after(block, *waits), 'grp', [(0, 1), (1, 0)]))  13.7 us
    pallas_call x12, Pallas kernels, call(): pl.pallas_call(kernel, out_shape=shapes or jax.ShapeDtypeStruct((rows, do...  11.3 us
    ppermute x9, waiting for transfers between devices, outer(): outs.append(lax.ppermute(after(block, *waits), 'ex', outer_pairs))  5.98 us
    ppermute x4, waiting for transfers between devices, sum_over_feat(): held, waits = (pairs[:, 0] + lax.ppermute(send, 'feat', partner), ())  5.06 us
    slice x1, local copies, waits for them, and re-layouts, line(): trains = [train[:, q * 4 * unit:(q + 1) * 4 * unit] for q in range(4)]  4.08 us
    select_n x3, other arithmetic, share(): return jnp.where(first_grp, rows[:half, here], rows[half:, here])  3.32 us
  transfers between devices with their start and end apart: 30, of which 13 were waited for; matrix products, arithmetic and copies ran while one was open for 7% of the time, Pallas kernels for 12%

profile of v23, /device:TPU:0, one launch (start us, length us, event | category | flops | bytes accessed | tf_op | source)
XLA Modules:
  0.0 94.3 jit_solution(10698277942003155205)
XLA Ops:
  1.1 3.1 %collective-permute-start = (bf16[32,5120]{1,0:T(8,128)(2,1)S(1)}, bf16[32,5120]{1,0:T(8,128)(2,1)S(1)}, u32[]{:S(2)}, u32[]{:S(2)}) collective-permute-start(bf16[32,5120]{1,0:T(8,128)(2,1)S(1)} %slice_select_fusion.2), channel_id=1, source_target_pairs={{0,4},{4,0},{8,12},{12,8},{1,5},{5,1},{9,13},{13,9},{2,6},{6,2},{1... | collective-permute-start | bytes 983048 | tf_op jit(solution)/shard_map/ppermute | solution.py:230
  4.2 1.1 %slice_select_fusion.1 = bf16[32,5120]{1,0:T(8,128)(2,1)S(1)} fusion(bf16[64,16384]{1,0:T(8,128)(2,1)} %test.2, pred[]{:T(512)S(6)} %eq.11), kind=kLoop, calls=%fused_computation.1 | loop fusion | flops 163840 | bytes 983041 | tf_op jit(solution)/shard_map/jit(_where)/select_n | solution.py:261
  5.3 3.2 %collective-permute-start.2 = (bf16[32,5120]{1,0:T(8,128)(2,1)S(1)}, bf16[32,5120]{1,0:T(8,128)(2,1)S(1)}, u32[]{:S(2)}, u32[]{:S(2)}) collective-permute-start(bf16[32,5120]{1,0:T(8,128)(2,1)S(1)} %slice_select_fusion.1), channel_id=1, source_target_pairs={{0,4},{4,0},{8,12},{12,8},{1,5},{5,1},{9,13},{13,9},{2,6},{6,2},{1... | collective-permute-start | bytes 983048 | tf_op jit(solution)/shard_map/ppermute | solution.py:230
  9.7 4.1 %fusion.10 = (bf16[256,4096]{1,0:T(8,128)(2,1)S(1)}, bf16[256,4096]{1,0:T(8,128)(2,1)S(1)}, bf16[256,4096]{1,0:T(8,128)(2,1)S(1)}, bf16[256,4096]{1,0:T(8,128)(2,1)S(1)}) fusion(bf16[256,16384]{1,0:T(8,128)(2,1)} %param.3), kind=kLoop, calls=%fused_computation.31 | loop fusion | bytes 16777216 | tf_op jit(solution)/shard_map/slice | solution.py:268
  14.6 2.5 %shard_map.39.refs_6_ = f32[64,256]{1,0:T(8,128)S(1)} custom-call(bf16[64,16384]{1,0:T(8,128)(2,1)S(1)} %copy-done, f32[1,16384]{1,0:T(1,128)S(1)} %bitcast.61, bf16[256,4096]{1,0:T(8,128)(2,1)S(1)} %get-tuple-element.68.refs_3_.refs_0_, bf16[256,4096]{1,0:T(8,128)(2,1)S(1)} %get-tuple-element.70.refs_4_.refs_1_.refs_3_, ...), custom_call_target="tpu_custom_call" | custom-call | flops 536870912 | bytes 10485760 | tf_op jit(solution)/shard_map/pallas_call | solution.py:191
  17.3 1.6 %collective-permute-start.10 = (bf16[32,5120]{1,0:T(8,128)(2,1)S(1)}, bf16[32,5120]{1,0:T(8,128)(2,1)S(1)}, u32[]{:S(2)}, u32[]{:S(2)}) collective-permute-start(bf16[32,5120]{1,0:T(8,128)(2,1)S(1)} %collective-permute-done.refs_0_), channel_id=1, source_target_pairs={{0,16},{16,0},{1,17},{17,1},{2,18},{18,2},{3,19},{19,3},{4,20},{20... | collective-permute-start | bytes 983048 | tf_op jit(solution)/shard_map/ppermute | solution.py:243
  19.3 1.5 %collective-permute-start.9 = (bf16[32,5120]{1,0:T(8,128)(2,1)S(1)}, bf16[32,5120]{1,0:T(8,128)(2,1)S(1)}, u32[]{:S(2)}, u32[]{:S(2)}) collective-permute-start(bf16[32,5120]{1,0:T(8,128)(2,1)S(1)} %collective-permute-done.2.refs_0_), channel_id=1, source_target_pairs={{0,16},{16,0},{1,17},{17,1},{2,18},{18,2},{3,19},{19,3},{4,20},{20... | collective-permute-start | bytes 983048 | tf_op jit(solution)/shard_map/ppermute | solution.py:243
  21.0 6.9 %collective-permute-done.10.refs_1_ = bf16[32,5120]{1,0:T(8,128)(2,1)S(1)} collective-permute-done((bf16[32,5120]{1,0:T(8,128)(2,1)S(1)}, bf16[32,5120]{1,0:T(8,128)(2,1)S(1)}, u32[]{:S(2)}, u32[]{:S(2)}) %collective-permute-start.10) | collective-permute-done | bytes 327712 | tf_op jit(solution)/shard_map/ppermute | solution.py:243
  27.9 2.0 %collective-permute-start.12 = (bf16[32,5120]{1,0:T(8,128)(2,1)S(1)}, bf16[32,5120]{1,0:T(8,128)(2,1)S(1)}, u32[]{:S(2)}, u32[]{:S(2)}) collective-permute-start(bf16[32,5120]{1,0:T(8,128)(2,1)S(1)} %broadcast_select_fusion.6), channel_id=1, source_target_pairs={{0,4},{4,0},{8,12},{12,8},{1,5},{5,1},{9,13},{13,9},{2,6},{6,2},{1... | collective-permute-start | bytes 983048 | tf_op jit(solution)/shard_map/ppermute | solution.py:230
  30.8 3.6 %collective-permute-done.9.refs_1_ = bf16[32,5120]{1,0:T(8,128)(2,1)S(1)} collective-permute-done((bf16[32,5120]{1,0:T(8,128)(2,1)S(1)}, bf16[32,5120]{1,0:T(8,128)(2,1)S(1)}, u32[]{:S(2)}, u32[]{:S(2)}) %collective-permute-start.9) | collective-permute-done | bytes 327712 | tf_op jit(solution)/shard_map/ppermute | solution.py:243
  34.6 1.5 %collective-permute-start.14 = (bf16[32,5120]{1,0:T(8,128)(2,1)S(1)}, bf16[32,5120]{1,0:T(8,128)(2,1)S(1)}, u32[]{:S(2)}, u32[]{:S(2)}) collective-permute-start(bf16[32,5120]{1,0:T(8,128)(2,1)S(1)} %collective-permute-done.1.refs_0_), channel_id=1, source_target_pairs={{0,16},{16,0},{1,17},{17,1},{2,18},{18,2},{3,19},{19,3},{4,20},{20... | collective-permute-start | bytes 983048 | tf_op jit(solution)/shard_map/ppermute | solution.py:243
  37.1 1.2 %collective-permute-start.13 = (bf16[32,5120]{1,0:T(8,128)(2,1)S(1)}, bf16[32,5120]{1,0:T(8,128)(2,1)S(1)}, u32[]{:S(2)}, u32[]{:S(2)}) collective-permute-start(bf16[32,5120]{1,0:T(8,128)(2,1)S(1)} %broadcast_select_fusion.5.refs_0_), channel_id=1, source_target_pairs={{0,16},{16,0},{1,17},{17,1},{2,18},{18,2},{3,19},{19,3},{4,20},{20... | collective-permute-start | bytes 983048 | tf_op jit(solution)/shard_map/ppermute | solution.py:243
  38.3 6.9 %collective-permute-done.14.refs_1_ = bf16[32,5120]{1,0:T(8,128)(2,1)S(1)} collective-permute-done((bf16[32,5120]{1,0:T(8,128)(2,1)S(1)}, bf16[32,5120]{1,0:T(8,128)(2,1)S(1)}, u32[]{:S(2)}, u32[]{:S(2)}) %collective-permute-start.14) | collective-permute-done | bytes 327712 | tf_op jit(solution)/shard_map/ppermute | solution.py:243
  45.2 1.9 %collective-permute-start.16 = (bf16[32,5120]{1,0:T(8,128)(2,1)S(1)}, bf16[32,5120]{1,0:T(8,128)(2,1)S(1)}, u32[]{:S(2)}, u32[]{:S(2)}) collective-permute-start(bf16[32,5120]{1,0:T(8,128)(2,1)S(1)} %collective-permute-done.5), channel_id=1, source_target_pairs={{0,4},{4,0},{8,12},{12,8},{1,5},{5,1},{9,13},{13,9},{2,6},{6,2},{1... | collective-permute-start | bytes 983048 | tf_op jit(solution)/shard_map/ppermute | solution.py:230
  47.1 1.6 %collective-permute-start.18 = (bf16[32,5120]{1,0:T(8,128)(2,1)S(1)}, bf16[32,5120]{1,0:T(8,128)(2,1)S(1)}, u32[]{:S(2)}, u32[]{:S(2)}) collective-permute-start(bf16[32,5120]{1,0:T(8,128)(2,1)S(1)} %broadcast_select_fusion.3.refs_0_), channel_id=1, source_target_pairs={{0,16},{16,0},{1,17},{17,1},{2,18},{18,2},{3,19},{19,3},{4,20},{20... | collective-permute-start | bytes 983048 | tf_op jit(solution)/shard_map/ppermute | solution.py:243
  49.8 2.5 %collective-permute-done.13.refs_1_ = bf16[32,5120]{1,0:T(8,128)(2,1)S(1)} collective-permute-done((bf16[32,5120]{1,0:T(8,128)(2,1)S(1)}, bf16[32,5120]{1,0:T(8,128)(2,1)S(1)}, u32[]{:S(2)}, u32[]{:S(2)}) %collective-permute-start.13) | collective-permute-done | bytes 327712 | tf_op jit(solution)/shard_map/ppermute | solution.py:243
  52.2 1.9 %collective-permute-start.15 = (bf16[32,5120]{1,0:T(8,128)(2,1)S(1)}, bf16[32,5120]{1,0:T(8,128)(2,1)S(1)}, u32[]{:S(2)}, u32[]{:S(2)}) collective-permute-start(bf16[32,5120]{1,0:T(8,128)(2,1)S(1)} %collective-permute-done.6), channel_id=1, source_target_pairs={{0,4},{4,0},{8,12},{12,8},{1,5},{5,1},{9,13},{13,9},{2,6},{6,2},{1... | collective-permute-start | bytes 983048 | tf_op jit(solution)/shard_map/ppermute | solution.py:230
  54.2 1.6 %collective-permute-start.17 = (bf16[32,5120]{1,0:T(8,128)(2,1)S(1)}, bf16[32,5120]{1,0:T(8,128)(2,1)S(1)}, u32[]{:S(2)}, u32[]{:S(2)}) collective-permute-start(bf16[32,5120]{1,0:T(8,128)(2,1)S(1)} %broadcast_select_fusion.4.refs_0_), channel_id=1, source_target_pairs={{0,16},{16,0},{1,17},{17,1},{2,18},{18,2},{3,19},{19,3},{4,20},{20... | collective-permute-start | bytes 983048 | tf_op jit(solution)/shard_map/ppermute | solution.py:243
  56.7 2.6 %collective-permute-done.18.refs_1_ = bf16[32,5120]{1,0:T(8,128)(2,1)S(1)} collective-permute-done((bf16[32,5120]{1,0:T(8,128)(2,1)S(1)}, bf16[32,5120]{1,0:T(8,128)(2,1)S(1)}, u32[]{:S(2)}, u32[]{:S(2)}) %collective-permute-start.18) | collective-permute-done | bytes 327712 | tf_op jit(solution)/shard_map/ppermute | solution.py:243
  60.3 2.2 %collective-permute-start.22 = (bf16[32,5120]{1,0:T(8,128)(2,1)S(1)}, bf16[32,5120]{1,0:T(8,128)(2,1)S(1)}, u32[]{:S(2)}, u32[]{:S(2)}) collective-permute-start(bf16[32,5120]{1,0:T(8,128)(2,1)S(1)} %collective-permute-done.7), channel_id=1, source_target_pairs={{0,4},{4,0},{8,12},{12,8},{1,5},{5,1},{9,13},{13,9},{2,6},{6,2},{1... | collective-permute-start | bytes 983048 | tf_op jit(solution)/shard_map/ppermute | solution.py:230
  62.5 1.6 %collective-permute-start.24 = (bf16[32,5120]{1,0:T(8,128)(2,1)S(1)}, bf16[32,5120]{1,0:T(8,128)(2,1)S(1)}, u32[]{:S(2)}, u32[]{:S(2)}) collective-permute-start(bf16[32,5120]{1,0:T(8,128)(2,1)S(1)} %broadcast_select_fusion.refs_0_), channel_id=1, source_target_pairs={{0,16},{16,0},{1,17},{17,1},{2,18},{18,2},{3,19},{19,3},{4,20},{20... | collective-permute-start | bytes 983048 | tf_op jit(solution)/shard_map/ppermute | solution.py:243
  64.1 1.9 %collective-permute-done.17.refs_1_ = bf16[32,5120]{1,0:T(8,128)(2,1)S(1)} collective-permute-done((bf16[32,5120]{1,0:T(8,128)(2,1)S(1)}, bf16[32,5120]{1,0:T(8,128)(2,1)S(1)}, u32[]{:S(2)}, u32[]{:S(2)}) %collective-permute-start.17) | collective-permute-done | bytes 327712 | tf_op jit(solution)/shard_map/ppermute | solution.py:243
  66.9 2.7 %collective-permute-start.19 = (bf16[32,5120]{1,0:T(8,128)(2,1)S(1)}, bf16[32,5120]{1,0:T(8,128)(2,1)S(1)}, u32[]{:S(2)}, u32[]{:S(2)}) collective-permute-start(bf16[32,5120]{1,0:T(8,128)(2,1)S(1)} %collective-permute-done.8), channel_id=1, source_target_pairs={{0,4},{4,0},{8,12},{12,8},{1,5},{5,1},{9,13},{13,9},{2,6},{6,2},{1... | collective-permute-start | bytes 983048 | tf_op jit(solution)/shard_map/ppermute | solution.py:230
  69.6 1.4 %collective-permute-done.22 = bf16[32,5120]{1,0:T(8,128)(2,1)S(1)} collective-permute-done((bf16[32,5120]{1,0:T(8,128)(2,1)S(1)}, bf16[32,5120]{1,0:T(8,128)(2,1)S(1)}, u32[]{:S(2)}, u32[]{:S(2)}) %collective-permute-start.22) | collective-permute-done | bytes 327712 | tf_op jit(solution)/shard_map/ppermute | solution.py:230
  71.0 1.6 %collective-permute-start.23 = (bf16[32,5120]{1,0:T(8,128)(2,1)S(1)}, bf16[32,5120]{1,0:T(8,128)(2,1)S(1)}, u32[]{:S(2)}, u32[]{:S(2)}) collective-permute-start(bf16[32,5120]{1,0:T(8,128)(2,1)S(1)} %broadcast_select_fusion.1.refs_0_), channel_id=1, source_target_pairs={{0,16},{16,0},{1,17},{17,1},{2,18},{18,2},{3,19},{19,3},{4,20},{20... | collective-permute-start | bytes 983048 | tf_op jit(solution)/shard_map/ppermute | solution.py:243
  73.3 4.1 %collective-permute-done.19 = bf16[32,5120]{1,0:T(8,128)(2,1)S(1)} collective-permute-done((bf16[32,5120]{1,0:T(8,128)(2,1)S(1)}, bf16[32,5120]{1,0:T(8,128)(2,1)S(1)}, u32[]{:S(2)}, u32[]{:S(2)}) %collective-permute-start.19) | collective-permute-done | bytes 327712 | tf_op jit(solution)/shard_map/ppermute | solution.py:230
  77.4 1.6 %collective-permute-start.20 = (bf16[32,5120]{1,0:T(8,128)(2,1)S(1)}, bf16[32,5120]{1,0:T(8,128)(2,1)S(1)}, u32[]{:S(2)}, u32[]{:S(2)}) collective-permute-start(bf16[32,5120]{1,0:T(8,128)(2,1)S(1)} %broadcast_select_fusion.2.refs_0_), channel_id=1, source_target_pairs={{0,16},{16,0},{1,17},{17,1},{2,18},{18,2},{3,19},{19,3},{4,20},{20... | collective-permute-start | bytes 983048 | tf_op jit(solution)/shard_map/ppermute | solution.py:243
  79.1 1.6 %collective-permute-start.26 = (f32[1,64,256]{2,1,0:T(8,128)S(1)}, f32[1,64,256]{2,1,0:T(8,128)S(1)}, u32[]{:S(2)}, u32[]{:S(2)}) collective-permute-start(f32[1,64,256]{2,1,0:T(8,128)S(1)} %slice_bitcast_fusion.6), channel_id=1, source_target_pairs={{0,2},{1,3},{2,0},{3,1},{4,6},{5,7},{6,4},{7,5},{8,10},{9,11},{10,... | collective-permute-start | bytes 196616 | tf_op jit(solution)/shard_map/ppermute | solution.py:253
  83.7 3.2 %collective-permute-done.20.refs_1_ = bf16[32,5120]{1,0:T(8,128)(2,1)S(1)} collective-permute-done((bf16[32,5120]{1,0:T(8,128)(2,1)S(1)}, bf16[32,5120]{1,0:T(8,128)(2,1)S(1)}, u32[]{:S(2)}, u32[]{:S(2)}) %collective-permute-start.20) | collective-permute-done | bytes 327712 | tf_op jit(solution)/shard_map/ppermute | solution.py:243
  88.0 1.3 %collective-permute-done.28 = f32[2,64,256]{2,1,0:T(8,128)S(1)} collective-permute-done((f32[2,64,256]{2,1,0:T(8,128)S(1)}, f32[2,64,256]{2,1,0:T(8,128)S(1)}, u32[]{:S(2)}, u32[]{:S(2)}) %collective-permute-start.28) | collective-permute-done | bytes 131104 | tf_op jit(solution)/shard_map/ppermute | solution.py:253
  89.3 1.6 %collective-permute-start.29 = (f32[1,64,256]{2,1,0:T(8,128)S(1)}, f32[1,64,256]{2,1,0:T(8,128)S(1)}, u32[]{:S(2)}, u32[]{:S(2)}) collective-permute-start(f32[1,64,256]{2,1,0:T(8,128)S(1)} %slice_bitcast_fusion.4), channel_id=1, source_target_pairs={{0,2},{1,3},{2,0},{3,1},{4,6},{5,7},{6,4},{7,5},{8,10},{9,11},{10,... | collective-permute-start | bytes 196616 | tf_op jit(solution)/shard_map/ppermute | solution.py:253
  90.9 2.8 %collective-permute-done.29 = f32[1,64,256]{2,1,0:T(8,128)S(1)} collective-permute-done((f32[1,64,256]{2,1,0:T(8,128)S(1)}, f32[1,64,256]{2,1,0:T(8,128)S(1)}, u32[]{:S(2)}, u32[]{:S(2)}) %collective-permute-start.29) | collective-permute-done | bytes 65568 | tf_op jit(solution)/shard_map/ppermute | solution.py:253
  (67 shorter events, 15.3 us)
Async XLA Ops:
  1.1 16.0 %collective-permute-start = (bf16[32,5120]{1,0:T(8,128)(2,1)S(1)}, bf16[32,5120]{1,0:T(8,128)(2,1)S(1)}, u32[]{:S(2)}, u32[]{:S(2)}) collective-permute-start(bf16[32,5120]{1,0:T(8,128)(2,1)S(1)} %slice_select_fusion.2), channel_id=1, source_target_pairs={{0,4},{4,0},{8,12},{12,8},{1,5},{5,1},{9,13},{13,9},{2,6},{6,2},{1... | collective-permute-start | bytes 983048 | tf_op jit(solution)/shard_map/ppermute | solution.py:230
  4.2 13.0 %collective-permute-start.3 = (bf16[32,5120]{1,0:T(8,128)(2,1)S(1)}, bf16[32,5120]{1,0:T(8,128)(2,1)S(1)}, u32[]{:S(2)}, u32[]{:S(2)}) collective-permute-start(bf16[32,5120]{1,0:T(8,128)(2,1)S(1)} %slice_select_fusion.2), channel_id=1, source_target_pairs={{0,1},{1,0},{2,3},{3,2},{4,8},{5,9},{6,10},{7,11},{8,4},{9,5},{10,... | collective-permute-start | bytes 983048 | tf_op jit(solution)/shard_map/ppermute | solution.py:234
  5.3 14.0 %collective-permute-start.2 = (bf16[32,5120]{1,0:T(8,128)(2,1)S(1)}, bf16[32,5120]{1,0:T(8,128)(2,1)S(1)}, u32[]{:S(2)}, u32[]{:S(2)}) collective-permute-start(bf16[32,5120]{1,0:T(8,128)(2,1)S(1)} %slice_select_fusion.1), channel_id=1, source_target_pairs={{0,4},{4,0},{8,12},{12,8},{1,5},{5,1},{9,13},{13,9},{2,6},{6,2},{1... | collective-permute-start | bytes 983048 | tf_op jit(solution)/shard_map/ppermute | solution.py:230
  9.6 4.1 %copy-start = (bf16[64,16384]{1,0:T(8,128)(2,1)S(1)}, bf16[64,16384]{1,0:T(8,128)(2,1)}, u32[]{:S(2)}) copy-start(bf16[64,16384]{1,0:T(8,128)(2,1)} %test.2) | copy-start | bytes 6291460
  13.8 0.8 copy-start.1
  17.1 13.7 %collective-permute-start.1 = (bf16[32,5120]{1,0:T(8,128)(2,1)S(1)}, bf16[32,5120]{1,0:T(8,128)(2,1)S(1)}, u32[]{:S(2)}, u32[]{:S(2)}) collective-permute-start(bf16[32,5120]{1,0:T(8,128)(2,1)S(1)} %slice_select_fusion), channel_id=1, source_target_pairs={{0,4},{4,0},{8,12},{12,8},{1,5},{5,1},{9,13},{13,9},{2,6},{6,2},{1... | collective-permute-start | bytes 983048 | tf_op jit(solution)/shard_map/ppermute | solution.py:230
  17.2 3.7 %collective-permute-start.4 = (bf16[32,5120]{1,0:T(8,128)(2,1)S(1)}, bf16[32,5120]{1,0:T(8,128)(2,1)S(1)}, u32[]{:S(2)}, u32[]{:S(2)}) collective-permute-start(bf16[32,5120]{1,0:T(8,128)(2,1)S(1)} %slice_select_fusion.1), channel_id=1, source_target_pairs={{0,1},{1,0},{2,3},{3,2},{4,8},{5,9},{6,10},{7,11},{8,4},{9,5},{10,... | collective-permute-start | bytes 983048 | tf_op jit(solution)/shard_map/ppermute | solution.py:234
  17.3 10.6 %collective-permute-start.10 = (bf16[32,5120]{1,0:T(8,128)(2,1)S(1)}, bf16[32,5120]{1,0:T(8,128)(2,1)S(1)}, u32[]{:S(2)}, u32[]{:S(2)}) collective-permute-start(bf16[32,5120]{1,0:T(8,128)(2,1)S(1)} %collective-permute-done.refs_0_), channel_id=1, source_target_pairs={{0,16},{16,0},{1,17},{17,1},{2,18},{18,2},{3,19},{19,3},{4,20},{20... | collective-permute-start | bytes 983048 | tf_op jit(solution)/shard_map/ppermute | solution.py:243
  19.3 15.1 %collective-permute-start.9 = (bf16[32,5120]{1,0:T(8,128)(2,1)S(1)}, bf16[32,5120]{1,0:T(8,128)(2,1)S(1)}, u32[]{:S(2)}, u32[]{:S(2)}) collective-permute-start(bf16[32,5120]{1,0:T(8,128)(2,1)S(1)} %collective-permute-done.2.refs_0_), channel_id=1, source_target_pairs={{0,16},{16,0},{1,17},{17,1},{2,18},{18,2},{3,19},{19,3},{4,20},{20... | collective-permute-start | bytes 983048 | tf_op jit(solution)/shard_map/ppermute | solution.py:243
  20.9 16.1 %collective-permute-start.5 = (bf16[32,5120]{1,0:T(8,128)(2,1)S(1)}, bf16[32,5120]{1,0:T(8,128)(2,1)S(1)}, u32[]{:S(2)}, u32[]{:S(2)}) collective-permute-start(bf16[32,5120]{1,0:T(8,128)(2,1)S(1)} %slice_select_fusion), channel_id=1, source_target_pairs={{0,1},{1,0},{2,3},{3,2},{4,8},{5,9},{6,10},{7,11},{8,4},{9,5},{10,... | collective-permute-start | bytes 983048 | tf_op jit(solution)/shard_map/ppermute | solution.py:234
  27.9 9.2 %collective-permute-start.12 = (bf16[32,5120]{1,0:T(8,128)(2,1)S(1)}, bf16[32,5120]{1,0:T(8,128)(2,1)S(1)}, u32[]{:S(2)}, u32[]{:S(2)}) collective-permute-start(bf16[32,5120]{1,0:T(8,128)(2,1)S(1)} %broadcast_select_fusion.6), channel_id=1, source_target_pairs={{0,4},{4,0},{8,12},{12,8},{1,5},{5,1},{9,13},{13,9},{2,6},{6,2},{1... | collective-permute-start | bytes 983048 | tf_op jit(solution)/shard_map/ppermute | solution.py:230
  34.4 12.7 %collective-permute-start.11 = (bf16[32,5120]{1,0:T(8,128)(2,1)S(1)}, bf16[32,5120]{1,0:T(8,128)(2,1)S(1)}, u32[]{:S(2)}, u32[]{:S(2)}) collective-permute-start(bf16[32,5120]{1,0:T(8,128)(2,1)S(1)} %broadcast_select_fusion.7), channel_id=1, source_target_pairs={{0,4},{4,0},{8,12},{12,8},{1,5},{5,1},{9,13},{13,9},{2,6},{6,2},{1... | collective-permute-start | bytes 983048 | tf_op jit(solution)/shard_map/ppermute | solution.py:230
  34.6 10.6 %collective-permute-start.14 = (bf16[32,5120]{1,0:T(8,128)(2,1)S(1)}, bf16[32,5120]{1,0:T(8,128)(2,1)S(1)}, u32[]{:S(2)}, u32[]{:S(2)}) collective-permute-start(bf16[32,5120]{1,0:T(8,128)(2,1)S(1)} %collective-permute-done.1.refs_0_), channel_id=1, source_target_pairs={{0,16},{16,0},{1,17},{17,1},{2,18},{18,2},{3,19},{19,3},{4,20},{20... | collective-permute-start | bytes 983048 | tf_op jit(solution)/shard_map/ppermute | solution.py:243
  37.0 12.7 %collective-permute-start.6 = (bf16[32,5120]{1,0:T(8,128)(2,1)S(1)}, bf16[32,5120]{1,0:T(8,128)(2,1)S(1)}, u32[]{:S(2)}, u32[]{:S(2)}) collective-permute-start(bf16[32,5120]{1,0:T(8,128)(2,1)S(1)} %collective-permute-done.refs_0_), channel_id=1, source_target_pairs={{0,1},{1,0},{2,3},{3,2},{4,8},{5,9},{6,10},{7,11},{8,4},{9,5},{10,... | collective-permute-start | bytes 983048 | tf_op jit(solution)/shard_map/ppermute | solution.py:234
  37.1 15.1 %collective-permute-start.13 = (bf16[32,5120]{1,0:T(8,128)(2,1)S(1)}, bf16[32,5120]{1,0:T(8,128)(2,1)S(1)}, u32[]{:S(2)}, u32[]{:S(2)}) collective-permute-start(bf16[32,5120]{1,0:T(8,128)(2,1)S(1)} %broadcast_select_fusion.5.refs_0_), channel_id=1, source_target_pairs={{0,16},{16,0},{1,17},{17,1},{2,18},{18,2},{3,19},{19,3},{4,20},{20... | collective-permute-start | bytes 983048 | tf_op jit(solution)/shard_map/ppermute | solution.py:243
  45.2 8.9 %collective-permute-start.16 = (bf16[32,5120]{1,0:T(8,128)(2,1)S(1)}, bf16[32,5120]{1,0:T(8,128)(2,1)S(1)}, u32[]{:S(2)}, u32[]{:S(2)}) collective-permute-start(bf16[32,5120]{1,0:T(8,128)(2,1)S(1)} %collective-permute-done.5), channel_id=1, source_target_pairs={{0,4},{4,0},{8,12},{12,8},{1,5},{5,1},{9,13},{13,9},{2,6},{6,2},{1... | collective-permute-start | bytes 983048 | tf_op jit(solution)/shard_map/ppermute | solution.py:230
  47.1 12.1 %collective-permute-start.18 = (bf16[32,5120]{1,0:T(8,128)(2,1)S(1)}, bf16[32,5120]{1,0:T(8,128)(2,1)S(1)}, u32[]{:S(2)}, u32[]{:S(2)}) collective-permute-start(bf16[32,5120]{1,0:T(8,128)(2,1)S(1)} %broadcast_select_fusion.3.refs_0_), channel_id=1, source_target_pairs={{0,16},{16,0},{1,17},{17,1},{2,18},{18,2},{3,19},{19,3},{4,20},{20... | collective-permute-start | bytes 983048 | tf_op jit(solution)/shard_map/ppermute | solution.py:243
  49.7 10.5 %collective-permute-start.7 = (bf16[32,5120]{1,0:T(8,128)(2,1)S(1)}, bf16[32,5120]{1,0:T(8,128)(2,1)S(1)}, u32[]{:S(2)}, u32[]{:S(2)}) collective-permute-start(bf16[32,5120]{1,0:T(8,128)(2,1)S(1)} %collective-permute-done.2.refs_0_), channel_id=1, source_target_pairs={{0,1},{1,0},{2,3},{3,2},{4,8},{5,9},{6,10},{7,11},{8,4},{9,5},{10,... | collective-permute-start | bytes 983048 | tf_op jit(solution)/shard_map/ppermute | solution.py:234
  52.2 10.3 %collective-permute-start.15 = (bf16[32,5120]{1,0:T(8,128)(2,1)S(1)}, bf16[32,5120]{1,0:T(8,128)(2,1)S(1)}, u32[]{:S(2)}, u32[]{:S(2)}) collective-permute-start(bf16[32,5120]{1,0:T(8,128)(2,1)S(1)} %collective-permute-done.6), channel_id=1, source_target_pairs={{0,4},{4,0},{8,12},{12,8},{1,5},{5,1},{9,13},{13,9},{2,6},{6,2},{1... | collective-permute-start | bytes 983048 | tf_op jit(solution)/shard_map/ppermute | solution.py:230
  54.2 11.9 %collective-permute-start.17 = (bf16[32,5120]{1,0:T(8,128)(2,1)S(1)}, bf16[32,5120]{1,0:T(8,128)(2,1)S(1)}, u32[]{:S(2)}, u32[]{:S(2)}) collective-permute-start(bf16[32,5120]{1,0:T(8,128)(2,1)S(1)} %broadcast_select_fusion.4.refs_0_), channel_id=1, source_target_pairs={{0,16},{16,0},{1,17},{17,1},{2,18},{18,2},{3,19},{19,3},{4,20},{20... | collective-permute-start | bytes 983048 | tf_op jit(solution)/shard_map/ppermute | solution.py:243
  60.2 6.8 %collective-permute-start.8 = (bf16[32,5120]{1,0:T(8,128)(2,1)S(1)}, bf16[32,5120]{1,0:T(8,128)(2,1)S(1)}, u32[]{:S(2)}, u32[]{:S(2)}) collective-permute-start(bf16[32,5120]{1,0:T(8,128)(2,1)S(1)} %collective-permute-done.1.refs_0_), channel_id=1, source_target_pairs={{0,1},{1,0},{2,3},{3,2},{4,8},{5,9},{6,10},{7,11},{8,4},{9,5},{10,... | collective-permute-start | bytes 983048 | tf_op jit(solution)/shard_map/ppermute | solution.py:234
  60.3 10.7 %collective-permute-start.22 = (bf16[32,5120]{1,0:T(8,128)(2,1)S(1)}, bf16[32,5120]{1,0:T(8,128)(2,1)S(1)}, u32[]{:S(2)}, u32[]{:S(2)}) collective-permute-start(bf16[32,5120]{1,0:T(8,128)(2,1)S(1)} %collective-permute-done.7), channel_id=1, source_target_pairs={{0,4},{4,0},{8,12},{12,8},{1,5},{5,1},{9,13},{13,9},{2,6},{6,2},{1... | collective-permute-start | bytes 983048 | tf_op jit(solution)/shard_map/ppermute | solution.py:230
  62.5 18.1 %collective-permute-start.24 = (bf16[32,5120]{1,0:T(8,128)(2,1)S(1)}, bf16[32,5120]{1,0:T(8,128)(2,1)S(1)}, u32[]{:S(2)}, u32[]{:S(2)}) collective-permute-start(bf16[32,5120]{1,0:T(8,128)(2,1)S(1)} %broadcast_select_fusion.refs_0_), channel_id=1, source_target_pairs={{0,16},{16,0},{1,17},{17,1},{2,18},{18,2},{3,19},{19,3},{4,20},{20... | collective-permute-start | bytes 983048 | tf_op jit(solution)/shard_map/ppermute | solution.py:243
  66.9 10.5 %collective-permute-start.19 = (bf16[32,5120]{1,0:T(8,128)(2,1)S(1)}, bf16[32,5120]{1,0:T(8,128)(2,1)S(1)}, u32[]{:S(2)}, u32[]{:S(2)}) collective-permute-start(bf16[32,5120]{1,0:T(8,128)(2,1)S(1)} %collective-permute-done.8), channel_id=1, source_target_pairs={{0,4},{4,0},{8,12},{12,8},{1,5},{5,1},{9,13},{13,9},{2,6},{6,2},{1... | collective-permute-start | bytes 983048 | tf_op jit(solution)/shard_map/ppermute | solution.py:230
  69.6 3.0 %collective-permute-start.21 = (bf16[64,2048]{1,0:T(8,128)(2,1)S(1)}, bf16[64,2048]{1,0:T(8,128)(2,1)S(1)}, u32[]{:S(2)}, u32[]{:S(2)}) collective-permute-start(bf16[64,2048]{1,0:T(8,128)(2,1)S(1)} %pad_maximum_fusion), channel_id=1, source_target_pairs={{0,1},{1,0},{2,3},{3,2},{4,8},{5,9},{6,10},{7,11},{8,4},{9,5},{10,... | collective-permute-start | bytes 786440 | tf_op jit(solution)/shard_map/ppermute | solution.py:234
  71.0 10.5 %collective-permute-start.23 = (bf16[32,5120]{1,0:T(8,128)(2,1)S(1)}, bf16[32,5120]{1,0:T(8,128)(2,1)S(1)}, u32[]{:S(2)}, u32[]{:S(2)}) collective-permute-start(bf16[32,5120]{1,0:T(8,128)(2,1)S(1)} %broadcast_select_fusion.1.refs_0_), channel_id=1, source_target_pairs={{0,16},{16,0},{1,17},{17,1},{2,18},{18,2},{3,19},{19,3},{4,20},{20... | collective-permute-start | bytes 983048 | tf_op jit(solution)/shard_map/ppermute | solution.py:243
  73.2 5.8 %collective-permute-start.25 = (f32[2,64,256]{2,1,0:T(8,128)S(1)}, f32[2,64,256]{2,1,0:T(8,128)S(1)}, u32[]{:S(2)}, u32[]{:S(2)}) collective-permute-start(f32[2,64,256]{2,1,0:T(8,128)S(1)} %slice_bitcast_fusion), channel_id=1, source_target_pairs={{0,1},{1,0},{2,3},{3,2},{4,5},{5,4},{6,7},{7,6},{8,9},{9,8},{10,11... | collective-permute-start | bytes 393224 | tf_op jit(solution)/shard_map/ppermute | solution.py:253
  77.4 9.5 %collective-permute-start.20 = (bf16[32,5120]{1,0:T(8,128)(2,1)S(1)}, bf16[32,5120]{1,0:T(8,128)(2,1)S(1)}, u32[]{:S(2)}, u32[]{:S(2)}) collective-permute-start(bf16[32,5120]{1,0:T(8,128)(2,1)S(1)} %broadcast_select_fusion.2.refs_0_), channel_id=1, source_target_pairs={{0,16},{16,0},{1,17},{17,1},{2,18},{18,2},{3,19},{19,3},{4,20},{20... | collective-permute-start | bytes 983048 | tf_op jit(solution)/shard_map/ppermute | solution.py:243
  79.1 4.3 %collective-permute-start.26 = (f32[1,64,256]{2,1,0:T(8,128)S(1)}, f32[1,64,256]{2,1,0:T(8,128)S(1)}, u32[]{:S(2)}, u32[]{:S(2)}) collective-permute-start(f32[1,64,256]{2,1,0:T(8,128)S(1)} %slice_bitcast_fusion.6), channel_id=1, source_target_pairs={{0,2},{1,3},{2,0},{3,1},{4,6},{5,7},{6,4},{7,5},{8,10},{9,11},{10,... | collective-permute-start | bytes 196616 | tf_op jit(solution)/shard_map/ppermute | solution.py:253
  83.4 4.5 %collective-permute-start.27 = (f32[64,256]{1,0:T(8,128)S(1)}, f32[64,256]{1,0:T(8,128)S(1)}, u32[]{:S(2)}, u32[]{:S(2)}) collective-permute-start(f32[64,256]{1,0:T(8,128)S(1)} %fusion.9), channel_id=1, source_target_pairs={{0,4},{4,0},{8,12},{12,8},{1,5},{5,1},{9,13},{13,9},{2,6},{6,2},{1... | collective-permute-start | bytes 196616 | tf_op jit(solution)/shard_map/ppermute | solution.py:319
  87.9 1.4 %collective-permute-start.28 = (f32[2,64,256]{2,1,0:T(8,128)S(1)}, f32[2,64,256]{2,1,0:T(8,128)S(1)}, u32[]{:S(2)}, u32[]{:S(2)}) collective-permute-start(f32[2,64,256]{2,1,0:T(8,128)S(1)} %slice_bitcast_fusion.2), channel_id=1, source_target_pairs={{0,1},{1,0},{2,3},{3,2},{4,5},{5,4},{6,7},{7,6},{8,9},{9,8},{10,11... | collective-permute-start | bytes 393224 | tf_op jit(solution)/shard_map/ppermute | solution.py:253
  89.3 4.3 %collective-permute-start.29 = (f32[1,64,256]{2,1,0:T(8,128)S(1)}, f32[1,64,256]{2,1,0:T(8,128)S(1)}, u32[]{:S(2)}, u32[]{:S(2)}) collective-permute-start(f32[1,64,256]{2,1,0:T(8,128)S(1)} %slice_bitcast_fusion.4), channel_id=1, source_target_pairs={{0,2},{1,3},{2,0},{3,1},{4,6},{5,7},{6,4},{7,5},{8,10},{9,11},{10,... | collective-permute-start | bytes 196616 | tf_op jit(solution)/shard_map/ppermute | solution.py:253

commit v24 on v23

--- a/solution.py
+++ b/solution.py
@@ -226,12 +226,12 @@
                 middle_pairs.append((i * n_feat + f, to[0] * n_feat + to[1]))
 
         def outer(name, block):
-            waits = outs[-2:-1] + swaps[-3:-2] + made[-4:-3] + (first if len(outs) == 3 else [])
+            waits = outs[-2:-1] + swaps[-4:-3] + made[-4:-3] + (first if len(outs) == 3 else [])
             outs.append(lax.ppermute(after(block, *waits), "ex", outer_pairs))
             done[name] = outs[-1]
 
         def middle(name, block):
-            middles.append(lax.ppermute(after(block, *middles[-1:]), ("ex", "feat"), middle_pairs))
+            middles.append(lax.ppermute(after(block, *middles[-1:], *swaps[-2:-1]), ("ex", "feat"), middle_pairs))
             done[name] = middles[-1]
 
         def swap(block):

time: 94.5 us -> 91.3 us (0.966)
  waiting for transfers between devices: 38.6 us -> 28.6 us
  starting transfers between devices: 34.9 us -> 41.6 us
    ppermute x9, waiting for transfers between devices: 27.5 us -> 9.54 us  [swap(): swaps.append(lax.ppermute(after(block, *waits), 'grp', [(0, 1), (1, 0)]))]
    ppermute x9, waiting for transfers between devices: 5.98 us -> 14 us  [outer(): outs.append(lax.ppermute(after(block, *waits), 'ex', outer_pairs))]
    ppermute x9, starting transfers between devices: 17.2 us -> 22.1 us  [outer(): outs.append(lax.ppermute(after(block, *waits), 'ex', outer_pairs))]
    ppermute x9, starting transfers between devices: 13.7 us -> 15 us  [swap(): swaps.append(lax.ppermute(after(block, *waits), 'grp', [(0, 1), (1, 0)]))]
  transfers between devices with their start and end apart: 30 -> 30, of which waited for: 13 -> 16; matrix products, arithmetic and copies ran while one was open for 7% -> 7% of each run, Pallas kernels for 12% -> 12%
where the time goes in v24:
time: 91.3 us; the launch traced here: 91.1 us
  starting transfers between devices  41.6 us (46%)
  waiting for transfers between devices  28.6 us (31%)
  Pallas kernels  11.3 us (12%)
  local copies, waits for them, and re-layouts  4.9 us (5%)
  other arithmetic  4.33 us (5%)
    ppermute x9, starting transfers between devices, outer(): outs.append(lax.ppermute(after(block, *waits), 'ex', outer_pairs))  22.1 us
    ppermute x9, starting transfers between devices, swap(): swaps.append(lax.ppermute(after(block, *waits), 'grp', [(0, 1), (1, 0)]))  15 us
    ppermute x9, waiting for transfers between devices, outer(): outs.append(lax.ppermute(after(block, *waits), 'ex', outer_pairs))  14 us
    pallas_call x12, Pallas kernels, call(): pl.pallas_call(kernel, out_shape=shapes or jax.ShapeDtypeStruct((rows, do...  11.3 us
    ppermute x9, waiting for transfers between devices, swap(): swaps.append(lax.ppermute(after(block, *waits), 'grp', [(0, 1), (1, 0)]))  9.54 us
    ppermute x4, waiting for transfers between devices, sum_over_feat(): held, waits = (pairs[:, 0] + lax.ppermute(send, 'feat', partner), ())  5.05 us
    slice x1, local copies, waits for them, and re-layouts, line(): trains = [train[:, q * 4 * unit:(q + 1) * 4 * unit] for q in range(4)]  4.08 us
    select_n x3, other arithmetic, share(): return jnp.where(first_grp, rows[:half, here], rows[half:, here])  3.33 us
  transfers between devices with their start and end apart: 30, of which 16 were waited for; matrix products, arithmetic and copies ran while one was open for 7% of the time, Pallas kernels for 12%

profile of v24, /device:TPU:0, one launch (start us, length us, event | category | flops | bytes accessed | tf_op | source)
XLA Modules:
  0.0 91.1 jit_solution(13859890516437011813)
XLA Ops:
  1.6 4.1 %collective-permute-start = (bf16[32,5120]{1,0:T(8,128)(2,1)S(1)}, bf16[32,5120]{1,0:T(8,128)(2,1)S(1)}, u32[]{:S(2)}, u32[]{:S(2)}) collective-permute-start(bf16[32,5120]{1,0:T(8,128)(2,1)S(1)} %slice_select_fusion.2), channel_id=1, source_target_pairs={{0,4},{4,0},{8,12},{12,8},{1,5},{5,1},{9,13},{13,9},{2,6},{6,2},{1... | collective-permute-start | bytes 983048 | tf_op jit(solution)/shard_map/ppermute | solution.py:230
  8.1 4.1 %fusion.10 = (bf16[256,4096]{1,0:T(8,128)(2,1)S(1)}, bf16[256,4096]{1,0:T(8,128)(2,1)S(1)}, bf16[256,4096]{1,0:T(8,128)(2,1)S(1)}, bf16[256,4096]{1,0:T(8,128)(2,1)S(1)}) fusion(bf16[256,16384]{1,0:T(8,128)(2,1)} %param.3), kind=kLoop, calls=%fused_computation.31 | loop fusion | bytes 16777216 | tf_op jit(solution)/shard_map/slice | solution.py:268
  13.1 2.5 %shard_map.38.refs_6_ = f32[64,256]{1,0:T(8,128)S(1)} custom-call(bf16[64,16384]{1,0:T(8,128)(2,1)S(1)} %copy-done, f32[1,16384]{1,0:T(1,128)S(1)} %bitcast.61, bf16[256,4096]{1,0:T(8,128)(2,1)S(1)} %get-tuple-element.68.refs_0_.refs_3_, bf16[256,4096]{1,0:T(8,128)(2,1)S(1)} %get-tuple-element.70.refs_1_.refs_4_.refs_3_, ...), custom_call_target="tpu_custom_call" | custom-call | flops 536870912 | bytes 10485760 | tf_op jit(solution)/shard_map/pallas_call | solution.py:191
  15.6 2.4 %collective-permute-start.1 = (bf16[32,5120]{1,0:T(8,128)(2,1)S(1)}, bf16[32,5120]{1,0:T(8,128)(2,1)S(1)}, u32[]{:S(2)}, u32[]{:S(2)}) collective-permute-start(bf16[32,5120]{1,0:T(8,128)(2,1)S(1)} %slice_select_fusion), channel_id=1, source_target_pairs={{0,4},{4,0},{8,12},{12,8},{1,5},{5,1},{9,13},{13,9},{2,6},{6,2},{1... | collective-permute-start | bytes 983048 | tf_op jit(solution)/shard_map/ppermute | solution.py:230
  18.1 1.5 %collective-permute-start.5 = (bf16[32,5120]{1,0:T(8,128)(2,1)S(1)}, bf16[32,5120]{1,0:T(8,128)(2,1)S(1)}, u32[]{:S(2)}, u32[]{:S(2)}) collective-permute-start(bf16[32,5120]{1,0:T(8,128)(2,1)S(1)} %collective-permute-done.refs_0_), channel_id=1, source_target_pairs={{0,16},{16,0},{1,17},{17,1},{2,18},{18,2},{3,19},{19,3},{4,20},{20... | collective-permute-start | bytes 983048 | tf_op jit(solution)/shard_map/ppermute | solution.py:243
  19.6 1.7 %collective-permute-done.2.refs_0_ = bf16[32,5120]{1,0:T(8,128)(2,1)S(1)} collective-permute-done((bf16[32,5120]{1,0:T(8,128)(2,1)S(1)}, bf16[32,5120]{1,0:T(8,128)(2,1)S(1)}, u32[]{:S(2)}, u32[]{:S(2)}) %collective-permute-start.2) | collective-permute-done | bytes 327712 | tf_op jit(solution)/shard_map/ppermute | solution.py:230
  21.4 2.1 %collective-permute-start.11 = (bf16[32,5120]{1,0:T(8,128)(2,1)S(1)}, bf16[32,5120]{1,0:T(8,128)(2,1)S(1)}, u32[]{:S(2)}, u32[]{:S(2)}) collective-permute-start(bf16[32,5120]{1,0:T(8,128)(2,1)S(1)} %broadcast_select_fusion.7), channel_id=1, source_target_pairs={{0,4},{4,0},{8,12},{12,8},{1,5},{5,1},{9,13},{13,9},{2,6},{6,2},{1... | collective-permute-start | bytes 983048 | tf_op jit(solution)/shard_map/ppermute | solution.py:230
  23.4 1.5 %collective-permute-start.7 = (bf16[32,5120]{1,0:T(8,128)(2,1)S(1)}, bf16[32,5120]{1,0:T(8,128)(2,1)S(1)}, u32[]{:S(2)}, u32[]{:S(2)}) collective-permute-start(bf16[32,5120]{1,0:T(8,128)(2,1)S(1)} %collective-permute-done.2.refs_0_), channel_id=1, source_target_pairs={{0,16},{16,0},{1,17},{17,1},{2,18},{18,2},{3,19},{19,3},{4,20},{20... | collective-permute-start | bytes 983048 | tf_op jit(solution)/shard_map/ppermute | solution.py:243
  25.0 3.4 %collective-permute-done.1.refs_0_ = bf16[32,5120]{1,0:T(8,128)(2,1)S(1)} collective-permute-done((bf16[32,5120]{1,0:T(8,128)(2,1)S(1)}, bf16[32,5120]{1,0:T(8,128)(2,1)S(1)}, u32[]{:S(2)}, u32[]{:S(2)}) %collective-permute-start.1) | collective-permute-done | bytes 327712 | tf_op jit(solution)/shard_map/ppermute | solution.py:230
  28.7 1.5 %collective-permute-start.9 = (bf16[32,5120]{1,0:T(8,128)(2,1)S(1)}, bf16[32,5120]{1,0:T(8,128)(2,1)S(1)}, u32[]{:S(2)}, u32[]{:S(2)}) collective-permute-start(bf16[32,5120]{1,0:T(8,128)(2,1)S(1)} %collective-permute-done.1.refs_0_), channel_id=1, source_target_pairs={{0,16},{16,0},{1,17},{17,1},{2,18},{18,2},{3,19},{19,3},{4,20},{20... | collective-permute-start | bytes 983048 | tf_op jit(solution)/shard_map/ppermute | solution.py:243
  31.2 2.2 %collective-permute-start.14 = (bf16[32,5120]{1,0:T(8,128)(2,1)S(1)}, bf16[32,5120]{1,0:T(8,128)(2,1)S(1)}, u32[]{:S(2)}, u32[]{:S(2)}) collective-permute-start(bf16[32,5120]{1,0:T(8,128)(2,1)S(1)} %broadcast_select_fusion.5), channel_id=1, source_target_pairs={{0,4},{4,0},{8,12},{12,8},{1,5},{5,1},{9,13},{13,9},{2,6},{6,2},{1... | collective-permute-start | bytes 983048 | tf_op jit(solution)/shard_map/ppermute | solution.py:230
  33.4 1.6 %collective-permute-done.11.refs_0_ = bf16[32,5120]{1,0:T(8,128)(2,1)S(1)} collective-permute-done((bf16[32,5120]{1,0:T(8,128)(2,1)S(1)}, bf16[32,5120]{1,0:T(8,128)(2,1)S(1)}, u32[]{:S(2)}, u32[]{:S(2)}) %collective-permute-start.11) | collective-permute-done | bytes 327712 | tf_op jit(solution)/shard_map/ppermute | solution.py:230
  35.1 1.9 %collective-permute-start.12 = (bf16[32,5120]{1,0:T(8,128)(2,1)S(1)}, bf16[32,5120]{1,0:T(8,128)(2,1)S(1)}, u32[]{:S(2)}, u32[]{:S(2)}) collective-permute-start(bf16[32,5120]{1,0:T(8,128)(2,1)S(1)} %broadcast_select_fusion.6.refs_0_), channel_id=1, source_target_pairs={{0,16},{16,0},{1,17},{17,1},{2,18},{18,2},{3,19},{19,3},{4,20},{20... | collective-permute-start | bytes 983048 | tf_op jit(solution)/shard_map/ppermute | solution.py:243
  38.1 2.5 %collective-permute-start.18 = (bf16[32,5120]{1,0:T(8,128)(2,1)S(1)}, bf16[32,5120]{1,0:T(8,128)(2,1)S(1)}, u32[]{:S(2)}, u32[]{:S(2)}) collective-permute-start(bf16[32,5120]{1,0:T(8,128)(2,1)S(1)} %collective-permute-done.6), channel_id=1, source_target_pairs={{0,4},{4,0},{8,12},{12,8},{1,5},{5,1},{9,13},{13,9},{2,6},{6,2},{1... | collective-permute-start | bytes 983048 | tf_op jit(solution)/shard_map/ppermute | solution.py:230
  40.6 1.5 %collective-permute-done.14.refs_1_ = bf16[32,5120]{1,0:T(8,128)(2,1)S(1)} collective-permute-done((bf16[32,5120]{1,0:T(8,128)(2,1)S(1)}, bf16[32,5120]{1,0:T(8,128)(2,1)S(1)}, u32[]{:S(2)}, u32[]{:S(2)}) %collective-permute-start.14) | collective-permute-done | bytes 327712 | tf_op jit(solution)/shard_map/ppermute | solution.py:230
  42.2 1.9 %collective-permute-start.16 = (bf16[32,5120]{1,0:T(8,128)(2,1)S(1)}, bf16[32,5120]{1,0:T(8,128)(2,1)S(1)}, u32[]{:S(2)}, u32[]{:S(2)}) collective-permute-start(bf16[32,5120]{1,0:T(8,128)(2,1)S(1)} %broadcast_select_fusion.4.refs_0_), channel_id=1, source_target_pairs={{0,16},{16,0},{1,17},{17,1},{2,18},{18,2},{3,19},{19,3},{4,20},{20... | collective-permute-start | bytes 983048 | tf_op jit(solution)/shard_map/ppermute | solution.py:243
  45.0 4.2 %collective-permute-done.12.refs_1_ = bf16[32,5120]{1,0:T(8,128)(2,1)S(1)} collective-permute-done((bf16[32,5120]{1,0:T(8,128)(2,1)S(1)}, bf16[32,5120]{1,0:T(8,128)(2,1)S(1)}, u32[]{:S(2)}, u32[]{:S(2)}) %collective-permute-start.12) | collective-permute-done | bytes 327712 | tf_op jit(solution)/shard_map/ppermute | solution.py:243
  50.2 2.1 %collective-permute-start.15 = (bf16[32,5120]{1,0:T(8,128)(2,1)S(1)}, bf16[32,5120]{1,0:T(8,128)(2,1)S(1)}, u32[]{:S(2)}, u32[]{:S(2)}) collective-permute-start(bf16[32,5120]{1,0:T(8,128)(2,1)S(1)} %collective-permute-done.8), channel_id=1, source_target_pairs={{0,4},{4,0},{8,12},{12,8},{1,5},{5,1},{9,13},{13,9},{2,6},{6,2},{1... | collective-permute-start | bytes 983048 | tf_op jit(solution)/shard_map/ppermute | solution.py:230
  52.3 1.6 %collective-permute-start.19 = (bf16[32,5120]{1,0:T(8,128)(2,1)S(1)}, bf16[32,5120]{1,0:T(8,128)(2,1)S(1)}, u32[]{:S(2)}, u32[]{:S(2)}) collective-permute-start(bf16[32,5120]{1,0:T(8,128)(2,1)S(1)} %broadcast_select_fusion.2.refs_0_), channel_id=1, source_target_pairs={{0,16},{16,0},{1,17},{17,1},{2,18},{18,2},{3,19},{19,3},{4,20},{20... | collective-permute-start | bytes 983048 | tf_op jit(solution)/shard_map/ppermute | solution.py:243
  53.9 1.8 %collective-permute-done.16.refs_1_ = bf16[32,5120]{1,0:T(8,128)(2,1)S(1)} collective-permute-done((bf16[32,5120]{1,0:T(8,128)(2,1)S(1)}, bf16[32,5120]{1,0:T(8,128)(2,1)S(1)}, u32[]{:S(2)}, u32[]{:S(2)}) %collective-permute-start.16) | collective-permute-done | bytes 327712 | tf_op jit(solution)/shard_map/ppermute | solution.py:243
  56.7 3.1 %collective-permute-start.22 = (bf16[32,5120]{1,0:T(8,128)(2,1)S(1)}, bf16[32,5120]{1,0:T(8,128)(2,1)S(1)}, u32[]{:S(2)}, u32[]{:S(2)}) collective-permute-start(bf16[32,5120]{1,0:T(8,128)(2,1)S(1)} %collective-permute-done.10), channel_id=1, source_target_pairs={{0,4},{4,0},{8,12},{12,8},{1,5},{5,1},{9,13},{13,9},{2,6},{6,2},{1... | collective-permute-start | bytes 983048 | tf_op jit(solution)/shard_map/ppermute | solution.py:230
  60.7 1.6 %collective-permute-start.24 = (bf16[32,5120]{1,0:T(8,128)(2,1)S(1)}, bf16[32,5120]{1,0:T(8,128)(2,1)S(1)}, u32[]{:S(2)}, u32[]{:S(2)}) collective-permute-start(bf16[32,5120]{1,0:T(8,128)(2,1)S(1)} %broadcast_select_fusion.refs_0_), channel_id=1, source_target_pairs={{0,16},{16,0},{1,17},{17,1},{2,18},{18,2},{3,19},{19,3},{4,20},{20... | collective-permute-start | bytes 983048 | tf_op jit(solution)/shard_map/ppermute | solution.py:243
  63.3 3.6 %collective-permute-start.17 = (bf16[32,5120]{1,0:T(8,128)(2,1)S(1)}, bf16[32,5120]{1,0:T(8,128)(2,1)S(1)}, u32[]{:S(2)}, u32[]{:S(2)}) collective-permute-start(bf16[32,5120]{1,0:T(8,128)(2,1)S(1)} %collective-permute-done.13), channel_id=1, source_target_pairs={{0,4},{4,0},{8,12},{12,8},{1,5},{5,1},{9,13},{13,9},{2,6},{6,2},{1... | collective-permute-start | bytes 983048 | tf_op jit(solution)/shard_map/ppermute | solution.py:230
  66.9 1.3 %collective-permute-done.22 = bf16[32,5120]{1,0:T(8,128)(2,1)S(1)} collective-permute-done((bf16[32,5120]{1,0:T(8,128)(2,1)S(1)}, bf16[32,5120]{1,0:T(8,128)(2,1)S(1)}, u32[]{:S(2)}, u32[]{:S(2)}) %collective-permute-start.22) | collective-permute-done | bytes 327712 | tf_op jit(solution)/shard_map/ppermute | solution.py:230
  68.2 1.9 %collective-permute-start.23 = (bf16[32,5120]{1,0:T(8,128)(2,1)S(1)}, bf16[32,5120]{1,0:T(8,128)(2,1)S(1)}, u32[]{:S(2)}, u32[]{:S(2)}) collective-permute-start(bf16[32,5120]{1,0:T(8,128)(2,1)S(1)} %broadcast_select_fusion.1.refs_0_), channel_id=1, source_target_pairs={{0,16},{16,0},{1,17},{17,1},{2,18},{18,2},{3,19},{19,3},{4,20},{20... | collective-permute-start | bytes 983048 | tf_op jit(solution)/shard_map/ppermute | solution.py:243
  70.7 3.6 %collective-permute-done.17 = bf16[32,5120]{1,0:T(8,128)(2,1)S(1)} collective-permute-done((bf16[32,5120]{1,0:T(8,128)(2,1)S(1)}, bf16[32,5120]{1,0:T(8,128)(2,1)S(1)}, u32[]{:S(2)}, u32[]{:S(2)}) %collective-permute-start.17) | collective-permute-done | bytes 327712 | tf_op jit(solution)/shard_map/ppermute | solution.py:230
  74.4 1.6 %collective-permute-start.20 = (bf16[32,5120]{1,0:T(8,128)(2,1)S(1)}, bf16[32,5120]{1,0:T(8,128)(2,1)S(1)}, u32[]{:S(2)}, u32[]{:S(2)}) collective-permute-start(bf16[32,5120]{1,0:T(8,128)(2,1)S(1)} %broadcast_select_fusion.3.refs_0_), channel_id=1, source_target_pairs={{0,16},{16,0},{1,17},{17,1},{2,18},{18,2},{3,19},{19,3},{4,20},{20... | collective-permute-start | bytes 983048 | tf_op jit(solution)/shard_map/ppermute | solution.py:243
  76.0 1.6 %collective-permute-start.26 = (f32[1,64,256]{2,1,0:T(8,128)S(1)}, f32[1,64,256]{2,1,0:T(8,128)S(1)}, u32[]{:S(2)}, u32[]{:S(2)}) collective-permute-start(f32[1,64,256]{2,1,0:T(8,128)S(1)} %slice_bitcast_fusion.6), channel_id=1, source_target_pairs={{0,2},{1,3},{2,0},{3,1},{4,6},{5,7},{6,4},{7,5},{8,10},{9,11},{10,... | collective-permute-start | bytes 196616 | tf_op jit(solution)/shard_map/ppermute | solution.py:253
  80.7 3.0 %collective-permute-done.20.refs_1_ = bf16[32,5120]{1,0:T(8,128)(2,1)S(1)} collective-permute-done((bf16[32,5120]{1,0:T(8,128)(2,1)S(1)}, bf16[32,5120]{1,0:T(8,128)(2,1)S(1)}, u32[]{:S(2)}, u32[]{:S(2)}) %collective-permute-start.20) | collective-permute-done | bytes 327712 | tf_op jit(solution)/shard_map/ppermute | solution.py:243
  84.8 1.3 %collective-permute-done.28 = f32[2,64,256]{2,1,0:T(8,128)S(1)} collective-permute-done((f32[2,64,256]{2,1,0:T(8,128)S(1)}, f32[2,64,256]{2,1,0:T(8,128)S(1)}, u32[]{:S(2)}, u32[]{:S(2)}) %collective-permute-start.28) | collective-permute-done | bytes 131104 | tf_op jit(solution)/shard_map/ppermute | solution.py:253
  86.1 1.6 %collective-permute-start.29 = (f32[1,64,256]{2,1,0:T(8,128)S(1)}, f32[1,64,256]{2,1,0:T(8,128)S(1)}, u32[]{:S(2)}, u32[]{:S(2)}) collective-permute-start(f32[1,64,256]{2,1,0:T(8,128)S(1)} %slice_bitcast_fusion.4), channel_id=1, source_target_pairs={{0,2},{1,3},{2,0},{3,1},{4,6},{5,7},{6,4},{7,5},{8,10},{9,11},{10,... | collective-permute-start | bytes 196616 | tf_op jit(solution)/shard_map/ppermute | solution.py:253
  87.7 2.8 %collective-permute-done.29 = f32[1,64,256]{2,1,0:T(8,128)S(1)} collective-permute-done((f32[1,64,256]{2,1,0:T(8,128)S(1)}, f32[1,64,256]{2,1,0:T(8,128)S(1)}, u32[]{:S(2)}, u32[]{:S(2)}) %collective-permute-start.29) | collective-permute-done | bytes 65568 | tf_op jit(solution)/shard_map/ppermute | solution.py:253
  (67 shorter events, 17.8 us)
Async XLA Ops:
  1.1 14.4 %collective-permute-start.3 = (bf16[32,5120]{1,0:T(8,128)(2,1)S(1)}, bf16[32,5120]{1,0:T(8,128)(2,1)S(1)}, u32[]{:S(2)}, u32[]{:S(2)}) collective-permute-start(bf16[32,5120]{1,0:T(8,128)(2,1)S(1)} %slice_select_fusion.2), channel_id=1, source_target_pairs={{0,1},{1,0},{2,3},{3,2},{4,8},{5,9},{6,10},{7,11},{8,4},{9,5},{10,... | collective-permute-start | bytes 983048 | tf_op jit(solution)/shard_map/ppermute | solution.py:234
  1.6 14.0 %collective-permute-start = (bf16[32,5120]{1,0:T(8,128)(2,1)S(1)}, bf16[32,5120]{1,0:T(8,128)(2,1)S(1)}, u32[]{:S(2)}, u32[]{:S(2)}) collective-permute-start(bf16[32,5120]{1,0:T(8,128)(2,1)S(1)} %slice_select_fusion.2), channel_id=1, source_target_pairs={{0,4},{4,0},{8,12},{12,8},{1,5},{5,1},{9,13},{13,9},{2,6},{6,2},{1... | collective-permute-start | bytes 983048 | tf_op jit(solution)/shard_map/ppermute | solution.py:230
  6.9 14.5 %collective-permute-start.2 = (bf16[32,5120]{1,0:T(8,128)(2,1)S(1)}, bf16[32,5120]{1,0:T(8,128)(2,1)S(1)}, u32[]{:S(2)}, u32[]{:S(2)}) collective-permute-start(bf16[32,5120]{1,0:T(8,128)(2,1)S(1)} %slice_select_fusion.1), channel_id=1, source_target_pairs={{0,4},{4,0},{8,12},{12,8},{1,5},{5,1},{9,13},{13,9},{2,6},{6,2},{1... | collective-permute-start | bytes 983048 | tf_op jit(solution)/shard_map/ppermute | solution.py:230
  8.1 4.1 %copy-start = (bf16[64,16384]{1,0:T(8,128)(2,1)S(1)}, bf16[64,16384]{1,0:T(8,128)(2,1)}, u32[]{:S(2)}) copy-start(bf16[64,16384]{1,0:T(8,128)(2,1)} %test.2) | copy-start | bytes 6291460
  12.2 0.8 copy-start.1
  15.6 13.2 %collective-permute-start.4 = (bf16[32,5120]{1,0:T(8,128)(2,1)S(1)}, bf16[32,5120]{1,0:T(8,128)(2,1)S(1)}, u32[]{:S(2)}, u32[]{:S(2)}) collective-permute-start(bf16[32,5120]{1,0:T(8,128)(2,1)S(1)} %slice_select_fusion.1), channel_id=1, source_target_pairs={{0,1},{1,0},{2,3},{3,2},{4,8},{5,9},{6,10},{7,11},{8,4},{9,5},{10,... | collective-permute-start | bytes 983048 | tf_op jit(solution)/shard_map/ppermute | solution.py:234
  15.6 12.8 %collective-permute-start.1 = (bf16[32,5120]{1,0:T(8,128)(2,1)S(1)}, bf16[32,5120]{1,0:T(8,128)(2,1)S(1)}, u32[]{:S(2)}, u32[]{:S(2)}) collective-permute-start(bf16[32,5120]{1,0:T(8,128)(2,1)S(1)} %slice_select_fusion), channel_id=1, source_target_pairs={{0,4},{4,0},{8,12},{12,8},{1,5},{5,1},{9,13},{13,9},{2,6},{6,2},{1... | collective-permute-start | bytes 983048 | tf_op jit(solution)/shard_map/ppermute | solution.py:230
  18.1 10.7 %collective-permute-start.5 = (bf16[32,5120]{1,0:T(8,128)(2,1)S(1)}, bf16[32,5120]{1,0:T(8,128)(2,1)S(1)}, u32[]{:S(2)}, u32[]{:S(2)}) collective-permute-start(bf16[32,5120]{1,0:T(8,128)(2,1)S(1)} %collective-permute-done.refs_0_), channel_id=1, source_target_pairs={{0,16},{16,0},{1,17},{17,1},{2,18},{18,2},{3,19},{19,3},{4,20},{20... | collective-permute-start | bytes 983048 | tf_op jit(solution)/shard_map/ppermute | solution.py:243
  21.4 13.6 %collective-permute-start.11 = (bf16[32,5120]{1,0:T(8,128)(2,1)S(1)}, bf16[32,5120]{1,0:T(8,128)(2,1)S(1)}, u32[]{:S(2)}, u32[]{:S(2)}) collective-permute-start(bf16[32,5120]{1,0:T(8,128)(2,1)S(1)} %broadcast_select_fusion.7), channel_id=1, source_target_pairs={{0,4},{4,0},{8,12},{12,8},{1,5},{5,1},{9,13},{13,9},{2,6},{6,2},{1... | collective-permute-start | bytes 983048 | tf_op jit(solution)/shard_map/ppermute | solution.py:230
  23.4 11.7 %collective-permute-start.7 = (bf16[32,5120]{1,0:T(8,128)(2,1)S(1)}, bf16[32,5120]{1,0:T(8,128)(2,1)S(1)}, u32[]{:S(2)}, u32[]{:S(2)}) collective-permute-start(bf16[32,5120]{1,0:T(8,128)(2,1)S(1)} %collective-permute-done.2.refs_0_), channel_id=1, source_target_pairs={{0,16},{16,0},{1,17},{17,1},{2,18},{18,2},{3,19},{19,3},{4,20},{20... | collective-permute-start | bytes 983048 | tf_op jit(solution)/shard_map/ppermute | solution.py:243
  28.7 9.3 %collective-permute-start.6 = (bf16[32,5120]{1,0:T(8,128)(2,1)S(1)}, bf16[32,5120]{1,0:T(8,128)(2,1)S(1)}, u32[]{:S(2)}, u32[]{:S(2)}) collective-permute-start(bf16[32,5120]{1,0:T(8,128)(2,1)S(1)} %slice_select_fusion), channel_id=1, source_target_pairs={{0,1},{1,0},{2,3},{3,2},{4,8},{5,9},{6,10},{7,11},{8,4},{9,5},{10,... | collective-permute-start | bytes 983048 | tf_op jit(solution)/shard_map/ppermute | solution.py:234
  28.7 13.4 %collective-permute-start.9 = (bf16[32,5120]{1,0:T(8,128)(2,1)S(1)}, bf16[32,5120]{1,0:T(8,128)(2,1)S(1)}, u32[]{:S(2)}, u32[]{:S(2)}) collective-permute-start(bf16[32,5120]{1,0:T(8,128)(2,1)S(1)} %collective-permute-done.1.refs_0_), channel_id=1, source_target_pairs={{0,16},{16,0},{1,17},{17,1},{2,18},{18,2},{3,19},{19,3},{4,20},{20... | collective-permute-start | bytes 983048 | tf_op jit(solution)/shard_map/ppermute | solution.py:243
  31.2 10.8 %collective-permute-start.14 = (bf16[32,5120]{1,0:T(8,128)(2,1)S(1)}, bf16[32,5120]{1,0:T(8,128)(2,1)S(1)}, u32[]{:S(2)}, u32[]{:S(2)}) collective-permute-start(bf16[32,5120]{1,0:T(8,128)(2,1)S(1)} %broadcast_select_fusion.5), channel_id=1, source_target_pairs={{0,4},{4,0},{8,12},{12,8},{1,5},{5,1},{9,13},{13,9},{2,6},{6,2},{1... | collective-permute-start | bytes 983048 | tf_op jit(solution)/shard_map/ppermute | solution.py:230
  35.1 14.0 %collective-permute-start.12 = (bf16[32,5120]{1,0:T(8,128)(2,1)S(1)}, bf16[32,5120]{1,0:T(8,128)(2,1)S(1)}, u32[]{:S(2)}, u32[]{:S(2)}) collective-permute-start(bf16[32,5120]{1,0:T(8,128)(2,1)S(1)} %broadcast_select_fusion.6.refs_0_), channel_id=1, source_target_pairs={{0,16},{16,0},{1,17},{17,1},{2,18},{18,2},{3,19},{19,3},{4,20},{20... | collective-permute-start | bytes 983048 | tf_op jit(solution)/shard_map/ppermute | solution.py:243
  38.0 12.1 %collective-permute-start.8 = (bf16[32,5120]{1,0:T(8,128)(2,1)S(1)}, bf16[32,5120]{1,0:T(8,128)(2,1)S(1)}, u32[]{:S(2)}, u32[]{:S(2)}) collective-permute-start(bf16[32,5120]{1,0:T(8,128)(2,1)S(1)} %collective-permute-done.refs_0_), channel_id=1, source_target_pairs={{0,1},{1,0},{2,3},{3,2},{4,8},{5,9},{6,10},{7,11},{8,4},{9,5},{10,... | collective-permute-start | bytes 983048 | tf_op jit(solution)/shard_map/ppermute | solution.py:234
  38.1 14.2 %collective-permute-start.18 = (bf16[32,5120]{1,0:T(8,128)(2,1)S(1)}, bf16[32,5120]{1,0:T(8,128)(2,1)S(1)}, u32[]{:S(2)}, u32[]{:S(2)}) collective-permute-start(bf16[32,5120]{1,0:T(8,128)(2,1)S(1)} %collective-permute-done.6), channel_id=1, source_target_pairs={{0,4},{4,0},{8,12},{12,8},{1,5},{5,1},{9,13},{13,9},{2,6},{6,2},{1... | collective-permute-start | bytes 983048 | tf_op jit(solution)/shard_map/ppermute | solution.py:230
  42.2 13.6 %collective-permute-start.16 = (bf16[32,5120]{1,0:T(8,128)(2,1)S(1)}, bf16[32,5120]{1,0:T(8,128)(2,1)S(1)}, u32[]{:S(2)}, u32[]{:S(2)}) collective-permute-start(bf16[32,5120]{1,0:T(8,128)(2,1)S(1)} %broadcast_select_fusion.4.refs_0_), channel_id=1, source_target_pairs={{0,16},{16,0},{1,17},{17,1},{2,18},{18,2},{3,19},{19,3},{4,20},{20... | collective-permute-start | bytes 983048 | tf_op jit(solution)/shard_map/ppermute | solution.py:243
  50.1 6.6 %collective-permute-start.10 = (bf16[32,5120]{1,0:T(8,128)(2,1)S(1)}, bf16[32,5120]{1,0:T(8,128)(2,1)S(1)}, u32[]{:S(2)}, u32[]{:S(2)}) collective-permute-start(bf16[32,5120]{1,0:T(8,128)(2,1)S(1)} %collective-permute-done.2.refs_0_), channel_id=1, source_target_pairs={{0,1},{1,0},{2,3},{3,2},{4,8},{5,9},{6,10},{7,11},{8,4},{9,5},{10,... | collective-permute-start | bytes 983048 | tf_op jit(solution)/shard_map/ppermute | solution.py:234
  50.2 10.5 %collective-permute-start.15 = (bf16[32,5120]{1,0:T(8,128)(2,1)S(1)}, bf16[32,5120]{1,0:T(8,128)(2,1)S(1)}, u32[]{:S(2)}, u32[]{:S(2)}) collective-permute-start(bf16[32,5120]{1,0:T(8,128)(2,1)S(1)} %collective-permute-done.8), channel_id=1, source_target_pairs={{0,4},{4,0},{8,12},{12,8},{1,5},{5,1},{9,13},{13,9},{2,6},{6,2},{1... | collective-permute-start | bytes 983048 | tf_op jit(solution)/shard_map/ppermute | solution.py:230
  52.3 10.0 %collective-permute-start.19 = (bf16[32,5120]{1,0:T(8,128)(2,1)S(1)}, bf16[32,5120]{1,0:T(8,128)(2,1)S(1)}, u32[]{:S(2)}, u32[]{:S(2)}) collective-permute-start(bf16[32,5120]{1,0:T(8,128)(2,1)S(1)} %broadcast_select_fusion.2.refs_0_), channel_id=1, source_target_pairs={{0,16},{16,0},{1,17},{17,1},{2,18},{18,2},{3,19},{19,3},{4,20},{20... | collective-permute-start | bytes 983048 | tf_op jit(solution)/shard_map/ppermute | solution.py:243
  56.7 6.6 %collective-permute-start.13 = (bf16[32,5120]{1,0:T(8,128)(2,1)S(1)}, bf16[32,5120]{1,0:T(8,128)(2,1)S(1)}, u32[]{:S(2)}, u32[]{:S(2)}) collective-permute-start(bf16[32,5120]{1,0:T(8,128)(2,1)S(1)} %collective-permute-done.1.refs_0_), channel_id=1, source_target_pairs={{0,1},{1,0},{2,3},{3,2},{4,8},{5,9},{6,10},{7,11},{8,4},{9,5},{10,... | collective-permute-start | bytes 983048 | tf_op jit(solution)/shard_map/ppermute | solution.py:234
  56.7 11.4 %collective-permute-start.22 = (bf16[32,5120]{1,0:T(8,128)(2,1)S(1)}, bf16[32,5120]{1,0:T(8,128)(2,1)S(1)}, u32[]{:S(2)}, u32[]{:S(2)}) collective-permute-start(bf16[32,5120]{1,0:T(8,128)(2,1)S(1)} %collective-permute-done.10), channel_id=1, source_target_pairs={{0,4},{4,0},{8,12},{12,8},{1,5},{5,1},{9,13},{13,9},{2,6},{6,2},{1... | collective-permute-start | bytes 983048 | tf_op jit(solution)/shard_map/ppermute | solution.py:230
  60.7 16.8 %collective-permute-start.24 = (bf16[32,5120]{1,0:T(8,128)(2,1)S(1)}, bf16[32,5120]{1,0:T(8,128)(2,1)S(1)}, u32[]{:S(2)}, u32[]{:S(2)}) collective-permute-start(bf16[32,5120]{1,0:T(8,128)(2,1)S(1)} %broadcast_select_fusion.refs_0_), channel_id=1, source_target_pairs={{0,16},{16,0},{1,17},{17,1},{2,18},{18,2},{3,19},{19,3},{4,20},{20... | collective-permute-start | bytes 983048 | tf_op jit(solution)/shard_map/ppermute | solution.py:243
  63.2 6.8 %collective-permute-start.21 = (bf16[64,2048]{1,0:T(8,128)(2,1)S(1)}, bf16[64,2048]{1,0:T(8,128)(2,1)S(1)}, u32[]{:S(2)}, u32[]{:S(2)}) collective-permute-start(bf16[64,2048]{1,0:T(8,128)(2,1)S(1)} %pad_maximum_fusion), channel_id=1, source_target_pairs={{0,1},{1,0},{2,3},{3,2},{4,8},{5,9},{6,10},{7,11},{8,4},{9,5},{10,... | collective-permute-start | bytes 786440 | tf_op jit(solution)/shard_map/ppermute | solution.py:234
  63.3 11.0 %collective-permute-start.17 = (bf16[32,5120]{1,0:T(8,128)(2,1)S(1)}, bf16[32,5120]{1,0:T(8,128)(2,1)S(1)}, u32[]{:S(2)}, u32[]{:S(2)}) collective-permute-start(bf16[32,5120]{1,0:T(8,128)(2,1)S(1)} %collective-permute-done.13), channel_id=1, source_target_pairs={{0,4},{4,0},{8,12},{12,8},{1,5},{5,1},{9,13},{13,9},{2,6},{6,2},{1... | collective-permute-start | bytes 983048 | tf_op jit(solution)/shard_map/ppermute | solution.py:230
  68.2 10.3 %collective-permute-start.23 = (bf16[32,5120]{1,0:T(8,128)(2,1)S(1)}, bf16[32,5120]{1,0:T(8,128)(2,1)S(1)}, u32[]{:S(2)}, u32[]{:S(2)}) collective-permute-start(bf16[32,5120]{1,0:T(8,128)(2,1)S(1)} %broadcast_select_fusion.1.refs_0_), channel_id=1, source_target_pairs={{0,16},{16,0},{1,17},{17,1},{2,18},{18,2},{3,19},{19,3},{4,20},{20... | collective-permute-start | bytes 983048 | tf_op jit(solution)/shard_map/ppermute | solution.py:243
  70.6 5.3 %collective-permute-start.25 = (f32[2,64,256]{2,1,0:T(8,128)S(1)}, f32[2,64,256]{2,1,0:T(8,128)S(1)}, u32[]{:S(2)}, u32[]{:S(2)}) collective-permute-start(f32[2,64,256]{2,1,0:T(8,128)S(1)} %slice_bitcast_fusion), channel_id=1, source_target_pairs={{0,1},{1,0},{2,3},{3,2},{4,5},{5,4},{6,7},{7,6},{8,9},{9,8},{10,11... | collective-permute-start | bytes 393224 | tf_op jit(solution)/shard_map/ppermute | solution.py:253
  74.4 9.3 %collective-permute-start.20 = (bf16[32,5120]{1,0:T(8,128)(2,1)S(1)}, bf16[32,5120]{1,0:T(8,128)(2,1)S(1)}, u32[]{:S(2)}, u32[]{:S(2)}) collective-permute-start(bf16[32,5120]{1,0:T(8,128)(2,1)S(1)} %broadcast_select_fusion.3.refs_0_), channel_id=1, source_target_pairs={{0,16},{16,0},{1,17},{17,1},{2,18},{18,2},{3,19},{19,3},{4,20},{20... | collective-permute-start | bytes 983048 | tf_op jit(solution)/shard_map/ppermute | solution.py:243
  76.0 4.3 %collective-permute-start.26 = (f32[1,64,256]{2,1,0:T(8,128)S(1)}, f32[1,64,256]{2,1,0:T(8,128)S(1)}, u32[]{:S(2)}, u32[]{:S(2)}) collective-permute-start(f32[1,64,256]{2,1,0:T(8,128)S(1)} %slice_bitcast_fusion.6), channel_id=1, source_target_pairs={{0,2},{1,3},{2,0},{3,1},{4,6},{5,7},{6,4},{7,5},{8,10},{9,11},{10,... | collective-permute-start | bytes 196616 | tf_op jit(solution)/shard_map/ppermute | solution.py:253
  80.4 4.3 %collective-permute-start.27 = (f32[64,256]{1,0:T(8,128)S(1)}, f32[64,256]{1,0:T(8,128)S(1)}, u32[]{:S(2)}, u32[]{:S(2)}) collective-permute-start(f32[64,256]{1,0:T(8,128)S(1)} %fusion.9), channel_id=1, source_target_pairs={{0,4},{4,0},{8,12},{12,8},{1,5},{5,1},{9,13},{13,9},{2,6},{6,2},{1... | collective-permute-start | bytes 196616 | tf_op jit(solution)/shard_map/ppermute | solution.py:319
  84.7 1.4 %collective-permute-start.28 = (f32[2,64,256]{2,1,0:T(8,128)S(1)}, f32[2,64,256]{2,1,0:T(8,128)S(1)}, u32[]{:S(2)}, u32[]{:S(2)}) collective-permute-start(f32[2,64,256]{2,1,0:T(8,128)S(1)} %slice_bitcast_fusion.2), channel_id=1, source_target_pairs={{0,1},{1,0},{2,3},{3,2},{4,5},{5,4},{6,7},{7,6},{8,9},{9,8},{10,11... | collective-permute-start | bytes 393224 | tf_op jit(solution)/shard_map/ppermute | solution.py:253
  86.1 4.3 %collective-permute-start.29 = (f32[1,64,256]{2,1,0:T(8,128)S(1)}, f32[1,64,256]{2,1,0:T(8,128)S(1)}, u32[]{:S(2)}, u32[]{:S(2)}) collective-permute-start(f32[1,64,256]{2,1,0:T(8,128)S(1)} %slice_bitcast_fusion.4), channel_id=1, source_target_pairs={{0,2},{1,3},{2,0},{3,1},{4,6},{5,7},{6,4},{7,5},{8,10},{9,11},{10,... | collective-permute-start | bytes 196616 | tf_op jit(solution)/shard_map/ppermute | solution.py:253

commit v25 on v24

--- a/solution.py
+++ b/solution.py
@@ -226,7 +226,7 @@
                 middle_pairs.append((i * n_feat + f, to[0] * n_feat + to[1]))
 
         def outer(name, block):
-            waits = outs[-2:-1] + swaps[-4:-3] + made[-4:-3] + (first if len(outs) == 3 else [])
+            waits = outs[-2:-1] + swaps[-4:-3] + made[-4:-3] + (first if len(outs) == 4 else [])
             outs.append(lax.ppermute(after(block, *waits), "ex", outer_pairs))
             done[name] = outs[-1]
 
@@ -266,10 +266,6 @@
         for start, count in zip(firsts, LINE):
             mine.append(share(after(test, *mine[-1:]), start, count))
         trains = [train[:, q * 4 * unit : (q + 1) * 4 * unit] for q in range(4)]
-        own = call(
-            functools.partial(line_own_kernel, unit), queries, docs, feats, [test, scale, *trains]
-        )
-        first = [own]
         widths = LINE[:2]
         shapes = [jax.ShapeDtypeStruct((half, w * unit), test.dtype) for w in widths]
         shapes.append(jax.ShapeDtypeStruct((half, n_grp * SHIP * unit), test.dtype))
@@ -278,7 +274,7 @@
             [test, trains[3]], shapes=shapes,
         )
 
-        sums = [own, None, None, None]
+        first, sums = [], [None] * n_ex
         n = len(LINE)
 
         def finish(t, c, block):
@@ -296,6 +292,12 @@
         for c in range(n):
             outer(f"E1{c}", mine[c])
             middle(f"O1{c}", mine[c])
+            if c == 0:
+                late = after(test, done["E10"])
+                sums[0] = call(
+                    functools.partial(line_own_kernel, unit), queries, docs, feats, [late, scale, *trains]
+                )
+                first.append(sums[0])
             finish(1, c, done[f"E1{c}"])
         for c in range(n):
             inner = done[f"O1{c}"]

time: 91.3 us -> 90.2 us (0.988)
  waiting for transfers between devices: 28.6 us -> 19.8 us
  starting transfers between devices: 41.6 us -> 49.3 us
    ppermute x9, waiting for transfers between devices: 9.54 us -> 3.14 us  [swap(): swaps.append(lax.ppermute(after(block, *waits), 'grp', [(0, 1), (1, 0)]))]
    ppermute x9, starting transfers between devices: 22.1 us -> 28.2 us  [outer(): outs.append(lax.ppermute(after(block, *waits), 'ex', outer_pairs))]
    ppermute x9, waiting for transfers between devices: 14 us -> 11.4 us  [outer(): outs.append(lax.ppermute(after(block, *waits), 'ex', outer_pairs))]
    ppermute x1, starting transfers between devices: 0.33 us -> 2.09 us  [line(): back = lax.ppermute(sum_over_feat(far), 'ex', outer_pairs)]
  transfers between devices with their start and end apart: 30 -> 30, of which waited for: 16 -> 14; matrix products, arithmetic and copies ran while one was open for 7% -> 7% of each run, Pallas kernels for 12% -> 12%
where the time goes in v25:
time: 90.2 us; the launch traced here: 90 us
  starting transfers between devices  49.3 us (55%)
  waiting for transfers between devices  19.8 us (22%)
  Pallas kernels  11.2 us (12%)
  local copies, waits for them, and re-layouts  4.9 us (5%)
  other arithmetic  4.33 us (5%)
    ppermute x9, starting transfers between devices, outer(): outs.append(lax.ppermute(after(block, *waits), 'ex', outer_pairs))  28.2 us
    ppermute x9, starting transfers between devices, swap(): swaps.append(lax.ppermute(after(block, *waits), 'grp', [(0, 1), (1, 0)]))  15 us
    ppermute x9, waiting for transfers between devices, outer(): outs.append(lax.ppermute(after(block, *waits), 'ex', outer_pairs))  11.4 us
    pallas_call x12, Pallas kernels, call(): pl.pallas_call(kernel, out_shape=shapes or jax.ShapeDtypeStruct((rows, do...  11.2 us
    ppermute x4, waiting for transfers between devices, sum_over_feat(): held, waits = (pairs[:, 0] + lax.ppermute(send, 'feat', partner), ())  5.06 us
    slice x1, local copies, waits for them, and re-layouts, line(): trains = [train[:, q * 4 * unit:(q + 1) * 4 * unit] for q in range(4)]  4.08 us
    select_n x3, other arithmetic, share(): return jnp.where(first_grp, rows[:half, here], rows[half:, here])  3.33 us
    ppermute x4, starting transfers between devices, sum_over_feat(): held, waits = (pairs[:, 0] + lax.ppermute(send, 'feat', partner), ())  3.2 us
  transfers between devices with their start and end apart: 30, of which 14 were waited for; matrix products, arithmetic and copies ran while one was open for 7% of the time, Pallas kernels for 12%

profile of v25, /device:TPU:0, one launch (start us, length us, event | category | flops | bytes accessed | tf_op | source)
XLA Modules:
  0.0 90.0 jit_solution(10234226469118954234)
XLA Ops:
  0.0 1.1 %slice_select_fusion.2 = bf16[32,5120]{1,0:T(8,128)(2,1)S(1)} fusion(bf16[64,16384]{1,0:T(8,128)(2,1)} %test.2, pred[]{:T(512)S(6)} %eq.11), kind=kLoop, calls=%fused_computation.2 | loop fusion | flops 163840 | bytes 983041 | tf_op jit(solution)/shard_map/jit(_where)/select_n | solution.py:261
  1.6 4.1 %collective-permute-start = (bf16[32,5120]{1,0:T(8,128)(2,1)S(1)}, bf16[32,5120]{1,0:T(8,128)(2,1)S(1)}, u32[]{:S(2)}, u32[]{:S(2)}) collective-permute-start(bf16[32,5120]{1,0:T(8,128)(2,1)S(1)} %slice_select_fusion.2), channel_id=1, source_target_pairs={{0,4},{4,0},{8,12},{12,8},{1,5},{5,1},{9,13},{13,9},{2,6},{6,2},{1... | collective-permute-start | bytes 983048 | tf_op jit(solution)/shard_map/ppermute | solution.py:230
  5.8 1.1 %slice_select_fusion.1 = bf16[32,5120]{1,0:T(8,128)(2,1)S(1)} fusion(bf16[64,16384]{1,0:T(8,128)(2,1)} %test.2, pred[]{:T(512)S(6)} %eq.11), kind=kLoop, calls=%fused_computation.1 | loop fusion | flops 163840 | bytes 983041 | tf_op jit(solution)/shard_map/jit(_where)/select_n | solution.py:261
  7.0 1.1 %slice_select_fusion = bf16[32,5120]{1,0:T(8,128)(2,1)S(1)} fusion(bf16[64,16384]{1,0:T(8,128)(2,1)} %test.2, pred[]{:T(512)S(6)} %eq.11), kind=kLoop, calls=%fused_computation | loop fusion | flops 163840 | bytes 983041 | tf_op jit(solution)/shard_map/jit(_where)/select_n | solution.py:261
  8.1 4.1 %fusion.10 = (bf16[256,4096]{1,0:T(8,128)(2,1)S(1)}, bf16[256,4096]{1,0:T(8,128)(2,1)S(1)}, bf16[256,4096]{1,0:T(8,128)(2,1)S(1)}, bf16[256,4096]{1,0:T(8,128)(2,1)S(1)}) fusion(bf16[256,16384]{1,0:T(8,128)(2,1)} %param.3), kind=kLoop, calls=%fused_computation.31 | loop fusion | bytes 16777216 | tf_op jit(solution)/shard_map/slice | solution.py:268
  13.1 1.2 %collective-permute-done.refs_0_ = bf16[32,5120]{1,0:T(8,128)(2,1)S(1)} collective-permute-done((bf16[32,5120]{1,0:T(8,128)(2,1)S(1)}, bf16[32,5120]{1,0:T(8,128)(2,1)S(1)}, u32[]{:S(2)}, u32[]{:S(2)}) %collective-permute-start) | collective-permute-done | bytes 327712 | tf_op jit(solution)/shard_map/ppermute | solution.py:230
  14.4 2.1 %collective-permute-start.1 = (bf16[32,5120]{1,0:T(8,128)(2,1)S(1)}, bf16[32,5120]{1,0:T(8,128)(2,1)S(1)}, u32[]{:S(2)}, u32[]{:S(2)}) collective-permute-start(bf16[32,5120]{1,0:T(8,128)(2,1)S(1)} %slice_select_fusion), channel_id=1, source_target_pairs={{0,4},{4,0},{8,12},{12,8},{1,5},{5,1},{9,13},{13,9},{2,6},{6,2},{1... | collective-permute-start | bytes 983048 | tf_op jit(solution)/shard_map/ppermute | solution.py:230
  16.4 1.5 %collective-permute-start.5 = (bf16[32,5120]{1,0:T(8,128)(2,1)S(1)}, bf16[32,5120]{1,0:T(8,128)(2,1)S(1)}, u32[]{:S(2)}, u32[]{:S(2)}) collective-permute-start(bf16[32,5120]{1,0:T(8,128)(2,1)S(1)} %collective-permute-done.refs_0_), channel_id=1, source_target_pairs={{0,16},{16,0},{1,17},{17,1},{2,18},{18,2},{3,19},{19,3},{4,20},{20... | collective-permute-start | bytes 983048 | tf_op jit(solution)/shard_map/ppermute | solution.py:243
  18.0 3.4 %collective-permute-done.2.refs_0_ = bf16[32,5120]{1,0:T(8,128)(2,1)S(1)} collective-permute-done((bf16[32,5120]{1,0:T(8,128)(2,1)S(1)}, bf16[32,5120]{1,0:T(8,128)(2,1)S(1)}, u32[]{:S(2)}, u32[]{:S(2)}) %collective-permute-start.2) | collective-permute-done | bytes 327712 | tf_op jit(solution)/shard_map/ppermute | solution.py:230
  21.4 2.1 %collective-permute-start.11 = (bf16[32,5120]{1,0:T(8,128)(2,1)S(1)}, bf16[32,5120]{1,0:T(8,128)(2,1)S(1)}, u32[]{:S(2)}, u32[]{:S(2)}) collective-permute-start(bf16[32,5120]{1,0:T(8,128)(2,1)S(1)} %broadcast_select_fusion.7), channel_id=1, source_target_pairs={{0,4},{4,0},{8,12},{12,8},{1,5},{5,1},{9,13},{13,9},{2,6},{6,2},{1... | collective-permute-start | bytes 983048 | tf_op jit(solution)/shard_map/ppermute | solution.py:230
  23.4 1.5 %collective-permute-start.7 = (bf16[32,5120]{1,0:T(8,128)(2,1)S(1)}, bf16[32,5120]{1,0:T(8,128)(2,1)S(1)}, u32[]{:S(2)}, u32[]{:S(2)}) collective-permute-start(bf16[32,5120]{1,0:T(8,128)(2,1)S(1)} %collective-permute-done.2.refs_0_), channel_id=1, source_target_pairs={{0,16},{16,0},{1,17},{17,1},{2,18},{18,2},{3,19},{19,3},{4,20},{20... | collective-permute-start | bytes 983048 | tf_op jit(solution)/shard_map/ppermute | solution.py:243
  25.0 2.5 %shard_map.39.refs_6_ = f32[64,256]{1,0:T(8,128)S(1)} custom-call(bf16[64,16384]{1,0:T(8,128)(2,1)S(1)} %copy-done, f32[1,16384]{1,0:T(1,128)S(1)} %bitcast.61, bf16[256,4096]{1,0:T(8,128)(2,1)S(1)} %get-tuple-element.70.refs_3_.refs_0_, bf16[256,4096]{1,0:T(8,128)(2,1)S(1)} %get-tuple-element.72.refs_4_.refs_1_.refs_3_, ...), custom_call_target="tpu_custom_call" | custom-call | flops 536870912 | bytes 10485760 | tf_op jit(solution)/shard_map/pallas_call | solution.py:191
  28.4 1.6 %collective-permute-start.9 = (bf16[32,5120]{1,0:T(8,128)(2,1)S(1)}, bf16[32,5120]{1,0:T(8,128)(2,1)S(1)}, u32[]{:S(2)}, u32[]{:S(2)}) collective-permute-start(bf16[32,5120]{1,0:T(8,128)(2,1)S(1)} %collective-permute-done.1.refs_0_), channel_id=1, source_target_pairs={{0,16},{16,0},{1,17},{17,1},{2,18},{18,2},{3,19},{19,3},{4,20},{20... | collective-permute-start | bytes 983048 | tf_op jit(solution)/shard_map/ppermute | solution.py:243
  30.9 2.5 %collective-permute-start.14 = (bf16[32,5120]{1,0:T(8,128)(2,1)S(1)}, bf16[32,5120]{1,0:T(8,128)(2,1)S(1)}, u32[]{:S(2)}, u32[]{:S(2)}) collective-permute-start(bf16[32,5120]{1,0:T(8,128)(2,1)S(1)} %broadcast_select_fusion.5), channel_id=1, source_target_pairs={{0,4},{4,0},{8,12},{12,8},{1,5},{5,1},{9,13},{13,9},{2,6},{6,2},{1... | collective-permute-start | bytes 983048 | tf_op jit(solution)/shard_map/ppermute | solution.py:230
  33.4 1.6 %collective-permute-done.11.refs_0_ = bf16[32,5120]{1,0:T(8,128)(2,1)S(1)} collective-permute-done((bf16[32,5120]{1,0:T(8,128)(2,1)S(1)}, bf16[32,5120]{1,0:T(8,128)(2,1)S(1)}, u32[]{:S(2)}, u32[]{:S(2)}) %collective-permute-start.11) | collective-permute-done | bytes 327712 | tf_op jit(solution)/shard_map/ppermute | solution.py:230
  35.0 2.0 %collective-permute-start.12 = (bf16[32,5120]{1,0:T(8,128)(2,1)S(1)}, bf16[32,5120]{1,0:T(8,128)(2,1)S(1)}, u32[]{:S(2)}, u32[]{:S(2)}) collective-permute-start(bf16[32,5120]{1,0:T(8,128)(2,1)S(1)} %broadcast_select_fusion.6.refs_0_), channel_id=1, source_target_pairs={{0,16},{16,0},{1,17},{17,1},{2,18},{18,2},{3,19},{19,3},{4,20},{20... | collective-permute-start | bytes 983048 | tf_op jit(solution)/shard_map/ppermute | solution.py:243
  38.1 2.5 %collective-permute-start.18 = (bf16[32,5120]{1,0:T(8,128)(2,1)S(1)}, bf16[32,5120]{1,0:T(8,128)(2,1)S(1)}, u32[]{:S(2)}, u32[]{:S(2)}) collective-permute-start(bf16[32,5120]{1,0:T(8,128)(2,1)S(1)} %collective-permute-done.6), channel_id=1, source_target_pairs={{0,4},{4,0},{8,12},{12,8},{1,5},{5,1},{9,13},{13,9},{2,6},{6,2},{1... | collective-permute-start | bytes 983048 | tf_op jit(solution)/shard_map/ppermute | solution.py:230
  40.6 1.5 %collective-permute-done.14.refs_1_ = bf16[32,5120]{1,0:T(8,128)(2,1)S(1)} collective-permute-done((bf16[32,5120]{1,0:T(8,128)(2,1)S(1)}, bf16[32,5120]{1,0:T(8,128)(2,1)S(1)}, u32[]{:S(2)}, u32[]{:S(2)}) %collective-permute-start.14) | collective-permute-done | bytes 327712 | tf_op jit(solution)/shard_map/ppermute | solution.py:230
  42.1 2.0 %collective-permute-start.16 = (bf16[32,5120]{1,0:T(8,128)(2,1)S(1)}, bf16[32,5120]{1,0:T(8,128)(2,1)S(1)}, u32[]{:S(2)}, u32[]{:S(2)}) collective-permute-start(bf16[32,5120]{1,0:T(8,128)(2,1)S(1)} %broadcast_select_fusion.4.refs_0_), channel_id=1, source_target_pairs={{0,16},{16,0},{1,17},{17,1},{2,18},{18,2},{3,19},{19,3},{4,20},{20... | collective-permute-start | bytes 983048 | tf_op jit(solution)/shard_map/ppermute | solution.py:243
  47.0 3.8 %collective-permute-start.15 = (bf16[32,5120]{1,0:T(8,128)(2,1)S(1)}, bf16[32,5120]{1,0:T(8,128)(2,1)S(1)}, u32[]{:S(2)}, u32[]{:S(2)}) collective-permute-start(bf16[32,5120]{1,0:T(8,128)(2,1)S(1)} %collective-permute-done.8), channel_id=1, source_target_pairs={{0,4},{4,0},{8,12},{12,8},{1,5},{5,1},{9,13},{13,9},{2,6},{6,2},{1... | collective-permute-start | bytes 983048 | tf_op jit(solution)/shard_map/ppermute | solution.py:230
  50.8 1.6 %collective-permute-start.19 = (bf16[32,5120]{1,0:T(8,128)(2,1)S(1)}, bf16[32,5120]{1,0:T(8,128)(2,1)S(1)}, u32[]{:S(2)}, u32[]{:S(2)}) collective-permute-start(bf16[32,5120]{1,0:T(8,128)(2,1)S(1)} %broadcast_select_fusion.2.refs_0_), channel_id=1, source_target_pairs={{0,16},{16,0},{1,17},{17,1},{2,18},{18,2},{3,19},{19,3},{4,20},{20... | collective-permute-start | bytes 983048 | tf_op jit(solution)/shard_map/ppermute | solution.py:243
  54.0 5.3 %collective-permute-start.22 = (bf16[32,5120]{1,0:T(8,128)(2,1)S(1)}, bf16[32,5120]{1,0:T(8,128)(2,1)S(1)}, u32[]{:S(2)}, u32[]{:S(2)}) collective-permute-start(bf16[32,5120]{1,0:T(8,128)(2,1)S(1)} %collective-permute-done.10), channel_id=1, source_target_pairs={{0,4},{4,0},{8,12},{12,8},{1,5},{5,1},{9,13},{13,9},{2,6},{6,2},{1... | collective-permute-start | bytes 983048 | tf_op jit(solution)/shard_map/ppermute | solution.py:230
  59.3 1.6 %collective-permute-start.24 = (bf16[32,5120]{1,0:T(8,128)(2,1)S(1)}, bf16[32,5120]{1,0:T(8,128)(2,1)S(1)}, u32[]{:S(2)}, u32[]{:S(2)}) collective-permute-start(bf16[32,5120]{1,0:T(8,128)(2,1)S(1)} %broadcast_select_fusion.refs_0_), channel_id=1, source_target_pairs={{0,16},{16,0},{1,17},{17,1},{2,18},{18,2},{3,19},{19,3},{4,20},{20... | collective-permute-start | bytes 983048 | tf_op jit(solution)/shard_map/ppermute | solution.py:243
  62.3 5.9 %collective-permute-start.17 = (bf16[32,5120]{1,0:T(8,128)(2,1)S(1)}, bf16[32,5120]{1,0:T(8,128)(2,1)S(1)}, u32[]{:S(2)}, u32[]{:S(2)}) collective-permute-start(bf16[32,5120]{1,0:T(8,128)(2,1)S(1)} %collective-permute-done.13), channel_id=1, source_target_pairs={{0,4},{4,0},{8,12},{12,8},{1,5},{5,1},{9,13},{13,9},{2,6},{6,2},{1... | collective-permute-start | bytes 983048 | tf_op jit(solution)/shard_map/ppermute | solution.py:230
  68.2 1.6 %collective-permute-start.23 = (bf16[32,5120]{1,0:T(8,128)(2,1)S(1)}, bf16[32,5120]{1,0:T(8,128)(2,1)S(1)}, u32[]{:S(2)}, u32[]{:S(2)}) collective-permute-start(bf16[32,5120]{1,0:T(8,128)(2,1)S(1)} %broadcast_select_fusion.1.refs_0_), channel_id=1, source_target_pairs={{0,16},{16,0},{1,17},{17,1},{2,18},{18,2},{3,19},{19,3},{4,20},{20... | collective-permute-start | bytes 983048 | tf_op jit(solution)/shard_map/ppermute | solution.py:243
  70.5 2.8 %collective-permute-done.17 = bf16[32,5120]{1,0:T(8,128)(2,1)S(1)} collective-permute-done((bf16[32,5120]{1,0:T(8,128)(2,1)S(1)}, bf16[32,5120]{1,0:T(8,128)(2,1)S(1)}, u32[]{:S(2)}, u32[]{:S(2)}) %collective-permute-start.17) | collective-permute-done | bytes 327712 | tf_op jit(solution)/shard_map/ppermute | solution.py:230
  73.3 1.6 %collective-permute-start.20 = (bf16[32,5120]{1,0:T(8,128)(2,1)S(1)}, bf16[32,5120]{1,0:T(8,128)(2,1)S(1)}, u32[]{:S(2)}, u32[]{:S(2)}) collective-permute-start(bf16[32,5120]{1,0:T(8,128)(2,1)S(1)} %broadcast_select_fusion.3.refs_0_), channel_id=1, source_target_pairs={{0,16},{16,0},{1,17},{17,1},{2,18},{18,2},{3,19},{19,3},{4,20},{20... | collective-permute-start | bytes 983048 | tf_op jit(solution)/shard_map/ppermute | solution.py:243
  74.9 1.6 %collective-permute-start.26 = (f32[1,64,256]{2,1,0:T(8,128)S(1)}, f32[1,64,256]{2,1,0:T(8,128)S(1)}, u32[]{:S(2)}, u32[]{:S(2)}) collective-permute-start(f32[1,64,256]{2,1,0:T(8,128)S(1)} %slice_bitcast_fusion.6), channel_id=1, source_target_pairs={{0,2},{1,3},{2,0},{3,1},{4,6},{5,7},{6,4},{7,5},{8,10},{9,11},{10,... | collective-permute-start | bytes 196616 | tf_op jit(solution)/shard_map/ppermute | solution.py:253
  79.3 2.1 %collective-permute-start.27 = (f32[64,256]{1,0:T(8,128)S(1)}, f32[64,256]{1,0:T(8,128)S(1)}, u32[]{:S(2)}, u32[]{:S(2)}) collective-permute-start(f32[64,256]{1,0:T(8,128)S(1)} %fusion.9), channel_id=1, source_target_pairs={{0,4},{4,0},{8,12},{12,8},{1,5},{5,1},{9,13},{13,9},{2,6},{6,2},{1... | collective-permute-start | bytes 196616 | tf_op jit(solution)/shard_map/ppermute | solution.py:321
  83.6 1.3 %collective-permute-done.28 = f32[2,64,256]{2,1,0:T(8,128)S(1)} collective-permute-done((f32[2,64,256]{2,1,0:T(8,128)S(1)}, f32[2,64,256]{2,1,0:T(8,128)S(1)}, u32[]{:S(2)}, u32[]{:S(2)}) %collective-permute-start.28) | collective-permute-done | bytes 131104 | tf_op jit(solution)/shard_map/ppermute | solution.py:253
  85.0 1.6 %collective-permute-start.29 = (f32[1,64,256]{2,1,0:T(8,128)S(1)}, f32[1,64,256]{2,1,0:T(8,128)S(1)}, u32[]{:S(2)}, u32[]{:S(2)}) collective-permute-start(f32[1,64,256]{2,1,0:T(8,128)S(1)} %slice_bitcast_fusion.4), channel_id=1, source_target_pairs={{0,2},{1,3},{2,0},{3,1},{4,6},{5,7},{6,4},{7,5},{8,10},{9,11},{10,... | collective-permute-start | bytes 196616 | tf_op jit(solution)/shard_map/ppermute | solution.py:253
  86.5 2.8 %collective-permute-done.29 = f32[1,64,256]{2,1,0:T(8,128)S(1)} collective-permute-done((f32[1,64,256]{2,1,0:T(8,128)S(1)}, f32[1,64,256]{2,1,0:T(8,128)S(1)}, u32[]{:S(2)}, u32[]{:S(2)}) %collective-permute-start.29) | collective-permute-done | bytes 65568 | tf_op jit(solution)/shard_map/ppermute | solution.py:253
  (67 shorter events, 16.9 us)
Async XLA Ops:
  1.1 11.9 %collective-permute-start.3 = (bf16[32,5120]{1,0:T(8,128)(2,1)S(1)}, bf16[32,5120]{1,0:T(8,128)(2,1)S(1)}, u32[]{:S(2)}, u32[]{:S(2)}) collective-permute-start(bf16[32,5120]{1,0:T(8,128)(2,1)S(1)} %slice_select_fusion.2), channel_id=1, source_target_pairs={{0,1},{1,0},{2,3},{3,2},{4,8},{5,9},{6,10},{7,11},{8,4},{9,5},{10,... | collective-permute-start | bytes 983048 | tf_op jit(solution)/shard_map/ppermute | solution.py:234
  1.6 12.7 %collective-permute-start = (bf16[32,5120]{1,0:T(8,128)(2,1)S(1)}, bf16[32,5120]{1,0:T(8,128)(2,1)S(1)}, u32[]{:S(2)}, u32[]{:S(2)}) collective-permute-start(bf16[32,5120]{1,0:T(8,128)(2,1)S(1)} %slice_select_fusion.2), channel_id=1, source_target_pairs={{0,4},{4,0},{8,12},{12,8},{1,5},{5,1},{9,13},{13,9},{2,6},{6,2},{1... | collective-permute-start | bytes 983048 | tf_op jit(solution)/shard_map/ppermute | solution.py:230
  6.9 14.5 %collective-permute-start.2 = (bf16[32,5120]{1,0:T(8,128)(2,1)S(1)}, bf16[32,5120]{1,0:T(8,128)(2,1)S(1)}, u32[]{:S(2)}, u32[]{:S(2)}) collective-permute-start(bf16[32,5120]{1,0:T(8,128)(2,1)S(1)} %slice_select_fusion.1), channel_id=1, source_target_pairs={{0,4},{4,0},{8,12},{12,8},{1,5},{5,1},{9,13},{13,9},{2,6},{6,2},{1... | collective-permute-start | bytes 983048 | tf_op jit(solution)/shard_map/ppermute | solution.py:230
  8.1 4.1 %copy-start = (bf16[64,16384]{1,0:T(8,128)(2,1)S(1)}, bf16[64,16384]{1,0:T(8,128)(2,1)}, u32[]{:S(2)}) copy-start(bf16[64,16384]{1,0:T(8,128)(2,1)} %test.2) | copy-start | bytes 6291460
  12.2 0.8 copy-start.1
  13.1 15.3 %collective-permute-start.4 = (bf16[32,5120]{1,0:T(8,128)(2,1)S(1)}, bf16[32,5120]{1,0:T(8,128)(2,1)S(1)}, u32[]{:S(2)}, u32[]{:S(2)}) collective-permute-start(bf16[32,5120]{1,0:T(8,128)(2,1)S(1)} %slice_select_fusion.1), channel_id=1, source_target_pairs={{0,1},{1,0},{2,3},{3,2},{4,8},{5,9},{6,10},{7,11},{8,4},{9,5},{10,... | collective-permute-start | bytes 983048 | tf_op jit(solution)/shard_map/ppermute | solution.py:234
  14.4 14.0 %collective-permute-start.1 = (bf16[32,5120]{1,0:T(8,128)(2,1)S(1)}, bf16[32,5120]{1,0:T(8,128)(2,1)S(1)}, u32[]{:S(2)}, u32[]{:S(2)}) collective-permute-start(bf16[32,5120]{1,0:T(8,128)(2,1)S(1)} %slice_select_fusion), channel_id=1, source_target_pairs={{0,4},{4,0},{8,12},{12,8},{1,5},{5,1},{9,13},{13,9},{2,6},{6,2},{1... | collective-permute-start | bytes 983048 | tf_op jit(solution)/shard_map/ppermute | solution.py:230
  16.4 12.0 %collective-permute-start.5 = (bf16[32,5120]{1,0:T(8,128)(2,1)S(1)}, bf16[32,5120]{1,0:T(8,128)(2,1)S(1)}, u32[]{:S(2)}, u32[]{:S(2)}) collective-permute-start(bf16[32,5120]{1,0:T(8,128)(2,1)S(1)} %collective-permute-done.refs_0_), channel_id=1, source_target_pairs={{0,16},{16,0},{1,17},{17,1},{2,18},{18,2},{3,19},{19,3},{4,20},{20... | collective-permute-start | bytes 983048 | tf_op jit(solution)/shard_map/ppermute | solution.py:243
  21.4 13.6 %collective-permute-start.11 = (bf16[32,5120]{1,0:T(8,128)(2,1)S(1)}, bf16[32,5120]{1,0:T(8,128)(2,1)S(1)}, u32[]{:S(2)}, u32[]{:S(2)}) collective-permute-start(bf16[32,5120]{1,0:T(8,128)(2,1)S(1)} %broadcast_select_fusion.7), channel_id=1, source_target_pairs={{0,4},{4,0},{8,12},{12,8},{1,5},{5,1},{9,13},{13,9},{2,6},{6,2},{1... | collective-permute-start | bytes 983048 | tf_op jit(solution)/shard_map/ppermute | solution.py:230
  23.4 11.6 %collective-permute-start.7 = (bf16[32,5120]{1,0:T(8,128)(2,1)S(1)}, bf16[32,5120]{1,0:T(8,128)(2,1)S(1)}, u32[]{:S(2)}, u32[]{:S(2)}) collective-permute-start(bf16[32,5120]{1,0:T(8,128)(2,1)S(1)} %collective-permute-done.2.refs_0_), channel_id=1, source_target_pairs={{0,16},{16,0},{1,17},{17,1},{2,18},{18,2},{3,19},{19,3},{4,20},{20... | collective-permute-start | bytes 983048 | tf_op jit(solution)/shard_map/ppermute | solution.py:243
  28.4 9.6 %collective-permute-start.6 = (bf16[32,5120]{1,0:T(8,128)(2,1)S(1)}, bf16[32,5120]{1,0:T(8,128)(2,1)S(1)}, u32[]{:S(2)}, u32[]{:S(2)}) collective-permute-start(bf16[32,5120]{1,0:T(8,128)(2,1)S(1)} %slice_select_fusion), channel_id=1, source_target_pairs={{0,1},{1,0},{2,3},{3,2},{4,8},{5,9},{6,10},{7,11},{8,4},{9,5},{10,... | collective-permute-start | bytes 983048 | tf_op jit(solution)/shard_map/ppermute | solution.py:234
  28.4 13.7 %collective-permute-start.9 = (bf16[32,5120]{1,0:T(8,128)(2,1)S(1)}, bf16[32,5120]{1,0:T(8,128)(2,1)S(1)}, u32[]{:S(2)}, u32[]{:S(2)}) collective-permute-start(bf16[32,5120]{1,0:T(8,128)(2,1)S(1)} %collective-permute-done.1.refs_0_), channel_id=1, source_target_pairs={{0,16},{16,0},{1,17},{17,1},{2,18},{18,2},{3,19},{19,3},{4,20},{20... | collective-permute-start | bytes 983048 | tf_op jit(solution)/shard_map/ppermute | solution.py:243
  30.9 11.1 %collective-permute-start.14 = (bf16[32,5120]{1,0:T(8,128)(2,1)S(1)}, bf16[32,5120]{1,0:T(8,128)(2,1)S(1)}, u32[]{:S(2)}, u32[]{:S(2)}) collective-permute-start(bf16[32,5120]{1,0:T(8,128)(2,1)S(1)} %broadcast_select_fusion.5), channel_id=1, source_target_pairs={{0,4},{4,0},{8,12},{12,8},{1,5},{5,1},{9,13},{13,9},{2,6},{6,2},{1... | collective-permute-start | bytes 983048 | tf_op jit(solution)/shard_map/ppermute | solution.py:230
  35.0 11.0 %collective-permute-start.12 = (bf16[32,5120]{1,0:T(8,128)(2,1)S(1)}, bf16[32,5120]{1,0:T(8,128)(2,1)S(1)}, u32[]{:S(2)}, u32[]{:S(2)}) collective-permute-start(bf16[32,5120]{1,0:T(8,128)(2,1)S(1)} %broadcast_select_fusion.6.refs_0_), channel_id=1, source_target_pairs={{0,16},{16,0},{1,17},{17,1},{2,18},{18,2},{3,19},{19,3},{4,20},{20... | collective-permute-start | bytes 983048 | tf_op jit(solution)/shard_map/ppermute | solution.py:243
  38.0 8.9 %collective-permute-start.8 = (bf16[32,5120]{1,0:T(8,128)(2,1)S(1)}, bf16[32,5120]{1,0:T(8,128)(2,1)S(1)}, u32[]{:S(2)}, u32[]{:S(2)}) collective-permute-start(bf16[32,5120]{1,0:T(8,128)(2,1)S(1)} %collective-permute-done.refs_0_), channel_id=1, source_target_pairs={{0,1},{1,0},{2,3},{3,2},{4,8},{5,9},{6,10},{7,11},{8,4},{9,5},{10,... | collective-permute-start | bytes 983048 | tf_op jit(solution)/shard_map/ppermute | solution.py:234
  38.1 12.7 %collective-permute-start.18 = (bf16[32,5120]{1,0:T(8,128)(2,1)S(1)}, bf16[32,5120]{1,0:T(8,128)(2,1)S(1)}, u32[]{:S(2)}, u32[]{:S(2)}) collective-permute-start(bf16[32,5120]{1,0:T(8,128)(2,1)S(1)} %collective-permute-done.6), channel_id=1, source_target_pairs={{0,4},{4,0},{8,12},{12,8},{1,5},{5,1},{9,13},{13,9},{2,6},{6,2},{1... | collective-permute-start | bytes 983048 | tf_op jit(solution)/shard_map/ppermute | solution.py:230
  42.1 11.0 %collective-permute-start.16 = (bf16[32,5120]{1,0:T(8,128)(2,1)S(1)}, bf16[32,5120]{1,0:T(8,128)(2,1)S(1)}, u32[]{:S(2)}, u32[]{:S(2)}) collective-permute-start(bf16[32,5120]{1,0:T(8,128)(2,1)S(1)} %broadcast_select_fusion.4.refs_0_), channel_id=1, source_target_pairs={{0,16},{16,0},{1,17},{17,1},{2,18},{18,2},{3,19},{19,3},{4,20},{20... | collective-permute-start | bytes 983048 | tf_op jit(solution)/shard_map/ppermute | solution.py:243
  46.9 7.0 %collective-permute-start.10 = (bf16[32,5120]{1,0:T(8,128)(2,1)S(1)}, bf16[32,5120]{1,0:T(8,128)(2,1)S(1)}, u32[]{:S(2)}, u32[]{:S(2)}) collective-permute-start(bf16[32,5120]{1,0:T(8,128)(2,1)S(1)} %collective-permute-done.2.refs_0_), channel_id=1, source_target_pairs={{0,1},{1,0},{2,3},{3,2},{4,8},{5,9},{6,10},{7,11},{8,4},{9,5},{10,... | collective-permute-start | bytes 983048 | tf_op jit(solution)/shard_map/ppermute | solution.py:234
  47.0 12.3 %collective-permute-start.15 = (bf16[32,5120]{1,0:T(8,128)(2,1)S(1)}, bf16[32,5120]{1,0:T(8,128)(2,1)S(1)}, u32[]{:S(2)}, u32[]{:S(2)}) collective-permute-start(bf16[32,5120]{1,0:T(8,128)(2,1)S(1)} %collective-permute-done.8), channel_id=1, source_target_pairs={{0,4},{4,0},{8,12},{12,8},{1,5},{5,1},{9,13},{13,9},{2,6},{6,2},{1... | collective-permute-start | bytes 983048 | tf_op jit(solution)/shard_map/ppermute | solution.py:230
  50.8 10.5 %collective-permute-start.19 = (bf16[32,5120]{1,0:T(8,128)(2,1)S(1)}, bf16[32,5120]{1,0:T(8,128)(2,1)S(1)}, u32[]{:S(2)}, u32[]{:S(2)}) collective-permute-start(bf16[32,5120]{1,0:T(8,128)(2,1)S(1)} %broadcast_select_fusion.2.refs_0_), channel_id=1, source_target_pairs={{0,16},{16,0},{1,17},{17,1},{2,18},{18,2},{3,19},{19,3},{4,20},{20... | collective-permute-start | bytes 983048 | tf_op jit(solution)/shard_map/ppermute | solution.py:243
  54.0 8.3 %collective-permute-start.13 = (bf16[32,5120]{1,0:T(8,128)(2,1)S(1)}, bf16[32,5120]{1,0:T(8,128)(2,1)S(1)}, u32[]{:S(2)}, u32[]{:S(2)}) collective-permute-start(bf16[32,5120]{1,0:T(8,128)(2,1)S(1)} %collective-permute-done.1.refs_0_), channel_id=1, source_target_pairs={{0,1},{1,0},{2,3},{3,2},{4,8},{5,9},{6,10},{7,11},{8,4},{9,5},{10,... | collective-permute-start | bytes 983048 | tf_op jit(solution)/shard_map/ppermute | solution.py:234
  54.0 14.2 %collective-permute-start.22 = (bf16[32,5120]{1,0:T(8,128)(2,1)S(1)}, bf16[32,5120]{1,0:T(8,128)(2,1)S(1)}, u32[]{:S(2)}, u32[]{:S(2)}) collective-permute-start(bf16[32,5120]{1,0:T(8,128)(2,1)S(1)} %collective-permute-done.10), channel_id=1, source_target_pairs={{0,4},{4,0},{8,12},{12,8},{1,5},{5,1},{9,13},{13,9},{2,6},{6,2},{1... | collective-permute-start | bytes 983048 | tf_op jit(solution)/shard_map/ppermute | solution.py:230
  59.3 17.1 %collective-permute-start.24 = (bf16[32,5120]{1,0:T(8,128)(2,1)S(1)}, bf16[32,5120]{1,0:T(8,128)(2,1)S(1)}, u32[]{:S(2)}, u32[]{:S(2)}) collective-permute-start(bf16[32,5120]{1,0:T(8,128)(2,1)S(1)} %broadcast_select_fusion.refs_0_), channel_id=1, source_target_pairs={{0,16},{16,0},{1,17},{17,1},{2,18},{18,2},{3,19},{19,3},{4,20},{20... | collective-permute-start | bytes 983048 | tf_op jit(solution)/shard_map/ppermute | solution.py:243
  62.3 7.6 %collective-permute-start.21 = (bf16[64,2048]{1,0:T(8,128)(2,1)S(1)}, bf16[64,2048]{1,0:T(8,128)(2,1)S(1)}, u32[]{:S(2)}, u32[]{:S(2)}) collective-permute-start(bf16[64,2048]{1,0:T(8,128)(2,1)S(1)} %pad_maximum_fusion), channel_id=1, source_target_pairs={{0,1},{1,0},{2,3},{3,2},{4,8},{5,9},{6,10},{7,11},{8,4},{9,5},{10,... | collective-permute-start | bytes 786440 | tf_op jit(solution)/shard_map/ppermute | solution.py:234
  62.3 10.9 %collective-permute-start.17 = (bf16[32,5120]{1,0:T(8,128)(2,1)S(1)}, bf16[32,5120]{1,0:T(8,128)(2,1)S(1)}, u32[]{:S(2)}, u32[]{:S(2)}) collective-permute-start(bf16[32,5120]{1,0:T(8,128)(2,1)S(1)} %collective-permute-done.13), channel_id=1, source_target_pairs={{0,4},{4,0},{8,12},{12,8},{1,5},{5,1},{9,13},{13,9},{2,6},{6,2},{1... | collective-permute-start | bytes 983048 | tf_op jit(solution)/shard_map/ppermute | solution.py:230
  68.2 9.1 %collective-permute-start.23 = (bf16[32,5120]{1,0:T(8,128)(2,1)S(1)}, bf16[32,5120]{1,0:T(8,128)(2,1)S(1)}, u32[]{:S(2)}, u32[]{:S(2)}) collective-permute-start(bf16[32,5120]{1,0:T(8,128)(2,1)S(1)} %broadcast_select_fusion.1.refs_0_), channel_id=1, source_target_pairs={{0,16},{16,0},{1,17},{17,1},{2,18},{18,2},{3,19},{19,3},{4,20},{20... | collective-permute-start | bytes 983048 | tf_op jit(solution)/shard_map/ppermute | solution.py:243
  70.4 4.5 %collective-permute-start.25 = (f32[2,64,256]{2,1,0:T(8,128)S(1)}, f32[2,64,256]{2,1,0:T(8,128)S(1)}, u32[]{:S(2)}, u32[]{:S(2)}) collective-permute-start(f32[2,64,256]{2,1,0:T(8,128)S(1)} %slice_bitcast_fusion), channel_id=1, source_target_pairs={{0,1},{1,0},{2,3},{3,2},{4,5},{5,4},{6,7},{7,6},{8,9},{9,8},{10,11... | collective-permute-start | bytes 393224 | tf_op jit(solution)/shard_map/ppermute | solution.py:253
  73.3 9.1 %collective-permute-start.20 = (bf16[32,5120]{1,0:T(8,128)(2,1)S(1)}, bf16[32,5120]{1,0:T(8,128)(2,1)S(1)}, u32[]{:S(2)}, u32[]{:S(2)}) collective-permute-start(bf16[32,5120]{1,0:T(8,128)(2,1)S(1)} %broadcast_select_fusion.3.refs_0_), channel_id=1, source_target_pairs={{0,16},{16,0},{1,17},{17,1},{2,18},{18,2},{3,19},{19,3},{4,20},{20... | collective-permute-start | bytes 983048 | tf_op jit(solution)/shard_map/ppermute | solution.py:243
  74.9 4.3 %collective-permute-start.26 = (f32[1,64,256]{2,1,0:T(8,128)S(1)}, f32[1,64,256]{2,1,0:T(8,128)S(1)}, u32[]{:S(2)}, u32[]{:S(2)}) collective-permute-start(f32[1,64,256]{2,1,0:T(8,128)S(1)} %slice_bitcast_fusion.6), channel_id=1, source_target_pairs={{0,2},{1,3},{2,0},{3,1},{4,6},{5,7},{6,4},{7,5},{8,10},{9,11},{10,... | collective-permute-start | bytes 196616 | tf_op jit(solution)/shard_map/ppermute | solution.py:253
  79.3 4.3 %collective-permute-start.27 = (f32[64,256]{1,0:T(8,128)S(1)}, f32[64,256]{1,0:T(8,128)S(1)}, u32[]{:S(2)}, u32[]{:S(2)}) collective-permute-start(f32[64,256]{1,0:T(8,128)S(1)} %fusion.9), channel_id=1, source_target_pairs={{0,4},{4,0},{8,12},{12,8},{1,5},{5,1},{9,13},{13,9},{2,6},{6,2},{1... | collective-permute-start | bytes 196616 | tf_op jit(solution)/shard_map/ppermute | solution.py:321
  83.6 1.3 %collective-permute-start.28 = (f32[2,64,256]{2,1,0:T(8,128)S(1)}, f32[2,64,256]{2,1,0:T(8,128)S(1)}, u32[]{:S(2)}, u32[]{:S(2)}) collective-permute-start(f32[2,64,256]{2,1,0:T(8,128)S(1)} %slice_bitcast_fusion.2), channel_id=1, source_target_pairs={{0,1},{1,0},{2,3},{3,2},{4,5},{5,4},{6,7},{7,6},{8,9},{9,8},{10,11... | collective-permute-start | bytes 393224 | tf_op jit(solution)/shard_map/ppermute | solution.py:253
  85.0 4.3 %collective-permute-start.29 = (f32[1,64,256]{2,1,0:T(8,128)S(1)}, f32[1,64,256]{2,1,0:T(8,128)S(1)}, u32[]{:S(2)}, u32[]{:S(2)}) collective-permute-start(f32[1,64,256]{2,1,0:T(8,128)S(1)} %slice_bitcast_fusion.4), channel_id=1, source_target_pairs={{0,2},{1,3},{2,0},{3,1},{4,6},{5,7},{6,4},{7,5},{8,10},{9,11},{10,... | collective-permute-start | bytes 196616 | tf_op jit(solution)/shard_map/ppermute | solution.py:253

commit v26 on v25

--- a/solution.py
+++ b/solution.py
@@ -225,13 +225,13 @@
                 to = (i, f ^ 1) if i in (0, n_ex - 1) else (n_ex - 1 - i, f)
                 middle_pairs.append((i * n_feat + f, to[0] * n_feat + to[1]))
 
-        def outer(name, block):
-            waits = outs[-2:-1] + swaps[-4:-3] + made[-4:-3] + (first if len(outs) == 4 else [])
+        def outer(name, block, *ahead):
+            waits = [*ahead] + outs[-2:-1] + swaps[-4:-3] + made[-4:-3] + (first if len(outs) == 4 else [])
             outs.append(lax.ppermute(after(block, *waits), "ex", outer_pairs))
             done[name] = outs[-1]
 
         def middle(name, block):
-            middles.append(lax.ppermute(after(block, *middles[-1:], *swaps[-2:-1]), ("ex", "feat"), middle_pairs))
+            middles.append(lax.ppermute(after(block, *middles[-1:]), ("ex", "feat"), middle_pairs))
             done[name] = middles[-1]
 
         def swap(block):
@@ -301,14 +301,15 @@
             finish(1, c, done[f"E1{c}"])
         for c in range(n):
             inner = done[f"O1{c}"]
-            outer(f"E2{c}", jnp.where(is_end, cargo[c], inner) if c < len(cargo) else inner)
+            ahead = done[f"O1{c + 1}"] if c + 1 < n else done["O20"]
+            outer(f"E2{c}", jnp.where(is_end, cargo[c], inner) if c < len(cargo) else inner, ahead)
             middle(f"O2{c}", done[f"E1{c}"])
             finish(2, c, jnp.where(is_end, done[f"E2{c}"], inner))
         end_tests = done["E20"][:, : own_tests.shape[1]]
         middle("OS", jnp.concatenate([own_tests, end_tests], axis=0))
         for c in range(n):
             inner = done[f"O2{c}"]
-            outer(f"E3{c}", inner)
+            outer(f"E3{c}", inner, *([done[f"O2{c + 1}"]] if c + 1 < n else []))
             last = finish(3, c, jnp.where(is_end, done[f"E3{c}"], inner))
         shape = jax.ShapeDtypeStruct((n_ex * queries, docs), jnp.float32)
         landed = [done["E20"], done["E21"]]

time: 90.2 us -> 91.7 us (1.017)
  waiting for transfers between devices: 19.8 us -> 21.5 us
  other arithmetic: 4.33 us -> 3.26 us
    ppermute x9, starting transfers between devices: 28.2 us -> 33.6 us  [outer(): outs.append(lax.ppermute(after(block, *waits), 'ex', outer_pairs))]
    ppermute x9, starting transfers between devices: 15 us -> 10.7 us  [swap(): swaps.append(lax.ppermute(after(block, *waits), 'grp', [(0, 1), (1, 0)]))]
    ppermute x9, waiting for transfers between devices: 11.4 us -> 12.6 us  [outer(): outs.append(lax.ppermute(after(block, *waits), 'ex', outer_pairs))]
    select_n x3, other arithmetic: 3.33 us -> 2.25 us  [share(): return jnp.where(first_grp, rows[:half, here], rows[half:, here])]
    ppermute x4, waiting for transfers between devices: 5.06 us -> 5.97 us  [sum_over_feat(): held, waits = (pairs[:, 0] + lax.ppermute(send, 'feat', partner), ())]
  transfers between devices with their start and end apart: 30 -> 30, of which waited for: 14 -> 9; matrix products, arithmetic and copies ran while one was open for 7% -> 6% of each run, Pallas kernels for 12% -> 12%
where the time goes in v26:
time: 91.7 us; the launch traced here: 91.5 us
  starting transfers between devices  50.2 us (55%)
  waiting for transfers between devices  21.5 us (23%)
  Pallas kernels  11.3 us (12%)
  local copies, waits for them, and re-layouts  4.84 us (5%)
  other arithmetic  3.26 us (4%)
    ppermute x9, starting transfers between devices, outer(): outs.append(lax.ppermute(after(block, *waits), 'ex', outer_pairs))  33.6 us
    ppermute x9, waiting for transfers between devices, outer(): outs.append(lax.ppermute(after(block, *waits), 'ex', outer_pairs))  12.6 us
    pallas_call x12, Pallas kernels, call(): pl.pallas_call(kernel, out_shape=shapes or jax.ShapeDtypeStruct((rows, do...  11.3 us
    ppermute x9, starting transfers between devices, swap(): swaps.append(lax.ppermute(after(block, *waits), 'grp', [(0, 1), (1, 0)]))  10.7 us
    ppermute x4, waiting for transfers between devices, sum_over_feat(): held, waits = (pairs[:, 0] + lax.ppermute(send, 'feat', partner), ())  5.97 us
    slice x1, local copies, waits for them, and re-layouts, line(): trains = [train[:, q * 4 * unit:(q + 1) * 4 * unit] for q in range(4)]  4.07 us
    ppermute x4, starting transfers between devices, sum_over_feat(): held, waits = (pairs[:, 0] + lax.ppermute(send, 'feat', partner), ())  3.26 us
    ppermute x9, waiting for transfers between devices, swap(): swaps.append(lax.ppermute(after(block, *waits), 'grp', [(0, 1), (1, 0)]))  2.95 us
  transfers between devices with their start and end apart: 30, of which 9 were waited for; matrix products, arithmetic and copies ran while one was open for 6% of the time, Pallas kernels for 12%

profile of v26, /device:TPU:0, one launch (start us, length us, event | category | flops | bytes accessed | tf_op | source)
XLA Modules:
  0.0 91.5 jit_solution(1864772261592273016)
XLA Ops:
  0.0 1.1 %slice_select_fusion.2 = bf16[32,5120]{1,0:T(8,128)(2,1)S(1)} fusion(bf16[64,16384]{1,0:T(8,128)(2,1)} %test.2, pred[]{:T(512)S(6)} %eq.11), kind=kLoop, calls=%fused_computation.2 | loop fusion | flops 163840 | bytes 983041 | tf_op jit(solution)/shard_map/jit(_where)/select_n | solution.py:261
  1.6 4.1 %collective-permute-start = (bf16[32,5120]{1,0:T(8,128)(2,1)S(1)}, bf16[32,5120]{1,0:T(8,128)(2,1)S(1)}, u32[]{:S(2)}, u32[]{:S(2)}) collective-permute-start(bf16[32,5120]{1,0:T(8,128)(2,1)S(1)} %slice_select_fusion.2), channel_id=1, source_target_pairs={{0,4},{4,0},{8,12},{12,8},{1,5},{5,1},{9,13},{13,9},{2,6},{6,2},{1... | collective-permute-start | bytes 983048 | tf_op jit(solution)/shard_map/ppermute | solution.py:230
  5.8 1.1 %slice_select_fusion.1 = bf16[32,5120]{1,0:T(8,128)(2,1)S(1)} fusion(bf16[64,16384]{1,0:T(8,128)(2,1)} %test.2, pred[]{:T(512)S(6)} %eq.11), kind=kLoop, calls=%fused_computation.1 | loop fusion | flops 163840 | bytes 983041 | tf_op jit(solution)/shard_map/jit(_where)/select_n | solution.py:261
  7.0 4.1 %fusion.10 = (bf16[256,4096]{1,0:T(8,128)(2,1)S(1)}, bf16[256,4096]{1,0:T(8,128)(2,1)S(1)}, bf16[256,4096]{1,0:T(8,128)(2,1)S(1)}, bf16[256,4096]{1,0:T(8,128)(2,1)S(1)}) fusion(bf16[256,16384]{1,0:T(8,128)(2,1)} %param.3), kind=kLoop, calls=%fused_computation.31 | loop fusion | bytes 16777216 | tf_op jit(solution)/shard_map/slice | solution.py:268
  12.0 2.3 %collective-permute-done.refs_0_ = bf16[32,5120]{1,0:T(8,128)(2,1)S(1)} collective-permute-done((bf16[32,5120]{1,0:T(8,128)(2,1)S(1)}, bf16[32,5120]{1,0:T(8,128)(2,1)S(1)}, u32[]{:S(2)}, u32[]{:S(2)}) %collective-permute-start) | collective-permute-done | bytes 327712 | tf_op jit(solution)/shard_map/ppermute | solution.py:230
  14.4 2.1 %collective-permute-start.1 = (bf16[32,5120]{1,0:T(8,128)(2,1)S(1)}, bf16[32,5120]{1,0:T(8,128)(2,1)S(1)}, u32[]{:S(2)}, u32[]{:S(2)}) collective-permute-start(bf16[32,5120]{1,0:T(8,128)(2,1)S(1)} %slice_select_fusion), channel_id=1, source_target_pairs={{0,4},{4,0},{8,12},{12,8},{1,5},{5,1},{9,13},{13,9},{2,6},{6,2},{1... | collective-permute-start | bytes 983048 | tf_op jit(solution)/shard_map/ppermute | solution.py:230
  16.4 1.5 %collective-permute-start.9 = (bf16[32,5120]{1,0:T(8,128)(2,1)S(1)}, bf16[32,5120]{1,0:T(8,128)(2,1)S(1)}, u32[]{:S(2)}, u32[]{:S(2)}) collective-permute-start(bf16[32,5120]{1,0:T(8,128)(2,1)S(1)} %collective-permute-done.refs_0_), channel_id=1, source_target_pairs={{0,16},{16,0},{1,17},{17,1},{2,18},{18,2},{3,19},{19,3},{4,20},{20... | collective-permute-start | bytes 983048 | tf_op jit(solution)/shard_map/ppermute | solution.py:243
  17.9 3.4 %collective-permute-done.2.refs_0_ = bf16[32,5120]{1,0:T(8,128)(2,1)S(1)} collective-permute-done((bf16[32,5120]{1,0:T(8,128)(2,1)S(1)}, bf16[32,5120]{1,0:T(8,128)(2,1)S(1)}, u32[]{:S(2)}, u32[]{:S(2)}) %collective-permute-start.2) | collective-permute-done | bytes 327712 | tf_op jit(solution)/shard_map/ppermute | solution.py:230
  21.4 1.5 %collective-permute-start.12 = (bf16[32,5120]{1,0:T(8,128)(2,1)S(1)}, bf16[32,5120]{1,0:T(8,128)(2,1)S(1)}, u32[]{:S(2)}, u32[]{:S(2)}) collective-permute-start(bf16[32,5120]{1,0:T(8,128)(2,1)S(1)} %collective-permute-done.2.refs_0_), channel_id=1, source_target_pairs={{0,16},{16,0},{1,17},{17,1},{2,18},{18,2},{3,19},{19,3},{4,20},{20... | collective-permute-start | bytes 983048 | tf_op jit(solution)/shard_map/ppermute | solution.py:243
  22.9 2.5 %shard_map.39.refs_6_ = f32[64,256]{1,0:T(8,128)S(1)} custom-call(bf16[64,16384]{1,0:T(8,128)(2,1)S(1)} %copy-done, f32[1,16384]{1,0:T(1,128)S(1)} %bitcast.61, bf16[256,4096]{1,0:T(8,128)(2,1)S(1)} %get-tuple-element.70.refs_3_.refs_0_, bf16[256,4096]{1,0:T(8,128)(2,1)S(1)} %get-tuple-element.72.refs_4_.refs_1_.refs_3_, ...), custom_call_target="tpu_custom_call" | custom-call | flops 536870912 | bytes 10485760 | tf_op jit(solution)/shard_map/pallas_call | solution.py:191
  25.4 2.1 %collective-permute-start.15 = (bf16[32,5120]{1,0:T(8,128)(2,1)S(1)}, bf16[32,5120]{1,0:T(8,128)(2,1)S(1)}, u32[]{:S(2)}, u32[]{:S(2)}) collective-permute-start(bf16[32,5120]{1,0:T(8,128)(2,1)S(1)} %broadcast_select_fusion.5), channel_id=1, source_target_pairs={{0,4},{4,0},{8,12},{12,8},{1,5},{5,1},{9,13},{13,9},{2,6},{6,2},{1... | collective-permute-start | bytes 983048 | tf_op jit(solution)/shard_map/ppermute | solution.py:230
  28.4 1.5 %collective-permute-start.11 = (bf16[32,5120]{1,0:T(8,128)(2,1)S(1)}, bf16[32,5120]{1,0:T(8,128)(2,1)S(1)}, u32[]{:S(2)}, u32[]{:S(2)}) collective-permute-start(bf16[32,5120]{1,0:T(8,128)(2,1)S(1)} %collective-permute-done.1.refs_0_), channel_id=1, source_target_pairs={{0,16},{16,0},{1,17},{17,1},{2,18},{18,2},{3,19},{19,3},{4,20},{20... | collective-permute-start | bytes 983048 | tf_op jit(solution)/shard_map/ppermute | solution.py:243
  31.9 5.5 %collective-permute-start.10 = (bf16[32,5120]{1,0:T(8,128)(2,1)S(1)}, bf16[32,5120]{1,0:T(8,128)(2,1)S(1)}, u32[]{:S(2)}, u32[]{:S(2)}) collective-permute-start(bf16[32,5120]{1,0:T(8,128)(2,1)S(1)} %broadcast_select_fusion.7), channel_id=1, source_target_pairs={{0,4},{4,0},{8,12},{12,8},{1,5},{5,1},{9,13},{13,9},{2,6},{6,2},{1... | collective-permute-start | bytes 983048 | tf_op jit(solution)/shard_map/ppermute | solution.py:230
  39.3 6.0 %collective-permute-start.18 = (bf16[32,5120]{1,0:T(8,128)(2,1)S(1)}, bf16[32,5120]{1,0:T(8,128)(2,1)S(1)}, u32[]{:S(2)}, u32[]{:S(2)}) collective-permute-start(bf16[32,5120]{1,0:T(8,128)(2,1)S(1)} %collective-permute-done.5), channel_id=1, source_target_pairs={{0,4},{4,0},{8,12},{12,8},{1,5},{5,1},{9,13},{13,9},{2,6},{6,2},{1... | collective-permute-start | bytes 983048 | tf_op jit(solution)/shard_map/ppermute | solution.py:230
  47.0 6.6 %collective-permute-start.13 = (bf16[32,5120]{1,0:T(8,128)(2,1)S(1)}, bf16[32,5120]{1,0:T(8,128)(2,1)S(1)}, u32[]{:S(2)}, u32[]{:S(2)}) collective-permute-start(bf16[32,5120]{1,0:T(8,128)(2,1)S(1)} %collective-permute-done.6), channel_id=1, source_target_pairs={{0,4},{4,0},{8,12},{12,8},{1,5},{5,1},{9,13},{13,9},{2,6},{6,2},{1... | collective-permute-start | bytes 983048 | tf_op jit(solution)/shard_map/ppermute | solution.py:230
  53.7 1.0 %collective-permute-start.19 = (bf16[32,5120]{1,0:T(8,128)(2,1)S(1)}, bf16[32,5120]{1,0:T(8,128)(2,1)S(1)}, u32[]{:S(2)}, u32[]{:S(2)}) collective-permute-start(bf16[32,5120]{1,0:T(8,128)(2,1)S(1)} %broadcast_select_fusion.2.refs_0_), channel_id=1, source_target_pairs={{0,16},{16,0},{1,17},{17,1},{2,18},{18,2},{3,19},{19,3},{4,20},{20... | collective-permute-start | bytes 983048 | tf_op jit(solution)/shard_map/ppermute | solution.py:243
  54.6 0.9 shard_map.43.refs_5_
  55.6 7.2 %collective-permute-start.22 = (bf16[32,5120]{1,0:T(8,128)(2,1)S(1)}, bf16[32,5120]{1,0:T(8,128)(2,1)S(1)}, u32[]{:S(2)}, u32[]{:S(2)}) collective-permute-start(bf16[32,5120]{1,0:T(8,128)(2,1)S(1)} %collective-permute-done.7), channel_id=1, source_target_pairs={{0,4},{4,0},{8,12},{12,8},{1,5},{5,1},{9,13},{13,9},{2,6},{6,2},{1... | collective-permute-start | bytes 983048 | tf_op jit(solution)/shard_map/ppermute | solution.py:230
  62.9 1.2 %collective-permute-start.24 = (bf16[32,5120]{1,0:T(8,128)(2,1)S(1)}, bf16[32,5120]{1,0:T(8,128)(2,1)S(1)}, u32[]{:S(2)}, u32[]{:S(2)}) collective-permute-start(bf16[32,5120]{1,0:T(8,128)(2,1)S(1)} %broadcast_select_fusion.refs_0_), channel_id=1, source_target_pairs={{0,16},{16,0},{1,17},{17,1},{2,18},{18,2},{3,19},{19,3},{4,20},{20... | collective-permute-start | bytes 983048 | tf_op jit(solution)/shard_map/ppermute | solution.py:243
  64.1 0.9 shard_map.44.refs_8_
  65.6 3.7 %collective-permute-done.22 = bf16[32,5120]{1,0:T(8,128)(2,1)S(1)} collective-permute-done((bf16[32,5120]{1,0:T(8,128)(2,1)S(1)}, bf16[32,5120]{1,0:T(8,128)(2,1)S(1)}, u32[]{:S(2)}, u32[]{:S(2)}) %collective-permute-start.22) | collective-permute-done | bytes 327712 | tf_op jit(solution)/shard_map/ppermute | solution.py:230
  69.3 1.2 %collective-permute-start.23 = (bf16[32,5120]{1,0:T(8,128)(2,1)S(1)}, bf16[32,5120]{1,0:T(8,128)(2,1)S(1)}, u32[]{:S(2)}, u32[]{:S(2)}) collective-permute-start(bf16[32,5120]{1,0:T(8,128)(2,1)S(1)} %broadcast_select_fusion.1.refs_0_), channel_id=1, source_target_pairs={{0,16},{16,0},{1,17},{17,1},{2,18},{18,2},{3,19},{19,3},{4,20},{20... | collective-permute-start | bytes 983048 | tf_op jit(solution)/shard_map/ppermute | solution.py:243
  70.5 2.3 %collective-permute-done.17 = bf16[32,5120]{1,0:T(8,128)(2,1)S(1)} collective-permute-done((bf16[32,5120]{1,0:T(8,128)(2,1)S(1)}, bf16[32,5120]{1,0:T(8,128)(2,1)S(1)}, u32[]{:S(2)}, u32[]{:S(2)}) %collective-permute-start.17) | collective-permute-done | bytes 327712 | tf_op jit(solution)/shard_map/ppermute | solution.py:230
  72.8 1.2 %collective-permute-start.20 = (bf16[32,5120]{1,0:T(8,128)(2,1)S(1)}, bf16[32,5120]{1,0:T(8,128)(2,1)S(1)}, u32[]{:S(2)}, u32[]{:S(2)}) collective-permute-start(bf16[32,5120]{1,0:T(8,128)(2,1)S(1)} %broadcast_select_fusion.3.refs_0_), channel_id=1, source_target_pairs={{0,16},{16,0},{1,17},{17,1},{2,18},{18,2},{3,19},{19,3},{4,20},{20... | collective-permute-start | bytes 983048 | tf_op jit(solution)/shard_map/ppermute | solution.py:243
  74.0 1.6 %collective-permute-start.26 = (f32[1,64,256]{2,1,0:T(8,128)S(1)}, f32[1,64,256]{2,1,0:T(8,128)S(1)}, u32[]{:S(2)}, u32[]{:S(2)}) collective-permute-start(f32[1,64,256]{2,1,0:T(8,128)S(1)} %slice_bitcast_fusion.6), channel_id=1, source_target_pairs={{0,2},{1,3},{2,0},{3,1},{4,6},{5,7},{6,4},{7,5},{8,10},{9,11},{10,... | collective-permute-start | bytes 196616 | tf_op jit(solution)/shard_map/ppermute | solution.py:253
  76.5 1.9 %collective-permute-done.26 = f32[1,64,256]{2,1,0:T(8,128)S(1)} collective-permute-done((f32[1,64,256]{2,1,0:T(8,128)S(1)}, f32[1,64,256]{2,1,0:T(8,128)S(1)}, u32[]{:S(2)}, u32[]{:S(2)}) %collective-permute-start.26) | collective-permute-done | bytes 65568 | tf_op jit(solution)/shard_map/ppermute | solution.py:253
  78.4 1.8 %collective-permute-start.27 = (f32[64,256]{1,0:T(8,128)S(1)}, f32[64,256]{1,0:T(8,128)S(1)}, u32[]{:S(2)}, u32[]{:S(2)}) collective-permute-start(f32[64,256]{1,0:T(8,128)S(1)} %fusion.9), channel_id=1, source_target_pairs={{0,4},{4,0},{8,12},{12,8},{1,5},{5,1},{9,13},{13,9},{2,6},{6,2},{1... | collective-permute-start | bytes 196616 | tf_op jit(solution)/shard_map/ppermute | solution.py:322
  81.1 2.9 %collective-permute-done.20.refs_1_ = bf16[32,5120]{1,0:T(8,128)(2,1)S(1)} collective-permute-done((bf16[32,5120]{1,0:T(8,128)(2,1)S(1)}, bf16[32,5120]{1,0:T(8,128)(2,1)S(1)}, u32[]{:S(2)}, u32[]{:S(2)}) %collective-permute-start.20) | collective-permute-done | bytes 327712 | tf_op jit(solution)/shard_map/ppermute | solution.py:243
  84.0 1.0 %shard_map.48 = f32[256,256]{1,0:T(8,128)S(1)} custom-call(bf16[32,5120]{1,0:T(8,128)(2,1)S(1)} %broadcast_select_fusion.3.refs_0_, bf16[32,5120]{1,0:T(8,128)(2,1)S(1)} %collective-permute-done.20.refs_1_, f32[1,16384]{1,0:T(1,128)S(1)} %bitcast.71, bf16[256,4096]{1,0:T(8,128)(2,1)S(1)} %get-tuple-element.69.refs_2_.refs_4_.refs_3_, ...), custom_call_target="tpu_custom_call" | custom-call | flops 671088640 | bytes 5242880 | tf_op jit(solution)/shard_map/pallas_call | solution.py:191
  85.1 1.3 %collective-permute-done.28 = f32[2,64,256]{2,1,0:T(8,128)S(1)} collective-permute-done((f32[2,64,256]{2,1,0:T(8,128)S(1)}, f32[2,64,256]{2,1,0:T(8,128)S(1)}, u32[]{:S(2)}, u32[]{:S(2)}) %collective-permute-start.28) | collective-permute-done | bytes 131104 | tf_op jit(solution)/shard_map/ppermute | solution.py:253
  86.5 1.6 %collective-permute-start.29 = (f32[1,64,256]{2,1,0:T(8,128)S(1)}, f32[1,64,256]{2,1,0:T(8,128)S(1)}, u32[]{:S(2)}, u32[]{:S(2)}) collective-permute-start(f32[1,64,256]{2,1,0:T(8,128)S(1)} %slice_bitcast_fusion.4), channel_id=1, source_target_pairs={{0,2},{1,3},{2,0},{3,1},{4,6},{5,7},{6,4},{7,5},{8,10},{9,11},{10,... | collective-permute-start | bytes 196616 | tf_op jit(solution)/shard_map/ppermute | solution.py:253
  88.1 2.8 %collective-permute-done.29 = f32[1,64,256]{2,1,0:T(8,128)S(1)} collective-permute-done((f32[1,64,256]{2,1,0:T(8,128)S(1)}, f32[1,64,256]{2,1,0:T(8,128)S(1)}, u32[]{:S(2)}, u32[]{:S(2)}) %collective-permute-start.29) | collective-permute-done | bytes 65568 | tf_op jit(solution)/shard_map/ppermute | solution.py:253
  (67 shorter events, 11.4 us)
Async XLA Ops:
  1.1 10.8 %collective-permute-start.3 = (bf16[32,5120]{1,0:T(8,128)(2,1)S(1)}, bf16[32,5120]{1,0:T(8,128)(2,1)S(1)}, u32[]{:S(2)}, u32[]{:S(2)}) collective-permute-start(bf16[32,5120]{1,0:T(8,128)(2,1)S(1)} %slice_select_fusion.2), channel_id=1, source_target_pairs={{0,1},{1,0},{2,3},{3,2},{4,8},{5,9},{6,10},{7,11},{8,4},{9,5},{10,... | collective-permute-start | bytes 983048 | tf_op jit(solution)/shard_map/ppermute | solution.py:234
  1.6 12.7 %collective-permute-start = (bf16[32,5120]{1,0:T(8,128)(2,1)S(1)}, bf16[32,5120]{1,0:T(8,128)(2,1)S(1)}, u32[]{:S(2)}, u32[]{:S(2)}) collective-permute-start(bf16[32,5120]{1,0:T(8,128)(2,1)S(1)} %slice_select_fusion.2), channel_id=1, source_target_pairs={{0,4},{4,0},{8,12},{12,8},{1,5},{5,1},{9,13},{13,9},{2,6},{6,2},{1... | collective-permute-start | bytes 983048 | tf_op jit(solution)/shard_map/ppermute | solution.py:230
  6.9 4.2 %copy-start = (bf16[64,16384]{1,0:T(8,128)(2,1)S(1)}, bf16[64,16384]{1,0:T(8,128)(2,1)}, u32[]{:S(2)}) copy-start(bf16[64,16384]{1,0:T(8,128)(2,1)} %test.2) | copy-start | bytes 6291460
  6.9 14.5 %collective-permute-start.2 = (bf16[32,5120]{1,0:T(8,128)(2,1)S(1)}, bf16[32,5120]{1,0:T(8,128)(2,1)S(1)}, u32[]{:S(2)}, u32[]{:S(2)}) collective-permute-start(bf16[32,5120]{1,0:T(8,128)(2,1)S(1)} %slice_select_fusion.1), channel_id=1, source_target_pairs={{0,4},{4,0},{8,12},{12,8},{1,5},{5,1},{9,13},{13,9},{2,6},{6,2},{1... | collective-permute-start | bytes 983048 | tf_op jit(solution)/shard_map/ppermute | solution.py:230
  11.1 0.8 copy-start.1
  11.9 13.5 %collective-permute-start.4 = (bf16[32,5120]{1,0:T(8,128)(2,1)S(1)}, bf16[32,5120]{1,0:T(8,128)(2,1)S(1)}, u32[]{:S(2)}, u32[]{:S(2)}) collective-permute-start(bf16[32,5120]{1,0:T(8,128)(2,1)S(1)} %slice_select_fusion.1), channel_id=1, source_target_pairs={{0,1},{1,0},{2,3},{3,2},{4,8},{5,9},{6,10},{7,11},{8,4},{9,5},{10,... | collective-permute-start | bytes 983048 | tf_op jit(solution)/shard_map/ppermute | solution.py:234
  14.4 14.0 %collective-permute-start.1 = (bf16[32,5120]{1,0:T(8,128)(2,1)S(1)}, bf16[32,5120]{1,0:T(8,128)(2,1)S(1)}, u32[]{:S(2)}, u32[]{:S(2)}) collective-permute-start(bf16[32,5120]{1,0:T(8,128)(2,1)S(1)} %slice_select_fusion), channel_id=1, source_target_pairs={{0,4},{4,0},{8,12},{12,8},{1,5},{5,1},{9,13},{13,9},{2,6},{6,2},{1... | collective-permute-start | bytes 983048 | tf_op jit(solution)/shard_map/ppermute | solution.py:230
  16.4 12.0 %collective-permute-start.9 = (bf16[32,5120]{1,0:T(8,128)(2,1)S(1)}, bf16[32,5120]{1,0:T(8,128)(2,1)S(1)}, u32[]{:S(2)}, u32[]{:S(2)}) collective-permute-start(bf16[32,5120]{1,0:T(8,128)(2,1)S(1)} %collective-permute-done.refs_0_), channel_id=1, source_target_pairs={{0,16},{16,0},{1,17},{17,1},{2,18},{18,2},{3,19},{19,3},{4,20},{20... | collective-permute-start | bytes 983048 | tf_op jit(solution)/shard_map/ppermute | solution.py:243
  21.4 9.5 %collective-permute-start.12 = (bf16[32,5120]{1,0:T(8,128)(2,1)S(1)}, bf16[32,5120]{1,0:T(8,128)(2,1)S(1)}, u32[]{:S(2)}, u32[]{:S(2)}) collective-permute-start(bf16[32,5120]{1,0:T(8,128)(2,1)S(1)} %collective-permute-done.2.refs_0_), channel_id=1, source_target_pairs={{0,16},{16,0},{1,17},{17,1},{2,18},{18,2},{3,19},{19,3},{4,20},{20... | collective-permute-start | bytes 983048 | tf_op jit(solution)/shard_map/ppermute | solution.py:243
  25.4 11.9 %collective-permute-start.15 = (bf16[32,5120]{1,0:T(8,128)(2,1)S(1)}, bf16[32,5120]{1,0:T(8,128)(2,1)S(1)}, u32[]{:S(2)}, u32[]{:S(2)}) collective-permute-start(bf16[32,5120]{1,0:T(8,128)(2,1)S(1)} %broadcast_select_fusion.5), channel_id=1, source_target_pairs={{0,4},{4,0},{8,12},{12,8},{1,5},{5,1},{9,13},{13,9},{2,6},{6,2},{1... | collective-permute-start | bytes 983048 | tf_op jit(solution)/shard_map/ppermute | solution.py:230
  27.6 4.2 %collective-permute-start.5 = (bf16[32,5120]{1,0:T(8,128)(2,1)S(1)}, bf16[32,5120]{1,0:T(8,128)(2,1)S(1)}, u32[]{:S(2)}, u32[]{:S(2)}) collective-permute-start(bf16[32,5120]{1,0:T(8,128)(2,1)S(1)} %slice_select_fusion), channel_id=1, source_target_pairs={{0,1},{1,0},{2,3},{3,2},{4,8},{5,9},{6,10},{7,11},{8,4},{9,5},{10,... | collective-permute-start | bytes 983048 | tf_op jit(solution)/shard_map/ppermute | solution.py:234
  28.4 9.8 %collective-permute-start.11 = (bf16[32,5120]{1,0:T(8,128)(2,1)S(1)}, bf16[32,5120]{1,0:T(8,128)(2,1)S(1)}, u32[]{:S(2)}, u32[]{:S(2)}) collective-permute-start(bf16[32,5120]{1,0:T(8,128)(2,1)S(1)} %collective-permute-done.1.refs_0_), channel_id=1, source_target_pairs={{0,16},{16,0},{1,17},{17,1},{2,18},{18,2},{3,19},{19,3},{4,20},{20... | collective-permute-start | bytes 983048 | tf_op jit(solution)/shard_map/ppermute | solution.py:243
  31.8 7.4 %collective-permute-start.6 = (bf16[32,5120]{1,0:T(8,128)(2,1)S(1)}, bf16[32,5120]{1,0:T(8,128)(2,1)S(1)}, u32[]{:S(2)}, u32[]{:S(2)}) collective-permute-start(bf16[32,5120]{1,0:T(8,128)(2,1)S(1)} %collective-permute-done.refs_0_), channel_id=1, source_target_pairs={{0,1},{1,0},{2,3},{3,2},{4,8},{5,9},{6,10},{7,11},{8,4},{9,5},{10,... | collective-permute-start | bytes 983048 | tf_op jit(solution)/shard_map/ppermute | solution.py:234
  31.9 13.4 %collective-permute-start.10 = (bf16[32,5120]{1,0:T(8,128)(2,1)S(1)}, bf16[32,5120]{1,0:T(8,128)(2,1)S(1)}, u32[]{:S(2)}, u32[]{:S(2)}) collective-permute-start(bf16[32,5120]{1,0:T(8,128)(2,1)S(1)} %broadcast_select_fusion.7), channel_id=1, source_target_pairs={{0,4},{4,0},{8,12},{12,8},{1,5},{5,1},{9,13},{13,9},{2,6},{6,2},{1... | collective-permute-start | bytes 983048 | tf_op jit(solution)/shard_map/ppermute | solution.py:230
  37.4 8.7 %collective-permute-start.16 = (bf16[32,5120]{1,0:T(8,128)(2,1)S(1)}, bf16[32,5120]{1,0:T(8,128)(2,1)S(1)}, u32[]{:S(2)}, u32[]{:S(2)}) collective-permute-start(bf16[32,5120]{1,0:T(8,128)(2,1)S(1)} %broadcast_select_fusion.4.refs_0_), channel_id=1, source_target_pairs={{0,16},{16,0},{1,17},{17,1},{2,18},{18,2},{3,19},{19,3},{4,20},{20... | collective-permute-start | bytes 983048 | tf_op jit(solution)/shard_map/ppermute | solution.py:243
  39.2 7.8 %collective-permute-start.7 = (bf16[32,5120]{1,0:T(8,128)(2,1)S(1)}, bf16[32,5120]{1,0:T(8,128)(2,1)S(1)}, u32[]{:S(2)}, u32[]{:S(2)}) collective-permute-start(bf16[32,5120]{1,0:T(8,128)(2,1)S(1)} %collective-permute-done.2.refs_0_), channel_id=1, source_target_pairs={{0,1},{1,0},{2,3},{3,2},{4,8},{5,9},{6,10},{7,11},{8,4},{9,5},{10,... | collective-permute-start | bytes 983048 | tf_op jit(solution)/shard_map/ppermute | solution.py:234
  39.3 14.4 %collective-permute-start.18 = (bf16[32,5120]{1,0:T(8,128)(2,1)S(1)}, bf16[32,5120]{1,0:T(8,128)(2,1)S(1)}, u32[]{:S(2)}, u32[]{:S(2)}) collective-permute-start(bf16[32,5120]{1,0:T(8,128)(2,1)S(1)} %collective-permute-done.5), channel_id=1, source_target_pairs={{0,4},{4,0},{8,12},{12,8},{1,5},{5,1},{9,13},{13,9},{2,6},{6,2},{1... | collective-permute-start | bytes 983048 | tf_op jit(solution)/shard_map/ppermute | solution.py:230
  45.3 9.4 %collective-permute-start.14 = (bf16[32,5120]{1,0:T(8,128)(2,1)S(1)}, bf16[32,5120]{1,0:T(8,128)(2,1)S(1)}, u32[]{:S(2)}, u32[]{:S(2)}) collective-permute-start(bf16[32,5120]{1,0:T(8,128)(2,1)S(1)} %broadcast_select_fusion.6.refs_0_), channel_id=1, source_target_pairs={{0,16},{16,0},{1,17},{17,1},{2,18},{18,2},{3,19},{19,3},{4,20},{20... | collective-permute-start | bytes 983048 | tf_op jit(solution)/shard_map/ppermute | solution.py:243
  47.0 8.6 %collective-permute-start.8 = (bf16[32,5120]{1,0:T(8,128)(2,1)S(1)}, bf16[32,5120]{1,0:T(8,128)(2,1)S(1)}, u32[]{:S(2)}, u32[]{:S(2)}) collective-permute-start(bf16[32,5120]{1,0:T(8,128)(2,1)S(1)} %collective-permute-done.1.refs_0_), channel_id=1, source_target_pairs={{0,1},{1,0},{2,3},{3,2},{4,8},{5,9},{6,10},{7,11},{8,4},{9,5},{10,... | collective-permute-start | bytes 983048 | tf_op jit(solution)/shard_map/ppermute | solution.py:234
  47.0 15.8 %collective-permute-start.13 = (bf16[32,5120]{1,0:T(8,128)(2,1)S(1)}, bf16[32,5120]{1,0:T(8,128)(2,1)S(1)}, u32[]{:S(2)}, u32[]{:S(2)}) collective-permute-start(bf16[32,5120]{1,0:T(8,128)(2,1)S(1)} %collective-permute-done.6), channel_id=1, source_target_pairs={{0,4},{4,0},{8,12},{12,8},{1,5},{5,1},{9,13},{13,9},{2,6},{6,2},{1... | collective-permute-start | bytes 983048 | tf_op jit(solution)/shard_map/ppermute | solution.py:230
  53.7 10.4 %collective-permute-start.19 = (bf16[32,5120]{1,0:T(8,128)(2,1)S(1)}, bf16[32,5120]{1,0:T(8,128)(2,1)S(1)}, u32[]{:S(2)}, u32[]{:S(2)}) collective-permute-start(bf16[32,5120]{1,0:T(8,128)(2,1)S(1)} %broadcast_select_fusion.2.refs_0_), channel_id=1, source_target_pairs={{0,16},{16,0},{1,17},{17,1},{2,18},{18,2},{3,19},{19,3},{4,20},{20... | collective-permute-start | bytes 983048 | tf_op jit(solution)/shard_map/ppermute | solution.py:243
  55.6 9.4 %collective-permute-start.21 = (bf16[64,2048]{1,0:T(8,128)(2,1)S(1)}, bf16[64,2048]{1,0:T(8,128)(2,1)S(1)}, u32[]{:S(2)}, u32[]{:S(2)}) collective-permute-start(bf16[64,2048]{1,0:T(8,128)(2,1)S(1)} %pad_maximum_fusion), channel_id=1, source_target_pairs={{0,1},{1,0},{2,3},{3,2},{4,8},{5,9},{6,10},{7,11},{8,4},{9,5},{10,... | collective-permute-start | bytes 786440 | tf_op jit(solution)/shard_map/ppermute | solution.py:234
  55.6 13.6 %collective-permute-start.22 = (bf16[32,5120]{1,0:T(8,128)(2,1)S(1)}, bf16[32,5120]{1,0:T(8,128)(2,1)S(1)}, u32[]{:S(2)}, u32[]{:S(2)}) collective-permute-start(bf16[32,5120]{1,0:T(8,128)(2,1)S(1)} %collective-permute-done.7), channel_id=1, source_target_pairs={{0,4},{4,0},{8,12},{12,8},{1,5},{5,1},{9,13},{13,9},{2,6},{6,2},{1... | collective-permute-start | bytes 983048 | tf_op jit(solution)/shard_map/ppermute | solution.py:230
  62.9 12.7 %collective-permute-start.24 = (bf16[32,5120]{1,0:T(8,128)(2,1)S(1)}, bf16[32,5120]{1,0:T(8,128)(2,1)S(1)}, u32[]{:S(2)}, u32[]{:S(2)}) collective-permute-start(bf16[32,5120]{1,0:T(8,128)(2,1)S(1)} %broadcast_select_fusion.refs_0_), channel_id=1, source_target_pairs={{0,16},{16,0},{1,17},{17,1},{2,18},{18,2},{3,19},{19,3},{4,20},{20... | collective-permute-start | bytes 983048 | tf_op jit(solution)/shard_map/ppermute | solution.py:243
  64.1 8.7 %collective-permute-start.17 = (bf16[32,5120]{1,0:T(8,128)(2,1)S(1)}, bf16[32,5120]{1,0:T(8,128)(2,1)S(1)}, u32[]{:S(2)}, u32[]{:S(2)}) collective-permute-start(bf16[32,5120]{1,0:T(8,128)(2,1)S(1)} %collective-permute-done.8), channel_id=1, source_target_pairs={{0,4},{4,0},{8,12},{12,8},{1,5},{5,1},{9,13},{13,9},{2,6},{6,2},{1... | collective-permute-start | bytes 983048 | tf_op jit(solution)/shard_map/ppermute | solution.py:230
  65.5 8.5 %collective-permute-start.25 = (f32[2,64,256]{2,1,0:T(8,128)S(1)}, f32[2,64,256]{2,1,0:T(8,128)S(1)}, u32[]{:S(2)}, u32[]{:S(2)}) collective-permute-start(f32[2,64,256]{2,1,0:T(8,128)S(1)} %slice_bitcast_fusion), channel_id=1, source_target_pairs={{0,1},{1,0},{2,3},{3,2},{4,5},{5,4},{6,7},{7,6},{8,9},{9,8},{10,11... | collective-permute-start | bytes 393224 | tf_op jit(solution)/shard_map/ppermute | solution.py:253
  69.3 10.9 %collective-permute-start.23 = (bf16[32,5120]{1,0:T(8,128)(2,1)S(1)}, bf16[32,5120]{1,0:T(8,128)(2,1)S(1)}, u32[]{:S(2)}, u32[]{:S(2)}) collective-permute-start(bf16[32,5120]{1,0:T(8,128)(2,1)S(1)} %broadcast_select_fusion.1.refs_0_), channel_id=1, source_target_pairs={{0,16},{16,0},{1,17},{17,1},{2,18},{18,2},{3,19},{19,3},{4,20},{20... | collective-permute-start | bytes 983048 | tf_op jit(solution)/shard_map/ppermute | solution.py:243
  72.8 11.2 %collective-permute-start.20 = (bf16[32,5120]{1,0:T(8,128)(2,1)S(1)}, bf16[32,5120]{1,0:T(8,128)(2,1)S(1)}, u32[]{:S(2)}, u32[]{:S(2)}) collective-permute-start(bf16[32,5120]{1,0:T(8,128)(2,1)S(1)} %broadcast_select_fusion.3.refs_0_), channel_id=1, source_target_pairs={{0,16},{16,0},{1,17},{17,1},{2,18},{18,2},{3,19},{19,3},{4,20},{20... | collective-permute-start | bytes 983048 | tf_op jit(solution)/shard_map/ppermute | solution.py:243
  74.0 4.3 %collective-permute-start.26 = (f32[1,64,256]{2,1,0:T(8,128)S(1)}, f32[1,64,256]{2,1,0:T(8,128)S(1)}, u32[]{:S(2)}, u32[]{:S(2)}) collective-permute-start(f32[1,64,256]{2,1,0:T(8,128)S(1)} %slice_bitcast_fusion.6), channel_id=1, source_target_pairs={{0,2},{1,3},{2,0},{3,1},{4,6},{5,7},{6,4},{7,5},{8,10},{9,11},{10,... | collective-permute-start | bytes 196616 | tf_op jit(solution)/shard_map/ppermute | solution.py:253
  78.4 6.6 %collective-permute-start.27 = (f32[64,256]{1,0:T(8,128)S(1)}, f32[64,256]{1,0:T(8,128)S(1)}, u32[]{:S(2)}, u32[]{:S(2)}) collective-permute-start(f32[64,256]{1,0:T(8,128)S(1)} %fusion.9), channel_id=1, source_target_pairs={{0,4},{4,0},{8,12},{12,8},{1,5},{5,1},{9,13},{13,9},{2,6},{6,2},{1... | collective-permute-start | bytes 196616 | tf_op jit(solution)/shard_map/ppermute | solution.py:322
  85.0 1.4 %collective-permute-start.28 = (f32[2,64,256]{2,1,0:T(8,128)S(1)}, f32[2,64,256]{2,1,0:T(8,128)S(1)}, u32[]{:S(2)}, u32[]{:S(2)}) collective-permute-start(f32[2,64,256]{2,1,0:T(8,128)S(1)} %slice_bitcast_fusion.2), channel_id=1, source_target_pairs={{0,1},{1,0},{2,3},{3,2},{4,5},{5,4},{6,7},{7,6},{8,9},{9,8},{10,11... | collective-permute-start | bytes 393224 | tf_op jit(solution)/shard_map/ppermute | solution.py:253
  86.5 4.3 %collective-permute-start.29 = (f32[1,64,256]{2,1,0:T(8,128)S(1)}, f32[1,64,256]{2,1,0:T(8,128)S(1)}, u32[]{:S(2)}, u32[]{:S(2)}) collective-permute-start(f32[1,64,256]{2,1,0:T(8,128)S(1)} %slice_bitcast_fusion.4), channel_id=1, source_target_pairs={{0,2},{1,3},{2,0},{3,1},{4,6},{5,7},{6,4},{7,5},{8,10},{9,11},{10,... | collective-permute-start | bytes 196616 | tf_op jit(solution)/shard_map/ppermute | solution.py:253

commit v27 on v25

--- a/solution.py
+++ b/solution.py
@@ -222,7 +222,7 @@
         middle_pairs = []
         for i in range(n_ex):
             for f in range(n_feat):
-                to = (i, f ^ 1) if i in (0, n_ex - 1) else (n_ex - 1 - i, f)
+                to = (i, f) if i in (0, n_ex - 1) else (n_ex - 1 - i, f)
                 middle_pairs.append((i * n_feat + f, to[0] * n_feat + to[1]))
 
         def outer(name, block):

time: 90.2 us -> 102 us (1.13)
  starting transfers between devices: 49.3 us -> 64.2 us
  waiting for transfers between devices: 19.8 us -> 17 us
    ppermute x9, starting transfers between devices: 28.2 us -> 39.5 us  [outer(): outs.append(lax.ppermute(after(block, *waits), 'ex', outer_pairs))]
    ppermute x9, waiting for transfers between devices: 11.4 us -> 6.95 us  [outer(): outs.append(lax.ppermute(after(block, *waits), 'ex', outer_pairs))]
    ppermute x7, starting transfers between devices: 0.88 us -> 4.76 us  [middle(): lax.ppermute(after(block, *middles[-1:], *swaps[-2:-1]), ('ex', 'feat'),...]
    ppermute x9, waiting for transfers between devices: 3.14 us -> 4.74 us  [swap(): swaps.append(lax.ppermute(after(block, *waits), 'grp', [(0, 1), (1, 0)]))]
  transfers between devices with their start and end apart: 30 -> 30, of which waited for: 14 -> 11; matrix products, arithmetic and copies ran while one was open for 7% -> 7% of each run, Pallas kernels for 12% -> 11%
where the time goes in v27:
time: 102 us
  starting transfers between devices  64.2 us (63%)
  waiting for transfers between devices  17 us (17%)
  Pallas kernels  11.3 us (11%)
  local copies, waits for them, and re-layouts  4.9 us (5%)
  other arithmetic  4.33 us (4%)
    ppermute x9, starting transfers between devices, outer(): outs.append(lax.ppermute(after(block, *waits), 'ex', outer_pairs))  39.5 us
    ppermute x9, starting transfers between devices, swap(): swaps.append(lax.ppermute(after(block, *waits), 'grp', [(0, 1), (1, 0)]))  14.6 us
    pallas_call x12, Pallas kernels, call(): pl.pallas_call(kernel, out_shape=shapes or jax.ShapeDtypeStruct((rows, do...  11.3 us
    ppermute x9, waiting for transfers between devices, outer(): outs.append(lax.ppermute(after(block, *waits), 'ex', outer_pairs))  6.95 us
    ppermute x4, waiting for transfers between devices, sum_over_feat(): held, waits = (pairs[:, 0] + lax.ppermute(send, 'feat', partner), ())  5.07 us
    ppermute x7, starting transfers between devices, middle(): lax.ppermute(after(block, *middles[-1:], *swaps[-2:-1]), ('ex', 'feat'),...  4.76 us
    ppermute x9, waiting for transfers between devices, swap(): swaps.append(lax.ppermute(after(block, *waits), 'grp', [(0, 1), (1, 0)]))  4.74 us
    slice x1, local copies, waits for them, and re-layouts, line(): trains = [train[:, q * 4 * unit:(q + 1) * 4 * unit] for q in range(4)]  4.08 us
  transfers between devices with their start and end apart: 30, of which 11 were waited for; matrix products, arithmetic and copies ran while one was open for 7% of the time, Pallas kernels for 11%

profile of v27, /device:TPU:0, one launch (start us, length us, event | category | flops | bytes accessed | tf_op | source)
XLA Modules:
  0.0 102.0 jit_solution(13065252180267836452)
XLA Ops:
  0.0 1.1 %slice_select_fusion.2 = bf16[32,5120]{1,0:T(8,128)(2,1)S(1)} fusion(bf16[64,16384]{1,0:T(8,128)(2,1)} %test.2, pred[]{:T(512)S(6)} %eq.11), kind=kLoop, calls=%fused_computation.2 | loop fusion | flops 163840 | bytes 983041 | tf_op jit(solution)/shard_map/jit(_where)/select_n | solution.py:261
  1.8 5.9 %collective-permute-start = (bf16[32,5120]{1,0:T(8,128)(2,1)S(1)}, bf16[32,5120]{1,0:T(8,128)(2,1)S(1)}, u32[]{:S(2)}, u32[]{:S(2)}) collective-permute-start(bf16[32,5120]{1,0:T(8,128)(2,1)S(1)} %slice_select_fusion.2), channel_id=1, source_target_pairs={{0,4},{4,0},{8,12},{12,8},{1,5},{5,1},{9,13},{13,9},{2,6},{6,2},{1... | collective-permute-start | bytes 983048 | tf_op jit(solution)/shard_map/ppermute | solution.py:230
  7.7 1.1 %slice_select_fusion.1 = bf16[32,5120]{1,0:T(8,128)(2,1)S(1)} fusion(bf16[64,16384]{1,0:T(8,128)(2,1)} %test.2, pred[]{:T(512)S(6)} %eq.11), kind=kLoop, calls=%fused_computation.1 | loop fusion | flops 163840 | bytes 983041 | tf_op jit(solution)/shard_map/jit(_where)/select_n | solution.py:261
  8.9 1.1 %slice_select_fusion = bf16[32,5120]{1,0:T(8,128)(2,1)S(1)} fusion(bf16[64,16384]{1,0:T(8,128)(2,1)} %test.2, pred[]{:T(512)S(6)} %eq.11), kind=kLoop, calls=%fused_computation | loop fusion | flops 163840 | bytes 983041 | tf_op jit(solution)/shard_map/jit(_where)/select_n | solution.py:261
  10.0 4.1 %fusion.10 = (bf16[256,4096]{1,0:T(8,128)(2,1)S(1)}, bf16[256,4096]{1,0:T(8,128)(2,1)S(1)}, bf16[256,4096]{1,0:T(8,128)(2,1)S(1)}, bf16[256,4096]{1,0:T(8,128)(2,1)S(1)}) fusion(bf16[256,16384]{1,0:T(8,128)(2,1)} %param.3), kind=kLoop, calls=%fused_computation.31 | loop fusion | bytes 16777216 | tf_op jit(solution)/shard_map/slice | solution.py:268
  16.3 3.2 %collective-permute-start.1 = (bf16[32,5120]{1,0:T(8,128)(2,1)S(1)}, bf16[32,5120]{1,0:T(8,128)(2,1)S(1)}, u32[]{:S(2)}, u32[]{:S(2)}) collective-permute-start(bf16[32,5120]{1,0:T(8,128)(2,1)S(1)} %slice_select_fusion), channel_id=1, source_target_pairs={{0,4},{4,0},{8,12},{12,8},{1,5},{5,1},{9,13},{13,9},{2,6},{6,2},{1... | collective-permute-start | bytes 983048 | tf_op jit(solution)/shard_map/ppermute | solution.py:230
  19.4 1.5 %collective-permute-start.5 = (bf16[32,5120]{1,0:T(8,128)(2,1)S(1)}, bf16[32,5120]{1,0:T(8,128)(2,1)S(1)}, u32[]{:S(2)}, u32[]{:S(2)}) collective-permute-start(bf16[32,5120]{1,0:T(8,128)(2,1)S(1)} %collective-permute-done.refs_0_), channel_id=1, source_target_pairs={{0,16},{16,0},{1,17},{17,1},{2,18},{18,2},{3,19},{19,3},{4,20},{20... | collective-permute-start | bytes 983048 | tf_op jit(solution)/shard_map/ppermute | solution.py:243
  21.0 2.3 %collective-permute-done.2.refs_0_ = bf16[32,5120]{1,0:T(8,128)(2,1)S(1)} collective-permute-done((bf16[32,5120]{1,0:T(8,128)(2,1)S(1)}, bf16[32,5120]{1,0:T(8,128)(2,1)S(1)}, u32[]{:S(2)}, u32[]{:S(2)}) %collective-permute-start.2) | collective-permute-done | bytes 327712 | tf_op jit(solution)/shard_map/ppermute | solution.py:230
  23.3 2.1 %collective-permute-start.11 = (bf16[32,5120]{1,0:T(8,128)(2,1)S(1)}, bf16[32,5120]{1,0:T(8,128)(2,1)S(1)}, u32[]{:S(2)}, u32[]{:S(2)}) collective-permute-start(bf16[32,5120]{1,0:T(8,128)(2,1)S(1)} %broadcast_select_fusion.7), channel_id=1, source_target_pairs={{0,4},{4,0},{8,12},{12,8},{1,5},{5,1},{9,13},{13,9},{2,6},{6,2},{1... | collective-permute-start | bytes 983048 | tf_op jit(solution)/shard_map/ppermute | solution.py:230
  25.4 1.5 %collective-permute-start.7 = (bf16[32,5120]{1,0:T(8,128)(2,1)S(1)}, bf16[32,5120]{1,0:T(8,128)(2,1)S(1)}, u32[]{:S(2)}, u32[]{:S(2)}) collective-permute-start(bf16[32,5120]{1,0:T(8,128)(2,1)S(1)} %collective-permute-done.2.refs_0_), channel_id=1, source_target_pairs={{0,16},{16,0},{1,17},{17,1},{2,18},{18,2},{3,19},{19,3},{4,20},{20... | collective-permute-start | bytes 983048 | tf_op jit(solution)/shard_map/ppermute | solution.py:243
  26.9 2.5 %shard_map.39.refs_6_ = f32[64,256]{1,0:T(8,128)S(1)} custom-call(bf16[64,16384]{1,0:T(8,128)(2,1)S(1)} %copy-done, f32[1,16384]{1,0:T(1,128)S(1)} %bitcast.61, bf16[256,4096]{1,0:T(8,128)(2,1)S(1)} %get-tuple-element.70.refs_3_.refs_0_, bf16[256,4096]{1,0:T(8,128)(2,1)S(1)} %get-tuple-element.72.refs_4_.refs_1_.refs_3_, ...), custom_call_target="tpu_custom_call" | custom-call | flops 536870912 | bytes 10485760 | tf_op jit(solution)/shard_map/pallas_call | solution.py:191
  31.0 1.6 %collective-permute-start.9 = (bf16[32,5120]{1,0:T(8,128)(2,1)S(1)}, bf16[32,5120]{1,0:T(8,128)(2,1)S(1)}, u32[]{:S(2)}, u32[]{:S(2)}) collective-permute-start(bf16[32,5120]{1,0:T(8,128)(2,1)S(1)} %collective-permute-done.1.refs_0_), channel_id=1, source_target_pairs={{0,16},{16,0},{1,17},{17,1},{2,18},{18,2},{3,19},{19,3},{4,20},{20... | collective-permute-start | bytes 983048 | tf_op jit(solution)/shard_map/ppermute | solution.py:243
  33.5 3.8 %collective-permute-start.14 = (bf16[32,5120]{1,0:T(8,128)(2,1)S(1)}, bf16[32,5120]{1,0:T(8,128)(2,1)S(1)}, u32[]{:S(2)}, u32[]{:S(2)}) collective-permute-start(bf16[32,5120]{1,0:T(8,128)(2,1)S(1)} %broadcast_select_fusion.5), channel_id=1, source_target_pairs={{0,4},{4,0},{8,12},{12,8},{1,5},{5,1},{9,13},{13,9},{2,6},{6,2},{1... | collective-permute-start | bytes 983048 | tf_op jit(solution)/shard_map/ppermute | solution.py:230
  37.4 1.6 %collective-permute-start.12 = (bf16[32,5120]{1,0:T(8,128)(2,1)S(1)}, bf16[32,5120]{1,0:T(8,128)(2,1)S(1)}, u32[]{:S(2)}, u32[]{:S(2)}) collective-permute-start(bf16[32,5120]{1,0:T(8,128)(2,1)S(1)} %broadcast_select_fusion.6.refs_0_), channel_id=1, source_target_pairs={{0,16},{16,0},{1,17},{17,1},{2,18},{18,2},{3,19},{19,3},{4,20},{20... | collective-permute-start | bytes 983048 | tf_op jit(solution)/shard_map/ppermute | solution.py:243
  40.6 3.5 %collective-permute-start.18 = (bf16[32,5120]{1,0:T(8,128)(2,1)S(1)}, bf16[32,5120]{1,0:T(8,128)(2,1)S(1)}, u32[]{:S(2)}, u32[]{:S(2)}) collective-permute-start(bf16[32,5120]{1,0:T(8,128)(2,1)S(1)} %collective-permute-done.6), channel_id=1, source_target_pairs={{0,4},{4,0},{8,12},{12,8},{1,5},{5,1},{9,13},{13,9},{2,6},{6,2},{1... | collective-permute-start | bytes 983048 | tf_op jit(solution)/shard_map/ppermute | solution.py:230
  44.5 2.1 %collective-permute-start.16 = (bf16[32,5120]{1,0:T(8,128)(2,1)S(1)}, bf16[32,5120]{1,0:T(8,128)(2,1)S(1)}, u32[]{:S(2)}, u32[]{:S(2)}) collective-permute-start(bf16[32,5120]{1,0:T(8,128)(2,1)S(1)} %broadcast_select_fusion.4.refs_0_), channel_id=1, source_target_pairs={{0,16},{16,0},{1,17},{17,1},{2,18},{18,2},{3,19},{19,3},{4,20},{20... | collective-permute-start | bytes 983048 | tf_op jit(solution)/shard_map/ppermute | solution.py:243
  47.5 3.7 %collective-permute-done.12.refs_1_ = bf16[32,5120]{1,0:T(8,128)(2,1)S(1)} collective-permute-done((bf16[32,5120]{1,0:T(8,128)(2,1)S(1)}, bf16[32,5120]{1,0:T(8,128)(2,1)S(1)}, u32[]{:S(2)}, u32[]{:S(2)}) %collective-permute-start.12) | collective-permute-done | bytes 327712 | tf_op jit(solution)/shard_map/ppermute | solution.py:243
  52.8 4.2 %collective-permute-start.15 = (bf16[32,5120]{1,0:T(8,128)(2,1)S(1)}, bf16[32,5120]{1,0:T(8,128)(2,1)S(1)}, u32[]{:S(2)}, u32[]{:S(2)}) collective-permute-start(bf16[32,5120]{1,0:T(8,128)(2,1)S(1)} %collective-permute-done.8), channel_id=1, source_target_pairs={{0,4},{4,0},{8,12},{12,8},{1,5},{5,1},{9,13},{13,9},{2,6},{6,2},{1... | collective-permute-start | bytes 983048 | tf_op jit(solution)/shard_map/ppermute | solution.py:230
  57.0 1.6 %collective-permute-start.19 = (bf16[32,5120]{1,0:T(8,128)(2,1)S(1)}, bf16[32,5120]{1,0:T(8,128)(2,1)S(1)}, u32[]{:S(2)}, u32[]{:S(2)}) collective-permute-start(bf16[32,5120]{1,0:T(8,128)(2,1)S(1)} %broadcast_select_fusion.2.refs_0_), channel_id=1, source_target_pairs={{0,16},{16,0},{1,17},{17,1},{2,18},{18,2},{3,19},{19,3},{4,20},{20... | collective-permute-start | bytes 983048 | tf_op jit(solution)/shard_map/ppermute | solution.py:243
  60.2 9.1 %collective-permute-start.22 = (bf16[32,5120]{1,0:T(8,128)(2,1)S(1)}, bf16[32,5120]{1,0:T(8,128)(2,1)S(1)}, u32[]{:S(2)}, u32[]{:S(2)}) collective-permute-start(bf16[32,5120]{1,0:T(8,128)(2,1)S(1)} %collective-permute-done.10), channel_id=1, source_target_pairs={{0,4},{4,0},{8,12},{12,8},{1,5},{5,1},{9,13},{13,9},{2,6},{6,2},{1... | collective-permute-start | bytes 983048 | tf_op jit(solution)/shard_map/ppermute | solution.py:230
  69.3 1.6 %collective-permute-start.24 = (bf16[32,5120]{1,0:T(8,128)(2,1)S(1)}, bf16[32,5120]{1,0:T(8,128)(2,1)S(1)}, u32[]{:S(2)}, u32[]{:S(2)}) collective-permute-start(bf16[32,5120]{1,0:T(8,128)(2,1)S(1)} %broadcast_select_fusion.refs_0_), channel_id=1, source_target_pairs={{0,16},{16,0},{1,17},{17,1},{2,18},{18,2},{3,19},{19,3},{4,20},{20... | collective-permute-start | bytes 983048 | tf_op jit(solution)/shard_map/ppermute | solution.py:243
  72.5 7.7 %collective-permute-start.17 = (bf16[32,5120]{1,0:T(8,128)(2,1)S(1)}, bf16[32,5120]{1,0:T(8,128)(2,1)S(1)}, u32[]{:S(2)}, u32[]{:S(2)}) collective-permute-start(bf16[32,5120]{1,0:T(8,128)(2,1)S(1)} %collective-permute-done.13), channel_id=1, source_target_pairs={{0,4},{4,0},{8,12},{12,8},{1,5},{5,1},{9,13},{13,9},{2,6},{6,2},{1... | collective-permute-start | bytes 983048 | tf_op jit(solution)/shard_map/ppermute | solution.py:230
  80.3 1.6 %collective-permute-start.23 = (bf16[32,5120]{1,0:T(8,128)(2,1)S(1)}, bf16[32,5120]{1,0:T(8,128)(2,1)S(1)}, u32[]{:S(2)}, u32[]{:S(2)}) collective-permute-start(bf16[32,5120]{1,0:T(8,128)(2,1)S(1)} %broadcast_select_fusion.1.refs_0_), channel_id=1, source_target_pairs={{0,16},{16,0},{1,17},{17,1},{2,18},{18,2},{3,19},{19,3},{4,20},{20... | collective-permute-start | bytes 983048 | tf_op jit(solution)/shard_map/ppermute | solution.py:243
  82.5 2.8 %collective-permute-done.17 = bf16[32,5120]{1,0:T(8,128)(2,1)S(1)} collective-permute-done((bf16[32,5120]{1,0:T(8,128)(2,1)S(1)}, bf16[32,5120]{1,0:T(8,128)(2,1)S(1)}, u32[]{:S(2)}, u32[]{:S(2)}) %collective-permute-start.17) | collective-permute-done | bytes 327712 | tf_op jit(solution)/shard_map/ppermute | solution.py:230
  85.3 1.6 %collective-permute-start.20 = (bf16[32,5120]{1,0:T(8,128)(2,1)S(1)}, bf16[32,5120]{1,0:T(8,128)(2,1)S(1)}, u32[]{:S(2)}, u32[]{:S(2)}) collective-permute-start(bf16[32,5120]{1,0:T(8,128)(2,1)S(1)} %broadcast_select_fusion.3.refs_0_), channel_id=1, source_target_pairs={{0,16},{16,0},{1,17},{17,1},{2,18},{18,2},{3,19},{19,3},{4,20},{20... | collective-permute-start | bytes 983048 | tf_op jit(solution)/shard_map/ppermute | solution.py:243
  86.9 1.6 %collective-permute-start.26 = (f32[1,64,256]{2,1,0:T(8,128)S(1)}, f32[1,64,256]{2,1,0:T(8,128)S(1)}, u32[]{:S(2)}, u32[]{:S(2)}) collective-permute-start(f32[1,64,256]{2,1,0:T(8,128)S(1)} %slice_bitcast_fusion.6), channel_id=1, source_target_pairs={{0,2},{1,3},{2,0},{3,1},{4,6},{5,7},{6,4},{7,5},{8,10},{9,11},{10,... | collective-permute-start | bytes 196616 | tf_op jit(solution)/shard_map/ppermute | solution.py:253
  91.3 2.1 %collective-permute-start.27 = (f32[64,256]{1,0:T(8,128)S(1)}, f32[64,256]{1,0:T(8,128)S(1)}, u32[]{:S(2)}, u32[]{:S(2)}) collective-permute-start(f32[64,256]{1,0:T(8,128)S(1)} %fusion.9), channel_id=1, source_target_pairs={{0,4},{4,0},{8,12},{12,8},{1,5},{5,1},{9,13},{13,9},{2,6},{6,2},{1... | collective-permute-start | bytes 196616 | tf_op jit(solution)/shard_map/ppermute | solution.py:321
  93.4 1.1 %collective-permute-done.20.refs_1_ = bf16[32,5120]{1,0:T(8,128)(2,1)S(1)} collective-permute-done((bf16[32,5120]{1,0:T(8,128)(2,1)S(1)}, bf16[32,5120]{1,0:T(8,128)(2,1)S(1)}, u32[]{:S(2)}, u32[]{:S(2)}) %collective-permute-start.20) | collective-permute-done | bytes 327712 | tf_op jit(solution)/shard_map/ppermute | solution.py:243
  94.4 1.0 shard_map.48
  95.6 1.3 %collective-permute-done.28 = f32[2,64,256]{2,1,0:T(8,128)S(1)} collective-permute-done((f32[2,64,256]{2,1,0:T(8,128)S(1)}, f32[2,64,256]{2,1,0:T(8,128)S(1)}, u32[]{:S(2)}, u32[]{:S(2)}) %collective-permute-start.28) | collective-permute-done | bytes 131104 | tf_op jit(solution)/shard_map/ppermute | solution.py:253
  97.0 1.6 %collective-permute-start.29 = (f32[1,64,256]{2,1,0:T(8,128)S(1)}, f32[1,64,256]{2,1,0:T(8,128)S(1)}, u32[]{:S(2)}, u32[]{:S(2)}) collective-permute-start(f32[1,64,256]{2,1,0:T(8,128)S(1)} %slice_bitcast_fusion.4), channel_id=1, source_target_pairs={{0,2},{1,3},{2,0},{3,1},{4,6},{5,7},{6,4},{7,5},{8,10},{9,11},{10,... | collective-permute-start | bytes 196616 | tf_op jit(solution)/shard_map/ppermute | solution.py:253
  98.5 2.8 %collective-permute-done.29 = f32[1,64,256]{2,1,0:T(8,128)S(1)} collective-permute-done((f32[1,64,256]{2,1,0:T(8,128)S(1)}, f32[1,64,256]{2,1,0:T(8,128)S(1)}, u32[]{:S(2)}, u32[]{:S(2)}) %collective-permute-start.29) | collective-permute-done | bytes 65568 | tf_op jit(solution)/shard_map/ppermute | solution.py:253
  (67 shorter events, 17.6 us)
Async XLA Ops:
  1.1 13.9 %collective-permute-start.3 = (bf16[32,5120]{1,0:T(8,128)(2,1)S(1)}, bf16[32,5120]{1,0:T(8,128)(2,1)S(1)}, u32[]{:S(2)}, u32[]{:S(2)}) collective-permute-start(bf16[32,5120]{1,0:T(8,128)(2,1)S(1)} %slice_select_fusion.2), channel_id=1, source_target_pairs={{0,0},{1,1},{2,2},{3,3},{4,8},{5,9},{6,10},{7,11},{8,4},{9,5},{10,... | collective-permute-start | bytes 983048 | tf_op jit(solution)/shard_map/ppermute | solution.py:234
  1.8 14.5 %collective-permute-start = (bf16[32,5120]{1,0:T(8,128)(2,1)S(1)}, bf16[32,5120]{1,0:T(8,128)(2,1)S(1)}, u32[]{:S(2)}, u32[]{:S(2)}) collective-permute-start(bf16[32,5120]{1,0:T(8,128)(2,1)S(1)} %slice_select_fusion.2), channel_id=1, source_target_pairs={{0,4},{4,0},{8,12},{12,8},{1,5},{5,1},{9,13},{13,9},{2,6},{6,2},{1... | collective-permute-start | bytes 983048 | tf_op jit(solution)/shard_map/ppermute | solution.py:230
  8.8 14.5 %collective-permute-start.2 = (bf16[32,5120]{1,0:T(8,128)(2,1)S(1)}, bf16[32,5120]{1,0:T(8,128)(2,1)S(1)}, u32[]{:S(2)}, u32[]{:S(2)}) collective-permute-start(bf16[32,5120]{1,0:T(8,128)(2,1)S(1)} %slice_select_fusion.1), channel_id=1, source_target_pairs={{0,4},{4,0},{8,12},{12,8},{1,5},{5,1},{9,13},{13,9},{2,6},{6,2},{1... | collective-permute-start | bytes 983048 | tf_op jit(solution)/shard_map/ppermute | solution.py:230
  10.0 4.1 %copy-start = (bf16[64,16384]{1,0:T(8,128)(2,1)S(1)}, bf16[64,16384]{1,0:T(8,128)(2,1)}, u32[]{:S(2)}) copy-start(bf16[64,16384]{1,0:T(8,128)(2,1)} %test.2) | copy-start | bytes 6291460
  14.1 0.8 copy-start.1
  15.0 15.3 %collective-permute-start.4 = (bf16[32,5120]{1,0:T(8,128)(2,1)S(1)}, bf16[32,5120]{1,0:T(8,128)(2,1)S(1)}, u32[]{:S(2)}, u32[]{:S(2)}) collective-permute-start(bf16[32,5120]{1,0:T(8,128)(2,1)S(1)} %slice_select_fusion.1), channel_id=1, source_target_pairs={{0,0},{1,1},{2,2},{3,3},{4,8},{5,9},{6,10},{7,11},{8,4},{9,5},{10,... | collective-permute-start | bytes 983048 | tf_op jit(solution)/shard_map/ppermute | solution.py:234
  16.3 14.0 %collective-permute-start.1 = (bf16[32,5120]{1,0:T(8,128)(2,1)S(1)}, bf16[32,5120]{1,0:T(8,128)(2,1)S(1)}, u32[]{:S(2)}, u32[]{:S(2)}) collective-permute-start(bf16[32,5120]{1,0:T(8,128)(2,1)S(1)} %slice_select_fusion), channel_id=1, source_target_pairs={{0,4},{4,0},{8,12},{12,8},{1,5},{5,1},{9,13},{13,9},{2,6},{6,2},{1... | collective-permute-start | bytes 983048 | tf_op jit(solution)/shard_map/ppermute | solution.py:230
  19.4 10.9 %collective-permute-start.5 = (bf16[32,5120]{1,0:T(8,128)(2,1)S(1)}, bf16[32,5120]{1,0:T(8,128)(2,1)S(1)}, u32[]{:S(2)}, u32[]{:S(2)}) collective-permute-start(bf16[32,5120]{1,0:T(8,128)(2,1)S(1)} %collective-permute-done.refs_0_), channel_id=1, source_target_pairs={{0,16},{16,0},{1,17},{17,1},{2,18},{18,2},{3,19},{19,3},{4,20},{20... | collective-permute-start | bytes 983048 | tf_op jit(solution)/shard_map/ppermute | solution.py:243
  23.3 14.0 %collective-permute-start.11 = (bf16[32,5120]{1,0:T(8,128)(2,1)S(1)}, bf16[32,5120]{1,0:T(8,128)(2,1)S(1)}, u32[]{:S(2)}, u32[]{:S(2)}) collective-permute-start(bf16[32,5120]{1,0:T(8,128)(2,1)S(1)} %broadcast_select_fusion.7), channel_id=1, source_target_pairs={{0,4},{4,0},{8,12},{12,8},{1,5},{5,1},{9,13},{13,9},{2,6},{6,2},{1... | collective-permute-start | bytes 983048 | tf_op jit(solution)/shard_map/ppermute | solution.py:230
  25.4 12.0 %collective-permute-start.7 = (bf16[32,5120]{1,0:T(8,128)(2,1)S(1)}, bf16[32,5120]{1,0:T(8,128)(2,1)S(1)}, u32[]{:S(2)}, u32[]{:S(2)}) collective-permute-start(bf16[32,5120]{1,0:T(8,128)(2,1)S(1)} %collective-permute-done.2.refs_0_), channel_id=1, source_target_pairs={{0,16},{16,0},{1,17},{17,1},{2,18},{18,2},{3,19},{19,3},{4,20},{20... | collective-permute-start | bytes 983048 | tf_op jit(solution)/shard_map/ppermute | solution.py:243
  30.3 9.6 %collective-permute-start.6 = (bf16[32,5120]{1,0:T(8,128)(2,1)S(1)}, bf16[32,5120]{1,0:T(8,128)(2,1)S(1)}, u32[]{:S(2)}, u32[]{:S(2)}) collective-permute-start(bf16[32,5120]{1,0:T(8,128)(2,1)S(1)} %slice_select_fusion), channel_id=1, source_target_pairs={{0,0},{1,1},{2,2},{3,3},{4,8},{5,9},{6,10},{7,11},{8,4},{9,5},{10,... | collective-permute-start | bytes 983048 | tf_op jit(solution)/shard_map/ppermute | solution.py:234
  31.0 13.5 %collective-permute-start.9 = (bf16[32,5120]{1,0:T(8,128)(2,1)S(1)}, bf16[32,5120]{1,0:T(8,128)(2,1)S(1)}, u32[]{:S(2)}, u32[]{:S(2)}) collective-permute-start(bf16[32,5120]{1,0:T(8,128)(2,1)S(1)} %collective-permute-done.1.refs_0_), channel_id=1, source_target_pairs={{0,16},{16,0},{1,17},{17,1},{2,18},{18,2},{3,19},{19,3},{4,20},{20... | collective-permute-start | bytes 983048 | tf_op jit(solution)/shard_map/ppermute | solution.py:243
  33.5 10.9 %collective-permute-start.14 = (bf16[32,5120]{1,0:T(8,128)(2,1)S(1)}, bf16[32,5120]{1,0:T(8,128)(2,1)S(1)}, u32[]{:S(2)}, u32[]{:S(2)}) collective-permute-start(bf16[32,5120]{1,0:T(8,128)(2,1)S(1)} %broadcast_select_fusion.5), channel_id=1, source_target_pairs={{0,4},{4,0},{8,12},{12,8},{1,5},{5,1},{9,13},{13,9},{2,6},{6,2},{1... | collective-permute-start | bytes 983048 | tf_op jit(solution)/shard_map/ppermute | solution.py:230
  37.4 13.8 %collective-permute-start.12 = (bf16[32,5120]{1,0:T(8,128)(2,1)S(1)}, bf16[32,5120]{1,0:T(8,128)(2,1)S(1)}, u32[]{:S(2)}, u32[]{:S(2)}) collective-permute-start(bf16[32,5120]{1,0:T(8,128)(2,1)S(1)} %broadcast_select_fusion.6.refs_0_), channel_id=1, source_target_pairs={{0,16},{16,0},{1,17},{17,1},{2,18},{18,2},{3,19},{19,3},{4,20},{20... | collective-permute-start | bytes 983048 | tf_op jit(solution)/shard_map/ppermute | solution.py:243
  39.9 12.1 %collective-permute-start.8 = (bf16[32,5120]{1,0:T(8,128)(2,1)S(1)}, bf16[32,5120]{1,0:T(8,128)(2,1)S(1)}, u32[]{:S(2)}, u32[]{:S(2)}) collective-permute-start(bf16[32,5120]{1,0:T(8,128)(2,1)S(1)} %collective-permute-done.refs_0_), channel_id=1, source_target_pairs={{0,0},{1,1},{2,2},{3,3},{4,8},{5,9},{6,10},{7,11},{8,4},{9,5},{10,... | collective-permute-start | bytes 983048 | tf_op jit(solution)/shard_map/ppermute | solution.py:234
  40.6 16.3 %collective-permute-start.18 = (bf16[32,5120]{1,0:T(8,128)(2,1)S(1)}, bf16[32,5120]{1,0:T(8,128)(2,1)S(1)}, u32[]{:S(2)}, u32[]{:S(2)}) collective-permute-start(bf16[32,5120]{1,0:T(8,128)(2,1)S(1)} %collective-permute-done.6), channel_id=1, source_target_pairs={{0,4},{4,0},{8,12},{12,8},{1,5},{5,1},{9,13},{13,9},{2,6},{6,2},{1... | collective-permute-start | bytes 983048 | tf_op jit(solution)/shard_map/ppermute | solution.py:230
  44.5 14.1 %collective-permute-start.16 = (bf16[32,5120]{1,0:T(8,128)(2,1)S(1)}, bf16[32,5120]{1,0:T(8,128)(2,1)S(1)}, u32[]{:S(2)}, u32[]{:S(2)}) collective-permute-start(bf16[32,5120]{1,0:T(8,128)(2,1)S(1)} %broadcast_select_fusion.4.refs_0_), channel_id=1, source_target_pairs={{0,16},{16,0},{1,17},{17,1},{2,18},{18,2},{3,19},{19,3},{4,20},{20... | collective-permute-start | bytes 983048 | tf_op jit(solution)/shard_map/ppermute | solution.py:243
  52.1 7.4 %collective-permute-start.10 = (bf16[32,5120]{1,0:T(8,128)(2,1)S(1)}, bf16[32,5120]{1,0:T(8,128)(2,1)S(1)}, u32[]{:S(2)}, u32[]{:S(2)}) collective-permute-start(bf16[32,5120]{1,0:T(8,128)(2,1)S(1)} %collective-permute-done.2.refs_0_), channel_id=1, source_target_pairs={{0,0},{1,1},{2,2},{3,3},{4,8},{5,9},{6,10},{7,11},{8,4},{9,5},{10,... | collective-permute-start | bytes 983048 | tf_op jit(solution)/shard_map/ppermute | solution.py:234
  52.8 16.5 %collective-permute-start.15 = (bf16[32,5120]{1,0:T(8,128)(2,1)S(1)}, bf16[32,5120]{1,0:T(8,128)(2,1)S(1)}, u32[]{:S(2)}, u32[]{:S(2)}) collective-permute-start(bf16[32,5120]{1,0:T(8,128)(2,1)S(1)} %collective-permute-done.8), channel_id=1, source_target_pairs={{0,4},{4,0},{8,12},{12,8},{1,5},{5,1},{9,13},{13,9},{2,6},{6,2},{1... | collective-permute-start | bytes 983048 | tf_op jit(solution)/shard_map/ppermute | solution.py:230
  57.0 13.9 %collective-permute-start.19 = (bf16[32,5120]{1,0:T(8,128)(2,1)S(1)}, bf16[32,5120]{1,0:T(8,128)(2,1)S(1)}, u32[]{:S(2)}, u32[]{:S(2)}) collective-permute-start(bf16[32,5120]{1,0:T(8,128)(2,1)S(1)} %broadcast_select_fusion.2.refs_0_), channel_id=1, source_target_pairs={{0,16},{16,0},{1,17},{17,1},{2,18},{18,2},{3,19},{19,3},{4,20},{20... | collective-permute-start | bytes 983048 | tf_op jit(solution)/shard_map/ppermute | solution.py:243
  59.5 12.3 %collective-permute-start.13 = (bf16[32,5120]{1,0:T(8,128)(2,1)S(1)}, bf16[32,5120]{1,0:T(8,128)(2,1)S(1)}, u32[]{:S(2)}, u32[]{:S(2)}) collective-permute-start(bf16[32,5120]{1,0:T(8,128)(2,1)S(1)} %collective-permute-done.1.refs_0_), channel_id=1, source_target_pairs={{0,0},{1,1},{2,2},{3,3},{4,8},{5,9},{6,10},{7,11},{8,4},{9,5},{10,... | collective-permute-start | bytes 983048 | tf_op jit(solution)/shard_map/ppermute | solution.py:234
  60.2 20.0 %collective-permute-start.22 = (bf16[32,5120]{1,0:T(8,128)(2,1)S(1)}, bf16[32,5120]{1,0:T(8,128)(2,1)S(1)}, u32[]{:S(2)}, u32[]{:S(2)}) collective-permute-start(bf16[32,5120]{1,0:T(8,128)(2,1)S(1)} %collective-permute-done.10), channel_id=1, source_target_pairs={{0,4},{4,0},{8,12},{12,8},{1,5},{5,1},{9,13},{13,9},{2,6},{6,2},{1... | collective-permute-start | bytes 983048 | tf_op jit(solution)/shard_map/ppermute | solution.py:230
  69.3 19.1 %collective-permute-start.24 = (bf16[32,5120]{1,0:T(8,128)(2,1)S(1)}, bf16[32,5120]{1,0:T(8,128)(2,1)S(1)}, u32[]{:S(2)}, u32[]{:S(2)}) collective-permute-start(bf16[32,5120]{1,0:T(8,128)(2,1)S(1)} %broadcast_select_fusion.refs_0_), channel_id=1, source_target_pairs={{0,16},{16,0},{1,17},{17,1},{2,18},{18,2},{3,19},{19,3},{4,20},{20... | collective-permute-start | bytes 983048 | tf_op jit(solution)/shard_map/ppermute | solution.py:243
  71.9 10.0 %collective-permute-start.21 = (bf16[64,2048]{1,0:T(8,128)(2,1)S(1)}, bf16[64,2048]{1,0:T(8,128)(2,1)S(1)}, u32[]{:S(2)}, u32[]{:S(2)}) collective-permute-start(bf16[64,2048]{1,0:T(8,128)(2,1)S(1)} %pad_maximum_fusion), channel_id=1, source_target_pairs={{0,0},{1,1},{2,2},{3,3},{4,8},{5,9},{6,10},{7,11},{8,4},{9,5},{10,... | collective-permute-start | bytes 786440 | tf_op jit(solution)/shard_map/ppermute | solution.py:234
  72.5 12.7 %collective-permute-start.17 = (bf16[32,5120]{1,0:T(8,128)(2,1)S(1)}, bf16[32,5120]{1,0:T(8,128)(2,1)S(1)}, u32[]{:S(2)}, u32[]{:S(2)}) collective-permute-start(bf16[32,5120]{1,0:T(8,128)(2,1)S(1)} %collective-permute-done.13), channel_id=1, source_target_pairs={{0,4},{4,0},{8,12},{12,8},{1,5},{5,1},{9,13},{13,9},{2,6},{6,2},{1... | collective-permute-start | bytes 983048 | tf_op jit(solution)/shard_map/ppermute | solution.py:230
  80.3 9.1 %collective-permute-start.23 = (bf16[32,5120]{1,0:T(8,128)(2,1)S(1)}, bf16[32,5120]{1,0:T(8,128)(2,1)S(1)}, u32[]{:S(2)}, u32[]{:S(2)}) collective-permute-start(bf16[32,5120]{1,0:T(8,128)(2,1)S(1)} %broadcast_select_fusion.1.refs_0_), channel_id=1, source_target_pairs={{0,16},{16,0},{1,17},{17,1},{2,18},{18,2},{3,19},{19,3},{4,20},{20... | collective-permute-start | bytes 983048 | tf_op jit(solution)/shard_map/ppermute | solution.py:243
  82.4 4.5 %collective-permute-start.25 = (f32[2,64,256]{2,1,0:T(8,128)S(1)}, f32[2,64,256]{2,1,0:T(8,128)S(1)}, u32[]{:S(2)}, u32[]{:S(2)}) collective-permute-start(f32[2,64,256]{2,1,0:T(8,128)S(1)} %slice_bitcast_fusion), channel_id=1, source_target_pairs={{0,1},{1,0},{2,3},{3,2},{4,5},{5,4},{6,7},{7,6},{8,9},{9,8},{10,11... | collective-permute-start | bytes 393224 | tf_op jit(solution)/shard_map/ppermute | solution.py:253
  85.3 9.1 %collective-permute-start.20 = (bf16[32,5120]{1,0:T(8,128)(2,1)S(1)}, bf16[32,5120]{1,0:T(8,128)(2,1)S(1)}, u32[]{:S(2)}, u32[]{:S(2)}) collective-permute-start(bf16[32,5120]{1,0:T(8,128)(2,1)S(1)} %broadcast_select_fusion.3.refs_0_), channel_id=1, source_target_pairs={{0,16},{16,0},{1,17},{17,1},{2,18},{18,2},{3,19},{19,3},{4,20},{20... | collective-permute-start | bytes 983048 | tf_op jit(solution)/shard_map/ppermute | solution.py:243
  86.9 4.3 %collective-permute-start.26 = (f32[1,64,256]{2,1,0:T(8,128)S(1)}, f32[1,64,256]{2,1,0:T(8,128)S(1)}, u32[]{:S(2)}, u32[]{:S(2)}) collective-permute-start(f32[1,64,256]{2,1,0:T(8,128)S(1)} %slice_bitcast_fusion.6), channel_id=1, source_target_pairs={{0,2},{1,3},{2,0},{3,1},{4,6},{5,7},{6,4},{7,5},{8,10},{9,11},{10,... | collective-permute-start | bytes 196616 | tf_op jit(solution)/shard_map/ppermute | solution.py:253
  91.3 4.3 %collective-permute-start.27 = (f32[64,256]{1,0:T(8,128)S(1)}, f32[64,256]{1,0:T(8,128)S(1)}, u32[]{:S(2)}, u32[]{:S(2)}) collective-permute-start(f32[64,256]{1,0:T(8,128)S(1)} %fusion.9), channel_id=1, source_target_pairs={{0,4},{4,0},{8,12},{12,8},{1,5},{5,1},{9,13},{13,9},{2,6},{6,2},{1... | collective-permute-start | bytes 196616 | tf_op jit(solution)/shard_map/ppermute | solution.py:321
  95.6 1.3 %collective-permute-start.28 = (f32[2,64,256]{2,1,0:T(8,128)S(1)}, f32[2,64,256]{2,1,0:T(8,128)S(1)}, u32[]{:S(2)}, u32[]{:S(2)}) collective-permute-start(f32[2,64,256]{2,1,0:T(8,128)S(1)} %slice_bitcast_fusion.2), channel_id=1, source_target_pairs={{0,1},{1,0},{2,3},{3,2},{4,5},{5,4},{6,7},{7,6},{8,9},{9,8},{10,11... | collective-permute-start | bytes 393224 | tf_op jit(solution)/shard_map/ppermute | solution.py:253
  97.0 4.3 %collective-permute-start.29 = (f32[1,64,256]{2,1,0:T(8,128)S(1)}, f32[1,64,256]{2,1,0:T(8,128)S(1)}, u32[]{:S(2)}, u32[]{:S(2)}) collective-permute-start(f32[1,64,256]{2,1,0:T(8,128)S(1)} %slice_bitcast_fusion.4), channel_id=1, source_target_pairs={{0,2},{1,3},{2,0},{3,1},{4,6},{5,7},{6,4},{7,5},{8,10},{9,11},{10,... | collective-permute-start | bytes 196616 | tf_op jit(solution)/shard_map/ppermute | solution.py:253

commit v28 on v20

--- a/solution.py
+++ b/solution.py
@@ -9,7 +9,7 @@
 
 CONTRACT = (((1,), (1,)), ((), ()))
 LANES = 128
-CHUNKS = 4
+CHUNKS = 5
 
 
 def product(rows, scale, train, unit):

time: 90.9 us -> 96.3 us (1.059)
  starting transfers between devices: 24.5 us -> 27.1 us
  waiting for transfers between devices: 46.2 us -> 48.6 us
  local copies, waits for them, and re-layouts: 4 us -> 5.27 us
  other arithmetic: 4.03 us -> 2.86 us
    ppermute x12 -> x15, starting transfers between devices: 5.33 us -> 7.96 us  [hop(): hops.append(lax.ppermute(after(block, *waits), 'ex', ring))]
    ppermute x12 -> x15, waiting for transfers between devices: 13 us -> 14.3 us  [swap(): swaps.append(lax.ppermute(after(block, *waits), 'grp', [(0, 1), (1, 0)]))]
    select_n x4 -> x5, other arithmetic: 3.36 us -> 2.19 us  [share(): return jnp.where(first_grp, rows[:half, columns], rows[half:, columns])]
    slice x1 -> x2, local copies, waits for them, and re-layouts: 3.97 us -> 5.11 us  [on_device(): trains = [train[:, here] for here in columns]]
    ppermute x12 -> x15, waiting for transfers between devices: 29.5 us -> 30.2 us  [hop(): hops.append(lax.ppermute(after(block, *waits), 'ex', ring))]
    ppermute x12 -> x15, starting transfers between devices: 17.2 us -> 17.5 us  [swap(): swaps.append(lax.ppermute(after(block, *waits), 'grp', [(0, 1), (1, 0)]))]
    pallas_call x13 -> x16, Pallas kernels: 11.8 us -> 12.1 us  [call(): pl.pallas_call(kernel, out_shape=jax.ShapeDtypeStruct((rows, docs), jnp.f...]
  transfers between devices with their start and end apart: 26 -> 32, of which waited for: 23 -> 20; matrix products, arithmetic and copies ran while one was open for 7% -> 7% of each run, Pallas kernels for 12% -> 12%
where the time goes in v28:
time: 96.3 us; the launch traced here: 96.1 us
  waiting for transfers between devices  48.6 us (50%)
  starting transfers between devices  27.1 us (28%)
  Pallas kernels  12.1 us (13%)
  local copies, waits for them, and re-layouts  5.27 us (5%)
  other arithmetic  2.86 us (3%)
    ppermute x15, waiting for transfers between devices, hop(): hops.append(lax.ppermute(after(block, *waits), 'ex', ring))  30.2 us
    ppermute x15, starting transfers between devices, swap(): swaps.append(lax.ppermute(after(block, *waits), 'grp', [(0, 1), (1, 0)]))  17.5 us
    ppermute x15, waiting for transfers between devices, swap(): swaps.append(lax.ppermute(after(block, *waits), 'grp', [(0, 1), (1, 0)]))  14.3 us
    pallas_call x16, Pallas kernels, call(): pl.pallas_call(kernel, out_shape=jax.ShapeDtypeStruct((rows, docs), jnp.f...  12.1 us
    ppermute x15, starting transfers between devices, hop(): hops.append(lax.ppermute(after(block, *waits), 'ex', ring))  7.96 us
    slice x2, local copies, waits for them, and re-layouts, on_device(): trains = [train[:, here] for here in columns]  5.11 us
    ppermute x2, waiting for transfers between devices, sum_over_feat(): held = pairs[:, 0] + lax.ppermute(pairs[:, 1], 'feat', partner)  4.11 us
    select_n x5, other arithmetic, share(): return jnp.where(first_grp, rows[:half, columns], rows[half:, columns])  2.19 us
  transfers between devices with their start and end apart: 32, of which 20 were waited for; matrix products, arithmetic and copies ran while one was open for 7% of the time, Pallas kernels for 12%

profile of v28, /device:TPU:0, one launch (start us, length us, event | category | flops | bytes accessed | tf_op | source)
XLA Modules:
  0.0 96.1 jit_solution(8781206790714511911)
XLA Ops:
  1.1 3.1 %collective-permute-start = (bf16[32,3200]{1,0:T(8,128)(2,1)S(1)}, bf16[32,3200]{1,0:T(8,128)(2,1)S(1)}, u32[]{:S(2)}, u32[]{:S(2)}) collective-permute-start(bf16[32,3200]{1,0:T(8,128)(2,1)S(1)} %slice_select_fusion.4), channel_id=1, source_target_pairs={{0,4},{4,8},{8,12},{12,0},{1,5},{5,9},{9,13},{13,1},{2,6},{6,10},{... | collective-permute-start | bytes 614408 | tf_op jit(solution)/shard_map/ppermute | solution.py:105
  4.1 1.1 %slice_select_fusion.2 = bf16[32,3328]{1,0:T(8,128)(2,1)S(1)} fusion(bf16[64,16384]{1,0:T(8,128)(2,1)} %test.1, pred[]{:T(512)S(6)} %eq.3), kind=kLoop, calls=%fused_computation.2 | loop fusion | flops 106496 | bytes 638977 | tf_op jit(solution)/shard_map/jit(_where)/select_n | solution.py:130
  5.2 1.6 %collective-permute-start.4 = (bf16[32,3328]{1,0:T(8,128)(2,1)S(1)}, bf16[32,3328]{1,0:T(8,128)(2,1)S(1)}, u32[]{:S(2)}, u32[]{:S(2)}) collective-permute-start(bf16[32,3328]{1,0:T(8,128)(2,1)S(1)} %slice_select_fusion.2), channel_id=1, source_target_pairs={{0,4},{4,8},{8,12},{12,0},{1,5},{5,9},{9,13},{13,1},{2,6},{6,10},{... | collective-permute-start | bytes 638984 | tf_op jit(solution)/shard_map/ppermute | solution.py:105
  6.8 2.1 %fusion.5 = (bf16[256,3200]{1,0:T(8,128)(2,1)S(1)}, bf16[256,3200]{1,0:T(8,128)(2,1)S(1)}) fusion(bf16[256,16384]{1,0:T(8,128)(2,1)} %param.3), kind=kLoop, calls=%fused_computation.15 | loop fusion | bytes 6553600 | tf_op jit(solution)/shard_map/slice | solution.py:136
  9.0 3.0 %fusion.4 = (bf16[256,3328]{1,0:T(8,128)(2,1)S(1)}, bf16[256,3328]{1,0:T(8,128)(2,1)S(1)}, bf16[256,3328]{1,0:T(8,128)(2,1)S(1)}) fusion(bf16[256,16384]{1,0:T(8,128)(2,1)} %param.3), kind=kLoop, calls=%fused_computation.14 | loop fusion | bytes 10223616 | tf_op jit(solution)/shard_map/slice | solution.py:136
  12.2 2.6 %shard_map.38.refs_4_ = f32[64,256]{1,0:T(8,128)S(1)} custom-call(bf16[64,16384]{1,0:T(8,128)(2,1)S(1)} %copy-done, f32[1,16384]{1,0:T(1,128)S(1)} %bitcast.28, bf16[256,3200]{1,0:T(8,128)(2,1)S(1)} %get-tuple-element.69.refs_3_.refs_0_, bf16[256,3328]{1,0:T(8,128)(2,1)S(1)} %get-tuple-element.66.refs_1_.refs_3_, ...), custom_call_target="tpu_custom_call" | custom-call | flops 536870912 | bytes 10485760 | tf_op jit(solution)/shard_map/pallas_call | solution.py:71
  14.8 1.6 %collective-permute-start.1 = (bf16[32,3200]{1,0:T(8,128)(2,1)S(1)}, bf16[32,3200]{1,0:T(8,128)(2,1)S(1)}, u32[]{:S(2)}, u32[]{:S(2)}) collective-permute-start(bf16[32,3200]{1,0:T(8,128)(2,1)S(1)} %slice_select_fusion.3), channel_id=1, source_target_pairs={{0,4},{4,8},{8,12},{12,0},{1,5},{5,9},{9,13},{13,1},{2,6},{6,10},{... | collective-permute-start | bytes 614408 | tf_op jit(solution)/shard_map/ppermute | solution.py:105
  16.5 1.5 %collective-permute-start.2 = (bf16[32,3200]{1,0:T(8,128)(2,1)S(1)}, bf16[32,3200]{1,0:T(8,128)(2,1)S(1)}, u32[]{:S(2)}, u32[]{:S(2)}) collective-permute-start(bf16[32,3200]{1,0:T(8,128)(2,1)S(1)} %collective-permute-done.refs_0_), channel_id=1, source_target_pairs={{0,16},{16,0},{1,17},{17,1},{2,18},{18,2},{3,19},{19,3},{4,20},{20... | collective-permute-start | bytes 614408 | tf_op jit(solution)/shard_map/ppermute | solution.py:114
  18.6 5.9 %collective-permute-done.2.refs_1_ = bf16[32,3200]{1,0:T(8,128)(2,1)S(1)} collective-permute-done((bf16[32,3200]{1,0:T(8,128)(2,1)S(1)}, bf16[32,3200]{1,0:T(8,128)(2,1)S(1)}, u32[]{:S(2)}, u32[]{:S(2)}) %collective-permute-start.2) | collective-permute-done | bytes 204832 | tf_op jit(solution)/shard_map/ppermute | solution.py:114
  25.2 1.7 %collective-permute-start.9 = (bf16[32,3200]{1,0:T(8,128)(2,1)S(1)}, bf16[32,3200]{1,0:T(8,128)(2,1)S(1)}, u32[]{:S(2)}, u32[]{:S(2)}) collective-permute-start(bf16[32,3200]{1,0:T(8,128)(2,1)S(1)} %collective-permute-done.1.refs_0_), channel_id=1, source_target_pairs={{0,16},{16,0},{1,17},{17,1},{2,18},{18,2},{3,19},{19,3},{4,20},{20... | collective-permute-start | bytes 614408 | tf_op jit(solution)/shard_map/ppermute | solution.py:114
  26.9 2.4 %collective-permute-done.5.refs_0_ = bf16[32,3328]{1,0:T(8,128)(2,1)S(1)} collective-permute-done((bf16[32,3328]{1,0:T(8,128)(2,1)S(1)}, bf16[32,3328]{1,0:T(8,128)(2,1)S(1)}, u32[]{:S(2)}, u32[]{:S(2)}) %collective-permute-start.5) | collective-permute-done | bytes 213024 | tf_op jit(solution)/shard_map/ppermute | solution.py:105
  29.3 1.5 %collective-permute-start.8 = (bf16[32,3328]{1,0:T(8,128)(2,1)S(1)}, bf16[32,3328]{1,0:T(8,128)(2,1)S(1)}, u32[]{:S(2)}, u32[]{:S(2)}) collective-permute-start(bf16[32,3328]{1,0:T(8,128)(2,1)S(1)} %collective-permute-done.5.refs_0_), channel_id=1, source_target_pairs={{0,16},{16,0},{1,17},{17,1},{2,18},{18,2},{3,19},{19,3},{4,20},{20... | collective-permute-start | bytes 638984 | tf_op jit(solution)/shard_map/ppermute | solution.py:114
  31.5 1.9 %collective-permute-done.9.refs_1_ = bf16[32,3200]{1,0:T(8,128)(2,1)S(1)} collective-permute-done((bf16[32,3200]{1,0:T(8,128)(2,1)S(1)}, bf16[32,3200]{1,0:T(8,128)(2,1)S(1)}, u32[]{:S(2)}, u32[]{:S(2)}) %collective-permute-start.9) | collective-permute-done | bytes 204832 | tf_op jit(solution)/shard_map/ppermute | solution.py:114
  33.4 2.6 %collective-permute-start.14 = (bf16[32,3328]{1,0:T(8,128)(2,1)S(1)}, bf16[32,3328]{1,0:T(8,128)(2,1)S(1)}, u32[]{:S(2)}, u32[]{:S(2)}) collective-permute-start(bf16[32,3328]{1,0:T(8,128)(2,1)S(1)} %collective-permute-done.3.refs_0_), channel_id=1, source_target_pairs={{0,16},{16,0},{1,17},{17,1},{2,18},{18,2},{3,19},{19,3},{4,20},{20... | collective-permute-start | bytes 638984 | tf_op jit(solution)/shard_map/ppermute | solution.py:114
  37.2 3.2 %collective-permute-done.7.refs_0_ = bf16[32,3200]{1,0:T(8,128)(2,1)S(1)} collective-permute-done((bf16[32,3200]{1,0:T(8,128)(2,1)S(1)}, bf16[32,3200]{1,0:T(8,128)(2,1)S(1)}, u32[]{:S(2)}, u32[]{:S(2)}) %collective-permute-start.7) | collective-permute-done | bytes 204832 | tf_op jit(solution)/shard_map/ppermute | solution.py:105
  43.2 3.4 %collective-permute-done.13.refs_0_ = bf16[32,3328]{1,0:T(8,128)(2,1)S(1)} collective-permute-done((bf16[32,3328]{1,0:T(8,128)(2,1)S(1)}, bf16[32,3328]{1,0:T(8,128)(2,1)S(1)}, u32[]{:S(2)}, u32[]{:S(2)}) %collective-permute-start.13) | collective-permute-done | bytes 213024 | tf_op jit(solution)/shard_map/ppermute | solution.py:105
  47.8 3.2 %collective-permute-done.10.refs_0_ = bf16[32,3200]{1,0:T(8,128)(2,1)S(1)} collective-permute-done((bf16[32,3200]{1,0:T(8,128)(2,1)S(1)}, bf16[32,3200]{1,0:T(8,128)(2,1)S(1)}, u32[]{:S(2)}, u32[]{:S(2)}) %collective-permute-start.10) | collective-permute-done | bytes 204832 | tf_op jit(solution)/shard_map/ppermute | solution.py:105
  51.0 4.3 %collective-permute-done.15.refs_0_ = bf16[32,3328]{1,0:T(8,128)(2,1)S(1)} collective-permute-done((bf16[32,3328]{1,0:T(8,128)(2,1)S(1)}, bf16[32,3328]{1,0:T(8,128)(2,1)S(1)}, u32[]{:S(2)}, u32[]{:S(2)}) %collective-permute-start.15) | collective-permute-done | bytes 213024 | tf_op jit(solution)/shard_map/ppermute | solution.py:105
  56.4 2.0 %collective-permute-done.19.refs_1_ = bf16[32,3200]{1,0:T(8,128)(2,1)S(1)} collective-permute-done((bf16[32,3200]{1,0:T(8,128)(2,1)S(1)}, bf16[32,3200]{1,0:T(8,128)(2,1)S(1)}, u32[]{:S(2)}, u32[]{:S(2)}) %collective-permute-start.19) | collective-permute-done | bytes 204832 | tf_op jit(solution)/shard_map/ppermute | solution.py:114
  59.4 1.1 %collective-permute-start.26 = (bf16[32,3328]{1,0:T(8,128)(2,1)S(1)}, bf16[32,3328]{1,0:T(8,128)(2,1)S(1)}, u32[]{:S(2)}, u32[]{:S(2)}) collective-permute-start(bf16[32,3328]{1,0:T(8,128)(2,1)S(1)} %collective-permute-done.12.refs_0_), channel_id=1, source_target_pairs={{0,16},{16,0},{1,17},{17,1},{2,18},{18,2},{3,19},{19,3},{4,20},{20... | collective-permute-start | bytes 638984 | tf_op jit(solution)/shard_map/ppermute | solution.py:114
  61.2 2.4 %collective-permute-done.17.refs_0_ = bf16[32,3200]{1,0:T(8,128)(2,1)S(1)} collective-permute-done((bf16[32,3200]{1,0:T(8,128)(2,1)S(1)}, bf16[32,3200]{1,0:T(8,128)(2,1)S(1)}, u32[]{:S(2)}, u32[]{:S(2)}) %collective-permute-start.17) | collective-permute-done | bytes 204832 | tf_op jit(solution)/shard_map/ppermute | solution.py:105
  63.6 3.1 %collective-permute-start.21 = (bf16[32,3200]{1,0:T(8,128)(2,1)S(1)}, bf16[32,3200]{1,0:T(8,128)(2,1)S(1)}, u32[]{:S(2)}, u32[]{:S(2)}) collective-permute-start(bf16[32,3200]{1,0:T(8,128)(2,1)S(1)} %collective-permute-done.17.refs_0_), channel_id=1, source_target_pairs={{0,16},{16,0},{1,17},{17,1},{2,18},{18,2},{3,19},{19,3},{4,20},{20... | collective-permute-start | bytes 614408 | tf_op jit(solution)/shard_map/ppermute | solution.py:114
  68.2 3.0 %collective-permute-done.23.refs_0_ = bf16[32,3328]{1,0:T(8,128)(2,1)S(1)} collective-permute-done((bf16[32,3328]{1,0:T(8,128)(2,1)S(1)}, bf16[32,3328]{1,0:T(8,128)(2,1)S(1)}, u32[]{:S(2)}, u32[]{:S(2)}) %collective-permute-start.23) | collective-permute-done | bytes 213024 | tf_op jit(solution)/shard_map/ppermute | solution.py:105
  72.7 2.9 %collective-permute-done.20.refs_0_ = bf16[32,3200]{1,0:T(8,128)(2,1)S(1)} collective-permute-done((bf16[32,3200]{1,0:T(8,128)(2,1)S(1)}, bf16[32,3200]{1,0:T(8,128)(2,1)S(1)}, u32[]{:S(2)}, u32[]{:S(2)}) %collective-permute-start.20) | collective-permute-done | bytes 204832 | tf_op jit(solution)/shard_map/ppermute | solution.py:105
  75.5 1.6 %collective-permute-start.29 = (bf16[32,3200]{1,0:T(8,128)(2,1)S(1)}, bf16[32,3200]{1,0:T(8,128)(2,1)S(1)}, u32[]{:S(2)}, u32[]{:S(2)}) collective-permute-start(bf16[32,3200]{1,0:T(8,128)(2,1)S(1)} %collective-permute-done.20.refs_0_), channel_id=1, source_target_pairs={{0,16},{16,0},{1,17},{17,1},{2,18},{18,2},{3,19},{19,3},{4,20},{20... | collective-permute-start | bytes 614408 | tf_op jit(solution)/shard_map/ppermute | solution.py:114
  77.2 1.7 %collective-permute-done.27.refs_0_ = bf16[32,3328]{1,0:T(8,128)(2,1)S(1)} collective-permute-done((bf16[32,3328]{1,0:T(8,128)(2,1)S(1)}, bf16[32,3328]{1,0:T(8,128)(2,1)S(1)}, u32[]{:S(2)}, u32[]{:S(2)}) %collective-permute-start.27) | collective-permute-done | bytes 213024 | tf_op jit(solution)/shard_map/ppermute | solution.py:105
  80.3 2.8 %collective-permute-done.22.refs_0_ = bf16[32,3328]{1,0:T(8,128)(2,1)S(1)} collective-permute-done((bf16[32,3328]{1,0:T(8,128)(2,1)S(1)}, bf16[32,3328]{1,0:T(8,128)(2,1)S(1)}, u32[]{:S(2)}, u32[]{:S(2)}) %collective-permute-start.22) | collective-permute-done | bytes 213024 | tf_op jit(solution)/shard_map/ppermute | solution.py:105
  83.2 1.6 %collective-permute-start.25 = (bf16[32,3328]{1,0:T(8,128)(2,1)S(1)}, bf16[32,3328]{1,0:T(8,128)(2,1)S(1)}, u32[]{:S(2)}, u32[]{:S(2)}) collective-permute-start(bf16[32,3328]{1,0:T(8,128)(2,1)S(1)} %collective-permute-done.22.refs_0_), channel_id=1, source_target_pairs={{0,16},{16,0},{1,17},{17,1},{2,18},{18,2},{3,19},{19,3},{4,20},{20... | collective-permute-start | bytes 638984 | tf_op jit(solution)/shard_map/ppermute | solution.py:114
  86.1 2.9 %collective-permute-done.25.refs_1_ = bf16[32,3328]{1,0:T(8,128)(2,1)S(1)} collective-permute-done((bf16[32,3328]{1,0:T(8,128)(2,1)S(1)}, bf16[32,3328]{1,0:T(8,128)(2,1)S(1)}, u32[]{:S(2)}, u32[]{:S(2)}) %collective-permute-start.25) | collective-permute-done | bytes 213024 | tf_op jit(solution)/shard_map/ppermute | solution.py:114
  89.8 1.3 %collective-permute-done.30 = f32[2,64,256]{2,1,0:T(8,128)S(1)} collective-permute-done((f32[2,64,256]{2,1,0:T(8,128)S(1)}, f32[2,64,256]{2,1,0:T(8,128)S(1)}, u32[]{:S(2)}, u32[]{:S(2)}) %collective-permute-start.30) | collective-permute-done | bytes 131104 | tf_op jit(solution)/shard_map/ppermute | solution.py:123
  91.2 1.6 %collective-permute-start.31 = (f32[1,64,256]{2,1,0:T(8,128)S(1)}, f32[1,64,256]{2,1,0:T(8,128)S(1)}, u32[]{:S(2)}, u32[]{:S(2)}) collective-permute-start(f32[1,64,256]{2,1,0:T(8,128)S(1)} %slice_bitcast_fusion.2), channel_id=1, source_target_pairs={{0,2},{1,3},{2,0},{3,1},{4,6},{5,7},{6,4},{7,5},{8,10},{9,11},{10,... | collective-permute-start | bytes 196616 | tf_op jit(solution)/shard_map/ppermute | solution.py:123
  92.7 2.8 %collective-permute-done.31 = f32[1,64,256]{2,1,0:T(8,128)S(1)} collective-permute-done((f32[1,64,256]{2,1,0:T(8,128)S(1)}, f32[1,64,256]{2,1,0:T(8,128)S(1)}, u32[]{:S(2)}, u32[]{:S(2)}) %collective-permute-start.31) | collective-permute-done | bytes 65568 | tf_op jit(solution)/shard_map/ppermute | solution.py:123
  (64 shorter events, 18.5 us)
Async XLA Ops:
  1.1 13.8 %collective-permute-start = (bf16[32,3200]{1,0:T(8,128)(2,1)S(1)}, bf16[32,3200]{1,0:T(8,128)(2,1)S(1)}, u32[]{:S(2)}, u32[]{:S(2)}) collective-permute-start(bf16[32,3200]{1,0:T(8,128)(2,1)S(1)} %slice_select_fusion.4), channel_id=1, source_target_pairs={{0,4},{4,8},{8,12},{12,0},{1,5},{5,9},{9,13},{13,1},{2,6},{6,10},{... | collective-permute-start | bytes 614408 | tf_op jit(solution)/shard_map/ppermute | solution.py:105
  5.2 12.8 %collective-permute-start.4 = (bf16[32,3328]{1,0:T(8,128)(2,1)S(1)}, bf16[32,3328]{1,0:T(8,128)(2,1)S(1)}, u32[]{:S(2)}, u32[]{:S(2)}) collective-permute-start(bf16[32,3328]{1,0:T(8,128)(2,1)S(1)} %slice_select_fusion.2), channel_id=1, source_target_pairs={{0,4},{4,8},{8,12},{12,0},{1,5},{5,9},{9,13},{13,1},{2,6},{6,10},{... | collective-permute-start | bytes 638984 | tf_op jit(solution)/shard_map/ppermute | solution.py:105
  14.8 10.3 %collective-permute-start.1 = (bf16[32,3200]{1,0:T(8,128)(2,1)S(1)}, bf16[32,3200]{1,0:T(8,128)(2,1)S(1)}, u32[]{:S(2)}, u32[]{:S(2)}) collective-permute-start(bf16[32,3200]{1,0:T(8,128)(2,1)S(1)} %slice_select_fusion.3), channel_id=1, source_target_pairs={{0,4},{4,8},{8,12},{12,0},{1,5},{5,9},{9,13},{13,1},{2,6},{6,10},{... | collective-permute-start | bytes 614408 | tf_op jit(solution)/shard_map/ppermute | solution.py:105
  16.5 8.0 %collective-permute-start.2 = (bf16[32,3200]{1,0:T(8,128)(2,1)S(1)}, bf16[32,3200]{1,0:T(8,128)(2,1)S(1)}, u32[]{:S(2)}, u32[]{:S(2)}) collective-permute-start(bf16[32,3200]{1,0:T(8,128)(2,1)S(1)} %collective-permute-done.refs_0_), channel_id=1, source_target_pairs={{0,16},{16,0},{1,17},{17,1},{2,18},{18,2},{3,19},{19,3},{4,20},{20... | collective-permute-start | bytes 614408 | tf_op jit(solution)/shard_map/ppermute | solution.py:114
  18.0 11.3 %collective-permute-start.5 = (bf16[32,3328]{1,0:T(8,128)(2,1)S(1)}, bf16[32,3328]{1,0:T(8,128)(2,1)S(1)}, u32[]{:S(2)}, u32[]{:S(2)}) collective-permute-start(bf16[32,3328]{1,0:T(8,128)(2,1)S(1)} %slice_select_fusion.1), channel_id=1, source_target_pairs={{0,4},{4,8},{8,12},{12,0},{1,5},{5,9},{9,13},{13,1},{2,6},{6,10},{... | collective-permute-start | bytes 638984 | tf_op jit(solution)/shard_map/ppermute | solution.py:105
  18.2 11.1 %collective-permute-start.6 = (bf16[32,3328]{1,0:T(8,128)(2,1)S(1)}, bf16[32,3328]{1,0:T(8,128)(2,1)S(1)}, u32[]{:S(2)}, u32[]{:S(2)}) collective-permute-start(bf16[32,3328]{1,0:T(8,128)(2,1)S(1)} %collective-permute-done.4.refs_0_), channel_id=1, source_target_pairs={{0,16},{16,0},{1,17},{17,1},{2,18},{18,2},{3,19},{19,3},{4,20},{20... | collective-permute-start | bytes 638984 | tf_op jit(solution)/shard_map/ppermute | solution.py:114
  25.1 8.3 %collective-permute-start.3 = (bf16[32,3328]{1,0:T(8,128)(2,1)S(1)}, bf16[32,3328]{1,0:T(8,128)(2,1)S(1)}, u32[]{:S(2)}, u32[]{:S(2)}) collective-permute-start(bf16[32,3328]{1,0:T(8,128)(2,1)S(1)} %slice_select_fusion), channel_id=1, source_target_pairs={{0,4},{4,8},{8,12},{12,0},{1,5},{5,9},{9,13},{13,1},{2,6},{6,10},{... | collective-permute-start | bytes 638984 | tf_op jit(solution)/shard_map/ppermute | solution.py:105
  25.2 8.2 %collective-permute-start.9 = (bf16[32,3200]{1,0:T(8,128)(2,1)S(1)}, bf16[32,3200]{1,0:T(8,128)(2,1)S(1)}, u32[]{:S(2)}, u32[]{:S(2)}) collective-permute-start(bf16[32,3200]{1,0:T(8,128)(2,1)S(1)} %collective-permute-done.1.refs_0_), channel_id=1, source_target_pairs={{0,16},{16,0},{1,17},{17,1},{2,18},{18,2},{3,19},{19,3},{4,20},{20... | collective-permute-start | bytes 614408 | tf_op jit(solution)/shard_map/ppermute | solution.py:114
  29.3 11.1 %collective-permute-start.8 = (bf16[32,3328]{1,0:T(8,128)(2,1)S(1)}, bf16[32,3328]{1,0:T(8,128)(2,1)S(1)}, u32[]{:S(2)}, u32[]{:S(2)}) collective-permute-start(bf16[32,3328]{1,0:T(8,128)(2,1)S(1)} %collective-permute-done.5.refs_0_), channel_id=1, source_target_pairs={{0,16},{16,0},{1,17},{17,1},{2,18},{18,2},{3,19},{19,3},{4,20},{20... | collective-permute-start | bytes 638984 | tf_op jit(solution)/shard_map/ppermute | solution.py:114
  31.4 9.0 %collective-permute-start.7 = (bf16[32,3200]{1,0:T(8,128)(2,1)S(1)}, bf16[32,3200]{1,0:T(8,128)(2,1)S(1)}, u32[]{:S(2)}, u32[]{:S(2)}) collective-permute-start(bf16[32,3200]{1,0:T(8,128)(2,1)S(1)} %collective-permute-done.refs_0_), channel_id=1, source_target_pairs={{0,4},{4,8},{8,12},{12,0},{1,5},{5,9},{9,13},{13,1},{2,6},{6,10},{... | collective-permute-start | bytes 614408 | tf_op jit(solution)/shard_map/ppermute | solution.py:105
  33.4 9.1 %collective-permute-start.14 = (bf16[32,3328]{1,0:T(8,128)(2,1)S(1)}, bf16[32,3328]{1,0:T(8,128)(2,1)S(1)}, u32[]{:S(2)}, u32[]{:S(2)}) collective-permute-start(bf16[32,3328]{1,0:T(8,128)(2,1)S(1)} %collective-permute-done.3.refs_0_), channel_id=1, source_target_pairs={{0,16},{16,0},{1,17},{17,1},{2,18},{18,2},{3,19},{19,3},{4,20},{20... | collective-permute-start | bytes 638984 | tf_op jit(solution)/shard_map/ppermute | solution.py:114
  36.6 10.0 %collective-permute-start.13 = (bf16[32,3328]{1,0:T(8,128)(2,1)S(1)}, bf16[32,3328]{1,0:T(8,128)(2,1)S(1)}, u32[]{:S(2)}, u32[]{:S(2)}) collective-permute-start(bf16[32,3328]{1,0:T(8,128)(2,1)S(1)} %collective-permute-done.4.refs_0_), channel_id=1, source_target_pairs={{0,4},{4,8},{8,12},{12,0},{1,5},{5,9},{9,13},{13,1},{2,6},{6,10},{... | collective-permute-start | bytes 638984 | tf_op jit(solution)/shard_map/ppermute | solution.py:105
  40.4 6.8 %collective-permute-start.11 = (bf16[32,3200]{1,0:T(8,128)(2,1)S(1)}, bf16[32,3200]{1,0:T(8,128)(2,1)S(1)}, u32[]{:S(2)}, u32[]{:S(2)}) collective-permute-start(bf16[32,3200]{1,0:T(8,128)(2,1)S(1)} %collective-permute-done.7.refs_0_), channel_id=1, source_target_pairs={{0,16},{16,0},{1,17},{17,1},{2,18},{18,2},{3,19},{19,3},{4,20},{20... | collective-permute-start | bytes 614408 | tf_op jit(solution)/shard_map/ppermute | solution.py:114
  41.6 9.3 %collective-permute-start.10 = (bf16[32,3200]{1,0:T(8,128)(2,1)S(1)}, bf16[32,3200]{1,0:T(8,128)(2,1)S(1)}, u32[]{:S(2)}, u32[]{:S(2)}) collective-permute-start(bf16[32,3200]{1,0:T(8,128)(2,1)S(1)} %collective-permute-done.1.refs_0_), channel_id=1, source_target_pairs={{0,4},{4,8},{8,12},{12,0},{1,5},{5,9},{9,13},{13,1},{2,6},{6,10},{... | collective-permute-start | bytes 614408 | tf_op jit(solution)/shard_map/ppermute | solution.py:105
  46.6 8.8 %collective-permute-start.15 = (bf16[32,3328]{1,0:T(8,128)(2,1)S(1)}, bf16[32,3328]{1,0:T(8,128)(2,1)S(1)}, u32[]{:S(2)}, u32[]{:S(2)}) collective-permute-start(bf16[32,3328]{1,0:T(8,128)(2,1)S(1)} %collective-permute-done.5.refs_0_), channel_id=1, source_target_pairs={{0,4},{4,8},{8,12},{12,0},{1,5},{5,9},{9,13},{13,1},{2,6},{6,10},{... | collective-permute-start | bytes 638984 | tf_op jit(solution)/shard_map/ppermute | solution.py:105
  46.6 8.8 %collective-permute-start.16 = (bf16[32,3328]{1,0:T(8,128)(2,1)S(1)}, bf16[32,3328]{1,0:T(8,128)(2,1)S(1)}, u32[]{:S(2)}, u32[]{:S(2)}) collective-permute-start(bf16[32,3328]{1,0:T(8,128)(2,1)S(1)} %collective-permute-done.13.refs_0_), channel_id=1, source_target_pairs={{0,16},{16,0},{1,17},{17,1},{2,18},{18,2},{3,19},{19,3},{4,20},{20... | collective-permute-start | bytes 638984 | tf_op jit(solution)/shard_map/ppermute | solution.py:114
  51.0 8.4 %collective-permute-start.12 = (bf16[32,3328]{1,0:T(8,128)(2,1)S(1)}, bf16[32,3328]{1,0:T(8,128)(2,1)S(1)}, u32[]{:S(2)}, u32[]{:S(2)}) collective-permute-start(bf16[32,3328]{1,0:T(8,128)(2,1)S(1)} %collective-permute-done.3.refs_0_), channel_id=1, source_target_pairs={{0,4},{4,8},{8,12},{12,0},{1,5},{5,9},{9,13},{13,1},{2,6},{6,10},{... | collective-permute-start | bytes 638984 | tf_op jit(solution)/shard_map/ppermute | solution.py:105
  51.0 7.4 %collective-permute-start.19 = (bf16[32,3200]{1,0:T(8,128)(2,1)S(1)}, bf16[32,3200]{1,0:T(8,128)(2,1)S(1)}, u32[]{:S(2)}, u32[]{:S(2)}) collective-permute-start(bf16[32,3200]{1,0:T(8,128)(2,1)S(1)} %collective-permute-done.10.refs_0_), channel_id=1, source_target_pairs={{0,16},{16,0},{1,17},{17,1},{2,18},{18,2},{3,19},{19,3},{4,20},{20... | collective-permute-start | bytes 614408 | tf_op jit(solution)/shard_map/ppermute | solution.py:114
  55.4 8.3 %collective-permute-start.18 = (bf16[32,3328]{1,0:T(8,128)(2,1)S(1)}, bf16[32,3328]{1,0:T(8,128)(2,1)S(1)}, u32[]{:S(2)}, u32[]{:S(2)}) collective-permute-start(bf16[32,3328]{1,0:T(8,128)(2,1)S(1)} %collective-permute-done.15.refs_0_), channel_id=1, source_target_pairs={{0,16},{16,0},{1,17},{17,1},{2,18},{18,2},{3,19},{19,3},{4,20},{20... | collective-permute-start | bytes 638984 | tf_op jit(solution)/shard_map/ppermute | solution.py:114
  56.0 7.6 %collective-permute-start.17 = (bf16[32,3200]{1,0:T(8,128)(2,1)S(1)}, bf16[32,3200]{1,0:T(8,128)(2,1)S(1)}, u32[]{:S(2)}, u32[]{:S(2)}) collective-permute-start(bf16[32,3200]{1,0:T(8,128)(2,1)S(1)} %collective-permute-done.7.refs_0_), channel_id=1, source_target_pairs={{0,4},{4,8},{8,12},{12,0},{1,5},{5,9},{9,13},{13,1},{2,6},{6,10},{... | collective-permute-start | bytes 614408 | tf_op jit(solution)/shard_map/ppermute | solution.py:105
  59.4 8.2 %collective-permute-start.26 = (bf16[32,3328]{1,0:T(8,128)(2,1)S(1)}, bf16[32,3328]{1,0:T(8,128)(2,1)S(1)}, u32[]{:S(2)}, u32[]{:S(2)}) collective-permute-start(bf16[32,3328]{1,0:T(8,128)(2,1)S(1)} %collective-permute-done.12.refs_0_), channel_id=1, source_target_pairs={{0,16},{16,0},{1,17},{17,1},{2,18},{18,2},{3,19},{19,3},{4,20},{20... | collective-permute-start | bytes 638984 | tf_op jit(solution)/shard_map/ppermute | solution.py:114
  61.1 10.0 %collective-permute-start.23 = (bf16[32,3328]{1,0:T(8,128)(2,1)S(1)}, bf16[32,3328]{1,0:T(8,128)(2,1)S(1)}, u32[]{:S(2)}, u32[]{:S(2)}) collective-permute-start(bf16[32,3328]{1,0:T(8,128)(2,1)S(1)} %collective-permute-done.13.refs_0_), channel_id=1, source_target_pairs={{0,4},{4,8},{8,12},{12,0},{1,5},{5,9},{9,13},{13,1},{2,6},{6,10},{... | collective-permute-start | bytes 638984 | tf_op jit(solution)/shard_map/ppermute | solution.py:105
  63.6 8.4 %collective-permute-start.21 = (bf16[32,3200]{1,0:T(8,128)(2,1)S(1)}, bf16[32,3200]{1,0:T(8,128)(2,1)S(1)}, u32[]{:S(2)}, u32[]{:S(2)}) collective-permute-start(bf16[32,3200]{1,0:T(8,128)(2,1)S(1)} %collective-permute-done.17.refs_0_), channel_id=1, source_target_pairs={{0,16},{16,0},{1,17},{17,1},{2,18},{18,2},{3,19},{19,3},{4,20},{20... | collective-permute-start | bytes 614408 | tf_op jit(solution)/shard_map/ppermute | solution.py:114
  67.3 8.2 %collective-permute-start.20 = (bf16[32,3200]{1,0:T(8,128)(2,1)S(1)}, bf16[32,3200]{1,0:T(8,128)(2,1)S(1)}, u32[]{:S(2)}, u32[]{:S(2)}) collective-permute-start(bf16[32,3200]{1,0:T(8,128)(2,1)S(1)} %collective-permute-done.10.refs_0_), channel_id=1, source_target_pairs={{0,4},{4,8},{8,12},{12,0},{1,5},{5,9},{9,13},{13,1},{2,6},{6,10},{... | collective-permute-start | bytes 614408 | tf_op jit(solution)/shard_map/ppermute | solution.py:105
  71.2 7.6 %collective-permute-start.27 = (bf16[32,3328]{1,0:T(8,128)(2,1)S(1)}, bf16[32,3328]{1,0:T(8,128)(2,1)S(1)}, u32[]{:S(2)}, u32[]{:S(2)}) collective-permute-start(bf16[32,3328]{1,0:T(8,128)(2,1)S(1)} %collective-permute-done.15.refs_0_), channel_id=1, source_target_pairs={{0,4},{4,8},{8,12},{12,0},{1,5},{5,9},{9,13},{13,1},{2,6},{6,10},{... | collective-permute-start | bytes 638984 | tf_op jit(solution)/shard_map/ppermute | solution.py:105
  71.2 8.5 %collective-permute-start.24 = (bf16[32,3328]{1,0:T(8,128)(2,1)S(1)}, bf16[32,3328]{1,0:T(8,128)(2,1)S(1)}, u32[]{:S(2)}, u32[]{:S(2)}) collective-permute-start(bf16[32,3328]{1,0:T(8,128)(2,1)S(1)} %collective-permute-done.23.refs_0_), channel_id=1, source_target_pairs={{0,16},{16,0},{1,17},{17,1},{2,18},{18,2},{3,19},{19,3},{4,20},{20... | collective-permute-start | bytes 638984 | tf_op jit(solution)/shard_map/ppermute | solution.py:114
  75.5 7.6 %collective-permute-start.22 = (bf16[32,3328]{1,0:T(8,128)(2,1)S(1)}, bf16[32,3328]{1,0:T(8,128)(2,1)S(1)}, u32[]{:S(2)}, u32[]{:S(2)}) collective-permute-start(bf16[32,3328]{1,0:T(8,128)(2,1)S(1)} %collective-permute-done.12.refs_0_), channel_id=1, source_target_pairs={{0,4},{4,8},{8,12},{12,0},{1,5},{5,9},{9,13},{13,1},{2,6},{6,10},{... | collective-permute-start | bytes 638984 | tf_op jit(solution)/shard_map/ppermute | solution.py:105
  75.5 9.3 %collective-permute-start.29 = (bf16[32,3200]{1,0:T(8,128)(2,1)S(1)}, bf16[32,3200]{1,0:T(8,128)(2,1)S(1)}, u32[]{:S(2)}, u32[]{:S(2)}) collective-permute-start(bf16[32,3200]{1,0:T(8,128)(2,1)S(1)} %collective-permute-done.20.refs_0_), channel_id=1, source_target_pairs={{0,16},{16,0},{1,17},{17,1},{2,18},{18,2},{3,19},{19,3},{4,20},{20... | collective-permute-start | bytes 614408 | tf_op jit(solution)/shard_map/ppermute | solution.py:114
  78.8 6.6 %collective-permute-start.28 = (bf16[32,3328]{1,0:T(8,128)(2,1)S(1)}, bf16[32,3328]{1,0:T(8,128)(2,1)S(1)}, u32[]{:S(2)}, u32[]{:S(2)}) collective-permute-start(bf16[32,3328]{1,0:T(8,128)(2,1)S(1)} %collective-permute-done.27.refs_0_), channel_id=1, source_target_pairs={{0,16},{16,0},{1,17},{17,1},{2,18},{18,2},{3,19},{19,3},{4,20},{20... | collective-permute-start | bytes 638984 | tf_op jit(solution)/shard_map/ppermute | solution.py:114
  83.2 5.8 %collective-permute-start.25 = (bf16[32,3328]{1,0:T(8,128)(2,1)S(1)}, bf16[32,3328]{1,0:T(8,128)(2,1)S(1)}, u32[]{:S(2)}, u32[]{:S(2)}) collective-permute-start(bf16[32,3328]{1,0:T(8,128)(2,1)S(1)} %collective-permute-done.22.refs_0_), channel_id=1, source_target_pairs={{0,16},{16,0},{1,17},{17,1},{2,18},{18,2},{3,19},{19,3},{4,20},{20... | collective-permute-start | bytes 638984 | tf_op jit(solution)/shard_map/ppermute | solution.py:114
  89.7 1.4 %collective-permute-start.30 = (f32[2,64,256]{2,1,0:T(8,128)S(1)}, f32[2,64,256]{2,1,0:T(8,128)S(1)}, u32[]{:S(2)}, u32[]{:S(2)}) collective-permute-start(f32[2,64,256]{2,1,0:T(8,128)S(1)} %slice_bitcast_fusion), channel_id=1, source_target_pairs={{0,1},{1,0},{2,3},{3,2},{4,5},{5,4},{6,7},{7,6},{8,9},{9,8},{10,11... | collective-permute-start | bytes 393224 | tf_op jit(solution)/shard_map/ppermute | solution.py:123
  91.2 4.3 %collective-permute-start.31 = (f32[1,64,256]{2,1,0:T(8,128)S(1)}, f32[1,64,256]{2,1,0:T(8,128)S(1)}, u32[]{:S(2)}, u32[]{:S(2)}) collective-permute-start(f32[1,64,256]{2,1,0:T(8,128)S(1)} %slice_bitcast_fusion.2), channel_id=1, source_target_pairs={{0,2},{1,3},{2,0},{3,1},{4,6},{5,7},{6,4},{7,5},{8,10},{9,11},{10,... | collective-permute-start | bytes 196616 | tf_op jit(solution)/shard_map/ppermute | solution.py:123
  (2 other events, 6.3 us)

commit v29 on v20

--- a/solution.py
+++ b/solution.py
@@ -50,7 +50,15 @@
     parts, (scale, train) = refs[:n_parts], refs[n_parts : n_parts + 2]
     sums, (out, kept) = refs[n_parts + 2 : -2], refs[-2:]
     column = lambda here: scale[:, start + here.start : start + here.stop]
-    total = product(arrived_rows(parts), column, train, unit) + sums[-1][...]
+    size = parts[0].shape[1]
+    blocks = n_parts // (train.shape[1] // size)
+
+    def rows(here):
+        piece, at = here.start // size, here.start % size
+        block = parts[piece * blocks : (piece + 1) * blocks]
+        return jnp.concatenate([p[:, at : at + here.stop - here.start] for p in block], axis=0)
+
+    total = product(rows, column, train, min(unit, size)) + sums[-1][...]
     queries = total.shape[0]
     half = queries // n_grp
     for t, value in enumerate([s[...] for s in sums[:-1]] + [total]):
@@ -142,11 +150,14 @@
         sums = [own] + [None] * final
         for t in range(1, n_ex):
             for c, (start, here) in enumerate(zip(starts, columns)):
+                if (t, c) == (final, CHUNKS - 1):
+                    pieces = [swap(hop(piece)) for piece in jnp.split(held[c], 2, axis=1)]
+                    parts = sum(pieces, [])
+                    operands = [*parts, scale, trains[c]]
+                    continue
                 held[c] = hop(held[c])
                 parts = swap(held[c])
                 operands = [*parts, scale, trains[c]]
-                if (t, c) == (final, CHUNKS - 1):
-                    continue
                 base = [] if sums[t] is None else [sums[t]]
                 sums[t] = call(
                     functools.partial(part_kernel, start, unit, len(parts), len(base)),

time: 90.9 us -> 90.8 us (level)
  waiting for transfers between devices: 46.2 us -> 43.8 us
  starting transfers between devices: 24.5 us -> 26.8 us
    ppermute x12 -> x13, waiting for transfers between devices: 13 us -> 9.33 us  [swap(): swaps.append(lax.ppermute(after(block, *waits), 'grp', [(0, 1), (1, 0)]))]
    ppermute x12 -> x13, starting transfers between devices: 5.33 us -> 6.73 us  [hop(): hops.append(lax.ppermute(after(block, *waits), 'ex', ring))]
    ppermute x12 -> x13, waiting for transfers between devices: 29.5 us -> 30.7 us  [hop(): hops.append(lax.ppermute(after(block, *waits), 'ex', ring))]
    ppermute x12 -> x13, starting transfers between devices: 17.2 us -> 18.2 us  [swap(): swaps.append(lax.ppermute(after(block, *waits), 'grp', [(0, 1), (1, 0)]))]
  transfers between devices with their start and end apart: 26 -> 28, of which waited for: 23 -> 23; matrix products, arithmetic and copies ran while one was open for 7% -> 7% of each run, Pallas kernels for 12% -> 12%
where the time goes in v29:
time: 90.8 us; the launch traced here: 90.6 us
  waiting for transfers between devices  43.8 us (48%)
  starting transfers between devices  26.8 us (30%)
  Pallas kernels  11.8 us (13%)
  local copies, waits for them, and re-layouts  4.13 us (5%)
  other arithmetic  3.88 us (4%)
    ppermute x13, waiting for transfers between devices, hop(): hops.append(lax.ppermute(after(block, *waits), 'ex', ring))  30.7 us
    ppermute x13, starting transfers between devices, swap(): swaps.append(lax.ppermute(after(block, *waits), 'grp', [(0, 1), (1, 0)]))  18.2 us
    pallas_call x13, Pallas kernels, call(): pl.pallas_call(kernel, out_shape=jax.ShapeDtypeStruct((rows, docs), jnp.f...  11.8 us
    ppermute x13, waiting for transfers between devices, swap(): swaps.append(lax.ppermute(after(block, *waits), 'grp', [(0, 1), (1, 0)]))  9.33 us
    ppermute x13, starting transfers between devices, hop(): hops.append(lax.ppermute(after(block, *waits), 'ex', ring))  6.73 us
    slice x1, local copies, waits for them, and re-layouts, on_device(): trains = [train[:, here] for here in columns]  4.08 us
    ppermute x2, waiting for transfers between devices, sum_over_feat(): held = pairs[:, 0] + lax.ppermute(pairs[:, 1], 'feat', partner)  3.82 us
    select_n x4, other arithmetic, share(): return jnp.where(first_grp, rows[:half, columns], rows[half:, columns])  3.21 us
  transfers between devices with their start and end apart: 28, of which 23 were waited for; matrix products, arithmetic and copies ran while one was open for 7% of the time, Pallas kernels for 12%

profile of v29, /device:TPU:0, one launch (start us, length us, event | category | flops | bytes accessed | tf_op | source)
XLA Modules:
  0.0 90.6 jit_solution(16173409711331584299)
XLA Ops:
  1.1 3.1 %collective-permute-start.3 = (bf16[32,4096]{1,0:T(8,128)(2,1)S(1)}, bf16[32,4096]{1,0:T(8,128)(2,1)S(1)}, u32[]{:S(2)}, u32[]{:S(2)}) collective-permute-start(bf16[32,4096]{1,0:T(8,128)(2,1)S(1)} %slice_select_fusion.3), channel_id=1, source_target_pairs={{0,4},{4,8},{8,12},{12,0},{1,5},{5,9},{9,13},{13,1},{2,6},{6,10},{... | collective-permute-start | bytes 786440 | tf_op jit(solution)/shard_map/ppermute | solution.py:113
  5.2 1.6 %collective-permute-start = (bf16[32,4096]{1,0:T(8,128)(2,1)S(1)}, bf16[32,4096]{1,0:T(8,128)(2,1)S(1)}, u32[]{:S(2)}, u32[]{:S(2)}) collective-permute-start(bf16[32,4096]{1,0:T(8,128)(2,1)S(1)} %slice_select_fusion.2), channel_id=1, source_target_pairs={{0,4},{4,8},{8,12},{12,0},{1,5},{5,9},{9,13},{13,1},{2,6},{6,10},{... | collective-permute-start | bytes 786440 | tf_op jit(solution)/shard_map/ppermute | solution.py:113
  7.9 4.1 %fusion.4 = (bf16[256,4096]{1,0:T(8,128)(2,1)S(1)}, bf16[256,4096]{1,0:T(8,128)(2,1)S(1)}, bf16[256,4096]{1,0:T(8,128)(2,1)S(1)}, bf16[256,4096]{1,0:T(8,128)(2,1)S(1)}) fusion(bf16[256,16384]{1,0:T(8,128)(2,1)} %param.3), kind=kLoop, calls=%fused_computation.13 | loop fusion | bytes 16777216 | tf_op jit(solution)/shard_map/slice | solution.py:144
  12.1 1.2 %collective-permute-done.3.refs_0_ = bf16[32,4096]{1,0:T(8,128)(2,1)S(1)} collective-permute-done((bf16[32,4096]{1,0:T(8,128)(2,1)S(1)}, bf16[32,4096]{1,0:T(8,128)(2,1)S(1)}, u32[]{:S(2)}, u32[]{:S(2)}) %collective-permute-start.3) | collective-permute-done | bytes 262176 | tf_op jit(solution)/shard_map/ppermute | solution.py:113
  13.7 1.5 %collective-permute-start.4 = (bf16[32,4096]{1,0:T(8,128)(2,1)S(1)}, bf16[32,4096]{1,0:T(8,128)(2,1)S(1)}, u32[]{:S(2)}, u32[]{:S(2)}) collective-permute-start(bf16[32,4096]{1,0:T(8,128)(2,1)S(1)} %collective-permute-done.3.refs_0_), channel_id=1, source_target_pairs={{0,16},{16,0},{1,17},{17,1},{2,18},{18,2},{3,19},{19,3},{4,20},{20... | collective-permute-start | bytes 786440 | tf_op jit(solution)/shard_map/ppermute | solution.py:122
  15.2 2.7 %shard_map.37.refs_6_ = f32[64,256]{1,0:T(8,128)S(1)} custom-call(bf16[64,16384]{1,0:T(8,128)(2,1)S(1)} %copy-done, f32[1,16384]{1,0:T(1,128)S(1)} %bitcast.28, bf16[256,4096]{1,0:T(8,128)(2,1)S(1)} %get-tuple-element.57.refs_0_.refs_3_, bf16[256,4096]{1,0:T(8,128)(2,1)S(1)} %get-tuple-element.56.refs_1_.refs_3_, ...), custom_call_target="tpu_custom_call" | custom-call | flops 536870912 | bytes 10485760 | tf_op jit(solution)/shard_map/pallas_call | solution.py:79
  18.9 1.8 %collective-permute-start.2 = (bf16[32,4096]{1,0:T(8,128)(2,1)S(1)}, bf16[32,4096]{1,0:T(8,128)(2,1)S(1)}, u32[]{:S(2)}, u32[]{:S(2)}) collective-permute-start(bf16[32,4096]{1,0:T(8,128)(2,1)S(1)} %collective-permute-done.refs_0_), channel_id=1, source_target_pairs={{0,16},{16,0},{1,17},{17,1},{2,18},{18,2},{3,19},{19,3},{4,20},{20... | collective-permute-start | bytes 786440 | tf_op jit(solution)/shard_map/ppermute | solution.py:122
  20.7 3.8 %collective-permute-done.7.refs_0_ = bf16[32,4096]{1,0:T(8,128)(2,1)S(1)} collective-permute-done((bf16[32,4096]{1,0:T(8,128)(2,1)S(1)}, bf16[32,4096]{1,0:T(8,128)(2,1)S(1)}, u32[]{:S(2)}, u32[]{:S(2)}) %collective-permute-start.7) | collective-permute-done | bytes 262176 | tf_op jit(solution)/shard_map/ppermute | solution.py:113
  24.5 1.8 %collective-permute-start.8 = (bf16[32,4096]{1,0:T(8,128)(2,1)S(1)}, bf16[32,4096]{1,0:T(8,128)(2,1)S(1)}, u32[]{:S(2)}, u32[]{:S(2)}) collective-permute-start(bf16[32,4096]{1,0:T(8,128)(2,1)S(1)} %collective-permute-done.7.refs_0_), channel_id=1, source_target_pairs={{0,16},{16,0},{1,17},{17,1},{2,18},{18,2},{3,19},{19,3},{4,20},{20... | collective-permute-start | bytes 786440 | tf_op jit(solution)/shard_map/ppermute | solution.py:122
  27.4 2.0 %collective-permute-done.1.refs_0_ = bf16[32,4096]{1,0:T(8,128)(2,1)S(1)} collective-permute-done((bf16[32,4096]{1,0:T(8,128)(2,1)S(1)}, bf16[32,4096]{1,0:T(8,128)(2,1)S(1)}, u32[]{:S(2)}, u32[]{:S(2)}) %collective-permute-start.1) | collective-permute-done | bytes 262176 | tf_op jit(solution)/shard_map/ppermute | solution.py:113
  29.4 2.3 %collective-permute-start.6 = (bf16[32,4096]{1,0:T(8,128)(2,1)S(1)}, bf16[32,4096]{1,0:T(8,128)(2,1)S(1)}, u32[]{:S(2)}, u32[]{:S(2)}) collective-permute-start(bf16[32,4096]{1,0:T(8,128)(2,1)S(1)} %collective-permute-done.1.refs_0_), channel_id=1, source_target_pairs={{0,16},{16,0},{1,17},{17,1},{2,18},{18,2},{3,19},{19,3},{4,20},{20... | collective-permute-start | bytes 786440 | tf_op jit(solution)/shard_map/ppermute | solution.py:122
  34.3 1.5 %collective-permute-done.11.refs_0_ = bf16[32,4096]{1,0:T(8,128)(2,1)S(1)} collective-permute-done((bf16[32,4096]{1,0:T(8,128)(2,1)S(1)}, bf16[32,4096]{1,0:T(8,128)(2,1)S(1)}, u32[]{:S(2)}, u32[]{:S(2)}) %collective-permute-start.11) | collective-permute-done | bytes 262176 | tf_op jit(solution)/shard_map/ppermute | solution.py:113
  35.8 2.1 %collective-permute-start.12 = (bf16[32,4096]{1,0:T(8,128)(2,1)S(1)}, bf16[32,4096]{1,0:T(8,128)(2,1)S(1)}, u32[]{:S(2)}, u32[]{:S(2)}) collective-permute-start(bf16[32,4096]{1,0:T(8,128)(2,1)S(1)} %collective-permute-done.11.refs_0_), channel_id=1, source_target_pairs={{0,16},{16,0},{1,17},{17,1},{2,18},{18,2},{3,19},{19,3},{4,20},{20... | collective-permute-start | bytes 786440 | tf_op jit(solution)/shard_map/ppermute | solution.py:122
  37.8 1.3 %collective-permute-done.6.refs_1_ = bf16[32,4096]{1,0:T(8,128)(2,1)S(1)} collective-permute-done((bf16[32,4096]{1,0:T(8,128)(2,1)S(1)}, bf16[32,4096]{1,0:T(8,128)(2,1)S(1)}, u32[]{:S(2)}, u32[]{:S(2)}) %collective-permute-start.6) | collective-permute-done | bytes 262176 | tf_op jit(solution)/shard_map/ppermute | solution.py:122
  39.9 3.2 %collective-permute-done.5.refs_0_ = bf16[32,4096]{1,0:T(8,128)(2,1)S(1)} collective-permute-done((bf16[32,4096]{1,0:T(8,128)(2,1)S(1)}, bf16[32,4096]{1,0:T(8,128)(2,1)S(1)}, u32[]{:S(2)}, u32[]{:S(2)}) %collective-permute-start.5) | collective-permute-done | bytes 262176 | tf_op jit(solution)/shard_map/ppermute | solution.py:113
  43.5 1.5 %collective-permute-done.12.refs_1_ = bf16[32,4096]{1,0:T(8,128)(2,1)S(1)} collective-permute-done((bf16[32,4096]{1,0:T(8,128)(2,1)S(1)}, bf16[32,4096]{1,0:T(8,128)(2,1)S(1)}, u32[]{:S(2)}, u32[]{:S(2)}) %collective-permute-start.12) | collective-permute-done | bytes 262176 | tf_op jit(solution)/shard_map/ppermute | solution.py:122
  45.1 3.1 %collective-permute-done.15.refs_0_ = bf16[32,4096]{1,0:T(8,128)(2,1)S(1)} collective-permute-done((bf16[32,4096]{1,0:T(8,128)(2,1)S(1)}, bf16[32,4096]{1,0:T(8,128)(2,1)S(1)}, u32[]{:S(2)}, u32[]{:S(2)}) %collective-permute-start.15) | collective-permute-done | bytes 262176 | tf_op jit(solution)/shard_map/ppermute | solution.py:113
  50.0 1.8 %collective-permute-done.10.refs_1_ = bf16[32,4096]{1,0:T(8,128)(2,1)S(1)} collective-permute-done((bf16[32,4096]{1,0:T(8,128)(2,1)S(1)}, bf16[32,4096]{1,0:T(8,128)(2,1)S(1)}, u32[]{:S(2)}, u32[]{:S(2)}) %collective-permute-start.10) | collective-permute-done | bytes 262176 | tf_op jit(solution)/shard_map/ppermute | solution.py:122
  51.8 1.1 %collective-permute-done.9.refs_0_ = bf16[32,4096]{1,0:T(8,128)(2,1)S(1)} collective-permute-done((bf16[32,4096]{1,0:T(8,128)(2,1)S(1)}, bf16[32,4096]{1,0:T(8,128)(2,1)S(1)}, u32[]{:S(2)}, u32[]{:S(2)}) %collective-permute-start.9) | collective-permute-done | bytes 262176 | tf_op jit(solution)/shard_map/ppermute | solution.py:113
  53.8 2.1 %collective-permute-start.14 = (bf16[32,4096]{1,0:T(8,128)(2,1)S(1)}, bf16[32,4096]{1,0:T(8,128)(2,1)S(1)}, u32[]{:S(2)}, u32[]{:S(2)}) collective-permute-start(bf16[32,4096]{1,0:T(8,128)(2,1)S(1)} %collective-permute-done.9.refs_0_), channel_id=1, source_target_pairs={{0,16},{16,0},{1,17},{17,1},{2,18},{18,2},{3,19},{19,3},{4,20},{20... | collective-permute-start | bytes 786440 | tf_op jit(solution)/shard_map/ppermute | solution.py:122
  57.6 3.4 %collective-permute-done.18.refs_0_ = bf16[32,4096]{1,0:T(8,128)(2,1)S(1)} collective-permute-done((bf16[32,4096]{1,0:T(8,128)(2,1)S(1)}, bf16[32,4096]{1,0:T(8,128)(2,1)S(1)}, u32[]{:S(2)}, u32[]{:S(2)}) %collective-permute-start.18) | collective-permute-done | bytes 262176 | tf_op jit(solution)/shard_map/ppermute | solution.py:113
  60.9 1.1 %collective-permute-start.19 = (bf16[32,4096]{1,0:T(8,128)(2,1)S(1)}, bf16[32,4096]{1,0:T(8,128)(2,1)S(1)}, u32[]{:S(2)}, u32[]{:S(2)}) collective-permute-start(bf16[32,4096]{1,0:T(8,128)(2,1)S(1)} %collective-permute-done.18.refs_0_), channel_id=1, source_target_pairs={{0,16},{16,0},{1,17},{17,1},{2,18},{18,2},{3,19},{19,3},{4,20},{20... | collective-permute-start | bytes 786440 | tf_op jit(solution)/shard_map/ppermute | solution.py:122
  62.0 4.2 %collective-permute-done.13.refs_0_ = bf16[32,4096]{1,0:T(8,128)(2,1)S(1)} collective-permute-done((bf16[32,4096]{1,0:T(8,128)(2,1)S(1)}, bf16[32,4096]{1,0:T(8,128)(2,1)S(1)}, u32[]{:S(2)}, u32[]{:S(2)}) %collective-permute-start.13) | collective-permute-done | bytes 262176 | tf_op jit(solution)/shard_map/ppermute | solution.py:113
  66.3 1.1 %collective-permute-start.23 = (bf16[32,4096]{1,0:T(8,128)(2,1)S(1)}, bf16[32,4096]{1,0:T(8,128)(2,1)S(1)}, u32[]{:S(2)}, u32[]{:S(2)}) collective-permute-start(bf16[32,4096]{1,0:T(8,128)(2,1)S(1)} %collective-permute-done.13.refs_0_), channel_id=1, source_target_pairs={{0,16},{16,0},{1,17},{17,1},{2,18},{18,2},{3,19},{19,3},{4,20},{20... | collective-permute-start | bytes 786440 | tf_op jit(solution)/shard_map/ppermute | solution.py:122
  69.1 1.1 %collective-permute-start.25 = (bf16[32,4096]{1,0:T(8,128)(2,1)S(1)}, bf16[32,4096]{1,0:T(8,128)(2,1)S(1)}, u32[]{:S(2)}, u32[]{:S(2)}) collective-permute-start(bf16[32,4096]{1,0:T(8,128)(2,1)S(1)} %collective-permute-done.21.refs_0_), channel_id=1, source_target_pairs={{0,16},{16,0},{1,17},{17,1},{2,18},{18,2},{3,19},{19,3},{4,20},{20... | collective-permute-start | bytes 786440 | tf_op jit(solution)/shard_map/ppermute | solution.py:122
  70.3 1.3 %collective-permute-start.22 = (bf16[32,2048]{1,0:T(8,128)(2,1)S(1)}, bf16[32,2048]{1,0:T(8,128)(2,1)S(1)}, u32[]{:S(2)}, u32[]{:S(2)}) collective-permute-start(bf16[32,2048]{1,0:T(8,128)(2,1)S(1)} %get-tuple-element.51), channel_id=1, source_target_pairs={{0,4},{4,8},{8,12},{12,0},{1,5},{5,9},{9,13},{13,1},{2,6},{6,10},{... | collective-permute-start | bytes 393224 | tf_op jit(solution)/shard_map/ppermute | solution.py:113
  72.3 4.7 %collective-permute-done.17.refs_0_ = bf16[32,2048]{1,0:T(8,128)(2,1)S(1)} collective-permute-done((bf16[32,2048]{1,0:T(8,128)(2,1)S(1)}, bf16[32,2048]{1,0:T(8,128)(2,1)S(1)}, u32[]{:S(2)}, u32[]{:S(2)}) %collective-permute-start.17) | collective-permute-done | bytes 131104 | tf_op jit(solution)/shard_map/ppermute | solution.py:113
  80.9 1.1 %collective-permute-done.20.refs_1_ = bf16[32,2048]{1,0:T(8,128)(2,1)S(1)} collective-permute-done((bf16[32,2048]{1,0:T(8,128)(2,1)S(1)}, bf16[32,2048]{1,0:T(8,128)(2,1)S(1)}, u32[]{:S(2)}, u32[]{:S(2)}) %collective-permute-start.20) | collective-permute-done | bytes 131104 | tf_op jit(solution)/shard_map/ppermute | solution.py:122
  82.0 1.4 %collective-permute-done.24.refs_3_ = bf16[32,2048]{1,0:T(8,128)(2,1)S(1)} collective-permute-done((bf16[32,2048]{1,0:T(8,128)(2,1)S(1)}, bf16[32,2048]{1,0:T(8,128)(2,1)S(1)}, u32[]{:S(2)}, u32[]{:S(2)}) %collective-permute-start.24) | collective-permute-done | bytes 131104 | tf_op jit(solution)/shard_map/ppermute | solution.py:122
  84.3 1.3 %collective-permute-done.26 = f32[2,64,256]{2,1,0:T(8,128)S(1)} collective-permute-done((f32[2,64,256]{2,1,0:T(8,128)S(1)}, f32[2,64,256]{2,1,0:T(8,128)S(1)}, u32[]{:S(2)}, u32[]{:S(2)}) %collective-permute-start.26) | collective-permute-done | bytes 131104 | tf_op jit(solution)/shard_map/ppermute | solution.py:131
  85.6 1.8 %collective-permute-start.27 = (f32[1,64,256]{2,1,0:T(8,128)S(1)}, f32[1,64,256]{2,1,0:T(8,128)S(1)}, u32[]{:S(2)}, u32[]{:S(2)}) collective-permute-start(f32[1,64,256]{2,1,0:T(8,128)S(1)} %slice_bitcast_fusion.2), channel_id=1, source_target_pairs={{0,2},{1,3},{2,0},{3,1},{4,6},{5,7},{6,4},{7,5},{8,10},{9,11},{10,... | collective-permute-start | bytes 196616 | tf_op jit(solution)/shard_map/ppermute | solution.py:131
  87.5 2.5 %collective-permute-done.27 = f32[1,64,256]{2,1,0:T(8,128)S(1)} collective-permute-done((f32[1,64,256]{2,1,0:T(8,128)S(1)}, f32[1,64,256]{2,1,0:T(8,128)S(1)}, u32[]{:S(2)}, u32[]{:S(2)}) %collective-permute-start.27) | collective-permute-done | bytes 65568 | tf_op jit(solution)/shard_map/ppermute | solution.py:131
  (52 shorter events, 21.9 us)
Async XLA Ops:
  1.1 12.2 %collective-permute-start.3 = (bf16[32,4096]{1,0:T(8,128)(2,1)S(1)}, bf16[32,4096]{1,0:T(8,128)(2,1)S(1)}, u32[]{:S(2)}, u32[]{:S(2)}) collective-permute-start(bf16[32,4096]{1,0:T(8,128)(2,1)S(1)} %slice_select_fusion.3), channel_id=1, source_target_pairs={{0,4},{4,8},{8,12},{12,0},{1,5},{5,9},{9,13},{13,1},{2,6},{6,10},{... | collective-permute-start | bytes 786440 | tf_op jit(solution)/shard_map/ppermute | solution.py:113
  5.2 13.7 %collective-permute-start = (bf16[32,4096]{1,0:T(8,128)(2,1)S(1)}, bf16[32,4096]{1,0:T(8,128)(2,1)S(1)}, u32[]{:S(2)}, u32[]{:S(2)}) collective-permute-start(bf16[32,4096]{1,0:T(8,128)(2,1)S(1)} %slice_select_fusion.2), channel_id=1, source_target_pairs={{0,4},{4,8},{8,12},{12,0},{1,5},{5,9},{9,13},{13,1},{2,6},{6,10},{... | collective-permute-start | bytes 786440 | tf_op jit(solution)/shard_map/ppermute | solution.py:113
  7.9 4.1 %copy-start = (bf16[64,16384]{1,0:T(8,128)(2,1)S(1)}, bf16[64,16384]{1,0:T(8,128)(2,1)}, u32[]{:S(2)}) copy-start(bf16[64,16384]{1,0:T(8,128)(2,1)} %test.1) | copy-start | bytes 6291460
  7.9 7.3 %copy-start.1 = (f32[16384]{0:T(1024)S(1)}, f32[16384]{0:T(1024)}, u32[]{:S(2)}) copy-start(f32[16384]{0:T(1024)} %param.5) | copy-start | bytes 196612
  13.3 11.2 %collective-permute-start.7 = (bf16[32,4096]{1,0:T(8,128)(2,1)S(1)}, bf16[32,4096]{1,0:T(8,128)(2,1)S(1)}, u32[]{:S(2)}, u32[]{:S(2)}) collective-permute-start(bf16[32,4096]{1,0:T(8,128)(2,1)S(1)} %slice_select_fusion.1), channel_id=1, source_target_pairs={{0,4},{4,8},{8,12},{12,0},{1,5},{5,9},{9,13},{13,1},{2,6},{6,10},{... | collective-permute-start | bytes 786440 | tf_op jit(solution)/shard_map/ppermute | solution.py:113
  13.7 10.8 %collective-permute-start.4 = (bf16[32,4096]{1,0:T(8,128)(2,1)S(1)}, bf16[32,4096]{1,0:T(8,128)(2,1)S(1)}, u32[]{:S(2)}, u32[]{:S(2)}) collective-permute-start(bf16[32,4096]{1,0:T(8,128)(2,1)S(1)} %collective-permute-done.3.refs_0_), channel_id=1, source_target_pairs={{0,16},{16,0},{1,17},{17,1},{2,18},{18,2},{3,19},{19,3},{4,20},{20... | collective-permute-start | bytes 786440 | tf_op jit(solution)/shard_map/ppermute | solution.py:122
  18.9 8.5 %collective-permute-start.2 = (bf16[32,4096]{1,0:T(8,128)(2,1)S(1)}, bf16[32,4096]{1,0:T(8,128)(2,1)S(1)}, u32[]{:S(2)}, u32[]{:S(2)}) collective-permute-start(bf16[32,4096]{1,0:T(8,128)(2,1)S(1)} %collective-permute-done.refs_0_), channel_id=1, source_target_pairs={{0,16},{16,0},{1,17},{17,1},{2,18},{18,2},{3,19},{19,3},{4,20},{20... | collective-permute-start | bytes 786440 | tf_op jit(solution)/shard_map/ppermute | solution.py:122
  20.7 8.7 %collective-permute-start.1 = (bf16[32,4096]{1,0:T(8,128)(2,1)S(1)}, bf16[32,4096]{1,0:T(8,128)(2,1)S(1)}, u32[]{:S(2)}, u32[]{:S(2)}) collective-permute-start(bf16[32,4096]{1,0:T(8,128)(2,1)S(1)} %slice_select_fusion), channel_id=1, source_target_pairs={{0,4},{4,8},{8,12},{12,0},{1,5},{5,9},{9,13},{13,1},{2,6},{6,10},{... | collective-permute-start | bytes 786440 | tf_op jit(solution)/shard_map/ppermute | solution.py:113
  24.5 9.0 %collective-permute-start.8 = (bf16[32,4096]{1,0:T(8,128)(2,1)S(1)}, bf16[32,4096]{1,0:T(8,128)(2,1)S(1)}, u32[]{:S(2)}, u32[]{:S(2)}) collective-permute-start(bf16[32,4096]{1,0:T(8,128)(2,1)S(1)} %collective-permute-done.7.refs_0_), channel_id=1, source_target_pairs={{0,16},{16,0},{1,17},{17,1},{2,18},{18,2},{3,19},{19,3},{4,20},{20... | collective-permute-start | bytes 786440 | tf_op jit(solution)/shard_map/ppermute | solution.py:122
  27.1 8.7 %collective-permute-start.11 = (bf16[32,4096]{1,0:T(8,128)(2,1)S(1)}, bf16[32,4096]{1,0:T(8,128)(2,1)S(1)}, u32[]{:S(2)}, u32[]{:S(2)}) collective-permute-start(bf16[32,4096]{1,0:T(8,128)(2,1)S(1)} %collective-permute-done.3.refs_0_), channel_id=1, source_target_pairs={{0,4},{4,8},{8,12},{12,0},{1,5},{5,9},{9,13},{13,1},{2,6},{6,10},{... | collective-permute-start | bytes 786440 | tf_op jit(solution)/shard_map/ppermute | solution.py:113
  29.4 9.8 %collective-permute-start.6 = (bf16[32,4096]{1,0:T(8,128)(2,1)S(1)}, bf16[32,4096]{1,0:T(8,128)(2,1)S(1)}, u32[]{:S(2)}, u32[]{:S(2)}) collective-permute-start(bf16[32,4096]{1,0:T(8,128)(2,1)S(1)} %collective-permute-done.1.refs_0_), channel_id=1, source_target_pairs={{0,16},{16,0},{1,17},{17,1},{2,18},{18,2},{3,19},{19,3},{4,20},{20... | collective-permute-start | bytes 786440 | tf_op jit(solution)/shard_map/ppermute | solution.py:122
  32.4 10.7 %collective-permute-start.5 = (bf16[32,4096]{1,0:T(8,128)(2,1)S(1)}, bf16[32,4096]{1,0:T(8,128)(2,1)S(1)}, u32[]{:S(2)}, u32[]{:S(2)}) collective-permute-start(bf16[32,4096]{1,0:T(8,128)(2,1)S(1)} %collective-permute-done.refs_0_), channel_id=1, source_target_pairs={{0,4},{4,8},{8,12},{12,0},{1,5},{5,9},{9,13},{13,1},{2,6},{6,10},{... | collective-permute-start | bytes 786440 | tf_op jit(solution)/shard_map/ppermute | solution.py:113
  35.8 9.3 %collective-permute-start.12 = (bf16[32,4096]{1,0:T(8,128)(2,1)S(1)}, bf16[32,4096]{1,0:T(8,128)(2,1)S(1)}, u32[]{:S(2)}, u32[]{:S(2)}) collective-permute-start(bf16[32,4096]{1,0:T(8,128)(2,1)S(1)} %collective-permute-done.11.refs_0_), channel_id=1, source_target_pairs={{0,16},{16,0},{1,17},{17,1},{2,18},{18,2},{3,19},{19,3},{4,20},{20... | collective-permute-start | bytes 786440 | tf_op jit(solution)/shard_map/ppermute | solution.py:122
  37.8 10.3 %collective-permute-start.15 = (bf16[32,4096]{1,0:T(8,128)(2,1)S(1)}, bf16[32,4096]{1,0:T(8,128)(2,1)S(1)}, u32[]{:S(2)}, u32[]{:S(2)}) collective-permute-start(bf16[32,4096]{1,0:T(8,128)(2,1)S(1)} %collective-permute-done.7.refs_0_), channel_id=1, source_target_pairs={{0,4},{4,8},{8,12},{12,0},{1,5},{5,9},{9,13},{13,1},{2,6},{6,10},{... | collective-permute-start | bytes 786440 | tf_op jit(solution)/shard_map/ppermute | solution.py:113
  43.1 8.7 %collective-permute-start.10 = (bf16[32,4096]{1,0:T(8,128)(2,1)S(1)}, bf16[32,4096]{1,0:T(8,128)(2,1)S(1)}, u32[]{:S(2)}, u32[]{:S(2)}) collective-permute-start(bf16[32,4096]{1,0:T(8,128)(2,1)S(1)} %collective-permute-done.5.refs_0_), channel_id=1, source_target_pairs={{0,16},{16,0},{1,17},{17,1},{2,18},{18,2},{3,19},{19,3},{4,20},{20... | collective-permute-start | bytes 786440 | tf_op jit(solution)/shard_map/ppermute | solution.py:122
  43.5 9.4 %collective-permute-start.9 = (bf16[32,4096]{1,0:T(8,128)(2,1)S(1)}, bf16[32,4096]{1,0:T(8,128)(2,1)S(1)}, u32[]{:S(2)}, u32[]{:S(2)}) collective-permute-start(bf16[32,4096]{1,0:T(8,128)(2,1)S(1)} %collective-permute-done.1.refs_0_), channel_id=1, source_target_pairs={{0,4},{4,8},{8,12},{12,0},{1,5},{5,9},{9,13},{13,1},{2,6},{6,10},{... | collective-permute-start | bytes 786440 | tf_op jit(solution)/shard_map/ppermute | solution.py:113
  48.1 8.7 %collective-permute-start.16 = (bf16[32,4096]{1,0:T(8,128)(2,1)S(1)}, bf16[32,4096]{1,0:T(8,128)(2,1)S(1)}, u32[]{:S(2)}, u32[]{:S(2)}) collective-permute-start(bf16[32,4096]{1,0:T(8,128)(2,1)S(1)} %collective-permute-done.15.refs_0_), channel_id=1, source_target_pairs={{0,16},{16,0},{1,17},{17,1},{2,18},{18,2},{3,19},{19,3},{4,20},{20... | collective-permute-start | bytes 786440 | tf_op jit(solution)/shard_map/ppermute | solution.py:122
  49.9 11.0 %collective-permute-start.18 = (bf16[32,4096]{1,0:T(8,128)(2,1)S(1)}, bf16[32,4096]{1,0:T(8,128)(2,1)S(1)}, u32[]{:S(2)}, u32[]{:S(2)}) collective-permute-start(bf16[32,4096]{1,0:T(8,128)(2,1)S(1)} %collective-permute-done.11.refs_0_), channel_id=1, source_target_pairs={{0,4},{4,8},{8,12},{12,0},{1,5},{5,9},{9,13},{13,1},{2,6},{6,10},{... | collective-permute-start | bytes 786440 | tf_op jit(solution)/shard_map/ppermute | solution.py:113
  53.7 12.6 %collective-permute-start.13 = (bf16[32,4096]{1,0:T(8,128)(2,1)S(1)}, bf16[32,4096]{1,0:T(8,128)(2,1)S(1)}, u32[]{:S(2)}, u32[]{:S(2)}) collective-permute-start(bf16[32,4096]{1,0:T(8,128)(2,1)S(1)} %collective-permute-done.5.refs_0_), channel_id=1, source_target_pairs={{0,4},{4,8},{8,12},{12,0},{1,5},{5,9},{9,13},{13,1},{2,6},{6,10},{... | collective-permute-start | bytes 786440 | tf_op jit(solution)/shard_map/ppermute | solution.py:113
  53.8 13.6 %collective-permute-start.14 = (bf16[32,4096]{1,0:T(8,128)(2,1)S(1)}, bf16[32,4096]{1,0:T(8,128)(2,1)S(1)}, u32[]{:S(2)}, u32[]{:S(2)}) collective-permute-start(bf16[32,4096]{1,0:T(8,128)(2,1)S(1)} %collective-permute-done.9.refs_0_), channel_id=1, source_target_pairs={{0,16},{16,0},{1,17},{17,1},{2,18},{18,2},{3,19},{19,3},{4,20},{20... | collective-permute-start | bytes 786440 | tf_op jit(solution)/shard_map/ppermute | solution.py:122
  60.9 8.2 %collective-permute-start.21 = (bf16[32,4096]{1,0:T(8,128)(2,1)S(1)}, bf16[32,4096]{1,0:T(8,128)(2,1)S(1)}, u32[]{:S(2)}, u32[]{:S(2)}) collective-permute-start(bf16[32,4096]{1,0:T(8,128)(2,1)S(1)} %collective-permute-done.15.refs_0_), channel_id=1, source_target_pairs={{0,4},{4,8},{8,12},{12,0},{1,5},{5,9},{9,13},{13,1},{2,6},{6,10},{... | collective-permute-start | bytes 786440 | tf_op jit(solution)/shard_map/ppermute | solution.py:113
  60.9 9.3 %collective-permute-start.19 = (bf16[32,4096]{1,0:T(8,128)(2,1)S(1)}, bf16[32,4096]{1,0:T(8,128)(2,1)S(1)}, u32[]{:S(2)}, u32[]{:S(2)}) collective-permute-start(bf16[32,4096]{1,0:T(8,128)(2,1)S(1)} %collective-permute-done.18.refs_0_), channel_id=1, source_target_pairs={{0,16},{16,0},{1,17},{17,1},{2,18},{18,2},{3,19},{19,3},{4,20},{20... | collective-permute-start | bytes 786440 | tf_op jit(solution)/shard_map/ppermute | solution.py:122
  66.3 11.7 %collective-permute-start.23 = (bf16[32,4096]{1,0:T(8,128)(2,1)S(1)}, bf16[32,4096]{1,0:T(8,128)(2,1)S(1)}, u32[]{:S(2)}, u32[]{:S(2)}) collective-permute-start(bf16[32,4096]{1,0:T(8,128)(2,1)S(1)} %collective-permute-done.13.refs_0_), channel_id=1, source_target_pairs={{0,16},{16,0},{1,17},{17,1},{2,18},{18,2},{3,19},{19,3},{4,20},{20... | collective-permute-start | bytes 786440 | tf_op jit(solution)/shard_map/ppermute | solution.py:122
  69.1 11.0 %collective-permute-start.25 = (bf16[32,4096]{1,0:T(8,128)(2,1)S(1)}, bf16[32,4096]{1,0:T(8,128)(2,1)S(1)}, u32[]{:S(2)}, u32[]{:S(2)}) collective-permute-start(bf16[32,4096]{1,0:T(8,128)(2,1)S(1)} %collective-permute-done.21.refs_0_), channel_id=1, source_target_pairs={{0,16},{16,0},{1,17},{17,1},{2,18},{18,2},{3,19},{19,3},{4,20},{20... | collective-permute-start | bytes 786440 | tf_op jit(solution)/shard_map/ppermute | solution.py:122
  70.2 6.8 %collective-permute-start.17 = (bf16[32,2048]{1,0:T(8,128)(2,1)S(1)}, bf16[32,2048]{1,0:T(8,128)(2,1)S(1)}, u32[]{:S(2)}, u32[]{:S(2)}) collective-permute-start(bf16[32,2048]{1,0:T(8,128)(2,1)S(1)} %get-tuple-element.46), channel_id=1, source_target_pairs={{0,4},{4,8},{8,12},{12,0},{1,5},{5,9},{9,13},{13,1},{2,6},{6,10},{... | collective-permute-start | bytes 393224 | tf_op jit(solution)/shard_map/ppermute | solution.py:113
  70.3 8.1 %collective-permute-start.22 = (bf16[32,2048]{1,0:T(8,128)(2,1)S(1)}, bf16[32,2048]{1,0:T(8,128)(2,1)S(1)}, u32[]{:S(2)}, u32[]{:S(2)}) collective-permute-start(bf16[32,2048]{1,0:T(8,128)(2,1)S(1)} %get-tuple-element.51), channel_id=1, source_target_pairs={{0,4},{4,8},{8,12},{12,0},{1,5},{5,9},{9,13},{13,1},{2,6},{6,10},{... | collective-permute-start | bytes 393224 | tf_op jit(solution)/shard_map/ppermute | solution.py:113
  77.0 5.0 %collective-permute-start.20 = (bf16[32,2048]{1,0:T(8,128)(2,1)S(1)}, bf16[32,2048]{1,0:T(8,128)(2,1)S(1)}, u32[]{:S(2)}, u32[]{:S(2)}) collective-permute-start(bf16[32,2048]{1,0:T(8,128)(2,1)S(1)} %collective-permute-done.17.refs_0_), channel_id=1, source_target_pairs={{0,16},{16,0},{1,17},{17,1},{2,18},{18,2},{3,19},{19,3},{4,20},{20... | collective-permute-start | bytes 393224 | tf_op jit(solution)/shard_map/ppermute | solution.py:122
  78.4 5.0 %collective-permute-start.24 = (bf16[32,2048]{1,0:T(8,128)(2,1)S(1)}, bf16[32,2048]{1,0:T(8,128)(2,1)S(1)}, u32[]{:S(2)}, u32[]{:S(2)}) collective-permute-start(bf16[32,2048]{1,0:T(8,128)(2,1)S(1)} %collective-permute-done.22.refs_2_), channel_id=1, source_target_pairs={{0,16},{16,0},{1,17},{17,1},{2,18},{18,2},{3,19},{19,3},{4,20},{20... | collective-permute-start | bytes 393224 | tf_op jit(solution)/shard_map/ppermute | solution.py:122
  84.2 1.4 %collective-permute-start.26 = (f32[2,64,256]{2,1,0:T(8,128)S(1)}, f32[2,64,256]{2,1,0:T(8,128)S(1)}, u32[]{:S(2)}, u32[]{:S(2)}) collective-permute-start(f32[2,64,256]{2,1,0:T(8,128)S(1)} %slice_bitcast_fusion), channel_id=1, source_target_pairs={{0,1},{1,0},{2,3},{3,2},{4,5},{5,4},{6,7},{7,6},{8,9},{9,8},{10,11... | collective-permute-start | bytes 393224 | tf_op jit(solution)/shard_map/ppermute | solution.py:131
  85.6 4.3 %collective-permute-start.27 = (f32[1,64,256]{2,1,0:T(8,128)S(1)}, f32[1,64,256]{2,1,0:T(8,128)S(1)}, u32[]{:S(2)}, u32[]{:S(2)}) collective-permute-start(f32[1,64,256]{2,1,0:T(8,128)S(1)} %slice_bitcast_fusion.2), channel_id=1, source_target_pairs={{0,2},{1,3},{2,0},{3,1},{4,6},{5,7},{6,4},{7,5},{8,10},{9,11},{10,... | collective-permute-start | bytes 196616 | tf_op jit(solution)/shard_map/ppermute | solution.py:131

commit v30 on v29

--- a/solution.py
+++ b/solution.py
@@ -108,9 +108,9 @@
         def after(block, *waits):
             return lax.optimization_barrier((block, waits))[0] if waits else block
 
-        def hop(block):
+        def hop(block, *ahead):
             waits = hops[-2:-1] + swaps[-4:-3] + made[-4:-3] + (first if len(hops) == 3 else [])
-            hops.append(lax.ppermute(after(block, *waits), "ex", ring))
+            hops.append(lax.ppermute(after(block, *waits, *ahead), "ex", ring))
             return hops[-1]
 
         def swap(block):
@@ -151,7 +151,9 @@
         for t in range(1, n_ex):
             for c, (start, here) in enumerate(zip(starts, columns)):
                 if (t, c) == (final, CHUNKS - 1):
-                    pieces = [swap(hop(piece)) for piece in jnp.split(held[c], 2, axis=1)]
+                    near, far = jnp.split(held[c], 2, axis=1)
+                    pieces = [swap(hop(near))]
+                    pieces.append(swap(hop(far, hops[-1])))
                     parts = sum(pieces, [])
                     operands = [*parts, scale, trains[c]]
                     continue

time: 90.8 us -> 93.9 us (1.034)
  waiting for transfers between devices: 43.8 us -> 50.1 us
  starting transfers between devices: 26.8 us -> 23.7 us
    ppermute x13, waiting for transfers between devices: 30.7 us -> 35.4 us  [hop(): hops.append(lax.ppermute(after(block, *waits, *ahead), 'ex', ring))]
    ppermute x13, starting transfers between devices: 18.2 us -> 15 us  [swap(): swaps.append(lax.ppermute(after(block, *waits), 'grp', [(0, 1), (1, 0)]))]
    ppermute x13, waiting for transfers between devices: 9.33 us -> 11 us  [swap(): swaps.append(lax.ppermute(after(block, *waits), 'grp', [(0, 1), (1, 0)]))]
    ppermute x2, starting transfers between devices: 1.91 us -> 3.25 us  [sum_over_feat(): held = pairs[:, 0] + lax.ppermute(pairs[:, 1], 'feat', partner)]
    ppermute x13, starting transfers between devices: 6.73 us -> 5.42 us  [hop(): hops.append(lax.ppermute(after(block, *waits, *ahead), 'ex', ring))]
  transfers between devices with their start and end apart: 28 -> 28, of which waited for: 23 -> 25; matrix products, arithmetic and copies ran while one was open for 7% -> 7% of each run, Pallas kernels for 12% -> 12%
where the time goes in v30:
time: 93.9 us; the launch traced here: 93.7 us
  waiting for transfers between devices  50.1 us (53%)
  starting transfers between devices  23.7 us (25%)
  Pallas kernels  11.8 us (13%)
  local copies, waits for them, and re-layouts  4.13 us (4%)
  other arithmetic  3.88 us (4%)
    ppermute x13, waiting for transfers between devices, hop(): hops.append(lax.ppermute(after(block, *waits, *ahead), 'ex', ring))  35.4 us
    ppermute x13, starting transfers between devices, swap(): swaps.append(lax.ppermute(after(block, *waits), 'grp', [(0, 1), (1, 0)]))  15 us
    pallas_call x13, Pallas kernels, call(): pl.pallas_call(kernel, out_shape=jax.ShapeDtypeStruct((rows, docs), jnp.f...  11.8 us
    ppermute x13, waiting for transfers between devices, swap(): swaps.append(lax.ppermute(after(block, *waits), 'grp', [(0, 1), (1, 0)]))  11 us
    ppermute x13, starting transfers between devices, hop(): hops.append(lax.ppermute(after(block, *waits, *ahead), 'ex', ring))  5.42 us
    slice x1, local copies, waits for them, and re-layouts, on_device(): trains = [train[:, here] for here in columns]  4.08 us
    ppermute x2, waiting for transfers between devices, sum_over_feat(): held = pairs[:, 0] + lax.ppermute(pairs[:, 1], 'feat', partner)  3.74 us
    ppermute x2, starting transfers between devices, sum_over_feat(): held = pairs[:, 0] + lax.ppermute(pairs[:, 1], 'feat', partner)  3.25 us
  transfers between devices with their start and end apart: 28, of which 25 were waited for; matrix products, arithmetic and copies ran while one was open for 7% of the time, Pallas kernels for 12%

profile of v30, /device:TPU:0, one launch (start us, length us, event | category | flops | bytes accessed | tf_op | source)
XLA Modules:
  0.0 93.7 jit_solution(799356784468096719)
XLA Ops:
  0.0 1.1 %slice_select_fusion.3 = bf16[32,4096]{1,0:T(8,128)(2,1)S(1)} fusion(bf16[64,16384]{1,0:T(8,128)(2,1)} %test.1, pred[]{:T(512)S(6)} %eq.3), kind=kLoop, calls=%fused_computation.3 | loop fusion | flops 131072 | bytes 786433 | tf_op jit(solution)/shard_map/jit(_where)/select_n | solution.py:138
  1.1 3.1 %collective-permute-start.3 = (bf16[32,4096]{1,0:T(8,128)(2,1)S(1)}, bf16[32,4096]{1,0:T(8,128)(2,1)S(1)}, u32[]{:S(2)}, u32[]{:S(2)}) collective-permute-start(bf16[32,4096]{1,0:T(8,128)(2,1)S(1)} %slice_select_fusion.3), channel_id=1, source_target_pairs={{0,4},{4,8},{8,12},{12,0},{1,5},{5,9},{9,13},{13,1},{2,6},{6,10},{... | collective-permute-start | bytes 786440 | tf_op jit(solution)/shard_map/ppermute | solution.py:113
  4.1 1.1 %slice_select_fusion.2 = bf16[32,4096]{1,0:T(8,128)(2,1)S(1)} fusion(bf16[64,16384]{1,0:T(8,128)(2,1)} %test.1, pred[]{:T(512)S(6)} %eq.3), kind=kLoop, calls=%fused_computation.2 | loop fusion | flops 131072 | bytes 786433 | tf_op jit(solution)/shard_map/jit(_where)/select_n | solution.py:138
  5.2 1.6 %collective-permute-start = (bf16[32,4096]{1,0:T(8,128)(2,1)S(1)}, bf16[32,4096]{1,0:T(8,128)(2,1)S(1)}, u32[]{:S(2)}, u32[]{:S(2)}) collective-permute-start(bf16[32,4096]{1,0:T(8,128)(2,1)S(1)} %slice_select_fusion.2), channel_id=1, source_target_pairs={{0,4},{4,8},{8,12},{12,0},{1,5},{5,9},{9,13},{13,1},{2,6},{6,10},{... | collective-permute-start | bytes 786440 | tf_op jit(solution)/shard_map/ppermute | solution.py:113
  6.8 1.1 %slice_select_fusion.1 = bf16[32,4096]{1,0:T(8,128)(2,1)S(1)} fusion(bf16[64,16384]{1,0:T(8,128)(2,1)} %test.1, pred[]{:T(512)S(6)} %eq.3), kind=kLoop, calls=%fused_computation.1 | loop fusion | flops 131072 | bytes 786433 | tf_op jit(solution)/shard_map/jit(_where)/select_n | solution.py:138
  7.9 4.1 %fusion.4 = (bf16[256,4096]{1,0:T(8,128)(2,1)S(1)}, bf16[256,4096]{1,0:T(8,128)(2,1)S(1)}, bf16[256,4096]{1,0:T(8,128)(2,1)S(1)}, bf16[256,4096]{1,0:T(8,128)(2,1)S(1)}) fusion(bf16[256,16384]{1,0:T(8,128)(2,1)} %param.3), kind=kLoop, calls=%fused_computation.13 | loop fusion | bytes 16777216 | tf_op jit(solution)/shard_map/slice | solution.py:144
  12.1 1.2 %collective-permute-done.3.refs_0_ = bf16[32,4096]{1,0:T(8,128)(2,1)S(1)} collective-permute-done((bf16[32,4096]{1,0:T(8,128)(2,1)S(1)}, bf16[32,4096]{1,0:T(8,128)(2,1)S(1)}, u32[]{:S(2)}, u32[]{:S(2)}) %collective-permute-start.3) | collective-permute-done | bytes 262176 | tf_op jit(solution)/shard_map/ppermute | solution.py:113
  13.7 1.5 %collective-permute-start.4 = (bf16[32,4096]{1,0:T(8,128)(2,1)S(1)}, bf16[32,4096]{1,0:T(8,128)(2,1)S(1)}, u32[]{:S(2)}, u32[]{:S(2)}) collective-permute-start(bf16[32,4096]{1,0:T(8,128)(2,1)S(1)} %collective-permute-done.3.refs_0_), channel_id=1, source_target_pairs={{0,16},{16,0},{1,17},{17,1},{2,18},{18,2},{3,19},{19,3},{4,20},{20... | collective-permute-start | bytes 786440 | tf_op jit(solution)/shard_map/ppermute | solution.py:122
  15.2 2.7 %shard_map.37.refs_6_ = f32[64,256]{1,0:T(8,128)S(1)} custom-call(bf16[64,16384]{1,0:T(8,128)(2,1)S(1)} %copy-done, f32[1,16384]{1,0:T(1,128)S(1)} %bitcast.28, bf16[256,4096]{1,0:T(8,128)(2,1)S(1)} %get-tuple-element.57.refs_0_.refs_3_, bf16[256,4096]{1,0:T(8,128)(2,1)S(1)} %get-tuple-element.56.refs_1_.refs_3_, ...), custom_call_target="tpu_custom_call" | custom-call | flops 536870912 | bytes 10485760 | tf_op jit(solution)/shard_map/pallas_call | solution.py:79
  18.9 1.8 %collective-permute-start.2 = (bf16[32,4096]{1,0:T(8,128)(2,1)S(1)}, bf16[32,4096]{1,0:T(8,128)(2,1)S(1)}, u32[]{:S(2)}, u32[]{:S(2)}) collective-permute-start(bf16[32,4096]{1,0:T(8,128)(2,1)S(1)} %collective-permute-done.refs_0_), channel_id=1, source_target_pairs={{0,16},{16,0},{1,17},{17,1},{2,18},{18,2},{3,19},{19,3},{4,20},{20... | collective-permute-start | bytes 786440 | tf_op jit(solution)/shard_map/ppermute | solution.py:122
  20.7 3.8 %collective-permute-done.7.refs_0_ = bf16[32,4096]{1,0:T(8,128)(2,1)S(1)} collective-permute-done((bf16[32,4096]{1,0:T(8,128)(2,1)S(1)}, bf16[32,4096]{1,0:T(8,128)(2,1)S(1)}, u32[]{:S(2)}, u32[]{:S(2)}) %collective-permute-start.7) | collective-permute-done | bytes 262176 | tf_op jit(solution)/shard_map/ppermute | solution.py:113
  24.5 1.8 %collective-permute-start.8 = (bf16[32,4096]{1,0:T(8,128)(2,1)S(1)}, bf16[32,4096]{1,0:T(8,128)(2,1)S(1)}, u32[]{:S(2)}, u32[]{:S(2)}) collective-permute-start(bf16[32,4096]{1,0:T(8,128)(2,1)S(1)} %collective-permute-done.7.refs_0_), channel_id=1, source_target_pairs={{0,16},{16,0},{1,17},{17,1},{2,18},{18,2},{3,19},{19,3},{4,20},{20... | collective-permute-start | bytes 786440 | tf_op jit(solution)/shard_map/ppermute | solution.py:122
  27.4 2.0 %collective-permute-done.1.refs_0_ = bf16[32,4096]{1,0:T(8,128)(2,1)S(1)} collective-permute-done((bf16[32,4096]{1,0:T(8,128)(2,1)S(1)}, bf16[32,4096]{1,0:T(8,128)(2,1)S(1)}, u32[]{:S(2)}, u32[]{:S(2)}) %collective-permute-start.1) | collective-permute-done | bytes 262176 | tf_op jit(solution)/shard_map/ppermute | solution.py:113
  29.4 2.3 %collective-permute-start.6 = (bf16[32,4096]{1,0:T(8,128)(2,1)S(1)}, bf16[32,4096]{1,0:T(8,128)(2,1)S(1)}, u32[]{:S(2)}, u32[]{:S(2)}) collective-permute-start(bf16[32,4096]{1,0:T(8,128)(2,1)S(1)} %collective-permute-done.1.refs_0_), channel_id=1, source_target_pairs={{0,16},{16,0},{1,17},{17,1},{2,18},{18,2},{3,19},{19,3},{4,20},{20... | collective-permute-start | bytes 786440 | tf_op jit(solution)/shard_map/ppermute | solution.py:122
  33.5 2.2 %collective-permute-done.11.refs_0_ = bf16[32,4096]{1,0:T(8,128)(2,1)S(1)} collective-permute-done((bf16[32,4096]{1,0:T(8,128)(2,1)S(1)}, bf16[32,4096]{1,0:T(8,128)(2,1)S(1)}, u32[]{:S(2)}, u32[]{:S(2)}) %collective-permute-start.11) | collective-permute-done | bytes 262176 | tf_op jit(solution)/shard_map/ppermute | solution.py:113
  35.8 2.1 %collective-permute-start.12 = (bf16[32,4096]{1,0:T(8,128)(2,1)S(1)}, bf16[32,4096]{1,0:T(8,128)(2,1)S(1)}, u32[]{:S(2)}, u32[]{:S(2)}) collective-permute-start(bf16[32,4096]{1,0:T(8,128)(2,1)S(1)} %collective-permute-done.11.refs_0_), channel_id=1, source_target_pairs={{0,16},{16,0},{1,17},{17,1},{2,18},{18,2},{3,19},{19,3},{4,20},{20... | collective-permute-start | bytes 786440 | tf_op jit(solution)/shard_map/ppermute | solution.py:122
  39.9 2.3 %collective-permute-done.5.refs_0_ = bf16[32,4096]{1,0:T(8,128)(2,1)S(1)} collective-permute-done((bf16[32,4096]{1,0:T(8,128)(2,1)S(1)}, bf16[32,4096]{1,0:T(8,128)(2,1)S(1)}, u32[]{:S(2)}, u32[]{:S(2)}) %collective-permute-start.5) | collective-permute-done | bytes 262176 | tf_op jit(solution)/shard_map/ppermute | solution.py:113
  42.2 1.3 %collective-permute-start.10 = (bf16[32,4096]{1,0:T(8,128)(2,1)S(1)}, bf16[32,4096]{1,0:T(8,128)(2,1)S(1)}, u32[]{:S(2)}, u32[]{:S(2)}) collective-permute-start(bf16[32,4096]{1,0:T(8,128)(2,1)S(1)} %collective-permute-done.5.refs_0_), channel_id=1, source_target_pairs={{0,16},{16,0},{1,17},{17,1},{2,18},{18,2},{3,19},{19,3},{4,20},{20... | collective-permute-start | bytes 786440 | tf_op jit(solution)/shard_map/ppermute | solution.py:122
  43.5 1.5 %collective-permute-done.12.refs_1_ = bf16[32,4096]{1,0:T(8,128)(2,1)S(1)} collective-permute-done((bf16[32,4096]{1,0:T(8,128)(2,1)S(1)}, bf16[32,4096]{1,0:T(8,128)(2,1)S(1)}, u32[]{:S(2)}, u32[]{:S(2)}) %collective-permute-start.12) | collective-permute-done | bytes 262176 | tf_op jit(solution)/shard_map/ppermute | solution.py:122
  45.8 3.0 %collective-permute-done.15.refs_0_ = bf16[32,4096]{1,0:T(8,128)(2,1)S(1)} collective-permute-done((bf16[32,4096]{1,0:T(8,128)(2,1)S(1)}, bf16[32,4096]{1,0:T(8,128)(2,1)S(1)}, u32[]{:S(2)}, u32[]{:S(2)}) %collective-permute-start.15) | collective-permute-done | bytes 262176 | tf_op jit(solution)/shard_map/ppermute | solution.py:113
  49.7 1.6 %collective-permute-done.10.refs_1_ = bf16[32,4096]{1,0:T(8,128)(2,1)S(1)} collective-permute-done((bf16[32,4096]{1,0:T(8,128)(2,1)S(1)}, bf16[32,4096]{1,0:T(8,128)(2,1)S(1)}, u32[]{:S(2)}, u32[]{:S(2)}) %collective-permute-start.10) | collective-permute-done | bytes 262176 | tf_op jit(solution)/shard_map/ppermute | solution.py:122
  51.3 3.2 %collective-permute-done.9.refs_0_ = bf16[32,4096]{1,0:T(8,128)(2,1)S(1)} collective-permute-done((bf16[32,4096]{1,0:T(8,128)(2,1)S(1)}, bf16[32,4096]{1,0:T(8,128)(2,1)S(1)}, u32[]{:S(2)}, u32[]{:S(2)}) %collective-permute-start.9) | collective-permute-done | bytes 262176 | tf_op jit(solution)/shard_map/ppermute | solution.py:113
  56.4 4.2 %collective-permute-done.18.refs_0_ = bf16[32,4096]{1,0:T(8,128)(2,1)S(1)} collective-permute-done((bf16[32,4096]{1,0:T(8,128)(2,1)S(1)}, bf16[32,4096]{1,0:T(8,128)(2,1)S(1)}, u32[]{:S(2)}, u32[]{:S(2)}) %collective-permute-start.18) | collective-permute-done | bytes 262176 | tf_op jit(solution)/shard_map/ppermute | solution.py:113
  62.3 1.4 %collective-permute-done.14.refs_1_ = bf16[32,4096]{1,0:T(8,128)(2,1)S(1)} collective-permute-done((bf16[32,4096]{1,0:T(8,128)(2,1)S(1)}, bf16[32,4096]{1,0:T(8,128)(2,1)S(1)}, u32[]{:S(2)}, u32[]{:S(2)}) %collective-permute-start.14) | collective-permute-done | bytes 262176 | tf_op jit(solution)/shard_map/ppermute | solution.py:122
  64.5 1.9 %collective-permute-done.13.refs_0_ = bf16[32,4096]{1,0:T(8,128)(2,1)S(1)} collective-permute-done((bf16[32,4096]{1,0:T(8,128)(2,1)S(1)}, bf16[32,4096]{1,0:T(8,128)(2,1)S(1)}, u32[]{:S(2)}, u32[]{:S(2)}) %collective-permute-start.13) | collective-permute-done | bytes 262176 | tf_op jit(solution)/shard_map/ppermute | solution.py:113
  66.8 3.9 %collective-permute-done.21.refs_0_ = bf16[32,4096]{1,0:T(8,128)(2,1)S(1)} collective-permute-done((bf16[32,4096]{1,0:T(8,128)(2,1)S(1)}, bf16[32,4096]{1,0:T(8,128)(2,1)S(1)}, u32[]{:S(2)}, u32[]{:S(2)}) %collective-permute-start.21) | collective-permute-done | bytes 262176 | tf_op jit(solution)/shard_map/ppermute | solution.py:113
  71.6 1.9 %collective-permute-done.17.refs_0_ = bf16[32,2048]{1,0:T(8,128)(2,1)S(1)} collective-permute-done((bf16[32,2048]{1,0:T(8,128)(2,1)S(1)}, bf16[32,2048]{1,0:T(8,128)(2,1)S(1)}, u32[]{:S(2)}, u32[]{:S(2)}) %collective-permute-start.17) | collective-permute-done | bytes 131104 | tf_op jit(solution)/shard_map/ppermute | solution.py:113
  75.5 4.8 %collective-permute-done.22.refs_2_ = bf16[32,2048]{1,0:T(8,128)(2,1)S(1)} collective-permute-done((bf16[32,2048]{1,0:T(8,128)(2,1)S(1)}, bf16[32,2048]{1,0:T(8,128)(2,1)S(1)}, u32[]{:S(2)}, u32[]{:S(2)}) %collective-permute-start.22) | collective-permute-done | bytes 131104 | tf_op jit(solution)/shard_map/ppermute | solution.py:113
  81.9 3.3 %collective-permute-done.24.refs_3_ = bf16[32,2048]{1,0:T(8,128)(2,1)S(1)} collective-permute-done((bf16[32,2048]{1,0:T(8,128)(2,1)S(1)}, bf16[32,2048]{1,0:T(8,128)(2,1)S(1)}, u32[]{:S(2)}, u32[]{:S(2)}) %collective-permute-start.24) | collective-permute-done | bytes 131104 | tf_op jit(solution)/shard_map/ppermute | solution.py:122
  86.1 1.3 %collective-permute-done.26 = f32[2,64,256]{2,1,0:T(8,128)S(1)} collective-permute-done((f32[2,64,256]{2,1,0:T(8,128)S(1)}, f32[2,64,256]{2,1,0:T(8,128)S(1)}, u32[]{:S(2)}, u32[]{:S(2)}) %collective-permute-start.26) | collective-permute-done | bytes 131104 | tf_op jit(solution)/shard_map/ppermute | solution.py:131
  87.5 3.2 %collective-permute-start.27 = (f32[1,64,256]{2,1,0:T(8,128)S(1)}, f32[1,64,256]{2,1,0:T(8,128)S(1)}, u32[]{:S(2)}, u32[]{:S(2)}) collective-permute-start(f32[1,64,256]{2,1,0:T(8,128)S(1)} %slice_bitcast_fusion.2), channel_id=1, source_target_pairs={{0,2},{1,3},{2,0},{3,1},{4,6},{5,7},{6,4},{7,5},{8,10},{9,11},{10,... | collective-permute-start | bytes 196616 | tf_op jit(solution)/shard_map/ppermute | solution.py:131
  90.7 2.4 %collective-permute-done.27 = f32[1,64,256]{2,1,0:T(8,128)S(1)} collective-permute-done((f32[1,64,256]{2,1,0:T(8,128)S(1)}, f32[1,64,256]{2,1,0:T(8,128)S(1)}, u32[]{:S(2)}, u32[]{:S(2)}) %collective-permute-start.27) | collective-permute-done | bytes 65568 | tf_op jit(solution)/shard_map/ppermute | solution.py:131
  (52 shorter events, 19.1 us)
Async XLA Ops:
  1.1 12.2 %collective-permute-start.3 = (bf16[32,4096]{1,0:T(8,128)(2,1)S(1)}, bf16[32,4096]{1,0:T(8,128)(2,1)S(1)}, u32[]{:S(2)}, u32[]{:S(2)}) collective-permute-start(bf16[32,4096]{1,0:T(8,128)(2,1)S(1)} %slice_select_fusion.3), channel_id=1, source_target_pairs={{0,4},{4,8},{8,12},{12,0},{1,5},{5,9},{9,13},{13,1},{2,6},{6,10},{... | collective-permute-start | bytes 786440 | tf_op jit(solution)/shard_map/ppermute | solution.py:113
  5.2 13.7 %collective-permute-start = (bf16[32,4096]{1,0:T(8,128)(2,1)S(1)}, bf16[32,4096]{1,0:T(8,128)(2,1)S(1)}, u32[]{:S(2)}, u32[]{:S(2)}) collective-permute-start(bf16[32,4096]{1,0:T(8,128)(2,1)S(1)} %slice_select_fusion.2), channel_id=1, source_target_pairs={{0,4},{4,8},{8,12},{12,0},{1,5},{5,9},{9,13},{13,1},{2,6},{6,10},{... | collective-permute-start | bytes 786440 | tf_op jit(solution)/shard_map/ppermute | solution.py:113
  7.9 4.1 %copy-start = (bf16[64,16384]{1,0:T(8,128)(2,1)S(1)}, bf16[64,16384]{1,0:T(8,128)(2,1)}, u32[]{:S(2)}) copy-start(bf16[64,16384]{1,0:T(8,128)(2,1)} %test.1) | copy-start | bytes 6291460
  7.9 7.3 %copy-start.1 = (f32[16384]{0:T(1024)S(1)}, f32[16384]{0:T(1024)}, u32[]{:S(2)}) copy-start(f32[16384]{0:T(1024)} %param.5) | copy-start | bytes 196612
  13.3 11.2 %collective-permute-start.7 = (bf16[32,4096]{1,0:T(8,128)(2,1)S(1)}, bf16[32,4096]{1,0:T(8,128)(2,1)S(1)}, u32[]{:S(2)}, u32[]{:S(2)}) collective-permute-start(bf16[32,4096]{1,0:T(8,128)(2,1)S(1)} %slice_select_fusion.1), channel_id=1, source_target_pairs={{0,4},{4,8},{8,12},{12,0},{1,5},{5,9},{9,13},{13,1},{2,6},{6,10},{... | collective-permute-start | bytes 786440 | tf_op jit(solution)/shard_map/ppermute | solution.py:113
  13.7 10.8 %collective-permute-start.4 = (bf16[32,4096]{1,0:T(8,128)(2,1)S(1)}, bf16[32,4096]{1,0:T(8,128)(2,1)S(1)}, u32[]{:S(2)}, u32[]{:S(2)}) collective-permute-start(bf16[32,4096]{1,0:T(8,128)(2,1)S(1)} %collective-permute-done.3.refs_0_), channel_id=1, source_target_pairs={{0,16},{16,0},{1,17},{17,1},{2,18},{18,2},{3,19},{19,3},{4,20},{20... | collective-permute-start | bytes 786440 | tf_op jit(solution)/shard_map/ppermute | solution.py:122
  18.9 8.5 %collective-permute-start.2 = (bf16[32,4096]{1,0:T(8,128)(2,1)S(1)}, bf16[32,4096]{1,0:T(8,128)(2,1)S(1)}, u32[]{:S(2)}, u32[]{:S(2)}) collective-permute-start(bf16[32,4096]{1,0:T(8,128)(2,1)S(1)} %collective-permute-done.refs_0_), channel_id=1, source_target_pairs={{0,16},{16,0},{1,17},{17,1},{2,18},{18,2},{3,19},{19,3},{4,20},{20... | collective-permute-start | bytes 786440 | tf_op jit(solution)/shard_map/ppermute | solution.py:122
  20.7 8.7 %collective-permute-start.1 = (bf16[32,4096]{1,0:T(8,128)(2,1)S(1)}, bf16[32,4096]{1,0:T(8,128)(2,1)S(1)}, u32[]{:S(2)}, u32[]{:S(2)}) collective-permute-start(bf16[32,4096]{1,0:T(8,128)(2,1)S(1)} %slice_select_fusion), channel_id=1, source_target_pairs={{0,4},{4,8},{8,12},{12,0},{1,5},{5,9},{9,13},{13,1},{2,6},{6,10},{... | collective-permute-start | bytes 786440 | tf_op jit(solution)/shard_map/ppermute | solution.py:113
  24.5 9.0 %collective-permute-start.8 = (bf16[32,4096]{1,0:T(8,128)(2,1)S(1)}, bf16[32,4096]{1,0:T(8,128)(2,1)S(1)}, u32[]{:S(2)}, u32[]{:S(2)}) collective-permute-start(bf16[32,4096]{1,0:T(8,128)(2,1)S(1)} %collective-permute-done.7.refs_0_), channel_id=1, source_target_pairs={{0,16},{16,0},{1,17},{17,1},{2,18},{18,2},{3,19},{19,3},{4,20},{20... | collective-permute-start | bytes 786440 | tf_op jit(solution)/shard_map/ppermute | solution.py:122
  27.1 8.7 %collective-permute-start.11 = (bf16[32,4096]{1,0:T(8,128)(2,1)S(1)}, bf16[32,4096]{1,0:T(8,128)(2,1)S(1)}, u32[]{:S(2)}, u32[]{:S(2)}) collective-permute-start(bf16[32,4096]{1,0:T(8,128)(2,1)S(1)} %collective-permute-done.3.refs_0_), channel_id=1, source_target_pairs={{0,4},{4,8},{8,12},{12,0},{1,5},{5,9},{9,13},{13,1},{2,6},{6,10},{... | collective-permute-start | bytes 786440 | tf_op jit(solution)/shard_map/ppermute | solution.py:113
  29.4 9.8 %collective-permute-start.6 = (bf16[32,4096]{1,0:T(8,128)(2,1)S(1)}, bf16[32,4096]{1,0:T(8,128)(2,1)S(1)}, u32[]{:S(2)}, u32[]{:S(2)}) collective-permute-start(bf16[32,4096]{1,0:T(8,128)(2,1)S(1)} %collective-permute-done.1.refs_0_), channel_id=1, source_target_pairs={{0,16},{16,0},{1,17},{17,1},{2,18},{18,2},{3,19},{19,3},{4,20},{20... | collective-permute-start | bytes 786440 | tf_op jit(solution)/shard_map/ppermute | solution.py:122
  32.4 9.8 %collective-permute-start.5 = (bf16[32,4096]{1,0:T(8,128)(2,1)S(1)}, bf16[32,4096]{1,0:T(8,128)(2,1)S(1)}, u32[]{:S(2)}, u32[]{:S(2)}) collective-permute-start(bf16[32,4096]{1,0:T(8,128)(2,1)S(1)} %collective-permute-done.refs_0_), channel_id=1, source_target_pairs={{0,4},{4,8},{8,12},{12,0},{1,5},{5,9},{9,13},{13,1},{2,6},{6,10},{... | collective-permute-start | bytes 786440 | tf_op jit(solution)/shard_map/ppermute | solution.py:113
  35.8 9.3 %collective-permute-start.12 = (bf16[32,4096]{1,0:T(8,128)(2,1)S(1)}, bf16[32,4096]{1,0:T(8,128)(2,1)S(1)}, u32[]{:S(2)}, u32[]{:S(2)}) collective-permute-start(bf16[32,4096]{1,0:T(8,128)(2,1)S(1)} %collective-permute-done.11.refs_0_), channel_id=1, source_target_pairs={{0,16},{16,0},{1,17},{17,1},{2,18},{18,2},{3,19},{19,3},{4,20},{20... | collective-permute-start | bytes 786440 | tf_op jit(solution)/shard_map/ppermute | solution.py:122
  38.6 10.2 %collective-permute-start.15 = (bf16[32,4096]{1,0:T(8,128)(2,1)S(1)}, bf16[32,4096]{1,0:T(8,128)(2,1)S(1)}, u32[]{:S(2)}, u32[]{:S(2)}) collective-permute-start(bf16[32,4096]{1,0:T(8,128)(2,1)S(1)} %collective-permute-done.7.refs_0_), channel_id=1, source_target_pairs={{0,4},{4,8},{8,12},{12,0},{1,5},{5,9},{9,13},{13,1},{2,6},{6,10},{... | collective-permute-start | bytes 786440 | tf_op jit(solution)/shard_map/ppermute | solution.py:113
  42.2 9.1 %collective-permute-start.10 = (bf16[32,4096]{1,0:T(8,128)(2,1)S(1)}, bf16[32,4096]{1,0:T(8,128)(2,1)S(1)}, u32[]{:S(2)}, u32[]{:S(2)}) collective-permute-start(bf16[32,4096]{1,0:T(8,128)(2,1)S(1)} %collective-permute-done.5.refs_0_), channel_id=1, source_target_pairs={{0,16},{16,0},{1,17},{17,1},{2,18},{18,2},{3,19},{19,3},{4,20},{20... | collective-permute-start | bytes 786440 | tf_op jit(solution)/shard_map/ppermute | solution.py:122
  43.5 11.0 %collective-permute-start.9 = (bf16[32,4096]{1,0:T(8,128)(2,1)S(1)}, bf16[32,4096]{1,0:T(8,128)(2,1)S(1)}, u32[]{:S(2)}, u32[]{:S(2)}) collective-permute-start(bf16[32,4096]{1,0:T(8,128)(2,1)S(1)} %collective-permute-done.1.refs_0_), channel_id=1, source_target_pairs={{0,4},{4,8},{8,12},{12,0},{1,5},{5,9},{9,13},{13,1},{2,6},{6,10},{... | collective-permute-start | bytes 786440 | tf_op jit(solution)/shard_map/ppermute | solution.py:113
  48.8 7.6 %collective-permute-start.16 = (bf16[32,4096]{1,0:T(8,128)(2,1)S(1)}, bf16[32,4096]{1,0:T(8,128)(2,1)S(1)}, u32[]{:S(2)}, u32[]{:S(2)}) collective-permute-start(bf16[32,4096]{1,0:T(8,128)(2,1)S(1)} %collective-permute-done.15.refs_0_), channel_id=1, source_target_pairs={{0,16},{16,0},{1,17},{17,1},{2,18},{18,2},{3,19},{19,3},{4,20},{20... | collective-permute-start | bytes 786440 | tf_op jit(solution)/shard_map/ppermute | solution.py:122
  49.7 10.9 %collective-permute-start.18 = (bf16[32,4096]{1,0:T(8,128)(2,1)S(1)}, bf16[32,4096]{1,0:T(8,128)(2,1)S(1)}, u32[]{:S(2)}, u32[]{:S(2)}) collective-permute-start(bf16[32,4096]{1,0:T(8,128)(2,1)S(1)} %collective-permute-done.11.refs_0_), channel_id=1, source_target_pairs={{0,4},{4,8},{8,12},{12,0},{1,5},{5,9},{9,13},{13,1},{2,6},{6,10},{... | collective-permute-start | bytes 786440 | tf_op jit(solution)/shard_map/ppermute | solution.py:113
  55.3 11.0 %collective-permute-start.13 = (bf16[32,4096]{1,0:T(8,128)(2,1)S(1)}, bf16[32,4096]{1,0:T(8,128)(2,1)S(1)}, u32[]{:S(2)}, u32[]{:S(2)}) collective-permute-start(bf16[32,4096]{1,0:T(8,128)(2,1)S(1)} %collective-permute-done.5.refs_0_), channel_id=1, source_target_pairs={{0,4},{4,8},{8,12},{12,0},{1,5},{5,9},{9,13},{13,1},{2,6},{6,10},{... | collective-permute-start | bytes 786440 | tf_op jit(solution)/shard_map/ppermute | solution.py:113
  55.4 8.3 %collective-permute-start.14 = (bf16[32,4096]{1,0:T(8,128)(2,1)S(1)}, bf16[32,4096]{1,0:T(8,128)(2,1)S(1)}, u32[]{:S(2)}, u32[]{:S(2)}) collective-permute-start(bf16[32,4096]{1,0:T(8,128)(2,1)S(1)} %collective-permute-done.9.refs_0_), channel_id=1, source_target_pairs={{0,16},{16,0},{1,17},{17,1},{2,18},{18,2},{3,19},{19,3},{4,20},{20... | collective-permute-start | bytes 786440 | tf_op jit(solution)/shard_map/ppermute | solution.py:122
  60.6 12.9 %collective-permute-start.19 = (bf16[32,4096]{1,0:T(8,128)(2,1)S(1)}, bf16[32,4096]{1,0:T(8,128)(2,1)S(1)}, u32[]{:S(2)}, u32[]{:S(2)}) collective-permute-start(bf16[32,4096]{1,0:T(8,128)(2,1)S(1)} %collective-permute-done.18.refs_0_), channel_id=1, source_target_pairs={{0,16},{16,0},{1,17},{17,1},{2,18},{18,2},{3,19},{19,3},{4,20},{20... | collective-permute-start | bytes 786440 | tf_op jit(solution)/shard_map/ppermute | solution.py:122
  62.2 8.5 %collective-permute-start.21 = (bf16[32,4096]{1,0:T(8,128)(2,1)S(1)}, bf16[32,4096]{1,0:T(8,128)(2,1)S(1)}, u32[]{:S(2)}, u32[]{:S(2)}) collective-permute-start(bf16[32,4096]{1,0:T(8,128)(2,1)S(1)} %collective-permute-done.15.refs_0_), channel_id=1, source_target_pairs={{0,4},{4,8},{8,12},{12,0},{1,5},{5,9},{9,13},{13,1},{2,6},{6,10},{... | collective-permute-start | bytes 786440 | tf_op jit(solution)/shard_map/ppermute | solution.py:113
  66.3 7.2 %collective-permute-start.17 = (bf16[32,2048]{1,0:T(8,128)(2,1)S(1)}, bf16[32,2048]{1,0:T(8,128)(2,1)S(1)}, u32[]{:S(2)}, u32[]{:S(2)}) collective-permute-start(bf16[32,2048]{1,0:T(8,128)(2,1)S(1)} %get-tuple-element.46), channel_id=1, source_target_pairs={{0,4},{4,8},{8,12},{12,0},{1,5},{5,9},{9,13},{13,1},{2,6},{6,10},{... | collective-permute-start | bytes 393224 | tf_op jit(solution)/shard_map/ppermute | solution.py:113
  66.3 9.2 %collective-permute-start.23 = (bf16[32,4096]{1,0:T(8,128)(2,1)S(1)}, bf16[32,4096]{1,0:T(8,128)(2,1)S(1)}, u32[]{:S(2)}, u32[]{:S(2)}) collective-permute-start(bf16[32,4096]{1,0:T(8,128)(2,1)S(1)} %collective-permute-done.13.refs_0_), channel_id=1, source_target_pairs={{0,16},{16,0},{1,17},{17,1},{2,18},{18,2},{3,19},{19,3},{4,20},{20... | collective-permute-start | bytes 786440 | tf_op jit(solution)/shard_map/ppermute | solution.py:122
  70.7 10.4 %collective-permute-start.25 = (bf16[32,4096]{1,0:T(8,128)(2,1)S(1)}, bf16[32,4096]{1,0:T(8,128)(2,1)S(1)}, u32[]{:S(2)}, u32[]{:S(2)}) collective-permute-start(bf16[32,4096]{1,0:T(8,128)(2,1)S(1)} %collective-permute-done.21.refs_0_), channel_id=1, source_target_pairs={{0,16},{16,0},{1,17},{17,1},{2,18},{18,2},{3,19},{19,3},{4,20},{20... | collective-permute-start | bytes 786440 | tf_op jit(solution)/shard_map/ppermute | solution.py:122
  73.5 6.8 %collective-permute-start.22 = (bf16[32,2048]{1,0:T(8,128)(2,1)S(1)}, bf16[32,2048]{1,0:T(8,128)(2,1)S(1)}, u32[]{:S(2)}, u32[]{:S(2)}) collective-permute-start(bf16[32,2048]{1,0:T(8,128)(2,1)S(1)} %get-tuple-element.51), channel_id=1, source_target_pairs={{0,4},{4,8},{8,12},{12,0},{1,5},{5,9},{9,13},{13,1},{2,6},{6,10},{... | collective-permute-start | bytes 393224 | tf_op jit(solution)/shard_map/ppermute | solution.py:113
  74.3 7.7 %collective-permute-start.20 = (bf16[32,2048]{1,0:T(8,128)(2,1)S(1)}, bf16[32,2048]{1,0:T(8,128)(2,1)S(1)}, u32[]{:S(2)}, u32[]{:S(2)}) collective-permute-start(bf16[32,2048]{1,0:T(8,128)(2,1)S(1)} %collective-permute-done.17.refs_0_), channel_id=1, source_target_pairs={{0,16},{16,0},{1,17},{17,1},{2,18},{18,2},{3,19},{19,3},{4,20},{20... | collective-permute-start | bytes 393224 | tf_op jit(solution)/shard_map/ppermute | solution.py:122
  80.3 5.0 %collective-permute-start.24 = (bf16[32,2048]{1,0:T(8,128)(2,1)S(1)}, bf16[32,2048]{1,0:T(8,128)(2,1)S(1)}, u32[]{:S(2)}, u32[]{:S(2)}) collective-permute-start(bf16[32,2048]{1,0:T(8,128)(2,1)S(1)} %collective-permute-done.22.refs_2_), channel_id=1, source_target_pairs={{0,16},{16,0},{1,17},{17,1},{2,18},{18,2},{3,19},{19,3},{4,20},{20... | collective-permute-start | bytes 393224 | tf_op jit(solution)/shard_map/ppermute | solution.py:122
  86.0 1.4 %collective-permute-start.26 = (f32[2,64,256]{2,1,0:T(8,128)S(1)}, f32[2,64,256]{2,1,0:T(8,128)S(1)}, u32[]{:S(2)}, u32[]{:S(2)}) collective-permute-start(f32[2,64,256]{2,1,0:T(8,128)S(1)} %slice_bitcast_fusion), channel_id=1, source_target_pairs={{0,1},{1,0},{2,3},{3,2},{4,5},{5,4},{6,7},{7,6},{8,9},{9,8},{10,11... | collective-permute-start | bytes 393224 | tf_op jit(solution)/shard_map/ppermute | solution.py:131
  87.5 5.6 %collective-permute-start.27 = (f32[1,64,256]{2,1,0:T(8,128)S(1)}, f32[1,64,256]{2,1,0:T(8,128)S(1)}, u32[]{:S(2)}, u32[]{:S(2)}) collective-permute-start(f32[1,64,256]{2,1,0:T(8,128)S(1)} %slice_bitcast_fusion.2), channel_id=1, source_target_pairs={{0,2},{1,3},{2,0},{3,1},{4,6},{5,7},{6,4},{7,5},{8,10},{9,11},{10,... | collective-permute-start | bytes 196616 | tf_op jit(solution)/shard_map/ppermute | solution.py:131
